TPU v7x, 32 devices: a whole 2x2x4 slice. The times are simulated.
32 devices in a mesh: groups: 2 (over y), expert: 4 (over z), dp: 4 (over x, core).
Axes of the slice: x: 2, y: 2, z: 4, core: 2. Of those that a mesh axis runs over, the one named last changes fastest.
Arguments:
- tokens: bfloat16 [512, 6144], P(('groups', 'expert'), 'dp'), parts along dimension 0, may hold values from -6 to 6
- expert_ids: int32 [512, 8], P(('groups', 'expert')), parts along dimension 0, may hold values from 0 to 31, all different within a row; in each aligned block of 64 rows (0 to 63, 64 to 127, ...) at most 32 rows name the same one
- scores: float32 [512, 8], P(('groups', 'expert')), parts along dimension 0, may hold values from -8 to 8
- w_gate: bfloat16 [32, 6144, 1024], P('expert', 'dp'), may hold values from -0.078125 to 0.078125
- w_up: bfloat16 [32, 6144, 1024], P('expert', 'dp'), may hold values from -0.078125 to 0.078125
- w_down: bfloat16 [32, 1024, 6144], P('expert', None, 'dp'), may hold values from -0.1875 to 0.1875
Outputs:
- mixed: bfloat16 [512, 6144], P(('groups', 'expert'), 'dp'), parts along dimension 0
There are 2 independent parts, one for each index of `groups`. A program takes and returns all parts, laid end to end along the dimension named above; an argument that names none is the same for every part. Nothing has to cross between parts.
Inputs may be any that keep to these rules, and one draw needn't show every extreme that they name: `expert_ids`: each row names 8 different experts; among the rows of one index of expert (aligned blocks of 64 rows) no expert is named by more than 32 rows, a bound that some block reaches.
All inputs are finite; a program needn't handle non-finite values.
Results may differ from a plain program's by a relative error of at most 0.024.
Values may be sent and summed in bfloat16 or wider, within the bound.
No kernel may reach another device: no remote copies, remote signals or barrier semaphores. Data moves between devices by JAX's collectives and lax.ppermute only.
A program may use at most 128 MiB of HBM per device.

v0:
```python
import functools

import jax
import jax.numpy as jnp
from jax import lax
from jax.experimental import pallas as pl
from jax.experimental.pallas import tpu as pltpu
from jax.sharding import PartitionSpec as P

LANES = 128
VMEM = pl.BlockSpec(memory_space=pltpu.VMEM)
SMEM = pl.BlockSpec(memory_space=pltpu.SMEM)
HERE = pl.BlockSpec(memory_space=pl.ANY)
NOWHERE = -1e6


def bits_of(n):
    return [b for b in range(n.bit_length() - 1)]


def flip(x, axis, k):
    return lax.ppermute(x, axis, [(i, i ^ k) for i in range(lax.axis_size(axis))])


def route_body(n, experts, per_chunk, rows, info, *refs):
    meta, (rank_t, rank, wt, sched) = refs[:n], refs[n:]
    tok, top = meta[0].shape[0], meta[0].shape[1] // 2
    first = info[0].astype(jnp.float32)
    lane = lax.broadcasted_iota(jnp.int32, (tok, LANES), 1).astype(jnp.float32)
    before = (
        lax.broadcasted_iota(jnp.int32, (tok, tok), 0) > lax.broadcasted_iota(jnp.int32, (tok, tok), 1)
    ).astype(jnp.bfloat16)
    seen = jnp.zeros((1, LANES), jnp.float32)
    for s in range(n):
        block = meta[s][...]
        affinity = 1.0 / (1.0 + jnp.exp(-block[:, top:]))
        share = 2.5 * affinity / jnp.sum(affinity, axis=1, keepdims=True)
        named = jnp.zeros((tok, LANES), jnp.float32)
        weight = jnp.zeros((tok, LANES), jnp.float32)
        for k in range(top):
            hit = jnp.where(block[:, k : k + 1] - first == lane, 1.0, 0.0)
            named = named + hit
            weight = weight + hit * share[:, k : k + 1]
        named = jnp.where(lane < experts, named, 0.0)
        place = jnp.dot(before, named.astype(jnp.bfloat16), preferred_element_type=jnp.float32) + seen
        rank[s * tok : (s + 1) * tok, :] = jnp.where(named > 0, place, NOWHERE)
        wt[s * tok : (s + 1) * tok, :] = weight
        seen = seen + jnp.sum(named, axis=0, keepdims=True)
    turned = jnp.transpose(rank[...])[: rank_t.shape[0]]
    rank_t[...] = turned
    count = jnp.sum((turned >= 0).astype(jnp.float32), axis=1, keepdims=True)
    shape = (rank_t.shape[0], LANES)
    j = lax.broadcasted_iota(jnp.int32, shape, 1).astype(jnp.float32)
    e = lax.broadcasted_iota(jnp.int32, shape, 0).astype(jnp.float32)
    ahead = ((seen > count) | ((seen == count) & (j < e))) & (j < experts)
    order = jnp.sum(ahead.astype(jnp.float32), axis=1, keepdims=True)
    large = jnp.where((order == j) & (e < experts), 1.0, 0.0)
    small = jnp.where((order == experts - 1 - j) & (e < experts), 1.0, 0.0)
    expert_a = jnp.sum(e * large, axis=0, keepdims=True)
    count_a = jnp.sum(count * large, axis=0, keepdims=True)
    if per_chunk == 2:
        expert_b = jnp.sum(e * small, axis=0, keepdims=True)
        count_b = jnp.sum(count * small, axis=0, keepdims=True)
    else:
        expert_b, count_b = expert_a, jnp.zeros_like(count_a)
        count_a = jnp.full_like(count_a, rows)
    sched[0:1] = expert_a.astype(jnp.int32)
    sched[1:2] = expert_b.astype(jnp.int32)
    sched[2:3] = count_a.astype(jnp.int32)
    sched[3:4] = (count_a + count_b).astype(jnp.int32)
    sched[4:8] = jnp.full((4, LANES), info[1], jnp.int32)


def route(meta, info, experts, per_chunk, rows):
    tokens = len(meta) * meta[0].shape[0]
    padded = -(-experts // 8) * 8
    return pl.pallas_call(
        functools.partial(route_body, len(meta), experts, per_chunk, rows),
        out_shape=(
            jax.ShapeDtypeStruct((padded, tokens), jnp.float32),
            jax.ShapeDtypeStruct((tokens, LANES), jnp.float32),
            jax.ShapeDtypeStruct((tokens, LANES), jnp.float32),
            jax.ShapeDtypeStruct((8, LANES), jnp.int32),
        ),
        in_specs=[SMEM] + [VMEM] * len(meta),
        out_specs=(VMEM,) * 4,
        name="route",
    )(info, *meta)


def put(out, at, left, right, rows, split):
    most = left.shape[0]
    if right is None:
        out[at] = left
        return
    head = min(rows - most, most)
    out[at[:-2] + (slice(0, head), at[-1])] = left[:head]
    if head < most:
        shared = lax.broadcasted_iota(jnp.int32, (most - head, left.shape[1]), 0) + head < split
        out[at[:-2] + (slice(head, most), at[-1])] = jnp.where(shared, left[head:], right[: most - head])
    out[at[:-2] + (slice(most, rows), at[-1])] = right[most - head :]


def gate_up_body(n, chunk, n_dp, most, after, sched, *refs):
    tokens, (rank_t, w_gate, w_up), refs = refs[:n], refs[n : n + 3], refs[n + 3 + after :]
    send, keep, feed, rows, held, feed_sem, held_sem = refs
    count = rows.shape[0]
    width = send.shape[2] // 2
    split = sched[2, chunk]
    experts = [sched[0, chunk]] + ([sched[1, chunk]] if most < count else [])
    loads = [(w, e) for w in (w_gate, w_up) for e in experts]
    copies = [
        pltpu.make_async_copy(w.at[e], held.at[i], held_sem.at[i]) for i, (w, e) in enumerate(loads)
    ]
    at, feeds = 0, []
    for s in range(n):
        tok = tokens[s].shape[0]
        feeds.append(pltpu.make_async_copy(tokens[s], feed.at[pl.ds(at, tok)], feed_sem.at[s]))
        at += tok
    for copy in feeds:
        copy.start()
    for copy in copies[: len(experts)]:
        copy.start()
    r = lax.broadcasted_iota(jnp.int32, (count, at), 0).astype(jnp.float32)
    pick = jnp.where(r == rank_t[pl.ds(experts[0], 1), :], 1.0, 0.0)
    if most < count:
        pick = pick + jnp.where(count - 1 - r == rank_t[pl.ds(experts[1], 1), :], 1.0, 0.0)
    for copy in feeds:
        copy.wait()
    rows[...] = jnp.dot(
        pick.astype(jnp.bfloat16), feed[...], preferred_element_type=jnp.float32
    ).astype(jnp.bfloat16)
    for m in range(2):
        first = m * len(experts)
        for copy in copies[first : first + len(experts)]:
            copy.wait()
        if m == 0:
            for copy in copies[len(experts) :]:
                copy.start()
        for l in range(n_dp):
            units = pl.ds(pl.multiple_of((l ^ sched[4, 0]) * width, width), width)
            left = jnp.dot(rows[:most], held[first, :, units], preferred_element_type=jnp.float32)
            right = None
            if most < count:
                right = jnp.dot(
                    rows[count - most :], held[first + 1, :, units], preferred_element_type=jnp.float32
                ).astype(jnp.bfloat16)
            to = (l // 2, slice(None), slice(m * width, (m + 1) * width))
            put(send if l % 2 else keep, to, left.astype(jnp.bfloat16), right, count, split)


def gate_up(tokens, rank_t, sched, w_gate, w_up, chunk, rows, most, n_dp, after):
    n, local = len(tokens), tokens[0].shape[1]
    hidden = w_gate.shape[2]
    out = jax.ShapeDtypeStruct((max(n_dp // 2, 1), rows, 2 * hidden // n_dp), jnp.bfloat16)
    mats = 2 * (2 if most < rows else 1)
    return pl.pallas_call(
        functools.partial(gate_up_body, n, chunk, n_dp, most, len(after)),
        out_shape=(out, out),
        in_specs=[SMEM] + [HERE] * n + [VMEM] + [HERE] * (2 + len(after)),
        out_specs=(VMEM, VMEM),
        scratch_shapes=[
            pltpu.VMEM((rank_t.shape[1], local), jnp.bfloat16),
            pltpu.VMEM((rows, local), jnp.bfloat16),
            pltpu.VMEM((mats, local, hidden), jnp.bfloat16),
            pltpu.SemaphoreType.DMA((n,)),
            pltpu.SemaphoreType.DMA((mats,)),
        ],
        compiler_params=pltpu.CompilerParams(vmem_limit_bytes=48 << 20),
        cost_estimate=pl.CostEstimate(
            flops=2 * mats * most * local * hidden,
            bytes_accessed=2 * mats * local * hidden,
            transcendentals=0,
        ),
        name="gate_up",
    )(sched, *tokens, rank_t, w_gate, w_up, *after)


def down_body(n_dp, n_out, chunk, first, most, after, sched, *refs):
    parts, (rank, wt, w_down), refs = refs[:n_dp], refs[n_dp : n_dp + 3], refs[n_dp + 3 :]
    before = None if first else refs[0]
    refs = refs[(0 if first else 1) + after :]
    outs, (hidden, mix, out, held, held_sem) = refs[:-5], refs[-5:]
    rows = hidden.shape[0]
    width = parts[0].shape[-1]
    split = sched[2, chunk]
    experts = [sched[0, chunk]] + ([sched[1, chunk]] if most < rows else [])
    copies = [
        pltpu.make_async_copy(w_down.at[e], held.at[i], held_sem.at[i]) for i, e in enumerate(experts)
    ]
    for copy in copies:
        copy.start()
    for l in range(n_dp):
        at = pl.multiple_of((l ^ sched[4, 0]) * width, width)
        hidden[:, pl.ds(at, width)] = parts[l][0]
    lane = lax.broadcasted_iota(jnp.int32, rank.shape, 1)
    column = lambda ref, e: jnp.sum(jnp.where(lane == e, ref[...], 0.0), axis=1, keepdims=True)
    r = lax.broadcasted_iota(jnp.int32, mix.shape, 1).astype(jnp.float32)
    share = jnp.where(r == column(rank, experts[0]), column(wt, experts[0]), 0.0)
    if most < rows:
        share = share + jnp.where(rows - 1 - r == column(rank, experts[1]), column(wt, experts[1]), 0.0)
    mix[...] = share.astype(jnp.bfloat16)
    for copy in copies:
        copy.wait()
    local = out.shape[1]
    block = 512 if local % 512 == 0 else 256 if local % 256 == 0 else local
    for i in range(local // block):
        cols = slice(i * block, (i + 1) * block)
        left = jnp.dot(hidden[:most], held[0, :, cols], preferred_element_type=jnp.float32)
        right = None
        if most < rows:
            right = jnp.dot(hidden[rows - most :], held[1, :, cols], preferred_element_type=jnp.float32)
            right = right.astype(jnp.bfloat16)
        put(out, (slice(None), cols), left.astype(jnp.bfloat16), right, rows, split)
        total = jnp.dot(mix[...], out[:, cols], preferred_element_type=jnp.float32)
        if not first:
            total = total + before[:, cols]
        tok = total.shape[0] // n_out
        for s in range(n_out):
            outs[s][:, cols] = total[s * tok : (s + 1) * tok].astype(outs[s].dtype)


def down(parts, rank, wt, sched, w_down, total, chunk, most, last, n_owner, after):
    n_dp = len(parts)
    _, rows, width = parts[0].shape
    _, hidden, local = w_down.shape
    tokens = rank.shape[0]
    n_out = n_owner if last else 1
    kind = jnp.bfloat16 if last else jnp.float32
    first = total is None
    mats = 2 if most < rows else 1
    outs = pl.pallas_call(
        functools.partial(down_body, n_dp, n_out, chunk, first, most, len(after)),
        out_shape=(jax.ShapeDtypeStruct((tokens // n_out, local), kind),) * n_out,
        in_specs=[SMEM]
        + [VMEM] * (n_dp + 2)
        + [HERE]
        + ([] if first else [VMEM])
        + [HERE] * len(after),
        out_specs=(VMEM,) * n_out,
        scratch_shapes=[
            pltpu.VMEM((rows, hidden), jnp.bfloat16),
            pltpu.VMEM((tokens, rows), jnp.bfloat16),
            pltpu.VMEM((rows, local), jnp.bfloat16),
            pltpu.VMEM((mats, hidden, local), jnp.bfloat16),
            pltpu.SemaphoreType.DMA((mats,)),
        ],
        compiler_params=pltpu.CompilerParams(vmem_limit_bytes=48 << 20),
        cost_estimate=pl.CostEstimate(
            flops=2 * local * (2 * most * hidden + rows * tokens),
            bytes_accessed=2 * mats * hidden * local + 8 * tokens * local,
            transcendentals=0,
        ),
        name="down",
    )(sched, *parts, rank, wt, w_down, *([] if first else [total]), *after)
    return outs if last else outs[0]


def finish_body(total, late, *refs):
    gate_up = total[...] + late[...].astype(jnp.float32)
    width = gate_up.shape[2] // 2
    gate, up = gate_up[:, :, :width], gate_up[:, :, width:]
    refs[-1][...] = (gate / (1.0 + jnp.exp(-gate)) * up).astype(jnp.bfloat16)


def partial_sums(send, keep, n_dp):
    total = keep.astype(jnp.float32)
    late = jnp.zeros(total.shape, jnp.bfloat16)
    for b in bits_of(n_dp):
        if b > 0:
            total = total + late.astype(jnp.float32)
            send = total[1::2].astype(jnp.bfloat16)
            total = total[0::2]
        late = flip(send, "dp", 1 << b)
    return total, late, send


def finish(total, late, after):
    return pl.pallas_call(
        finish_body,
        out_shape=jax.ShapeDtypeStruct(total.shape[:2] + (total.shape[2] // 2,), jnp.bfloat16),
        in_specs=[VMEM] * 2 + [HERE] * len(after),
        out_specs=VMEM,
        cost_estimate=pl.CostEstimate(flops=0, bytes_accessed=1 << 20, transcendentals=total.size // 2),
        name="finish",
    )(total, late, *after)


def all_parts(share, n_dp):
    parts = {0: share}
    for b in reversed(bits_of(n_dp)):
        for l in list(parts):
            parts[l | 1 << b] = flip(parts[l], "dp", 1 << b)
    return [parts[l] for l in range(n_dp)]


def on_device(tokens, expert_ids, scores, w_gate, w_up, w_down):
    n_owner, n_dp = lax.axis_size("expert"), lax.axis_size("dp")
    tok_rows, top = expert_ids.shape
    experts = w_gate.shape[0]
    capacity = 2 * tok_rows * top // (experts * n_owner)
    per_chunk = 2 if experts % 2 == 0 else 1
    most = n_owner * capacity
    rows = per_chunk * most
    chunks = experts // per_chunk

    meta = jnp.concatenate([expert_ids.astype(jnp.float32), scores], axis=1)
    feeds = gathered(tokens, "expert")
    metas = [meta] + [
        lax.ppermute(meta, "expert", [(i, (i - k) % n_owner) for i in range(n_owner)])
        for k in gathered_order(n_owner)[1:]
    ]
    info = jnp.stack([lax.axis_index("expert") * experts, lax.axis_index("dp")]).astype(jnp.int32)
    rank_t, rank, wt, sched = route(metas, info, experts, per_chunk, rows)

    shares, sent, parts, total = [], [], [], None
    add = lambda c, after: down(
        parts[c], rank, wt, sched, w_down, total, c, most, c == chunks - 1, n_owner, after
    )
    for c in range(chunks):
        after = ([sent[c - 2]] if c >= 2 else []) + ([shares[c - 3]] if c >= 3 else [])
        send, keep = gate_up(feeds, rank_t, sched, w_gate, w_up, c, rows, most, n_dp, after)
        mine, late, last_sent = partial_sums(send, keep, n_dp)
        sent.append(last_sent)
        if c == chunks - 1 and c > 0:
            total = add(0, [last_sent])
        shares.append(finish(mine, late, [] if total is None else [total]))
        parts.append(all_parts(shares[-1], n_dp))
    for c in range(1 if chunks > 1 else 0, chunks):
        total = add(c, [shares[-1]])
    return returned(total, "expert")


def gathered_order(n):
    near = [d for s in range(1, n // 2) for d in (-s, s)]
    return [0] + near + ([n // 2] if n > 1 else [])


def gathered(x, axis):
    n = lax.axis_size(axis)
    up, down_ = [(i, (i + 1) % n) for i in range(n)], [(i, (i - 1) % n) for i in range(n)]
    below = above = x
    found = [x]
    for _ in range(1, n // 2):
        below, above = lax.ppermute(below, axis, up), lax.ppermute(above, axis, down_)
        found += [below, above]
    if n > 1:
        half = x.shape[0] // 2
        found += [lax.ppermute(below[:half], axis, up), lax.ppermute(above[half:], axis, down_)]
    return found


def returned(partials, axis):
    n = lax.axis_size(axis)
    order = gathered_order(n)
    mixed = partials[0].astype(jnp.float32)
    for k, partial in zip(order[1:], partials[1:]):
        there = lax.ppermute(partial, axis, [(i, (i + k) % n) for i in range(n)])
        mixed = mixed + there.astype(jnp.float32)
    return mixed.astype(jnp.bfloat16)


def solution(mesh):
    in_specs = (
        P(("groups", "expert"), "dp"),
        P(("groups", "expert"), None),
        P(("groups", "expert"), None),
        P("expert", "dp", None),
        P("expert", "dp", None),
        P("expert", None, "dp"),
    )
    out_specs = P(("groups", "expert"), "dp")
    return jax.shard_map(
        on_device, mesh=mesh, in_specs=in_specs, out_specs=out_specs, check_vma=False
    )
```

profile of v0, /device:TPU:0, one launch (start us, length us, event | category | flops | bytes accessed | tf_op | source)
XLA Modules:
  0.0 141.1 jit_solution(15938810440324075145)
XLA Ops:
  0.0 5.0 %collective-permute-start.4 = (bf16[64,1536]{1,0:T(8,128)(2,1)}, bf16[64,1536]{1,0:T(8,128)(2,1)S(1)}, u32[]{:S(2)}, u32[]{:S(2)}) collective-permute-start(bf16[64,1536]{1,0:T(8,128)(2,1)} %refs_0_.7), channel_id=1, source_target_pairs={{0,12},{4,0},{8,4},{12,8},{1,13},{5,1},{9,5},{13,9},{2,14},{6,2},{... | collective-permute-start | bytes 589832 | tf_op jit(solution)/shard_map/ppermute | solution.py:345
  6.5 1.1 collective-permute-start.2
  7.6 2.9 %collective-permute-start.1 = (f32[64,16]{1,0:T(8,128)S(1)}, f32[64,16]{1,0:T(8,128)S(1)}, u32[]{:S(2)}, u32[]{:S(2)}) collective-permute-start(f32[64,16]{1,0:T(8,128)S(1)} %copy.12.refs_0_), channel_id=1, source_target_pairs={{0,12},{4,0},{8,4},{12,8},{1,13},{5,1},{9,5},{13,9},{2,14},{6,2},{... | collective-permute-start | bytes 12296 | tf_op jit(solution)/shard_map/ppermute | solution.py:310
  11.0 3.9 %collective-permute-start.6 = (bf16[32,1536]{1,0:T(8,128)(2,1)S(1)}, bf16[32,1536]{1,0:T(8,128)(2,1)S(1)}, u32[]{:S(2)}, u32[]{:S(2)}) collective-permute-start(bf16[32,1536]{1,0:T(8,128)(2,1)S(1)} %slice.53), channel_id=1, source_target_pairs={{0,12},{4,0},{8,4},{12,8},{1,13},{5,1},{9,5},{13,9},{2,14},{6,2},{... | collective-permute-start | bytes 294920 | tf_op jit(solution)/shard_map/ppermute | solution.py:349
  15.8 1.6 %collective-permute-start.5 = (bf16[32,1536]{1,0:T(8,128)(2,1)S(1)}, bf16[32,1536]{1,0:T(8,128)(2,1)S(1)}, u32[]{:S(2)}, u32[]{:S(2)}) collective-permute-start(bf16[32,1536]{1,0:T(8,128)(2,1)S(1)} %slice.52), channel_id=1, source_target_pairs={{0,4},{4,8},{8,12},{12,0},{1,5},{5,9},{9,13},{13,1},{2,6},{6,10},{... | collective-permute-start | bytes 294920 | tf_op jit(solution)/shard_map/ppermute | solution.py:349
  19.2 3.0 %route.1 = (f32[8,256]{1,0:T(8,128)}, f32[256,128]{1,0:T(8,128)}, f32[256,128]{1,0:T(8,128)}, s32[8,128]{1,0:T(8,128)}) custom-call(s32[2]{0:T(128)} %pad_add_fusion.info, f32[64,16]{1,0:T(8,128)} %copy-done.19, f32[64,16]{1,0:T(8,128)} %copy-done.22, f32[64,16]{1,0:T(8,128)} %copy-done.21, f32[64,16]{1,0:T(8,128)} %copy-done.20), custom_call_target="tpu_custom_call" | custom-call | tf_op jit(solution)/shard_map/route/pallas_call | solution.py:77
  24.5 8.5 %gate_up.5 = (bf16[2,256,512]{2,1,0:T(8,128)(2,1)S(1)}, bf16[2,256,512]{2,1,0:T(8,128)(2,1)S(1)}) custom-call(s32[8,128]{1,0:T(8,128)S(1)} %copy-done.9, bf16[64,1536]{1,0:T(8,128)(2,1)S(1)} %copy-done.3, bf16[64,1536]{1,0:T(8,128)(2,1)S(1)} %collective-permute-done.3.refs_1_, bf16[64,1536]{1,0:T(8,128)(2,1)S(1)} %collective-permute-done.4.refs_2_, ...), custom_call_target="tpu_custom_call" | custom-call | flops 1610612736 | bytes 12582912 | tf_op jit(solution)/shard_map/gate_up/pallas_call | solution.py:157
  33.1 8.5 %gate_up.4 = (bf16[2,256,512]{2,1,0:T(8,128)(2,1)S(1)}, bf16[2,256,512]{2,1,0:T(8,128)(2,1)S(1)}) custom-call(s32[8,128]{1,0:T(8,128)S(1)} %copy-done.9, bf16[64,1536]{1,0:T(8,128)(2,1)S(1)} %copy-done.3, bf16[64,1536]{1,0:T(8,128)(2,1)S(1)} %collective-permute-done.3.refs_1_, bf16[64,1536]{1,0:T(8,128)(2,1)S(1)} %collective-permute-done.4.refs_2_, ...), custom_call_target="tpu_custom_call" | custom-call | flops 1610612736 | bytes 12582912 | tf_op jit(solution)/shard_map/gate_up/pallas_call | solution.py:157
  42.4 1.6 %collective-permute-start.9 = (bf16[1,256,512]{2,1,0:T(8,128)(2,1)S(1)}, bf16[1,256,512]{2,1,0:T(8,128)(2,1)}, u32[]{:S(2)}, u32[]{:S(2)}) collective-permute-start(bf16[1,256,512]{2,1,0:T(8,128)(2,1)S(1)} %slice.68.refs_8_), channel_id=1, source_target_pairs={{0,2},{1,3},{2,0},{3,1},{4,6},{5,7},{6,4},{7,5},{8,10},{9,11},{10,... | collective-permute-start | bytes 786440 | tf_op jit(solution)/shard_map/ppermute | solution.py:22
  43.9 8.5 %gate_up.7 = (bf16[2,256,512]{2,1,0:T(8,128)(2,1)S(1)}, bf16[2,256,512]{2,1,0:T(8,128)(2,1)S(1)}) custom-call(s32[8,128]{1,0:T(8,128)S(1)} %copy-done.10, bf16[64,1536]{1,0:T(8,128)(2,1)S(1)} %copy-done.4, bf16[64,1536]{1,0:T(8,128)(2,1)S(1)} %collective-permute-done.3.refs_1_, bf16[64,1536]{1,0:T(8,128)(2,1)S(1)} %collective-permute-done.4.refs_2_, ...), custom_call_target="tpu_custom_call" | custom-call | flops 1610612736 | bytes 12582912 | tf_op jit(solution)/shard_map/gate_up/pallas_call | solution.py:157
  53.6 1.9 %finish.4.refs_9_.refs_0_ = bf16[1,256,256]{2,1,0:T(8,128)(2,1)} custom-call(f32[1,256,512]{2,1,0:T(8,128)} %slice.55.total, bf16[1,256,512]{2,1,0:T(8,128)(2,1)} %collective-permute-done.9.late), custom_call_target="tpu_custom_call" | custom-call | bytes 1048576 | tf_op jit(solution)/shard_map/finish/pallas_call | solution.py:279
  55.5 8.7 %gate_up.6 = (bf16[2,256,512]{2,1,0:T(8,128)(2,1)S(1)}, bf16[2,256,512]{2,1,0:T(8,128)(2,1)S(1)}) custom-call(s32[8,128]{1,0:T(8,128)S(1)} %copy-done.10, bf16[64,1536]{1,0:T(8,128)(2,1)S(1)} %copy-done.4, bf16[64,1536]{1,0:T(8,128)(2,1)S(1)} %collective-permute-done.3.refs_1_, bf16[64,1536]{1,0:T(8,128)(2,1)S(1)} %collective-permute-done.4.refs_2_, ...), custom_call_target="tpu_custom_call" | custom-call | flops 1610612736 | bytes 12582912 | tf_op jit(solution)/shard_map/gate_up/pallas_call | solution.py:157
  65.2 1.5 %collective-permute-start.13 = (bf16[1,256,256]{2,1,0:T(8,128)(2,1)}, bf16[1,256,256]{2,1,0:T(8,128)(2,1)S(1)}, u32[]{:S(2)}, u32[]{:S(2)}) collective-permute-start(bf16[1,256,256]{2,1,0:T(8,128)(2,1)} %finish.4.refs_9_.refs_0_), channel_id=1, source_target_pairs={{0,2},{1,3},{2,0},{3,1},{4,6},{5,7},{6,4},{7,5},{8,10},{9,11},{10,... | collective-permute-start | bytes 393224 | tf_op jit(solution)/shard_map/ppermute | solution.py:22
  66.7 1.2 convert_add_fusion
  69.2 1.2 collective-permute-start.11
  70.4 6.3 %collective-permute-done.13.refs_2_ = bf16[1,256,256]{2,1,0:T(8,128)(2,1)S(1)} collective-permute-done((bf16[1,256,256]{2,1,0:T(8,128)(2,1)}, bf16[1,256,256]{2,1,0:T(8,128)(2,1)S(1)}, u32[]{:S(2)}, u32[]{:S(2)}) %collective-permute-start.13) | collective-permute-done | bytes 131104 | tf_op jit(solution)/shard_map/ppermute | solution.py:22
  78.2 2.0 %finish.7.refs_0_ = bf16[1,256,256]{2,1,0:T(8,128)(2,1)} custom-call(f32[1,256,512]{2,1,0:T(8,128)} %slice.61.total, bf16[1,256,512]{2,1,0:T(8,128)(2,1)} %copy-done.17), custom_call_target="tpu_custom_call" | custom-call | bytes 1048576 | tf_op jit(solution)/shard_map/finish/pallas_call | solution.py:279
  80.7 1.9 %slice.59.total = f32[1,256,512]{2,1,0:T(8,128)} slice(f32[2,256,512]{2,1,0:T(8,128)} %copy-done.15), slice={[0:1], [0:256], [0:512]} | slice | bytes 1048576 | tf_op jit(solution)/shard_map/slice | solution.py:273
  83.3 1.9 %finish.6.refs_0_ = bf16[1,256,256]{2,1,0:T(8,128)(2,1)} custom-call(f32[1,256,512]{2,1,0:T(8,128)} %slice.59.total, bf16[1,256,512]{2,1,0:T(8,128)(2,1)} %copy-done.18), custom_call_target="tpu_custom_call" | custom-call | bytes 1048576 | tf_op jit(solution)/shard_map/finish/pallas_call | solution.py:279
  85.1 1.5 %collective-permute-start.21 = (bf16[1,256,256]{2,1,0:T(8,128)(2,1)}, bf16[1,256,256]{2,1,0:T(8,128)(2,1)S(1)}, u32[]{:S(2)}, u32[]{:S(2)}) collective-permute-start(bf16[1,256,256]{2,1,0:T(8,128)(2,1)} %finish.6.refs_0_), channel_id=1, source_target_pairs={{0,2},{1,3},{2,0},{3,1},{4,6},{5,7},{6,4},{7,5},{8,10},{9,11},{10,... | collective-permute-start | bytes 393224 | tf_op jit(solution)/shard_map/ppermute | solution.py:22
  86.6 5.4 %down.4.refs_0_.refs_7_ = f32[256,1536]{1,0:T(8,128)S(1)} custom-call(s32[8,128]{1,0:T(8,128)S(1)} %copy-done.10, bf16[1,256,256]{2,1,0:T(8,128)(2,1)} %finish.4.refs_9_.refs_0_, bf16[1,256,256]{2,1,0:T(8,128)(2,1)S(1)} %collective-permute-done.12.refs_1_, bf16[1,256,256]{2,1,0:T(8,128)(2,1)S(1)} %collective-permute-done.13.refs_2_, ...), custom_call_target="tpu_custom_call" | custom-call | flops 1006632960 | bytes 9437184 | tf_op jit(solution)/shard_map/down/pallas_call | solution.py:232
  92.0 1.2 copy-done
  94.8 1.9 %finish.5.refs_8_.refs_0_ = bf16[1,256,256]{2,1,0:T(8,128)(2,1)} custom-call(f32[1,256,512]{2,1,0:T(8,128)} %slice.57.total, bf16[1,256,512]{2,1,0:T(8,128)(2,1)} %copy-done.16, f32[256,1536]{1,0:T(8,128)} %copy-done), custom_call_target="tpu_custom_call" | custom-call | bytes 1048576 | tf_op jit(solution)/shard_map/finish/pallas_call | solution.py:279
  98.2 4.0 %collective-permute-done.16.refs_2_ = bf16[1,256,256]{2,1,0:T(8,128)(2,1)S(1)} collective-permute-done((bf16[1,256,256]{2,1,0:T(8,128)(2,1)}, bf16[1,256,256]{2,1,0:T(8,128)(2,1)S(1)}, u32[]{:S(2)}, u32[]{:S(2)}) %collective-permute-start.16) | collective-permute-done | bytes 131104 | tf_op jit(solution)/shard_map/ppermute | solution.py:22
  102.2 1.4 copy-done.1
  104.5 5.2 %down.5.refs_7_ = f32[256,1536]{1,0:T(8,128)S(1)} custom-call(s32[8,128]{1,0:T(8,128)S(1)} %copy-done.10, bf16[1,256,256]{2,1,0:T(8,128)(2,1)S(1)} %copy-done.7, bf16[1,256,256]{2,1,0:T(8,128)(2,1)S(1)} %collective-permute-done.24.refs_1_, bf16[1,256,256]{2,1,0:T(8,128)(2,1)S(1)} %collective-permute-done.25.refs_2_, ...), custom_call_target="tpu_custom_call" | custom-call | flops 1006632960 | bytes 9437184 | tf_op jit(solution)/shard_map/down/pallas_call | solution.py:232
  109.7 5.2 %down.6.refs_7_ = f32[256,1536]{1,0:T(8,128)S(1)} custom-call(s32[8,128]{1,0:T(8,128)S(1)} %copy-done.10, bf16[1,256,256]{2,1,0:T(8,128)(2,1)S(1)} %copy-done.8, bf16[1,256,256]{2,1,0:T(8,128)(2,1)S(1)} %collective-permute-done.20.refs_1_, bf16[1,256,256]{2,1,0:T(8,128)(2,1)S(1)} %collective-permute-done.21.refs_2_, ...), custom_call_target="tpu_custom_call" | custom-call | flops 1006632960 | bytes 9437184 | tf_op jit(solution)/shard_map/down/pallas_call | solution.py:232
  114.9 5.1 %down.7 = (bf16[64,1536]{1,0:T(8,128)(2,1)S(1)}, bf16[64,1536]{1,0:T(8,128)(2,1)S(1)}, bf16[64,1536]{1,0:T(8,128)(2,1)S(1)}, bf16[64,1536]{1,0:T(8,128)(2,1)S(1)}) custom-call(s32[8,128]{1,0:T(8,128)S(1)} %copy-done.10, bf16[1,256,256]{2,1,0:T(8,128)(2,1)S(1)} %copy-done.2, bf16[1,256,256]{2,1,0:T(8,128)(2,1)S(1)} %collective-permute-done.15.refs_1_, ...), custom_call_target="tpu_custom_call" | custom-call | flops 1006632960 | bytes 9437184 | tf_op jit(solution)/shard_map/down/pallas_call | solution.py:232
  120.1 2.6 %collective-permute-start.27 = (bf16[64,1536]{1,0:T(8,128)(2,1)S(1)}, bf16[64,1536]{1,0:T(8,128)(2,1)S(1)}, u32[]{:S(2)}, u32[]{:S(2)}) collective-permute-start(bf16[64,1536]{1,0:T(8,128)(2,1)S(1)} %get-tuple-element.34), channel_id=1, source_target_pairs={{0,12},{4,0},{8,4},{12,8},{1,13},{5,1},{9,5},{13,9},{2,14},{6,2},{... | collective-permute-start | bytes 589832 | tf_op jit(solution)/shard_map/ppermute | solution.py:358
  123.3 4.6 %collective-permute-done.27 = bf16[64,1536]{1,0:T(8,128)(2,1)S(1)} collective-permute-done((bf16[64,1536]{1,0:T(8,128)(2,1)S(1)}, bf16[64,1536]{1,0:T(8,128)(2,1)S(1)}, u32[]{:S(2)}, u32[]{:S(2)}) %collective-permute-start.27) | collective-permute-done | bytes 196640 | tf_op jit(solution)/shard_map/ppermute | solution.py:358
  128.0 4.8 %collective-permute-done.28 = bf16[64,1536]{1,0:T(8,128)(2,1)S(1)} collective-permute-done((bf16[64,1536]{1,0:T(8,128)(2,1)S(1)}, bf16[64,1536]{1,0:T(8,128)(2,1)S(1)}, u32[]{:S(2)}, u32[]{:S(2)}) %collective-permute-start.28) | collective-permute-done | bytes 196640 | tf_op jit(solution)/shard_map/ppermute | solution.py:358
  132.8 7.6 %collective-permute-done.29 = bf16[64,1536]{1,0:T(8,128)(2,1)S(1)} collective-permute-done((bf16[64,1536]{1,0:T(8,128)(2,1)S(1)}, bf16[64,1536]{1,0:T(8,128)(2,1)S(1)}, u32[]{:S(2)}, u32[]{:S(2)}) %collective-permute-start.29) | collective-permute-done | bytes 196640 | tf_op jit(solution)/shard_map/ppermute | solution.py:358
  (106 shorter events, 19.5 us)
Async XLA Ops:
  0.0 11.0 %collective-permute-start.4 = (bf16[64,1536]{1,0:T(8,128)(2,1)}, bf16[64,1536]{1,0:T(8,128)(2,1)S(1)}, u32[]{:S(2)}, u32[]{:S(2)}) collective-permute-start(bf16[64,1536]{1,0:T(8,128)(2,1)} %refs_0_.7), channel_id=1, source_target_pairs={{0,12},{4,0},{8,4},{12,8},{1,13},{5,1},{9,5},{13,9},{2,14},{6,2},{... | collective-permute-start | bytes 589832 | tf_op jit(solution)/shard_map/ppermute | solution.py:345
  5.0 10.7 %collective-permute-start.3 = (bf16[64,1536]{1,0:T(8,128)(2,1)}, bf16[64,1536]{1,0:T(8,128)(2,1)S(1)}, u32[]{:S(2)}, u32[]{:S(2)}) collective-permute-start(bf16[64,1536]{1,0:T(8,128)(2,1)} %refs_0_.7), channel_id=1, source_target_pairs={{0,4},{4,8},{8,12},{12,0},{1,5},{5,9},{9,13},{13,1},{2,6},{6,10},{... | collective-permute-start | bytes 589832 | tf_op jit(solution)/shard_map/ppermute | solution.py:345
  6.5 11.5 %collective-permute-start.2 = (f32[64,16]{1,0:T(8,128)S(1)}, f32[64,16]{1,0:T(8,128)S(1)}, u32[]{:S(2)}, u32[]{:S(2)}) collective-permute-start(f32[64,16]{1,0:T(8,128)S(1)} %copy.12.refs_0_), channel_id=1, source_target_pairs={{0,8},{4,12},{8,0},{12,4},{1,9},{5,13},{9,1},{13,5},{2,10},{6,14},... | collective-permute-start | bytes 12296 | tf_op jit(solution)/shard_map/ppermute | solution.py:310
  7.6 10.4 %collective-permute-start.1 = (f32[64,16]{1,0:T(8,128)S(1)}, f32[64,16]{1,0:T(8,128)S(1)}, u32[]{:S(2)}, u32[]{:S(2)}) collective-permute-start(f32[64,16]{1,0:T(8,128)S(1)} %copy.12.refs_0_), channel_id=1, source_target_pairs={{0,12},{4,0},{8,4},{12,8},{1,13},{5,1},{9,5},{13,9},{2,14},{6,2},{... | collective-permute-start | bytes 12296 | tf_op jit(solution)/shard_map/ppermute | solution.py:310
  10.5 7.5 %collective-permute-start = (f32[64,16]{1,0:T(8,128)S(1)}, f32[64,16]{1,0:T(8,128)S(1)}, u32[]{:S(2)}, u32[]{:S(2)}) collective-permute-start(f32[64,16]{1,0:T(8,128)S(1)} %copy.12.refs_0_), channel_id=1, source_target_pairs={{0,4},{4,8},{8,12},{12,0},{1,5},{5,9},{9,13},{13,1},{2,6},{6,10},{... | collective-permute-start | bytes 12296 | tf_op jit(solution)/shard_map/ppermute | solution.py:310
  11.0 11.2 %collective-permute-start.6 = (bf16[32,1536]{1,0:T(8,128)(2,1)S(1)}, bf16[32,1536]{1,0:T(8,128)(2,1)S(1)}, u32[]{:S(2)}, u32[]{:S(2)}) collective-permute-start(bf16[32,1536]{1,0:T(8,128)(2,1)S(1)} %slice.53), channel_id=1, source_target_pairs={{0,12},{4,0},{8,4},{12,8},{1,13},{5,1},{9,5},{13,9},{2,14},{6,2},{... | collective-permute-start | bytes 294920 | tf_op jit(solution)/shard_map/ppermute | solution.py:349
  15.8 6.5 %collective-permute-start.5 = (bf16[32,1536]{1,0:T(8,128)(2,1)S(1)}, bf16[32,1536]{1,0:T(8,128)(2,1)S(1)}, u32[]{:S(2)}, u32[]{:S(2)}) collective-permute-start(bf16[32,1536]{1,0:T(8,128)(2,1)S(1)} %slice.52), channel_id=1, source_target_pairs={{0,4},{4,8},{8,12},{12,0},{1,5},{5,9},{9,13},{13,1},{2,6},{6,10},{... | collective-permute-start | bytes 294920 | tf_op jit(solution)/shard_map/ppermute | solution.py:349
  33.0 9.1 %collective-permute-start.8 = (bf16[2,256,512]{2,1,0:T(8,128)(2,1)S(1)}, bf16[2,256,512]{2,1,0:T(8,128)(2,1)S(1)}, u32[]{:S(2)}, u32[]{:S(2)}) collective-permute-start(bf16[2,256,512]{2,1,0:T(8,128)(2,1)S(1)} %get-tuple-element.26), channel_id=1, source_target_pairs={{0,1},{1,0},{2,3},{3,2},{4,5},{5,4},{6,7},{7,6},{8,9},{9,8},{10,11... | collective-permute-start | bytes 1572872 | tf_op jit(solution)/shard_map/ppermute | solution.py:22
  41.6 10.9 %collective-permute-start.7 = (bf16[2,256,512]{2,1,0:T(8,128)(2,1)S(1)}, bf16[2,256,512]{2,1,0:T(8,128)(2,1)S(1)}, u32[]{:S(2)}, u32[]{:S(2)}) collective-permute-start(bf16[2,256,512]{2,1,0:T(8,128)(2,1)S(1)} %get-tuple-element.24), channel_id=1, source_target_pairs={{0,1},{1,0},{2,3},{3,2},{4,5},{5,4},{6,7},{7,6},{8,9},{9,8},{10,11... | collective-permute-start | bytes 1572872 | tf_op jit(solution)/shard_map/ppermute | solution.py:22
  42.4 11.2 %collective-permute-start.9 = (bf16[1,256,512]{2,1,0:T(8,128)(2,1)S(1)}, bf16[1,256,512]{2,1,0:T(8,128)(2,1)}, u32[]{:S(2)}, u32[]{:S(2)}) collective-permute-start(bf16[1,256,512]{2,1,0:T(8,128)(2,1)S(1)} %slice.68.refs_8_), channel_id=1, source_target_pairs={{0,2},{1,3},{2,0},{3,1},{4,6},{5,7},{6,4},{7,5},{8,10},{9,11},{10,... | collective-permute-start | bytes 786440 | tf_op jit(solution)/shard_map/ppermute | solution.py:22
  52.4 14.3 %collective-permute-start.18 = (bf16[2,256,512]{2,1,0:T(8,128)(2,1)S(1)}, bf16[2,256,512]{2,1,0:T(8,128)(2,1)}, u32[]{:S(2)}, u32[]{:S(2)}) collective-permute-start(bf16[2,256,512]{2,1,0:T(8,128)(2,1)S(1)} %get-tuple-element.32), channel_id=1, source_target_pairs={{0,1},{1,0},{2,3},{3,2},{4,5},{5,4},{6,7},{7,6},{8,9},{9,8},{10,11... | collective-permute-start | bytes 1572872 | tf_op jit(solution)/shard_map/ppermute | solution.py:22
  55.5 31.2 %copy-start.5 = (f32[256,128]{1,0:T(8,128)S(1)}, f32[256,128]{1,0:T(8,128)}, u32[]{:S(2)}) copy-start(f32[256,128]{1,0:T(8,128)} %get-tuple-element.29.refs_4_) | copy-start | bytes 393220
  55.5 31.2 %copy-start.6 = (f32[256,128]{1,0:T(8,128)S(1)}, f32[256,128]{1,0:T(8,128)}, u32[]{:S(2)}) copy-start(f32[256,128]{1,0:T(8,128)} %get-tuple-element.30.refs_5_) | copy-start | bytes 393220
  64.1 4.5 %collective-permute-start.10 = (bf16[2,256,512]{2,1,0:T(8,128)(2,1)S(1)}, bf16[2,256,512]{2,1,0:T(8,128)(2,1)S(1)}, u32[]{:S(2)}, u32[]{:S(2)}) collective-permute-start(bf16[2,256,512]{2,1,0:T(8,128)(2,1)S(1)} %get-tuple-element.28), channel_id=1, source_target_pairs={{0,1},{1,0},{2,3},{3,2},{4,5},{5,4},{6,7},{7,6},{8,9},{9,8},{10,11... | collective-permute-start | bytes 1572872 | tf_op jit(solution)/shard_map/ppermute | solution.py:22
  64.7 12.8 %collective-permute-start.23 = (bf16[1,256,512]{2,1,0:T(8,128)(2,1)S(1)}, bf16[1,256,512]{2,1,0:T(8,128)(2,1)S(1)}, u32[]{:S(2)}, u32[]{:S(2)}) collective-permute-start(bf16[1,256,512]{2,1,0:T(8,128)(2,1)S(1)} %slice.69.refs_8_), channel_id=1, source_target_pairs={{0,2},{1,3},{2,0},{3,1},{4,6},{5,7},{6,4},{7,5},{8,10},{9,11},{10,... | collective-permute-start | bytes 786440 | tf_op jit(solution)/shard_map/ppermute | solution.py:22
  65.2 11.4 %collective-permute-start.13 = (bf16[1,256,256]{2,1,0:T(8,128)(2,1)}, bf16[1,256,256]{2,1,0:T(8,128)(2,1)S(1)}, u32[]{:S(2)}, u32[]{:S(2)}) collective-permute-start(bf16[1,256,256]{2,1,0:T(8,128)(2,1)} %finish.4.refs_9_.refs_0_), channel_id=1, source_target_pairs={{0,2},{1,3},{2,0},{3,1},{4,6},{5,7},{6,4},{7,5},{8,10},{9,11},{10,... | collective-permute-start | bytes 393224 | tf_op jit(solution)/shard_map/ppermute | solution.py:22
  68.0 14.6 %collective-permute-start.19 = (bf16[1,256,512]{2,1,0:T(8,128)(2,1)S(1)}, bf16[1,256,512]{2,1,0:T(8,128)(2,1)S(1)}, u32[]{:S(2)}, u32[]{:S(2)}) collective-permute-start(bf16[1,256,512]{2,1,0:T(8,128)(2,1)S(1)} %slice.66), channel_id=1, source_target_pairs={{0,2},{1,3},{2,0},{3,1},{4,6},{5,7},{6,4},{7,5},{8,10},{9,11},{10,... | collective-permute-start | bytes 786440 | tf_op jit(solution)/shard_map/ppermute | solution.py:22
  69.2 24.9 %collective-permute-start.11 = (bf16[1,256,512]{2,1,0:T(8,128)(2,1)S(1)}, bf16[1,256,512]{2,1,0:T(8,128)(2,1)S(1)}, u32[]{:S(2)}, u32[]{:S(2)}) collective-permute-start(bf16[1,256,512]{2,1,0:T(8,128)(2,1)S(1)} %slice.67.refs_7_), channel_id=1, source_target_pairs={{0,2},{1,3},{2,0},{3,1},{4,6},{5,7},{6,4},{7,5},{8,10},{9,11},{10,... | collective-permute-start | bytes 786440 | tf_op jit(solution)/shard_map/ppermute | solution.py:22
  70.3 14.8 %collective-permute-start.12 = (bf16[1,256,256]{2,1,0:T(8,128)(2,1)}, bf16[1,256,256]{2,1,0:T(8,128)(2,1)S(1)}, u32[]{:S(2)}, u32[]{:S(2)}) collective-permute-start(bf16[1,256,256]{2,1,0:T(8,128)(2,1)} %finish.4.refs_9_.refs_0_), channel_id=1, source_target_pairs={{0,1},{1,0},{2,3},{3,2},{4,5},{5,4},{6,7},{7,6},{8,9},{9,8},{10,11... | collective-permute-start | bytes 393224 | tf_op jit(solution)/shard_map/ppermute | solution.py:22
  76.6 10.0 %collective-permute-start.14 = (bf16[1,256,256]{2,1,0:T(8,128)(2,1)S(1)}, bf16[1,256,256]{2,1,0:T(8,128)(2,1)S(1)}, u32[]{:S(2)}, u32[]{:S(2)}) collective-permute-start(bf16[1,256,256]{2,1,0:T(8,128)(2,1)S(1)} %collective-permute-done.13.refs_2_), channel_id=1, source_target_pairs={{0,1},{1,0},{2,3},{3,2},{4,5},{5,4},{6,7},{7,6},{8,9},{9,8},{10,11... | collective-permute-start | bytes 393224 | tf_op jit(solution)/shard_map/ppermute | solution.py:22
  80.2 17.0 %collective-permute-start.25 = (bf16[1,256,256]{2,1,0:T(8,128)(2,1)}, bf16[1,256,256]{2,1,0:T(8,128)(2,1)S(1)}, u32[]{:S(2)}, u32[]{:S(2)}) collective-permute-start(bf16[1,256,256]{2,1,0:T(8,128)(2,1)} %finish.7.refs_0_), channel_id=1, source_target_pairs={{0,2},{1,3},{2,0},{3,1},{4,6},{5,7},{6,4},{7,5},{8,10},{9,11},{10,... | collective-permute-start | bytes 393224 | tf_op jit(solution)/shard_map/ppermute | solution.py:22
  82.6 15.2 %collective-permute-start.24 = (bf16[1,256,256]{2,1,0:T(8,128)(2,1)}, bf16[1,256,256]{2,1,0:T(8,128)(2,1)S(1)}, u32[]{:S(2)}, u32[]{:S(2)}) collective-permute-start(bf16[1,256,256]{2,1,0:T(8,128)(2,1)} %finish.7.refs_0_), channel_id=1, source_target_pairs={{0,1},{1,0},{2,3},{3,2},{4,5},{5,4},{6,7},{7,6},{8,9},{9,8},{10,11... | collective-permute-start | bytes 393224 | tf_op jit(solution)/shard_map/ppermute | solution.py:22
  85.1 12.6 %collective-permute-start.21 = (bf16[1,256,256]{2,1,0:T(8,128)(2,1)}, bf16[1,256,256]{2,1,0:T(8,128)(2,1)S(1)}, u32[]{:S(2)}, u32[]{:S(2)}) collective-permute-start(bf16[1,256,256]{2,1,0:T(8,128)(2,1)} %finish.6.refs_0_), channel_id=1, source_target_pairs={{0,2},{1,3},{2,0},{3,1},{4,6},{5,7},{6,4},{7,5},{8,10},{9,11},{10,... | collective-permute-start | bytes 393224 | tf_op jit(solution)/shard_map/ppermute | solution.py:22
  96.6 5.6 %collective-permute-start.16 = (bf16[1,256,256]{2,1,0:T(8,128)(2,1)}, bf16[1,256,256]{2,1,0:T(8,128)(2,1)S(1)}, u32[]{:S(2)}, u32[]{:S(2)}) collective-permute-start(bf16[1,256,256]{2,1,0:T(8,128)(2,1)} %finish.5.refs_8_.refs_0_), channel_id=1, source_target_pairs={{0,2},{1,3},{2,0},{3,1},{4,6},{5,7},{6,4},{7,5},{8,10},{9,11},{10,... | collective-permute-start | bytes 393224 | tf_op jit(solution)/shard_map/ppermute | solution.py:22
  97.2 5.0 %collective-permute-start.26 = (bf16[1,256,256]{2,1,0:T(8,128)(2,1)S(1)}, bf16[1,256,256]{2,1,0:T(8,128)(2,1)S(1)}, u32[]{:S(2)}, u32[]{:S(2)}) collective-permute-start(bf16[1,256,256]{2,1,0:T(8,128)(2,1)S(1)} %collective-permute-done.25.refs_2_), channel_id=1, source_target_pairs={{0,1},{1,0},{2,3},{3,2},{4,5},{5,4},{6,7},{7,6},{8,9},{9,8},{10,11... | collective-permute-start | bytes 393224 | tf_op jit(solution)/shard_map/ppermute | solution.py:22
  97.2 12.5 %collective-permute-start.20 = (bf16[1,256,256]{2,1,0:T(8,128)(2,1)S(1)}, bf16[1,256,256]{2,1,0:T(8,128)(2,1)S(1)}, u32[]{:S(2)}, u32[]{:S(2)}) collective-permute-start(bf16[1,256,256]{2,1,0:T(8,128)(2,1)S(1)} %copy-done.8), channel_id=1, source_target_pairs={{0,1},{1,0},{2,3},{3,2},{4,5},{5,4},{6,7},{7,6},{8,9},{9,8},{10,11... | collective-permute-start | bytes 393224 | tf_op jit(solution)/shard_map/ppermute | solution.py:22
  97.7 12.0 %collective-permute-start.22 = (bf16[1,256,256]{2,1,0:T(8,128)(2,1)S(1)}, bf16[1,256,256]{2,1,0:T(8,128)(2,1)S(1)}, u32[]{:S(2)}, u32[]{:S(2)}) collective-permute-start(bf16[1,256,256]{2,1,0:T(8,128)(2,1)S(1)} %collective-permute-done.21.refs_2_), channel_id=1, source_target_pairs={{0,1},{1,0},{2,3},{3,2},{4,5},{5,4},{6,7},{7,6},{8,9},{9,8},{10,11... | collective-permute-start | bytes 393224 | tf_op jit(solution)/shard_map/ppermute | solution.py:22
  97.8 17.1 %collective-permute-start.15 = (bf16[1,256,256]{2,1,0:T(8,128)(2,1)}, bf16[1,256,256]{2,1,0:T(8,128)(2,1)S(1)}, u32[]{:S(2)}, u32[]{:S(2)}) collective-permute-start(bf16[1,256,256]{2,1,0:T(8,128)(2,1)} %finish.5.refs_8_.refs_0_), channel_id=1, source_target_pairs={{0,1},{1,0},{2,3},{3,2},{4,5},{5,4},{6,7},{7,6},{8,9},{9,8},{10,11... | collective-permute-start | bytes 393224 | tf_op jit(solution)/shard_map/ppermute | solution.py:22
  102.2 12.7 %collective-permute-start.17 = (bf16[1,256,256]{2,1,0:T(8,128)(2,1)S(1)}, bf16[1,256,256]{2,1,0:T(8,128)(2,1)S(1)}, u32[]{:S(2)}, u32[]{:S(2)}) collective-permute-start(bf16[1,256,256]{2,1,0:T(8,128)(2,1)S(1)} %collective-permute-done.16.refs_2_), channel_id=1, source_target_pairs={{0,1},{1,0},{2,3},{3,2},{4,5},{5,4},{6,7},{7,6},{8,9},{9,8},{10,11... | collective-permute-start | bytes 393224 | tf_op jit(solution)/shard_map/ppermute | solution.py:22
  120.1 7.9 %collective-permute-start.27 = (bf16[64,1536]{1,0:T(8,128)(2,1)S(1)}, bf16[64,1536]{1,0:T(8,128)(2,1)S(1)}, u32[]{:S(2)}, u32[]{:S(2)}) collective-permute-start(bf16[64,1536]{1,0:T(8,128)(2,1)S(1)} %get-tuple-element.34), channel_id=1, source_target_pairs={{0,12},{4,0},{8,4},{12,8},{1,13},{5,1},{9,5},{13,9},{2,14},{6,2},{... | collective-permute-start | bytes 589832 | tf_op jit(solution)/shard_map/ppermute | solution.py:358
  122.7 10.1 %collective-permute-start.28 = (bf16[64,1536]{1,0:T(8,128)(2,1)S(1)}, bf16[64,1536]{1,0:T(8,128)(2,1)S(1)}, u32[]{:S(2)}, u32[]{:S(2)}) collective-permute-start(bf16[64,1536]{1,0:T(8,128)(2,1)S(1)} %get-tuple-element.35), channel_id=1, source_target_pairs={{0,4},{4,8},{8,12},{12,0},{1,5},{5,9},{9,13},{13,1},{2,6},{6,10},{... | collective-permute-start | bytes 589832 | tf_op jit(solution)/shard_map/ppermute | solution.py:358
  122.7 17.6 %collective-permute-start.29 = (bf16[64,1536]{1,0:T(8,128)(2,1)S(1)}, bf16[64,1536]{1,0:T(8,128)(2,1)S(1)}, u32[]{:S(2)}, u32[]{:S(2)}) collective-permute-start(bf16[64,1536]{1,0:T(8,128)(2,1)S(1)} %get-tuple-element.36), channel_id=1, source_target_pairs={{0,8},{4,12},{8,0},{12,4},{1,9},{5,13},{9,1},{13,5},{2,10},{6,14},... | collective-permute-start | bytes 589832 | tf_op jit(solution)/shard_map/ppermute | solution.py:358
  (21 other events, 112.5 us)
where the time goes:
time: 142 us; the launch traced here: 141 us
  Pallas kernels  65.5 us (46%)
  starting transfers between devices  28.7 us (20%)
  waiting for transfers between devices  28.2 us (20%)
  local copies, waits for them, and re-layouts  13.9 us (10%)
  other arithmetic  4.48 us (3%)
    pallas_call x4, Pallas kernels, gate_up(): pl.pallas_call(functools.partial(gate_up_body, n, chunk, n_dp, most, len(...  34.1 us
    pallas_call x4, Pallas kernels, down(): pl.pallas_call(functools.partial(down_body, n_dp, n_out, chunk, first, mo...  20.9 us
    ppermute x3, waiting for transfers between devices, returned(): there = lax.ppermute(partial, axis, [(i, (i + k) % n) for i in range(n)])  17 us
    ppermute x20, starting transfers between devices, flip(): lax.ppermute(x, axis, [(i, i ^ k) for i in range(lax.axis_size(axis))])  10.4 us
    ppermute x20, waiting for transfers between devices, flip(): lax.ppermute(x, axis, [(i, i ^ k) for i in range(lax.axis_size(axis))])  10.3 us
    unnamed x46, local copies, waits for them, and re-layouts  9.26 us
    pallas_call x4, Pallas kernels, finish(): pl.pallas_call(finish_body, out_shape=jax.ShapeDtypeStruct(total.shape[:2...  7.59 us
    ppermute x1, starting transfers between devices, gathered(): lax.ppermute(above, axis, down_)  5.05 us
  transfers between devices with their start and end apart: 30, of which 6 were waited for; matrix products, arithmetic and copies ran while one was open for 6% of the time, Pallas kernels for 37%

commit v1 on v0

--- a/solution.py
+++ b/solution.py
@@ -101,6 +101,11 @@
     out[at[:-2] + (slice(most, rows), at[-1])] = right[most - head :]
 
 
+def turned_dot(w, x):
+    turned = lax.dot_general(w, x, (((0,), (1,)), ((), ())), preferred_element_type=jnp.float32)
+    return jnp.transpose(turned).astype(jnp.bfloat16)
+
+
 def gate_up_body(n, chunk, n_dp, most, after, sched, *refs):
     tokens, (rank_t, w_gate, w_up), refs = refs[:n], refs[n : n + 3], refs[n + 3 + after :]
     send, keep, feed, rows, held, feed_sem, held_sem = refs
@@ -139,14 +144,10 @@
                 copy.start()
         for l in range(n_dp):
             units = pl.ds(pl.multiple_of((l ^ sched[4, 0]) * width, width), width)
-            left = jnp.dot(rows[:most], held[first, :, units], preferred_element_type=jnp.float32)
-            right = None
-            if most < count:
-                right = jnp.dot(
-                    rows[count - most :], held[first + 1, :, units], preferred_element_type=jnp.float32
-                ).astype(jnp.bfloat16)
+            left = turned_dot(held[first, :, units], rows[:most])
+            right = turned_dot(held[first + 1, :, units], rows[count - most :]) if most < count else None
             to = (l // 2, slice(None), slice(m * width, (m + 1) * width))
-            put(send if l % 2 else keep, to, left.astype(jnp.bfloat16), right, count, split)
+            put(send if l % 2 else keep, to, left, right, count, split)
 
 
 def gate_up(tokens, rank_t, sched, w_gate, w_up, chunk, rows, most, n_dp, after):
@@ -166,7 +167,7 @@
             pltpu.SemaphoreType.DMA((n,)),
             pltpu.SemaphoreType.DMA((mats,)),
         ],
-        compiler_params=pltpu.CompilerParams(vmem_limit_bytes=48 << 20),
+        compiler_params=pltpu.CompilerParams(vmem_limit_bytes=40 << 20),
         cost_estimate=pl.CostEstimate(
             flops=2 * mats * most * local * hidden,
             bytes_accessed=2 * mats * local * hidden,
@@ -206,12 +207,9 @@
     block = 512 if local % 512 == 0 else 256 if local % 256 == 0 else local
     for i in range(local // block):
         cols = slice(i * block, (i + 1) * block)
-        left = jnp.dot(hidden[:most], held[0, :, cols], preferred_element_type=jnp.float32)
-        right = None
-        if most < rows:
-            right = jnp.dot(hidden[rows - most :], held[1, :, cols], preferred_element_type=jnp.float32)
-            right = right.astype(jnp.bfloat16)
-        put(out, (slice(None), cols), left.astype(jnp.bfloat16), right, rows, split)
+        left = turned_dot(held[0, :, cols], hidden[:most])
+        right = turned_dot(held[1, :, cols], hidden[rows - most :]) if most < rows else None
+        put(out, (slice(None), cols), left, right, rows, split)
         total = jnp.dot(mix[...], out[:, cols], preferred_element_type=jnp.float32)
         if not first:
             total = total + before[:, cols]
@@ -245,7 +243,7 @@
             pltpu.VMEM((mats, hidden, local), jnp.bfloat16),
             pltpu.SemaphoreType.DMA((mats,)),
         ],
-        compiler_params=pltpu.CompilerParams(vmem_limit_bytes=48 << 20),
+        compiler_params=pltpu.CompilerParams(vmem_limit_bytes=40 << 20),
         cost_estimate=pl.CostEstimate(
             flops=2 * local * (2 * most * hidden + rows * tokens),
             bytes_accessed=2 * mats * hidden * local + 8 * tokens * local,
@@ -254,13 +252,6 @@
         name="down",
     )(sched, *parts, rank, wt, w_down, *([] if first else [total]), *after)
     return outs if last else outs[0]
-
-
-def finish_body(total, late, *refs):
-    gate_up = total[...] + late[...].astype(jnp.float32)
-    width = gate_up.shape[2] // 2
-    gate, up = gate_up[:, :, :width], gate_up[:, :, width:]
-    refs[-1][...] = (gate / (1.0 + jnp.exp(-gate)) * up).astype(jnp.bfloat16)
 
 
 def partial_sums(send, keep, n_dp):
@@ -276,14 +267,11 @@
 
 
 def finish(total, late, after):
-    return pl.pallas_call(
-        finish_body,
-        out_shape=jax.ShapeDtypeStruct(total.shape[:2] + (total.shape[2] // 2,), jnp.bfloat16),
-        in_specs=[VMEM] * 2 + [HERE] * len(after),
-        out_specs=VMEM,
-        cost_estimate=pl.CostEstimate(flops=0, bytes_accessed=1 << 20, transcendentals=total.size // 2),
-        name="finish",
-    )(total, late, *after)
+    if after:
+        late, *_ = lax.optimization_barrier((late, *after))
+    gate_up = total + late.astype(jnp.float32)
+    width = gate_up.shape[2] // 2
+    return (jax.nn.silu(gate_up[:, :, :width]) * gate_up[:, :, width:]).astype(jnp.bfloat16)
 
 
 def all_parts(share, n_dp):

time: 142 us -> 133 us (0.937)
  local copies, waits for them, and re-layouts: 13.9 us -> 3.75 us
  Pallas kernels: 65.5 us -> 67.6 us
    pallas_call x4 -> x0, Pallas kernels: 7.59 us -> none  [finish(): pl.pallas_call(finish_body, out_shape=jax.ShapeDtypeStruct(total.shape[:2...]
    unnamed x46 -> x20, local copies, waits for them, and re-layouts: 9.26 us -> 3.51 us
    pallas_call x4, Pallas kernels: 34.1 us -> 39.5 us  [gate_up(): pl.pallas_call(functools.partial(gate_up_body, n, chunk, n_dp, most, len(...]
    slice x4 -> x0, local copies, waits for them, and re-layouts: 4.4 us -> none  [partial_sums(): total = total[0::2]]
    pallas_call x4, Pallas kernels: 20.9 us -> 25.1 us  [down(): pl.pallas_call(functools.partial(down_body, n_dp, n_out, chunk, first, mo...]
  transfers between devices with their start and end apart: 30 -> 30, of which waited for: 6 -> 8; matrix products, arithmetic and copies ran while one was open for 6% -> 3% of each run, Pallas kernels for 37% -> 39%
where the time goes in v1:
time: 133 us
  Pallas kernels  67.6 us (51%)
  waiting for transfers between devices  29.3 us (22%)
  starting transfers between devices  27.7 us (21%)
  other arithmetic  4.02 us (3%)
  local copies, waits for them, and re-layouts  3.75 us (3%)
    pallas_call x4, Pallas kernels, gate_up(): pl.pallas_call(functools.partial(gate_up_body, n, chunk, n_dp, most, len(...  39.5 us
    pallas_call x4, Pallas kernels, down(): pl.pallas_call(functools.partial(down_body, n_dp, n_out, chunk, first, mo...  25.1 us
    ppermute x3, waiting for transfers between devices, returned(): there = lax.ppermute(partial, axis, [(i, (i + k) % n) for i in range(n)])  17 us
    ppermute x20, waiting for transfers between devices, flip(): lax.ppermute(x, axis, [(i, i ^ k) for i in range(lax.axis_size(axis))])  11.4 us
    ppermute x20, starting transfers between devices, flip(): lax.ppermute(x, axis, [(i, i ^ k) for i in range(lax.axis_size(axis))])  9.52 us
    ppermute x1, starting transfers between devices, gathered(): lax.ppermute(above, axis, down_)  5.05 us
    ppermute x3, starting transfers between devices, on_device(): lax.ppermute(meta, 'expert', [(i, (i - k) % n_owner) for i in range(n_own...  4.45 us
    ppermute x1, starting transfers between devices, gathered(): lax.ppermute(above[half:], axis, down_)  3.93 us
  transfers between devices with their start and end apart: 30, of which 8 were waited for; matrix products, arithmetic and copies ran while one was open for 3% of the time, Pallas kernels for 39%

profile of v1, /device:TPU:0, one launch (start us, length us, event | category | flops | bytes accessed | tf_op | source)
XLA Modules:
  0.0 132.7 jit_solution(3829405067623915001)
XLA Ops:
  0.0 5.0 %collective-permute-start.4 = (bf16[64,1536]{1,0:T(8,128)(2,1)}, bf16[64,1536]{1,0:T(8,128)(2,1)S(1)}, u32[]{:S(2)}, u32[]{:S(2)}) collective-permute-start(bf16[64,1536]{1,0:T(8,128)(2,1)} %refs_0_.7), channel_id=1, source_target_pairs={{0,12},{4,0},{8,4},{12,8},{1,13},{5,1},{9,5},{13,9},{2,14},{6,2},{... | collective-permute-start | bytes 589832 | tf_op jit(solution)/shard_map/ppermute | solution.py:333
  5.1 0.7 convert_element_type.70
  5.7 0.7 pad_maximum_fusion
  6.5 1.1 collective-permute-start.2
  7.6 2.9 %collective-permute-start.1 = (f32[64,16]{1,0:T(8,128)S(1)}, f32[64,16]{1,0:T(8,128)S(1)}, u32[]{:S(2)}, u32[]{:S(2)}) collective-permute-start(f32[64,16]{1,0:T(8,128)S(1)} %copy.12.refs_0_), channel_id=1, source_target_pairs={{0,12},{4,0},{8,4},{12,8},{1,13},{5,1},{9,5},{13,9},{2,14},{6,2},{... | collective-permute-start | bytes 12296 | tf_op jit(solution)/shard_map/ppermute | solution.py:298
  11.0 3.9 %collective-permute-start.6 = (bf16[32,1536]{1,0:T(8,128)(2,1)S(1)}, bf16[32,1536]{1,0:T(8,128)(2,1)S(1)}, u32[]{:S(2)}, u32[]{:S(2)}) collective-permute-start(bf16[32,1536]{1,0:T(8,128)(2,1)S(1)} %slice.85), channel_id=1, source_target_pairs={{0,12},{4,0},{8,4},{12,8},{1,13},{5,1},{9,5},{13,9},{2,14},{6,2},{... | collective-permute-start | bytes 294920 | tf_op jit(solution)/shard_map/ppermute | solution.py:337
  14.9 0.8 collective-permute-done.3.refs_1_
  15.8 1.6 %collective-permute-start.5 = (bf16[32,1536]{1,0:T(8,128)(2,1)S(1)}, bf16[32,1536]{1,0:T(8,128)(2,1)S(1)}, u32[]{:S(2)}, u32[]{:S(2)}) collective-permute-start(bf16[32,1536]{1,0:T(8,128)(2,1)S(1)} %slice.84), channel_id=1, source_target_pairs={{0,4},{4,8},{8,12},{12,0},{1,5},{5,9},{9,13},{13,1},{2,6},{6,10},{... | collective-permute-start | bytes 294920 | tf_op jit(solution)/shard_map/ppermute | solution.py:337
  19.2 3.0 %route.1 = (f32[8,256]{1,0:T(8,128)}, f32[256,128]{1,0:T(8,128)}, f32[256,128]{1,0:T(8,128)}, s32[8,128]{1,0:T(8,128)}) custom-call(s32[2]{0:T(128)} %pad_add_fusion.info, f32[64,16]{1,0:T(8,128)} %copy-done.6, f32[64,16]{1,0:T(8,128)} %copy-done.9, f32[64,16]{1,0:T(8,128)} %copy-done.8, f32[64,16]{1,0:T(8,128)} %copy-done.7), custom_call_target="tpu_custom_call" | custom-call | tf_op jit(solution)/shard_map/route/pallas_call | solution.py:77
  22.2 0.9 copy-done
  23.2 0.7 copy-done.3
  23.8 0.7 copy-done.5
  24.5 9.8 %gate_up.5 = (bf16[2,256,512]{2,1,0:T(8,128)(2,1)S(1)}, bf16[2,256,512]{2,1,0:T(8,128)(2,1)S(1)}) custom-call(s32[8,128]{1,0:T(8,128)S(1)} %copy-done.3, bf16[64,1536]{1,0:T(8,128)(2,1)S(1)} %copy-done, bf16[64,1536]{1,0:T(8,128)(2,1)S(1)} %collective-permute-done.3.refs_1_, bf16[64,1536]{1,0:T(8,128)(2,1)S(1)} %collective-permute-done.4.refs_2_, ...), custom_call_target="tpu_custom_call" | custom-call | flops 1610612736 | bytes 12582912 | tf_op jit(solution)/shard_map/gate_up/pallas_call | solution.py:158
  34.4 9.8 %gate_up.4 = (bf16[2,256,512]{2,1,0:T(8,128)(2,1)S(1)}, bf16[2,256,512]{2,1,0:T(8,128)(2,1)S(1)}) custom-call(s32[8,128]{1,0:T(8,128)S(1)} %copy-done.3, bf16[64,1536]{1,0:T(8,128)(2,1)S(1)} %copy-done, bf16[64,1536]{1,0:T(8,128)(2,1)S(1)} %collective-permute-done.3.refs_1_, bf16[64,1536]{1,0:T(8,128)(2,1)S(1)} %collective-permute-done.4.refs_2_, ...), custom_call_target="tpu_custom_call" | custom-call | flops 1610612736 | bytes 12582912 | tf_op jit(solution)/shard_map/gate_up/pallas_call | solution.py:158
  45.1 1.6 %collective-permute-start.9 = (bf16[1,256,512]{2,1,0:T(8,128)(2,1)S(1)}, bf16[1,256,512]{2,1,0:T(8,128)(2,1)S(1)}, u32[]{:S(2)}, u32[]{:S(2)}) collective-permute-start(bf16[1,256,512]{2,1,0:T(8,128)(2,1)S(1)} %slice.128.refs_8_), channel_id=1, source_target_pairs={{0,2},{1,3},{2,0},{3,1},{4,6},{5,7},{6,4},{7,5},{8,10},{9,11},{10,... | collective-permute-start | bytes 786440 | tf_op jit(solution)/shard_map/ppermute | solution.py:22
  46.6 10.0 %gate_up.7 = (bf16[2,256,512]{2,1,0:T(8,128)(2,1)S(1)}, bf16[2,256,512]{2,1,0:T(8,128)(2,1)S(1)}) custom-call(s32[8,128]{1,0:T(8,128)S(1)} %copy-done.3, bf16[64,1536]{1,0:T(8,128)(2,1)S(1)} %copy-done, bf16[64,1536]{1,0:T(8,128)(2,1)S(1)} %collective-permute-done.3.refs_1_, bf16[64,1536]{1,0:T(8,128)(2,1)S(1)} %collective-permute-done.4.refs_2_, ...), custom_call_target="tpu_custom_call" | custom-call | flops 1610612736 | bytes 12582912 | tf_op jit(solution)/shard_map/gate_up/pallas_call | solution.py:158
  57.7 1.6 %collective-permute-start.13 = (bf16[1,256,256]{2,1,0:T(8,128)(2,1)S(1)}, bf16[1,256,256]{2,1,0:T(8,128)(2,1)S(1)}, u32[]{:S(2)}, u32[]{:S(2)}) collective-permute-start(bf16[1,256,256]{2,1,0:T(8,128)(2,1)S(1)} %fusion.3.refs_9_.refs_0_), channel_id=1, source_target_pairs={{0,2},{1,3},{2,0},{3,1},{4,6},{5,7},{6,4},{7,5},{8,10},{9,11},{10,... | collective-permute-start | bytes 393224 | tf_op jit(solution)/shard_map/ppermute | solution.py:22
  59.3 9.8 %gate_up.6 = (bf16[2,256,512]{2,1,0:T(8,128)(2,1)S(1)}, bf16[2,256,512]{2,1,0:T(8,128)(2,1)S(1)}) custom-call(s32[8,128]{1,0:T(8,128)S(1)} %copy-done.3, bf16[64,1536]{1,0:T(8,128)(2,1)S(1)} %copy-done, bf16[64,1536]{1,0:T(8,128)(2,1)S(1)} %collective-permute-done.3.refs_1_, bf16[64,1536]{1,0:T(8,128)(2,1)S(1)} %collective-permute-done.4.refs_2_, ...), custom_call_target="tpu_custom_call" | custom-call | flops 1610612736 | bytes 12582912 | tf_op jit(solution)/shard_map/gate_up/pallas_call | solution.py:158
  71.2 1.5 %collective-permute-start.19 = (bf16[1,256,512]{2,1,0:T(8,128)(2,1)S(1)}, bf16[1,256,512]{2,1,0:T(8,128)(2,1)S(1)}, u32[]{:S(2)}, u32[]{:S(2)}) collective-permute-start(bf16[1,256,512]{2,1,0:T(8,128)(2,1)S(1)} %slice.126), channel_id=1, source_target_pairs={{0,2},{1,3},{2,0},{3,1},{4,6},{5,7},{6,4},{7,5},{8,10},{9,11},{10,... | collective-permute-start | bytes 786440 | tf_op jit(solution)/shard_map/ppermute | solution.py:22
  73.6 6.2 %down.4.refs_7_ = f32[256,1536]{1,0:T(8,128)S(1)} custom-call(s32[8,128]{1,0:T(8,128)S(1)} %copy-done.4, bf16[1,256,256]{2,1,0:T(8,128)(2,1)S(1)} %fusion.3.refs_9_.refs_0_, bf16[1,256,256]{2,1,0:T(8,128)(2,1)S(1)} %collective-permute-done.12.refs_1_, bf16[1,256,256]{2,1,0:T(8,128)(2,1)S(1)} %collective-permute-done.13.refs_2_, ...), custom_call_target="tpu_custom_call" | custom-call | flops 1006632960 | bytes 9437184 | tf_op jit(solution)/shard_map/down/pallas_call | solution.py:230
  79.8 2.1 %collective-permute-done.19 = bf16[1,256,512]{2,1,0:T(8,128)(2,1)S(1)} collective-permute-done((bf16[1,256,512]{2,1,0:T(8,128)(2,1)S(1)}, bf16[1,256,512]{2,1,0:T(8,128)(2,1)S(1)}, u32[]{:S(2)}, u32[]{:S(2)}) %collective-permute-start.19) | collective-permute-done | bytes 262176 | tf_op jit(solution)/shard_map/ppermute | solution.py:22
  82.2 5.4 %collective-permute-done.11 = bf16[1,256,512]{2,1,0:T(8,128)(2,1)S(1)} collective-permute-done((bf16[1,256,512]{2,1,0:T(8,128)(2,1)S(1)}, bf16[1,256,512]{2,1,0:T(8,128)(2,1)S(1)}, u32[]{:S(2)}, u32[]{:S(2)}) %collective-permute-start.11) | collective-permute-done | bytes 262176 | tf_op jit(solution)/shard_map/ppermute | solution.py:22
  88.3 1.8 %collective-permute-done.21.refs_2_ = bf16[1,256,256]{2,1,0:T(8,128)(2,1)S(1)} collective-permute-done((bf16[1,256,256]{2,1,0:T(8,128)(2,1)S(1)}, bf16[1,256,256]{2,1,0:T(8,128)(2,1)S(1)}, u32[]{:S(2)}, u32[]{:S(2)}) %collective-permute-start.21) | collective-permute-done | bytes 131104 | tf_op jit(solution)/shard_map/ppermute | solution.py:22
  90.6 2.1 %collective-permute-done.16.refs_2_ = bf16[1,256,256]{2,1,0:T(8,128)(2,1)S(1)} collective-permute-done((bf16[1,256,256]{2,1,0:T(8,128)(2,1)S(1)}, bf16[1,256,256]{2,1,0:T(8,128)(2,1)S(1)}, u32[]{:S(2)}, u32[]{:S(2)}) %collective-permute-start.16) | collective-permute-done | bytes 131104 | tf_op jit(solution)/shard_map/ppermute | solution.py:22
  92.7 6.2 %down.5.refs_7_ = f32[256,1536]{1,0:T(8,128)S(1)} custom-call(s32[8,128]{1,0:T(8,128)S(1)} %copy-done.4, bf16[1,256,256]{2,1,0:T(8,128)(2,1)S(1)} %fusion.refs_0_, bf16[1,256,256]{2,1,0:T(8,128)(2,1)S(1)} %collective-permute-done.24.refs_1_, bf16[1,256,256]{2,1,0:T(8,128)(2,1)S(1)} %collective-permute-done.25.refs_2_, ...), custom_call_target="tpu_custom_call" | custom-call | flops 1006632960 | bytes 9437184 | tf_op jit(solution)/shard_map/down/pallas_call | solution.py:230
  99.0 6.5 %down.6.refs_7_ = f32[256,1536]{1,0:T(8,128)S(1)} custom-call(s32[8,128]{1,0:T(8,128)S(1)} %copy-done.4, bf16[1,256,256]{2,1,0:T(8,128)(2,1)S(1)} %fusion.1.refs_0_, bf16[1,256,256]{2,1,0:T(8,128)(2,1)S(1)} %collective-permute-done.20.refs_1_, bf16[1,256,256]{2,1,0:T(8,128)(2,1)S(1)} %collective-permute-done.21.refs_2_, ...), custom_call_target="tpu_custom_call" | custom-call | flops 1006632960 | bytes 9437184 | tf_op jit(solution)/shard_map/down/pallas_call | solution.py:230
  105.5 6.2 %down.7 = (bf16[64,1536]{1,0:T(8,128)(2,1)S(1)}, bf16[64,1536]{1,0:T(8,128)(2,1)S(1)}, bf16[64,1536]{1,0:T(8,128)(2,1)S(1)}, bf16[64,1536]{1,0:T(8,128)(2,1)S(1)}) custom-call(s32[8,128]{1,0:T(8,128)S(1)} %copy-done.4, bf16[1,256,256]{2,1,0:T(8,128)(2,1)S(1)} %fusion.2.refs_8_.refs_0_, bf16[1,256,256]{2,1,0:T(8,128)(2,1)S(1)} %collective-permute-done.15.refs_1_, ...), custom_call_target="tpu_custom_call" | custom-call | flops 1006632960 | bytes 9437184 | tf_op jit(solution)/shard_map/down/pallas_call | solution.py:230
  111.7 2.5 %collective-permute-start.27 = (bf16[64,1536]{1,0:T(8,128)(2,1)S(1)}, bf16[64,1536]{1,0:T(8,128)(2,1)S(1)}, u32[]{:S(2)}, u32[]{:S(2)}) collective-permute-start(bf16[64,1536]{1,0:T(8,128)(2,1)S(1)} %get-tuple-element.36), channel_id=1, source_target_pairs={{0,12},{4,0},{8,4},{12,8},{1,13},{5,1},{9,5},{13,9},{2,14},{6,2},{... | collective-permute-start | bytes 589832 | tf_op jit(solution)/shard_map/ppermute | solution.py:346
  114.9 4.6 %collective-permute-done.27 = bf16[64,1536]{1,0:T(8,128)(2,1)S(1)} collective-permute-done((bf16[64,1536]{1,0:T(8,128)(2,1)S(1)}, bf16[64,1536]{1,0:T(8,128)(2,1)S(1)}, u32[]{:S(2)}, u32[]{:S(2)}) %collective-permute-start.27) | collective-permute-done | bytes 196640 | tf_op jit(solution)/shard_map/ppermute | solution.py:346
  119.5 4.8 %collective-permute-done.28 = bf16[64,1536]{1,0:T(8,128)(2,1)S(1)} collective-permute-done((bf16[64,1536]{1,0:T(8,128)(2,1)S(1)}, bf16[64,1536]{1,0:T(8,128)(2,1)S(1)}, u32[]{:S(2)}, u32[]{:S(2)}) %collective-permute-start.28) | collective-permute-done | bytes 196640 | tf_op jit(solution)/shard_map/ppermute | solution.py:346
  124.3 7.6 %collective-permute-done.29 = bf16[64,1536]{1,0:T(8,128)(2,1)S(1)} collective-permute-done((bf16[64,1536]{1,0:T(8,128)(2,1)S(1)}, bf16[64,1536]{1,0:T(8,128)(2,1)S(1)}, u32[]{:S(2)}, u32[]{:S(2)}) %collective-permute-start.29) | collective-permute-done | bytes 196640 | tf_op jit(solution)/shard_map/ppermute | solution.py:346
  131.9 0.8 add_convert_fusion
  (80 shorter events, 9.5 us)
Async XLA Ops:
  0.0 11.0 %collective-permute-start.4 = (bf16[64,1536]{1,0:T(8,128)(2,1)}, bf16[64,1536]{1,0:T(8,128)(2,1)S(1)}, u32[]{:S(2)}, u32[]{:S(2)}) collective-permute-start(bf16[64,1536]{1,0:T(8,128)(2,1)} %refs_0_.7), channel_id=1, source_target_pairs={{0,12},{4,0},{8,4},{12,8},{1,13},{5,1},{9,5},{13,9},{2,14},{6,2},{... | collective-permute-start | bytes 589832 | tf_op jit(solution)/shard_map/ppermute | solution.py:333
  5.0 10.7 %collective-permute-start.3 = (bf16[64,1536]{1,0:T(8,128)(2,1)}, bf16[64,1536]{1,0:T(8,128)(2,1)S(1)}, u32[]{:S(2)}, u32[]{:S(2)}) collective-permute-start(bf16[64,1536]{1,0:T(8,128)(2,1)} %refs_0_.7), channel_id=1, source_target_pairs={{0,4},{4,8},{8,12},{12,0},{1,5},{5,9},{9,13},{13,1},{2,6},{6,10},{... | collective-permute-start | bytes 589832 | tf_op jit(solution)/shard_map/ppermute | solution.py:333
  6.5 11.5 %collective-permute-start.2 = (f32[64,16]{1,0:T(8,128)S(1)}, f32[64,16]{1,0:T(8,128)S(1)}, u32[]{:S(2)}, u32[]{:S(2)}) collective-permute-start(f32[64,16]{1,0:T(8,128)S(1)} %copy.12.refs_0_), channel_id=1, source_target_pairs={{0,8},{4,12},{8,0},{12,4},{1,9},{5,13},{9,1},{13,5},{2,10},{6,14},... | collective-permute-start | bytes 12296 | tf_op jit(solution)/shard_map/ppermute | solution.py:298
  7.6 10.4 %collective-permute-start.1 = (f32[64,16]{1,0:T(8,128)S(1)}, f32[64,16]{1,0:T(8,128)S(1)}, u32[]{:S(2)}, u32[]{:S(2)}) collective-permute-start(f32[64,16]{1,0:T(8,128)S(1)} %copy.12.refs_0_), channel_id=1, source_target_pairs={{0,12},{4,0},{8,4},{12,8},{1,13},{5,1},{9,5},{13,9},{2,14},{6,2},{... | collective-permute-start | bytes 12296 | tf_op jit(solution)/shard_map/ppermute | solution.py:298
  10.5 7.5 %collective-permute-start = (f32[64,16]{1,0:T(8,128)S(1)}, f32[64,16]{1,0:T(8,128)S(1)}, u32[]{:S(2)}, u32[]{:S(2)}) collective-permute-start(f32[64,16]{1,0:T(8,128)S(1)} %copy.12.refs_0_), channel_id=1, source_target_pairs={{0,4},{4,8},{8,12},{12,0},{1,5},{5,9},{9,13},{13,1},{2,6},{6,10},{... | collective-permute-start | bytes 12296 | tf_op jit(solution)/shard_map/ppermute | solution.py:298
  11.0 11.2 %collective-permute-start.6 = (bf16[32,1536]{1,0:T(8,128)(2,1)S(1)}, bf16[32,1536]{1,0:T(8,128)(2,1)S(1)}, u32[]{:S(2)}, u32[]{:S(2)}) collective-permute-start(bf16[32,1536]{1,0:T(8,128)(2,1)S(1)} %slice.85), channel_id=1, source_target_pairs={{0,12},{4,0},{8,4},{12,8},{1,13},{5,1},{9,5},{13,9},{2,14},{6,2},{... | collective-permute-start | bytes 294920 | tf_op jit(solution)/shard_map/ppermute | solution.py:337
  15.8 6.5 %collective-permute-start.5 = (bf16[32,1536]{1,0:T(8,128)(2,1)S(1)}, bf16[32,1536]{1,0:T(8,128)(2,1)S(1)}, u32[]{:S(2)}, u32[]{:S(2)}) collective-permute-start(bf16[32,1536]{1,0:T(8,128)(2,1)S(1)} %slice.84), channel_id=1, source_target_pairs={{0,4},{4,8},{8,12},{12,0},{1,5},{5,9},{9,13},{13,1},{2,6},{6,10},{... | collective-permute-start | bytes 294920 | tf_op jit(solution)/shard_map/ppermute | solution.py:337
  34.4 10.5 %collective-permute-start.8 = (bf16[2,256,512]{2,1,0:T(8,128)(2,1)S(1)}, bf16[2,256,512]{2,1,0:T(8,128)(2,1)S(1)}, u32[]{:S(2)}, u32[]{:S(2)}) collective-permute-start(bf16[2,256,512]{2,1,0:T(8,128)(2,1)S(1)} %get-tuple-element.27), channel_id=1, source_target_pairs={{0,1},{1,0},{2,3},{3,2},{4,5},{5,4},{6,7},{7,6},{8,9},{9,8},{10,11... | collective-permute-start | bytes 1572872 | tf_op jit(solution)/shard_map/ppermute | solution.py:22
  44.3 12.4 %collective-permute-start.7 = (bf16[2,256,512]{2,1,0:T(8,128)(2,1)S(1)}, bf16[2,256,512]{2,1,0:T(8,128)(2,1)S(1)}, u32[]{:S(2)}, u32[]{:S(2)}) collective-permute-start(bf16[2,256,512]{2,1,0:T(8,128)(2,1)S(1)} %get-tuple-element.25), channel_id=1, source_target_pairs={{0,1},{1,0},{2,3},{3,2},{4,5},{5,4},{6,7},{7,6},{8,9},{9,8},{10,11... | collective-permute-start | bytes 1572872 | tf_op jit(solution)/shard_map/ppermute | solution.py:22
  45.1 12.5 %collective-permute-start.9 = (bf16[1,256,512]{2,1,0:T(8,128)(2,1)S(1)}, bf16[1,256,512]{2,1,0:T(8,128)(2,1)S(1)}, u32[]{:S(2)}, u32[]{:S(2)}) collective-permute-start(bf16[1,256,512]{2,1,0:T(8,128)(2,1)S(1)} %slice.128.refs_8_), channel_id=1, source_target_pairs={{0,2},{1,3},{2,0},{3,1},{4,6},{5,7},{6,4},{7,5},{8,10},{9,11},{10,... | collective-permute-start | bytes 786440 | tf_op jit(solution)/shard_map/ppermute | solution.py:22
  56.6 13.8 %collective-permute-start.18 = (bf16[2,256,512]{2,1,0:T(8,128)(2,1)S(1)}, bf16[2,256,512]{2,1,0:T(8,128)(2,1)S(1)}, u32[]{:S(2)}, u32[]{:S(2)}) collective-permute-start(bf16[2,256,512]{2,1,0:T(8,128)(2,1)S(1)} %get-tuple-element.34), channel_id=1, source_target_pairs={{0,1},{1,0},{2,3},{3,2},{4,5},{5,4},{6,7},{7,6},{8,9},{9,8},{10,11... | collective-permute-start | bytes 1572872 | tf_op jit(solution)/shard_map/ppermute | solution.py:22
  56.9 12.8 %collective-permute-start.23 = (bf16[1,256,512]{2,1,0:T(8,128)(2,1)S(1)}, bf16[1,256,512]{2,1,0:T(8,128)(2,1)S(1)}, u32[]{:S(2)}, u32[]{:S(2)}) collective-permute-start(bf16[1,256,512]{2,1,0:T(8,128)(2,1)S(1)} %slice.129.refs_8_), channel_id=1, source_target_pairs={{0,2},{1,3},{2,0},{3,1},{4,6},{5,7},{6,4},{7,5},{8,10},{9,11},{10,... | collective-permute-start | bytes 786440 | tf_op jit(solution)/shard_map/ppermute | solution.py:22
  57.7 15.9 %copy-start.1 = (f32[256,128]{1,0:T(8,128)S(1)}, f32[256,128]{1,0:T(8,128)}, u32[]{:S(2)}) copy-start(f32[256,128]{1,0:T(8,128)} %get-tuple-element.30.refs_4_) | copy-start | bytes 393220
  57.7 15.9 %copy-start.2 = (f32[256,128]{1,0:T(8,128)S(1)}, f32[256,128]{1,0:T(8,128)}, u32[]{:S(2)}) copy-start(f32[256,128]{1,0:T(8,128)} %get-tuple-element.31.refs_5_) | copy-start | bytes 393220
  57.7 12.8 %collective-permute-start.13 = (bf16[1,256,256]{2,1,0:T(8,128)(2,1)S(1)}, bf16[1,256,256]{2,1,0:T(8,128)(2,1)S(1)}, u32[]{:S(2)}, u32[]{:S(2)}) collective-permute-start(bf16[1,256,256]{2,1,0:T(8,128)(2,1)S(1)} %fusion.3.refs_9_.refs_0_), channel_id=1, source_target_pairs={{0,2},{1,3},{2,0},{3,1},{4,6},{5,7},{6,4},{7,5},{8,10},{9,11},{10,... | collective-permute-start | bytes 393224 | tf_op jit(solution)/shard_map/ppermute | solution.py:22
  59.3 13.7 %collective-permute-start.12 = (bf16[1,256,256]{2,1,0:T(8,128)(2,1)S(1)}, bf16[1,256,256]{2,1,0:T(8,128)(2,1)S(1)}, u32[]{:S(2)}, u32[]{:S(2)}) collective-permute-start(bf16[1,256,256]{2,1,0:T(8,128)(2,1)S(1)} %fusion.3.refs_9_.refs_0_), channel_id=1, source_target_pairs={{0,1},{1,0},{2,3},{3,2},{4,5},{5,4},{6,7},{7,6},{8,9},{9,8},{10,11... | collective-permute-start | bytes 393224 | tf_op jit(solution)/shard_map/ppermute | solution.py:22
  69.1 2.1 %collective-permute-start.10 = (bf16[2,256,512]{2,1,0:T(8,128)(2,1)S(1)}, bf16[2,256,512]{2,1,0:T(8,128)(2,1)S(1)}, u32[]{:S(2)}, u32[]{:S(2)}) collective-permute-start(bf16[2,256,512]{2,1,0:T(8,128)(2,1)S(1)} %get-tuple-element.29), channel_id=1, source_target_pairs={{0,1},{1,0},{2,3},{3,2},{4,5},{5,4},{6,7},{7,6},{8,9},{9,8},{10,11... | collective-permute-start | bytes 1572872 | tf_op jit(solution)/shard_map/ppermute | solution.py:22
  69.9 17.9 %collective-permute-start.25 = (bf16[1,256,256]{2,1,0:T(8,128)(2,1)S(1)}, bf16[1,256,256]{2,1,0:T(8,128)(2,1)S(1)}, u32[]{:S(2)}, u32[]{:S(2)}) collective-permute-start(bf16[1,256,256]{2,1,0:T(8,128)(2,1)S(1)} %fusion.refs_0_), channel_id=1, source_target_pairs={{0,2},{1,3},{2,0},{3,1},{4,6},{5,7},{6,4},{7,5},{8,10},{9,11},{10,... | collective-permute-start | bytes 393224 | tf_op jit(solution)/shard_map/ppermute | solution.py:22
  70.5 19.7 %collective-permute-start.24 = (bf16[1,256,256]{2,1,0:T(8,128)(2,1)S(1)}, bf16[1,256,256]{2,1,0:T(8,128)(2,1)S(1)}, u32[]{:S(2)}, u32[]{:S(2)}) collective-permute-start(bf16[1,256,256]{2,1,0:T(8,128)(2,1)S(1)} %fusion.refs_0_), channel_id=1, source_target_pairs={{0,1},{1,0},{2,3},{3,2},{4,5},{5,4},{6,7},{7,6},{8,9},{9,8},{10,11... | collective-permute-start | bytes 393224 | tf_op jit(solution)/shard_map/ppermute | solution.py:22
  70.5 3.1 %collective-permute-start.14 = (bf16[1,256,256]{2,1,0:T(8,128)(2,1)S(1)}, bf16[1,256,256]{2,1,0:T(8,128)(2,1)S(1)}, u32[]{:S(2)}, u32[]{:S(2)}) collective-permute-start(bf16[1,256,256]{2,1,0:T(8,128)(2,1)S(1)} %collective-permute-done.13.refs_2_), channel_id=1, source_target_pairs={{0,1},{1,0},{2,3},{3,2},{4,5},{5,4},{6,7},{7,6},{8,9},{9,8},{10,11... | collective-permute-start | bytes 393224 | tf_op jit(solution)/shard_map/ppermute | solution.py:22
  71.2 10.7 %collective-permute-start.19 = (bf16[1,256,512]{2,1,0:T(8,128)(2,1)S(1)}, bf16[1,256,512]{2,1,0:T(8,128)(2,1)S(1)}, u32[]{:S(2)}, u32[]{:S(2)}) collective-permute-start(bf16[1,256,512]{2,1,0:T(8,128)(2,1)S(1)} %slice.126), channel_id=1, source_target_pairs={{0,2},{1,3},{2,0},{3,1},{4,6},{5,7},{6,4},{7,5},{8,10},{9,11},{10,... | collective-permute-start | bytes 786440 | tf_op jit(solution)/shard_map/ppermute | solution.py:22
  72.9 14.6 %collective-permute-start.11 = (bf16[1,256,512]{2,1,0:T(8,128)(2,1)S(1)}, bf16[1,256,512]{2,1,0:T(8,128)(2,1)S(1)}, u32[]{:S(2)}, u32[]{:S(2)}) collective-permute-start(bf16[1,256,512]{2,1,0:T(8,128)(2,1)S(1)} %slice.127.refs_7_), channel_id=1, source_target_pairs={{0,2},{1,3},{2,0},{3,1},{4,6},{5,7},{6,4},{7,5},{8,10},{9,11},{10,... | collective-permute-start | bytes 786440 | tf_op jit(solution)/shard_map/ppermute | solution.py:22
  82.1 8.1 %collective-permute-start.21 = (bf16[1,256,256]{2,1,0:T(8,128)(2,1)S(1)}, bf16[1,256,256]{2,1,0:T(8,128)(2,1)S(1)}, u32[]{:S(2)}, u32[]{:S(2)}) collective-permute-start(bf16[1,256,256]{2,1,0:T(8,128)(2,1)S(1)} %fusion.1.refs_0_), channel_id=1, source_target_pairs={{0,2},{1,3},{2,0},{3,1},{4,6},{5,7},{6,4},{7,5},{8,10},{9,11},{10,... | collective-permute-start | bytes 393224 | tf_op jit(solution)/shard_map/ppermute | solution.py:22
  87.7 5.0 %collective-permute-start.16 = (bf16[1,256,256]{2,1,0:T(8,128)(2,1)S(1)}, bf16[1,256,256]{2,1,0:T(8,128)(2,1)S(1)}, u32[]{:S(2)}, u32[]{:S(2)}) collective-permute-start(bf16[1,256,256]{2,1,0:T(8,128)(2,1)S(1)} %fusion.2.refs_8_.refs_0_), channel_id=1, source_target_pairs={{0,2},{1,3},{2,0},{3,1},{4,6},{5,7},{6,4},{7,5},{8,10},{9,11},{10,... | collective-permute-start | bytes 393224 | tf_op jit(solution)/shard_map/ppermute | solution.py:22
  87.8 4.9 %collective-permute-start.26 = (bf16[1,256,256]{2,1,0:T(8,128)(2,1)S(1)}, bf16[1,256,256]{2,1,0:T(8,128)(2,1)S(1)}, u32[]{:S(2)}, u32[]{:S(2)}) collective-permute-start(bf16[1,256,256]{2,1,0:T(8,128)(2,1)S(1)} %collective-permute-done.25.refs_2_), channel_id=1, source_target_pairs={{0,1},{1,0},{2,3},{3,2},{4,5},{5,4},{6,7},{7,6},{8,9},{9,8},{10,11... | collective-permute-start | bytes 393224 | tf_op jit(solution)/shard_map/ppermute | solution.py:22
  87.8 11.1 %collective-permute-start.20 = (bf16[1,256,256]{2,1,0:T(8,128)(2,1)S(1)}, bf16[1,256,256]{2,1,0:T(8,128)(2,1)S(1)}, u32[]{:S(2)}, u32[]{:S(2)}) collective-permute-start(bf16[1,256,256]{2,1,0:T(8,128)(2,1)S(1)} %fusion.1.refs_0_), channel_id=1, source_target_pairs={{0,1},{1,0},{2,3},{3,2},{4,5},{5,4},{6,7},{7,6},{8,9},{9,8},{10,11... | collective-permute-start | bytes 393224 | tf_op jit(solution)/shard_map/ppermute | solution.py:22
  90.1 8.9 %collective-permute-start.22 = (bf16[1,256,256]{2,1,0:T(8,128)(2,1)S(1)}, bf16[1,256,256]{2,1,0:T(8,128)(2,1)S(1)}, u32[]{:S(2)}, u32[]{:S(2)}) collective-permute-start(bf16[1,256,256]{2,1,0:T(8,128)(2,1)S(1)} %collective-permute-done.21.refs_2_), channel_id=1, source_target_pairs={{0,1},{1,0},{2,3},{3,2},{4,5},{5,4},{6,7},{7,6},{8,9},{9,8},{10,11... | collective-permute-start | bytes 393224 | tf_op jit(solution)/shard_map/ppermute | solution.py:22
  90.1 15.4 %collective-permute-start.15 = (bf16[1,256,256]{2,1,0:T(8,128)(2,1)S(1)}, bf16[1,256,256]{2,1,0:T(8,128)(2,1)S(1)}, u32[]{:S(2)}, u32[]{:S(2)}) collective-permute-start(bf16[1,256,256]{2,1,0:T(8,128)(2,1)S(1)} %fusion.2.refs_8_.refs_0_), channel_id=1, source_target_pairs={{0,1},{1,0},{2,3},{3,2},{4,5},{5,4},{6,7},{7,6},{8,9},{9,8},{10,11... | collective-permute-start | bytes 393224 | tf_op jit(solution)/shard_map/ppermute | solution.py:22
  92.7 12.8 %collective-permute-start.17 = (bf16[1,256,256]{2,1,0:T(8,128)(2,1)S(1)}, bf16[1,256,256]{2,1,0:T(8,128)(2,1)S(1)}, u32[]{:S(2)}, u32[]{:S(2)}) collective-permute-start(bf16[1,256,256]{2,1,0:T(8,128)(2,1)S(1)} %collective-permute-done.16.refs_2_), channel_id=1, source_target_pairs={{0,1},{1,0},{2,3},{3,2},{4,5},{5,4},{6,7},{7,6},{8,9},{9,8},{10,11... | collective-permute-start | bytes 393224 | tf_op jit(solution)/shard_map/ppermute | solution.py:22
  111.7 7.8 %collective-permute-start.27 = (bf16[64,1536]{1,0:T(8,128)(2,1)S(1)}, bf16[64,1536]{1,0:T(8,128)(2,1)S(1)}, u32[]{:S(2)}, u32[]{:S(2)}) collective-permute-start(bf16[64,1536]{1,0:T(8,128)(2,1)S(1)} %get-tuple-element.36), channel_id=1, source_target_pairs={{0,12},{4,0},{8,4},{12,8},{1,13},{5,1},{9,5},{13,9},{2,14},{6,2},{... | collective-permute-start | bytes 589832 | tf_op jit(solution)/shard_map/ppermute | solution.py:346
  114.3 10.1 %collective-permute-start.28 = (bf16[64,1536]{1,0:T(8,128)(2,1)S(1)}, bf16[64,1536]{1,0:T(8,128)(2,1)S(1)}, u32[]{:S(2)}, u32[]{:S(2)}) collective-permute-start(bf16[64,1536]{1,0:T(8,128)(2,1)S(1)} %get-tuple-element.37), channel_id=1, source_target_pairs={{0,4},{4,8},{8,12},{12,0},{1,5},{5,9},{9,13},{13,1},{2,6},{6,10},{... | collective-permute-start | bytes 589832 | tf_op jit(solution)/shard_map/ppermute | solution.py:346
  114.3 17.7 %collective-permute-start.29 = (bf16[64,1536]{1,0:T(8,128)(2,1)S(1)}, bf16[64,1536]{1,0:T(8,128)(2,1)S(1)}, u32[]{:S(2)}, u32[]{:S(2)}) collective-permute-start(bf16[64,1536]{1,0:T(8,128)(2,1)S(1)} %get-tuple-element.38), channel_id=1, source_target_pairs={{0,8},{4,12},{8,0},{12,4},{1,9},{5,13},{9,1},{13,5},{2,10},{6,14},... | collective-permute-start | bytes 589832 | tf_op jit(solution)/shard_map/ppermute | solution.py:346
  (8 other events, 31.5 us)

commit v2 on v1

v2 whole, which is shorter than its diff:
```python
import functools

import jax
import jax.numpy as jnp
from jax import lax
from jax.experimental import pallas as pl
from jax.experimental.pallas import tpu as pltpu
from jax.sharding import PartitionSpec as P

LANES = 128
VMEM = pl.BlockSpec(memory_space=pltpu.VMEM)
SMEM = pl.BlockSpec(memory_space=pltpu.SMEM)
HERE = pl.BlockSpec(memory_space=pl.ANY)
FAR = pl.BlockSpec(memory_space=pltpu.HBM)
NOWHERE = -1e6


def bits_of(n):
    return [b for b in range(n.bit_length() - 1)]


def flip(x, axis, k):
    return lax.ppermute(x, axis, [(i, i ^ k) for i in range(lax.axis_size(axis))])


def route_body(n, experts, per_chunk, rows, info, *refs):
    meta, (rank, wt, sched) = refs[:n], refs[n:]
    tok, top = meta[0].shape[1], meta[0].shape[0] // 2
    padded = rank.shape[0]
    first = info[0].astype(jnp.float32)
    e = lax.broadcasted_iota(jnp.int32, (padded, tok), 0).astype(jnp.float32)
    before = (
        lax.broadcasted_iota(jnp.int32, (tok, tok), 0) < lax.broadcasted_iota(jnp.int32, (tok, tok), 1)
    ).astype(jnp.bfloat16)
    count = jnp.zeros((padded, 1), jnp.float32)
    for s in range(n):
        ids, scores = meta[s][:top], meta[s][top:]
        affinity = 1.0 / (1.0 + jnp.exp(-scores))
        share = 2.5 * affinity / jnp.sum(affinity, axis=0, keepdims=True)
        named = jnp.zeros((padded, tok), jnp.float32)
        weight = jnp.zeros((padded, tok), jnp.float32)
        for k in range(top):
            hit = jnp.where(ids[k : k + 1] - first == e, 1.0, 0.0)
            named = named + hit
            weight = weight + hit * share[k : k + 1]
        named = jnp.where(e < experts, named, 0.0)
        place = jnp.dot(named.astype(jnp.bfloat16), before, preferred_element_type=jnp.float32) + count
        rank[:, s * tok : (s + 1) * tok] = jnp.where(named > 0, place, NOWHERE)
        wt[:, s * tok : (s + 1) * tok] = weight
        count = count + jnp.sum(named, axis=1, keepdims=True)
    shape = (padded, LANES)
    j = lax.broadcasted_iota(jnp.int32, shape, 1).astype(jnp.float32)
    e = lax.broadcasted_iota(jnp.int32, shape, 0).astype(jnp.float32)
    other = jnp.sum(jnp.where(e == j, count, 0.0), axis=0, keepdims=True)
    ahead = ((other > count) | ((other == count) & (j < e))) & (j < experts)
    order = jnp.sum(ahead.astype(jnp.float32), axis=1, keepdims=True)
    large = jnp.where((order == j) & (e < experts), 1.0, 0.0)
    small = jnp.where((order == experts - 1 - j) & (e < experts), 1.0, 0.0)
    expert_a = jnp.sum(e * large, axis=0, keepdims=True)
    count_a = jnp.sum(count * large, axis=0, keepdims=True)
    if per_chunk == 2:
        expert_b = jnp.sum(e * small, axis=0, keepdims=True)
    else:
        expert_b = expert_a
        count_a = jnp.full_like(count_a, rows)
    sched[0:1] = expert_a.astype(jnp.int32)
    sched[1:2] = expert_b.astype(jnp.int32)
    sched[2:3] = count_a.astype(jnp.int32)
    sched[3:8] = jnp.full((5, LANES), info[1], jnp.int32)


def route(meta, info, experts, per_chunk, rows):
    tokens = len(meta) * meta[0].shape[1]
    padded = -(-experts // 8) * 8
    return pl.pallas_call(
        functools.partial(route_body, len(meta), experts, per_chunk, rows),
        out_shape=(
            jax.ShapeDtypeStruct((padded, tokens), jnp.float32),
            jax.ShapeDtypeStruct((padded, tokens), jnp.float32),
            jax.ShapeDtypeStruct((8, LANES), jnp.int32),
        ),
        in_specs=[SMEM] + [VMEM] * len(meta),
        out_specs=(VMEM,) * 3,
        name="route",
    )(info, *meta)


def put(out, at, sides, rows, split):
    left, right = sides[0], sides[-1]
    most = left.shape[0]
    if len(sides) == 1:
        out[at] = left
        return
    head = min(rows - most, most)
    out[at[:-2] + (slice(0, head), at[-1])] = left[:head]
    if head < most:
        shared = lax.broadcasted_iota(jnp.int32, (most - head, left.shape[1]), 0) + head < split
        out[at[:-2] + (slice(head, most), at[-1])] = jnp.where(shared, left[head:], right[: most - head])
    out[at[:-2] + (slice(most, rows), at[-1])] = right[most - head :]


def gate_up_body(n, chunk, n_dp, most, after, sched_in, *refs):
    tokens, (rank_in, w_gate, w_up), refs = refs[:n], refs[n : n + 3], refs[n + 3 + after :]
    send, keep, sched, rank, feed, rows, held, small_sem, feed_sem, held_sem = refs
    count = rows.shape[0]
    width = send.shape[2] // 2
    order = pltpu.make_async_copy(sched_in, sched, small_sem.at[0])
    ranks = pltpu.make_async_copy(rank_in, rank, small_sem.at[1])
    order.start()
    ranks.start()
    at, feeds = 0, []
    for s in range(n):
        tok = tokens[s].shape[0]
        feeds.append(pltpu.make_async_copy(tokens[s], feed.at[pl.ds(at, tok)], feed_sem.at[s]))
        at += tok
    for copy in feeds:
        copy.start()
    order.wait()
    split = sched[2, chunk]
    experts = [sched[0, chunk]] + ([sched[1, chunk]] if most < count else [])
    pieces = list(range(1, n_dp, 2)) + list(range(0, n_dp, 2))
    copies = {}
    for l in pieces:
        units = pl.ds(pl.multiple_of((l ^ sched[3, 0]) * width, width), width)
        for m, w in enumerate((w_gate, w_up)):
            for x, e in enumerate(experts):
                i = m * len(experts) + x
                copies[l, m, x] = pltpu.make_async_copy(
                    w.at[e, :, units], held.at[i, :, pl.ds(l * width, width)], held_sem.at[l, i]
                )
                copies[l, m, x].start()
    ranks.wait()
    r = lax.broadcasted_iota(jnp.int32, (count, at), 0).astype(jnp.float32)
    pick = jnp.where(r == rank[pl.ds(experts[0], 1), :], 1.0, 0.0)
    if most < count:
        pick = pick + jnp.where(count - 1 - r == rank[pl.ds(experts[1], 1), :], 1.0, 0.0)
    for copy in feeds:
        copy.wait()
    rows[...] = jnp.dot(
        pick.astype(jnp.bfloat16), feed[...], preferred_element_type=jnp.float32
    ).astype(jnp.bfloat16)
    for l in pieces:
        units = slice(l * width, (l + 1) * width)
        for m in range(2):
            sides = []
            for x, part in enumerate((rows[:most], rows[count - most :])[: len(experts)]):
                copies[l, m, x].wait()
                sides.append(
                    jnp.dot(
                        part, held[m * len(experts) + x, :, units], preferred_element_type=jnp.float32
                    ).astype(jnp.bfloat16)
                )
            to = (l // 2, slice(None), slice(m * width, (m + 1) * width))
            put(send if l % 2 else keep, to, sides, count, split)


def gate_up(tokens, rank, sched, w_gate, w_up, chunk, rows, most, n_dp, after):
    n, local = len(tokens), tokens[0].shape[1]
    hidden = w_gate.shape[2]
    out = jax.ShapeDtypeStruct((max(n_dp // 2, 1), rows, 2 * hidden // n_dp), jnp.bfloat16)
    mats = 2 * (2 if most < rows else 1)
    return pl.pallas_call(
        functools.partial(gate_up_body, n, chunk, n_dp, most, len(after)),
        out_shape=(out, out),
        in_specs=[FAR, FAR] + [HERE] * (n - 1) + [FAR] * 3 + [HERE] * len(after),
        out_specs=(VMEM, VMEM),
        scratch_shapes=[
            pltpu.SMEM(sched.shape, jnp.int32),
            pltpu.VMEM(rank.shape, jnp.float32),
            pltpu.VMEM((rank.shape[1], local), jnp.bfloat16),
            pltpu.VMEM((rows, local), jnp.bfloat16),
            pltpu.VMEM((mats, local, hidden), jnp.bfloat16),
            pltpu.SemaphoreType.DMA((2,)),
            pltpu.SemaphoreType.DMA((n,)),
            pltpu.SemaphoreType.DMA((n_dp, mats)),
        ],
        compiler_params=pltpu.CompilerParams(vmem_limit_bytes=40 << 20),
        cost_estimate=pl.CostEstimate(
            flops=8 * mats * most * local * hidden,
            bytes_accessed=2 * mats * local * hidden,
            transcendentals=0,
        ),
        name="gate_up",
    )(sched, *tokens, rank, w_gate, w_up, *after)


def down_body(n_dp, cuts, chunk, first, most, after, sched_in, *refs):
    parts, (rank_in, wt_in, w_down), refs = refs[:n_dp], refs[n_dp : n_dp + 3], refs[n_dp + 3 :]
    before = None if first else refs[0]
    refs = refs[(0 if first else 1) + after :]
    outs, refs = refs[: len(cuts)], refs[len(cuts) :]
    sched, rank, wt, hidden, mix, out, held, small_sem, held_sem = refs
    rows = hidden.shape[0]
    width = parts[0].shape[-1]
    local = out.shape[1]
    smalls = [
        pltpu.make_async_copy(source, to, small_sem.at[i])
        for i, (source, to) in enumerate(((sched_in, sched), (rank_in, rank), (wt_in, wt)))
    ]
    for copy in smalls:
        copy.start()
    smalls[0].wait()
    split = sched[2, chunk]
    experts = [sched[0, chunk]] + ([sched[1, chunk]] if most < rows else [])
    block = 512 if local % 512 == 0 else 256 if local % 256 == 0 else local
    copies = {}
    for i in range(local // block):
        for x, e in enumerate(experts):
            cols = pl.ds(i * block, block)
            copies[i, x] = pltpu.make_async_copy(
                w_down.at[e, :, cols], held.at[x, :, cols], held_sem.at[i, x]
            )
            copies[i, x].start()
    for l in range(n_dp):
        at = pl.multiple_of((l ^ sched[3, 0]) * width, width)
        hidden[:, pl.ds(at, width)] = parts[l][0]
    smalls[1].wait()
    smalls[2].wait()
    r = lax.broadcasted_iota(jnp.int32, mix.shape, 0).astype(jnp.float32)
    row = lambda ref, e: ref[pl.ds(e, 1), :]
    share = jnp.where(r == row(rank, experts[0]), row(wt, experts[0]), 0.0)
    if most < rows:
        share = share + jnp.where(rows - 1 - r == row(rank, experts[1]), row(wt, experts[1]), 0.0)
    mix[...] = share.astype(jnp.bfloat16)
    for i in range(local // block):
        cols = slice(i * block, (i + 1) * block)
        sides = []
        for x, part in enumerate((hidden[:most], hidden[rows - most :])[: len(experts)]):
            copies[i, x].wait()
            sides.append(
                jnp.dot(part, held[x, :, cols], preferred_element_type=jnp.float32).astype(jnp.bfloat16)
            )
        put(out, (slice(None), cols), sides, rows, split)
        total = lax.dot_general(
            mix[...], out[:, cols], (((0,), (0,)), ((), ())), preferred_element_type=jnp.float32
        )
        if not first:
            total = total + before[:, cols]
        at = 0
        for to, cut in zip(outs, cuts):
            to[:, cols] = total[at : at + cut].astype(to.dtype)
            at += cut


def down(parts, rank, wt, sched, w_down, total, chunk, most, cuts, after):
    n_dp = len(parts)
    _, rows, width = parts[0].shape
    _, hidden, local = w_down.shape
    tokens = rank.shape[1]
    first, last = total is None, len(cuts) > 1
    kind = jnp.bfloat16 if last else jnp.float32
    mats = 2 if most < rows else 1
    outs = pl.pallas_call(
        functools.partial(down_body, n_dp, cuts, chunk, first, most, len(after)),
        out_shape=tuple(jax.ShapeDtypeStruct((cut, local), kind) for cut in cuts),
        in_specs=[FAR]
        + [VMEM] * n_dp
        + [FAR] * 3
        + ([] if first else [VMEM])
        + [HERE] * len(after),
        out_specs=(VMEM,) * len(cuts),
        scratch_shapes=[
            pltpu.SMEM(sched.shape, jnp.int32),
            pltpu.VMEM(rank.shape, jnp.float32),
            pltpu.VMEM(rank.shape, jnp.float32),
            pltpu.VMEM((rows, hidden), jnp.bfloat16),
            pltpu.VMEM((rows, tokens), jnp.bfloat16),
            pltpu.VMEM((rows, local), jnp.bfloat16),
            pltpu.VMEM((mats, hidden, local), jnp.bfloat16),
            pltpu.SemaphoreType.DMA((3,)),
            pltpu.SemaphoreType.DMA((local // 256 + 1, mats)),
        ],
        compiler_params=pltpu.CompilerParams(vmem_limit_bytes=40 << 20),
        cost_estimate=pl.CostEstimate(
            flops=8 * local * (mats * most * hidden + rows * tokens),
            bytes_accessed=2 * mats * hidden * local + 8 * tokens * local,
            transcendentals=0,
        ),
        name="down",
    )(sched, *parts, rank, wt, w_down, *([] if first else [total]), *after)
    return outs if last else outs[0]


def partial_sums(send, keep, n_dp):
    total = keep.astype(jnp.float32)
    late = jnp.zeros(total.shape, jnp.bfloat16)
    for b in bits_of(n_dp):
        if b > 0:
            total = total + late.astype(jnp.float32)
            send = total[1::2].astype(jnp.bfloat16)
            total = total[0::2]
        late = flip(send, "dp", 1 << b)
    return total, late, send


def finish(total, late, after):
    if after:
        late, *_ = lax.optimization_barrier((late, *after))
    gate_up = total + late.astype(jnp.float32)
    width = gate_up.shape[2] // 2
    return (jax.nn.silu(gate_up[:, :, :width]) * gate_up[:, :, width:]).astype(jnp.bfloat16)


def all_parts(share, n_dp):
    parts = {0: share}
    for b in reversed(bits_of(n_dp)):
        for l in list(parts):
            parts[l | 1 << b] = flip(parts[l], "dp", 1 << b)
    return [parts[l] for l in range(n_dp)]


def on_device(tokens, expert_ids, scores, w_gate, w_up, w_down):
    n_owner, n_dp = lax.axis_size("expert"), lax.axis_size("dp")
    tok_rows, top = expert_ids.shape
    experts = w_gate.shape[0]
    capacity = 2 * tok_rows * top // (experts * n_owner)
    per_chunk = 2 if experts % 2 == 0 else 1
    most = n_owner * capacity
    rows = per_chunk * most
    chunks = experts // per_chunk

    meta = jnp.concatenate([expert_ids.T.astype(jnp.float32), scores.T], axis=0)
    feeds = gathered(tokens, "expert")
    metas = [meta] + [
        lax.ppermute(meta, "expert", [(i, (i - k) % n_owner) for i in range(n_owner)])
        for k in gathered_order(n_owner)[1:]
    ]
    info = jnp.stack([lax.axis_index("expert") * experts, lax.axis_index("dp")]).astype(jnp.int32)
    rank, wt, sched = route(metas, info, experts, per_chunk, rows)

    shares, sent, parts, total = [], [], [], None
    cuts = [feed.shape[0] for feed in feeds]

    def add(c, after):
        return down(
            parts[c], rank, wt, sched, w_down, total, c, most,
            cuts if c == chunks - 1 else [sum(cuts)], after,
        )

    for c in range(chunks):
        after = ([sent[c - 1]] if c >= 1 else []) + ([shares[c - 2]] if c >= 2 else [])
        send, keep = gate_up(feeds, rank, sched, w_gate, w_up, c, rows, most, n_dp, after)
        mine, late, last_sent = partial_sums(send, keep, n_dp)
        sent.append(last_sent)
        if c == chunks - 1 and c > 0:
            total = add(0, [last_sent, shares[-1]])
        shares.append(finish(mine, late, [] if total is None else [total]))
        parts.append(all_parts(shares[-1], n_dp))
    for c in range(1 if chunks > 1 else 0, chunks):
        total = add(c, [shares[-1]] if c == 1 else [])
    return returned(total, "expert") if n_owner > 1 else total[0].astype(jnp.bfloat16)


def gathered_order(n):
    near = [d for s in range(1, n // 2) for d in (-s, s)]
    return [0] + near + ([n // 2] if n > 1 else [])


def gathered(x, axis):
    n = lax.axis_size(axis)
    up, down_ = [(i, (i + 1) % n) for i in range(n)], [(i, (i - 1) % n) for i in range(n)]
    below = above = x
    found = [x]
    for _ in range(1, n // 2):
        below, above = lax.ppermute(below, axis, up), lax.ppermute(above, axis, down_)
        found += [below, above]
    if n > 1:
        half = x.shape[0] // 2
        found += [lax.ppermute(below[:half], axis, up), lax.ppermute(above[half:], axis, down_)]
    return found


def returned(partials, axis):
    n = lax.axis_size(axis)
    up, down_ = [(i, (i + 1) % n) for i in range(n)], [(i, (i - 1) % n) for i in range(n)]
    wide = lambda x: x.astype(jnp.float32)
    near = {0: partials[0]}
    for k, partial in zip(gathered_order(n)[1:-1], partials[1:-2]):
        near[k] = partial
    half = partials[-1].shape[0]
    low, high = lax.ppermute(partials[-2], axis, down_), lax.ppermute(partials[-1], axis, up)
    halves = True
    for s in range(n // 2 - 1, 0, -1):
        a, b = wide(near[-s]), wide(near[s])
        if halves:
            a = jnp.concatenate([a[:half] + wide(low), a[half:]], axis=0)
            b = jnp.concatenate([b[:half], b[half:] + wide(high)], axis=0)
        else:
            a, b = a + wide(low), b + wide(high)
        low = lax.ppermute(a.astype(jnp.bfloat16), axis, down_)
        high = lax.ppermute(b.astype(jnp.bfloat16), axis, up)
        halves = False
    if halves:
        back = jnp.concatenate([wide(low), wide(high)], axis=0)
    else:
        back = wide(low) + wide(high)
    return (wide(near[0]) + back).astype(jnp.bfloat16)


def solution(mesh):
    in_specs = (
        P(("groups", "expert"), "dp"),
        P(("groups", "expert"), None),
        P(("groups", "expert"), None),
        P("expert", "dp", None),
        P("expert", "dp", None),
        P("expert", None, "dp"),
    )
    out_specs = P(("groups", "expert"), "dp")
    return jax.shard_map(
        on_device, mesh=mesh, in_specs=in_specs, out_specs=out_specs, check_vma=False
    )
```

time: 133 us -> 118 us (0.89)
  Pallas kernels: 67.6 us -> 52.1 us
  starting transfers between devices: 27.7 us -> 32.2 us
  waiting for transfers between devices: 29.3 us -> 25.7 us
    pallas_call x4, Pallas kernels: 39.5 us -> 32.3 us  [gate_up(): pl.pallas_call(functools.partial(gate_up_body, n, chunk, n_dp, most, len(...]
    pallas_call x4, Pallas kernels: 25.1 us -> 18.1 us  [down(): pl.pallas_call(functools.partial(down_body, n_dp, cuts, chunk, first, mos...]
    ppermute x3 -> x4, waiting for transfers between devices: 17 us -> 10.9 us  [the longest x1 4.61 us: returned(): low = lax.ppermute(a.astype(jnp.bfloat16), axis, down_)]
    ppermute x3 -> x4, starting transfers between devices: 3.17 us -> 7.48 us  [the longest x1 4.33 us: returned(): low = lax.ppermute(a.astype(jnp.bfloat16), axis, down_)]
    ppermute x20, starting transfers between devices: 9.52 us -> 12.7 us  [flip(): lax.ppermute(x, axis, [(i, i ^ k) for i in range(lax.axis_size(axis))])]
    ppermute x1, starting transfers between devices: 5.05 us -> 2.03 us  [gathered(): lax.ppermute(above, axis, down_)]
    ppermute x1, starting transfers between devices: 0.01 us -> 3.02 us  [gathered(): lax.ppermute(below, axis, up)]
    ppermute x1, waiting for transfers between devices: 0.01 us -> 2.87 us  [gathered(): lax.ppermute(above, axis, down_)]
  transfers between devices with their start and end apart: 30 -> 31, of which waited for: 8 -> 10; matrix products, arithmetic and copies ran while one was open for 3% -> 3% of each run, Pallas kernels for 39% -> 33%
where the time goes in v2:
time: 118 us
  Pallas kernels  52.1 us (44%)
  starting transfers between devices  32.2 us (27%)
  waiting for transfers between devices  25.7 us (22%)
  other arithmetic  4.04 us (3%)
  local copies, waits for them, and re-layouts  3.63 us (3%)
    pallas_call x4, Pallas kernels, gate_up(): pl.pallas_call(functools.partial(gate_up_body, n, chunk, n_dp, most, len(...  32.3 us
    pallas_call x4, Pallas kernels, down(): pl.pallas_call(functools.partial(down_body, n_dp, cuts, chunk, first, mos...  18.1 us
    ppermute x20, starting transfers between devices, flip(): lax.ppermute(x, axis, [(i, i ^ k) for i in range(lax.axis_size(axis))])  12.7 us
    ppermute x20, waiting for transfers between devices, flip(): lax.ppermute(x, axis, [(i, i ^ k) for i in range(lax.axis_size(axis))])  11.2 us
    ppermute x1, waiting for transfers between devices, returned(): low = lax.ppermute(a.astype(jnp.bfloat16), axis, down_)  4.61 us
    ppermute x1, starting transfers between devices, returned(): low = lax.ppermute(a.astype(jnp.bfloat16), axis, down_)  4.33 us
    ppermute x3, starting transfers between devices, on_device(): lax.ppermute(meta, 'expert', [(i, (i - k) % n_owner) for i in range(n_own...  3.83 us
    unnamed x18, local copies, waits for them, and re-layouts  3.46 us
  transfers between devices with their start and end apart: 31, of which 10 were waited for; matrix products, arithmetic and copies ran while one was open for 3% of the time, Pallas kernels for 33%

profile of v2, /device:TPU:0, one launch (start us, length us, event | category | flops | bytes accessed | tf_op | source)
XLA Modules:
  0.0 118.1 jit_solution(5272994256551002484)
XLA Ops:
  0.0 3.0 %collective-permute-start.3 = (bf16[64,1536]{1,0:T(8,128)(2,1)}, bf16[64,1536]{1,0:T(8,128)(2,1)S(1)}, u32[]{:S(2)}, u32[]{:S(2)}) collective-permute-start(bf16[64,1536]{1,0:T(8,128)(2,1)} %refs_0_.7), channel_id=1, source_target_pairs={{0,4},{4,8},{8,12},{12,0},{1,5},{5,9},{9,13},{13,1},{2,6},{6,10},{... | collective-permute-start | bytes 589832 | tf_op jit(solution)/shard_map/ppermute | solution.py:365
  3.0 2.0 %collective-permute-start.4 = (bf16[64,1536]{1,0:T(8,128)(2,1)}, bf16[64,1536]{1,0:T(8,128)(2,1)S(1)}, u32[]{:S(2)}, u32[]{:S(2)}) collective-permute-start(bf16[64,1536]{1,0:T(8,128)(2,1)} %refs_0_.7), channel_id=1, source_target_pairs={{0,12},{4,0},{8,4},{12,8},{1,13},{5,1},{9,5},{13,9},{2,14},{6,2},{... | collective-permute-start | bytes 589832 | tf_op jit(solution)/shard_map/ppermute | solution.py:365
  6.4 3.8 %collective-permute-start.1 = (f32[16,64]{1,0:T(8,128)S(1)}, f32[16,64]{1,0:T(8,128)S(1)}, u32[]{:S(2)}, u32[]{:S(2)}) collective-permute-start(f32[16,64]{1,0:T(8,128)S(1)} %pad_maximum_fusion.2.refs_0_), channel_id=1, source_target_pairs={{0,12},{4,0},{8,4},{12,8},{1,13},{5,1},{9,5},{13,9},{2,14},{6,2},{... | collective-permute-start | bytes 12296 | tf_op jit(solution)/shard_map/ppermute | solution.py:325
  10.3 0.8 collective-permute-done.3.refs_1_
  11.1 2.9 %collective-permute-done.4.refs_2_ = bf16[64,1536]{1,0:T(8,128)(2,1)S(1)} collective-permute-done((bf16[64,1536]{1,0:T(8,128)(2,1)}, bf16[64,1536]{1,0:T(8,128)(2,1)S(1)}, u32[]{:S(2)}, u32[]{:S(2)}) %collective-permute-start.4) | collective-permute-done | bytes 196640 | tf_op jit(solution)/shard_map/ppermute | solution.py:365
  14.0 3.2 %collective-permute-start.6 = (bf16[32,1536]{1,0:T(8,128)(2,1)S(1)}, bf16[32,1536]{1,0:T(8,128)(2,1)S(1)}, u32[]{:S(2)}, u32[]{:S(2)}) collective-permute-start(bf16[32,1536]{1,0:T(8,128)(2,1)S(1)} %slice.111), channel_id=1, source_target_pairs={{0,12},{4,0},{8,4},{12,8},{1,13},{5,1},{9,5},{13,9},{2,14},{6,2},{... | collective-permute-start | bytes 294920 | tf_op jit(solution)/shard_map/ppermute | solution.py:369
  19.0 1.6 %route.1 = (f32[8,256]{1,0:T(8,128)}, f32[8,256]{1,0:T(8,128)}, s32[8,128]{1,0:T(8,128)}) custom-call(s32[2]{0:T(128)} %pad_add_fusion.info, f32[16,64]{1,0:T(8,128)} %copy-done.5, f32[16,64]{1,0:T(8,128)} %copy-done.6, f32[16,64]{1,0:T(8,128)} %copy-done.7, f32[16,64]{1,0:T(8,128)} %copy-done.8), custom_call_target="tpu_custom_call" | custom-call | tf_op jit(solution)/shard_map/route/pallas_call | solution.py:75
  20.6 0.9 copy-done
  22.9 8.0 %gate_up.4 = (bf16[2,256,512]{2,1,0:T(8,128)(2,1)S(1)}, bf16[2,256,512]{2,1,0:T(8,128)(2,1)S(1)}) custom-call(s32[8,128]{1,0:T(8,128)S(1)} %copy-done.2, bf16[64,1536]{1,0:T(8,128)(2,1)S(1)} %copy-done, bf16[64,1536]{1,0:T(8,128)(2,1)S(1)} %collective-permute-done.3.refs_1_, bf16[64,1536]{1,0:T(8,128)(2,1)S(1)} %collective-permute-done.4.refs_2_, ...), custom_call_target="tpu_custom_call" | custom-call | flops 6442450944 | bytes 12582912 | tf_op jit(solution)/shard_map/gate_up/pallas_call | solution.py:162
  31.0 1.9 %collective-permute-done.7 = bf16[2,256,512]{2,1,0:T(8,128)(2,1)S(1)} collective-permute-done((bf16[2,256,512]{2,1,0:T(8,128)(2,1)S(1)}, bf16[2,256,512]{2,1,0:T(8,128)(2,1)S(1)}, u32[]{:S(2)}, u32[]{:S(2)}) %collective-permute-start.7) | collective-permute-done | bytes 524320 | tf_op jit(solution)/shard_map/ppermute | solution.py:23
  33.1 1.6 %collective-permute-start.9 = (bf16[1,256,512]{2,1,0:T(8,128)(2,1)S(1)}, bf16[1,256,512]{2,1,0:T(8,128)(2,1)S(1)}, u32[]{:S(2)}, u32[]{:S(2)}) collective-permute-start(bf16[1,256,512]{2,1,0:T(8,128)(2,1)S(1)} %slice.159.refs_8_), channel_id=1, source_target_pairs={{0,2},{1,3},{2,0},{3,1},{4,6},{5,7},{6,4},{7,5},{8,10},{9,11},{10,... | collective-permute-start | bytes 786440 | tf_op jit(solution)/shard_map/ppermute | solution.py:23
  34.7 8.0 %gate_up.5 = (bf16[2,256,512]{2,1,0:T(8,128)(2,1)S(1)}, bf16[2,256,512]{2,1,0:T(8,128)(2,1)S(1)}) custom-call(s32[8,128]{1,0:T(8,128)S(1)} %copy-done.2, bf16[64,1536]{1,0:T(8,128)(2,1)S(1)} %copy-done, bf16[64,1536]{1,0:T(8,128)(2,1)S(1)} %collective-permute-done.3.refs_1_, bf16[64,1536]{1,0:T(8,128)(2,1)S(1)} %collective-permute-done.4.refs_2_, ...), custom_call_target="tpu_custom_call" | custom-call | flops 6442450944 | bytes 12582912 | tf_op jit(solution)/shard_map/gate_up/pallas_call | solution.py:162
  43.0 1.7 %collective-permute-done.8 = bf16[2,256,512]{2,1,0:T(8,128)(2,1)S(1)} collective-permute-done((bf16[2,256,512]{2,1,0:T(8,128)(2,1)S(1)}, bf16[2,256,512]{2,1,0:T(8,128)(2,1)S(1)}, u32[]{:S(2)}, u32[]{:S(2)}) %collective-permute-start.8) | collective-permute-done | bytes 524320 | tf_op jit(solution)/shard_map/ppermute | solution.py:23
  45.5 8.0 %gate_up.6 = (bf16[2,256,512]{2,1,0:T(8,128)(2,1)S(1)}, bf16[2,256,512]{2,1,0:T(8,128)(2,1)S(1)}) custom-call(s32[8,128]{1,0:T(8,128)S(1)} %copy-done.2, bf16[64,1536]{1,0:T(8,128)(2,1)S(1)} %copy-done, bf16[64,1536]{1,0:T(8,128)(2,1)S(1)} %collective-permute-done.3.refs_1_, bf16[64,1536]{1,0:T(8,128)(2,1)S(1)} %collective-permute-done.4.refs_2_, ...), custom_call_target="tpu_custom_call" | custom-call | flops 6442450944 | bytes 12582912 | tf_op jit(solution)/shard_map/gate_up/pallas_call | solution.py:162
  53.6 1.6 %collective-permute-start.15 = (bf16[1,256,256]{2,1,0:T(8,128)(2,1)S(1)}, bf16[1,256,256]{2,1,0:T(8,128)(2,1)S(1)}, u32[]{:S(2)}, u32[]{:S(2)}) collective-permute-start(bf16[1,256,256]{2,1,0:T(8,128)(2,1)S(1)} %fusion.3.refs_9_.refs_0_), channel_id=1, source_target_pairs={{0,2},{1,3},{2,0},{3,1},{4,6},{5,7},{6,4},{7,5},{8,10},{9,11},{10,... | collective-permute-start | bytes 393224 | tf_op jit(solution)/shard_map/ppermute | solution.py:23
  56.1 1.6 %collective-permute-start.17 = (bf16[1,256,512]{2,1,0:T(8,128)(2,1)S(1)}, bf16[1,256,512]{2,1,0:T(8,128)(2,1)S(1)}, u32[]{:S(2)}, u32[]{:S(2)}) collective-permute-start(bf16[1,256,512]{2,1,0:T(8,128)(2,1)S(1)} %slice.157.refs_8_), channel_id=1, source_target_pairs={{0,2},{1,3},{2,0},{3,1},{4,6},{5,7},{6,4},{7,5},{8,10},{9,11},{10,... | collective-permute-start | bytes 786440 | tf_op jit(solution)/shard_map/ppermute | solution.py:23
  57.7 8.2 %gate_up.7 = (bf16[2,256,512]{2,1,0:T(8,128)(2,1)S(1)}, bf16[2,256,512]{2,1,0:T(8,128)(2,1)S(1)}) custom-call(s32[8,128]{1,0:T(8,128)S(1)} %copy-done.2, bf16[64,1536]{1,0:T(8,128)(2,1)S(1)} %copy-done, bf16[64,1536]{1,0:T(8,128)(2,1)S(1)} %collective-permute-done.3.refs_1_, bf16[64,1536]{1,0:T(8,128)(2,1)S(1)} %collective-permute-done.4.refs_2_, ...), custom_call_target="tpu_custom_call" | custom-call | flops 6442450944 | bytes 12582912 | tf_op jit(solution)/shard_map/gate_up/pallas_call | solution.py:162
  67.0 0.9 collective-permute-done.17
  68.1 1.6 %collective-permute-start.22 = (bf16[1,256,256]{2,1,0:T(8,128)(2,1)S(1)}, bf16[1,256,256]{2,1,0:T(8,128)(2,1)S(1)}, u32[]{:S(2)}, u32[]{:S(2)}) collective-permute-start(bf16[1,256,256]{2,1,0:T(8,128)(2,1)S(1)} %fusion.1.refs_8_.refs_0_), channel_id=1, source_target_pairs={{0,2},{1,3},{2,0},{3,1},{4,6},{5,7},{6,4},{7,5},{8,10},{9,11},{10,... | collective-permute-start | bytes 393224 | tf_op jit(solution)/shard_map/ppermute | solution.py:23
  70.2 3.9 %collective-permute-done.22.refs_2_ = bf16[1,256,256]{2,1,0:T(8,128)(2,1)S(1)} collective-permute-done((bf16[1,256,256]{2,1,0:T(8,128)(2,1)S(1)}, bf16[1,256,256]{2,1,0:T(8,128)(2,1)S(1)}, u32[]{:S(2)}, u32[]{:S(2)}) %collective-permute-start.22) | collective-permute-done | bytes 131104 | tf_op jit(solution)/shard_map/ppermute | solution.py:23
  74.1 1.5 %collective-permute-start.13 = (bf16[1,256,512]{2,1,0:T(8,128)(2,1)S(1)}, bf16[1,256,512]{2,1,0:T(8,128)(2,1)S(1)}, u32[]{:S(2)}, u32[]{:S(2)}) collective-permute-start(bf16[1,256,512]{2,1,0:T(8,128)(2,1)S(1)} %slice.156.refs_7_), channel_id=1, source_target_pairs={{0,2},{1,3},{2,0},{3,1},{4,6},{5,7},{6,4},{7,5},{8,10},{9,11},{10,... | collective-permute-start | bytes 786440 | tf_op jit(solution)/shard_map/ppermute | solution.py:23
  75.6 4.5 %down.4.refs_7_ = f32[256,1536]{1,0:T(8,128)S(1)} custom-call(s32[8,128]{1,0:T(8,128)S(1)} %copy-done.3, bf16[1,256,256]{2,1,0:T(8,128)(2,1)S(1)} %fusion.3.refs_9_.refs_0_, bf16[1,256,256]{2,1,0:T(8,128)(2,1)S(1)} %collective-permute-done.14.refs_1_, bf16[1,256,256]{2,1,0:T(8,128)(2,1)S(1)} %collective-permute-done.15.refs_2_, ...), custom_call_target="tpu_custom_call" | custom-call | flops 4026531840 | bytes 9437184 | tf_op jit(solution)/shard_map/down/pallas_call | solution.py:253
  80.1 2.7 %collective-permute-done.13 = bf16[1,256,512]{2,1,0:T(8,128)(2,1)S(1)} collective-permute-done((bf16[1,256,512]{2,1,0:T(8,128)(2,1)S(1)}, bf16[1,256,512]{2,1,0:T(8,128)(2,1)S(1)}, u32[]{:S(2)}, u32[]{:S(2)}) %collective-permute-start.13) | collective-permute-done | bytes 262176 | tf_op jit(solution)/shard_map/ppermute | solution.py:23
  83.0 1.6 %collective-permute-start.19 = (bf16[1,256,256]{2,1,0:T(8,128)(2,1)S(1)}, bf16[1,256,256]{2,1,0:T(8,128)(2,1)S(1)}, u32[]{:S(2)}, u32[]{:S(2)}) collective-permute-start(bf16[1,256,256]{2,1,0:T(8,128)(2,1)S(1)} %fusion.refs_8_.refs_0_), channel_id=1, source_target_pairs={{0,2},{1,3},{2,0},{3,1},{4,6},{5,7},{6,4},{7,5},{8,10},{9,11},{10,... | collective-permute-start | bytes 393224 | tf_op jit(solution)/shard_map/ppermute | solution.py:23
  84.6 4.5 %down.5.refs_7_ = f32[256,1536]{1,0:T(8,128)S(1)} custom-call(s32[8,128]{1,0:T(8,128)S(1)} %copy-done.3, bf16[1,256,256]{2,1,0:T(8,128)(2,1)S(1)} %fusion.2.refs_9_.refs_0_, bf16[1,256,256]{2,1,0:T(8,128)(2,1)S(1)} %collective-permute-done.24.refs_1_, bf16[1,256,256]{2,1,0:T(8,128)(2,1)S(1)} %collective-permute-done.25.refs_2_, ...), custom_call_target="tpu_custom_call" | custom-call | flops 4026531840 | bytes 9437184 | tf_op jit(solution)/shard_map/down/pallas_call | solution.py:253
  89.7 4.5 %down.6.refs_7_ = f32[256,1536]{1,0:T(8,128)S(1)} custom-call(s32[8,128]{1,0:T(8,128)S(1)} %copy-done.3, bf16[1,256,256]{2,1,0:T(8,128)(2,1)S(1)} %fusion.1.refs_8_.refs_0_, bf16[1,256,256]{2,1,0:T(8,128)(2,1)S(1)} %collective-permute-done.21.refs_1_, bf16[1,256,256]{2,1,0:T(8,128)(2,1)S(1)} %collective-permute-done.22.refs_2_, ...), custom_call_target="tpu_custom_call" | custom-call | flops 4026531840 | bytes 9437184 | tf_op jit(solution)/shard_map/down/pallas_call | solution.py:253
  94.3 4.5 %down.7 = (bf16[64,1536]{1,0:T(8,128)(2,1)S(1)}, bf16[64,1536]{1,0:T(8,128)(2,1)S(1)}, bf16[64,1536]{1,0:T(8,128)(2,1)S(1)}, bf16[32,1536]{1,0:T(8,128)(2,1)S(1)}, bf16[32,1536]{1,0:T(8,128)(2,1)S(1)}) custom-call(s32[8,128]{1,0:T(8,128)S(1)} %copy-done.3, bf16[1,256,256]{2,1,0:T(8,128)(2,1)S(1)} %fusion.refs_8_.refs_0_, ...), custom_call_target="tpu_custom_call" | custom-call | flops 4026531840 | bytes 9437184 | tf_op jit(solution)/shard_map/down/pallas_call | solution.py:253
  98.8 3.0 %collective-permute-start.27 = (bf16[32,1536]{1,0:T(8,128)(2,1)S(1)}, bf16[32,1536]{1,0:T(8,128)(2,1)S(1)}, u32[]{:S(2)}, u32[]{:S(2)}) collective-permute-start(bf16[32,1536]{1,0:T(8,128)(2,1)S(1)} %get-tuple-element.36), channel_id=1, source_target_pairs={{0,12},{4,0},{8,4},{12,8},{1,13},{5,1},{9,5},{13,9},{2,14},{6,2},{... | collective-permute-start | bytes 294920 | tf_op jit(solution)/shard_map/ppermute | solution.py:381
  101.9 3.1 %collective-permute-done.27 = bf16[32,1536]{1,0:T(8,128)(2,1)S(1)} collective-permute-done((bf16[32,1536]{1,0:T(8,128)(2,1)S(1)}, bf16[32,1536]{1,0:T(8,128)(2,1)S(1)}, u32[]{:S(2)}, u32[]{:S(2)}) %collective-permute-start.27) | collective-permute-done | bytes 98336 | tf_op jit(solution)/shard_map/ppermute | solution.py:381
  105.1 4.3 %collective-permute-start.28 = (bf16[64,1536]{1,0:T(8,128)(2,1)S(1)}, bf16[64,1536]{1,0:T(8,128)(2,1)S(1)}, u32[]{:S(2)}, u32[]{:S(2)}) collective-permute-start(bf16[64,1536]{1,0:T(8,128)(2,1)S(1)} %pad_maximum_fusion), channel_id=1, source_target_pairs={{0,12},{4,0},{8,4},{12,8},{1,13},{5,1},{9,5},{13,9},{2,14},{6,2},{... | collective-permute-start | bytes 589832 | tf_op jit(solution)/shard_map/ppermute | solution.py:390
  109.6 4.6 %collective-permute-done.28 = bf16[64,1536]{1,0:T(8,128)(2,1)S(1)} collective-permute-done((bf16[64,1536]{1,0:T(8,128)(2,1)S(1)}, bf16[64,1536]{1,0:T(8,128)(2,1)S(1)}, u32[]{:S(2)}, u32[]{:S(2)}) %collective-permute-start.28) | collective-permute-done | bytes 196640 | tf_op jit(solution)/shard_map/ppermute | solution.py:390
  114.2 3.1 %collective-permute-done.30 = bf16[64,1536]{1,0:T(8,128)(2,1)S(1)} collective-permute-done((bf16[64,1536]{1,0:T(8,128)(2,1)S(1)}, bf16[64,1536]{1,0:T(8,128)(2,1)S(1)}, u32[]{:S(2)}, u32[]{:S(2)}) %collective-permute-start.30) | collective-permute-done | bytes 196640 | tf_op jit(solution)/shard_map/ppermute | solution.py:391
  (85 shorter events, 10.3 us)
Async XLA Ops:
  0.0 11.0 %collective-permute-start.3 = (bf16[64,1536]{1,0:T(8,128)(2,1)}, bf16[64,1536]{1,0:T(8,128)(2,1)S(1)}, u32[]{:S(2)}, u32[]{:S(2)}) collective-permute-start(bf16[64,1536]{1,0:T(8,128)(2,1)} %refs_0_.7), channel_id=1, source_target_pairs={{0,4},{4,8},{8,12},{12,0},{1,5},{5,9},{9,13},{13,1},{2,6},{6,10},{... | collective-permute-start | bytes 589832 | tf_op jit(solution)/shard_map/ppermute | solution.py:365
  3.0 11.0 %collective-permute-start.4 = (bf16[64,1536]{1,0:T(8,128)(2,1)}, bf16[64,1536]{1,0:T(8,128)(2,1)S(1)}, u32[]{:S(2)}, u32[]{:S(2)}) collective-permute-start(bf16[64,1536]{1,0:T(8,128)(2,1)} %refs_0_.7), channel_id=1, source_target_pairs={{0,12},{4,0},{8,4},{12,8},{1,13},{5,1},{9,5},{13,9},{2,14},{6,2},{... | collective-permute-start | bytes 589832 | tf_op jit(solution)/shard_map/ppermute | solution.py:365
  6.4 11.3 %collective-permute-start = (f32[16,64]{1,0:T(8,128)S(1)}, f32[16,64]{1,0:T(8,128)S(1)}, u32[]{:S(2)}, u32[]{:S(2)}) collective-permute-start(f32[16,64]{1,0:T(8,128)S(1)} %pad_maximum_fusion.2.refs_0_), channel_id=1, source_target_pairs={{0,4},{4,8},{8,12},{12,0},{1,5},{5,9},{9,13},{13,1},{2,6},{6,10},{... | collective-permute-start | bytes 12296 | tf_op jit(solution)/shard_map/ppermute | solution.py:325
  6.4 11.3 %collective-permute-start.1 = (f32[16,64]{1,0:T(8,128)S(1)}, f32[16,64]{1,0:T(8,128)S(1)}, u32[]{:S(2)}, u32[]{:S(2)}) collective-permute-start(f32[16,64]{1,0:T(8,128)S(1)} %pad_maximum_fusion.2.refs_0_), channel_id=1, source_target_pairs={{0,12},{4,0},{8,4},{12,8},{1,13},{5,1},{9,5},{13,9},{2,14},{6,2},{... | collective-permute-start | bytes 12296 | tf_op jit(solution)/shard_map/ppermute | solution.py:325
  10.3 7.5 %collective-permute-start.2 = (f32[16,64]{1,0:T(8,128)S(1)}, f32[16,64]{1,0:T(8,128)S(1)}, u32[]{:S(2)}, u32[]{:S(2)}) collective-permute-start(f32[16,64]{1,0:T(8,128)S(1)} %pad_maximum_fusion.2.refs_0_), channel_id=1, source_target_pairs={{0,8},{4,12},{8,0},{12,4},{1,9},{5,13},{9,1},{13,5},{2,10},{6,14},... | collective-permute-start | bytes 12296 | tf_op jit(solution)/shard_map/ppermute | solution.py:325
  11.0 9.5 %collective-permute-start.5 = (bf16[32,1536]{1,0:T(8,128)(2,1)S(1)}, bf16[32,1536]{1,0:T(8,128)(2,1)S(1)}, u32[]{:S(2)}, u32[]{:S(2)}) collective-permute-start(bf16[32,1536]{1,0:T(8,128)(2,1)S(1)} %slice.110), channel_id=1, source_target_pairs={{0,4},{4,8},{8,12},{12,0},{1,5},{5,9},{9,13},{13,1},{2,6},{6,10},{... | collective-permute-start | bytes 294920 | tf_op jit(solution)/shard_map/ppermute | solution.py:369
  14.0 6.6 %collective-permute-start.6 = (bf16[32,1536]{1,0:T(8,128)(2,1)S(1)}, bf16[32,1536]{1,0:T(8,128)(2,1)S(1)}, u32[]{:S(2)}, u32[]{:S(2)}) collective-permute-start(bf16[32,1536]{1,0:T(8,128)(2,1)S(1)} %slice.111), channel_id=1, source_target_pairs={{0,12},{4,0},{8,4},{12,8},{1,13},{5,1},{9,5},{13,9},{2,14},{6,2},{... | collective-permute-start | bytes 294920 | tf_op jit(solution)/shard_map/ppermute | solution.py:369
  30.9 2.0 %collective-permute-start.7 = (bf16[2,256,512]{2,1,0:T(8,128)(2,1)S(1)}, bf16[2,256,512]{2,1,0:T(8,128)(2,1)S(1)}, u32[]{:S(2)}, u32[]{:S(2)}) collective-permute-start(bf16[2,256,512]{2,1,0:T(8,128)(2,1)S(1)} %get-tuple-element.25), channel_id=1, source_target_pairs={{0,1},{1,0},{2,3},{3,2},{4,5},{5,4},{6,7},{7,6},{8,9},{9,8},{10,11... | collective-permute-start | bytes 1572872 | tf_op jit(solution)/shard_map/ppermute | solution.py:23
  33.1 9.7 %collective-permute-start.9 = (bf16[1,256,512]{2,1,0:T(8,128)(2,1)S(1)}, bf16[1,256,512]{2,1,0:T(8,128)(2,1)S(1)}, u32[]{:S(2)}, u32[]{:S(2)}) collective-permute-start(bf16[1,256,512]{2,1,0:T(8,128)(2,1)S(1)} %slice.159.refs_8_), channel_id=1, source_target_pairs={{0,2},{1,3},{2,0},{3,1},{4,6},{5,7},{6,4},{7,5},{8,10},{9,11},{10,... | collective-permute-start | bytes 786440 | tf_op jit(solution)/shard_map/ppermute | solution.py:23
  42.7 2.0 %collective-permute-start.8 = (bf16[2,256,512]{2,1,0:T(8,128)(2,1)S(1)}, bf16[2,256,512]{2,1,0:T(8,128)(2,1)S(1)}, u32[]{:S(2)}, u32[]{:S(2)}) collective-permute-start(bf16[2,256,512]{2,1,0:T(8,128)(2,1)S(1)} %get-tuple-element.27), channel_id=1, source_target_pairs={{0,1},{1,0},{2,3},{3,2},{4,5},{5,4},{6,7},{7,6},{8,9},{9,8},{10,11... | collective-permute-start | bytes 1572872 | tf_op jit(solution)/shard_map/ppermute | solution.py:23
  44.9 10.3 %collective-permute-start.11 = (bf16[1,256,512]{2,1,0:T(8,128)(2,1)S(1)}, bf16[1,256,512]{2,1,0:T(8,128)(2,1)S(1)}, u32[]{:S(2)}, u32[]{:S(2)}) collective-permute-start(bf16[1,256,512]{2,1,0:T(8,128)(2,1)S(1)} %slice.158.refs_8_), channel_id=1, source_target_pairs={{0,2},{1,3},{2,0},{3,1},{4,6},{5,7},{6,4},{7,5},{8,10},{9,11},{10,... | collective-permute-start | bytes 786440 | tf_op jit(solution)/shard_map/ppermute | solution.py:23
  53.5 2.4 %collective-permute-start.10 = (bf16[2,256,512]{2,1,0:T(8,128)(2,1)S(1)}, bf16[2,256,512]{2,1,0:T(8,128)(2,1)S(1)}, u32[]{:S(2)}, u32[]{:S(2)}) collective-permute-start(bf16[2,256,512]{2,1,0:T(8,128)(2,1)S(1)} %get-tuple-element.29), channel_id=1, source_target_pairs={{0,1},{1,0},{2,3},{3,2},{4,5},{5,4},{6,7},{7,6},{8,9},{9,8},{10,11... | collective-permute-start | bytes 1572872 | tf_op jit(solution)/shard_map/ppermute | solution.py:23
  53.6 12.9 %collective-permute-start.15 = (bf16[1,256,256]{2,1,0:T(8,128)(2,1)S(1)}, bf16[1,256,256]{2,1,0:T(8,128)(2,1)S(1)}, u32[]{:S(2)}, u32[]{:S(2)}) collective-permute-start(bf16[1,256,256]{2,1,0:T(8,128)(2,1)S(1)} %fusion.3.refs_9_.refs_0_), channel_id=1, source_target_pairs={{0,2},{1,3},{2,0},{3,1},{4,6},{5,7},{6,4},{7,5},{8,10},{9,11},{10,... | collective-permute-start | bytes 393224 | tf_op jit(solution)/shard_map/ppermute | solution.py:23
  55.3 11.3 %collective-permute-start.25 = (bf16[1,256,256]{2,1,0:T(8,128)(2,1)S(1)}, bf16[1,256,256]{2,1,0:T(8,128)(2,1)S(1)}, u32[]{:S(2)}, u32[]{:S(2)}) collective-permute-start(bf16[1,256,256]{2,1,0:T(8,128)(2,1)S(1)} %fusion.2.refs_9_.refs_0_), channel_id=1, source_target_pairs={{0,2},{1,3},{2,0},{3,1},{4,6},{5,7},{6,4},{7,5},{8,10},{9,11},{10,... | collective-permute-start | bytes 393224 | tf_op jit(solution)/shard_map/ppermute | solution.py:23
  56.1 19.5 %copy-start.3 = (s32[8,128]{1,0:T(8,128)S(1)}, s32[8,128]{1,0:T(8,128)}, u32[]{:S(2)}) copy-start(s32[8,128]{1,0:T(8,128)} %get-tuple-element.22.sched_in) | copy-start | bytes 12292
  56.1 11.8 %collective-permute-start.17 = (bf16[1,256,512]{2,1,0:T(8,128)(2,1)S(1)}, bf16[1,256,512]{2,1,0:T(8,128)(2,1)S(1)}, u32[]{:S(2)}, u32[]{:S(2)}) collective-permute-start(bf16[1,256,512]{2,1,0:T(8,128)(2,1)S(1)} %slice.157.refs_8_), channel_id=1, source_target_pairs={{0,2},{1,3},{2,0},{3,1},{4,6},{5,7},{6,4},{7,5},{8,10},{9,11},{10,... | collective-permute-start | bytes 786440 | tf_op jit(solution)/shard_map/ppermute | solution.py:23
  65.9 2.2 %collective-permute-start.12 = (bf16[2,256,512]{2,1,0:T(8,128)(2,1)S(1)}, bf16[2,256,512]{2,1,0:T(8,128)(2,1)S(1)}, u32[]{:S(2)}, u32[]{:S(2)}) collective-permute-start(bf16[2,256,512]{2,1,0:T(8,128)(2,1)S(1)} %get-tuple-element.31), channel_id=1, source_target_pairs={{0,1},{1,0},{2,3},{3,2},{4,5},{5,4},{6,7},{7,6},{8,9},{9,8},{10,11... | collective-permute-start | bytes 1572872 | tf_op jit(solution)/shard_map/ppermute | solution.py:23
  66.0 3.9 %collective-permute-start.14 = (bf16[1,256,256]{2,1,0:T(8,128)(2,1)S(1)}, bf16[1,256,256]{2,1,0:T(8,128)(2,1)S(1)}, u32[]{:S(2)}, u32[]{:S(2)}) collective-permute-start(bf16[1,256,256]{2,1,0:T(8,128)(2,1)S(1)} %fusion.3.refs_9_.refs_0_), channel_id=1, source_target_pairs={{0,1},{1,0},{2,3},{3,2},{4,5},{5,4},{6,7},{7,6},{8,9},{9,8},{10,11... | collective-permute-start | bytes 393224 | tf_op jit(solution)/shard_map/ppermute | solution.py:23
  66.5 7.6 %collective-permute-start.16 = (bf16[1,256,256]{2,1,0:T(8,128)(2,1)S(1)}, bf16[1,256,256]{2,1,0:T(8,128)(2,1)S(1)}, u32[]{:S(2)}, u32[]{:S(2)}) collective-permute-start(bf16[1,256,256]{2,1,0:T(8,128)(2,1)S(1)} %collective-permute-done.15.refs_2_), channel_id=1, source_target_pairs={{0,1},{1,0},{2,3},{3,2},{4,5},{5,4},{6,7},{7,6},{8,9},{9,8},{10,11... | collective-permute-start | bytes 393224 | tf_op jit(solution)/shard_map/ppermute | solution.py:23
  66.6 18.0 %collective-permute-start.24 = (bf16[1,256,256]{2,1,0:T(8,128)(2,1)S(1)}, bf16[1,256,256]{2,1,0:T(8,128)(2,1)S(1)}, u32[]{:S(2)}, u32[]{:S(2)}) collective-permute-start(bf16[1,256,256]{2,1,0:T(8,128)(2,1)S(1)} %fusion.2.refs_9_.refs_0_), channel_id=1, source_target_pairs={{0,1},{1,0},{2,3},{3,2},{4,5},{5,4},{6,7},{7,6},{8,9},{9,8},{10,11... | collective-permute-start | bytes 393224 | tf_op jit(solution)/shard_map/ppermute | solution.py:23
  67.9 16.6 %collective-permute-start.26 = (bf16[1,256,256]{2,1,0:T(8,128)(2,1)S(1)}, bf16[1,256,256]{2,1,0:T(8,128)(2,1)S(1)}, u32[]{:S(2)}, u32[]{:S(2)}) collective-permute-start(bf16[1,256,256]{2,1,0:T(8,128)(2,1)S(1)} %collective-permute-done.25.refs_2_), channel_id=1, source_target_pairs={{0,1},{1,0},{2,3},{3,2},{4,5},{5,4},{6,7},{7,6},{8,9},{9,8},{10,11... | collective-permute-start | bytes 393224 | tf_op jit(solution)/shard_map/ppermute | solution.py:23
  68.1 6.0 %collective-permute-start.22 = (bf16[1,256,256]{2,1,0:T(8,128)(2,1)S(1)}, bf16[1,256,256]{2,1,0:T(8,128)(2,1)S(1)}, u32[]{:S(2)}, u32[]{:S(2)}) collective-permute-start(bf16[1,256,256]{2,1,0:T(8,128)(2,1)S(1)} %fusion.1.refs_8_.refs_0_), channel_id=1, source_target_pairs={{0,2},{1,3},{2,0},{3,1},{4,6},{5,7},{6,4},{7,5},{8,10},{9,11},{10,... | collective-permute-start | bytes 393224 | tf_op jit(solution)/shard_map/ppermute | solution.py:23
  69.9 19.8 %collective-permute-start.21 = (bf16[1,256,256]{2,1,0:T(8,128)(2,1)S(1)}, bf16[1,256,256]{2,1,0:T(8,128)(2,1)S(1)}, u32[]{:S(2)}, u32[]{:S(2)}) collective-permute-start(bf16[1,256,256]{2,1,0:T(8,128)(2,1)S(1)} %fusion.1.refs_8_.refs_0_), channel_id=1, source_target_pairs={{0,1},{1,0},{2,3},{3,2},{4,5},{5,4},{6,7},{7,6},{8,9},{9,8},{10,11... | collective-permute-start | bytes 393224 | tf_op jit(solution)/shard_map/ppermute | solution.py:23
  74.1 15.6 %collective-permute-start.23 = (bf16[1,256,256]{2,1,0:T(8,128)(2,1)S(1)}, bf16[1,256,256]{2,1,0:T(8,128)(2,1)S(1)}, u32[]{:S(2)}, u32[]{:S(2)}) collective-permute-start(bf16[1,256,256]{2,1,0:T(8,128)(2,1)S(1)} %collective-permute-done.22.refs_2_), channel_id=1, source_target_pairs={{0,1},{1,0},{2,3},{3,2},{4,5},{5,4},{6,7},{7,6},{8,9},{9,8},{10,11... | collective-permute-start | bytes 393224 | tf_op jit(solution)/shard_map/ppermute | solution.py:23
  74.1 8.7 %collective-permute-start.13 = (bf16[1,256,512]{2,1,0:T(8,128)(2,1)S(1)}, bf16[1,256,512]{2,1,0:T(8,128)(2,1)S(1)}, u32[]{:S(2)}, u32[]{:S(2)}) collective-permute-start(bf16[1,256,512]{2,1,0:T(8,128)(2,1)S(1)} %slice.156.refs_7_), channel_id=1, source_target_pairs={{0,2},{1,3},{2,0},{3,1},{4,6},{5,7},{6,4},{7,5},{8,10},{9,11},{10,... | collective-permute-start | bytes 786440 | tf_op jit(solution)/shard_map/ppermute | solution.py:23
  83.0 6.1 %collective-permute-start.19 = (bf16[1,256,256]{2,1,0:T(8,128)(2,1)S(1)}, bf16[1,256,256]{2,1,0:T(8,128)(2,1)S(1)}, u32[]{:S(2)}, u32[]{:S(2)}) collective-permute-start(bf16[1,256,256]{2,1,0:T(8,128)(2,1)S(1)} %fusion.refs_8_.refs_0_), channel_id=1, source_target_pairs={{0,2},{1,3},{2,0},{3,1},{4,6},{5,7},{6,4},{7,5},{8,10},{9,11},{10,... | collective-permute-start | bytes 393224 | tf_op jit(solution)/shard_map/ppermute | solution.py:23
  84.5 9.7 %collective-permute-start.18 = (bf16[1,256,256]{2,1,0:T(8,128)(2,1)S(1)}, bf16[1,256,256]{2,1,0:T(8,128)(2,1)S(1)}, u32[]{:S(2)}, u32[]{:S(2)}) collective-permute-start(bf16[1,256,256]{2,1,0:T(8,128)(2,1)S(1)} %fusion.refs_8_.refs_0_), channel_id=1, source_target_pairs={{0,1},{1,0},{2,3},{3,2},{4,5},{5,4},{6,7},{7,6},{8,9},{9,8},{10,11... | collective-permute-start | bytes 393224 | tf_op jit(solution)/shard_map/ppermute | solution.py:23
  89.1 5.1 %collective-permute-start.20 = (bf16[1,256,256]{2,1,0:T(8,128)(2,1)S(1)}, bf16[1,256,256]{2,1,0:T(8,128)(2,1)S(1)}, u32[]{:S(2)}, u32[]{:S(2)}) collective-permute-start(bf16[1,256,256]{2,1,0:T(8,128)(2,1)S(1)} %collective-permute-done.19.refs_2_), channel_id=1, source_target_pairs={{0,1},{1,0},{2,3},{3,2},{4,5},{5,4},{6,7},{7,6},{8,9},{9,8},{10,11... | collective-permute-start | bytes 393224 | tf_op jit(solution)/shard_map/ppermute | solution.py:23
  98.8 6.3 %collective-permute-start.27 = (bf16[32,1536]{1,0:T(8,128)(2,1)S(1)}, bf16[32,1536]{1,0:T(8,128)(2,1)S(1)}, u32[]{:S(2)}, u32[]{:S(2)}) collective-permute-start(bf16[32,1536]{1,0:T(8,128)(2,1)S(1)} %get-tuple-element.36), channel_id=1, source_target_pairs={{0,12},{4,0},{8,4},{12,8},{1,13},{5,1},{9,5},{13,9},{2,14},{6,2},{... | collective-permute-start | bytes 294920 | tf_op jit(solution)/shard_map/ppermute | solution.py:381
  101.8 7.6 %collective-permute-start.29 = (bf16[32,1536]{1,0:T(8,128)(2,1)S(1)}, bf16[32,1536]{1,0:T(8,128)(2,1)S(1)}, u32[]{:S(2)}, u32[]{:S(2)}) collective-permute-start(bf16[32,1536]{1,0:T(8,128)(2,1)S(1)} %get-tuple-element.38), channel_id=1, source_target_pairs={{0,4},{4,8},{8,12},{12,0},{1,5},{5,9},{9,13},{13,1},{2,6},{6,10},{... | collective-permute-start | bytes 294920 | tf_op jit(solution)/shard_map/ppermute | solution.py:381
  105.1 9.1 %collective-permute-start.28 = (bf16[64,1536]{1,0:T(8,128)(2,1)S(1)}, bf16[64,1536]{1,0:T(8,128)(2,1)S(1)}, u32[]{:S(2)}, u32[]{:S(2)}) collective-permute-start(bf16[64,1536]{1,0:T(8,128)(2,1)S(1)} %pad_maximum_fusion), channel_id=1, source_target_pairs={{0,12},{4,0},{8,4},{12,8},{1,13},{5,1},{9,5},{13,9},{2,14},{6,2},{... | collective-permute-start | bytes 589832 | tf_op jit(solution)/shard_map/ppermute | solution.py:390
  109.5 7.8 %collective-permute-start.30 = (bf16[64,1536]{1,0:T(8,128)(2,1)S(1)}, bf16[64,1536]{1,0:T(8,128)(2,1)S(1)}, u32[]{:S(2)}, u32[]{:S(2)}) collective-permute-start(bf16[64,1536]{1,0:T(8,128)(2,1)S(1)} %pad_maximum_fusion.1), channel_id=1, source_target_pairs={{0,4},{4,8},{8,12},{12,0},{1,5},{5,9},{9,13},{13,1},{2,6},{6,10},{... | collective-permute-start | bytes 589832 | tf_op jit(solution)/shard_map/ppermute | solution.py:391
  (8 other events, 34.9 us)

commit v3 on v2

--- a/solution.py
+++ b/solution.py
@@ -81,6 +81,7 @@
         ),
         in_specs=[SMEM] + [VMEM] * len(meta),
         out_specs=(VMEM,) * 3,
+        compiler_params=pltpu.CompilerParams(vmem_limit_bytes=40 << 20),
         name="route",
     )(info, *meta)
 
@@ -128,7 +129,13 @@
                 copies[l, m, x] = pltpu.make_async_copy(
                     w.at[e, :, units], held.at[i, :, pl.ds(l * width, width)], held_sem.at[l, i]
                 )
+
+    def fetch(l):
+        for m in range(2):
+            for x in range(len(experts)):
                 copies[l, m, x].start()
+
+    fetch(pieces[0])
     ranks.wait()
     r = lax.broadcasted_iota(jnp.int32, (count, at), 0).astype(jnp.float32)
     pick = jnp.where(r == rank[pl.ds(experts[0], 1), :], 1.0, 0.0)
@@ -139,8 +146,10 @@
     rows[...] = jnp.dot(
         pick.astype(jnp.bfloat16), feed[...], preferred_element_type=jnp.float32
     ).astype(jnp.bfloat16)
-    for l in pieces:
+    for l, ahead in zip(pieces, pieces[1:] + [None]):
         units = slice(l * width, (l + 1) * width)
+        if ahead is not None:
+            fetch(ahead)
         for m in range(2):
             sides = []
             for x, part in enumerate((rows[:most], rows[count - most :])[: len(experts)]):
@@ -342,12 +351,15 @@
         send, keep = gate_up(feeds, rank, sched, w_gate, w_up, c, rows, most, n_dp, after)
         mine, late, last_sent = partial_sums(send, keep, n_dp)
         sent.append(last_sent)
-        if c == chunks - 1 and c > 0:
-            total = add(0, [last_sent, shares[-1]])
-        shares.append(finish(mine, late, [] if total is None else [total]))
-        parts.append(all_parts(shares[-1], n_dp))
-    for c in range(1 if chunks > 1 else 0, chunks):
-        total = add(c, [shares[-1]] if c == 1 else [])
+        if c > 0:
+            parts.append(all_parts(lax.optimization_barrier((shares[-1], last_sent))[0], n_dp))
+        early = range(min(2, c)) if c == chunks - 1 else []
+        for d in early:
+            total = add(d, [last_sent, shares[-1]])
+        shares.append(finish(mine, late, [total] if early else []))
+    parts.append(all_parts(shares[-1], n_dp))
+    for c in range(len(early), chunks):
+        total = add(c, [shares[-1]] if c < chunks - 1 else [])
     return returned(total, "expert") if n_owner > 1 else total[0].astype(jnp.bfloat16)
 
 

time: 118 us -> 113 us (0.958)
  local copies, waits for them, and re-layouts: 3.63 us -> 1.09 us
  starting transfers between devices: 32.2 us -> 31 us
    ppermute x1, waiting for transfers between devices: 0.01 us -> 3.56 us  [returned(): lax.ppermute(partials[-1], axis, up)]
    ppermute x20, waiting for transfers between devices: 11.2 us -> 7.59 us  [flip(): lax.ppermute(x, axis, [(i, i ^ k) for i in range(lax.axis_size(axis))])]
    ppermute x1, waiting for transfers between devices: 3.13 us -> 5.72 us  [returned(): high = lax.ppermute(b.astype(jnp.bfloat16), axis, up)]
    unnamed x18 -> x2, local copies, waits for them, and re-layouts: 3.46 us -> 0.93 us
    ppermute x1, waiting for transfers between devices: 4.61 us -> 2.17 us  [returned(): low = lax.ppermute(a.astype(jnp.bfloat16), axis, down_)]
    ppermute x1, waiting for transfers between devices: 3.13 us -> 0.94 us  [returned(): lax.ppermute(partials[-2], axis, down_)]
    ppermute x1, starting transfers between devices: 0.05 us -> 1.67 us  [returned(): lax.ppermute(partials[-1], axis, up)]
    ppermute x1, starting transfers between devices: 4.33 us -> 2.93 us  [returned(): low = lax.ppermute(a.astype(jnp.bfloat16), axis, down_)]
  transfers between devices with their start and end apart: 31 -> 31, of which waited for: 10 -> 12; matrix products, arithmetic and copies ran while one was open for 3% -> 2% of each run, Pallas kernels for 33% -> 34%
where the time goes in v3:
time: 113 us; the launch traced here: 112 us
  Pallas kernels  51.2 us (45%)
  starting transfers between devices  31 us (27%)
  waiting for transfers between devices  25.2 us (22%)
  other arithmetic  3.48 us (3%)
    pallas_call x4, Pallas kernels, gate_up(): pl.pallas_call(functools.partial(gate_up_body, n, chunk, n_dp, most, len(...  32.3 us
    pallas_call x4, Pallas kernels, down(): pl.pallas_call(functools.partial(down_body, n_dp, cuts, chunk, first, mos...  18.1 us
    ppermute x20, starting transfers between devices, flip(): lax.ppermute(x, axis, [(i, i ^ k) for i in range(lax.axis_size(axis))])  11.8 us
    ppermute x20, waiting for transfers between devices, flip(): lax.ppermute(x, axis, [(i, i ^ k) for i in range(lax.axis_size(axis))])  7.59 us
    ppermute x1, waiting for transfers between devices, returned(): high = lax.ppermute(b.astype(jnp.bfloat16), axis, up)  5.72 us
    ppermute x3, starting transfers between devices, on_device(): lax.ppermute(meta, 'expert', [(i, (i - k) % n_owner) for i in range(n_own...  3.83 us
    ppermute x1, waiting for transfers between devices, returned(): lax.ppermute(partials[-1], axis, up)  3.56 us
    ppermute x1, starting transfers between devices, gathered(): lax.ppermute(above[half:], axis, down_)  3.15 us
  transfers between devices with their start and end apart: 31, of which 12 were waited for; matrix products, arithmetic and copies ran while one was open for 2% of the time, Pallas kernels for 34%

profile of v3, /device:TPU:0, one launch (start us, length us, event | category | flops | bytes accessed | tf_op | source)
XLA Modules:
  0.0 112.3 jit_solution(6762480224502844677)
XLA Ops:
  0.0 3.0 %collective-permute-start.3 = (bf16[64,1536]{1,0:T(8,128)(2,1)}, bf16[64,1536]{1,0:T(8,128)(2,1)S(1)}, u32[]{:S(2)}, u32[]{:S(2)}) collective-permute-start(bf16[64,1536]{1,0:T(8,128)(2,1)} %refs_0_.7), channel_id=1, source_target_pairs={{0,4},{4,8},{8,12},{12,0},{1,5},{5,9},{9,13},{13,1},{2,6},{6,10},{... | collective-permute-start | bytes 589832 | tf_op jit(solution)/shard_map/ppermute | solution.py:377
  3.0 2.0 %collective-permute-start.4 = (bf16[64,1536]{1,0:T(8,128)(2,1)}, bf16[64,1536]{1,0:T(8,128)(2,1)S(1)}, u32[]{:S(2)}, u32[]{:S(2)}) collective-permute-start(bf16[64,1536]{1,0:T(8,128)(2,1)} %refs_0_.7), channel_id=1, source_target_pairs={{0,12},{4,0},{8,4},{12,8},{1,13},{5,1},{9,5},{13,9},{2,14},{6,2},{... | collective-permute-start | bytes 589832 | tf_op jit(solution)/shard_map/ppermute | solution.py:377
  6.4 3.8 %collective-permute-start.1 = (f32[16,64]{1,0:T(8,128)S(1)}, f32[16,64]{1,0:T(8,128)S(1)}, u32[]{:S(2)}, u32[]{:S(2)}) collective-permute-start(f32[16,64]{1,0:T(8,128)S(1)} %pad_maximum_fusion.2.refs_0_), channel_id=1, source_target_pairs={{0,12},{4,0},{8,4},{12,8},{1,13},{5,1},{9,5},{13,9},{2,14},{6,2},{... | collective-permute-start | bytes 12296 | tf_op jit(solution)/shard_map/ppermute | solution.py:334
  10.3 0.8 collective-permute-done.3.refs_1_
  11.1 2.9 %collective-permute-done.4.refs_2_ = bf16[64,1536]{1,0:T(8,128)(2,1)S(1)} collective-permute-done((bf16[64,1536]{1,0:T(8,128)(2,1)}, bf16[64,1536]{1,0:T(8,128)(2,1)S(1)}, u32[]{:S(2)}, u32[]{:S(2)}) %collective-permute-start.4) | collective-permute-done | bytes 196640 | tf_op jit(solution)/shard_map/ppermute | solution.py:377
  14.0 3.2 %collective-permute-start.6 = (bf16[32,1536]{1,0:T(8,128)(2,1)S(1)}, bf16[32,1536]{1,0:T(8,128)(2,1)S(1)}, u32[]{:S(2)}, u32[]{:S(2)}) collective-permute-start(bf16[32,1536]{1,0:T(8,128)(2,1)S(1)} %slice.111), channel_id=1, source_target_pairs={{0,12},{4,0},{8,4},{12,8},{1,13},{5,1},{9,5},{13,9},{2,14},{6,2},{... | collective-permute-start | bytes 294920 | tf_op jit(solution)/shard_map/ppermute | solution.py:381
  18.7 0.9 collective-permute-done.6.refs_4_
  19.6 0.9 copy-done
  20.5 8.0 %gate_up.4 = (bf16[2,256,512]{2,1,0:T(8,128)(2,1)S(1)}, bf16[2,256,512]{2,1,0:T(8,128)(2,1)S(1)}) custom-call(s32[8,128]{1,0:T(8,128)S(1)} %get-tuple-element.25.sched_in, bf16[64,1536]{1,0:T(8,128)(2,1)S(1)} %copy-done, bf16[64,1536]{1,0:T(8,128)(2,1)S(1)} %collective-permute-done.3.refs_1_, bf16[64,1536]{1,0:T(8,128)(2,1)S(1)} %collective-permute-done.4.refs_2_, ...), custom_call_target="tpu_custom_call" | custom-call | flops 6442450944 | bytes 12582912 | tf_op jit(solution)/shard_map/gate_up/pallas_call | solution.py:171
  28.6 1.9 %collective-permute-done.7 = bf16[2,256,512]{2,1,0:T(8,128)(2,1)S(1)} collective-permute-done((bf16[2,256,512]{2,1,0:T(8,128)(2,1)S(1)}, bf16[2,256,512]{2,1,0:T(8,128)(2,1)S(1)}, u32[]{:S(2)}, u32[]{:S(2)}) %collective-permute-start.7) | collective-permute-done | bytes 524320 | tf_op jit(solution)/shard_map/ppermute | solution.py:23
  30.7 1.8 %collective-permute-start.9 = (bf16[1,256,512]{2,1,0:T(8,128)(2,1)S(1)}, bf16[1,256,512]{2,1,0:T(8,128)(2,1)S(1)}, u32[]{:S(2)}, u32[]{:S(2)}) collective-permute-start(bf16[1,256,512]{2,1,0:T(8,128)(2,1)S(1)} %slice.159.refs_8_), channel_id=1, source_target_pairs={{0,2},{1,3},{2,0},{3,1},{4,6},{5,7},{6,4},{7,5},{8,10},{9,11},{10,... | collective-permute-start | bytes 786440 | tf_op jit(solution)/shard_map/ppermute | solution.py:23
  32.5 8.0 %gate_up.5 = (bf16[2,256,512]{2,1,0:T(8,128)(2,1)S(1)}, bf16[2,256,512]{2,1,0:T(8,128)(2,1)S(1)}) custom-call(s32[8,128]{1,0:T(8,128)S(1)} %get-tuple-element.25.sched_in, bf16[64,1536]{1,0:T(8,128)(2,1)S(1)} %copy-done, bf16[64,1536]{1,0:T(8,128)(2,1)S(1)} %collective-permute-done.3.refs_1_, bf16[64,1536]{1,0:T(8,128)(2,1)S(1)} %collective-permute-done.4.refs_2_, ...), custom_call_target="tpu_custom_call" | custom-call | flops 6442450944 | bytes 12582912 | tf_op jit(solution)/shard_map/gate_up/pallas_call | solution.py:171
  40.8 1.7 %collective-permute-done.8 = bf16[2,256,512]{2,1,0:T(8,128)(2,1)S(1)} collective-permute-done((bf16[2,256,512]{2,1,0:T(8,128)(2,1)S(1)}, bf16[2,256,512]{2,1,0:T(8,128)(2,1)S(1)}, u32[]{:S(2)}, u32[]{:S(2)}) %collective-permute-start.8) | collective-permute-done | bytes 524320 | tf_op jit(solution)/shard_map/ppermute | solution.py:23
  43.1 8.0 %gate_up.6 = (bf16[2,256,512]{2,1,0:T(8,128)(2,1)S(1)}, bf16[2,256,512]{2,1,0:T(8,128)(2,1)S(1)}) custom-call(s32[8,128]{1,0:T(8,128)S(1)} %get-tuple-element.25.sched_in, bf16[64,1536]{1,0:T(8,128)(2,1)S(1)} %copy-done, bf16[64,1536]{1,0:T(8,128)(2,1)S(1)} %collective-permute-done.3.refs_1_, bf16[64,1536]{1,0:T(8,128)(2,1)S(1)} %collective-permute-done.4.refs_2_, ...), custom_call_target="tpu_custom_call" | custom-call | flops 6442450944 | bytes 12582912 | tf_op jit(solution)/shard_map/gate_up/pallas_call | solution.py:171
  51.2 1.8 %collective-permute-start.18 = (bf16[1,256,256]{2,1,0:T(8,128)(2,1)S(1)}, bf16[1,256,256]{2,1,0:T(8,128)(2,1)S(1)}, u32[]{:S(2)}, u32[]{:S(2)}) collective-permute-start(bf16[1,256,256]{2,1,0:T(8,128)(2,1)S(1)} %fusion.3.refs_9_.refs_0_), channel_id=1, source_target_pairs={{0,2},{1,3},{2,0},{3,1},{4,6},{5,7},{6,4},{7,5},{8,10},{9,11},{10,... | collective-permute-start | bytes 393224 | tf_op jit(solution)/shard_map/ppermute | solution.py:23
  53.4 1.7 %collective-permute-start.20 = (bf16[1,256,512]{2,1,0:T(8,128)(2,1)S(1)}, bf16[1,256,512]{2,1,0:T(8,128)(2,1)S(1)}, u32[]{:S(2)}, u32[]{:S(2)}) collective-permute-start(bf16[1,256,512]{2,1,0:T(8,128)(2,1)S(1)} %slice.157.refs_8_), channel_id=1, source_target_pairs={{0,2},{1,3},{2,0},{3,1},{4,6},{5,7},{6,4},{7,5},{8,10},{9,11},{10,... | collective-permute-start | bytes 786440 | tf_op jit(solution)/shard_map/ppermute | solution.py:23
  55.4 8.2 %gate_up.7 = (bf16[2,256,512]{2,1,0:T(8,128)(2,1)S(1)}, bf16[2,256,512]{2,1,0:T(8,128)(2,1)S(1)}) custom-call(s32[8,128]{1,0:T(8,128)S(1)} %get-tuple-element.25.sched_in, bf16[64,1536]{1,0:T(8,128)(2,1)S(1)} %copy-done, bf16[64,1536]{1,0:T(8,128)(2,1)S(1)} %collective-permute-done.3.refs_1_, bf16[64,1536]{1,0:T(8,128)(2,1)S(1)} %collective-permute-done.4.refs_2_, ...), custom_call_target="tpu_custom_call" | custom-call | flops 6442450944 | bytes 12582912 | tf_op jit(solution)/shard_map/gate_up/pallas_call | solution.py:171
  64.3 1.2 %collective-permute-done.15.refs_2_ = bf16[1,256,256]{2,1,0:T(8,128)(2,1)S(1)} collective-permute-done((bf16[1,256,256]{2,1,0:T(8,128)(2,1)S(1)}, bf16[1,256,256]{2,1,0:T(8,128)(2,1)S(1)}, u32[]{:S(2)}, u32[]{:S(2)}) %collective-permute-start.15) | collective-permute-done | bytes 131104 | tf_op jit(solution)/shard_map/ppermute | solution.py:23
  66.4 1.8 %collective-permute-start.13 = (bf16[1,256,512]{2,1,0:T(8,128)(2,1)S(1)}, bf16[1,256,512]{2,1,0:T(8,128)(2,1)S(1)}, u32[]{:S(2)}, u32[]{:S(2)}) collective-permute-start(bf16[1,256,512]{2,1,0:T(8,128)(2,1)S(1)} %slice.156.refs_7_.refs_8_), channel_id=1, source_target_pairs={{0,2},{1,3},{2,0},{3,1},{4,6},{5,7},{6,4},{7,5},{8,10},{9,11},{10,... | collective-permute-start | bytes 786440 | tf_op jit(solution)/shard_map/ppermute | solution.py:23
  68.5 4.5 %down.4.refs_7_ = f32[256,1536]{1,0:T(8,128)S(1)} custom-call(s32[8,128]{1,0:T(8,128)S(1)} %get-tuple-element.25.sched_in, bf16[1,256,256]{2,1,0:T(8,128)(2,1)S(1)} %fusion.3.refs_9_.refs_0_, bf16[1,256,256]{2,1,0:T(8,128)(2,1)S(1)} %collective-permute-done.17.refs_1_, bf16[1,256,256]{2,1,0:T(8,128)(2,1)S(1)} %collective-permute-done.18.refs_2_, ...), custom_call_target="tpu_custom_call" | custom-call | flops 4026531840 | bytes 9437184 | tf_op jit(solution)/shard_map/down/pallas_call | solution.py:262
  73.1 4.5 %down.5.refs_7_ = f32[256,1536]{1,0:T(8,128)S(1)} custom-call(s32[8,128]{1,0:T(8,128)S(1)} %get-tuple-element.25.sched_in, bf16[1,256,256]{2,1,0:T(8,128)(2,1)S(1)} %fusion.2.refs_9_.refs_0_, bf16[1,256,256]{2,1,0:T(8,128)(2,1)S(1)} %collective-permute-done.14.refs_1_, bf16[1,256,256]{2,1,0:T(8,128)(2,1)S(1)} %collective-permute-done.15.refs_2_, ...), custom_call_target="tpu_custom_call" | custom-call | flops 4026531840 | bytes 9437184 | tf_op jit(solution)/shard_map/down/pallas_call | solution.py:262
  77.8 1.8 %collective-permute-start.22 = (bf16[1,256,256]{2,1,0:T(8,128)(2,1)S(1)}, bf16[1,256,256]{2,1,0:T(8,128)(2,1)S(1)}, u32[]{:S(2)}, u32[]{:S(2)}) collective-permute-start(bf16[1,256,256]{2,1,0:T(8,128)(2,1)S(1)} %fusion.refs_8_.refs_0_), channel_id=1, source_target_pairs={{0,2},{1,3},{2,0},{3,1},{4,6},{5,7},{6,4},{7,5},{8,10},{9,11},{10,... | collective-permute-start | bytes 393224 | tf_op jit(solution)/shard_map/ppermute | solution.py:23
  80.1 2.7 %collective-permute-done.22.refs_2_ = bf16[1,256,256]{2,1,0:T(8,128)(2,1)S(1)} collective-permute-done((bf16[1,256,256]{2,1,0:T(8,128)(2,1)S(1)}, bf16[1,256,256]{2,1,0:T(8,128)(2,1)S(1)}, u32[]{:S(2)}, u32[]{:S(2)}) %collective-permute-start.22) | collective-permute-done | bytes 131104 | tf_op jit(solution)/shard_map/ppermute | solution.py:23
  82.8 4.5 %down.6.refs_7_ = f32[256,1536]{1,0:T(8,128)S(1)} custom-call(s32[8,128]{1,0:T(8,128)S(1)} %get-tuple-element.25.sched_in, bf16[1,256,256]{2,1,0:T(8,128)(2,1)S(1)} %fusion.1.refs_8_.refs_9_.refs_0_, bf16[1,256,256]{2,1,0:T(8,128)(2,1)S(1)} %collective-permute-done.24.refs_1_, bf16[1,256,256]{2,1,0:T(8,128)(2,1)S(1)} %collective-permute-done.25.refs_2_, ...), custom_call_target="tpu_custom_call" | custom-call | flops 4026531840 | bytes 9437184 | tf_op jit(solution)/shard_map/down/pallas_call | solution.py:262
  87.4 4.5 %down.7 = (bf16[64,1536]{1,0:T(8,128)(2,1)S(1)}, bf16[64,1536]{1,0:T(8,128)(2,1)S(1)}, bf16[64,1536]{1,0:T(8,128)(2,1)S(1)}, bf16[32,1536]{1,0:T(8,128)(2,1)S(1)}, bf16[32,1536]{1,0:T(8,128)(2,1)S(1)}) custom-call(s32[8,128]{1,0:T(8,128)S(1)} %get-tuple-element.25.sched_in, bf16[1,256,256]{2,1,0:T(8,128)(2,1)S(1)} %fusion.refs_8_.refs_0_, ...), custom_call_target="tpu_custom_call" | custom-call | flops 4026531840 | bytes 9437184 | tf_op jit(solution)/shard_map/down/pallas_call | solution.py:262
  91.9 1.7 %collective-permute-start.29 = (bf16[32,1536]{1,0:T(8,128)(2,1)S(1)}, bf16[32,1536]{1,0:T(8,128)(2,1)S(1)}, u32[]{:S(2)}, u32[]{:S(2)}) collective-permute-start(bf16[32,1536]{1,0:T(8,128)(2,1)S(1)} %get-tuple-element.44), channel_id=1, source_target_pairs={{0,4},{4,8},{8,12},{12,0},{1,5},{5,9},{9,13},{13,1},{2,6},{6,10},{... | collective-permute-start | bytes 294920 | tf_op jit(solution)/shard_map/ppermute | solution.py:393
  93.6 2.5 %collective-permute-start.27 = (bf16[32,1536]{1,0:T(8,128)(2,1)S(1)}, bf16[32,1536]{1,0:T(8,128)(2,1)S(1)}, u32[]{:S(2)}, u32[]{:S(2)}) collective-permute-start(bf16[32,1536]{1,0:T(8,128)(2,1)S(1)} %get-tuple-element.42), channel_id=1, source_target_pairs={{0,12},{4,0},{8,4},{12,8},{1,13},{5,1},{9,5},{13,9},{2,14},{6,2},{... | collective-permute-start | bytes 294920 | tf_op jit(solution)/shard_map/ppermute | solution.py:393
  96.1 3.6 %collective-permute-done.29 = bf16[32,1536]{1,0:T(8,128)(2,1)S(1)} collective-permute-done((bf16[32,1536]{1,0:T(8,128)(2,1)S(1)}, bf16[32,1536]{1,0:T(8,128)(2,1)S(1)}, u32[]{:S(2)}, u32[]{:S(2)}) %collective-permute-start.29) | collective-permute-done | bytes 98336 | tf_op jit(solution)/shard_map/ppermute | solution.py:393
  99.8 0.9 collective-permute-done.27
  100.8 2.9 %collective-permute-start.28 = (bf16[64,1536]{1,0:T(8,128)(2,1)S(1)}, bf16[64,1536]{1,0:T(8,128)(2,1)S(1)}, u32[]{:S(2)}, u32[]{:S(2)}) collective-permute-start(bf16[64,1536]{1,0:T(8,128)(2,1)S(1)} %pad_maximum_fusion), channel_id=1, source_target_pairs={{0,12},{4,0},{8,4},{12,8},{1,13},{5,1},{9,5},{13,9},{2,14},{6,2},{... | collective-permute-start | bytes 589832 | tf_op jit(solution)/shard_map/ppermute | solution.py:402
  103.7 5.7 %collective-permute-done.30 = bf16[64,1536]{1,0:T(8,128)(2,1)S(1)} collective-permute-done((bf16[64,1536]{1,0:T(8,128)(2,1)S(1)}, bf16[64,1536]{1,0:T(8,128)(2,1)S(1)}, u32[]{:S(2)}, u32[]{:S(2)}) %collective-permute-start.30) | collective-permute-done | bytes 196640 | tf_op jit(solution)/shard_map/ppermute | solution.py:403
  109.4 2.2 %collective-permute-done.28 = bf16[64,1536]{1,0:T(8,128)(2,1)S(1)} collective-permute-done((bf16[64,1536]{1,0:T(8,128)(2,1)S(1)}, bf16[64,1536]{1,0:T(8,128)(2,1)S(1)}, u32[]{:S(2)}, u32[]{:S(2)}) %collective-permute-start.28) | collective-permute-done | bytes 196640 | tf_op jit(solution)/shard_map/ppermute | solution.py:402
  (69 shorter events, 8.2 us)
Async XLA Ops:
  0.0 11.0 %collective-permute-start.3 = (bf16[64,1536]{1,0:T(8,128)(2,1)}, bf16[64,1536]{1,0:T(8,128)(2,1)S(1)}, u32[]{:S(2)}, u32[]{:S(2)}) collective-permute-start(bf16[64,1536]{1,0:T(8,128)(2,1)} %refs_0_.7), channel_id=1, source_target_pairs={{0,4},{4,8},{8,12},{12,0},{1,5},{5,9},{9,13},{13,1},{2,6},{6,10},{... | collective-permute-start | bytes 589832 | tf_op jit(solution)/shard_map/ppermute | solution.py:377
  3.0 11.0 %collective-permute-start.4 = (bf16[64,1536]{1,0:T(8,128)(2,1)}, bf16[64,1536]{1,0:T(8,128)(2,1)S(1)}, u32[]{:S(2)}, u32[]{:S(2)}) collective-permute-start(bf16[64,1536]{1,0:T(8,128)(2,1)} %refs_0_.7), channel_id=1, source_target_pairs={{0,12},{4,0},{8,4},{12,8},{1,13},{5,1},{9,5},{13,9},{2,14},{6,2},{... | collective-permute-start | bytes 589832 | tf_op jit(solution)/shard_map/ppermute | solution.py:377
  6.4 10.8 %collective-permute-start = (f32[16,64]{1,0:T(8,128)S(1)}, f32[16,64]{1,0:T(8,128)S(1)}, u32[]{:S(2)}, u32[]{:S(2)}) collective-permute-start(f32[16,64]{1,0:T(8,128)S(1)} %pad_maximum_fusion.2.refs_0_), channel_id=1, source_target_pairs={{0,4},{4,8},{8,12},{12,0},{1,5},{5,9},{9,13},{13,1},{2,6},{6,10},{... | collective-permute-start | bytes 12296 | tf_op jit(solution)/shard_map/ppermute | solution.py:334
  6.4 10.8 %collective-permute-start.1 = (f32[16,64]{1,0:T(8,128)S(1)}, f32[16,64]{1,0:T(8,128)S(1)}, u32[]{:S(2)}, u32[]{:S(2)}) collective-permute-start(f32[16,64]{1,0:T(8,128)S(1)} %pad_maximum_fusion.2.refs_0_), channel_id=1, source_target_pairs={{0,12},{4,0},{8,4},{12,8},{1,13},{5,1},{9,5},{13,9},{2,14},{6,2},{... | collective-permute-start | bytes 12296 | tf_op jit(solution)/shard_map/ppermute | solution.py:334
  10.3 7.0 %collective-permute-start.2 = (f32[16,64]{1,0:T(8,128)S(1)}, f32[16,64]{1,0:T(8,128)S(1)}, u32[]{:S(2)}, u32[]{:S(2)}) collective-permute-start(f32[16,64]{1,0:T(8,128)S(1)} %pad_maximum_fusion.2.refs_0_), channel_id=1, source_target_pairs={{0,8},{4,12},{8,0},{12,4},{1,9},{5,13},{9,1},{13,5},{2,10},{6,14},... | collective-permute-start | bytes 12296 | tf_op jit(solution)/shard_map/ppermute | solution.py:334
  11.0 7.6 %collective-permute-start.5 = (bf16[32,1536]{1,0:T(8,128)(2,1)S(1)}, bf16[32,1536]{1,0:T(8,128)(2,1)S(1)}, u32[]{:S(2)}, u32[]{:S(2)}) collective-permute-start(bf16[32,1536]{1,0:T(8,128)(2,1)S(1)} %slice.110), channel_id=1, source_target_pairs={{0,4},{4,8},{8,12},{12,0},{1,5},{5,9},{9,13},{13,1},{2,6},{6,10},{... | collective-permute-start | bytes 294920 | tf_op jit(solution)/shard_map/ppermute | solution.py:381
  14.0 5.6 %collective-permute-start.6 = (bf16[32,1536]{1,0:T(8,128)(2,1)S(1)}, bf16[32,1536]{1,0:T(8,128)(2,1)S(1)}, u32[]{:S(2)}, u32[]{:S(2)}) collective-permute-start(bf16[32,1536]{1,0:T(8,128)(2,1)S(1)} %slice.111), channel_id=1, source_target_pairs={{0,12},{4,0},{8,4},{12,8},{1,13},{5,1},{9,5},{13,9},{2,14},{6,2},{... | collective-permute-start | bytes 294920 | tf_op jit(solution)/shard_map/ppermute | solution.py:381
  19.6 0.9 copy-start
  28.5 2.0 %collective-permute-start.7 = (bf16[2,256,512]{2,1,0:T(8,128)(2,1)S(1)}, bf16[2,256,512]{2,1,0:T(8,128)(2,1)S(1)}, u32[]{:S(2)}, u32[]{:S(2)}) collective-permute-start(bf16[2,256,512]{2,1,0:T(8,128)(2,1)S(1)} %get-tuple-element.28), channel_id=1, source_target_pairs={{0,1},{1,0},{2,3},{3,2},{4,5},{5,4},{6,7},{7,6},{8,9},{9,8},{10,11... | collective-permute-start | bytes 1572872 | tf_op jit(solution)/shard_map/ppermute | solution.py:23
  30.7 9.9 %collective-permute-start.9 = (bf16[1,256,512]{2,1,0:T(8,128)(2,1)S(1)}, bf16[1,256,512]{2,1,0:T(8,128)(2,1)S(1)}, u32[]{:S(2)}, u32[]{:S(2)}) collective-permute-start(bf16[1,256,512]{2,1,0:T(8,128)(2,1)S(1)} %slice.159.refs_8_), channel_id=1, source_target_pairs={{0,2},{1,3},{2,0},{3,1},{4,6},{5,7},{6,4},{7,5},{8,10},{9,11},{10,... | collective-permute-start | bytes 786440 | tf_op jit(solution)/shard_map/ppermute | solution.py:23
  40.5 2.0 %collective-permute-start.8 = (bf16[2,256,512]{2,1,0:T(8,128)(2,1)S(1)}, bf16[2,256,512]{2,1,0:T(8,128)(2,1)S(1)}, u32[]{:S(2)}, u32[]{:S(2)}) collective-permute-start(bf16[2,256,512]{2,1,0:T(8,128)(2,1)S(1)} %get-tuple-element.30), channel_id=1, source_target_pairs={{0,1},{1,0},{2,3},{3,2},{4,5},{5,4},{6,7},{7,6},{8,9},{9,8},{10,11... | collective-permute-start | bytes 1572872 | tf_op jit(solution)/shard_map/ppermute | solution.py:23
  42.7 10.3 %collective-permute-start.11 = (bf16[1,256,512]{2,1,0:T(8,128)(2,1)S(1)}, bf16[1,256,512]{2,1,0:T(8,128)(2,1)S(1)}, u32[]{:S(2)}, u32[]{:S(2)}) collective-permute-start(bf16[1,256,512]{2,1,0:T(8,128)(2,1)S(1)} %slice.158.refs_8_), channel_id=1, source_target_pairs={{0,2},{1,3},{2,0},{3,1},{4,6},{5,7},{6,4},{7,5},{8,10},{9,11},{10,... | collective-permute-start | bytes 786440 | tf_op jit(solution)/shard_map/ppermute | solution.py:23
  51.1 2.0 %collective-permute-start.10 = (bf16[2,256,512]{2,1,0:T(8,128)(2,1)S(1)}, bf16[2,256,512]{2,1,0:T(8,128)(2,1)S(1)}, u32[]{:S(2)}, u32[]{:S(2)}) collective-permute-start(bf16[2,256,512]{2,1,0:T(8,128)(2,1)S(1)} %get-tuple-element.32), channel_id=1, source_target_pairs={{0,1},{1,0},{2,3},{3,2},{4,5},{5,4},{6,7},{7,6},{8,9},{9,8},{10,11... | collective-permute-start | bytes 1572872 | tf_op jit(solution)/shard_map/ppermute | solution.py:23
  51.2 13.1 %collective-permute-start.18 = (bf16[1,256,256]{2,1,0:T(8,128)(2,1)S(1)}, bf16[1,256,256]{2,1,0:T(8,128)(2,1)S(1)}, u32[]{:S(2)}, u32[]{:S(2)}) collective-permute-start(bf16[1,256,256]{2,1,0:T(8,128)(2,1)S(1)} %fusion.3.refs_9_.refs_0_), channel_id=1, source_target_pairs={{0,2},{1,3},{2,0},{3,1},{4,6},{5,7},{6,4},{7,5},{8,10},{9,11},{10,... | collective-permute-start | bytes 393224 | tf_op jit(solution)/shard_map/ppermute | solution.py:23
  53.4 12.2 %collective-permute-start.20 = (bf16[1,256,512]{2,1,0:T(8,128)(2,1)S(1)}, bf16[1,256,512]{2,1,0:T(8,128)(2,1)S(1)}, u32[]{:S(2)}, u32[]{:S(2)}) collective-permute-start(bf16[1,256,512]{2,1,0:T(8,128)(2,1)S(1)} %slice.157.refs_8_), channel_id=1, source_target_pairs={{0,2},{1,3},{2,0},{3,1},{4,6},{5,7},{6,4},{7,5},{8,10},{9,11},{10,... | collective-permute-start | bytes 786440 | tf_op jit(solution)/shard_map/ppermute | solution.py:23
  55.1 10.5 %collective-permute-start.15 = (bf16[1,256,256]{2,1,0:T(8,128)(2,1)S(1)}, bf16[1,256,256]{2,1,0:T(8,128)(2,1)S(1)}, u32[]{:S(2)}, u32[]{:S(2)}) collective-permute-start(bf16[1,256,256]{2,1,0:T(8,128)(2,1)S(1)} %fusion.2.refs_9_.refs_0_), channel_id=1, source_target_pairs={{0,2},{1,3},{2,0},{3,1},{4,6},{5,7},{6,4},{7,5},{8,10},{9,11},{10,... | collective-permute-start | bytes 393224 | tf_op jit(solution)/shard_map/ppermute | solution.py:23
  63.7 2.6 %collective-permute-start.12 = (bf16[2,256,512]{2,1,0:T(8,128)(2,1)S(1)}, bf16[2,256,512]{2,1,0:T(8,128)(2,1)S(1)}, u32[]{:S(2)}, u32[]{:S(2)}) collective-permute-start(bf16[2,256,512]{2,1,0:T(8,128)(2,1)S(1)} %get-tuple-element.34), channel_id=1, source_target_pairs={{0,1},{1,0},{2,3},{3,2},{4,5},{5,4},{6,7},{7,6},{8,9},{9,8},{10,11... | collective-permute-start | bytes 1572872 | tf_op jit(solution)/shard_map/ppermute | solution.py:23
  63.8 4.5 %collective-permute-start.17 = (bf16[1,256,256]{2,1,0:T(8,128)(2,1)S(1)}, bf16[1,256,256]{2,1,0:T(8,128)(2,1)S(1)}, u32[]{:S(2)}, u32[]{:S(2)}) collective-permute-start(bf16[1,256,256]{2,1,0:T(8,128)(2,1)S(1)} %fusion.3.refs_9_.refs_0_), channel_id=1, source_target_pairs={{0,1},{1,0},{2,3},{3,2},{4,5},{5,4},{6,7},{7,6},{8,9},{9,8},{10,11... | collective-permute-start | bytes 393224 | tf_op jit(solution)/shard_map/ppermute | solution.py:23
  64.3 4.3 %collective-permute-start.19 = (bf16[1,256,256]{2,1,0:T(8,128)(2,1)S(1)}, bf16[1,256,256]{2,1,0:T(8,128)(2,1)S(1)}, u32[]{:S(2)}, u32[]{:S(2)}) collective-permute-start(bf16[1,256,256]{2,1,0:T(8,128)(2,1)S(1)} %collective-permute-done.18.refs_2_), channel_id=1, source_target_pairs={{0,1},{1,0},{2,3},{3,2},{4,5},{5,4},{6,7},{7,6},{8,9},{9,8},{10,11... | collective-permute-start | bytes 393224 | tf_op jit(solution)/shard_map/ppermute | solution.py:23
  65.5 7.5 %collective-permute-start.14 = (bf16[1,256,256]{2,1,0:T(8,128)(2,1)S(1)}, bf16[1,256,256]{2,1,0:T(8,128)(2,1)S(1)}, u32[]{:S(2)}, u32[]{:S(2)}) collective-permute-start(bf16[1,256,256]{2,1,0:T(8,128)(2,1)S(1)} %fusion.2.refs_9_.refs_0_), channel_id=1, source_target_pairs={{0,1},{1,0},{2,3},{3,2},{4,5},{5,4},{6,7},{7,6},{8,9},{9,8},{10,11... | collective-permute-start | bytes 393224 | tf_op jit(solution)/shard_map/ppermute | solution.py:23
  65.5 7.5 %collective-permute-start.16 = (bf16[1,256,256]{2,1,0:T(8,128)(2,1)S(1)}, bf16[1,256,256]{2,1,0:T(8,128)(2,1)S(1)}, u32[]{:S(2)}, u32[]{:S(2)}) collective-permute-start(bf16[1,256,256]{2,1,0:T(8,128)(2,1)S(1)} %collective-permute-done.15.refs_2_), channel_id=1, source_target_pairs={{0,1},{1,0},{2,3},{3,2},{4,5},{5,4},{6,7},{7,6},{8,9},{9,8},{10,11... | collective-permute-start | bytes 393224 | tf_op jit(solution)/shard_map/ppermute | solution.py:23
  66.4 11.2 %collective-permute-start.13 = (bf16[1,256,512]{2,1,0:T(8,128)(2,1)S(1)}, bf16[1,256,512]{2,1,0:T(8,128)(2,1)S(1)}, u32[]{:S(2)}, u32[]{:S(2)}) collective-permute-start(bf16[1,256,512]{2,1,0:T(8,128)(2,1)S(1)} %slice.156.refs_7_.refs_8_), channel_id=1, source_target_pairs={{0,2},{1,3},{2,0},{3,1},{4,6},{5,7},{6,4},{7,5},{8,10},{9,11},{10,... | collective-permute-start | bytes 786440 | tf_op jit(solution)/shard_map/ppermute | solution.py:23
  68.2 11.4 %collective-permute-start.25 = (bf16[1,256,256]{2,1,0:T(8,128)(2,1)S(1)}, bf16[1,256,256]{2,1,0:T(8,128)(2,1)S(1)}, u32[]{:S(2)}, u32[]{:S(2)}) collective-permute-start(bf16[1,256,256]{2,1,0:T(8,128)(2,1)S(1)} %fusion.1.refs_8_.refs_9_.refs_0_), channel_id=1, source_target_pairs={{0,2},{1,3},{2,0},{3,1},{4,6},{5,7},{6,4},{7,5},{8,10},{9,11},{10,... | collective-permute-start | bytes 393224 | tf_op jit(solution)/shard_map/ppermute | solution.py:23
  77.8 5.0 %collective-permute-start.22 = (bf16[1,256,256]{2,1,0:T(8,128)(2,1)S(1)}, bf16[1,256,256]{2,1,0:T(8,128)(2,1)S(1)}, u32[]{:S(2)}, u32[]{:S(2)}) collective-permute-start(bf16[1,256,256]{2,1,0:T(8,128)(2,1)S(1)} %fusion.refs_8_.refs_0_), channel_id=1, source_target_pairs={{0,2},{1,3},{2,0},{3,1},{4,6},{5,7},{6,4},{7,5},{8,10},{9,11},{10,... | collective-permute-start | bytes 393224 | tf_op jit(solution)/shard_map/ppermute | solution.py:23
  79.6 3.3 %collective-permute-start.24 = (bf16[1,256,256]{2,1,0:T(8,128)(2,1)S(1)}, bf16[1,256,256]{2,1,0:T(8,128)(2,1)S(1)}, u32[]{:S(2)}, u32[]{:S(2)}) collective-permute-start(bf16[1,256,256]{2,1,0:T(8,128)(2,1)S(1)} %fusion.1.refs_8_.refs_9_.refs_0_), channel_id=1, source_target_pairs={{0,1},{1,0},{2,3},{3,2},{4,5},{5,4},{6,7},{7,6},{8,9},{9,8},{10,11... | collective-permute-start | bytes 393224 | tf_op jit(solution)/shard_map/ppermute | solution.py:23
  79.6 3.3 %collective-permute-start.26 = (bf16[1,256,256]{2,1,0:T(8,128)(2,1)S(1)}, bf16[1,256,256]{2,1,0:T(8,128)(2,1)S(1)}, u32[]{:S(2)}, u32[]{:S(2)}) collective-permute-start(bf16[1,256,256]{2,1,0:T(8,128)(2,1)S(1)} %collective-permute-done.25.refs_2_), channel_id=1, source_target_pairs={{0,1},{1,0},{2,3},{3,2},{4,5},{5,4},{6,7},{7,6},{8,9},{9,8},{10,11... | collective-permute-start | bytes 393224 | tf_op jit(solution)/shard_map/ppermute | solution.py:23
  80.1 7.3 %collective-permute-start.21 = (bf16[1,256,256]{2,1,0:T(8,128)(2,1)S(1)}, bf16[1,256,256]{2,1,0:T(8,128)(2,1)S(1)}, u32[]{:S(2)}, u32[]{:S(2)}) collective-permute-start(bf16[1,256,256]{2,1,0:T(8,128)(2,1)S(1)} %fusion.refs_8_.refs_0_), channel_id=1, source_target_pairs={{0,1},{1,0},{2,3},{3,2},{4,5},{5,4},{6,7},{7,6},{8,9},{9,8},{10,11... | collective-permute-start | bytes 393224 | tf_op jit(solution)/shard_map/ppermute | solution.py:23
  82.8 4.6 %collective-permute-start.23 = (bf16[1,256,256]{2,1,0:T(8,128)(2,1)S(1)}, bf16[1,256,256]{2,1,0:T(8,128)(2,1)S(1)}, u32[]{:S(2)}, u32[]{:S(2)}) collective-permute-start(bf16[1,256,256]{2,1,0:T(8,128)(2,1)S(1)} %collective-permute-done.22.refs_2_), channel_id=1, source_target_pairs={{0,1},{1,0},{2,3},{3,2},{4,5},{5,4},{6,7},{7,6},{8,9},{9,8},{10,11... | collective-permute-start | bytes 393224 | tf_op jit(solution)/shard_map/ppermute | solution.py:23
  91.9 7.7 %collective-permute-start.29 = (bf16[32,1536]{1,0:T(8,128)(2,1)S(1)}, bf16[32,1536]{1,0:T(8,128)(2,1)S(1)}, u32[]{:S(2)}, u32[]{:S(2)}) collective-permute-start(bf16[32,1536]{1,0:T(8,128)(2,1)S(1)} %get-tuple-element.44), channel_id=1, source_target_pairs={{0,4},{4,8},{8,12},{12,0},{1,5},{5,9},{9,13},{13,1},{2,6},{6,10},{... | collective-permute-start | bytes 294920 | tf_op jit(solution)/shard_map/ppermute | solution.py:393
  93.6 7.1 %collective-permute-start.27 = (bf16[32,1536]{1,0:T(8,128)(2,1)S(1)}, bf16[32,1536]{1,0:T(8,128)(2,1)S(1)}, u32[]{:S(2)}, u32[]{:S(2)}) collective-permute-start(bf16[32,1536]{1,0:T(8,128)(2,1)S(1)} %get-tuple-element.42), channel_id=1, source_target_pairs={{0,12},{4,0},{8,4},{12,8},{1,13},{5,1},{9,5},{13,9},{2,14},{6,2},{... | collective-permute-start | bytes 294920 | tf_op jit(solution)/shard_map/ppermute | solution.py:393
  99.7 9.7 %collective-permute-start.30 = (bf16[64,1536]{1,0:T(8,128)(2,1)S(1)}, bf16[64,1536]{1,0:T(8,128)(2,1)S(1)}, u32[]{:S(2)}, u32[]{:S(2)}) collective-permute-start(bf16[64,1536]{1,0:T(8,128)(2,1)S(1)} %pad_maximum_fusion.1), channel_id=1, source_target_pairs={{0,4},{4,8},{8,12},{12,0},{1,5},{5,9},{9,13},{13,1},{2,6},{6,10},{... | collective-permute-start | bytes 589832 | tf_op jit(solution)/shard_map/ppermute | solution.py:403
  100.8 10.8 %collective-permute-start.28 = (bf16[64,1536]{1,0:T(8,128)(2,1)S(1)}, bf16[64,1536]{1,0:T(8,128)(2,1)S(1)}, u32[]{:S(2)}, u32[]{:S(2)}) collective-permute-start(bf16[64,1536]{1,0:T(8,128)(2,1)S(1)} %pad_maximum_fusion), channel_id=1, source_target_pairs={{0,12},{4,0},{8,4},{12,8},{1,13},{5,1},{9,5},{13,9},{2,14},{6,2},{... | collective-permute-start | bytes 589832 | tf_op jit(solution)/shard_map/ppermute | solution.py:402

commit v4 on v3

v4 whole, which is shorter than its diff:
```python
import functools

import jax
import jax.numpy as jnp
from jax import lax
from jax.experimental import pallas as pl
from jax.experimental.pallas import tpu as pltpu
from jax.sharding import PartitionSpec as P

LANES = 128
VMEM = pl.BlockSpec(memory_space=pltpu.VMEM)
SMEM = pl.BlockSpec(memory_space=pltpu.SMEM)
HERE = pl.BlockSpec(memory_space=pl.ANY)
FAR = pl.BlockSpec(memory_space=pltpu.HBM)
NOWHERE = -1e6


def bits_of(n):
    return [b for b in range(n.bit_length() - 1)]


def flip(x, axis, k):
    return lax.ppermute(x, axis, [(i, i ^ k) for i in range(lax.axis_size(axis))])


def route_body(n, experts, info, *refs):
    meta, (rank, wt) = refs[:n], refs[n:]
    tok, top = meta[0].shape[1], meta[0].shape[0] // 2
    padded = rank.shape[0]
    first = info[0].astype(jnp.float32)
    e = lax.broadcasted_iota(jnp.int32, (padded, tok), 0).astype(jnp.float32)
    before = (
        lax.broadcasted_iota(jnp.int32, (tok, tok), 0) < lax.broadcasted_iota(jnp.int32, (tok, tok), 1)
    ).astype(jnp.bfloat16)
    count = jnp.zeros((padded, 1), jnp.float32)
    for s in range(n):
        ids, scores = meta[s][:top], meta[s][top:]
        affinity = 1.0 / (1.0 + jnp.exp(-scores))
        share = 2.5 * affinity / jnp.sum(affinity, axis=0, keepdims=True)
        named = jnp.zeros((padded, tok), jnp.float32)
        weight = jnp.zeros((padded, tok), jnp.float32)
        for k in range(top):
            hit = jnp.where(ids[k : k + 1] - first == e, 1.0, 0.0)
            named = named + hit
            weight = weight + hit * share[k : k + 1]
        named = jnp.where(e < experts, named, 0.0)
        place = jnp.dot(named.astype(jnp.bfloat16), before, preferred_element_type=jnp.float32) + count
        rank[:, s * tok : (s + 1) * tok] = jnp.where(named > 0, place, NOWHERE)
        wt[:, s * tok : (s + 1) * tok] = weight
        count = count + jnp.sum(named, axis=1, keepdims=True)


def route(meta, info, experts):
    tokens = len(meta) * meta[0].shape[1]
    table = jax.ShapeDtypeStruct((-(-experts // 8) * 8, tokens), jnp.float32)
    return pl.pallas_call(
        functools.partial(route_body, len(meta), experts),
        out_shape=(table, table),
        in_specs=[SMEM] + [VMEM] * len(meta),
        out_specs=(VMEM, VMEM),
        compiler_params=pltpu.CompilerParams(vmem_limit_bytes=40 << 20),
        name="route",
    )(info, *meta)


def gate_up_body(n, experts, n_dp, after, info, *refs):
    tokens, (rank_in, w_gate, w_up), refs = refs[:n], refs[n : n + 3], refs[n + 3 + after :]
    send, keep, rank, feed, rows, held, rank_sem, feed_sem, held_sem = refs
    most = rows.shape[0] // len(experts)
    width = send.shape[2] // 2
    pieces = list(range(1, n_dp, 2)) + list(range(0, n_dp, 2))
    mats = [(m, x) for m in range(2) for x in range(len(experts))]

    def copy(l, m, x):
        units = pl.ds(pl.multiple_of((l ^ info[1]) * width, width), width)
        i = m * len(experts) + x
        return pltpu.make_async_copy(
            (w_gate, w_up)[m].at[experts[x], :, units],
            held.at[i, :, pl.ds(l * width, width)],
            held_sem.at[l, i],
        )

    ranks = pltpu.make_async_copy(rank_in, rank, rank_sem.at[0])
    ranks.start()
    at, feeds = 0, []
    for s in range(n):
        tok = tokens[s].shape[0]
        feeds.append(pltpu.make_async_copy(tokens[s], feed.at[pl.ds(at, tok)], feed_sem.at[s]))
        at += tok
    for part in feeds:
        part.start()
    for m, x in mats:
        copy(pieces[0], m, x).start()
    ranks.wait()
    r = lax.broadcasted_iota(jnp.int32, (most, at), 0).astype(jnp.float32)
    pick = jnp.concatenate(
        [jnp.where(r == rank[e : e + 1, :], 1.0, 0.0).astype(jnp.bfloat16) for e in experts], axis=0
    )
    for part in feeds:
        part.wait()
    rows[...] = jnp.dot(pick, feed[...], preferred_element_type=jnp.float32).astype(jnp.bfloat16)
    for l, ahead in zip(pieces, pieces[1:] + [None]):
        if ahead is not None:
            for m, x in mats:
                copy(ahead, m, x).start()
        to = send if l % 2 else keep
        for m, x in mats:
            copy(l, m, x).wait()
            mine = slice(x * most, (x + 1) * most)
            to[l // 2, mine, m * width : (m + 1) * width] = jnp.dot(
                rows[mine],
                held[m * len(experts) + x, :, l * width : (l + 1) * width],
                preferred_element_type=jnp.float32,
            ).astype(jnp.bfloat16)


def gate_up(tokens, rank, info, w_gate, w_up, experts, most, n_dp, after):
    n, local = len(tokens), tokens[0].shape[1]
    hidden = w_gate.shape[2]
    rows, mats = most * len(experts), 2 * len(experts)
    out = jax.ShapeDtypeStruct((max(n_dp // 2, 1), rows, 2 * hidden // n_dp), jnp.bfloat16)
    return pl.pallas_call(
        functools.partial(gate_up_body, n, experts, n_dp, len(after)),
        out_shape=(out, out),
        in_specs=[SMEM] + [HERE] * (n + 3 + len(after)),
        out_specs=(VMEM, VMEM),
        scratch_shapes=[
            pltpu.VMEM(rank.shape, jnp.float32),
            pltpu.VMEM((rank.shape[1], local), jnp.bfloat16),
            pltpu.VMEM((rows, local), jnp.bfloat16),
            pltpu.VMEM((mats, local, hidden), jnp.bfloat16),
            pltpu.SemaphoreType.DMA((1,)),
            pltpu.SemaphoreType.DMA((n,)),
            pltpu.SemaphoreType.DMA((n_dp, mats)),
        ],
        compiler_params=pltpu.CompilerParams(vmem_limit_bytes=40 << 20),
        cost_estimate=pl.CostEstimate(
            flops=8 * mats * most * local * hidden,
            bytes_accessed=2 * mats * local * hidden,
            transcendentals=0,
        ),
        name="gate_up",
    )(info, *tokens, rank, w_gate, w_up, *after)


def down_body(n_part, cuts, experts, first, after, info, *refs):
    parts, (rank, wt, w_down), refs = refs[:n_part], refs[n_part : n_part + 3], refs[n_part + 3 :]
    before = None if first else refs[0]
    refs = refs[(0 if first else 1) + after :]
    outs, (hidden, mix, out, held, held_sem) = refs[: len(cuts)], refs[len(cuts) :]
    most = hidden.shape[0] // len(experts)
    width = parts[0].shape[-1]
    local = out.shape[1]
    block = 512 if local % 512 == 0 else 256 if local % 256 == 0 else local
    copies = {}
    for i in range(local // block):
        for x, e in enumerate(experts):
            cols = pl.ds(i * block, block)
            copies[i, x] = pltpu.make_async_copy(
                w_down.at[e, :, cols], held.at[x, :, cols], held_sem.at[i, x]
            )
            copies[i, x].start()
    for p, part in enumerate(parts):
        for j in range(part.shape[0]):
            at = pl.multiple_of(((2 * j + p) ^ info[1]) * width, width)
            hidden[:, pl.ds(at, width)] = part[j]
    r = lax.broadcasted_iota(jnp.int32, (most, mix.shape[1]), 0).astype(jnp.float32)
    for x, e in enumerate(experts):
        mix[x * most : (x + 1) * most, :] = jnp.where(
            r == rank[e : e + 1, :], wt[e : e + 1, :], 0.0
        ).astype(jnp.bfloat16)
    for i in range(local // block):
        cols = slice(i * block, (i + 1) * block)
        for x in range(len(experts)):
            mine = slice(x * most, (x + 1) * most)
            copies[i, x].wait()
            out[mine, cols] = jnp.dot(
                hidden[mine], held[x, :, cols], preferred_element_type=jnp.float32
            ).astype(jnp.bfloat16)
        total = lax.dot_general(
            mix[...], out[:, cols], (((0,), (0,)), ((), ())), preferred_element_type=jnp.float32
        )
        if not first:
            total = total + before[:, cols]
        at = 0
        for to, cut in zip(outs, cuts):
            to[:, cols] = total[at : at + cut].astype(to.dtype)
            at += cut


def down(parts, rank, wt, info, w_down, total, experts, cuts, after):
    rows = parts[0].shape[1]
    _, hidden, local = w_down.shape
    tokens = rank.shape[1]
    first, last = total is None, len(cuts) > 1
    kind = jnp.bfloat16 if last else jnp.float32
    mats = len(experts)
    outs = pl.pallas_call(
        functools.partial(down_body, len(parts), cuts, experts, first, len(after)),
        out_shape=tuple(jax.ShapeDtypeStruct((cut, local), kind) for cut in cuts),
        in_specs=[SMEM]
        + [VMEM] * (len(parts) + 2)
        + [HERE]
        + ([] if first else [VMEM])
        + [HERE] * len(after),
        out_specs=(VMEM,) * len(cuts),
        scratch_shapes=[
            pltpu.VMEM((rows, hidden), jnp.bfloat16),
            pltpu.VMEM((rows, tokens), jnp.bfloat16),
            pltpu.VMEM((rows, local), jnp.bfloat16),
            pltpu.VMEM((mats, hidden, local), jnp.bfloat16),
            pltpu.SemaphoreType.DMA((local // 256 + 1, mats)),
        ],
        compiler_params=pltpu.CompilerParams(vmem_limit_bytes=40 << 20),
        cost_estimate=pl.CostEstimate(
            flops=8 * local * rows * (hidden + tokens),
            bytes_accessed=2 * mats * hidden * local + 8 * tokens * local,
            transcendentals=0,
        ),
        name="down",
    )(info, *parts, rank, wt, w_down, *([] if first else [total]), *after)
    return outs if last else outs[0]


def chip_sums(send, keep, n_dp):
    total = keep.astype(jnp.float32)
    late = jnp.zeros(total.shape, jnp.float32)
    for b in bits_of(n_dp):
        if b > 0:
            total = total + late
            send = total.astype(jnp.bfloat16)
        late = flip(send, "dp", 1 << b).astype(jnp.float32)
        if b > 0:
            pairs = (late.shape[0] >> b, 2, 1 << (b - 1)) + late.shape[1:]
            late = jnp.flip(late.reshape(pairs), axis=1).reshape(late.shape)
    return total, late, send


def finish(total, late, after):
    if after:
        late, *_ = lax.optimization_barrier((late, *after))
    gate_up = total + late
    width = gate_up.shape[2] // 2
    return (jax.nn.silu(gate_up[:, :, :width]) * gate_up[:, :, width:]).astype(jnp.bfloat16)


def all_parts(mine, n_dp):
    return [mine, flip(mine, "dp", 1)] if n_dp > 1 else [mine]


def on_device(tokens, expert_ids, scores, w_gate, w_up, w_down):
    n_owner, n_dp = lax.axis_size("expert"), lax.axis_size("dp")
    tok_rows, top = expert_ids.shape
    experts = w_gate.shape[0]
    capacity = 2 * tok_rows * top // (experts * n_owner)
    per_chunk = 2 if experts % 2 == 0 else 1
    most = n_owner * capacity
    chunks = experts // per_chunk

    meta = jnp.concatenate([expert_ids.T.astype(jnp.float32), scores.T], axis=0)
    feeds = gathered(tokens, "expert")
    metas = [meta] + [
        lax.ppermute(meta, "expert", [(i, (i - k) % n_owner) for i in range(n_owner)])
        for k in gathered_order(n_owner)[1:]
    ]
    info = jnp.stack([lax.axis_index("expert") * experts, lax.axis_index("dp")]).astype(jnp.int32)
    rank, wt = route(metas, info, experts)

    cuts = [feed.shape[0] for feed in feeds]
    of = lambda c: list(range(c * per_chunk, (c + 1) * per_chunk))
    shares, sent, parts, total = [], [], [], None

    def add(c, after):
        outs = cuts if c == chunks - 1 else [sum(cuts)]
        return down(parts[c], rank, wt, info, w_down, total, of(c), outs, after)

    for c in range(chunks):
        after = ([sent[c - 1]] if c >= 1 else []) + ([shares[c - 2]] if c >= 2 else [])
        send, keep = gate_up(feeds, rank, info, w_gate, w_up, of(c), most, n_dp, after)
        if c > 0:
            send = lax.optimization_barrier((send, shares[-1]))[0]
        mine, late, last_sent = chip_sums(send, keep, n_dp)
        sent.append(last_sent)
        if c > 0:
            parts.append(all_parts(lax.optimization_barrier((shares[-1], last_sent))[0], n_dp))
        early = range(c) if c == chunks - 1 else []
        for d in early:
            total = add(d, [last_sent, shares[-1]] if d == 0 else [])
        shares.append(finish(mine, late, [total] if early else []))
    parts.append(all_parts(shares[-1], n_dp))
    total = add(chunks - 1, [])
    return returned(total, "expert") if n_owner > 1 else total[0].astype(jnp.bfloat16)


def gathered_order(n):
    near = [d for s in range(1, n // 2) for d in (-s, s)]
    return [0] + near + ([n // 2] if n > 1 else [])


def gathered(x, axis):
    n = lax.axis_size(axis)
    up, down_ = [(i, (i + 1) % n) for i in range(n)], [(i, (i - 1) % n) for i in range(n)]
    below = above = x
    found = [x]
    for _ in range(1, n // 2):
        below, above = lax.ppermute(below, axis, up), lax.ppermute(above, axis, down_)
        found += [below, above]
    if n > 1:
        half = x.shape[0] // 2
        found += [lax.ppermute(below[:half], axis, up), lax.ppermute(above[half:], axis, down_)]
    return found


def returned(partials, axis):
    n = lax.axis_size(axis)
    up, down_ = [(i, (i + 1) % n) for i in range(n)], [(i, (i - 1) % n) for i in range(n)]
    wide = lambda x: x.astype(jnp.float32)
    near = {0: partials[0]}
    for k, partial in zip(gathered_order(n)[1:-1], partials[1:-2]):
        near[k] = partial
    half = partials[-1].shape[0]
    low, high = lax.ppermute(partials[-2], axis, down_), lax.ppermute(partials[-1], axis, up)
    halves = True
    for s in range(n // 2 - 1, 0, -1):
        a, b = wide(near[-s]), wide(near[s])
        if halves:
            a = jnp.concatenate([a[:half] + wide(low), a[half:]], axis=0)
            b = jnp.concatenate([b[:half], b[half:] + wide(high)], axis=0)
        else:
            a, b = a + wide(low), b + wide(high)
        low = lax.ppermute(a.astype(jnp.bfloat16), axis, down_)
        high = lax.ppermute(b.astype(jnp.bfloat16), axis, up)
        halves = False
    if halves:
        back = jnp.concatenate([wide(low), wide(high)], axis=0)
    else:
        back = wide(low) + wide(high)
    return (wide(near[0]) + back).astype(jnp.bfloat16)


def solution(mesh):
    in_specs = (
        P(("groups", "expert"), "dp"),
        P(("groups", "expert"), None),
        P(("groups", "expert"), None),
        P("expert", "dp", None),
        P("expert", "dp", None),
        P("expert", None, "dp"),
    )
    out_specs = P(("groups", "expert"), "dp")
    return jax.shard_map(
        on_device, mesh=mesh, in_specs=in_specs, out_specs=out_specs, check_vma=False
    )
```

time: 113 us -> 126 us (1.12)
  waiting for transfers between devices: 25.2 us -> 35.5 us
  other arithmetic: 3.48 us -> 5.82 us
  starting transfers between devices: 31 us -> 28.9 us
  local copies, waits for them, and re-layouts: 1.09 us -> 2.8 us
  Pallas kernels: 51.2 us -> 52.6 us
    ppermute x20 -> x12, waiting for transfers between devices: 7.59 us -> 19 us  [flip(): lax.ppermute(x, axis, [(i, i ^ k) for i in range(lax.axis_size(axis))])]
    ppermute x1, waiting for transfers between devices: 3.56 us -> 0.01 us  [returned(): lax.ppermute(partials[-1], axis, up)]
    ppermute x20 -> x12, starting transfers between devices: 11.8 us -> 8.47 us  [flip(): lax.ppermute(x, axis, [(i, i ^ k) for i in range(lax.axis_size(axis))])]
    ppermute x1, waiting for transfers between devices: 2.17 us -> 5.24 us  [returned(): low = lax.ppermute(a.astype(jnp.bfloat16), axis, down_)]
    ppermute x1, waiting for transfers between devices: 5.72 us -> 2.9 us  [returned(): high = lax.ppermute(b.astype(jnp.bfloat16), axis, up)]
    ppermute x1, waiting for transfers between devices: 0.94 us -> 3.06 us  [returned(): lax.ppermute(partials[-2], axis, down_)]
    ppermute x1, starting transfers between devices: 1.67 us -> 0.05 us  [returned(): lax.ppermute(partials[-1], axis, up)]
    pallas_call x9, Pallas kernels: 51.2 us -> 52.6 us  [the longest x4 34.5 us: gate_up(): pl.pallas_call(functools.partial(gate_up_body, n, experts, n_dp, len(afte...]
  transfers between devices with their start and end apart: 31 -> 23, of which waited for: 12 -> 15; matrix products, arithmetic and copies ran while one was open for 2% -> 1% of each run, Pallas kernels for 34% -> 32%
where the time goes in v4:
time: 126 us
  Pallas kernels  52.6 us (42%)
  waiting for transfers between devices  35.5 us (28%)
  starting transfers between devices  28.9 us (23%)
  other arithmetic  5.82 us (5%)
  local copies, waits for them, and re-layouts  2.8 us (2%)
    pallas_call x4, Pallas kernels, gate_up(): pl.pallas_call(functools.partial(gate_up_body, n, experts, n_dp, len(afte...  34.5 us
    ppermute x12, waiting for transfers between devices, flip(): lax.ppermute(x, axis, [(i, i ^ k) for i in range(lax.axis_size(axis))])  19 us
    pallas_call x4, Pallas kernels, down(): pl.pallas_call(functools.partial(down_body, len(parts), cuts, experts, fi...  17.4 us
    ppermute x12, starting transfers between devices, flip(): lax.ppermute(x, axis, [(i, i ^ k) for i in range(lax.axis_size(axis))])  8.47 us
    ppermute x1, waiting for transfers between devices, returned(): low = lax.ppermute(a.astype(jnp.bfloat16), axis, down_)  5.24 us
    ppermute x1, starting transfers between devices, returned(): low = lax.ppermute(a.astype(jnp.bfloat16), axis, down_)  4.33 us
    ppermute x1, starting transfers between devices, returned(): lax.ppermute(partials[-2], axis, down_)  3.84 us
    ppermute x3, starting transfers between devices, on_device(): lax.ppermute(meta, 'expert', [(i, (i - k) % n_owner) for i in range(n_own...  3.83 us
  transfers between devices with their start and end apart: 23, of which 15 were waited for; matrix products, arithmetic and copies ran while one was open for 1% of the time, Pallas kernels for 32%

profile of v4, /device:TPU:0, one launch (start us, length us, event | category | flops | bytes accessed | tf_op | source)
XLA Modules:
  0.0 125.9 jit_solution(16221602403702001372)
XLA Ops:
  0.0 3.0 %collective-permute-start = (bf16[64,1536]{1,0:T(8,128)(2,1)}, bf16[64,1536]{1,0:T(8,128)(2,1)S(1)}, u32[]{:S(2)}, u32[]{:S(2)}) collective-permute-start(bf16[64,1536]{1,0:T(8,128)(2,1)} %refs_0_.7), channel_id=1, source_target_pairs={{0,4},{4,8},{8,12},{12,0},{1,5},{5,9},{9,13},{13,1},{2,6},{6,10},{... | collective-permute-start | bytes 589832 | tf_op jit(solution)/shard_map/ppermute | solution.py:306
  3.0 2.0 %collective-permute-start.1 = (bf16[64,1536]{1,0:T(8,128)(2,1)}, bf16[64,1536]{1,0:T(8,128)(2,1)S(1)}, u32[]{:S(2)}, u32[]{:S(2)}) collective-permute-start(bf16[64,1536]{1,0:T(8,128)(2,1)} %refs_0_.7), channel_id=1, source_target_pairs={{0,12},{4,0},{8,4},{12,8},{1,13},{5,1},{9,5},{13,9},{2,14},{6,2},{... | collective-permute-start | bytes 589832 | tf_op jit(solution)/shard_map/ppermute | solution.py:306
  6.4 3.8 %collective-permute-start.5 = (f32[16,64]{1,0:T(8,128)S(1)}, f32[16,64]{1,0:T(8,128)S(1)}, u32[]{:S(2)}, u32[]{:S(2)}) collective-permute-start(f32[16,64]{1,0:T(8,128)S(1)} %pad_maximum_fusion.2.refs_0_), channel_id=1, source_target_pairs={{0,12},{4,0},{8,4},{12,8},{1,13},{5,1},{9,5},{13,9},{2,14},{6,2},{... | collective-permute-start | bytes 12296 | tf_op jit(solution)/shard_map/ppermute | solution.py:263
  11.1 2.9 %collective-permute-done.1.refs_2_ = bf16[64,1536]{1,0:T(8,128)(2,1)S(1)} collective-permute-done((bf16[64,1536]{1,0:T(8,128)(2,1)}, bf16[64,1536]{1,0:T(8,128)(2,1)S(1)}, u32[]{:S(2)}, u32[]{:S(2)}) %collective-permute-start.1) | collective-permute-done | bytes 196640 | tf_op jit(solution)/shard_map/ppermute | solution.py:306
  14.0 3.2 %collective-permute-start.3 = (bf16[32,1536]{1,0:T(8,128)(2,1)S(1)}, bf16[32,1536]{1,0:T(8,128)(2,1)S(1)}, u32[]{:S(2)}, u32[]{:S(2)}) collective-permute-start(bf16[32,1536]{1,0:T(8,128)(2,1)S(1)} %slice.67), channel_id=1, source_target_pairs={{0,12},{4,0},{8,4},{12,8},{1,13},{5,1},{9,5},{13,9},{2,14},{6,2},{... | collective-permute-start | bytes 294920 | tf_op jit(solution)/shard_map/ppermute | solution.py:310
  20.5 8.6 %gate_up.4 = (bf16[2,256,512]{2,1,0:T(8,128)(2,1)S(1)}, bf16[2,256,512]{2,1,0:T(8,128)(2,1)S(1)}) custom-call(s32[2]{0:T(128)S(1)} %pad_add_fusion.info, bf16[64,1536]{1,0:T(8,128)(2,1)S(1)} %copy-done, bf16[64,1536]{1,0:T(8,128)(2,1)S(1)} %collective-permute-done.refs_1_, bf16[64,1536]{1,0:T(8,128)(2,1)S(1)} %collective-permute-done.1.refs_2_, ...), custom_call_target="tpu_custom_call" | custom-call | flops 6442450944 | bytes 12582912 | tf_op jit(solution)/shard_map/gate_up/pallas_call | solution.py:122
  29.1 1.9 %collective-permute-done.7 = bf16[2,256,512]{2,1,0:T(8,128)(2,1)S(1)} collective-permute-done((bf16[2,256,512]{2,1,0:T(8,128)(2,1)S(1)}, bf16[2,256,512]{2,1,0:T(8,128)(2,1)S(1)}, u32[]{:S(2)}, u32[]{:S(2)}) %collective-permute-start.7) | collective-permute-done | bytes 524320 | tf_op jit(solution)/shard_map/ppermute | solution.py:23
  31.2 1.8 %collective-permute-start.8 = (bf16[2,256,512]{2,1,0:T(8,128)(2,1)S(1)}, bf16[2,256,512]{2,1,0:T(8,128)(2,1)S(1)}, u32[]{:S(2)}, u32[]{:S(2)}) collective-permute-start(bf16[2,256,512]{2,1,0:T(8,128)(2,1)S(1)} %fusion.refs_8_), channel_id=1, source_target_pairs={{0,2},{1,3},{2,0},{3,1},{4,6},{5,7},{6,4},{7,5},{8,10},{9,11},{10,... | collective-permute-start | bytes 1572872 | tf_op jit(solution)/shard_map/ppermute | solution.py:23
  33.0 8.6 %gate_up.5 = (bf16[2,256,512]{2,1,0:T(8,128)(2,1)S(1)}, bf16[2,256,512]{2,1,0:T(8,128)(2,1)S(1)}) custom-call(s32[2]{0:T(128)S(1)} %pad_add_fusion.info, bf16[64,1536]{1,0:T(8,128)(2,1)S(1)} %copy-done, bf16[64,1536]{1,0:T(8,128)(2,1)S(1)} %collective-permute-done.refs_1_, bf16[64,1536]{1,0:T(8,128)(2,1)S(1)} %collective-permute-done.1.refs_2_, ...), custom_call_target="tpu_custom_call" | custom-call | flops 6442450944 | bytes 12582912 | tf_op jit(solution)/shard_map/gate_up/pallas_call | solution.py:122
  41.5 3.7 %collective-permute-done.8 = bf16[2,256,512]{2,1,0:T(8,128)(2,1)S(1)} collective-permute-done((bf16[2,256,512]{2,1,0:T(8,128)(2,1)S(1)}, bf16[2,256,512]{2,1,0:T(8,128)(2,1)S(1)}, u32[]{:S(2)}, u32[]{:S(2)}) %collective-permute-start.8) | collective-permute-done | bytes 524320 | tf_op jit(solution)/shard_map/ppermute | solution.py:23
  45.8 1.9 %collective-permute-done.9 = bf16[2,256,512]{2,1,0:T(8,128)(2,1)S(1)} collective-permute-done((bf16[2,256,512]{2,1,0:T(8,128)(2,1)S(1)}, bf16[2,256,512]{2,1,0:T(8,128)(2,1)S(1)}, u32[]{:S(2)}, u32[]{:S(2)}) %collective-permute-start.9) | collective-permute-done | bytes 524320 | tf_op jit(solution)/shard_map/ppermute | solution.py:23
  47.9 1.8 %collective-permute-start.10 = (bf16[2,256,512]{2,1,0:T(8,128)(2,1)S(1)}, bf16[2,256,512]{2,1,0:T(8,128)(2,1)S(1)}, u32[]{:S(2)}, u32[]{:S(2)}) collective-permute-start(bf16[2,256,512]{2,1,0:T(8,128)(2,1)S(1)} %fusion.1.refs_8_), channel_id=1, source_target_pairs={{0,2},{1,3},{2,0},{3,1},{4,6},{5,7},{6,4},{7,5},{8,10},{9,11},{10,... | collective-permute-start | bytes 1572872 | tf_op jit(solution)/shard_map/ppermute | solution.py:23
  49.6 8.8 %gate_up.6 = (bf16[2,256,512]{2,1,0:T(8,128)(2,1)S(1)}, bf16[2,256,512]{2,1,0:T(8,128)(2,1)S(1)}) custom-call(s32[2]{0:T(128)S(1)} %pad_add_fusion.info, bf16[64,1536]{1,0:T(8,128)(2,1)S(1)} %copy-done, bf16[64,1536]{1,0:T(8,128)(2,1)S(1)} %collective-permute-done.refs_1_, bf16[64,1536]{1,0:T(8,128)(2,1)S(1)} %collective-permute-done.1.refs_2_, ...), custom_call_target="tpu_custom_call" | custom-call | flops 6442450944 | bytes 12582912 | tf_op jit(solution)/shard_map/gate_up/pallas_call | solution.py:122
  58.4 3.5 %collective-permute-done.10 = bf16[2,256,512]{2,1,0:T(8,128)(2,1)S(1)} collective-permute-done((bf16[2,256,512]{2,1,0:T(8,128)(2,1)S(1)}, bf16[2,256,512]{2,1,0:T(8,128)(2,1)S(1)}, u32[]{:S(2)}, u32[]{:S(2)}) %collective-permute-start.10) | collective-permute-done | bytes 524320 | tf_op jit(solution)/shard_map/ppermute | solution.py:23
  62.5 1.9 %collective-permute-done.11 = bf16[2,256,512]{2,1,0:T(8,128)(2,1)S(1)} collective-permute-done((bf16[2,256,512]{2,1,0:T(8,128)(2,1)S(1)}, bf16[2,256,512]{2,1,0:T(8,128)(2,1)S(1)}, u32[]{:S(2)}, u32[]{:S(2)}) %collective-permute-start.11) | collective-permute-done | bytes 524320 | tf_op jit(solution)/shard_map/ppermute | solution.py:23
  64.5 1.8 %collective-permute-start.12 = (bf16[2,256,512]{2,1,0:T(8,128)(2,1)S(1)}, bf16[2,256,512]{2,1,0:T(8,128)(2,1)S(1)}, u32[]{:S(2)}, u32[]{:S(2)}) collective-permute-start(bf16[2,256,512]{2,1,0:T(8,128)(2,1)S(1)} %fusion.2.refs_8_), channel_id=1, source_target_pairs={{0,2},{1,3},{2,0},{3,1},{4,6},{5,7},{6,4},{7,5},{8,10},{9,11},{10,... | collective-permute-start | bytes 1572872 | tf_op jit(solution)/shard_map/ppermute | solution.py:23
  66.3 8.6 %gate_up.7 = (bf16[2,256,512]{2,1,0:T(8,128)(2,1)S(1)}, bf16[2,256,512]{2,1,0:T(8,128)(2,1)S(1)}) custom-call(s32[2]{0:T(128)S(1)} %pad_add_fusion.info, bf16[64,1536]{1,0:T(8,128)(2,1)S(1)} %copy-done, bf16[64,1536]{1,0:T(8,128)(2,1)S(1)} %collective-permute-done.refs_1_, bf16[64,1536]{1,0:T(8,128)(2,1)S(1)} %collective-permute-done.1.refs_2_, ...), custom_call_target="tpu_custom_call" | custom-call | flops 6442450944 | bytes 12582912 | tf_op jit(solution)/shard_map/gate_up/pallas_call | solution.py:122
  74.9 3.7 %collective-permute-done.12 = bf16[2,256,512]{2,1,0:T(8,128)(2,1)S(1)} collective-permute-done((bf16[2,256,512]{2,1,0:T(8,128)(2,1)S(1)}, bf16[2,256,512]{2,1,0:T(8,128)(2,1)S(1)}, u32[]{:S(2)}, u32[]{:S(2)}) %collective-permute-start.12) | collective-permute-done | bytes 524320 | tf_op jit(solution)/shard_map/ppermute | solution.py:23
  79.7 1.3 %collective-permute-done.13 = bf16[2,256,512]{2,1,0:T(8,128)(2,1)S(1)} collective-permute-done((bf16[2,256,512]{2,1,0:T(8,128)(2,1)S(1)}, bf16[2,256,512]{2,1,0:T(8,128)(2,1)S(1)}, u32[]{:S(2)}, u32[]{:S(2)}) %collective-permute-start.13) | collective-permute-done | bytes 524320 | tf_op jit(solution)/shard_map/ppermute | solution.py:23
  81.9 1.7 %collective-permute-start.14 = (bf16[2,256,512]{2,1,0:T(8,128)(2,1)S(1)}, bf16[2,256,512]{2,1,0:T(8,128)(2,1)}, u32[]{:S(2)}, u32[]{:S(2)}) collective-permute-start(bf16[2,256,512]{2,1,0:T(8,128)(2,1)S(1)} %fusion.4.refs_5_), channel_id=1, source_target_pairs={{0,2},{1,3},{2,0},{3,1},{4,6},{5,7},{6,4},{7,5},{8,10},{9,11},{10,... | collective-permute-start | bytes 1572872 | tf_op jit(solution)/shard_map/ppermute | solution.py:23
  83.6 4.4 %down.4.refs_5_ = f32[256,1536]{1,0:T(8,128)S(1)} custom-call(s32[2]{0:T(128)S(1)} %pad_add_fusion.info, bf16[2,256,256]{2,1,0:T(8,128)(2,1)S(1)} %fusion.8.refs_9_.refs_0_, bf16[2,256,256]{2,1,0:T(8,128)(2,1)S(1)} %collective-permute-done.17.refs_1_, f32[8,256]{1,0:T(8,128)S(1)} %get-tuple-element.27.refs_5_.refs_2_, ...), custom_call_target="tpu_custom_call" | custom-call | flops 4026531840 | bytes 9437184 | tf_op jit(solution)/shard_map/down/pallas_call | solution.py:198
  88.0 4.4 %down.5.refs_5_ = f32[256,1536]{1,0:T(8,128)S(1)} custom-call(s32[2]{0:T(128)S(1)} %pad_add_fusion.info, bf16[2,256,256]{2,1,0:T(8,128)(2,1)S(1)} %fusion.7.refs_9_.refs_0_, bf16[2,256,256]{2,1,0:T(8,128)(2,1)S(1)} %collective-permute-done.16.refs_1_, f32[8,256]{1,0:T(8,128)S(1)} %get-tuple-element.27.refs_5_.refs_2_, ...), custom_call_target="tpu_custom_call" | custom-call | flops 4026531840 | bytes 9437184 | tf_op jit(solution)/shard_map/down/pallas_call | solution.py:198
  92.4 4.4 %down.6.refs_5_ = f32[256,1536]{1,0:T(8,128)S(1)} custom-call(s32[2]{0:T(128)S(1)} %pad_add_fusion.info, bf16[2,256,256]{2,1,0:T(8,128)(2,1)S(1)} %fusion.6.refs_6_.refs_0_, bf16[2,256,256]{2,1,0:T(8,128)(2,1)S(1)} %collective-permute-done.15.refs_1_, f32[8,256]{1,0:T(8,128)S(1)} %get-tuple-element.27.refs_5_.refs_2_, ...), custom_call_target="tpu_custom_call" | custom-call | flops 4026531840 | bytes 9437184 | tf_op jit(solution)/shard_map/down/pallas_call | solution.py:198
  96.7 1.2 reshape.27
  97.9 1.3 %fusion.3 = f32[2,256,512]{2,1,0:T(8,128)S(1)} fusion(f32[2,256,512]{2,1,0:T(8,128)S(1)} %reshape.27, bf16[2,256,512]{2,1,0:T(8,128)(2,1)} %copy-done.1, bf16[2,256,512]{2,1,0:T(8,128)(2,1)S(1)} %get-tuple-element.36), kind=kLoop, calls=%fused_computation.10 | loop fusion | flops 1048576 | bytes 3145728 | tf_op jit(solution)/shard_map/add | solution.py:242
  99.9 1.2 collective-permute-done.18.refs_1_
  101.1 4.4 %down.7 = (bf16[64,1536]{1,0:T(8,128)(2,1)S(1)}, bf16[64,1536]{1,0:T(8,128)(2,1)S(1)}, bf16[64,1536]{1,0:T(8,128)(2,1)S(1)}, bf16[32,1536]{1,0:T(8,128)(2,1)S(1)}, bf16[32,1536]{1,0:T(8,128)(2,1)S(1)}) custom-call(s32[2]{0:T(128)S(1)} %pad_add_fusion.info, bf16[2,256,256]{2,1,0:T(8,128)(2,1)S(1)} %fusion.5.refs_0_, ...), custom_call_target="tpu_custom_call" | custom-call | flops 4026531840 | bytes 9437184 | tf_op jit(solution)/shard_map/down/pallas_call | solution.py:198
  105.5 3.8 %collective-permute-start.19 = (bf16[32,1536]{1,0:T(8,128)(2,1)S(1)}, bf16[32,1536]{1,0:T(8,128)(2,1)S(1)}, u32[]{:S(2)}, u32[]{:S(2)}) collective-permute-start(bf16[32,1536]{1,0:T(8,128)(2,1)S(1)} %get-tuple-element.46), channel_id=1, source_target_pairs={{0,12},{4,0},{8,4},{12,8},{1,13},{5,1},{9,5},{13,9},{2,14},{6,2},{... | collective-permute-start | bytes 294920 | tf_op jit(solution)/shard_map/ppermute | solution.py:322
  109.4 3.1 %collective-permute-done.19 = bf16[32,1536]{1,0:T(8,128)(2,1)S(1)} collective-permute-done((bf16[32,1536]{1,0:T(8,128)(2,1)S(1)}, bf16[32,1536]{1,0:T(8,128)(2,1)S(1)}, u32[]{:S(2)}, u32[]{:S(2)}) %collective-permute-start.19) | collective-permute-done | bytes 98336 | tf_op jit(solution)/shard_map/ppermute | solution.py:322
  112.5 4.3 %collective-permute-start.20 = (bf16[64,1536]{1,0:T(8,128)(2,1)S(1)}, bf16[64,1536]{1,0:T(8,128)(2,1)S(1)}, u32[]{:S(2)}, u32[]{:S(2)}) collective-permute-start(bf16[64,1536]{1,0:T(8,128)(2,1)S(1)} %pad_maximum_fusion), channel_id=1, source_target_pairs={{0,12},{4,0},{8,4},{12,8},{1,13},{5,1},{9,5},{13,9},{2,14},{6,2},{... | collective-permute-start | bytes 589832 | tf_op jit(solution)/shard_map/ppermute | solution.py:331
  117.0 5.2 %collective-permute-done.20 = bf16[64,1536]{1,0:T(8,128)(2,1)S(1)} collective-permute-done((bf16[64,1536]{1,0:T(8,128)(2,1)S(1)}, bf16[64,1536]{1,0:T(8,128)(2,1)S(1)}, u32[]{:S(2)}, u32[]{:S(2)}) %collective-permute-start.20) | collective-permute-done | bytes 196640 | tf_op jit(solution)/shard_map/ppermute | solution.py:331
  122.2 2.9 %collective-permute-done.22 = bf16[64,1536]{1,0:T(8,128)(2,1)S(1)} collective-permute-done((bf16[64,1536]{1,0:T(8,128)(2,1)S(1)}, bf16[64,1536]{1,0:T(8,128)(2,1)S(1)}, u32[]{:S(2)}, u32[]{:S(2)}) %collective-permute-start.22) | collective-permute-done | bytes 196640 | tf_op jit(solution)/shard_map/ppermute | solution.py:332
  (55 shorter events, 10.9 us)
Async XLA Ops:
  0.0 11.0 %collective-permute-start = (bf16[64,1536]{1,0:T(8,128)(2,1)}, bf16[64,1536]{1,0:T(8,128)(2,1)S(1)}, u32[]{:S(2)}, u32[]{:S(2)}) collective-permute-start(bf16[64,1536]{1,0:T(8,128)(2,1)} %refs_0_.7), channel_id=1, source_target_pairs={{0,4},{4,8},{8,12},{12,0},{1,5},{5,9},{9,13},{13,1},{2,6},{6,10},{... | collective-permute-start | bytes 589832 | tf_op jit(solution)/shard_map/ppermute | solution.py:306
  3.0 11.0 %collective-permute-start.1 = (bf16[64,1536]{1,0:T(8,128)(2,1)}, bf16[64,1536]{1,0:T(8,128)(2,1)S(1)}, u32[]{:S(2)}, u32[]{:S(2)}) collective-permute-start(bf16[64,1536]{1,0:T(8,128)(2,1)} %refs_0_.7), channel_id=1, source_target_pairs={{0,12},{4,0},{8,4},{12,8},{1,13},{5,1},{9,5},{13,9},{2,14},{6,2},{... | collective-permute-start | bytes 589832 | tf_op jit(solution)/shard_map/ppermute | solution.py:306
  6.4 10.8 %collective-permute-start.4 = (f32[16,64]{1,0:T(8,128)S(1)}, f32[16,64]{1,0:T(8,128)S(1)}, u32[]{:S(2)}, u32[]{:S(2)}) collective-permute-start(f32[16,64]{1,0:T(8,128)S(1)} %pad_maximum_fusion.2.refs_0_), channel_id=1, source_target_pairs={{0,4},{4,8},{8,12},{12,0},{1,5},{5,9},{9,13},{13,1},{2,6},{6,10},{... | collective-permute-start | bytes 12296 | tf_op jit(solution)/shard_map/ppermute | solution.py:263
  6.4 10.8 %collective-permute-start.5 = (f32[16,64]{1,0:T(8,128)S(1)}, f32[16,64]{1,0:T(8,128)S(1)}, u32[]{:S(2)}, u32[]{:S(2)}) collective-permute-start(f32[16,64]{1,0:T(8,128)S(1)} %pad_maximum_fusion.2.refs_0_), channel_id=1, source_target_pairs={{0,12},{4,0},{8,4},{12,8},{1,13},{5,1},{9,5},{13,9},{2,14},{6,2},{... | collective-permute-start | bytes 12296 | tf_op jit(solution)/shard_map/ppermute | solution.py:263
  10.3 7.0 %collective-permute-start.6 = (f32[16,64]{1,0:T(8,128)S(1)}, f32[16,64]{1,0:T(8,128)S(1)}, u32[]{:S(2)}, u32[]{:S(2)}) collective-permute-start(f32[16,64]{1,0:T(8,128)S(1)} %pad_maximum_fusion.2.refs_0_), channel_id=1, source_target_pairs={{0,8},{4,12},{8,0},{12,4},{1,9},{5,13},{9,1},{13,5},{2,10},{6,14},... | collective-permute-start | bytes 12296 | tf_op jit(solution)/shard_map/ppermute | solution.py:263
  11.0 7.6 %collective-permute-start.2 = (bf16[32,1536]{1,0:T(8,128)(2,1)S(1)}, bf16[32,1536]{1,0:T(8,128)(2,1)S(1)}, u32[]{:S(2)}, u32[]{:S(2)}) collective-permute-start(bf16[32,1536]{1,0:T(8,128)(2,1)S(1)} %slice.66), channel_id=1, source_target_pairs={{0,4},{4,8},{8,12},{12,0},{1,5},{5,9},{9,13},{13,1},{2,6},{6,10},{... | collective-permute-start | bytes 294920 | tf_op jit(solution)/shard_map/ppermute | solution.py:310
  14.0 5.6 %collective-permute-start.3 = (bf16[32,1536]{1,0:T(8,128)(2,1)S(1)}, bf16[32,1536]{1,0:T(8,128)(2,1)S(1)}, u32[]{:S(2)}, u32[]{:S(2)}) collective-permute-start(bf16[32,1536]{1,0:T(8,128)(2,1)S(1)} %slice.67), channel_id=1, source_target_pairs={{0,12},{4,0},{8,4},{12,8},{1,13},{5,1},{9,5},{13,9},{2,14},{6,2},{... | collective-permute-start | bytes 294920 | tf_op jit(solution)/shard_map/ppermute | solution.py:310
  19.6 0.9 copy-start
  29.1 2.0 %collective-permute-start.7 = (bf16[2,256,512]{2,1,0:T(8,128)(2,1)S(1)}, bf16[2,256,512]{2,1,0:T(8,128)(2,1)S(1)}, u32[]{:S(2)}, u32[]{:S(2)}) collective-permute-start(bf16[2,256,512]{2,1,0:T(8,128)(2,1)S(1)} %get-tuple-element.29), channel_id=1, source_target_pairs={{0,1},{1,0},{2,3},{3,2},{4,5},{5,4},{6,7},{7,6},{8,9},{9,8},{10,11... | collective-permute-start | bytes 1572872 | tf_op jit(solution)/shard_map/ppermute | solution.py:23
  31.2 14.0 %collective-permute-start.8 = (bf16[2,256,512]{2,1,0:T(8,128)(2,1)S(1)}, bf16[2,256,512]{2,1,0:T(8,128)(2,1)S(1)}, u32[]{:S(2)}, u32[]{:S(2)}) collective-permute-start(bf16[2,256,512]{2,1,0:T(8,128)(2,1)S(1)} %fusion.refs_8_), channel_id=1, source_target_pairs={{0,2},{1,3},{2,0},{3,1},{4,6},{5,7},{6,4},{7,5},{8,10},{9,11},{10,... | collective-permute-start | bytes 1572872 | tf_op jit(solution)/shard_map/ppermute | solution.py:23
  45.7 2.0 %collective-permute-start.9 = (bf16[2,256,512]{2,1,0:T(8,128)(2,1)S(1)}, bf16[2,256,512]{2,1,0:T(8,128)(2,1)S(1)}, u32[]{:S(2)}, u32[]{:S(2)}) collective-permute-start(bf16[2,256,512]{2,1,0:T(8,128)(2,1)S(1)} %get-tuple-element.32), channel_id=1, source_target_pairs={{0,1},{1,0},{2,3},{3,2},{4,5},{5,4},{6,7},{7,6},{8,9},{9,8},{10,11... | collective-permute-start | bytes 1572872 | tf_op jit(solution)/shard_map/ppermute | solution.py:23
  47.9 14.0 %collective-permute-start.10 = (bf16[2,256,512]{2,1,0:T(8,128)(2,1)S(1)}, bf16[2,256,512]{2,1,0:T(8,128)(2,1)S(1)}, u32[]{:S(2)}, u32[]{:S(2)}) collective-permute-start(bf16[2,256,512]{2,1,0:T(8,128)(2,1)S(1)} %fusion.1.refs_8_), channel_id=1, source_target_pairs={{0,2},{1,3},{2,0},{3,1},{4,6},{5,7},{6,4},{7,5},{8,10},{9,11},{10,... | collective-permute-start | bytes 1572872 | tf_op jit(solution)/shard_map/ppermute | solution.py:23
  62.4 2.0 %collective-permute-start.11 = (bf16[2,256,512]{2,1,0:T(8,128)(2,1)S(1)}, bf16[2,256,512]{2,1,0:T(8,128)(2,1)S(1)}, u32[]{:S(2)}, u32[]{:S(2)}) collective-permute-start(bf16[2,256,512]{2,1,0:T(8,128)(2,1)S(1)} %get-tuple-element.35), channel_id=1, source_target_pairs={{0,1},{1,0},{2,3},{3,2},{4,5},{5,4},{6,7},{7,6},{8,9},{9,8},{10,11... | collective-permute-start | bytes 1572872 | tf_op jit(solution)/shard_map/ppermute | solution.py:23
  64.5 14.0 %collective-permute-start.12 = (bf16[2,256,512]{2,1,0:T(8,128)(2,1)S(1)}, bf16[2,256,512]{2,1,0:T(8,128)(2,1)S(1)}, u32[]{:S(2)}, u32[]{:S(2)}) collective-permute-start(bf16[2,256,512]{2,1,0:T(8,128)(2,1)S(1)} %fusion.2.refs_8_), channel_id=1, source_target_pairs={{0,2},{1,3},{2,0},{3,1},{4,6},{5,7},{6,4},{7,5},{8,10},{9,11},{10,... | collective-permute-start | bytes 1572872 | tf_op jit(solution)/shard_map/ppermute | solution.py:23
  79.1 2.0 %collective-permute-start.13 = (bf16[2,256,512]{2,1,0:T(8,128)(2,1)S(1)}, bf16[2,256,512]{2,1,0:T(8,128)(2,1)S(1)}, u32[]{:S(2)}, u32[]{:S(2)}) collective-permute-start(bf16[2,256,512]{2,1,0:T(8,128)(2,1)S(1)} %get-tuple-element.38), channel_id=1, source_target_pairs={{0,1},{1,0},{2,3},{3,2},{4,5},{5,4},{6,7},{7,6},{8,9},{9,8},{10,11... | collective-permute-start | bytes 1572872 | tf_op jit(solution)/shard_map/ppermute | solution.py:23
  79.2 4.4 %collective-permute-start.17 = (bf16[2,256,256]{2,1,0:T(8,128)(2,1)S(1)}, bf16[2,256,256]{2,1,0:T(8,128)(2,1)S(1)}, u32[]{:S(2)}, u32[]{:S(2)}) collective-permute-start(bf16[2,256,256]{2,1,0:T(8,128)(2,1)S(1)} %fusion.8.refs_9_.refs_0_), channel_id=1, source_target_pairs={{0,1},{1,0},{2,3},{3,2},{4,5},{5,4},{6,7},{7,6},{8,9},{9,8},{10,11... | collective-permute-start | bytes 786440 | tf_op jit(solution)/shard_map/ppermute | solution.py:23
  79.7 8.3 %collective-permute-start.16 = (bf16[2,256,256]{2,1,0:T(8,128)(2,1)S(1)}, bf16[2,256,256]{2,1,0:T(8,128)(2,1)S(1)}, u32[]{:S(2)}, u32[]{:S(2)}) collective-permute-start(bf16[2,256,256]{2,1,0:T(8,128)(2,1)S(1)} %fusion.7.refs_9_.refs_0_), channel_id=1, source_target_pairs={{0,1},{1,0},{2,3},{3,2},{4,5},{5,4},{6,7},{7,6},{8,9},{9,8},{10,11... | collective-permute-start | bytes 786440 | tf_op jit(solution)/shard_map/ppermute | solution.py:23
  81.1 0.8 copy-start.1
  81.9 14.8 %collective-permute-start.14 = (bf16[2,256,512]{2,1,0:T(8,128)(2,1)S(1)}, bf16[2,256,512]{2,1,0:T(8,128)(2,1)}, u32[]{:S(2)}, u32[]{:S(2)}) collective-permute-start(bf16[2,256,512]{2,1,0:T(8,128)(2,1)S(1)} %fusion.4.refs_5_), channel_id=1, source_target_pairs={{0,2},{1,3},{2,0},{3,1},{4,6},{5,7},{6,4},{7,5},{8,10},{9,11},{10,... | collective-permute-start | bytes 1572872 | tf_op jit(solution)/shard_map/ppermute | solution.py:23
  83.6 8.8 %collective-permute-start.15 = (bf16[2,256,256]{2,1,0:T(8,128)(2,1)S(1)}, bf16[2,256,256]{2,1,0:T(8,128)(2,1)S(1)}, u32[]{:S(2)}, u32[]{:S(2)}) collective-permute-start(bf16[2,256,256]{2,1,0:T(8,128)(2,1)S(1)} %fusion.6.refs_6_.refs_0_), channel_id=1, source_target_pairs={{0,1},{1,0},{2,3},{3,2},{4,5},{5,4},{6,7},{7,6},{8,9},{9,8},{10,11... | collective-permute-start | bytes 786440 | tf_op jit(solution)/shard_map/ppermute | solution.py:23
  99.4 1.7 %collective-permute-start.18 = (bf16[2,256,256]{2,1,0:T(8,128)(2,1)S(1)}, bf16[2,256,256]{2,1,0:T(8,128)(2,1)S(1)}, u32[]{:S(2)}, u32[]{:S(2)}) collective-permute-start(bf16[2,256,256]{2,1,0:T(8,128)(2,1)S(1)} %fusion.5.refs_0_), channel_id=1, source_target_pairs={{0,1},{1,0},{2,3},{3,2},{4,5},{5,4},{6,7},{7,6},{8,9},{9,8},{10,11... | collective-permute-start | bytes 786440 | tf_op jit(solution)/shard_map/ppermute | solution.py:23
  105.5 7.0 %collective-permute-start.19 = (bf16[32,1536]{1,0:T(8,128)(2,1)S(1)}, bf16[32,1536]{1,0:T(8,128)(2,1)S(1)}, u32[]{:S(2)}, u32[]{:S(2)}) collective-permute-start(bf16[32,1536]{1,0:T(8,128)(2,1)S(1)} %get-tuple-element.46), channel_id=1, source_target_pairs={{0,12},{4,0},{8,4},{12,8},{1,13},{5,1},{9,5},{13,9},{2,14},{6,2},{... | collective-permute-start | bytes 294920 | tf_op jit(solution)/shard_map/ppermute | solution.py:322
  109.3 7.5 %collective-permute-start.21 = (bf16[32,1536]{1,0:T(8,128)(2,1)S(1)}, bf16[32,1536]{1,0:T(8,128)(2,1)S(1)}, u32[]{:S(2)}, u32[]{:S(2)}) collective-permute-start(bf16[32,1536]{1,0:T(8,128)(2,1)S(1)} %get-tuple-element.48), channel_id=1, source_target_pairs={{0,4},{4,8},{8,12},{12,0},{1,5},{5,9},{9,13},{13,1},{2,6},{6,10},{... | collective-permute-start | bytes 294920 | tf_op jit(solution)/shard_map/ppermute | solution.py:322
  112.5 9.7 %collective-permute-start.20 = (bf16[64,1536]{1,0:T(8,128)(2,1)S(1)}, bf16[64,1536]{1,0:T(8,128)(2,1)S(1)}, u32[]{:S(2)}, u32[]{:S(2)}) collective-permute-start(bf16[64,1536]{1,0:T(8,128)(2,1)S(1)} %pad_maximum_fusion), channel_id=1, source_target_pairs={{0,12},{4,0},{8,4},{12,8},{1,13},{5,1},{9,5},{13,9},{2,14},{6,2},{... | collective-permute-start | bytes 589832 | tf_op jit(solution)/shard_map/ppermute | solution.py:331
  116.9 8.2 %collective-permute-start.22 = (bf16[64,1536]{1,0:T(8,128)(2,1)S(1)}, bf16[64,1536]{1,0:T(8,128)(2,1)S(1)}, u32[]{:S(2)}, u32[]{:S(2)}) collective-permute-start(bf16[64,1536]{1,0:T(8,128)(2,1)S(1)} %pad_maximum_fusion.1), channel_id=1, source_target_pairs={{0,4},{4,8},{8,12},{12,0},{1,5},{5,9},{9,13},{13,1},{2,6},{6,10},{... | collective-permute-start | bytes 589832 | tf_op jit(solution)/shard_map/ppermute | solution.py:332

commit v5 on v4

--- a/solution.py
+++ b/solution.py
@@ -63,87 +63,141 @@
     )(info, *meta)
 
 
-def gate_up_body(n, experts, n_dp, after, info, *refs):
-    tokens, (rank_in, w_gate, w_up), refs = refs[:n], refs[n : n + 3], refs[n + 3 + after :]
-    send, keep, rank, feed, rows, held, rank_sem, feed_sem, held_sem = refs
-    most = rows.shape[0] // len(experts)
-    width = send.shape[2] // 2
-    pieces = list(range(1, n_dp, 2)) + list(range(0, n_dp, 2))
-    mats = [(m, x) for m in range(2) for x in range(len(experts))]
-
-    def copy(l, m, x):
-        units = pl.ds(pl.multiple_of((l ^ info[1]) * width, width), width)
-        i = m * len(experts) + x
-        return pltpu.make_async_copy(
-            (w_gate, w_up)[m].at[experts[x], :, units],
-            held.at[i, :, pl.ds(l * width, width)],
-            held_sem.at[l, i],
+def fetches(w_gate, w_up, experts, units, to, sem):
+    return [
+        pltpu.make_async_copy(w.at[e, :, units], to.at[i], sem.at[i])
+        for i, (w, e) in enumerate((w, e) for w in (w_gate, w_up) for e in experts)
+    ]
+
+
+def units_of(l, info, width):
+    return pl.ds(pl.multiple_of((l ^ info[1]) * width, width), width)
+
+
+def products(rows, weights, to, j):
+    most = rows.shape[0] * 2 // weights.shape[0]
+    width = weights.shape[2]
+    for i in range(weights.shape[0]):
+        m, x = divmod(i, weights.shape[0] // 2)
+        mine = slice(x * most, (x + 1) * most)
+        to[j, mine, m * width : (m + 1) * width] = jnp.dot(
+            rows[mine], weights[i], preferred_element_type=jnp.float32
+        ).astype(jnp.bfloat16)
+
+
+def shares_body(n, experts, shares, ahead, after, info, *refs):
+    sources, refs = refs[: n + 1] if n else refs[:1], refs[n + 1 if n else 1 :]
+    (given, w_gate, w_up), refs = refs[:3], refs[3 + after :]
+    to, refs = refs[0], refs[1:]
+    width = given.shape[2]
+    rows = sources[0]
+    if n:
+        rows, refs = refs[0], refs[1:]
+    if ahead is not None:
+        handed, refs = refs[0], refs[1:]
+    held, held_sem, handed_sem, refs = refs[0], refs[1], refs[2], refs[3:]
+    rest = [
+        fetches(w_gate, w_up, experts, units_of(l, info, width), held.at[j], held_sem.at[j])
+        for j, l in enumerate(shares[1:])
+    ]
+    on = []
+    if ahead is not None:
+        on = fetches(w_gate, w_up, ahead[0], units_of(ahead[1], info, width), handed, handed_sem)
+    if n:
+        feed, feed_sem = refs
+        at, feeds = 0, []
+        for s in range(n):
+            tok = sources[s].shape[0]
+            feeds.append(pltpu.make_async_copy(sources[s], feed.at[pl.ds(at, tok)], feed_sem.at[s]))
+            at += tok
+        for copy in feeds:
+            copy.start()
+    for copies in rest + [on]:
+        for copy in copies:
+            copy.start()
+    if n:
+        rank = sources[n]
+        most = rows.shape[0] // len(experts)
+        r = lax.broadcasted_iota(jnp.int32, (most, at), 0).astype(jnp.float32)
+        pick = jnp.concatenate(
+            [jnp.where(r == rank[e : e + 1, :], 1.0, 0.0).astype(jnp.bfloat16) for e in experts], axis=0
         )
-
-    ranks = pltpu.make_async_copy(rank_in, rank, rank_sem.at[0])
-    ranks.start()
-    at, feeds = 0, []
-    for s in range(n):
-        tok = tokens[s].shape[0]
-        feeds.append(pltpu.make_async_copy(tokens[s], feed.at[pl.ds(at, tok)], feed_sem.at[s]))
-        at += tok
-    for part in feeds:
-        part.start()
-    for m, x in mats:
-        copy(pieces[0], m, x).start()
-    ranks.wait()
-    r = lax.broadcasted_iota(jnp.int32, (most, at), 0).astype(jnp.float32)
-    pick = jnp.concatenate(
-        [jnp.where(r == rank[e : e + 1, :], 1.0, 0.0).astype(jnp.bfloat16) for e in experts], axis=0
-    )
-    for part in feeds:
-        part.wait()
-    rows[...] = jnp.dot(pick, feed[...], preferred_element_type=jnp.float32).astype(jnp.bfloat16)
-    for l, ahead in zip(pieces, pieces[1:] + [None]):
-        if ahead is not None:
-            for m, x in mats:
-                copy(ahead, m, x).start()
-        to = send if l % 2 else keep
-        for m, x in mats:
-            copy(l, m, x).wait()
-            mine = slice(x * most, (x + 1) * most)
-            to[l // 2, mine, m * width : (m + 1) * width] = jnp.dot(
-                rows[mine],
-                held[m * len(experts) + x, :, l * width : (l + 1) * width],
-                preferred_element_type=jnp.float32,
-            ).astype(jnp.bfloat16)
-
-
-def gate_up(tokens, rank, info, w_gate, w_up, experts, most, n_dp, after):
-    n, local = len(tokens), tokens[0].shape[1]
-    hidden = w_gate.shape[2]
-    rows, mats = most * len(experts), 2 * len(experts)
-    out = jax.ShapeDtypeStruct((max(n_dp // 2, 1), rows, 2 * hidden // n_dp), jnp.bfloat16)
+        for copy in feeds:
+            copy.wait()
+        rows[...] = jnp.dot(pick, feed[...], preferred_element_type=jnp.float32).astype(jnp.bfloat16)
+    products(rows, given, to, 0)
+    for j, copies in enumerate(rest):
+        for copy in copies:
+            copy.wait()
+        products(rows, held.at[j], to, j + 1)
+    for copy in on:
+        copy.wait()
+
+
+def some_shares(sources, info, given, w_gate, w_up, experts, most, shares, ahead, after):
+    n = len(sources) - 1
+    mats, local, width = given.shape
+    rows = most * len(experts)
+    pieces = max(len(shares) - 1, 1)
+    out = [jax.ShapeDtypeStruct((len(shares), rows, 2 * width), jnp.bfloat16)]
+    if n:
+        out.append(jax.ShapeDtypeStruct((rows, local), jnp.bfloat16))
+    if ahead is not None:
+        out.append(jax.ShapeDtypeStruct(given.shape, jnp.bfloat16))
+    scratch = [
+        pltpu.VMEM((pieces, mats, local, width), jnp.bfloat16),
+        pltpu.SemaphoreType.DMA((pieces, mats)),
+        pltpu.SemaphoreType.DMA((mats,)),
+    ]
+    if n:
+        scratch += [
+            pltpu.VMEM((sources[-1].shape[1], local), jnp.bfloat16),
+            pltpu.SemaphoreType.DMA((n,)),
+        ]
     return pl.pallas_call(
-        functools.partial(gate_up_body, n, experts, n_dp, len(after)),
-        out_shape=(out, out),
-        in_specs=[SMEM] + [HERE] * (n + 3 + len(after)),
+        functools.partial(shares_body, n, experts, shares, ahead, len(after)),
+        out_shape=tuple(out),
+        in_specs=[SMEM] + [HERE] * n + [VMEM] * 2 + [HERE] * (2 + len(after)),
+        out_specs=(VMEM,) * len(out),
+        scratch_shapes=scratch,
+        compiler_params=pltpu.CompilerParams(vmem_limit_bytes=40 << 20),
+        cost_estimate=pl.CostEstimate(flops=1, bytes_accessed=1, transcendentals=0),
+        name="send_shares" if n else "keep_shares",
+    )(info, *sources, given, w_gate, w_up, *after)
+
+
+def stage_body(experts, share, info, tokens, w_gate, w_up, copied, handed, sem, handed_sem):
+    width = handed.shape[2]
+    own = pltpu.make_async_copy(tokens, copied, sem.at[0])
+    own.start()
+    copies = fetches(w_gate, w_up, experts, units_of(share, info, width), handed, handed_sem)
+    for copy in copies:
+        copy.start()
+    own.wait()
+    for copy in copies:
+        copy.wait()
+
+
+def stage(tokens, info, w_gate, w_up, experts, share, n_dp):
+    _, local, hidden = w_gate.shape
+    mats = 2 * len(experts)
+    return pl.pallas_call(
+        functools.partial(stage_body, experts, share),
+        out_shape=(
+            jax.ShapeDtypeStruct(tokens.shape, tokens.dtype),
+            jax.ShapeDtypeStruct((mats, local, hidden // n_dp), jnp.bfloat16),
+        ),
+        in_specs=[SMEM] + [HERE] * 3,
         out_specs=(VMEM, VMEM),
-        scratch_shapes=[
-            pltpu.VMEM(rank.shape, jnp.float32),
-            pltpu.VMEM((rank.shape[1], local), jnp.bfloat16),
-            pltpu.VMEM((rows, local), jnp.bfloat16),
-            pltpu.VMEM((mats, local, hidden), jnp.bfloat16),
-            pltpu.SemaphoreType.DMA((1,)),
-            pltpu.SemaphoreType.DMA((n,)),
-            pltpu.SemaphoreType.DMA((n_dp, mats)),
-        ],
+        scratch_shapes=[pltpu.SemaphoreType.DMA((1,)), pltpu.SemaphoreType.DMA((mats,))],
         compiler_params=pltpu.CompilerParams(vmem_limit_bytes=40 << 20),
-        cost_estimate=pl.CostEstimate(
-            flops=8 * mats * most * local * hidden,
-            bytes_accessed=2 * mats * local * hidden,
-            transcendentals=0,
-        ),
-        name="gate_up",
-    )(info, *tokens, rank, w_gate, w_up, *after)
-
-
-def down_body(n_part, cuts, experts, first, after, info, *refs):
+        cost_estimate=pl.CostEstimate(flops=1, bytes_accessed=1, transcendentals=0),
+        name="stage",
+    )(info, tokens, w_gate, w_up)
+
+
+def down_body(lanes, cuts, experts, first, after, info, *refs):
+    n_part = len(lanes)
     parts, (rank, wt, w_down), refs = refs[:n_part], refs[n_part : n_part + 3], refs[n_part + 3 :]
     before = None if first else refs[0]
     refs = refs[(0 if first else 1) + after :]
@@ -160,10 +214,9 @@
                 w_down.at[e, :, cols], held.at[x, :, cols], held_sem.at[i, x]
             )
             copies[i, x].start()
-    for p, part in enumerate(parts):
-        for j in range(part.shape[0]):
-            at = pl.multiple_of(((2 * j + p) ^ info[1]) * width, width)
-            hidden[:, pl.ds(at, width)] = part[j]
+    for part, (at, shares) in zip(parts, lanes):
+        for j, l in enumerate(shares):
+            hidden[:, units_of(l, info, width)] = part[j, :, at : at + width]
     r = lax.broadcasted_iota(jnp.int32, (most, mix.shape[1]), 0).astype(jnp.float32)
     for x, e in enumerate(experts):
         mix[x * most : (x + 1) * most, :] = jnp.where(
@@ -189,6 +242,7 @@
 
 
 def down(parts, rank, wt, info, w_down, total, experts, cuts, after):
+    parts, lanes = [part for part, *_ in parts], [tuple(where) for _, *where in parts]
     rows = parts[0].shape[1]
     _, hidden, local = w_down.shape
     tokens = rank.shape[1]
@@ -196,7 +250,7 @@
     kind = jnp.bfloat16 if last else jnp.float32
     mats = len(experts)
     outs = pl.pallas_call(
-        functools.partial(down_body, len(parts), cuts, experts, first, len(after)),
+        functools.partial(down_body, lanes, cuts, experts, first, len(after)),
         out_shape=tuple(jax.ShapeDtypeStruct((cut, local), kind) for cut in cuts),
         in_specs=[SMEM]
         + [VMEM] * (len(parts) + 2)
@@ -222,30 +276,32 @@
     return outs if last else outs[0]
 
 
-def chip_sums(send, keep, n_dp):
-    total = keep.astype(jnp.float32)
-    late = jnp.zeros(total.shape, jnp.float32)
-    for b in bits_of(n_dp):
-        if b > 0:
-            total = total + late
-            send = total.astype(jnp.bfloat16)
-        late = flip(send, "dp", 1 << b).astype(jnp.float32)
-        if b > 0:
-            pairs = (late.shape[0] >> b, 2, 1 << (b - 1)) + late.shape[1:]
-            late = jnp.flip(late.reshape(pairs), axis=1).reshape(late.shape)
-    return total, late, send
-
-
 def finish(total, late, after):
     if after:
         late, *_ = lax.optimization_barrier((late, *after))
-    gate_up = total + late
+    gate_up = total + late.astype(jnp.float32)
     width = gate_up.shape[2] // 2
     return (jax.nn.silu(gate_up[:, :, :width]) * gate_up[:, :, width:]).astype(jnp.bfloat16)
 
 
-def all_parts(mine, n_dp):
-    return [mine, flip(mine, "dp", 1)] if n_dp > 1 else [mine]
+def chip_sums(send, keep, bits):
+    total = keep.astype(jnp.float32) + flip(send, "dp", 1).astype(jnp.float32)
+    for b in bits[1:-1]:
+        total = total[0::2] + flip(total[1::2].astype(jnp.bfloat16), "dp", 1 << b).astype(jnp.float32)
+    return total[0::2], total[1::2].astype(jnp.bfloat16)
+
+
+def everyone_s(share, other, at, bits):
+    width = share.shape[2]
+    top = 1 << bits[-1]
+    parts = [(share, 0, [0]), (other, at, [top])]
+    held, whose = jnp.concatenate([share, other[:, :, at : at + width]], axis=0), [0, top]
+    for b in reversed(bits[:-1]):
+        theirs = flip(held, "dp", 1 << b)
+        parts.append((theirs, 0, [l | 1 << b for l in whose]))
+        if b > 0:
+            held, whose = jnp.concatenate([held, theirs], axis=0), whose + parts[-1][2]
+    return parts
 
 
 def on_device(tokens, expert_ids, scores, w_gate, w_up, w_down):
@@ -268,26 +324,46 @@
 
     cuts = [feed.shape[0] for feed in feeds]
     of = lambda c: list(range(c * per_chunk, (c + 1) * per_chunk))
-    shares, sent, parts, total = [], [], [], None
+    bits = bits_of(n_dp)
+    cross = 1 << bits[-1]
+    odd, even = list(range(1, n_dp, 2)), list(range(0, n_dp, 2))
+    feeds[0], given = stage(tokens, info, w_gate, w_up, of(0), odd[0], n_dp)
+    sent, parts, total = [], [], None
+    share = kept = late = None
 
     def add(c, after):
         outs = cuts if c == chunks - 1 else [sum(cuts)]
         return down(parts[c], rank, wt, info, w_down, total, of(c), outs, after)
 
     for c in range(chunks):
-        after = ([sent[c - 1]] if c >= 1 else []) + ([shares[c - 2]] if c >= 2 else [])
-        send, keep = gate_up(feeds, rank, info, w_gate, w_up, of(c), most, n_dp, after)
+        last = c == chunks - 1
+        send, rows, given = some_shares(
+            [*feeds, rank], info, given, w_gate, w_up, of(c), most, odd, (of(c), 0), sent[-1:]
+        )
+        keep, *given = some_shares(
+            [rows], info, given, w_gate, w_up, of(c), most, even, None if last else (of(c + 1), odd[0]), []
+        )
+        given = given[0] if given else None
+        before, behind = kept, late
+        kept, out = chip_sums(send, keep, bits)
+        width = out.shape[2]
         if c > 0:
-            send = lax.optimization_barrier((send, shares[-1]))[0]
-        mine, late, last_sent = chip_sums(send, keep, n_dp)
-        sent.append(last_sent)
+            share = finish(before, behind[:, :, :width], [])
+            out = jnp.concatenate([out, share], axis=2)
+        sent.append(out)
+        late = flip(out, "dp", cross)
         if c > 0:
-            parts.append(all_parts(lax.optimization_barrier((shares[-1], last_sent))[0], n_dp))
-        early = range(c) if c == chunks - 1 else []
-        for d in early:
-            total = add(d, [last_sent, shares[-1]] if d == 0 else [])
-        shares.append(finish(mine, late, [total] if early else []))
-    parts.append(all_parts(shares[-1], n_dp))
+            parts.append(everyone_s(share, late, width, bits))
+        if last:
+            for d in range(min(c - 1, 2)):
+                total = add(d, [out] if d == 0 else [])
+    share = finish(kept, late[:, :, :width], [] if total is None else [total])
+    other = flip(share, "dp", cross)
+    for c in range(max(min(chunks - 2, 2), 0), chunks - 1):
+        total = add(c, [share])
+    if total is not None:
+        other = lax.optimization_barrier((other, total))[0]
+    parts.append(everyone_s(share, other, 0, bits))
     total = add(chunks - 1, [])
     return returned(total, "expert") if n_owner > 1 else total[0].astype(jnp.bfloat16)
 

time: 126 us -> 108 us (0.86)
  waiting for transfers between devices: 35.5 us -> 16.9 us
  Pallas kernels: 52.6 us -> 56.9 us
  other arithmetic: 5.82 us -> 3.67 us
  local copies, waits for them, and re-layouts: 2.8 us -> 1.14 us
    ppermute x12 -> x13, waiting for transfers between devices: 19 us -> 6.64 us  [flip(): lax.ppermute(x, axis, [(i, i ^ k) for i in range(lax.axis_size(axis))])]
    ppermute x1, waiting for transfers between devices: 5.24 us -> 0.35 us  [returned(): low = lax.ppermute(a.astype(jnp.bfloat16), axis, down_)]
    pallas_call x8 -> x13, Pallas kernels: 51.9 us -> 56.1 us  [the longest x8 36 us: some_shares(): pl.pallas_call(functools.partial(shares_body, n, experts, shares, ahead,...]
    ppermute x1, waiting for transfers between devices: 0.01 us -> 3.59 us  [returned(): lax.ppermute(partials[-1], axis, up)]
    ppermute x1, waiting for transfers between devices: 3.06 us -> 0.01 us  [returned(): lax.ppermute(partials[-2], axis, down_)]
    ppermute x1, starting transfers between devices: 2.03 us -> 5.05 us  [gathered(): lax.ppermute(above, axis, down_)]
    ppermute x1, starting transfers between devices: 3.02 us -> 0.01 us  [gathered(): lax.ppermute(below, axis, up)]
    ppermute x1, waiting for transfers between devices: 2.87 us -> 0.01 us  [gathered(): lax.ppermute(above, axis, down_)]
  transfers between devices with their start and end apart: 23 -> 24, of which waited for: 15 -> 11; matrix products, arithmetic and copies ran while one was open for 1% -> 2% of each run, Pallas kernels for 32% -> 44%
where the time goes in v5:
time: 108 us
  Pallas kernels  56.9 us (53%)
  starting transfers between devices  28.8 us (27%)
  waiting for transfers between devices  16.9 us (16%)
  other arithmetic  3.67 us (3%)
  local copies, waits for them, and re-layouts  1.14 us (1%)
    pallas_call x8, Pallas kernels, some_shares(): pl.pallas_call(functools.partial(shares_body, n, experts, shares, ahead,...  36 us
    pallas_call x4, Pallas kernels, down(): pl.pallas_call(functools.partial(down_body, lanes, cuts, experts, first,...  17.4 us
    ppermute x13, waiting for transfers between devices, flip(): lax.ppermute(x, axis, [(i, i ^ k) for i in range(lax.axis_size(axis))])  6.64 us
    ppermute x13, starting transfers between devices, flip(): lax.ppermute(x, axis, [(i, i ^ k) for i in range(lax.axis_size(axis))])  5.78 us
    ppermute x1, waiting for transfers between devices, returned(): high = lax.ppermute(b.astype(jnp.bfloat16), axis, up)  5.34 us
    ppermute x1, starting transfers between devices, gathered(): lax.ppermute(above, axis, down_)  5.05 us
    ppermute x3, starting transfers between devices, on_device(): lax.ppermute(meta, 'expert', [(i, (i - k) % n_owner) for i in range(n_own...  4.39 us
    ppermute x1, starting transfers between devices, gathered(): lax.ppermute(above[half:], axis, down_)  4.08 us
  transfers between devices with their start and end apart: 24, of which 11 were waited for; matrix products, arithmetic and copies ran while one was open for 2% of the time, Pallas kernels for 44%

profile of v5, /device:TPU:0, one launch (start us, length us, event | category | flops | bytes accessed | tf_op | source)
XLA Modules:
  0.0 107.9 jit_solution(12390119713618631173)
XLA Ops:
  0.0 5.0 %collective-permute-start.1 = (bf16[64,1536]{1,0:T(8,128)(2,1)}, bf16[64,1536]{1,0:T(8,128)(2,1)S(1)}, u32[]{:S(2)}, u32[]{:S(2)}) collective-permute-start(bf16[64,1536]{1,0:T(8,128)(2,1)} %tokens.1), channel_id=1, source_target_pairs={{0,12},{4,0},{8,4},{12,8},{1,13},{5,1},{9,5},{13,9},{2,14},{6,2},{... | collective-permute-start | bytes 589832 | tf_op jit(solution)/shard_map/ppermute | solution.py:382
  6.4 1.0 collective-permute-start.6
  7.4 2.8 %collective-permute-start.5 = (f32[16,64]{1,0:T(8,128)S(1)}, f32[16,64]{1,0:T(8,128)S(1)}, u32[]{:S(2)}, u32[]{:S(2)}) collective-permute-start(f32[16,64]{1,0:T(8,128)S(1)} %pad_maximum_fusion.9.refs_0_), channel_id=1, source_target_pairs={{0,12},{4,0},{8,4},{12,8},{1,13},{5,1},{9,5},{13,9},{2,14},{6,2},{... | collective-permute-start | bytes 12296 | tf_op jit(solution)/shard_map/ppermute | solution.py:319
  10.8 4.1 %collective-permute-start.3 = (bf16[32,1536]{1,0:T(8,128)(2,1)S(1)}, bf16[32,1536]{1,0:T(8,128)(2,1)S(1)}, u32[]{:S(2)}, u32[]{:S(2)}) collective-permute-start(bf16[32,1536]{1,0:T(8,128)(2,1)S(1)} %slice.135), channel_id=1, source_target_pairs={{0,12},{4,0},{8,4},{12,8},{1,13},{5,1},{9,5},{13,9},{2,14},{6,2},{... | collective-permute-start | bytes 294920 | tf_op jit(solution)/shard_map/ppermute | solution.py:386
  15.6 1.7 %collective-permute-start.2 = (bf16[32,1536]{1,0:T(8,128)(2,1)S(1)}, bf16[32,1536]{1,0:T(8,128)(2,1)S(1)}, u32[]{:S(2)}, u32[]{:S(2)}) collective-permute-start(bf16[32,1536]{1,0:T(8,128)(2,1)S(1)} %slice.134), channel_id=1, source_target_pairs={{0,4},{4,8},{8,12},{12,0},{1,5},{5,9},{9,13},{13,1},{2,6},{6,10},{... | collective-permute-start | bytes 294920 | tf_op jit(solution)/shard_map/ppermute | solution.py:386
  17.4 0.9 copy-done
  18.3 2.7 %stage.1 = (bf16[64,1536]{1,0:T(8,128)(2,1)S(1)}, bf16[4,1536,256]{2,1,0:T(8,128)(2,1)S(1)}) custom-call(s32[2]{0:T(128)S(1)} %pad_add_fusion.info, bf16[64,1536]{1,0:T(8,128)(2,1)S(1)} %copy-done, bf16[8,1536,1024]{2,1,0:T(8,128)(2,1)} %refs_2_.7, bf16[8,1536,1024]{2,1,0:T(8,128)(2,1)} %refs_3_.7), custom_call_target="tpu_custom_call" | custom-call | flops 1 | bytes 1 | tf_op jit(solution)/shard_map/stage/pallas_call | solution.py:184
  21.1 0.8 route.1
  22.1 4.9 %send_shares.4 = (bf16[2,256,512]{2,1,0:T(8,128)(2,1)S(1)}, bf16[256,1536]{1,0:T(8,128)(2,1)S(1)}, bf16[4,1536,256]{2,1,0:T(8,128)(2,1)S(1)}) custom-call(s32[2]{0:T(128)S(1)} %pad_add_fusion.info, bf16[64,1536]{1,0:T(8,128)(2,1)S(1)} %get-tuple-element.34.refs_0_, bf16[64,1536]{1,0:T(8,128)(2,1)S(1)} %collective-permute-done.refs_1_, ...), custom_call_target="tpu_custom_call" | custom-call | flops 1 | bytes 1 | tf_op jit(solution)/shard_map/send_shares/pallas_call | solution.py:157
  27.1 4.2 %keep_shares.4 = (bf16[2,256,512]{2,1,0:T(8,128)(2,1)S(1)}, bf16[4,1536,256]{2,1,0:T(8,128)(2,1)S(1)}) custom-call(s32[2]{0:T(128)S(1)} %pad_add_fusion.info, bf16[256,1536]{1,0:T(8,128)(2,1)S(1)} %get-tuple-element.37.refs_0_, bf16[4,1536,256]{2,1,0:T(8,128)(2,1)S(1)} %get-tuple-element.38.refs_1_, bf16[8,1536,1024]{2,1,0:T(8,128)(2,1)} %refs_2_.7, ...), custom_call_target="tpu_custom_call" | custom-call | flops 1 | bytes 1 | tf_op jit(solution)/shard_map/keep_shares/pallas_call | solution.py:157
  31.5 1.7 %collective-permute-start.9 = (bf16[1,256,512]{2,1,0:T(8,128)(2,1)S(1)}, bf16[1,256,512]{2,1,0:T(8,128)(2,1)S(1)}, u32[]{:S(2)}, u32[]{:S(2)}) collective-permute-start(bf16[1,256,512]{2,1,0:T(8,128)(2,1)S(1)} %slice.191.refs_9_), channel_id=1, source_target_pairs={{0,2},{1,3},{2,0},{3,1},{4,6},{5,7},{6,4},{7,5},{8,10},{9,11},{10,... | collective-permute-start | bytes 786440 | tf_op jit(solution)/shard_map/ppermute | solution.py:23
  33.2 4.9 %send_shares.5 = (bf16[2,256,512]{2,1,0:T(8,128)(2,1)S(1)}, bf16[256,1536]{1,0:T(8,128)(2,1)S(1)}, bf16[4,1536,256]{2,1,0:T(8,128)(2,1)S(1)}) custom-call(s32[2]{0:T(128)S(1)} %pad_add_fusion.info, bf16[64,1536]{1,0:T(8,128)(2,1)S(1)} %get-tuple-element.34.refs_0_, bf16[64,1536]{1,0:T(8,128)(2,1)S(1)} %collective-permute-done.refs_1_, ...), custom_call_target="tpu_custom_call" | custom-call | flops 1 | bytes 1 | tf_op jit(solution)/shard_map/send_shares/pallas_call | solution.py:157
  38.3 4.2 %keep_shares.5 = (bf16[2,256,512]{2,1,0:T(8,128)(2,1)S(1)}, bf16[4,1536,256]{2,1,0:T(8,128)(2,1)S(1)}) custom-call(s32[2]{0:T(128)S(1)} %pad_add_fusion.info, bf16[256,1536]{1,0:T(8,128)(2,1)S(1)} %get-tuple-element.42.refs_0_, bf16[4,1536,256]{2,1,0:T(8,128)(2,1)S(1)} %get-tuple-element.43.refs_1_, bf16[8,1536,1024]{2,1,0:T(8,128)(2,1)} %refs_2_.7, ...), custom_call_target="tpu_custom_call" | custom-call | flops 1 | bytes 1 | tf_op jit(solution)/shard_map/keep_shares/pallas_call | solution.py:157
  43.5 4.9 %send_shares.6 = (bf16[2,256,512]{2,1,0:T(8,128)(2,1)S(1)}, bf16[256,1536]{1,0:T(8,128)(2,1)S(1)}, bf16[4,1536,256]{2,1,0:T(8,128)(2,1)S(1)}) custom-call(s32[2]{0:T(128)S(1)} %pad_add_fusion.info, bf16[64,1536]{1,0:T(8,128)(2,1)S(1)} %get-tuple-element.34.refs_0_, bf16[64,1536]{1,0:T(8,128)(2,1)S(1)} %collective-permute-done.refs_1_, ...), custom_call_target="tpu_custom_call" | custom-call | flops 1 | bytes 1 | tf_op jit(solution)/shard_map/send_shares/pallas_call | solution.py:157
  48.5 4.3 %keep_shares.6 = (bf16[2,256,512]{2,1,0:T(8,128)(2,1)S(1)}, bf16[4,1536,256]{2,1,0:T(8,128)(2,1)S(1)}) custom-call(s32[2]{0:T(128)S(1)} %pad_add_fusion.info, bf16[256,1536]{1,0:T(8,128)(2,1)S(1)} %get-tuple-element.47.refs_0_, bf16[4,1536,256]{2,1,0:T(8,128)(2,1)S(1)} %get-tuple-element.48.refs_1_, bf16[8,1536,1024]{2,1,0:T(8,128)(2,1)} %refs_2_.7, ...), custom_call_target="tpu_custom_call" | custom-call | flops 1 | bytes 1 | tf_op jit(solution)/shard_map/keep_shares/pallas_call | solution.py:157
  52.8 1.6 %collective-permute-done.11.refs_1_ = bf16[1,256,768]{2,1,0:T(8,128)(2,1)S(1)} collective-permute-done((bf16[1,256,768]{2,1,0:T(8,128)(2,1)S(1)}, bf16[1,256,768]{2,1,0:T(8,128)(2,1)S(1)}, u32[]{:S(2)}, u32[]{:S(2)}) %collective-permute-start.11) | collective-permute-done | bytes 393248 | tf_op jit(solution)/shard_map/ppermute | solution.py:23
  55.4 5.1 %send_shares.7 = (bf16[2,256,512]{2,1,0:T(8,128)(2,1)S(1)}, bf16[256,1536]{1,0:T(8,128)(2,1)S(1)}, bf16[4,1536,256]{2,1,0:T(8,128)(2,1)S(1)}) custom-call(s32[2]{0:T(128)S(1)} %pad_add_fusion.info, bf16[64,1536]{1,0:T(8,128)(2,1)S(1)} %get-tuple-element.34.refs_0_, bf16[64,1536]{1,0:T(8,128)(2,1)S(1)} %collective-permute-done.refs_1_, ...), custom_call_target="tpu_custom_call" | custom-call | flops 1 | bytes 1 | tf_op jit(solution)/shard_map/send_shares/pallas_call | solution.py:157
  61.1 3.5 %keep_shares.7 = bf16[2,256,512]{2,1,0:T(8,128)(2,1)S(1)} custom-call(s32[2]{0:T(128)S(1)} %pad_add_fusion.info, bf16[256,1536]{1,0:T(8,128)(2,1)S(1)} %get-tuple-element.52.refs_0_, bf16[4,1536,256]{2,1,0:T(8,128)(2,1)S(1)} %get-tuple-element.53.refs_1_, bf16[8,1536,1024]{2,1,0:T(8,128)(2,1)} %refs_2_.7, bf16[8,1536,1024]{2,1,0:T(8,128)(2,1)} %refs_3_.7), custom_call_target="tpu_custom_call" | custom-call | flops 1 | bytes 1 | tf_op jit(solution)/shard_map/keep_shares/pallas_call | solution.py:157
  64.6 0.9 collective-permute-done.13.refs_1_
  66.0 0.9 collective-permute-start.14
  66.9 4.3 %down.4.refs_6_ = f32[256,1536]{1,0:T(8,128)S(1)} custom-call(s32[2]{0:T(128)S(1)} %pad_add_fusion.info, bf16[1,256,256]{2,1,0:T(8,128)(2,1)S(1)} %fusion.3.refs_0_, bf16[1,256,768]{2,1,0:T(8,128)(2,1)S(1)} %collective-permute-done.11.refs_1_, bf16[2,256,256]{2,1,0:T(8,128)(2,1)S(1)} %collective-permute-done.16.refs_2_, ...), custom_call_target="tpu_custom_call" | custom-call | flops 4026531840 | bytes 9437184 | tf_op jit(solution)/shard_map/down/pallas_call | solution.py:252
  71.3 4.4 %down.5.refs_6_ = f32[256,1536]{1,0:T(8,128)S(1)} custom-call(s32[2]{0:T(128)S(1)} %pad_add_fusion.info, bf16[1,256,256]{2,1,0:T(8,128)(2,1)S(1)} %fusion.2.refs_0_, bf16[1,256,768]{2,1,0:T(8,128)(2,1)S(1)} %collective-permute-done.13.refs_1_, bf16[2,256,256]{2,1,0:T(8,128)(2,1)S(1)} %collective-permute-done.15.refs_2_, ...), custom_call_target="tpu_custom_call" | custom-call | flops 4026531840 | bytes 9437184 | tf_op jit(solution)/shard_map/down/pallas_call | solution.py:252
  75.6 1.9 %collective-permute-done.14.refs_1_ = bf16[1,256,768]{2,1,0:T(8,128)(2,1)S(1)} collective-permute-done((bf16[1,256,768]{2,1,0:T(8,128)(2,1)S(1)}, bf16[1,256,768]{2,1,0:T(8,128)(2,1)S(1)}, u32[]{:S(2)}, u32[]{:S(2)}) %collective-permute-start.14) | collective-permute-done | bytes 393248 | tf_op jit(solution)/shard_map/ppermute | solution.py:23
  77.9 0.9 collective-permute-start.17
  79.2 4.4 %down.6.refs_6_ = f32[256,1536]{1,0:T(8,128)S(1)} custom-call(s32[2]{0:T(128)S(1)} %pad_add_fusion.info, bf16[1,256,256]{2,1,0:T(8,128)(2,1)S(1)} %fusion.1.refs_0_, bf16[1,256,768]{2,1,0:T(8,128)(2,1)S(1)} %collective-permute-done.14.refs_1_, bf16[2,256,256]{2,1,0:T(8,128)(2,1)S(1)} %collective-permute-done.18.refs_2_, ...), custom_call_target="tpu_custom_call" | custom-call | flops 4026531840 | bytes 9437184 | tf_op jit(solution)/shard_map/down/pallas_call | solution.py:252
  83.9 1.5 %collective-permute-done.19.refs_2_ = bf16[2,256,256]{2,1,0:T(8,128)(2,1)S(1)} collective-permute-done((bf16[2,256,256]{2,1,0:T(8,128)(2,1)S(1)}, bf16[2,256,256]{2,1,0:T(8,128)(2,1)S(1)}, u32[]{:S(2)}, u32[]{:S(2)}) %collective-permute-start.19) | collective-permute-done | bytes 262176 | tf_op jit(solution)/shard_map/ppermute | solution.py:23
  85.5 4.4 %down.7 = (bf16[64,1536]{1,0:T(8,128)(2,1)S(1)}, bf16[64,1536]{1,0:T(8,128)(2,1)S(1)}, bf16[64,1536]{1,0:T(8,128)(2,1)S(1)}, bf16[32,1536]{1,0:T(8,128)(2,1)S(1)}, bf16[32,1536]{1,0:T(8,128)(2,1)S(1)}) custom-call(s32[2]{0:T(128)S(1)} %pad_add_fusion.info, bf16[1,256,256]{2,1,0:T(8,128)(2,1)S(1)} %fusion.refs_7_.refs_0_, ...), custom_call_target="tpu_custom_call" | custom-call | flops 4026531840 | bytes 9437184 | tf_op jit(solution)/shard_map/down/pallas_call | solution.py:252
  89.9 3.9 %collective-permute-start.20 = (bf16[32,1536]{1,0:T(8,128)(2,1)S(1)}, bf16[32,1536]{1,0:T(8,128)(2,1)S(1)}, u32[]{:S(2)}, u32[]{:S(2)}) collective-permute-start(bf16[32,1536]{1,0:T(8,128)(2,1)S(1)} %get-tuple-element.60), channel_id=1, source_target_pairs={{0,12},{4,0},{8,4},{12,8},{1,13},{5,1},{9,5},{13,9},{2,14},{6,2},{... | collective-permute-start | bytes 294920 | tf_op jit(solution)/shard_map/ppermute | solution.py:398
  93.8 3.6 %collective-permute-done.22 = bf16[32,1536]{1,0:T(8,128)(2,1)S(1)} collective-permute-done((bf16[32,1536]{1,0:T(8,128)(2,1)S(1)}, bf16[32,1536]{1,0:T(8,128)(2,1)S(1)}, u32[]{:S(2)}, u32[]{:S(2)}) %collective-permute-start.22) | collective-permute-done | bytes 98336 | tf_op jit(solution)/shard_map/ppermute | solution.py:398
  97.6 3.9 %collective-permute-start.21 = (bf16[64,1536]{1,0:T(8,128)(2,1)S(1)}, bf16[64,1536]{1,0:T(8,128)(2,1)S(1)}, u32[]{:S(2)}, u32[]{:S(2)}) collective-permute-start(bf16[64,1536]{1,0:T(8,128)(2,1)S(1)} %pad_maximum_fusion.7), channel_id=1, source_target_pairs={{0,12},{4,0},{8,4},{12,8},{1,13},{5,1},{9,5},{13,9},{2,14},{6,2},{... | collective-permute-start | bytes 589832 | tf_op jit(solution)/shard_map/ppermute | solution.py:407
  101.4 5.3 %collective-permute-done.23 = bf16[64,1536]{1,0:T(8,128)(2,1)S(1)} collective-permute-done((bf16[64,1536]{1,0:T(8,128)(2,1)S(1)}, bf16[64,1536]{1,0:T(8,128)(2,1)S(1)}, u32[]{:S(2)}, u32[]{:S(2)}) %collective-permute-start.23) | collective-permute-done | bytes 196640 | tf_op jit(solution)/shard_map/ppermute | solution.py:408
  107.1 0.8 add_convert_fusion
  (71 shorter events, 8.1 us)
Async XLA Ops:
  0.0 10.8 %collective-permute-start.1 = (bf16[64,1536]{1,0:T(8,128)(2,1)}, bf16[64,1536]{1,0:T(8,128)(2,1)S(1)}, u32[]{:S(2)}, u32[]{:S(2)}) collective-permute-start(bf16[64,1536]{1,0:T(8,128)(2,1)} %tokens.1), channel_id=1, source_target_pairs={{0,12},{4,0},{8,4},{12,8},{1,13},{5,1},{9,5},{13,9},{2,14},{6,2},{... | collective-permute-start | bytes 589832 | tf_op jit(solution)/shard_map/ppermute | solution.py:382
  5.0 10.6 %collective-permute-start = (bf16[64,1536]{1,0:T(8,128)(2,1)}, bf16[64,1536]{1,0:T(8,128)(2,1)S(1)}, u32[]{:S(2)}, u32[]{:S(2)}) collective-permute-start(bf16[64,1536]{1,0:T(8,128)(2,1)} %tokens.1), channel_id=1, source_target_pairs={{0,4},{4,8},{8,12},{12,0},{1,5},{5,9},{9,13},{13,1},{2,6},{6,10},{... | collective-permute-start | bytes 589832 | tf_op jit(solution)/shard_map/ppermute | solution.py:382
  6.4 14.6 %collective-permute-start.6 = (f32[16,64]{1,0:T(8,128)S(1)}, f32[16,64]{1,0:T(8,128)S(1)}, u32[]{:S(2)}, u32[]{:S(2)}) collective-permute-start(f32[16,64]{1,0:T(8,128)S(1)} %pad_maximum_fusion.9.refs_0_), channel_id=1, source_target_pairs={{0,8},{4,12},{8,0},{12,4},{1,9},{5,13},{9,1},{13,5},{2,10},{6,14},... | collective-permute-start | bytes 12296 | tf_op jit(solution)/shard_map/ppermute | solution.py:319
  7.4 13.6 %collective-permute-start.5 = (f32[16,64]{1,0:T(8,128)S(1)}, f32[16,64]{1,0:T(8,128)S(1)}, u32[]{:S(2)}, u32[]{:S(2)}) collective-permute-start(f32[16,64]{1,0:T(8,128)S(1)} %pad_maximum_fusion.9.refs_0_), channel_id=1, source_target_pairs={{0,12},{4,0},{8,4},{12,8},{1,13},{5,1},{9,5},{13,9},{2,14},{6,2},{... | collective-permute-start | bytes 12296 | tf_op jit(solution)/shard_map/ppermute | solution.py:319
  10.3 10.8 %collective-permute-start.4 = (f32[16,64]{1,0:T(8,128)S(1)}, f32[16,64]{1,0:T(8,128)S(1)}, u32[]{:S(2)}, u32[]{:S(2)}) collective-permute-start(f32[16,64]{1,0:T(8,128)S(1)} %pad_maximum_fusion.9.refs_0_), channel_id=1, source_target_pairs={{0,4},{4,8},{8,12},{12,0},{1,5},{5,9},{9,13},{13,1},{2,6},{6,10},{... | collective-permute-start | bytes 12296 | tf_op jit(solution)/shard_map/ppermute | solution.py:319
  10.8 11.0 %collective-permute-start.3 = (bf16[32,1536]{1,0:T(8,128)(2,1)S(1)}, bf16[32,1536]{1,0:T(8,128)(2,1)S(1)}, u32[]{:S(2)}, u32[]{:S(2)}) collective-permute-start(bf16[32,1536]{1,0:T(8,128)(2,1)S(1)} %slice.135), channel_id=1, source_target_pairs={{0,12},{4,0},{8,4},{12,8},{1,13},{5,1},{9,5},{13,9},{2,14},{6,2},{... | collective-permute-start | bytes 294920 | tf_op jit(solution)/shard_map/ppermute | solution.py:386
  15.6 6.5 %collective-permute-start.2 = (bf16[32,1536]{1,0:T(8,128)(2,1)S(1)}, bf16[32,1536]{1,0:T(8,128)(2,1)S(1)}, u32[]{:S(2)}, u32[]{:S(2)}) collective-permute-start(bf16[32,1536]{1,0:T(8,128)(2,1)S(1)} %slice.134), channel_id=1, source_target_pairs={{0,4},{4,8},{8,12},{12,0},{1,5},{5,9},{9,13},{13,1},{2,6},{6,10},{... | collective-permute-start | bytes 294920 | tf_op jit(solution)/shard_map/ppermute | solution.py:386
  17.4 0.9 copy-start
  27.0 4.3 %collective-permute-start.7 = (bf16[2,256,512]{2,1,0:T(8,128)(2,1)S(1)}, bf16[2,256,512]{2,1,0:T(8,128)(2,1)S(1)}, u32[]{:S(2)}, u32[]{:S(2)}) collective-permute-start(bf16[2,256,512]{2,1,0:T(8,128)(2,1)S(1)} %get-tuple-element.41), channel_id=1, source_target_pairs={{0,1},{1,0},{2,3},{3,2},{4,5},{5,4},{6,7},{7,6},{8,9},{9,8},{10,11... | collective-permute-start | bytes 1572872 | tf_op jit(solution)/shard_map/ppermute | solution.py:23
  31.5 11.0 %collective-permute-start.9 = (bf16[1,256,512]{2,1,0:T(8,128)(2,1)S(1)}, bf16[1,256,512]{2,1,0:T(8,128)(2,1)S(1)}, u32[]{:S(2)}, u32[]{:S(2)}) collective-permute-start(bf16[1,256,512]{2,1,0:T(8,128)(2,1)S(1)} %slice.191.refs_9_), channel_id=1, source_target_pairs={{0,2},{1,3},{2,0},{3,1},{4,6},{5,7},{6,4},{7,5},{8,10},{9,11},{10,... | collective-permute-start | bytes 786440 | tf_op jit(solution)/shard_map/ppermute | solution.py:23
  38.1 4.7 %collective-permute-start.8 = (bf16[2,256,512]{2,1,0:T(8,128)(2,1)S(1)}, bf16[2,256,512]{2,1,0:T(8,128)(2,1)S(1)}, u32[]{:S(2)}, u32[]{:S(2)}) collective-permute-start(bf16[2,256,512]{2,1,0:T(8,128)(2,1)S(1)} %get-tuple-element.46), channel_id=1, source_target_pairs={{0,1},{1,0},{2,3},{3,2},{4,5},{5,4},{6,7},{7,6},{8,9},{9,8},{10,11... | collective-permute-start | bytes 1572872 | tf_op jit(solution)/shard_map/ppermute | solution.py:23
  43.0 11.4 %collective-permute-start.11 = (bf16[1,256,768]{2,1,0:T(8,128)(2,1)S(1)}, bf16[1,256,768]{2,1,0:T(8,128)(2,1)S(1)}, u32[]{:S(2)}, u32[]{:S(2)}) collective-permute-start(bf16[1,256,768]{2,1,0:T(8,128)(2,1)S(1)} %pad_maximum_fusion.refs_9_), channel_id=1, source_target_pairs={{0,2},{1,3},{2,0},{3,1},{4,6},{5,7},{6,4},{7,5},{8,10},{9,11},{10,... | collective-permute-start | bytes 1179656 | tf_op jit(solution)/shard_map/ppermute | solution.py:23
  48.4 6.1 %collective-permute-start.10 = (bf16[2,256,512]{2,1,0:T(8,128)(2,1)S(1)}, bf16[2,256,512]{2,1,0:T(8,128)(2,1)S(1)}, u32[]{:S(2)}, u32[]{:S(2)}) collective-permute-start(bf16[2,256,512]{2,1,0:T(8,128)(2,1)S(1)} %get-tuple-element.51), channel_id=1, source_target_pairs={{0,1},{1,0},{2,3},{3,2},{4,5},{5,4},{6,7},{7,6},{8,9},{9,8},{10,11... | collective-permute-start | bytes 1572872 | tf_op jit(solution)/shard_map/ppermute | solution.py:23
  54.8 10.6 %collective-permute-start.13 = (bf16[1,256,768]{2,1,0:T(8,128)(2,1)S(1)}, bf16[1,256,768]{2,1,0:T(8,128)(2,1)S(1)}, u32[]{:S(2)}, u32[]{:S(2)}) collective-permute-start(bf16[1,256,768]{2,1,0:T(8,128)(2,1)S(1)} %pad_maximum_fusion.1.refs_9_), channel_id=1, source_target_pairs={{0,2},{1,3},{2,0},{3,1},{4,6},{5,7},{6,4},{7,5},{8,10},{9,11},{10,... | collective-permute-start | bytes 1179656 | tf_op jit(solution)/shard_map/ppermute | solution.py:23
  55.4 11.5 %collective-permute-start.16 = (bf16[2,256,256]{2,1,0:T(8,128)(2,1)S(1)}, bf16[2,256,256]{2,1,0:T(8,128)(2,1)S(1)}, u32[]{:S(2)}, u32[]{:S(2)}) collective-permute-start(bf16[2,256,256]{2,1,0:T(8,128)(2,1)S(1)} %pad_maximum_fusion.4), channel_id=1, source_target_pairs={{0,1},{1,0},{2,3},{3,2},{4,5},{5,4},{6,7},{7,6},{8,9},{9,8},{10,11... | collective-permute-start | bytes 786440 | tf_op jit(solution)/shard_map/ppermute | solution.py:23
  60.5 5.2 %collective-permute-start.12 = (bf16[2,256,512]{2,1,0:T(8,128)(2,1)S(1)}, bf16[2,256,512]{2,1,0:T(8,128)(2,1)S(1)}, u32[]{:S(2)}, u32[]{:S(2)}) collective-permute-start(bf16[2,256,512]{2,1,0:T(8,128)(2,1)S(1)} %get-tuple-element.54), channel_id=1, source_target_pairs={{0,1},{1,0},{2,3},{3,2},{4,5},{5,4},{6,7},{7,6},{8,9},{9,8},{10,11... | collective-permute-start | bytes 1572872 | tf_op jit(solution)/shard_map/ppermute | solution.py:23
  65.5 5.8 %collective-permute-start.15 = (bf16[2,256,256]{2,1,0:T(8,128)(2,1)S(1)}, bf16[2,256,256]{2,1,0:T(8,128)(2,1)S(1)}, u32[]{:S(2)}, u32[]{:S(2)}) collective-permute-start(bf16[2,256,256]{2,1,0:T(8,128)(2,1)S(1)} %pad_maximum_fusion.3), channel_id=1, source_target_pairs={{0,1},{1,0},{2,3},{3,2},{4,5},{5,4},{6,7},{7,6},{8,9},{9,8},{10,11... | collective-permute-start | bytes 786440 | tf_op jit(solution)/shard_map/ppermute | solution.py:23
  66.0 11.6 %collective-permute-start.14 = (bf16[1,256,768]{2,1,0:T(8,128)(2,1)S(1)}, bf16[1,256,768]{2,1,0:T(8,128)(2,1)S(1)}, u32[]{:S(2)}, u32[]{:S(2)}) collective-permute-start(bf16[1,256,768]{2,1,0:T(8,128)(2,1)S(1)} %pad_maximum_fusion.2.refs_6_), channel_id=1, source_target_pairs={{0,2},{1,3},{2,0},{3,1},{4,6},{5,7},{6,4},{7,5},{8,10},{9,11},{10,... | collective-permute-start | bytes 1179656 | tf_op jit(solution)/shard_map/ppermute | solution.py:23
  77.6 1.6 %collective-permute-start.18 = (bf16[2,256,256]{2,1,0:T(8,128)(2,1)S(1)}, bf16[2,256,256]{2,1,0:T(8,128)(2,1)S(1)}, u32[]{:S(2)}, u32[]{:S(2)}) collective-permute-start(bf16[2,256,256]{2,1,0:T(8,128)(2,1)S(1)} %pad_maximum_fusion.5), channel_id=1, source_target_pairs={{0,1},{1,0},{2,3},{3,2},{4,5},{5,4},{6,7},{7,6},{8,9},{9,8},{10,11... | collective-permute-start | bytes 786440 | tf_op jit(solution)/shard_map/ppermute | solution.py:23
  77.9 6.0 %collective-permute-start.17 = (bf16[1,256,256]{2,1,0:T(8,128)(2,1)S(1)}, bf16[1,256,256]{2,1,0:T(8,128)(2,1)S(1)}, u32[]{:S(2)}, u32[]{:S(2)}) collective-permute-start(bf16[1,256,256]{2,1,0:T(8,128)(2,1)S(1)} %fusion.refs_7_.refs_0_), channel_id=1, source_target_pairs={{0,2},{1,3},{2,0},{3,1},{4,6},{5,7},{6,4},{7,5},{8,10},{9,11},{10,... | collective-permute-start | bytes 393224 | tf_op jit(solution)/shard_map/ppermute | solution.py:23
  83.9 1.6 %collective-permute-start.19 = (bf16[2,256,256]{2,1,0:T(8,128)(2,1)S(1)}, bf16[2,256,256]{2,1,0:T(8,128)(2,1)S(1)}, u32[]{:S(2)}, u32[]{:S(2)}) collective-permute-start(bf16[2,256,256]{2,1,0:T(8,128)(2,1)S(1)} %pad_maximum_fusion.6), channel_id=1, source_target_pairs={{0,1},{1,0},{2,3},{3,2},{4,5},{5,4},{6,7},{7,6},{8,9},{9,8},{10,11... | collective-permute-start | bytes 786440 | tf_op jit(solution)/shard_map/ppermute | solution.py:23
  89.8 7.5 %collective-permute-start.22 = (bf16[32,1536]{1,0:T(8,128)(2,1)S(1)}, bf16[32,1536]{1,0:T(8,128)(2,1)S(1)}, u32[]{:S(2)}, u32[]{:S(2)}) collective-permute-start(bf16[32,1536]{1,0:T(8,128)(2,1)S(1)} %get-tuple-element.62), channel_id=1, source_target_pairs={{0,4},{4,8},{8,12},{12,0},{1,5},{5,9},{9,13},{13,1},{2,6},{6,10},{... | collective-permute-start | bytes 294920 | tf_op jit(solution)/shard_map/ppermute | solution.py:398
  89.9 7.6 %collective-permute-start.20 = (bf16[32,1536]{1,0:T(8,128)(2,1)S(1)}, bf16[32,1536]{1,0:T(8,128)(2,1)S(1)}, u32[]{:S(2)}, u32[]{:S(2)}) collective-permute-start(bf16[32,1536]{1,0:T(8,128)(2,1)S(1)} %get-tuple-element.60), channel_id=1, source_target_pairs={{0,12},{4,0},{8,4},{12,8},{1,13},{5,1},{9,5},{13,9},{2,14},{6,2},{... | collective-permute-start | bytes 294920 | tf_op jit(solution)/shard_map/ppermute | solution.py:398
  97.4 9.3 %collective-permute-start.23 = (bf16[64,1536]{1,0:T(8,128)(2,1)S(1)}, bf16[64,1536]{1,0:T(8,128)(2,1)S(1)}, u32[]{:S(2)}, u32[]{:S(2)}) collective-permute-start(bf16[64,1536]{1,0:T(8,128)(2,1)S(1)} %pad_maximum_fusion.8), channel_id=1, source_target_pairs={{0,4},{4,8},{8,12},{12,0},{1,5},{5,9},{9,13},{13,1},{2,6},{6,10},{... | collective-permute-start | bytes 589832 | tf_op jit(solution)/shard_map/ppermute | solution.py:408
  97.6 9.5 %collective-permute-start.21 = (bf16[64,1536]{1,0:T(8,128)(2,1)S(1)}, bf16[64,1536]{1,0:T(8,128)(2,1)S(1)}, u32[]{:S(2)}, u32[]{:S(2)}) collective-permute-start(bf16[64,1536]{1,0:T(8,128)(2,1)S(1)} %pad_maximum_fusion.7), channel_id=1, source_target_pairs={{0,12},{4,0},{8,4},{12,8},{1,13},{5,1},{9,5},{13,9},{2,14},{6,2},{... | collective-permute-start | bytes 589832 | tf_op jit(solution)/shard_map/ppermute | solution.py:407

commit v6 on v5

--- a/solution.py
+++ b/solution.py
@@ -63,46 +63,42 @@
     )(info, *meta)
 
 
-def fetches(w_gate, w_up, experts, units, to, sem):
-    return [
-        pltpu.make_async_copy(w.at[e, :, units], to.at[i], sem.at[i])
-        for i, (w, e) in enumerate((w, e) for w in (w_gate, w_up) for e in experts)
-    ]
-
-
-def units_of(l, info, width):
-    return pl.ds(pl.multiple_of((l ^ info[1]) * width, width), width)
-
-
-def products(rows, weights, to, j):
-    most = rows.shape[0] * 2 // weights.shape[0]
-    width = weights.shape[2]
-    for i in range(weights.shape[0]):
-        m, x = divmod(i, weights.shape[0] // 2)
+def backwards(l, n):
+    bits = bits_of(n)
+    return sum((((l >> b) & 1) << (len(bits) - 1 - b) for b in bits), 0 * l)
+
+
+def units_of(l, info, n, width):
+    return pl.ds(pl.multiple_of((backwards(l, n) ^ info[2]) * width, width), width)
+
+
+def fetches(w, experts, side, info, to, sem):
+    half = to.shape[2]
+    units = pl.ds(pl.multiple_of(((info[1] & 1) ^ side) * half, half), half)
+    return [pltpu.make_async_copy(w.at[e, :, units], to.at[x], sem.at[x]) for x, e in enumerate(experts)]
+
+
+def products(rows, weights, to, m, info):
+    most = rows.shape[0] // weights.shape[0]
+    shares, width = to.shape[0], to.shape[2] // 2
+    for x in range(weights.shape[0]):
         mine = slice(x * most, (x + 1) * most)
-        to[j, mine, m * width : (m + 1) * width] = jnp.dot(
-            rows[mine], weights[i], preferred_element_type=jnp.float32
-        ).astype(jnp.bfloat16)
-
-
-def shares_body(n, experts, shares, ahead, after, info, *refs):
-    sources, refs = refs[: n + 1] if n else refs[:1], refs[n + 1 if n else 1 :]
+        part = jnp.dot(rows[mine], weights[x], preferred_element_type=jnp.float32).astype(jnp.bfloat16)
+        for q in range(shares):
+            j = backwards(q, shares) ^ (info[1] >> 1)
+            to[j, mine, m * width : (m + 1) * width] = part[:, q * width : (q + 1) * width]
+
+
+def half_body(n, experts, side, ahead, after, info, *refs):
+    sources, refs = refs[: max(n + 1, 1)], refs[max(n + 1, 1) :]
     (given, w_gate, w_up), refs = refs[:3], refs[3 + after :]
     to, refs = refs[0], refs[1:]
-    width = given.shape[2]
     rows = sources[0]
     if n:
         rows, refs = refs[0], refs[1:]
     if ahead is not None:
         handed, refs = refs[0], refs[1:]
-    held, held_sem, handed_sem, refs = refs[0], refs[1], refs[2], refs[3:]
-    rest = [
-        fetches(w_gate, w_up, experts, units_of(l, info, width), held.at[j], held_sem.at[j])
-        for j, l in enumerate(shares[1:])
-    ]
-    on = []
-    if ahead is not None:
-        on = fetches(w_gate, w_up, ahead[0], units_of(ahead[1], info, width), handed, handed_sem)
+    (held, held_sem, handed_sem), refs = refs[:3], refs[3:]
     if n:
         feed, feed_sem = refs
         at, feeds = 0, []
@@ -112,9 +108,12 @@
             at += tok
         for copy in feeds:
             copy.start()
-    for copies in rest + [on]:
-        for copy in copies:
-            copy.start()
+    rest = fetches(w_up, experts, side, info, held, held_sem)
+    on = []
+    if ahead is not None:
+        on = fetches(w_gate, ahead[0], ahead[1], info, handed, handed_sem)
+    for copy in rest + on:
+        copy.start()
     if n:
         rank = sources[n]
         most = rows.shape[0] // len(experts)
@@ -125,29 +124,27 @@
         for copy in feeds:
             copy.wait()
         rows[...] = jnp.dot(pick, feed[...], preferred_element_type=jnp.float32).astype(jnp.bfloat16)
-    products(rows, given, to, 0)
-    for j, copies in enumerate(rest):
-        for copy in copies:
-            copy.wait()
-        products(rows, held.at[j], to, j + 1)
+    products(rows, given, to, 0, info)
+    for copy in rest:
+        copy.wait()
+    products(rows, held, to, 1, info)
     for copy in on:
         copy.wait()
 
 
-def some_shares(sources, info, given, w_gate, w_up, experts, most, shares, ahead, after):
+def half_units(sources, info, given, w_gate, w_up, experts, most, n_dp, side, ahead, after):
     n = len(sources) - 1
-    mats, local, width = given.shape
+    _, local, half = given.shape
     rows = most * len(experts)
-    pieces = max(len(shares) - 1, 1)
-    out = [jax.ShapeDtypeStruct((len(shares), rows, 2 * width), jnp.bfloat16)]
+    out = [jax.ShapeDtypeStruct((n_dp // 2, rows, 4 * half // n_dp), jnp.bfloat16)]
     if n:
         out.append(jax.ShapeDtypeStruct((rows, local), jnp.bfloat16))
     if ahead is not None:
         out.append(jax.ShapeDtypeStruct(given.shape, jnp.bfloat16))
     scratch = [
-        pltpu.VMEM((pieces, mats, local, width), jnp.bfloat16),
-        pltpu.SemaphoreType.DMA((pieces, mats)),
-        pltpu.SemaphoreType.DMA((mats,)),
+        pltpu.VMEM(given.shape, jnp.bfloat16),
+        pltpu.SemaphoreType.DMA((len(experts),)),
+        pltpu.SemaphoreType.DMA((len(experts),)),
     ]
     if n:
         scratch += [
@@ -155,45 +152,41 @@
             pltpu.SemaphoreType.DMA((n,)),
         ]
     return pl.pallas_call(
-        functools.partial(shares_body, n, experts, shares, ahead, len(after)),
+        functools.partial(half_body, n, experts, side, ahead, len(after)),
         out_shape=tuple(out),
         in_specs=[SMEM] + [HERE] * n + [VMEM] * 2 + [HERE] * (2 + len(after)),
         out_specs=(VMEM,) * len(out),
         scratch_shapes=scratch,
         compiler_params=pltpu.CompilerParams(vmem_limit_bytes=40 << 20),
         cost_estimate=pl.CostEstimate(flops=1, bytes_accessed=1, transcendentals=0),
-        name="send_shares" if n else "keep_shares",
+        name="send_half" if n else "keep_half",
     )(info, *sources, given, w_gate, w_up, *after)
 
 
-def stage_body(experts, share, info, tokens, w_gate, w_up, copied, handed, sem, handed_sem):
-    width = handed.shape[2]
-    own = pltpu.make_async_copy(tokens, copied, sem.at[0])
-    own.start()
-    copies = fetches(w_gate, w_up, experts, units_of(share, info, width), handed, handed_sem)
+def stage_body(experts, side, info, w_gate, handed, sem):
+    copies = fetches(w_gate, experts, side, info, handed, sem)
     for copy in copies:
         copy.start()
-    own.wait()
     for copy in copies:
         copy.wait()
 
 
-def stage(tokens, info, w_gate, w_up, experts, share, n_dp):
+def stage(info, w_gate, experts, side):
     _, local, hidden = w_gate.shape
-    mats = 2 * len(experts)
     return pl.pallas_call(
-        functools.partial(stage_body, experts, share),
-        out_shape=(
-            jax.ShapeDtypeStruct(tokens.shape, tokens.dtype),
-            jax.ShapeDtypeStruct((mats, local, hidden // n_dp), jnp.bfloat16),
-        ),
-        in_specs=[SMEM] + [HERE] * 3,
-        out_specs=(VMEM, VMEM),
-        scratch_shapes=[pltpu.SemaphoreType.DMA((1,)), pltpu.SemaphoreType.DMA((mats,))],
+        functools.partial(stage_body, experts, side),
+        out_shape=jax.ShapeDtypeStruct((len(experts), local, hidden // 2), jnp.bfloat16),
+        in_specs=[SMEM, HERE],
+        out_specs=VMEM,
+        scratch_shapes=[pltpu.SemaphoreType.DMA((len(experts),))],
         compiler_params=pltpu.CompilerParams(vmem_limit_bytes=40 << 20),
         cost_estimate=pl.CostEstimate(flops=1, bytes_accessed=1, transcendentals=0),
         name="stage",
-    )(info, tokens, w_gate, w_up)
+    )(info, w_gate)
+
+
+def block_of(local):
+    return 512 if local % 512 == 0 else 256 if local % 256 == 0 else local
 
 
 def down_body(lanes, cuts, experts, first, after, info, *refs):
@@ -204,8 +197,9 @@
     outs, (hidden, mix, out, held, held_sem) = refs[: len(cuts)], refs[len(cuts) :]
     most = hidden.shape[0] // len(experts)
     width = parts[0].shape[-1]
+    n_dp = hidden.shape[1] // width
     local = out.shape[1]
-    block = 512 if local % 512 == 0 else 256 if local % 256 == 0 else local
+    block = block_of(local)
     copies = {}
     for i in range(local // block):
         for x, e in enumerate(experts):
@@ -216,7 +210,7 @@
             copies[i, x].start()
     for part, (at, shares) in zip(parts, lanes):
         for j, l in enumerate(shares):
-            hidden[:, units_of(l, info, width)] = part[j, :, at : at + width]
+            hidden[:, units_of(l, info, n_dp, width)] = part[j, :, at : at + width]
     r = lax.broadcasted_iota(jnp.int32, (most, mix.shape[1]), 0).astype(jnp.float32)
     for x, e in enumerate(experts):
         mix[x * most : (x + 1) * most, :] = jnp.where(
@@ -235,10 +229,13 @@
         )
         if not first:
             total = total + before[:, cols]
-        at = 0
-        for to, cut in zip(outs, cuts):
-            to[:, cols] = total[at : at + cut].astype(to.dtype)
+        at, left = 0, i * block
+        for k, (cut, wide) in enumerate(cuts):
+            if 0 <= left < wide:
+                outs[k][:, left : left + block] = total[at : at + cut].astype(outs[k].dtype)
             at += cut
+            if at == total.shape[0]:
+                at, left = 0, left - wide
 
 
 def down(parts, rank, wt, info, w_down, total, experts, cuts, after):
@@ -251,7 +248,7 @@
     mats = len(experts)
     outs = pl.pallas_call(
         functools.partial(down_body, lanes, cuts, experts, first, len(after)),
-        out_shape=tuple(jax.ShapeDtypeStruct((cut, local), kind) for cut in cuts),
+        out_shape=tuple(jax.ShapeDtypeStruct(cut, kind) for cut in cuts),
         in_specs=[SMEM]
         + [VMEM] * (len(parts) + 2)
         + [HERE]
@@ -314,34 +311,38 @@
     chunks = experts // per_chunk
 
     meta = jnp.concatenate([expert_ids.T.astype(jnp.float32), scores.T], axis=0)
-    feeds = gathered(tokens, "expert")
     metas = [meta] + [
         lax.ppermute(meta, "expert", [(i, (i - k) % n_owner) for i in range(n_owner)])
         for k in gathered_order(n_owner)[1:]
     ]
-    info = jnp.stack([lax.axis_index("expert") * experts, lax.axis_index("dp")]).astype(jnp.int32)
+    me = lax.axis_index("dp").astype(jnp.int32)
+    first = lax.axis_index("expert").astype(jnp.int32) * experts
+    info = jnp.stack([first, me, backwards(me, n_dp)])
+    of = lambda c: list(range(c * per_chunk, (c + 1) * per_chunk))
+    given = stage(info, w_gate, of(0), 1)
+    feeds = gathered(tokens, "expert", (given, *metas[1:]))
     rank, wt = route(metas, info, experts)
 
-    cuts = [feed.shape[0] for feed in feeds]
-    of = lambda c: list(range(c * per_chunk, (c + 1) * per_chunk))
+    tall, wide = [feed.shape[0] for feed in feeds], tokens.shape[1]
+    narrow = wide // block_of(wide) // 2 * block_of(wide)
+    final = [(cut, wide - narrow) for cut in tall] + ([(cut, narrow) for cut in tall] if narrow else [])
     bits = bits_of(n_dp)
     cross = 1 << bits[-1]
-    odd, even = list(range(1, n_dp, 2)), list(range(0, n_dp, 2))
-    feeds[0], given = stage(tokens, info, w_gate, w_up, of(0), odd[0], n_dp)
     sent, parts, total = [], [], None
     share = kept = late = None
 
     def add(c, after):
-        outs = cuts if c == chunks - 1 else [sum(cuts)]
+        outs = final if c == chunks - 1 else [(sum(tall), wide)]
         return down(parts[c], rank, wt, info, w_down, total, of(c), outs, after)
 
     for c in range(chunks):
         last = c == chunks - 1
-        send, rows, given = some_shares(
-            [*feeds, rank], info, given, w_gate, w_up, of(c), most, odd, (of(c), 0), sent[-1:]
+        send, rows, given = half_units(
+            [*feeds, rank], info, given, w_gate, w_up, of(c), most, n_dp, 1, (of(c), 0), sent[-1:]
         )
-        keep, *given = some_shares(
-            [rows], info, given, w_gate, w_up, of(c), most, even, None if last else (of(c + 1), odd[0]), []
+        ahead = None if last else (of(c + 1), 1)
+        keep, *given = half_units(
+            [rows], info, given, w_gate, w_up, of(c), most, n_dp, 0, ahead, []
         )
         given = given[0] if given else None
         before, behind = kept, late
@@ -365,7 +366,8 @@
         other = lax.optimization_barrier((other, total))[0]
     parts.append(everyone_s(share, other, 0, bits))
     total = add(chunks - 1, [])
-    return returned(total, "expert") if n_owner > 1 else total[0].astype(jnp.bfloat16)
+    mixed = [returned(total[k : k + len(tall)], "expert") for k in range(0, len(total), len(tall))]
+    return jnp.concatenate(mixed, axis=1).astype(jnp.bfloat16)
 
 
 def gathered_order(n):
@@ -373,7 +375,7 @@
     return [0] + near + ([n // 2] if n > 1 else [])
 
 
-def gathered(x, axis):
+def gathered(x, axis, beside):
     n = lax.axis_size(axis)
     up, down_ = [(i, (i + 1) % n) for i in range(n)], [(i, (i - 1) % n) for i in range(n)]
     below = above = x
@@ -383,6 +385,7 @@
         found += [below, above]
     if n > 1:
         half = x.shape[0] // 2
+        below, above, *_ = lax.optimization_barrier((below, above, *beside))
         found += [lax.ppermute(below[:half], axis, up), lax.ppermute(above[half:], axis, down_)]
     return found
 
@@ -392,6 +395,8 @@
     up, down_ = [(i, (i + 1) % n) for i in range(n)], [(i, (i - 1) % n) for i in range(n)]
     wide = lambda x: x.astype(jnp.float32)
     near = {0: partials[0]}
+    if n == 1:
+        return wide(near[0])
     for k, partial in zip(gathered_order(n)[1:-1], partials[1:-2]):
         near[k] = partial
     half = partials[-1].shape[0]
@@ -411,7 +416,7 @@
         back = jnp.concatenate([wide(low), wide(high)], axis=0)
     else:
         back = wide(low) + wide(high)
-    return (wide(near[0]) + back).astype(jnp.bfloat16)
+    return wide(near[0]) + back
 
 
 def solution(mesh):

time: 108 us -> 111 us (1.028)
  waiting for transfers between devices: 16.9 us -> 20.3 us
  starting transfers between devices: 28.8 us -> 31.1 us
  Pallas kernels: 56.9 us -> 54.7 us
    ppermute x1, waiting for transfers between devices: 0.25 us -> 4.2 us  [gathered(): lax.ppermute(below[:half], axis, up)]
    ppermute x1 -> x2, starting transfers between devices: 3.85 us -> 7.7 us  [returned(): low = lax.ppermute(a.astype(jnp.bfloat16), axis, down_)]
    ppermute x1 -> x2, waiting for transfers between devices: 3.59 us -> 0.84 us  [returned(): lax.ppermute(partials[-1], axis, up)]
    ppermute x1 -> x2, waiting for transfers between devices: 5.34 us -> 2.96 us  [returned(): high = lax.ppermute(b.astype(jnp.bfloat16), axis, up)]
    ppermute x3, waiting for transfers between devices: 0.01 us -> 2.35 us  [on_device(): lax.ppermute(meta, 'expert', [(i, (i - k) % n_owner) for i in range(n_own...]
    pallas_call x9, Pallas kernels: 38.7 us -> 36.6 us  [the longest x8 34.1 us: half_units(): pl.pallas_call(functools.partial(half_body, n, experts, side, ahead, len(...]
    ppermute x1 -> x2, starting transfers between devices: 0.06 us -> 2.06 us  [returned(): lax.ppermute(partials[-1], axis, up)]
    ppermute x1, starting transfers between devices: 1.7 us -> 0.01 us  [gathered(): lax.ppermute(below[:half], axis, up)]
  transfers between devices with their start and end apart: 24 -> 28, of which waited for: 11 -> 15; matrix products, arithmetic and copies ran while one was open for 2% -> 2% of each run, Pallas kernels for 44% -> 41%
where the time goes in v6:
time: 111 us
  Pallas kernels  54.7 us (49%)
  starting transfers between devices  31.1 us (28%)
  waiting for transfers between devices  20.3 us (18%)
  other arithmetic  3.73 us (3%)
    pallas_call x8, Pallas kernels, half_units(): pl.pallas_call(functools.partial(half_body, n, experts, side, ahead, len(...  34.1 us
    pallas_call x4, Pallas kernels, down(): pl.pallas_call(functools.partial(down_body, lanes, cuts, experts, first,...  17.4 us
    ppermute x13, waiting for transfers between devices, flip(): lax.ppermute(x, axis, [(i, i ^ k) for i in range(lax.axis_size(axis))])  8.23 us
    ppermute x2, starting transfers between devices, returned(): low = lax.ppermute(a.astype(jnp.bfloat16), axis, down_)  7.7 us
    ppermute x13, starting transfers between devices, flip(): lax.ppermute(x, axis, [(i, i ^ k) for i in range(lax.axis_size(axis))])  5.17 us
    ppermute x1, starting transfers between devices, gathered(): lax.ppermute(above, axis, down_)  5.05 us
    ppermute x3, starting transfers between devices, on_device(): lax.ppermute(meta, 'expert', [(i, (i - k) % n_owner) for i in range(n_own...  4.39 us
    ppermute x1, waiting for transfers between devices, gathered(): lax.ppermute(below[:half], axis, up)  4.2 us
  transfers between devices with their start and end apart: 28, of which 15 were waited for; matrix products, arithmetic and copies ran while one was open for 2% of the time, Pallas kernels for 41%

profile of v6, /device:TPU:0, one launch (start us, length us, event | category | flops | bytes accessed | tf_op | source)
XLA Modules:
  0.0 110.6 jit_solution(9662171626543474021)
XLA Ops:
  0.0 5.0 %collective-permute-start.1 = (bf16[64,1536]{1,0:T(8,128)(2,1)}, bf16[64,1536]{1,0:T(8,128)(2,1)S(1)}, u32[]{:S(2)}, u32[]{:S(2)}) collective-permute-start(bf16[64,1536]{1,0:T(8,128)(2,1)} %refs_0_.7), channel_id=1, source_target_pairs={{0,12},{4,0},{8,4},{12,8},{1,13},{5,1},{9,5},{13,9},{2,14},{6,2},{... | collective-permute-start | bytes 589832 | tf_op jit(solution)/shard_map/ppermute | solution.py:384
  6.4 1.0 collective-permute-start.4
  7.4 2.8 %collective-permute-start.3 = (f32[16,64]{1,0:T(8,128)S(1)}, f32[16,64]{1,0:T(8,128)S(1)}, u32[]{:S(2)}, u32[]{:S(2)}) collective-permute-start(f32[16,64]{1,0:T(8,128)S(1)} %pad_maximum_fusion.12.refs_0_), channel_id=1, source_target_pairs={{0,12},{4,0},{8,4},{12,8},{1,13},{5,1},{9,5},{13,9},{2,14},{6,2},{... | collective-permute-start | bytes 12296 | tf_op jit(solution)/shard_map/ppermute | solution.py:315
  10.9 2.4 %stage.1.refs_6_ = bf16[2,1536,512]{2,1,0:T(8,128)(2,1)S(1)} custom-call(s32[3]{0:T(128)S(1)} %pad_add_fusion.info, bf16[8,1536,1024]{2,1,0:T(8,128)(2,1)} %refs_2_.7), custom_call_target="tpu_custom_call" | custom-call | flops 1 | bytes 1 | tf_op jit(solution)/shard_map/stage/pallas_call | solution.py:176
  14.1 1.6 %collective-permute-done.2.refs_1_ = f32[16,64]{1,0:T(8,128)S(1)} collective-permute-done((f32[16,64]{1,0:T(8,128)S(1)}, f32[16,64]{1,0:T(8,128)S(1)}, u32[]{:S(2)}, u32[]{:S(2)}) %collective-permute-start.2) | collective-permute-done | bytes 4128 | tf_op jit(solution)/shard_map/ppermute | solution.py:315
  15.7 2.8 %collective-permute-start.6 = (bf16[32,1536]{1,0:T(8,128)(2,1)S(1)}, bf16[32,1536]{1,0:T(8,128)(2,1)S(1)}, u32[]{:S(2)}, u32[]{:S(2)}) collective-permute-start(bf16[32,1536]{1,0:T(8,128)(2,1)S(1)} %slice.125), channel_id=1, source_target_pairs={{0,12},{4,0},{8,4},{12,8},{1,13},{5,1},{9,5},{13,9},{2,14},{6,2},{... | collective-permute-start | bytes 294920 | tf_op jit(solution)/shard_map/ppermute | solution.py:389
  18.5 0.7 route.1
  19.2 1.5 %collective-permute-done.6.refs_4_ = bf16[32,1536]{1,0:T(8,128)(2,1)S(1)} collective-permute-done((bf16[32,1536]{1,0:T(8,128)(2,1)S(1)}, bf16[32,1536]{1,0:T(8,128)(2,1)S(1)}, u32[]{:S(2)}, u32[]{:S(2)}) %collective-permute-start.6) | collective-permute-done | bytes 98336 | tf_op jit(solution)/shard_map/ppermute | solution.py:389
  20.7 4.2 %collective-permute-done.5.refs_3_ = bf16[32,1536]{1,0:T(8,128)(2,1)S(1)} collective-permute-done((bf16[32,1536]{1,0:T(8,128)(2,1)S(1)}, bf16[32,1536]{1,0:T(8,128)(2,1)S(1)}, u32[]{:S(2)}, u32[]{:S(2)}) %collective-permute-start.5) | collective-permute-done | bytes 98336 | tf_op jit(solution)/shard_map/ppermute | solution.py:389
  24.9 4.6 %send_half.4 = (bf16[2,256,512]{2,1,0:T(8,128)(2,1)S(1)}, bf16[256,1536]{1,0:T(8,128)(2,1)S(1)}, bf16[2,1536,512]{2,1,0:T(8,128)(2,1)S(1)}) custom-call(s32[3]{0:T(128)S(1)} %pad_add_fusion.info, bf16[64,1536]{1,0:T(8,128)(2,1)S(1)} %copy-done, bf16[64,1536]{1,0:T(8,128)(2,1)S(1)} %collective-permute-done.refs_1_, ...), custom_call_target="tpu_custom_call" | custom-call | flops 1 | bytes 1 | tf_op jit(solution)/shard_map/send_half/pallas_call | solution.py:154
  29.6 4.2 %keep_half.4 = (bf16[2,256,512]{2,1,0:T(8,128)(2,1)S(1)}, bf16[2,1536,512]{2,1,0:T(8,128)(2,1)S(1)}) custom-call(s32[3]{0:T(128)S(1)} %pad_add_fusion.info, bf16[256,1536]{1,0:T(8,128)(2,1)S(1)} %get-tuple-element.42.refs_0_, bf16[2,1536,512]{2,1,0:T(8,128)(2,1)S(1)} %get-tuple-element.43.refs_1_, bf16[8,1536,1024]{2,1,0:T(8,128)(2,1)} %refs_2_.7, ...), custom_call_target="tpu_custom_call" | custom-call | flops 1 | bytes 1 | tf_op jit(solution)/shard_map/keep_half/pallas_call | solution.py:154
  34.0 1.6 %collective-permute-start.9 = (bf16[1,256,512]{2,1,0:T(8,128)(2,1)S(1)}, bf16[1,256,512]{2,1,0:T(8,128)(2,1)S(1)}, u32[]{:S(2)}, u32[]{:S(2)}) collective-permute-start(bf16[1,256,512]{2,1,0:T(8,128)(2,1)S(1)} %slice.219.refs_9_), channel_id=1, source_target_pairs={{0,2},{1,3},{2,0},{3,1},{4,6},{5,7},{6,4},{7,5},{8,10},{9,11},{10,... | collective-permute-start | bytes 786440 | tf_op jit(solution)/shard_map/ppermute | solution.py:23
  35.5 4.6 %send_half.5 = (bf16[2,256,512]{2,1,0:T(8,128)(2,1)S(1)}, bf16[256,1536]{1,0:T(8,128)(2,1)S(1)}, bf16[2,1536,512]{2,1,0:T(8,128)(2,1)S(1)}) custom-call(s32[3]{0:T(128)S(1)} %pad_add_fusion.info, bf16[64,1536]{1,0:T(8,128)(2,1)S(1)} %copy-done, bf16[64,1536]{1,0:T(8,128)(2,1)S(1)} %collective-permute-done.refs_1_, ...), custom_call_target="tpu_custom_call" | custom-call | flops 1 | bytes 1 | tf_op jit(solution)/shard_map/send_half/pallas_call | solution.py:154
  40.2 4.0 %keep_half.5 = (bf16[2,256,512]{2,1,0:T(8,128)(2,1)S(1)}, bf16[2,1536,512]{2,1,0:T(8,128)(2,1)S(1)}) custom-call(s32[3]{0:T(128)S(1)} %pad_add_fusion.info, bf16[256,1536]{1,0:T(8,128)(2,1)S(1)} %get-tuple-element.47.refs_0_, bf16[2,1536,512]{2,1,0:T(8,128)(2,1)S(1)} %get-tuple-element.48.refs_1_, bf16[8,1536,1024]{2,1,0:T(8,128)(2,1)} %refs_2_.7, ...), custom_call_target="tpu_custom_call" | custom-call | flops 1 | bytes 1 | tf_op jit(solution)/shard_map/keep_half/pallas_call | solution.py:154
  45.3 4.6 %send_half.6 = (bf16[2,256,512]{2,1,0:T(8,128)(2,1)S(1)}, bf16[256,1536]{1,0:T(8,128)(2,1)S(1)}, bf16[2,1536,512]{2,1,0:T(8,128)(2,1)S(1)}) custom-call(s32[3]{0:T(128)S(1)} %pad_add_fusion.info, bf16[64,1536]{1,0:T(8,128)(2,1)S(1)} %copy-done, bf16[64,1536]{1,0:T(8,128)(2,1)S(1)} %collective-permute-done.refs_1_, ...), custom_call_target="tpu_custom_call" | custom-call | flops 1 | bytes 1 | tf_op jit(solution)/shard_map/send_half/pallas_call | solution.py:154
  50.1 4.0 %keep_half.6 = (bf16[2,256,512]{2,1,0:T(8,128)(2,1)S(1)}, bf16[2,1536,512]{2,1,0:T(8,128)(2,1)S(1)}) custom-call(s32[3]{0:T(128)S(1)} %pad_add_fusion.info, bf16[256,1536]{1,0:T(8,128)(2,1)S(1)} %get-tuple-element.52.refs_0_, bf16[2,1536,512]{2,1,0:T(8,128)(2,1)S(1)} %get-tuple-element.53.refs_1_, bf16[8,1536,1024]{2,1,0:T(8,128)(2,1)} %refs_2_.7, ...), custom_call_target="tpu_custom_call" | custom-call | flops 1 | bytes 1 | tf_op jit(solution)/shard_map/keep_half/pallas_call | solution.py:154
  54.1 2.2 %collective-permute-done.11.refs_1_ = bf16[1,256,768]{2,1,0:T(8,128)(2,1)S(1)} collective-permute-done((bf16[1,256,768]{2,1,0:T(8,128)(2,1)S(1)}, bf16[1,256,768]{2,1,0:T(8,128)(2,1)S(1)}, u32[]{:S(2)}, u32[]{:S(2)}) %collective-permute-start.11) | collective-permute-done | bytes 393248 | tf_op jit(solution)/shard_map/ppermute | solution.py:23
  57.4 4.8 %send_half.7 = (bf16[2,256,512]{2,1,0:T(8,128)(2,1)S(1)}, bf16[256,1536]{1,0:T(8,128)(2,1)S(1)}, bf16[2,1536,512]{2,1,0:T(8,128)(2,1)S(1)}) custom-call(s32[3]{0:T(128)S(1)} %pad_add_fusion.info, bf16[64,1536]{1,0:T(8,128)(2,1)S(1)} %copy-done, bf16[64,1536]{1,0:T(8,128)(2,1)S(1)} %collective-permute-done.refs_1_, ...), custom_call_target="tpu_custom_call" | custom-call | flops 1 | bytes 1 | tf_op jit(solution)/shard_map/send_half/pallas_call | solution.py:154
  62.7 3.5 %keep_half.7 = bf16[2,256,512]{2,1,0:T(8,128)(2,1)S(1)} custom-call(s32[3]{0:T(128)S(1)} %pad_add_fusion.info, bf16[256,1536]{1,0:T(8,128)(2,1)S(1)} %get-tuple-element.57.refs_0_, bf16[2,1536,512]{2,1,0:T(8,128)(2,1)S(1)} %get-tuple-element.58.refs_1_, bf16[8,1536,1024]{2,1,0:T(8,128)(2,1)} %refs_2_.7, bf16[8,1536,1024]{2,1,0:T(8,128)(2,1)} %refs_3_.7), custom_call_target="tpu_custom_call" | custom-call | flops 1 | bytes 1 | tf_op jit(solution)/shard_map/keep_half/pallas_call | solution.py:154
  66.2 1.3 %collective-permute-done.13.refs_1_ = bf16[1,256,768]{2,1,0:T(8,128)(2,1)S(1)} collective-permute-done((bf16[1,256,768]{2,1,0:T(8,128)(2,1)S(1)}, bf16[1,256,768]{2,1,0:T(8,128)(2,1)S(1)}, u32[]{:S(2)}, u32[]{:S(2)}) %collective-permute-start.13) | collective-permute-done | bytes 393248 | tf_op jit(solution)/shard_map/ppermute | solution.py:23
  68.6 4.3 %down.4.refs_6_ = f32[256,1536]{1,0:T(8,128)S(1)} custom-call(s32[3]{0:T(128)S(1)} %pad_add_fusion.info, bf16[1,256,256]{2,1,0:T(8,128)(2,1)S(1)} %fusion.3.refs_0_, bf16[1,256,768]{2,1,0:T(8,128)(2,1)S(1)} %collective-permute-done.11.refs_1_, bf16[2,256,256]{2,1,0:T(8,128)(2,1)S(1)} %collective-permute-done.16.refs_2_, ...), custom_call_target="tpu_custom_call" | custom-call | flops 4026531840 | bytes 9437184 | tf_op jit(solution)/shard_map/down/pallas_call | solution.py:249
  72.9 4.4 %down.5.refs_6_ = f32[256,1536]{1,0:T(8,128)S(1)} custom-call(s32[3]{0:T(128)S(1)} %pad_add_fusion.info, bf16[1,256,256]{2,1,0:T(8,128)(2,1)S(1)} %fusion.2.refs_0_, bf16[1,256,768]{2,1,0:T(8,128)(2,1)S(1)} %collective-permute-done.13.refs_1_, bf16[2,256,256]{2,1,0:T(8,128)(2,1)S(1)} %collective-permute-done.15.refs_2_, ...), custom_call_target="tpu_custom_call" | custom-call | flops 4026531840 | bytes 9437184 | tf_op jit(solution)/shard_map/down/pallas_call | solution.py:249
  77.3 2.3 %collective-permute-done.14.refs_1_ = bf16[1,256,768]{2,1,0:T(8,128)(2,1)S(1)} collective-permute-done((bf16[1,256,768]{2,1,0:T(8,128)(2,1)S(1)}, bf16[1,256,768]{2,1,0:T(8,128)(2,1)S(1)}, u32[]{:S(2)}, u32[]{:S(2)}) %collective-permute-start.14) | collective-permute-done | bytes 393248 | tf_op jit(solution)/shard_map/ppermute | solution.py:23
  80.5 0.7 collective-permute-done.18.refs_2_
  81.2 4.4 %down.6.refs_6_ = f32[256,1536]{1,0:T(8,128)S(1)} custom-call(s32[3]{0:T(128)S(1)} %pad_add_fusion.info, bf16[1,256,256]{2,1,0:T(8,128)(2,1)S(1)} %fusion.1.refs_0_, bf16[1,256,768]{2,1,0:T(8,128)(2,1)S(1)} %collective-permute-done.14.refs_1_, bf16[2,256,256]{2,1,0:T(8,128)(2,1)S(1)} %collective-permute-done.18.refs_2_, ...), custom_call_target="tpu_custom_call" | custom-call | flops 4026531840 | bytes 9437184 | tf_op jit(solution)/shard_map/down/pallas_call | solution.py:249
  85.9 1.5 %collective-permute-done.19.refs_2_ = bf16[2,256,256]{2,1,0:T(8,128)(2,1)S(1)} collective-permute-done((bf16[2,256,256]{2,1,0:T(8,128)(2,1)S(1)}, bf16[2,256,256]{2,1,0:T(8,128)(2,1)S(1)}, u32[]{:S(2)}, u32[]{:S(2)}) %collective-permute-start.19) | collective-permute-done | bytes 262176 | tf_op jit(solution)/shard_map/ppermute | solution.py:23
  87.5 4.4 %down.7 = (bf16[64,1024]{1,0:T(8,128)(2,1)S(1)}, bf16[64,1024]{1,0:T(8,128)(2,1)S(1)}, bf16[64,1024]{1,0:T(8,128)(2,1)S(1)}, bf16[32,1024]{1,0:T(8,128)(2,1)S(1)...) custom-call(s32[3]{0:T(128)S(1)} %pad_add_fusion.info, ...), custom_call_target="tpu_custom_call" | custom-call | flops 4026531840 | bytes 9437184 | tf_op jit(solution)/shard_map/down/pallas_call | solution.py:249
  91.9 3.8 %collective-permute-start.24 = (bf16[32,512]{1,0:T(8,128)(2,1)S(1)}, bf16[32,512]{1,0:T(8,128)(2,1)S(1)}, u32[]{:S(2)}, u32[]{:S(2)}) collective-permute-start(bf16[32,512]{1,0:T(8,128)(2,1)S(1)} %get-tuple-element.70), channel_id=1, source_target_pairs={{0,12},{4,0},{8,4},{12,8},{1,13},{5,1},{9,5},{13,9},{2,14},{6,2},{... | collective-permute-start | bytes 98312 | tf_op jit(solution)/shard_map/ppermute | solution.py:403
  95.8 2.0 %collective-permute-start.22 = (bf16[32,1024]{1,0:T(8,128)(2,1)S(1)}, bf16[32,1024]{1,0:T(8,128)(2,1)S(1)}, u32[]{:S(2)}, u32[]{:S(2)}) collective-permute-start(bf16[32,1024]{1,0:T(8,128)(2,1)S(1)} %get-tuple-element.67), channel_id=1, source_target_pairs={{0,4},{4,8},{8,12},{12,0},{1,5},{5,9},{9,13},{13,1},{2,6},{6,10},{... | collective-permute-start | bytes 196616 | tf_op jit(solution)/shard_map/ppermute | solution.py:403
  98.1 3.9 %collective-permute-start.25 = (bf16[64,512]{1,0:T(8,128)(2,1)S(1)}, bf16[64,512]{1,0:T(8,128)(2,1)S(1)}, u32[]{:S(2)}, u32[]{:S(2)}) collective-permute-start(bf16[64,512]{1,0:T(8,128)(2,1)S(1)} %pad_maximum_fusion.10), channel_id=1, source_target_pairs={{0,12},{4,0},{8,4},{12,8},{1,13},{5,1},{9,5},{13,9},{2,14},{6,2},{... | collective-permute-start | bytes 196616 | tf_op jit(solution)/shard_map/ppermute | solution.py:412
  102.8 3.9 %collective-permute-start.21 = (bf16[64,1024]{1,0:T(8,128)(2,1)S(1)}, bf16[64,1024]{1,0:T(8,128)(2,1)S(1)}, u32[]{:S(2)}, u32[]{:S(2)}) collective-permute-start(bf16[64,1024]{1,0:T(8,128)(2,1)S(1)} %pad_maximum_fusion.8), channel_id=1, source_target_pairs={{0,12},{4,0},{8,4},{12,8},{1,13},{5,1},{9,5},{13,9},{2,14},{6,2},{... | collective-permute-start | bytes 393224 | tf_op jit(solution)/shard_map/ppermute | solution.py:412
  106.7 3.0 %collective-permute-done.23 = bf16[64,1024]{1,0:T(8,128)(2,1)S(1)} collective-permute-done((bf16[64,1024]{1,0:T(8,128)(2,1)S(1)}, bf16[64,1024]{1,0:T(8,128)(2,1)S(1)}, u32[]{:S(2)}, u32[]{:S(2)}) %collective-permute-start.23) | collective-permute-done | bytes 131104 | tf_op jit(solution)/shard_map/ppermute | solution.py:413
  (87 shorter events, 10.5 us)
Async XLA Ops:
  0.0 15.7 %collective-permute-start.1 = (bf16[64,1536]{1,0:T(8,128)(2,1)}, bf16[64,1536]{1,0:T(8,128)(2,1)S(1)}, u32[]{:S(2)}, u32[]{:S(2)}) collective-permute-start(bf16[64,1536]{1,0:T(8,128)(2,1)} %refs_0_.7), channel_id=1, source_target_pairs={{0,12},{4,0},{8,4},{12,8},{1,13},{5,1},{9,5},{13,9},{2,14},{6,2},{... | collective-permute-start | bytes 589832 | tf_op jit(solution)/shard_map/ppermute | solution.py:384
  5.0 10.7 %collective-permute-start = (bf16[64,1536]{1,0:T(8,128)(2,1)}, bf16[64,1536]{1,0:T(8,128)(2,1)S(1)}, u32[]{:S(2)}, u32[]{:S(2)}) collective-permute-start(bf16[64,1536]{1,0:T(8,128)(2,1)} %refs_0_.7), channel_id=1, source_target_pairs={{0,4},{4,8},{8,12},{12,0},{1,5},{5,9},{9,13},{13,1},{2,6},{6,10},{... | collective-permute-start | bytes 589832 | tf_op jit(solution)/shard_map/ppermute | solution.py:384
  6.4 7.6 %collective-permute-start.4 = (f32[16,64]{1,0:T(8,128)S(1)}, f32[16,64]{1,0:T(8,128)S(1)}, u32[]{:S(2)}, u32[]{:S(2)}) collective-permute-start(f32[16,64]{1,0:T(8,128)S(1)} %pad_maximum_fusion.12.refs_0_), channel_id=1, source_target_pairs={{0,8},{4,12},{8,0},{12,4},{1,9},{5,13},{9,1},{13,5},{2,10},{6,14},... | collective-permute-start | bytes 12296 | tf_op jit(solution)/shard_map/ppermute | solution.py:315
  7.4 6.7 %collective-permute-start.3 = (f32[16,64]{1,0:T(8,128)S(1)}, f32[16,64]{1,0:T(8,128)S(1)}, u32[]{:S(2)}, u32[]{:S(2)}) collective-permute-start(f32[16,64]{1,0:T(8,128)S(1)} %pad_maximum_fusion.12.refs_0_), channel_id=1, source_target_pairs={{0,12},{4,0},{8,4},{12,8},{1,13},{5,1},{9,5},{13,9},{2,14},{6,2},{... | collective-permute-start | bytes 12296 | tf_op jit(solution)/shard_map/ppermute | solution.py:315
  10.3 5.4 %collective-permute-start.2 = (f32[16,64]{1,0:T(8,128)S(1)}, f32[16,64]{1,0:T(8,128)S(1)}, u32[]{:S(2)}, u32[]{:S(2)}) collective-permute-start(f32[16,64]{1,0:T(8,128)S(1)} %pad_maximum_fusion.12.refs_0_), channel_id=1, source_target_pairs={{0,4},{4,8},{8,12},{12,0},{1,5},{5,9},{9,13},{13,1},{2,6},{6,10},{... | collective-permute-start | bytes 12296 | tf_op jit(solution)/shard_map/ppermute | solution.py:315
  10.9 14.0 %copy-start = (bf16[64,1536]{1,0:T(8,128)(2,1)S(1)}, bf16[64,1536]{1,0:T(8,128)(2,1)}, u32[]{:S(2)}) copy-start(bf16[64,1536]{1,0:T(8,128)(2,1)} %refs_0_.7) | copy-start | bytes 589828
  15.7 5.0 %collective-permute-start.6 = (bf16[32,1536]{1,0:T(8,128)(2,1)S(1)}, bf16[32,1536]{1,0:T(8,128)(2,1)S(1)}, u32[]{:S(2)}, u32[]{:S(2)}) collective-permute-start(bf16[32,1536]{1,0:T(8,128)(2,1)S(1)} %slice.125), channel_id=1, source_target_pairs={{0,12},{4,0},{8,4},{12,8},{1,13},{5,1},{9,5},{13,9},{2,14},{6,2},{... | collective-permute-start | bytes 294920 | tf_op jit(solution)/shard_map/ppermute | solution.py:389
  18.5 6.4 %collective-permute-start.5 = (bf16[32,1536]{1,0:T(8,128)(2,1)S(1)}, bf16[32,1536]{1,0:T(8,128)(2,1)S(1)}, u32[]{:S(2)}, u32[]{:S(2)}) collective-permute-start(bf16[32,1536]{1,0:T(8,128)(2,1)S(1)} %slice.124), channel_id=1, source_target_pairs={{0,4},{4,8},{8,12},{12,0},{1,5},{5,9},{9,13},{13,1},{2,6},{6,10},{... | collective-permute-start | bytes 294920 | tf_op jit(solution)/shard_map/ppermute | solution.py:389
  29.5 4.2 %collective-permute-start.7 = (bf16[2,256,512]{2,1,0:T(8,128)(2,1)S(1)}, bf16[2,256,512]{2,1,0:T(8,128)(2,1)S(1)}, u32[]{:S(2)}, u32[]{:S(2)}) collective-permute-start(bf16[2,256,512]{2,1,0:T(8,128)(2,1)S(1)} %get-tuple-element.46), channel_id=1, source_target_pairs={{0,1},{1,0},{2,3},{3,2},{4,5},{5,4},{6,7},{7,6},{8,9},{9,8},{10,11... | collective-permute-start | bytes 1572872 | tf_op jit(solution)/shard_map/ppermute | solution.py:23
  34.0 10.3 %collective-permute-start.9 = (bf16[1,256,512]{2,1,0:T(8,128)(2,1)S(1)}, bf16[1,256,512]{2,1,0:T(8,128)(2,1)S(1)}, u32[]{:S(2)}, u32[]{:S(2)}) collective-permute-start(bf16[1,256,512]{2,1,0:T(8,128)(2,1)S(1)} %slice.219.refs_9_), channel_id=1, source_target_pairs={{0,2},{1,3},{2,0},{3,1},{4,6},{5,7},{6,4},{7,5},{8,10},{9,11},{10,... | collective-permute-start | bytes 786440 | tf_op jit(solution)/shard_map/ppermute | solution.py:23
  40.1 4.3 %collective-permute-start.8 = (bf16[2,256,512]{2,1,0:T(8,128)(2,1)S(1)}, bf16[2,256,512]{2,1,0:T(8,128)(2,1)S(1)}, u32[]{:S(2)}, u32[]{:S(2)}) collective-permute-start(bf16[2,256,512]{2,1,0:T(8,128)(2,1)S(1)} %get-tuple-element.51), channel_id=1, source_target_pairs={{0,1},{1,0},{2,3},{3,2},{4,5},{5,4},{6,7},{7,6},{8,9},{9,8},{10,11... | collective-permute-start | bytes 1572872 | tf_op jit(solution)/shard_map/ppermute | solution.py:23
  44.7 11.6 %collective-permute-start.11 = (bf16[1,256,768]{2,1,0:T(8,128)(2,1)S(1)}, bf16[1,256,768]{2,1,0:T(8,128)(2,1)S(1)}, u32[]{:S(2)}, u32[]{:S(2)}) collective-permute-start(bf16[1,256,768]{2,1,0:T(8,128)(2,1)S(1)} %pad_maximum_fusion.refs_9_), channel_id=1, source_target_pairs={{0,2},{1,3},{2,0},{3,1},{4,6},{5,7},{6,4},{7,5},{8,10},{9,11},{10,... | collective-permute-start | bytes 1179656 | tf_op jit(solution)/shard_map/ppermute | solution.py:23
  49.9 6.5 %collective-permute-start.10 = (bf16[2,256,512]{2,1,0:T(8,128)(2,1)S(1)}, bf16[2,256,512]{2,1,0:T(8,128)(2,1)S(1)}, u32[]{:S(2)}, u32[]{:S(2)}) collective-permute-start(bf16[2,256,512]{2,1,0:T(8,128)(2,1)S(1)} %get-tuple-element.56), channel_id=1, source_target_pairs={{0,1},{1,0},{2,3},{3,2},{4,5},{5,4},{6,7},{7,6},{8,9},{9,8},{10,11... | collective-permute-start | bytes 1572872 | tf_op jit(solution)/shard_map/ppermute | solution.py:23
  56.7 10.8 %collective-permute-start.13 = (bf16[1,256,768]{2,1,0:T(8,128)(2,1)S(1)}, bf16[1,256,768]{2,1,0:T(8,128)(2,1)S(1)}, u32[]{:S(2)}, u32[]{:S(2)}) collective-permute-start(bf16[1,256,768]{2,1,0:T(8,128)(2,1)S(1)} %pad_maximum_fusion.1.refs_9_), channel_id=1, source_target_pairs={{0,2},{1,3},{2,0},{3,1},{4,6},{5,7},{6,4},{7,5},{8,10},{9,11},{10,... | collective-permute-start | bytes 1179656 | tf_op jit(solution)/shard_map/ppermute | solution.py:23
  57.3 11.3 %collective-permute-start.16 = (bf16[2,256,256]{2,1,0:T(8,128)(2,1)S(1)}, bf16[2,256,256]{2,1,0:T(8,128)(2,1)S(1)}, u32[]{:S(2)}, u32[]{:S(2)}) collective-permute-start(bf16[2,256,256]{2,1,0:T(8,128)(2,1)S(1)} %pad_maximum_fusion.4), channel_id=1, source_target_pairs={{0,1},{1,0},{2,3},{3,2},{4,5},{5,4},{6,7},{7,6},{8,9},{9,8},{10,11... | collective-permute-start | bytes 786440 | tf_op jit(solution)/shard_map/ppermute | solution.py:23
  62.2 5.6 %collective-permute-start.12 = (bf16[2,256,512]{2,1,0:T(8,128)(2,1)S(1)}, bf16[2,256,512]{2,1,0:T(8,128)(2,1)S(1)}, u32[]{:S(2)}, u32[]{:S(2)}) collective-permute-start(bf16[2,256,512]{2,1,0:T(8,128)(2,1)S(1)} %get-tuple-element.59), channel_id=1, source_target_pairs={{0,1},{1,0},{2,3},{3,2},{4,5},{5,4},{6,7},{7,6},{8,9},{9,8},{10,11... | collective-permute-start | bytes 1572872 | tf_op jit(solution)/shard_map/ppermute | solution.py:23
  67.5 5.4 %collective-permute-start.15 = (bf16[2,256,256]{2,1,0:T(8,128)(2,1)S(1)}, bf16[2,256,256]{2,1,0:T(8,128)(2,1)S(1)}, u32[]{:S(2)}, u32[]{:S(2)}) collective-permute-start(bf16[2,256,256]{2,1,0:T(8,128)(2,1)S(1)} %pad_maximum_fusion.3), channel_id=1, source_target_pairs={{0,1},{1,0},{2,3},{3,2},{4,5},{5,4},{6,7},{7,6},{8,9},{9,8},{10,11... | collective-permute-start | bytes 786440 | tf_op jit(solution)/shard_map/ppermute | solution.py:23
  68.0 11.6 %collective-permute-start.14 = (bf16[1,256,768]{2,1,0:T(8,128)(2,1)S(1)}, bf16[1,256,768]{2,1,0:T(8,128)(2,1)S(1)}, u32[]{:S(2)}, u32[]{:S(2)}) collective-permute-start(bf16[1,256,768]{2,1,0:T(8,128)(2,1)S(1)} %pad_maximum_fusion.2.refs_6_), channel_id=1, source_target_pairs={{0,2},{1,3},{2,0},{3,1},{4,6},{5,7},{6,4},{7,5},{8,10},{9,11},{10,... | collective-permute-start | bytes 1179656 | tf_op jit(solution)/shard_map/ppermute | solution.py:23
  79.6 1.6 %collective-permute-start.18 = (bf16[2,256,256]{2,1,0:T(8,128)(2,1)S(1)}, bf16[2,256,256]{2,1,0:T(8,128)(2,1)S(1)}, u32[]{:S(2)}, u32[]{:S(2)}) collective-permute-start(bf16[2,256,256]{2,1,0:T(8,128)(2,1)S(1)} %pad_maximum_fusion.5), channel_id=1, source_target_pairs={{0,1},{1,0},{2,3},{3,2},{4,5},{5,4},{6,7},{7,6},{8,9},{9,8},{10,11... | collective-permute-start | bytes 786440 | tf_op jit(solution)/shard_map/ppermute | solution.py:23
  79.9 6.0 %collective-permute-start.17 = (bf16[1,256,256]{2,1,0:T(8,128)(2,1)S(1)}, bf16[1,256,256]{2,1,0:T(8,128)(2,1)S(1)}, u32[]{:S(2)}, u32[]{:S(2)}) collective-permute-start(bf16[1,256,256]{2,1,0:T(8,128)(2,1)S(1)} %fusion.refs_7_.refs_0_), channel_id=1, source_target_pairs={{0,2},{1,3},{2,0},{3,1},{4,6},{5,7},{6,4},{7,5},{8,10},{9,11},{10,... | collective-permute-start | bytes 393224 | tf_op jit(solution)/shard_map/ppermute | solution.py:23
  85.9 1.6 %collective-permute-start.19 = (bf16[2,256,256]{2,1,0:T(8,128)(2,1)S(1)}, bf16[2,256,256]{2,1,0:T(8,128)(2,1)S(1)}, u32[]{:S(2)}, u32[]{:S(2)}) collective-permute-start(bf16[2,256,256]{2,1,0:T(8,128)(2,1)S(1)} %pad_maximum_fusion.6), channel_id=1, source_target_pairs={{0,1},{1,0},{2,3},{3,2},{4,5},{5,4},{6,7},{7,6},{8,9},{9,8},{10,11... | collective-permute-start | bytes 786440 | tf_op jit(solution)/shard_map/ppermute | solution.py:23
  91.8 6.1 %collective-permute-start.26 = (bf16[32,512]{1,0:T(8,128)(2,1)S(1)}, bf16[32,512]{1,0:T(8,128)(2,1)S(1)}, u32[]{:S(2)}, u32[]{:S(2)}) collective-permute-start(bf16[32,512]{1,0:T(8,128)(2,1)S(1)} %get-tuple-element.72), channel_id=1, source_target_pairs={{0,4},{4,8},{8,12},{12,0},{1,5},{5,9},{9,13},{13,1},{2,6},{6,10},{... | collective-permute-start | bytes 98312 | tf_op jit(solution)/shard_map/ppermute | solution.py:403
  91.9 6.1 %collective-permute-start.24 = (bf16[32,512]{1,0:T(8,128)(2,1)S(1)}, bf16[32,512]{1,0:T(8,128)(2,1)S(1)}, u32[]{:S(2)}, u32[]{:S(2)}) collective-permute-start(bf16[32,512]{1,0:T(8,128)(2,1)S(1)} %get-tuple-element.70), channel_id=1, source_target_pairs={{0,12},{4,0},{8,4},{12,8},{1,13},{5,1},{9,5},{13,9},{2,14},{6,2},{... | collective-permute-start | bytes 98312 | tf_op jit(solution)/shard_map/ppermute | solution.py:403
  95.7 7.0 %collective-permute-start.20 = (bf16[32,1024]{1,0:T(8,128)(2,1)S(1)}, bf16[32,1024]{1,0:T(8,128)(2,1)S(1)}, u32[]{:S(2)}, u32[]{:S(2)}) collective-permute-start(bf16[32,1024]{1,0:T(8,128)(2,1)S(1)} %get-tuple-element.65), channel_id=1, source_target_pairs={{0,12},{4,0},{8,4},{12,8},{1,13},{5,1},{9,5},{13,9},{2,14},{6,2},{... | collective-permute-start | bytes 196616 | tf_op jit(solution)/shard_map/ppermute | solution.py:403
  95.8 6.8 %collective-permute-start.22 = (bf16[32,1024]{1,0:T(8,128)(2,1)S(1)}, bf16[32,1024]{1,0:T(8,128)(2,1)S(1)}, u32[]{:S(2)}, u32[]{:S(2)}) collective-permute-start(bf16[32,1024]{1,0:T(8,128)(2,1)S(1)} %get-tuple-element.67), channel_id=1, source_target_pairs={{0,4},{4,8},{8,12},{12,0},{1,5},{5,9},{9,13},{13,1},{2,6},{6,10},{... | collective-permute-start | bytes 196616 | tf_op jit(solution)/shard_map/ppermute | solution.py:403
  97.9 8.7 %collective-permute-start.27 = (bf16[64,512]{1,0:T(8,128)(2,1)S(1)}, bf16[64,512]{1,0:T(8,128)(2,1)S(1)}, u32[]{:S(2)}, u32[]{:S(2)}) collective-permute-start(bf16[64,512]{1,0:T(8,128)(2,1)S(1)} %pad_maximum_fusion.11), channel_id=1, source_target_pairs={{0,4},{4,8},{8,12},{12,0},{1,5},{5,9},{9,13},{13,1},{2,6},{6,10},{... | collective-permute-start | bytes 196616 | tf_op jit(solution)/shard_map/ppermute | solution.py:413
  98.1 8.6 %collective-permute-start.25 = (bf16[64,512]{1,0:T(8,128)(2,1)S(1)}, bf16[64,512]{1,0:T(8,128)(2,1)S(1)}, u32[]{:S(2)}, u32[]{:S(2)}) collective-permute-start(bf16[64,512]{1,0:T(8,128)(2,1)S(1)} %pad_maximum_fusion.10), channel_id=1, source_target_pairs={{0,12},{4,0},{8,4},{12,8},{1,13},{5,1},{9,5},{13,9},{2,14},{6,2},{... | collective-permute-start | bytes 196616 | tf_op jit(solution)/shard_map/ppermute | solution.py:412
  102.7 7.0 %collective-permute-start.23 = (bf16[64,1024]{1,0:T(8,128)(2,1)S(1)}, bf16[64,1024]{1,0:T(8,128)(2,1)S(1)}, u32[]{:S(2)}, u32[]{:S(2)}) collective-permute-start(bf16[64,1024]{1,0:T(8,128)(2,1)S(1)} %pad_maximum_fusion.9), channel_id=1, source_target_pairs={{0,4},{4,8},{8,12},{12,0},{1,5},{5,9},{9,13},{13,1},{2,6},{6,10},{... | collective-permute-start | bytes 393224 | tf_op jit(solution)/shard_map/ppermute | solution.py:413
  102.8 7.1 %collective-permute-start.21 = (bf16[64,1024]{1,0:T(8,128)(2,1)S(1)}, bf16[64,1024]{1,0:T(8,128)(2,1)S(1)}, u32[]{:S(2)}, u32[]{:S(2)}) collective-permute-start(bf16[64,1024]{1,0:T(8,128)(2,1)S(1)} %pad_maximum_fusion.8), channel_id=1, source_target_pairs={{0,12},{4,0},{8,4},{12,8},{1,13},{5,1},{9,5},{13,9},{2,14},{6,2},{... | collective-permute-start | bytes 393224 | tf_op jit(solution)/shard_map/ppermute | solution.py:412

commit v7 on v6

v7 whole, which is shorter than its diff:
```python
import functools

import jax
import jax.numpy as jnp
from jax import lax
from jax.experimental import pallas as pl
from jax.experimental.pallas import tpu as pltpu
from jax.sharding import PartitionSpec as P

LANES = 128
VMEM = pl.BlockSpec(memory_space=pltpu.VMEM)
SMEM = pl.BlockSpec(memory_space=pltpu.SMEM)
HERE = pl.BlockSpec(memory_space=pl.ANY)
FAR = pl.BlockSpec(memory_space=pltpu.HBM)
NOWHERE = -1e6


def bits_of(n):
    return [b for b in range(n.bit_length() - 1)]


def flip(x, axis, k):
    return lax.ppermute(x, axis, [(i, i ^ k) for i in range(lax.axis_size(axis))])


def route_body(n, experts, info, *refs):
    meta, (rank, wt) = refs[:n], refs[n:]
    tok, top = meta[0].shape[1], meta[0].shape[0] // 2
    padded = rank.shape[0]
    first = info[0].astype(jnp.float32)
    e = lax.broadcasted_iota(jnp.int32, (padded, tok), 0).astype(jnp.float32)
    before = (
        lax.broadcasted_iota(jnp.int32, (tok, tok), 0) < lax.broadcasted_iota(jnp.int32, (tok, tok), 1)
    ).astype(jnp.bfloat16)
    count = jnp.zeros((padded, 1), jnp.float32)
    for s in range(n):
        ids, scores = meta[s][:top], meta[s][top:]
        affinity = 1.0 / (1.0 + jnp.exp(-scores))
        share = 2.5 * affinity / jnp.sum(affinity, axis=0, keepdims=True)
        named = jnp.zeros((padded, tok), jnp.float32)
        weight = jnp.zeros((padded, tok), jnp.float32)
        for k in range(top):
            hit = jnp.where(ids[k : k + 1] - first == e, 1.0, 0.0)
            named = named + hit
            weight = weight + hit * share[k : k + 1]
        named = jnp.where(e < experts, named, 0.0)
        place = jnp.dot(named.astype(jnp.bfloat16), before, preferred_element_type=jnp.float32) + count
        rank[:, s * tok : (s + 1) * tok] = jnp.where(named > 0, place, NOWHERE)
        wt[:, s * tok : (s + 1) * tok] = weight
        count = count + jnp.sum(named, axis=1, keepdims=True)


def route(meta, info, experts):
    tokens = len(meta) * meta[0].shape[1]
    table = jax.ShapeDtypeStruct((-(-experts // 8) * 8, tokens), jnp.float32)
    return pl.pallas_call(
        functools.partial(route_body, len(meta), experts),
        out_shape=(table, table),
        in_specs=[SMEM] + [VMEM] * len(meta),
        out_specs=(VMEM, VMEM),
        compiler_params=pltpu.CompilerParams(vmem_limit_bytes=40 << 20),
        name="route",
    )(info, *meta)


def backwards(l, n):
    bits = bits_of(n)
    return sum((((l >> b) & 1) << (len(bits) - 1 - b) for b in bits), 0 * l)


def units_of(l, info, n, width):
    return pl.ds(pl.multiple_of((backwards(l, n) ^ info[2]) * width, width), width)


def set_shape(need, weights):
    (_, depth, wide), (experts, side) = weights[0].shape, need
    return (len(experts), depth, wide) if side is None else (2, len(experts), depth, wide // 2)


def set_copies(need, weights, info, to, sem):
    experts, side = need
    if side is None:
        return [pltpu.make_async_copy(weights[0].at[e], to.at[x], sem.at[x]) for x, e in enumerate(experts)]
    half = to.shape[-1]
    units = pl.ds(pl.multiple_of(((info[1] & 1) ^ side) * half, half), half)
    return [
        pltpu.make_async_copy(w.at[e, :, units], to.at[m, x], sem.at[m * len(experts) + x])
        for m, w in enumerate(weights)
        for x, e in enumerate(experts)
    ]


def call(body, name, info, inputs, weights, ahead, after, outs, scratch, limit=24):
    n_in, n_out = len(inputs), len(outs)
    outs = list(outs)
    weights = [] if ahead is None else weights[2:] if ahead[1] is None else weights[:2]
    if ahead is not None:
        outs.append(jax.ShapeDtypeStruct(set_shape(ahead, weights), jnp.bfloat16))
        scratch = scratch + [pltpu.SemaphoreType.DMA((2 * len(ahead[0]),))]

    def whole(info, *refs):
        own, far = refs[:n_in], refs[n_in : n_in + len(weights)]
        rest = refs[n_in + len(weights) + len(after) :]
        results, rest = rest[: len(outs)], rest[len(outs) :]
        on = []
        if ahead is not None:
            on = set_copies(ahead, far, info, results[-1], rest[-1])
            rest = rest[:-1]
        body(info, own, results[:n_out], rest, lambda: [copy.start() for copy in on])
        for copy in on:
            copy.wait()

    return pl.pallas_call(
        whole,
        out_shape=tuple(outs),
        in_specs=[SMEM] + [spec for _, spec in inputs] + [HERE] * (len(weights) + len(after)),
        out_specs=(VMEM,) * len(outs),
        scratch_shapes=scratch,
        compiler_params=pltpu.CompilerParams(vmem_limit_bytes=limit << 20),
        cost_estimate=pl.CostEstimate(flops=1, bytes_accessed=1, transcendentals=0),
        name=name,
    )(info, *[x for x, _ in inputs], *weights, *after)


def stage(info, weights, need, after):
    body = lambda info, own, outs, rest, fetch: fetch()
    return call(body, "stage", info, [], weights, need, after, [], [], 40)[0]


def products(rows, given, to, info):
    most = rows.shape[0] // given.shape[1]
    shares, width = to.shape[0], to.shape[2] // 2
    for m in range(2):
        for x in range(given.shape[1]):
            mine = slice(x * most, (x + 1) * most)
            part = jnp.dot(rows[mine], given[m, x], preferred_element_type=jnp.float32)
            part = part.astype(jnp.bfloat16)
            for q in range(shares):
                j = backwards(q, shares) ^ (info[1] >> 1)
                to[j, mine, m * width : (m + 1) * width] = part[:, q * width : (q + 1) * width]


def send_body(experts, info, own, outs, rest, fetch):
    sources, rank, given = own[:-2], own[-2], own[-1]
    (to, rows), (feed, feed_sem) = outs, rest
    at, feeds = 0, []
    for s, source in enumerate(sources):
        tok = source.shape[0]
        feeds.append(pltpu.make_async_copy(source, feed.at[pl.ds(at, tok)], feed_sem.at[s]))
        at += tok
    for copy in feeds:
        copy.start()
    fetch()
    most = rows.shape[0] // len(experts)
    r = lax.broadcasted_iota(jnp.int32, (most, at), 0).astype(jnp.float32)
    pick = jnp.concatenate(
        [jnp.where(r == rank[e : e + 1, :], 1.0, 0.0).astype(jnp.bfloat16) for e in experts], axis=0
    )
    for copy in feeds:
        copy.wait()
    rows[...] = jnp.dot(pick, feed[...], preferred_element_type=jnp.float32).astype(jnp.bfloat16)
    products(rows, given, to, info)


def keep_body(info, own, outs, rest, fetch):
    fetch()
    rows, given = own
    products(rows, given, outs[0], info)


def part_shape(given, most, n_dp):
    _, experts, _, half = given.shape
    return jax.ShapeDtypeStruct((n_dp // 2, most * experts, 4 * half // n_dp), jnp.bfloat16)


def send_half(feeds, rank, info, given, weights, experts, most, n_dp, ahead, after):
    local = given.shape[2]
    rows = jax.ShapeDtypeStruct((most * len(experts), local), jnp.bfloat16)
    scratch = [
        pltpu.VMEM((rank.shape[1], local), jnp.bfloat16),
        pltpu.SemaphoreType.DMA((len(feeds),)),
    ]
    inputs = [(feed, HERE) for feed in feeds] + [(rank, VMEM), (given, VMEM)]
    outs = [part_shape(given, most, n_dp), rows]
    body = functools.partial(send_body, experts)
    return call(body, "send_half", info, inputs, weights, ahead, after, outs, scratch)


def keep_half(rows, info, given, weights, most, n_dp, ahead):
    inputs = [(rows, VMEM), (given, VMEM)]
    outs = [part_shape(given, most, n_dp)]
    return call(keep_body, "keep_half", info, inputs, weights, ahead, [], outs, [])


def down_body(lanes, experts, first, info, own, outs, rest, fetch):
    fetch()
    parts, (rank, wt, given) = own[: len(lanes)], own[len(lanes) : len(lanes) + 3]
    before = None if first else own[-1]
    hidden, mix, out = rest
    most = hidden.shape[0] // len(experts)
    width = parts[0].shape[-1]
    n_dp = hidden.shape[1] // width
    for part, (at, shares) in zip(parts, lanes):
        for j, l in enumerate(shares):
            hidden[:, units_of(l, info, n_dp, width)] = part[j, :, at : at + width]
    r = lax.broadcasted_iota(jnp.int32, (most, mix.shape[1]), 0).astype(jnp.float32)
    for x, e in enumerate(experts):
        mix[x * most : (x + 1) * most, :] = jnp.where(
            r == rank[e : e + 1, :], wt[e : e + 1, :], 0.0
        ).astype(jnp.bfloat16)
    local = out.shape[1]
    block = 512 if local % 512 == 0 else 256 if local % 256 == 0 else local
    for i in range(local // block):
        cols = slice(i * block, (i + 1) * block)
        for x in range(len(experts)):
            mine = slice(x * most, (x + 1) * most)
            out[mine, cols] = jnp.dot(
                hidden[mine], given[x, :, cols], preferred_element_type=jnp.float32
            ).astype(jnp.bfloat16)
        total = lax.dot_general(
            mix[...], out[:, cols], (((0,), (0,)), ((), ())), preferred_element_type=jnp.float32
        )
        if not first:
            total = total + before[:, cols]
        at = 0
        for to in outs:
            to[:, cols] = total[at : at + to.shape[0]].astype(to.dtype)
            at += to.shape[0]


def down(parts, rank, wt, info, given, weights, total, experts, cuts, ahead, after):
    parts, lanes = [part for part, *_ in parts], [tuple(where) for _, *where in parts]
    rows = parts[0].shape[1]
    _, hidden, local = given.shape
    kind = jnp.bfloat16 if len(cuts) > 1 else jnp.float32
    before = [] if total is None else [total]
    outs = [jax.ShapeDtypeStruct((cut, local), kind) for cut in cuts]
    scratch = [
        pltpu.VMEM((rows, hidden), jnp.bfloat16),
        pltpu.VMEM((rows, rank.shape[1]), jnp.bfloat16),
        pltpu.VMEM((rows, local), jnp.bfloat16),
    ]
    inputs = [(x, VMEM) for x in (*parts, rank, wt, given, *before)]
    body = functools.partial(down_body, lanes, experts, total is None)
    return call(body, "down", info, inputs, weights, ahead, after, outs, scratch)


def finish(total, late, after):
    if after:
        late, *_ = lax.optimization_barrier((late, *after))
    gate_up = total + late.astype(jnp.float32)
    width = gate_up.shape[2] // 2
    return (jax.nn.silu(gate_up[:, :, :width]) * gate_up[:, :, width:]).astype(jnp.bfloat16)


def chip_sums(send, keep, bits):
    total = keep.astype(jnp.float32) + flip(send, "dp", 1).astype(jnp.float32)
    for b in bits[1:-1]:
        total = total[0::2] + flip(total[1::2].astype(jnp.bfloat16), "dp", 1 << b).astype(jnp.float32)
    return total[0::2], total[1::2].astype(jnp.bfloat16)


def everyone_s(share, other, at, bits):
    width = share.shape[2]
    top = 1 << bits[-1]
    parts = [(share, 0, [0]), (other, at, [top])]
    held, whose = jnp.concatenate([share, other[:, :, at : at + width]], axis=0), [0, top]
    for b in reversed(bits[:-1]):
        theirs = flip(held, "dp", 1 << b)
        parts.append((theirs, 0, [l | 1 << b for l in whose]))
        if b > 0:
            held, whose = jnp.concatenate([held, theirs], axis=0), whose + parts[-1][2]
    return parts


def on_device(tokens, expert_ids, scores, w_gate, w_up, w_down):
    n_owner, n_dp = lax.axis_size("expert"), lax.axis_size("dp")
    tok_rows, top = expert_ids.shape
    experts = w_gate.shape[0]
    capacity = 2 * tok_rows * top // (experts * n_owner)
    per_chunk = 2 if experts % 2 == 0 else 1
    most = n_owner * capacity
    chunks = experts // per_chunk

    meta = jnp.concatenate([expert_ids.T.astype(jnp.float32), scores.T], axis=0)
    me = lax.axis_index("dp").astype(jnp.int32)
    first = lax.axis_index("expert").astype(jnp.int32) * experts
    info = jnp.stack([first, me, backwards(me, n_dp)])
    of = lambda c: list(range(c * per_chunk, (c + 1) * per_chunk))
    weights = (w_gate, w_up, w_down)
    needs = [(of(c), side) for c in range(chunks) for side in (1, 0)] + [(of(c), None) for c in range(chunks)]
    given = {0: stage(info, weights, needs[0], [])}

    def fetched(k, outs):
        if k + 2 < len(needs):
            *outs, given[k + 2] = outs
        return outs

    ahead = lambda k: needs[k + 2] if k + 2 < len(needs) else None

    meta = lax.optimization_barrier((meta, given[0]))[0]
    metas = [meta] + [
        lax.ppermute(meta, "expert", [(i, (i - k) % n_owner) for i in range(n_owner)])
        for k in gathered_order(n_owner)[1:]
    ]
    feeds, halfway = gathered(tokens, "expert", metas)
    given[1] = stage(info, weights, needs[1], halfway)
    rank, wt = route(metas, info, experts)

    tall, wide = [feed.shape[0] for feed in feeds], tokens.shape[1]
    bits = bits_of(n_dp)
    cross = 1 << bits[-1]
    sent, parts, total = [], [], None
    share = kept = late = None

    def add(c, after):
        k, cuts = 2 * chunks + c, tall if c == chunks - 1 else [sum(tall)]
        outs = down(parts[c], rank, wt, info, given[k], weights, total, of(c), cuts, ahead(k), after)
        outs = fetched(k, outs)
        return outs if c == chunks - 1 else outs[0]

    for c in range(chunks):
        last = c == chunks - 1
        k = 2 * c
        send, rows = fetched(
            k, send_half(feeds, rank, info, given[k], weights, of(c), most, n_dp, ahead(k), sent[-1:] or [given[1]])
        )
        k = 2 * c + 1
        (keep,) = fetched(k, keep_half(rows, info, given[k], weights, most, n_dp, ahead(k)))
        before, behind = kept, late
        kept, out = chip_sums(send, keep, bits)
        width = out.shape[2]
        if c > 0:
            share = finish(before, behind[:, :, :width], [])
            out = jnp.concatenate([out, share], axis=2)
        sent.append(out)
        late = flip(out, "dp", cross)
        if c > 0:
            parts.append(everyone_s(share, late, width, bits))
        if last:
            for d in range(min(c - 1, 2)):
                total = add(d, [out] if d == 0 else [])
    share = finish(kept, late[:, :, :width], [] if total is None else [total])
    other = flip(share, "dp", cross)
    for c in range(max(min(chunks - 2, 2), 0), chunks - 1):
        total = add(c, [share])
    if total is not None:
        other = lax.optimization_barrier((other, total))[0]
    parts.append(everyone_s(share, other, 0, bits))
    total = add(chunks - 1, [])
    return returned(total, "expert").astype(jnp.bfloat16)


def gathered_order(n):
    near = [d for s in range(1, n // 2) for d in (-s, s)]
    return [0] + near + ([n // 2] if n > 1 else [])


def gathered(x, axis, beside):
    n = lax.axis_size(axis)
    up, down_ = [(i, (i + 1) % n) for i in range(n)], [(i, (i - 1) % n) for i in range(n)]
    below = above = x
    found, halfway = [x], []
    for _ in range(1, n // 2):
        below, above = lax.ppermute(below, axis, up), lax.ppermute(above, axis, down_)
        found += [below, above]
    if n > 1:
        half = x.shape[0] // 2
        below, above, *_ = lax.optimization_barrier((below, above, *beside))
        halfway = [below]
        found += [lax.ppermute(below[:half], axis, up), lax.ppermute(above[half:], axis, down_)]
    return found, halfway


def returned(partials, axis):
    n = lax.axis_size(axis)
    up, down_ = [(i, (i + 1) % n) for i in range(n)], [(i, (i - 1) % n) for i in range(n)]
    wide = lambda x: x.astype(jnp.float32)
    near = {0: partials[0]}
    if n == 1:
        return wide(near[0])
    for k, partial in zip(gathered_order(n)[1:-1], partials[1:-2]):
        near[k] = partial
    half = partials[-1].shape[0]
    low, high = lax.ppermute(partials[-2], axis, down_), lax.ppermute(partials[-1], axis, up)
    halves = True
    for s in range(n // 2 - 1, 0, -1):
        a, b = wide(near[-s]), wide(near[s])
        if halves:
            a = jnp.concatenate([a[:half] + wide(low), a[half:]], axis=0)
            b = jnp.concatenate([b[:half], b[half:] + wide(high)], axis=0)
        else:
            a, b = a + wide(low), b + wide(high)
        low = lax.ppermute(a.astype(jnp.bfloat16), axis, down_)
        high = lax.ppermute(b.astype(jnp.bfloat16), axis, up)
        halves = False
    if halves:
        back = jnp.concatenate([wide(low), wide(high)], axis=0)
    else:
        back = wide(low) + wide(high)
    return wide(near[0]) + back


def solution(mesh):
    in_specs = (
        P(("groups", "expert"), "dp"),
        P(("groups", "expert"), None),
        P(("groups", "expert"), None),
        P("expert", "dp", None),
        P("expert", "dp", None),
        P("expert", None, "dp"),
    )
    out_specs = P(("groups", "expert"), "dp")
    return jax.shard_map(
        on_device, mesh=mesh, in_specs=in_specs, out_specs=out_specs, check_vma=False
    )
```

time: 111 us -> 108 us (0.973)
  starting transfers between devices: 31.1 us -> 25.4 us
  waiting for transfers between devices: 20.3 us -> 24.9 us
  Pallas kernels: 54.7 us -> 53.5 us
    ppermute x2 -> x1, waiting for transfers between devices: 0.22 us -> 4.85 us  [returned(): low = lax.ppermute(a.astype(jnp.bfloat16), axis, down_)]
    ppermute x1, waiting for transfers between devices: 4.2 us -> 0.01 us  [gathered(): lax.ppermute(below[:half], axis, up)]
    ppermute x2 -> x1, starting transfers between devices: 7.7 us -> 4.33 us  [returned(): low = lax.ppermute(a.astype(jnp.bfloat16), axis, down_)]
    ppermute x2 -> x1, waiting for transfers between devices: 0.01 us -> 3.11 us  [returned(): lax.ppermute(partials[-2], axis, down_)]
    ppermute x1, starting transfers between devices: 5.05 us -> 2.03 us  [gathered(): lax.ppermute(above, axis, down_)]
    ppermute x1, starting transfers between devices: 0.01 us -> 3.02 us  [gathered(): lax.ppermute(below, axis, up)]
    ppermute x3, waiting for transfers between devices: 2.35 us -> 4.55 us  [on_device(): lax.ppermute(meta, 'expert', [(i, (i - k) % n_owner) for i in range(n_own...]
    ppermute x2 -> x1, starting transfers between devices: 2.06 us -> 0.05 us  [returned(): lax.ppermute(partials[-1], axis, up)]
  transfers between devices with their start and end apart: 28 -> 24, of which waited for: 15 -> 11; matrix products, arithmetic and copies ran while one was open for 2% -> 1% of each run, Pallas kernels for 41% -> 43%
where the time goes in v7:
time: 108 us
  Pallas kernels  53.5 us (50%)
  starting transfers between devices  25.4 us (24%)
  waiting for transfers between devices  24.9 us (23%)
  other arithmetic  2.98 us (3%)
    pallas_call x14, Pallas kernels, call(): pl.pallas_call(whole, out_shape=tuple(outs), in_specs=[SMEM] + [spec for...  52.8 us
    ppermute x13, waiting for transfers between devices, flip(): lax.ppermute(x, axis, [(i, i ^ k) for i in range(lax.axis_size(axis))])  9.51 us
    ppermute x13, starting transfers between devices, flip(): lax.ppermute(x, axis, [(i, i ^ k) for i in range(lax.axis_size(axis))])  5.83 us
    ppermute x1, waiting for transfers between devices, returned(): low = lax.ppermute(a.astype(jnp.bfloat16), axis, down_)  4.85 us
    ppermute x3, waiting for transfers between devices, on_device(): lax.ppermute(meta, 'expert', [(i, (i - k) % n_owner) for i in range(n_own...  4.55 us
    ppermute x1, starting transfers between devices, returned(): low = lax.ppermute(a.astype(jnp.bfloat16), axis, down_)  4.33 us
    ppermute x3, starting transfers between devices, on_device(): lax.ppermute(meta, 'expert', [(i, (i - k) % n_owner) for i in range(n_own...  3.87 us
    ppermute x1, starting transfers between devices, gathered(): lax.ppermute(above[half:], axis, down_)  3.85 us
  transfers between devices with their start and end apart: 24, of which 11 were waited for; matrix products, arithmetic and copies ran while one was open for 1% of the time, Pallas kernels for 43%

profile of v7, /device:TPU:0, one launch (start us, length us, event | category | flops | bytes accessed | tf_op | source)
XLA Modules:
  0.0 107.6 jit_solution(11327341014504052062)
XLA Ops:
  0.0 3.0 %collective-permute-start = (bf16[64,1536]{1,0:T(8,128)(2,1)}, bf16[64,1536]{1,0:T(8,128)(2,1)S(1)}, u32[]{:S(2)}, u32[]{:S(2)}) collective-permute-start(bf16[64,1536]{1,0:T(8,128)(2,1)} %refs_0_.11), channel_id=1, source_target_pairs={{0,4},{4,8},{8,12},{12,0},{1,5},{5,9},{9,13},{13,1},{2,6},{6,10},{... | collective-permute-start | bytes 589832 | tf_op jit(solution)/shard_map/ppermute | solution.py:365
  3.0 2.0 %collective-permute-start.1 = (bf16[64,1536]{1,0:T(8,128)(2,1)}, bf16[64,1536]{1,0:T(8,128)(2,1)S(1)}, u32[]{:S(2)}, u32[]{:S(2)}) collective-permute-start(bf16[64,1536]{1,0:T(8,128)(2,1)} %refs_0_.11), channel_id=1, source_target_pairs={{0,12},{4,0},{8,4},{12,8},{1,13},{5,1},{9,5},{13,9},{2,14},{6,2},{... | collective-permute-start | bytes 589832 | tf_op jit(solution)/shard_map/ppermute | solution.py:365
  5.8 3.4 %stage.2.refs_6_ = bf16[2,2,1536,512]{3,2,1,0:T(8,128)(2,1)S(1)} custom-call(s32[3]{0:T(128)S(1)} %pad_add_fusion.info, bf16[8,1536,1024]{2,1,0:T(8,128)(2,1)} %refs_2_.6, bf16[8,1536,1024]{2,1,0:T(8,128)(2,1)} %refs_3_.5), custom_call_target="tpu_custom_call" | custom-call | flops 1 | bytes 1 | tf_op jit(solution)/shard_map/stage/pallas_call | solution.py:113
  9.3 3.8 %collective-permute-start.3 = (f32[16,64]{1,0:T(8,128)S(1)}, f32[16,64]{1,0:T(8,128)S(1)}, u32[]{:S(2)}, u32[]{:S(2)}) collective-permute-start(f32[16,64]{1,0:T(8,128)S(1)} %pad_maximum_fusion.9.refs_0_), channel_id=1, source_target_pairs={{0,12},{4,0},{8,4},{12,8},{1,13},{5,1},{9,5},{13,9},{2,14},{6,2},{... | collective-permute-start | bytes 12296 | tf_op jit(solution)/shard_map/ppermute | solution.py:303
  13.1 1.7 %collective-permute-done.2.refs_1_ = f32[16,64]{1,0:T(8,128)S(1)} collective-permute-done((f32[16,64]{1,0:T(8,128)S(1)}, f32[16,64]{1,0:T(8,128)S(1)}, u32[]{:S(2)}, u32[]{:S(2)}) %collective-permute-start.2) | collective-permute-done | bytes 4128 | tf_op jit(solution)/shard_map/ppermute | solution.py:303
  14.8 2.9 %collective-permute-done.4.refs_3_ = f32[16,64]{1,0:T(8,128)S(1)} collective-permute-done((f32[16,64]{1,0:T(8,128)S(1)}, f32[16,64]{1,0:T(8,128)S(1)}, u32[]{:S(2)}, u32[]{:S(2)}) %collective-permute-start.4) | collective-permute-done | bytes 4128 | tf_op jit(solution)/shard_map/ppermute | solution.py:303
  17.8 3.9 %collective-permute-start.6 = (bf16[32,1536]{1,0:T(8,128)(2,1)S(1)}, bf16[32,1536]{1,0:T(8,128)(2,1)S(1)}, u32[]{:S(2)}, u32[]{:S(2)}) collective-permute-start(bf16[32,1536]{1,0:T(8,128)(2,1)S(1)} %slice.105), channel_id=1, source_target_pairs={{0,12},{4,0},{8,4},{12,8},{1,13},{5,1},{9,5},{13,9},{2,14},{6,2},{... | collective-permute-start | bytes 294920 | tf_op jit(solution)/shard_map/ppermute | solution.py:371
  22.4 3.4 %stage.3.refs_9_.refs_1_ = bf16[2,2,1536,512]{3,2,1,0:T(8,128)(2,1)S(1)} custom-call(s32[3]{0:T(128)S(1)} %pad_add_fusion.info, bf16[8,1536,1024]{2,1,0:T(8,128)(2,1)} %refs_2_.6, bf16[8,1536,1024]{2,1,0:T(8,128)(2,1)} %refs_3_.5, bf16[64,1536]{1,0:T(8,128)(2,1)S(1)} %collective-permute-done.refs_2_.refs_1_), custom_call_target="tpu_custom_call" | custom-call | flops 1 | bytes 1 | tf_op jit(solution)/shard_map/stage/pallas_call | solution.py:113
  25.9 4.5 %send_half.4 = (bf16[2,256,512]{2,1,0:T(8,128)(2,1)S(1)}, bf16[256,1536]{1,0:T(8,128)(2,1)S(1)}, bf16[2,2,1536,512]{3,2,1,0:T(8,128)(2,1)S(1)}) custom-call(s32[3]{0:T(128)S(1)} %pad_add_fusion.info, bf16[64,1536]{1,0:T(8,128)(2,1)S(1)} %copy-done.4, bf16[64,1536]{1,0:T(8,128)(2,1)S(1)} %collective-permute-done.refs_2_.refs_1_, ...), custom_call_target="tpu_custom_call" | custom-call | flops 1 | bytes 1 | tf_op jit(solution)/shard_map/send_half/pallas_call | solution.py:113
  30.4 4.3 %keep_half.4 = (bf16[2,256,512]{2,1,0:T(8,128)(2,1)S(1)}, bf16[2,2,1536,512]{3,2,1,0:T(8,128)(2,1)S(1)}) custom-call(s32[3]{0:T(128)S(1)} %pad_add_fusion.info, bf16[256,1536]{1,0:T(8,128)(2,1)S(1)} %get-tuple-element.46.refs_0_, bf16[2,2,1536,512]{3,2,1,0:T(8,128)(2,1)S(1)} %stage.3.refs_9_.refs_1_, bf16[8,1536,1024]{2,1,0:T(8,128)(2,1)} %refs_2_.6, ...), custom_call_target="tpu_custom_call" | custom-call | flops 1 | bytes 1 | tf_op jit(solution)/shard_map/keep_half/pallas_call | solution.py:113
  35.0 1.8 %collective-permute-start.9 = (bf16[1,256,512]{2,1,0:T(8,128)(2,1)S(1)}, bf16[1,256,512]{2,1,0:T(8,128)(2,1)S(1)}, u32[]{:S(2)}, u32[]{:S(2)}) collective-permute-start(bf16[1,256,512]{2,1,0:T(8,128)(2,1)S(1)} %slice.189.refs_9_), channel_id=1, source_target_pairs={{0,2},{1,3},{2,0},{3,1},{4,6},{5,7},{6,4},{7,5},{8,10},{9,11},{10,... | collective-permute-start | bytes 786440 | tf_op jit(solution)/shard_map/ppermute | solution.py:23
  36.8 4.5 %send_half.5 = (bf16[2,256,512]{2,1,0:T(8,128)(2,1)S(1)}, bf16[256,1536]{1,0:T(8,128)(2,1)S(1)}, bf16[2,2,1536,512]{3,2,1,0:T(8,128)(2,1)S(1)}) custom-call(s32[3]{0:T(128)S(1)} %pad_add_fusion.info, bf16[64,1536]{1,0:T(8,128)(2,1)S(1)} %copy-done.4, bf16[64,1536]{1,0:T(8,128)(2,1)S(1)} %collective-permute-done.refs_2_.refs_1_, ...), custom_call_target="tpu_custom_call" | custom-call | flops 1 | bytes 1 | tf_op jit(solution)/shard_map/send_half/pallas_call | solution.py:113
  41.4 4.2 %keep_half.5 = (bf16[2,256,512]{2,1,0:T(8,128)(2,1)S(1)}, bf16[2,2,1536,512]{3,2,1,0:T(8,128)(2,1)S(1)}) custom-call(s32[3]{0:T(128)S(1)} %pad_add_fusion.info, bf16[256,1536]{1,0:T(8,128)(2,1)S(1)} %get-tuple-element.50.refs_0_, bf16[2,2,1536,512]{3,2,1,0:T(8,128)(2,1)S(1)} %get-tuple-element.51.refs_1_, bf16[8,1536,1024]{2,1,0:T(8,128)(2,1)} %refs_2_.6, ...), custom_call_target="tpu_custom_call" | custom-call | flops 1 | bytes 1 | tf_op jit(solution)/shard_map/keep_half/pallas_call | solution.py:113
  46.4 4.5 %send_half.6 = (bf16[2,256,512]{2,1,0:T(8,128)(2,1)S(1)}, bf16[256,1536]{1,0:T(8,128)(2,1)S(1)}, bf16[2,2,1536,512]{3,2,1,0:T(8,128)(2,1)S(1)}) custom-call(s32[3]{0:T(128)S(1)} %pad_add_fusion.info, bf16[64,1536]{1,0:T(8,128)(2,1)S(1)} %copy-done.4, bf16[64,1536]{1,0:T(8,128)(2,1)S(1)} %collective-permute-done.refs_2_.refs_1_, ...), custom_call_target="tpu_custom_call" | custom-call | flops 1 | bytes 1 | tf_op jit(solution)/shard_map/send_half/pallas_call | solution.py:113
  51.1 4.2 %keep_half.6 = (bf16[2,256,512]{2,1,0:T(8,128)(2,1)S(1)}, bf16[2,2,1536,512]{3,2,1,0:T(8,128)(2,1)S(1)}) custom-call(s32[3]{0:T(128)S(1)} %pad_add_fusion.info, bf16[256,1536]{1,0:T(8,128)(2,1)S(1)} %get-tuple-element.55.refs_0_, bf16[2,2,1536,512]{3,2,1,0:T(8,128)(2,1)S(1)} %get-tuple-element.56.refs_1_, bf16[8,1536,1024]{2,1,0:T(8,128)(2,1)} %refs_2_.6, ...), custom_call_target="tpu_custom_call" | custom-call | flops 1 | bytes 1 | tf_op jit(solution)/shard_map/keep_half/pallas_call | solution.py:113
  55.4 2.2 %collective-permute-done.11.refs_1_ = bf16[1,256,768]{2,1,0:T(8,128)(2,1)S(1)} collective-permute-done((bf16[1,256,768]{2,1,0:T(8,128)(2,1)S(1)}, bf16[1,256,768]{2,1,0:T(8,128)(2,1)S(1)}, u32[]{:S(2)}, u32[]{:S(2)}) %collective-permute-start.11) | collective-permute-done | bytes 393248 | tf_op jit(solution)/shard_map/ppermute | solution.py:23
  58.4 4.7 %send_half.7 = (bf16[2,256,512]{2,1,0:T(8,128)(2,1)S(1)}, bf16[256,1536]{1,0:T(8,128)(2,1)S(1)}, bf16[2,1024,1536]{2,1,0:T(8,128)(2,1)S(1)}) custom-call(s32[3]{0:T(128)S(1)} %pad_add_fusion.info, bf16[64,1536]{1,0:T(8,128)(2,1)S(1)} %copy-done.4, bf16[64,1536]{1,0:T(8,128)(2,1)S(1)} %copy-done.1, bf16[64,1536]{1,0:T(8,128)(2,1)S(1)} %copy-done.3, ...), custom_call_target="tpu_custom_call" | custom-call | flops 1 | bytes 1 | tf_op jit(solution)/shard_map/send_half/pallas_call | solution.py:113
  63.1 3.6 %keep_half.7 = (bf16[2,256,512]{2,1,0:T(8,128)(2,1)S(1)}, bf16[2,1024,1536]{2,1,0:T(8,128)(2,1)S(1)}) custom-call(s32[3]{0:T(128)S(1)} %pad_add_fusion.info, bf16[256,1536]{1,0:T(8,128)(2,1)S(1)} %get-tuple-element.59.refs_0_, bf16[2,2,1536,512]{3,2,1,0:T(8,128)(2,1)S(1)} %get-tuple-element.60.refs_1_, bf16[8,1024,1536]{2,1,0:T(8,128)(2,1)} %refs_7_.9), custom_call_target="tpu_custom_call" | custom-call | flops 1 | bytes 1 | tf_op jit(solution)/shard_map/keep_half/pallas_call | solution.py:113
  66.8 1.9 %collective-permute-done.13.refs_1_ = bf16[1,256,768]{2,1,0:T(8,128)(2,1)S(1)} collective-permute-done((bf16[1,256,768]{2,1,0:T(8,128)(2,1)S(1)}, bf16[1,256,768]{2,1,0:T(8,128)(2,1)S(1)}, u32[]{:S(2)}, u32[]{:S(2)}) %collective-permute-start.13) | collective-permute-done | bytes 393248 | tf_op jit(solution)/shard_map/ppermute | solution.py:23
  70.2 0.9 collective-permute-done.16.refs_2_
  71.2 3.4 %down.4 = (f32[256,1536]{1,0:T(8,128)S(1)}, bf16[2,1024,1536]{2,1,0:T(8,128)(2,1)S(1)}) custom-call(s32[3]{0:T(128)S(1)} %pad_add_fusion.info, bf16[1,256,256]{2,1,0:T(8,128)(2,1)S(1)} %fusion.3.refs_0_, bf16[1,256,768]{2,1,0:T(8,128)(2,1)S(1)} %copy-done.6, bf16[2,256,256]{2,1,0:T(8,128)(2,1)S(1)} %collective-permute-done.16.refs_2_, ...), custom_call_target="tpu_custom_call" | custom-call | flops 1 | bytes 1 | tf_op jit(solution)/shard_map/down/pallas_call | solution.py:113
  74.6 3.5 %down.5 = (f32[256,1536]{1,0:T(8,128)S(1)}, bf16[2,1024,1536]{2,1,0:T(8,128)(2,1)S(1)}) custom-call(s32[3]{0:T(128)S(1)} %pad_add_fusion.info, bf16[1,256,256]{2,1,0:T(8,128)(2,1)S(1)} %fusion.2.refs_0_, bf16[1,256,768]{2,1,0:T(8,128)(2,1)S(1)} %collective-permute-done.13.refs_1_, bf16[2,256,256]{2,1,0:T(8,128)(2,1)S(1)} %collective-permute-done.15.refs_2_, ...), custom_call_target="tpu_custom_call" | custom-call | flops 1 | bytes 1 | tf_op jit(solution)/shard_map/down/pallas_call | solution.py:113
  79.3 1.6 %collective-permute-start.17 = (bf16[1,256,256]{2,1,0:T(8,128)(2,1)S(1)}, bf16[1,256,256]{2,1,0:T(8,128)(2,1)S(1)}, u32[]{:S(2)}, u32[]{:S(2)}) collective-permute-start(bf16[1,256,256]{2,1,0:T(8,128)(2,1)S(1)} %fusion.refs_7_.refs_0_), channel_id=1, source_target_pairs={{0,2},{1,3},{2,0},{3,1},{4,6},{5,7},{6,4},{7,5},{8,10},{9,11},{10,... | collective-permute-start | bytes 393224 | tf_op jit(solution)/shard_map/ppermute | solution.py:23
  80.9 2.3 %down.6.refs_6_ = f32[256,1536]{1,0:T(8,128)S(1)} custom-call(s32[3]{0:T(128)S(1)} %pad_add_fusion.info, bf16[1,256,256]{2,1,0:T(8,128)(2,1)S(1)} %fusion.1.refs_0_, bf16[1,256,768]{2,1,0:T(8,128)(2,1)S(1)} %collective-permute-done.14.refs_1_, bf16[2,256,256]{2,1,0:T(8,128)(2,1)S(1)} %collective-permute-done.18.refs_2_, ...), custom_call_target="tpu_custom_call" | custom-call | flops 1 | bytes 1 | tf_op jit(solution)/shard_map/down/pallas_call | solution.py:113
  83.1 2.1 %collective-permute-done.17.refs_1_ = bf16[1,256,256]{2,1,0:T(8,128)(2,1)S(1)} collective-permute-done((bf16[1,256,256]{2,1,0:T(8,128)(2,1)S(1)}, bf16[1,256,256]{2,1,0:T(8,128)(2,1)S(1)}, u32[]{:S(2)}, u32[]{:S(2)}) %collective-permute-start.17) | collective-permute-done | bytes 131104 | tf_op jit(solution)/shard_map/ppermute | solution.py:23
  85.3 1.5 %collective-permute-done.19.refs_2_ = bf16[2,256,256]{2,1,0:T(8,128)(2,1)S(1)} collective-permute-done((bf16[2,256,256]{2,1,0:T(8,128)(2,1)S(1)}, bf16[2,256,256]{2,1,0:T(8,128)(2,1)S(1)}, u32[]{:S(2)}, u32[]{:S(2)}) %collective-permute-start.19) | collective-permute-done | bytes 262176 | tf_op jit(solution)/shard_map/ppermute | solution.py:23
  86.9 2.3 %down.7 = (bf16[64,1536]{1,0:T(8,128)(2,1)S(1)}, bf16[64,1536]{1,0:T(8,128)(2,1)S(1)}, bf16[64,1536]{1,0:T(8,128)(2,1)S(1)}, bf16[32,1536]{1,0:T(8,128)(2,1)S(1)}, bf16[32,1536]{1,0:T(8,128)(2,1)S(1)}) custom-call(s32[3]{0:T(128)S(1)} %pad_add_fusion.info, bf16[1,256,256]{2,1,0:T(8,128)(2,1)S(1)} %fusion.refs_7_.refs_0_, ...), custom_call_target="tpu_custom_call" | custom-call | flops 1 | bytes 1 | tf_op jit(solution)/shard_map/down/pallas_call | solution.py:113
  89.1 2.3 %collective-permute-start.20 = (bf16[32,1536]{1,0:T(8,128)(2,1)S(1)}, bf16[32,1536]{1,0:T(8,128)(2,1)S(1)}, u32[]{:S(2)}, u32[]{:S(2)}) collective-permute-start(bf16[32,1536]{1,0:T(8,128)(2,1)S(1)} %get-tuple-element.74), channel_id=1, source_target_pairs={{0,12},{4,0},{8,4},{12,8},{1,13},{5,1},{9,5},{13,9},{2,14},{6,2},{... | collective-permute-start | bytes 294920 | tf_op jit(solution)/shard_map/ppermute | solution.py:385
  91.5 3.1 %collective-permute-done.20 = bf16[32,1536]{1,0:T(8,128)(2,1)S(1)} collective-permute-done((bf16[32,1536]{1,0:T(8,128)(2,1)S(1)}, bf16[32,1536]{1,0:T(8,128)(2,1)S(1)}, u32[]{:S(2)}, u32[]{:S(2)}) %collective-permute-start.20) | collective-permute-done | bytes 98336 | tf_op jit(solution)/shard_map/ppermute | solution.py:385
  94.6 4.3 %collective-permute-start.21 = (bf16[64,1536]{1,0:T(8,128)(2,1)S(1)}, bf16[64,1536]{1,0:T(8,128)(2,1)S(1)}, u32[]{:S(2)}, u32[]{:S(2)}) collective-permute-start(bf16[64,1536]{1,0:T(8,128)(2,1)S(1)} %pad_maximum_fusion.7), channel_id=1, source_target_pairs={{0,12},{4,0},{8,4},{12,8},{1,13},{5,1},{9,5},{13,9},{2,14},{6,2},{... | collective-permute-start | bytes 589832 | tf_op jit(solution)/shard_map/ppermute | solution.py:394
  99.1 4.9 %collective-permute-done.21 = bf16[64,1536]{1,0:T(8,128)(2,1)S(1)} collective-permute-done((bf16[64,1536]{1,0:T(8,128)(2,1)S(1)}, bf16[64,1536]{1,0:T(8,128)(2,1)S(1)}, u32[]{:S(2)}, u32[]{:S(2)}) %collective-permute-start.21) | collective-permute-done | bytes 196640 | tf_op jit(solution)/shard_map/ppermute | solution.py:394
  104.0 2.9 %collective-permute-done.23 = bf16[64,1536]{1,0:T(8,128)(2,1)S(1)} collective-permute-done((bf16[64,1536]{1,0:T(8,128)(2,1)S(1)}, bf16[64,1536]{1,0:T(8,128)(2,1)S(1)}, u32[]{:S(2)}, u32[]{:S(2)}) %collective-permute-start.23) | collective-permute-done | bytes 196640 | tf_op jit(solution)/shard_map/ppermute | solution.py:395
  (87 shorter events, 7.5 us)
Async XLA Ops:
  0.0 17.7 %collective-permute-start = (bf16[64,1536]{1,0:T(8,128)(2,1)}, bf16[64,1536]{1,0:T(8,128)(2,1)S(1)}, u32[]{:S(2)}, u32[]{:S(2)}) collective-permute-start(bf16[64,1536]{1,0:T(8,128)(2,1)} %refs_0_.11), channel_id=1, source_target_pairs={{0,4},{4,8},{8,12},{12,0},{1,5},{5,9},{9,13},{13,1},{2,6},{6,10},{... | collective-permute-start | bytes 589832 | tf_op jit(solution)/shard_map/ppermute | solution.py:365
  3.0 14.7 %collective-permute-start.1 = (bf16[64,1536]{1,0:T(8,128)(2,1)}, bf16[64,1536]{1,0:T(8,128)(2,1)S(1)}, u32[]{:S(2)}, u32[]{:S(2)}) collective-permute-start(bf16[64,1536]{1,0:T(8,128)(2,1)} %refs_0_.11), channel_id=1, source_target_pairs={{0,12},{4,0},{8,4},{12,8},{1,13},{5,1},{9,5},{13,9},{2,14},{6,2},{... | collective-permute-start | bytes 589832 | tf_op jit(solution)/shard_map/ppermute | solution.py:365
  9.3 5.5 %collective-permute-start.2 = (f32[16,64]{1,0:T(8,128)S(1)}, f32[16,64]{1,0:T(8,128)S(1)}, u32[]{:S(2)}, u32[]{:S(2)}) collective-permute-start(f32[16,64]{1,0:T(8,128)S(1)} %pad_maximum_fusion.9.refs_0_), channel_id=1, source_target_pairs={{0,4},{4,8},{8,12},{12,0},{1,5},{5,9},{9,13},{13,1},{2,6},{6,10},{... | collective-permute-start | bytes 12296 | tf_op jit(solution)/shard_map/ppermute | solution.py:303
  9.3 5.5 %collective-permute-start.3 = (f32[16,64]{1,0:T(8,128)S(1)}, f32[16,64]{1,0:T(8,128)S(1)}, u32[]{:S(2)}, u32[]{:S(2)}) collective-permute-start(f32[16,64]{1,0:T(8,128)S(1)} %pad_maximum_fusion.9.refs_0_), channel_id=1, source_target_pairs={{0,12},{4,0},{8,4},{12,8},{1,13},{5,1},{9,5},{13,9},{2,14},{6,2},{... | collective-permute-start | bytes 12296 | tf_op jit(solution)/shard_map/ppermute | solution.py:303
  13.1 4.5 %collective-permute-start.4 = (f32[16,64]{1,0:T(8,128)S(1)}, f32[16,64]{1,0:T(8,128)S(1)}, u32[]{:S(2)}, u32[]{:S(2)}) collective-permute-start(f32[16,64]{1,0:T(8,128)S(1)} %pad_maximum_fusion.9.refs_0_), channel_id=1, source_target_pairs={{0,8},{4,12},{8,0},{12,4},{1,9},{5,13},{9,1},{13,5},{2,10},{6,14},... | collective-permute-start | bytes 12296 | tf_op jit(solution)/shard_map/ppermute | solution.py:303
  17.7 28.7 %copy-start = (bf16[64,1536]{1,0:T(8,128)(2,1)}, bf16[64,1536]{1,0:T(8,128)(2,1)S(1)}, u32[]{:S(2)}) copy-start(bf16[64,1536]{1,0:T(8,128)(2,1)S(1)} %collective-permute-done.refs_2_.refs_1_) | copy-start | bytes 589828
  17.7 28.7 %copy-start.2 = (bf16[64,1536]{1,0:T(8,128)(2,1)}, bf16[64,1536]{1,0:T(8,128)(2,1)S(1)}, u32[]{:S(2)}) copy-start(bf16[64,1536]{1,0:T(8,128)(2,1)S(1)} %collective-permute-done.1.refs_2_) | copy-start | bytes 589828
  17.7 8.1 %collective-permute-start.5 = (bf16[32,1536]{1,0:T(8,128)(2,1)S(1)}, bf16[32,1536]{1,0:T(8,128)(2,1)S(1)}, u32[]{:S(2)}, u32[]{:S(2)}) collective-permute-start(bf16[32,1536]{1,0:T(8,128)(2,1)S(1)} %slice.104), channel_id=1, source_target_pairs={{0,4},{4,8},{8,12},{12,0},{1,5},{5,9},{9,13},{13,1},{2,6},{6,10},{... | collective-permute-start | bytes 294920 | tf_op jit(solution)/shard_map/ppermute | solution.py:371
  17.8 8.0 %collective-permute-start.6 = (bf16[32,1536]{1,0:T(8,128)(2,1)S(1)}, bf16[32,1536]{1,0:T(8,128)(2,1)S(1)}, u32[]{:S(2)}, u32[]{:S(2)}) collective-permute-start(bf16[32,1536]{1,0:T(8,128)(2,1)S(1)} %slice.105), channel_id=1, source_target_pairs={{0,12},{4,0},{8,4},{12,8},{1,13},{5,1},{9,5},{13,9},{2,14},{6,2},{... | collective-permute-start | bytes 294920 | tf_op jit(solution)/shard_map/ppermute | solution.py:371
  22.4 3.5 %copy-start.4 = (bf16[64,1536]{1,0:T(8,128)(2,1)S(1)}, bf16[64,1536]{1,0:T(8,128)(2,1)}, u32[]{:S(2)}) copy-start(bf16[64,1536]{1,0:T(8,128)(2,1)} %refs_0_.11) | copy-start | bytes 589828
  30.3 4.4 %collective-permute-start.7 = (bf16[2,256,512]{2,1,0:T(8,128)(2,1)S(1)}, bf16[2,256,512]{2,1,0:T(8,128)(2,1)S(1)}, u32[]{:S(2)}, u32[]{:S(2)}) collective-permute-start(bf16[2,256,512]{2,1,0:T(8,128)(2,1)S(1)} %get-tuple-element.48), channel_id=1, source_target_pairs={{0,1},{1,0},{2,3},{3,2},{4,5},{5,4},{6,7},{7,6},{8,9},{9,8},{10,11... | collective-permute-start | bytes 1572872 | tf_op jit(solution)/shard_map/ppermute | solution.py:23
  35.0 10.6 %collective-permute-start.9 = (bf16[1,256,512]{2,1,0:T(8,128)(2,1)S(1)}, bf16[1,256,512]{2,1,0:T(8,128)(2,1)S(1)}, u32[]{:S(2)}, u32[]{:S(2)}) collective-permute-start(bf16[1,256,512]{2,1,0:T(8,128)(2,1)S(1)} %slice.189.refs_9_), channel_id=1, source_target_pairs={{0,2},{1,3},{2,0},{3,1},{4,6},{5,7},{6,4},{7,5},{8,10},{9,11},{10,... | collective-permute-start | bytes 786440 | tf_op jit(solution)/shard_map/ppermute | solution.py:23
  41.3 4.5 %collective-permute-start.8 = (bf16[2,256,512]{2,1,0:T(8,128)(2,1)S(1)}, bf16[2,256,512]{2,1,0:T(8,128)(2,1)S(1)}, u32[]{:S(2)}, u32[]{:S(2)}) collective-permute-start(bf16[2,256,512]{2,1,0:T(8,128)(2,1)S(1)} %get-tuple-element.53), channel_id=1, source_target_pairs={{0,1},{1,0},{2,3},{3,2},{4,5},{5,4},{6,7},{7,6},{8,9},{9,8},{10,11... | collective-permute-start | bytes 1572872 | tf_op jit(solution)/shard_map/ppermute | solution.py:23
  46.0 11.5 %collective-permute-start.11 = (bf16[1,256,768]{2,1,0:T(8,128)(2,1)S(1)}, bf16[1,256,768]{2,1,0:T(8,128)(2,1)S(1)}, u32[]{:S(2)}, u32[]{:S(2)}) collective-permute-start(bf16[1,256,768]{2,1,0:T(8,128)(2,1)S(1)} %pad_maximum_fusion.refs_9_), channel_id=1, source_target_pairs={{0,2},{1,3},{2,0},{3,1},{4,6},{5,7},{6,4},{7,5},{8,10},{9,11},{10,... | collective-permute-start | bytes 1179656 | tf_op jit(solution)/shard_map/ppermute | solution.py:23
  50.9 6.8 %collective-permute-start.10 = (bf16[2,256,512]{2,1,0:T(8,128)(2,1)S(1)}, bf16[2,256,512]{2,1,0:T(8,128)(2,1)S(1)}, u32[]{:S(2)}, u32[]{:S(2)}) collective-permute-start(bf16[2,256,512]{2,1,0:T(8,128)(2,1)S(1)} %get-tuple-element.58), channel_id=1, source_target_pairs={{0,1},{1,0},{2,3},{3,2},{4,5},{5,4},{6,7},{7,6},{8,9},{9,8},{10,11... | collective-permute-start | bytes 1572872 | tf_op jit(solution)/shard_map/ppermute | solution.py:23
  51.1 7.2 %copy-start.1 = (bf16[64,1536]{1,0:T(8,128)(2,1)S(1)}, bf16[64,1536]{1,0:T(8,128)(2,1)}, u32[]{:S(2)}) copy-start(bf16[64,1536]{1,0:T(8,128)(2,1)} %copy-done) | copy-start | bytes 589828
  51.1 7.2 %copy-start.3 = (bf16[64,1536]{1,0:T(8,128)(2,1)S(1)}, bf16[64,1536]{1,0:T(8,128)(2,1)}, u32[]{:S(2)}) copy-start(bf16[64,1536]{1,0:T(8,128)(2,1)} %copy-done.2) | copy-start | bytes 589828
  57.6 5.5 %copy-start.5 = (bf16[1,256,768]{2,1,0:T(8,128)(2,1)}, bf16[1,256,768]{2,1,0:T(8,128)(2,1)S(1)}, u32[]{:S(2)}) copy-start(bf16[1,256,768]{2,1,0:T(8,128)(2,1)S(1)} %collective-permute-done.11.refs_1_) | copy-start | bytes 1179652
  58.0 10.7 %collective-permute-start.13 = (bf16[1,256,768]{2,1,0:T(8,128)(2,1)S(1)}, bf16[1,256,768]{2,1,0:T(8,128)(2,1)S(1)}, u32[]{:S(2)}, u32[]{:S(2)}) collective-permute-start(bf16[1,256,768]{2,1,0:T(8,128)(2,1)S(1)} %pad_maximum_fusion.1.refs_8_), channel_id=1, source_target_pairs={{0,2},{1,3},{2,0},{3,1},{4,6},{5,7},{6,4},{7,5},{8,10},{9,11},{10,... | collective-permute-start | bytes 1179656 | tf_op jit(solution)/shard_map/ppermute | solution.py:23
  63.0 5.9 %collective-permute-start.12 = (bf16[2,256,512]{2,1,0:T(8,128)(2,1)S(1)}, bf16[2,256,512]{2,1,0:T(8,128)(2,1)S(1)}, u32[]{:S(2)}, u32[]{:S(2)}) collective-permute-start(bf16[2,256,512]{2,1,0:T(8,128)(2,1)S(1)} %get-tuple-element.62), channel_id=1, source_target_pairs={{0,1},{1,0},{2,3},{3,2},{4,5},{5,4},{6,7},{7,6},{8,9},{9,8},{10,11... | collective-permute-start | bytes 1572872 | tf_op jit(solution)/shard_map/ppermute | solution.py:23
  63.1 6.4 %slice-start = ((bf16[1,256,768]{2,1,0:T(8,128)(2,1)}), bf16[1,256,256]{2,1,0:T(8,128)(2,1)S(1)}, s32[]{:S(2)}) async-start(bf16[1,256,768]{2,1,0:T(8,128)(2,1)} %copy-done.5), calls=%async_computation | async-start | bytes 262144 | tf_op jit(solution)/shard_map/slice | solution.py:267
  66.8 4.4 %copy-start.6 = (bf16[1,256,768]{2,1,0:T(8,128)(2,1)S(1)}, bf16[1,256,768]{2,1,0:T(8,128)(2,1)}, u32[]{:S(2)}) copy-start(bf16[1,256,768]{2,1,0:T(8,128)(2,1)} %copy-done.5) | copy-start | bytes 1179652
  69.1 9.8 %collective-permute-start.14 = (bf16[1,256,768]{2,1,0:T(8,128)(2,1)S(1)}, bf16[1,256,768]{2,1,0:T(8,128)(2,1)S(1)}, u32[]{:S(2)}, u32[]{:S(2)}) collective-permute-start(bf16[1,256,768]{2,1,0:T(8,128)(2,1)S(1)} %pad_maximum_fusion.2.refs_7_), channel_id=1, source_target_pairs={{0,2},{1,3},{2,0},{3,1},{4,6},{5,7},{6,4},{7,5},{8,10},{9,11},{10,... | collective-permute-start | bytes 1179656 | tf_op jit(solution)/shard_map/ppermute | solution.py:23
  69.5 1.6 %collective-permute-start.16 = (bf16[2,256,256]{2,1,0:T(8,128)(2,1)S(1)}, bf16[2,256,256]{2,1,0:T(8,128)(2,1)S(1)}, u32[]{:S(2)}, u32[]{:S(2)}) collective-permute-start(bf16[2,256,256]{2,1,0:T(8,128)(2,1)S(1)} %pad_maximum_fusion.4), channel_id=1, source_target_pairs={{0,1},{1,0},{2,3},{3,2},{4,5},{5,4},{6,7},{7,6},{8,9},{9,8},{10,11... | collective-permute-start | bytes 786440 | tf_op jit(solution)/shard_map/ppermute | solution.py:23
  69.7 4.9 %collective-permute-start.15 = (bf16[2,256,256]{2,1,0:T(8,128)(2,1)S(1)}, bf16[2,256,256]{2,1,0:T(8,128)(2,1)S(1)}, u32[]{:S(2)}, u32[]{:S(2)}) collective-permute-start(bf16[2,256,256]{2,1,0:T(8,128)(2,1)S(1)} %pad_maximum_fusion.3), channel_id=1, source_target_pairs={{0,1},{1,0},{2,3},{3,2},{4,5},{5,4},{6,7},{7,6},{8,9},{9,8},{10,11... | collective-permute-start | bytes 786440 | tf_op jit(solution)/shard_map/ppermute | solution.py:23
  79.0 1.9 %collective-permute-start.18 = (bf16[2,256,256]{2,1,0:T(8,128)(2,1)S(1)}, bf16[2,256,256]{2,1,0:T(8,128)(2,1)S(1)}, u32[]{:S(2)}, u32[]{:S(2)}) collective-permute-start(bf16[2,256,256]{2,1,0:T(8,128)(2,1)S(1)} %pad_maximum_fusion.5), channel_id=1, source_target_pairs={{0,1},{1,0},{2,3},{3,2},{4,5},{5,4},{6,7},{7,6},{8,9},{9,8},{10,11... | collective-permute-start | bytes 786440 | tf_op jit(solution)/shard_map/ppermute | solution.py:23
  79.3 6.0 %collective-permute-start.17 = (bf16[1,256,256]{2,1,0:T(8,128)(2,1)S(1)}, bf16[1,256,256]{2,1,0:T(8,128)(2,1)S(1)}, u32[]{:S(2)}, u32[]{:S(2)}) collective-permute-start(bf16[1,256,256]{2,1,0:T(8,128)(2,1)S(1)} %fusion.refs_7_.refs_0_), channel_id=1, source_target_pairs={{0,2},{1,3},{2,0},{3,1},{4,6},{5,7},{6,4},{7,5},{8,10},{9,11},{10,... | collective-permute-start | bytes 393224 | tf_op jit(solution)/shard_map/ppermute | solution.py:23
  85.3 1.6 %collective-permute-start.19 = (bf16[2,256,256]{2,1,0:T(8,128)(2,1)S(1)}, bf16[2,256,256]{2,1,0:T(8,128)(2,1)S(1)}, u32[]{:S(2)}, u32[]{:S(2)}) collective-permute-start(bf16[2,256,256]{2,1,0:T(8,128)(2,1)S(1)} %pad_maximum_fusion.6), channel_id=1, source_target_pairs={{0,1},{1,0},{2,3},{3,2},{4,5},{5,4},{6,7},{7,6},{8,9},{9,8},{10,11... | collective-permute-start | bytes 786440 | tf_op jit(solution)/shard_map/ppermute | solution.py:23
  89.1 5.5 %collective-permute-start.20 = (bf16[32,1536]{1,0:T(8,128)(2,1)S(1)}, bf16[32,1536]{1,0:T(8,128)(2,1)S(1)}, u32[]{:S(2)}, u32[]{:S(2)}) collective-permute-start(bf16[32,1536]{1,0:T(8,128)(2,1)S(1)} %get-tuple-element.74), channel_id=1, source_target_pairs={{0,12},{4,0},{8,4},{12,8},{1,13},{5,1},{9,5},{13,9},{2,14},{6,2},{... | collective-permute-start | bytes 294920 | tf_op jit(solution)/shard_map/ppermute | solution.py:385
  91.4 7.6 %collective-permute-start.22 = (bf16[32,1536]{1,0:T(8,128)(2,1)S(1)}, bf16[32,1536]{1,0:T(8,128)(2,1)S(1)}, u32[]{:S(2)}, u32[]{:S(2)}) collective-permute-start(bf16[32,1536]{1,0:T(8,128)(2,1)S(1)} %get-tuple-element.76), channel_id=1, source_target_pairs={{0,4},{4,8},{8,12},{12,0},{1,5},{5,9},{9,13},{13,1},{2,6},{6,10},{... | collective-permute-start | bytes 294920 | tf_op jit(solution)/shard_map/ppermute | solution.py:385
  94.6 9.3 %collective-permute-start.21 = (bf16[64,1536]{1,0:T(8,128)(2,1)S(1)}, bf16[64,1536]{1,0:T(8,128)(2,1)S(1)}, u32[]{:S(2)}, u32[]{:S(2)}) collective-permute-start(bf16[64,1536]{1,0:T(8,128)(2,1)S(1)} %pad_maximum_fusion.7), channel_id=1, source_target_pairs={{0,12},{4,0},{8,4},{12,8},{1,13},{5,1},{9,5},{13,9},{2,14},{6,2},{... | collective-permute-start | bytes 589832 | tf_op jit(solution)/shard_map/ppermute | solution.py:394
  99.0 7.8 %collective-permute-start.23 = (bf16[64,1536]{1,0:T(8,128)(2,1)S(1)}, bf16[64,1536]{1,0:T(8,128)(2,1)S(1)}, u32[]{:S(2)}, u32[]{:S(2)}) collective-permute-start(bf16[64,1536]{1,0:T(8,128)(2,1)S(1)} %pad_maximum_fusion.8), channel_id=1, source_target_pairs={{0,4},{4,8},{8,12},{12,0},{1,5},{5,9},{9,13},{13,1},{2,6},{6,10},{... | collective-permute-start | bytes 589832 | tf_op jit(solution)/shard_map/ppermute | solution.py:395
  (1 other events, 3.4 us)

commit v8 on v7

--- a/solution.py
+++ b/solution.py
@@ -106,7 +106,7 @@
         if ahead is not None:
             on = set_copies(ahead, far, info, results[-1], rest[-1])
             rest = rest[:-1]
-        body(info, own, results[:n_out], rest, lambda: [copy.start() for copy in on])
+        body(info, own, results[:n_out], rest, lambda: [copy.start(priority=i % 2) for i, copy in enumerate(on)])
         for copy in on:
             copy.wait()
 

time: 108 us -> 108 us (level)
  no operation moved by 1% of the time
where the time goes in v8:
time: 108 us
  Pallas kernels  53.2 us (49%)
  waiting for transfers between devices  25.5 us (24%)
  starting transfers between devices  25.1 us (23%)
  other arithmetic  2.98 us (3%)
    pallas_call x14, Pallas kernels, call(): pl.pallas_call(whole, out_shape=tuple(outs), in_specs=[SMEM] + [spec for...  52.5 us
    ppermute x13, waiting for transfers between devices, flip(): lax.ppermute(x, axis, [(i, i ^ k) for i in range(lax.axis_size(axis))])  10 us
    ppermute x13, starting transfers between devices, flip(): lax.ppermute(x, axis, [(i, i ^ k) for i in range(lax.axis_size(axis))])  5.56 us
    ppermute x1, waiting for transfers between devices, returned(): low = lax.ppermute(a.astype(jnp.bfloat16), axis, down_)  4.89 us
    ppermute x3, waiting for transfers between devices, on_device(): lax.ppermute(meta, 'expert', [(i, (i - k) % n_owner) for i in range(n_own...  4.55 us
    ppermute x1, starting transfers between devices, returned(): low = lax.ppermute(a.astype(jnp.bfloat16), axis, down_)  4.33 us
    ppermute x3, starting transfers between devices, on_device(): lax.ppermute(meta, 'expert', [(i, (i - k) % n_owner) for i in range(n_own...  3.87 us
    ppermute x1, starting transfers between devices, gathered(): lax.ppermute(above[half:], axis, down_)  3.85 us
  transfers between devices with their start and end apart: 24, of which 11 were waited for; matrix products, arithmetic and copies ran while one was open for 1% of the time, Pallas kernels for 43%

profile of v8, /device:TPU:0, one launch (start us, length us, event | category | flops | bytes accessed | tf_op | source)
XLA Modules:
  0.0 107.6 jit_solution(2315117765077745081)
XLA Ops:
  0.0 3.0 %collective-permute-start = (bf16[64,1536]{1,0:T(8,128)(2,1)}, bf16[64,1536]{1,0:T(8,128)(2,1)S(1)}, u32[]{:S(2)}, u32[]{:S(2)}) collective-permute-start(bf16[64,1536]{1,0:T(8,128)(2,1)} %refs_0_.11), channel_id=1, source_target_pairs={{0,4},{4,8},{8,12},{12,0},{1,5},{5,9},{9,13},{13,1},{2,6},{6,10},{... | collective-permute-start | bytes 589832 | tf_op jit(solution)/shard_map/ppermute | solution.py:365
  3.0 2.0 %collective-permute-start.1 = (bf16[64,1536]{1,0:T(8,128)(2,1)}, bf16[64,1536]{1,0:T(8,128)(2,1)S(1)}, u32[]{:S(2)}, u32[]{:S(2)}) collective-permute-start(bf16[64,1536]{1,0:T(8,128)(2,1)} %refs_0_.11), channel_id=1, source_target_pairs={{0,12},{4,0},{8,4},{12,8},{1,13},{5,1},{9,5},{13,9},{2,14},{6,2},{... | collective-permute-start | bytes 589832 | tf_op jit(solution)/shard_map/ppermute | solution.py:365
  5.8 3.4 %stage.2.refs_6_ = bf16[2,2,1536,512]{3,2,1,0:T(8,128)(2,1)S(1)} custom-call(s32[3]{0:T(128)S(1)} %pad_add_fusion.info, bf16[8,1536,1024]{2,1,0:T(8,128)(2,1)} %refs_2_.6, bf16[8,1536,1024]{2,1,0:T(8,128)(2,1)} %refs_3_.5), custom_call_target="tpu_custom_call" | custom-call | flops 1 | bytes 1 | tf_op jit(solution)/shard_map/stage/pallas_call | solution.py:113
  9.3 3.8 %collective-permute-start.3 = (f32[16,64]{1,0:T(8,128)S(1)}, f32[16,64]{1,0:T(8,128)S(1)}, u32[]{:S(2)}, u32[]{:S(2)}) collective-permute-start(f32[16,64]{1,0:T(8,128)S(1)} %pad_maximum_fusion.9.refs_0_), channel_id=1, source_target_pairs={{0,12},{4,0},{8,4},{12,8},{1,13},{5,1},{9,5},{13,9},{2,14},{6,2},{... | collective-permute-start | bytes 12296 | tf_op jit(solution)/shard_map/ppermute | solution.py:303
  13.1 1.7 %collective-permute-done.2.refs_1_ = f32[16,64]{1,0:T(8,128)S(1)} collective-permute-done((f32[16,64]{1,0:T(8,128)S(1)}, f32[16,64]{1,0:T(8,128)S(1)}, u32[]{:S(2)}, u32[]{:S(2)}) %collective-permute-start.2) | collective-permute-done | bytes 4128 | tf_op jit(solution)/shard_map/ppermute | solution.py:303
  14.8 2.9 %collective-permute-done.4.refs_3_ = f32[16,64]{1,0:T(8,128)S(1)} collective-permute-done((f32[16,64]{1,0:T(8,128)S(1)}, f32[16,64]{1,0:T(8,128)S(1)}, u32[]{:S(2)}, u32[]{:S(2)}) %collective-permute-start.4) | collective-permute-done | bytes 4128 | tf_op jit(solution)/shard_map/ppermute | solution.py:303
  17.8 3.9 %collective-permute-start.6 = (bf16[32,1536]{1,0:T(8,128)(2,1)S(1)}, bf16[32,1536]{1,0:T(8,128)(2,1)S(1)}, u32[]{:S(2)}, u32[]{:S(2)}) collective-permute-start(bf16[32,1536]{1,0:T(8,128)(2,1)S(1)} %slice.105), channel_id=1, source_target_pairs={{0,12},{4,0},{8,4},{12,8},{1,13},{5,1},{9,5},{13,9},{2,14},{6,2},{... | collective-permute-start | bytes 294920 | tf_op jit(solution)/shard_map/ppermute | solution.py:371
  22.4 3.4 %stage.3.refs_9_.refs_1_ = bf16[2,2,1536,512]{3,2,1,0:T(8,128)(2,1)S(1)} custom-call(s32[3]{0:T(128)S(1)} %pad_add_fusion.info, bf16[8,1536,1024]{2,1,0:T(8,128)(2,1)} %refs_2_.6, bf16[8,1536,1024]{2,1,0:T(8,128)(2,1)} %refs_3_.5, bf16[64,1536]{1,0:T(8,128)(2,1)S(1)} %collective-permute-done.refs_2_.refs_1_), custom_call_target="tpu_custom_call" | custom-call | flops 1 | bytes 1 | tf_op jit(solution)/shard_map/stage/pallas_call | solution.py:113
  25.9 4.5 %send_half.4 = (bf16[2,256,512]{2,1,0:T(8,128)(2,1)S(1)}, bf16[256,1536]{1,0:T(8,128)(2,1)S(1)}, bf16[2,2,1536,512]{3,2,1,0:T(8,128)(2,1)S(1)}) custom-call(s32[3]{0:T(128)S(1)} %pad_add_fusion.info, bf16[64,1536]{1,0:T(8,128)(2,1)S(1)} %copy-done.4, bf16[64,1536]{1,0:T(8,128)(2,1)S(1)} %collective-permute-done.refs_2_.refs_1_, ...), custom_call_target="tpu_custom_call" | custom-call | flops 1 | bytes 1 | tf_op jit(solution)/shard_map/send_half/pallas_call | solution.py:113
  30.4 4.3 %keep_half.4 = (bf16[2,256,512]{2,1,0:T(8,128)(2,1)S(1)}, bf16[2,2,1536,512]{3,2,1,0:T(8,128)(2,1)S(1)}) custom-call(s32[3]{0:T(128)S(1)} %pad_add_fusion.info, bf16[256,1536]{1,0:T(8,128)(2,1)S(1)} %get-tuple-element.46.refs_0_, bf16[2,2,1536,512]{3,2,1,0:T(8,128)(2,1)S(1)} %stage.3.refs_9_.refs_1_, bf16[8,1536,1024]{2,1,0:T(8,128)(2,1)} %refs_2_.6, ...), custom_call_target="tpu_custom_call" | custom-call | flops 1 | bytes 1 | tf_op jit(solution)/shard_map/keep_half/pallas_call | solution.py:113
  35.0 1.8 %collective-permute-start.9 = (bf16[1,256,512]{2,1,0:T(8,128)(2,1)S(1)}, bf16[1,256,512]{2,1,0:T(8,128)(2,1)S(1)}, u32[]{:S(2)}, u32[]{:S(2)}) collective-permute-start(bf16[1,256,512]{2,1,0:T(8,128)(2,1)S(1)} %slice.189.refs_9_), channel_id=1, source_target_pairs={{0,2},{1,3},{2,0},{3,1},{4,6},{5,7},{6,4},{7,5},{8,10},{9,11},{10,... | collective-permute-start | bytes 786440 | tf_op jit(solution)/shard_map/ppermute | solution.py:23
  36.8 4.5 %send_half.5 = (bf16[2,256,512]{2,1,0:T(8,128)(2,1)S(1)}, bf16[256,1536]{1,0:T(8,128)(2,1)S(1)}, bf16[2,2,1536,512]{3,2,1,0:T(8,128)(2,1)S(1)}) custom-call(s32[3]{0:T(128)S(1)} %pad_add_fusion.info, bf16[64,1536]{1,0:T(8,128)(2,1)S(1)} %copy-done.4, bf16[64,1536]{1,0:T(8,128)(2,1)S(1)} %collective-permute-done.refs_2_.refs_1_, ...), custom_call_target="tpu_custom_call" | custom-call | flops 1 | bytes 1 | tf_op jit(solution)/shard_map/send_half/pallas_call | solution.py:113
  41.4 4.2 %keep_half.5 = (bf16[2,256,512]{2,1,0:T(8,128)(2,1)S(1)}, bf16[2,2,1536,512]{3,2,1,0:T(8,128)(2,1)S(1)}) custom-call(s32[3]{0:T(128)S(1)} %pad_add_fusion.info, bf16[256,1536]{1,0:T(8,128)(2,1)S(1)} %get-tuple-element.50.refs_0_, bf16[2,2,1536,512]{3,2,1,0:T(8,128)(2,1)S(1)} %get-tuple-element.51.refs_1_, bf16[8,1536,1024]{2,1,0:T(8,128)(2,1)} %refs_2_.6, ...), custom_call_target="tpu_custom_call" | custom-call | flops 1 | bytes 1 | tf_op jit(solution)/shard_map/keep_half/pallas_call | solution.py:113
  46.4 4.5 %send_half.6 = (bf16[2,256,512]{2,1,0:T(8,128)(2,1)S(1)}, bf16[256,1536]{1,0:T(8,128)(2,1)S(1)}, bf16[2,2,1536,512]{3,2,1,0:T(8,128)(2,1)S(1)}) custom-call(s32[3]{0:T(128)S(1)} %pad_add_fusion.info, bf16[64,1536]{1,0:T(8,128)(2,1)S(1)} %copy-done.4, bf16[64,1536]{1,0:T(8,128)(2,1)S(1)} %collective-permute-done.refs_2_.refs_1_, ...), custom_call_target="tpu_custom_call" | custom-call | flops 1 | bytes 1 | tf_op jit(solution)/shard_map/send_half/pallas_call | solution.py:113
  51.1 4.2 %keep_half.6 = (bf16[2,256,512]{2,1,0:T(8,128)(2,1)S(1)}, bf16[2,2,1536,512]{3,2,1,0:T(8,128)(2,1)S(1)}) custom-call(s32[3]{0:T(128)S(1)} %pad_add_fusion.info, bf16[256,1536]{1,0:T(8,128)(2,1)S(1)} %get-tuple-element.55.refs_0_, bf16[2,2,1536,512]{3,2,1,0:T(8,128)(2,1)S(1)} %get-tuple-element.56.refs_1_, bf16[8,1536,1024]{2,1,0:T(8,128)(2,1)} %refs_2_.6, ...), custom_call_target="tpu_custom_call" | custom-call | flops 1 | bytes 1 | tf_op jit(solution)/shard_map/keep_half/pallas_call | solution.py:113
  55.3 2.2 %collective-permute-done.11.refs_1_ = bf16[1,256,768]{2,1,0:T(8,128)(2,1)S(1)} collective-permute-done((bf16[1,256,768]{2,1,0:T(8,128)(2,1)S(1)}, bf16[1,256,768]{2,1,0:T(8,128)(2,1)S(1)}, u32[]{:S(2)}, u32[]{:S(2)}) %collective-permute-start.11) | collective-permute-done | bytes 393248 | tf_op jit(solution)/shard_map/ppermute | solution.py:23
  58.3 4.6 %send_half.7 = (bf16[2,256,512]{2,1,0:T(8,128)(2,1)S(1)}, bf16[256,1536]{1,0:T(8,128)(2,1)S(1)}, bf16[2,1024,1536]{2,1,0:T(8,128)(2,1)S(1)}) custom-call(s32[3]{0:T(128)S(1)} %pad_add_fusion.info, bf16[64,1536]{1,0:T(8,128)(2,1)S(1)} %copy-done.4, bf16[64,1536]{1,0:T(8,128)(2,1)S(1)} %copy-done.1, bf16[64,1536]{1,0:T(8,128)(2,1)S(1)} %copy-done.3, ...), custom_call_target="tpu_custom_call" | custom-call | flops 1 | bytes 1 | tf_op jit(solution)/shard_map/send_half/pallas_call | solution.py:113
  63.1 3.4 %keep_half.7 = (bf16[2,256,512]{2,1,0:T(8,128)(2,1)S(1)}, bf16[2,1024,1536]{2,1,0:T(8,128)(2,1)S(1)}) custom-call(s32[3]{0:T(128)S(1)} %pad_add_fusion.info, bf16[256,1536]{1,0:T(8,128)(2,1)S(1)} %get-tuple-element.59.refs_0_, bf16[2,2,1536,512]{3,2,1,0:T(8,128)(2,1)S(1)} %get-tuple-element.60.refs_1_, bf16[8,1024,1536]{2,1,0:T(8,128)(2,1)} %refs_7_.9), custom_call_target="tpu_custom_call" | custom-call | flops 1 | bytes 1 | tf_op jit(solution)/shard_map/keep_half/pallas_call | solution.py:113
  66.5 2.1 %collective-permute-done.13.refs_1_ = bf16[1,256,768]{2,1,0:T(8,128)(2,1)S(1)} collective-permute-done((bf16[1,256,768]{2,1,0:T(8,128)(2,1)S(1)}, bf16[1,256,768]{2,1,0:T(8,128)(2,1)S(1)}, u32[]{:S(2)}, u32[]{:S(2)}) %collective-permute-start.13) | collective-permute-done | bytes 393248 | tf_op jit(solution)/shard_map/ppermute | solution.py:23
  71.1 3.4 %down.4 = (f32[256,1536]{1,0:T(8,128)S(1)}, bf16[2,1024,1536]{2,1,0:T(8,128)(2,1)S(1)}) custom-call(s32[3]{0:T(128)S(1)} %pad_add_fusion.info, bf16[1,256,256]{2,1,0:T(8,128)(2,1)S(1)} %fusion.3.refs_0_, bf16[1,256,768]{2,1,0:T(8,128)(2,1)S(1)} %copy-done.6, bf16[2,256,256]{2,1,0:T(8,128)(2,1)S(1)} %collective-permute-done.16.refs_2_, ...), custom_call_target="tpu_custom_call" | custom-call | flops 1 | bytes 1 | tf_op jit(solution)/shard_map/down/pallas_call | solution.py:113
  74.5 3.5 %down.5 = (f32[256,1536]{1,0:T(8,128)S(1)}, bf16[2,1024,1536]{2,1,0:T(8,128)(2,1)S(1)}) custom-call(s32[3]{0:T(128)S(1)} %pad_add_fusion.info, bf16[1,256,256]{2,1,0:T(8,128)(2,1)S(1)} %fusion.2.refs_0_, bf16[1,256,768]{2,1,0:T(8,128)(2,1)S(1)} %collective-permute-done.13.refs_1_, bf16[2,256,256]{2,1,0:T(8,128)(2,1)S(1)} %collective-permute-done.15.refs_2_, ...), custom_call_target="tpu_custom_call" | custom-call | flops 1 | bytes 1 | tf_op jit(solution)/shard_map/down/pallas_call | solution.py:113
  78.0 0.9 collective-permute-done.14.refs_1_
  79.2 1.4 %collective-permute-start.17 = (bf16[1,256,256]{2,1,0:T(8,128)(2,1)S(1)}, bf16[1,256,256]{2,1,0:T(8,128)(2,1)S(1)}, u32[]{:S(2)}, u32[]{:S(2)}) collective-permute-start(bf16[1,256,256]{2,1,0:T(8,128)(2,1)S(1)} %fusion.refs_7_.refs_0_), channel_id=1, source_target_pairs={{0,2},{1,3},{2,0},{3,1},{4,6},{5,7},{6,4},{7,5},{8,10},{9,11},{10,... | collective-permute-start | bytes 393224 | tf_op jit(solution)/shard_map/ppermute | solution.py:23
  80.6 2.3 %down.6.refs_6_ = f32[256,1536]{1,0:T(8,128)S(1)} custom-call(s32[3]{0:T(128)S(1)} %pad_add_fusion.info, bf16[1,256,256]{2,1,0:T(8,128)(2,1)S(1)} %fusion.1.refs_0_, bf16[1,256,768]{2,1,0:T(8,128)(2,1)S(1)} %collective-permute-done.14.refs_1_, bf16[2,256,256]{2,1,0:T(8,128)(2,1)S(1)} %collective-permute-done.18.refs_2_, ...), custom_call_target="tpu_custom_call" | custom-call | flops 1 | bytes 1 | tf_op jit(solution)/shard_map/down/pallas_call | solution.py:113
  82.9 2.3 %collective-permute-done.17.refs_1_ = bf16[1,256,256]{2,1,0:T(8,128)(2,1)S(1)} collective-permute-done((bf16[1,256,256]{2,1,0:T(8,128)(2,1)S(1)}, bf16[1,256,256]{2,1,0:T(8,128)(2,1)S(1)}, u32[]{:S(2)}, u32[]{:S(2)}) %collective-permute-start.17) | collective-permute-done | bytes 131104 | tf_op jit(solution)/shard_map/ppermute | solution.py:23
  85.3 1.5 %collective-permute-done.19.refs_2_ = bf16[2,256,256]{2,1,0:T(8,128)(2,1)S(1)} collective-permute-done((bf16[2,256,256]{2,1,0:T(8,128)(2,1)S(1)}, bf16[2,256,256]{2,1,0:T(8,128)(2,1)S(1)}, u32[]{:S(2)}, u32[]{:S(2)}) %collective-permute-start.19) | collective-permute-done | bytes 262176 | tf_op jit(solution)/shard_map/ppermute | solution.py:23
  86.8 2.3 %down.7 = (bf16[64,1536]{1,0:T(8,128)(2,1)S(1)}, bf16[64,1536]{1,0:T(8,128)(2,1)S(1)}, bf16[64,1536]{1,0:T(8,128)(2,1)S(1)}, bf16[32,1536]{1,0:T(8,128)(2,1)S(1)}, bf16[32,1536]{1,0:T(8,128)(2,1)S(1)}) custom-call(s32[3]{0:T(128)S(1)} %pad_add_fusion.info, bf16[1,256,256]{2,1,0:T(8,128)(2,1)S(1)} %fusion.refs_7_.refs_0_, ...), custom_call_target="tpu_custom_call" | custom-call | flops 1 | bytes 1 | tf_op jit(solution)/shard_map/down/pallas_call | solution.py:113
  89.1 2.3 %collective-permute-start.20 = (bf16[32,1536]{1,0:T(8,128)(2,1)S(1)}, bf16[32,1536]{1,0:T(8,128)(2,1)S(1)}, u32[]{:S(2)}, u32[]{:S(2)}) collective-permute-start(bf16[32,1536]{1,0:T(8,128)(2,1)S(1)} %get-tuple-element.74), channel_id=1, source_target_pairs={{0,12},{4,0},{8,4},{12,8},{1,13},{5,1},{9,5},{13,9},{2,14},{6,2},{... | collective-permute-start | bytes 294920 | tf_op jit(solution)/shard_map/ppermute | solution.py:385
  91.4 3.1 %collective-permute-done.20 = bf16[32,1536]{1,0:T(8,128)(2,1)S(1)} collective-permute-done((bf16[32,1536]{1,0:T(8,128)(2,1)S(1)}, bf16[32,1536]{1,0:T(8,128)(2,1)S(1)}, u32[]{:S(2)}, u32[]{:S(2)}) %collective-permute-start.20) | collective-permute-done | bytes 98336 | tf_op jit(solution)/shard_map/ppermute | solution.py:385
  94.6 4.3 %collective-permute-start.21 = (bf16[64,1536]{1,0:T(8,128)(2,1)S(1)}, bf16[64,1536]{1,0:T(8,128)(2,1)S(1)}, u32[]{:S(2)}, u32[]{:S(2)}) collective-permute-start(bf16[64,1536]{1,0:T(8,128)(2,1)S(1)} %pad_maximum_fusion.7), channel_id=1, source_target_pairs={{0,12},{4,0},{8,4},{12,8},{1,13},{5,1},{9,5},{13,9},{2,14},{6,2},{... | collective-permute-start | bytes 589832 | tf_op jit(solution)/shard_map/ppermute | solution.py:394
  99.1 4.9 %collective-permute-done.21 = bf16[64,1536]{1,0:T(8,128)(2,1)S(1)} collective-permute-done((bf16[64,1536]{1,0:T(8,128)(2,1)S(1)}, bf16[64,1536]{1,0:T(8,128)(2,1)S(1)}, u32[]{:S(2)}, u32[]{:S(2)}) %collective-permute-start.21) | collective-permute-done | bytes 196640 | tf_op jit(solution)/shard_map/ppermute | solution.py:394
  104.0 2.9 %collective-permute-done.23 = bf16[64,1536]{1,0:T(8,128)(2,1)S(1)} collective-permute-done((bf16[64,1536]{1,0:T(8,128)(2,1)S(1)}, bf16[64,1536]{1,0:T(8,128)(2,1)S(1)}, u32[]{:S(2)}, u32[]{:S(2)}) %collective-permute-start.23) | collective-permute-done | bytes 196640 | tf_op jit(solution)/shard_map/ppermute | solution.py:395
  (87 shorter events, 7.5 us)
Async XLA Ops:
  0.0 17.7 %collective-permute-start = (bf16[64,1536]{1,0:T(8,128)(2,1)}, bf16[64,1536]{1,0:T(8,128)(2,1)S(1)}, u32[]{:S(2)}, u32[]{:S(2)}) collective-permute-start(bf16[64,1536]{1,0:T(8,128)(2,1)} %refs_0_.11), channel_id=1, source_target_pairs={{0,4},{4,8},{8,12},{12,0},{1,5},{5,9},{9,13},{13,1},{2,6},{6,10},{... | collective-permute-start | bytes 589832 | tf_op jit(solution)/shard_map/ppermute | solution.py:365
  3.0 14.7 %collective-permute-start.1 = (bf16[64,1536]{1,0:T(8,128)(2,1)}, bf16[64,1536]{1,0:T(8,128)(2,1)S(1)}, u32[]{:S(2)}, u32[]{:S(2)}) collective-permute-start(bf16[64,1536]{1,0:T(8,128)(2,1)} %refs_0_.11), channel_id=1, source_target_pairs={{0,12},{4,0},{8,4},{12,8},{1,13},{5,1},{9,5},{13,9},{2,14},{6,2},{... | collective-permute-start | bytes 589832 | tf_op jit(solution)/shard_map/ppermute | solution.py:365
  9.3 5.6 %collective-permute-start.2 = (f32[16,64]{1,0:T(8,128)S(1)}, f32[16,64]{1,0:T(8,128)S(1)}, u32[]{:S(2)}, u32[]{:S(2)}) collective-permute-start(f32[16,64]{1,0:T(8,128)S(1)} %pad_maximum_fusion.9.refs_0_), channel_id=1, source_target_pairs={{0,4},{4,8},{8,12},{12,0},{1,5},{5,9},{9,13},{13,1},{2,6},{6,10},{... | collective-permute-start | bytes 12296 | tf_op jit(solution)/shard_map/ppermute | solution.py:303
  9.3 5.5 %collective-permute-start.3 = (f32[16,64]{1,0:T(8,128)S(1)}, f32[16,64]{1,0:T(8,128)S(1)}, u32[]{:S(2)}, u32[]{:S(2)}) collective-permute-start(f32[16,64]{1,0:T(8,128)S(1)} %pad_maximum_fusion.9.refs_0_), channel_id=1, source_target_pairs={{0,12},{4,0},{8,4},{12,8},{1,13},{5,1},{9,5},{13,9},{2,14},{6,2},{... | collective-permute-start | bytes 12296 | tf_op jit(solution)/shard_map/ppermute | solution.py:303
  13.1 4.5 %collective-permute-start.4 = (f32[16,64]{1,0:T(8,128)S(1)}, f32[16,64]{1,0:T(8,128)S(1)}, u32[]{:S(2)}, u32[]{:S(2)}) collective-permute-start(f32[16,64]{1,0:T(8,128)S(1)} %pad_maximum_fusion.9.refs_0_), channel_id=1, source_target_pairs={{0,8},{4,12},{8,0},{12,4},{1,9},{5,13},{9,1},{13,5},{2,10},{6,14},... | collective-permute-start | bytes 12296 | tf_op jit(solution)/shard_map/ppermute | solution.py:303
  17.7 28.7 %copy-start = (bf16[64,1536]{1,0:T(8,128)(2,1)}, bf16[64,1536]{1,0:T(8,128)(2,1)S(1)}, u32[]{:S(2)}) copy-start(bf16[64,1536]{1,0:T(8,128)(2,1)S(1)} %collective-permute-done.refs_2_.refs_1_) | copy-start | bytes 589828
  17.7 28.7 %copy-start.2 = (bf16[64,1536]{1,0:T(8,128)(2,1)}, bf16[64,1536]{1,0:T(8,128)(2,1)S(1)}, u32[]{:S(2)}) copy-start(bf16[64,1536]{1,0:T(8,128)(2,1)S(1)} %collective-permute-done.1.refs_2_) | copy-start | bytes 589828
  17.7 8.1 %collective-permute-start.5 = (bf16[32,1536]{1,0:T(8,128)(2,1)S(1)}, bf16[32,1536]{1,0:T(8,128)(2,1)S(1)}, u32[]{:S(2)}, u32[]{:S(2)}) collective-permute-start(bf16[32,1536]{1,0:T(8,128)(2,1)S(1)} %slice.104), channel_id=1, source_target_pairs={{0,4},{4,8},{8,12},{12,0},{1,5},{5,9},{9,13},{13,1},{2,6},{6,10},{... | collective-permute-start | bytes 294920 | tf_op jit(solution)/shard_map/ppermute | solution.py:371
  17.8 8.0 %collective-permute-start.6 = (bf16[32,1536]{1,0:T(8,128)(2,1)S(1)}, bf16[32,1536]{1,0:T(8,128)(2,1)S(1)}, u32[]{:S(2)}, u32[]{:S(2)}) collective-permute-start(bf16[32,1536]{1,0:T(8,128)(2,1)S(1)} %slice.105), channel_id=1, source_target_pairs={{0,12},{4,0},{8,4},{12,8},{1,13},{5,1},{9,5},{13,9},{2,14},{6,2},{... | collective-permute-start | bytes 294920 | tf_op jit(solution)/shard_map/ppermute | solution.py:371
  22.4 3.4 %copy-start.4 = (bf16[64,1536]{1,0:T(8,128)(2,1)S(1)}, bf16[64,1536]{1,0:T(8,128)(2,1)}, u32[]{:S(2)}) copy-start(bf16[64,1536]{1,0:T(8,128)(2,1)} %refs_0_.11) | copy-start | bytes 589828
  30.3 4.4 %collective-permute-start.7 = (bf16[2,256,512]{2,1,0:T(8,128)(2,1)S(1)}, bf16[2,256,512]{2,1,0:T(8,128)(2,1)S(1)}, u32[]{:S(2)}, u32[]{:S(2)}) collective-permute-start(bf16[2,256,512]{2,1,0:T(8,128)(2,1)S(1)} %get-tuple-element.48), channel_id=1, source_target_pairs={{0,1},{1,0},{2,3},{3,2},{4,5},{5,4},{6,7},{7,6},{8,9},{9,8},{10,11... | collective-permute-start | bytes 1572872 | tf_op jit(solution)/shard_map/ppermute | solution.py:23
  35.0 10.6 %collective-permute-start.9 = (bf16[1,256,512]{2,1,0:T(8,128)(2,1)S(1)}, bf16[1,256,512]{2,1,0:T(8,128)(2,1)S(1)}, u32[]{:S(2)}, u32[]{:S(2)}) collective-permute-start(bf16[1,256,512]{2,1,0:T(8,128)(2,1)S(1)} %slice.189.refs_9_), channel_id=1, source_target_pairs={{0,2},{1,3},{2,0},{3,1},{4,6},{5,7},{6,4},{7,5},{8,10},{9,11},{10,... | collective-permute-start | bytes 786440 | tf_op jit(solution)/shard_map/ppermute | solution.py:23
  41.2 4.6 %collective-permute-start.8 = (bf16[2,256,512]{2,1,0:T(8,128)(2,1)S(1)}, bf16[2,256,512]{2,1,0:T(8,128)(2,1)S(1)}, u32[]{:S(2)}, u32[]{:S(2)}) collective-permute-start(bf16[2,256,512]{2,1,0:T(8,128)(2,1)S(1)} %get-tuple-element.53), channel_id=1, source_target_pairs={{0,1},{1,0},{2,3},{3,2},{4,5},{5,4},{6,7},{7,6},{8,9},{9,8},{10,11... | collective-permute-start | bytes 1572872 | tf_op jit(solution)/shard_map/ppermute | solution.py:23
  46.0 11.5 %collective-permute-start.11 = (bf16[1,256,768]{2,1,0:T(8,128)(2,1)S(1)}, bf16[1,256,768]{2,1,0:T(8,128)(2,1)S(1)}, u32[]{:S(2)}, u32[]{:S(2)}) collective-permute-start(bf16[1,256,768]{2,1,0:T(8,128)(2,1)S(1)} %pad_maximum_fusion.refs_9_), channel_id=1, source_target_pairs={{0,2},{1,3},{2,0},{3,1},{4,6},{5,7},{6,4},{7,5},{8,10},{9,11},{10,... | collective-permute-start | bytes 1179656 | tf_op jit(solution)/shard_map/ppermute | solution.py:23
  50.9 6.9 %collective-permute-start.10 = (bf16[2,256,512]{2,1,0:T(8,128)(2,1)S(1)}, bf16[2,256,512]{2,1,0:T(8,128)(2,1)S(1)}, u32[]{:S(2)}, u32[]{:S(2)}) collective-permute-start(bf16[2,256,512]{2,1,0:T(8,128)(2,1)S(1)} %get-tuple-element.58), channel_id=1, source_target_pairs={{0,1},{1,0},{2,3},{3,2},{4,5},{5,4},{6,7},{7,6},{8,9},{9,8},{10,11... | collective-permute-start | bytes 1572872 | tf_op jit(solution)/shard_map/ppermute | solution.py:23
  51.1 7.2 %copy-start.1 = (bf16[64,1536]{1,0:T(8,128)(2,1)S(1)}, bf16[64,1536]{1,0:T(8,128)(2,1)}, u32[]{:S(2)}) copy-start(bf16[64,1536]{1,0:T(8,128)(2,1)} %copy-done) | copy-start | bytes 589828
  51.1 7.2 %copy-start.3 = (bf16[64,1536]{1,0:T(8,128)(2,1)S(1)}, bf16[64,1536]{1,0:T(8,128)(2,1)}, u32[]{:S(2)}) copy-start(bf16[64,1536]{1,0:T(8,128)(2,1)} %copy-done.2) | copy-start | bytes 589828
  57.5 5.5 %copy-start.5 = (bf16[1,256,768]{2,1,0:T(8,128)(2,1)}, bf16[1,256,768]{2,1,0:T(8,128)(2,1)S(1)}, u32[]{:S(2)}) copy-start(bf16[1,256,768]{2,1,0:T(8,128)(2,1)S(1)} %collective-permute-done.11.refs_1_) | copy-start | bytes 1179652
  58.0 10.7 %collective-permute-start.13 = (bf16[1,256,768]{2,1,0:T(8,128)(2,1)S(1)}, bf16[1,256,768]{2,1,0:T(8,128)(2,1)S(1)}, u32[]{:S(2)}, u32[]{:S(2)}) collective-permute-start(bf16[1,256,768]{2,1,0:T(8,128)(2,1)S(1)} %pad_maximum_fusion.1.refs_8_), channel_id=1, source_target_pairs={{0,2},{1,3},{2,0},{3,1},{4,6},{5,7},{6,4},{7,5},{8,10},{9,11},{10,... | collective-permute-start | bytes 1179656 | tf_op jit(solution)/shard_map/ppermute | solution.py:23
  63.0 5.9 %collective-permute-start.12 = (bf16[2,256,512]{2,1,0:T(8,128)(2,1)S(1)}, bf16[2,256,512]{2,1,0:T(8,128)(2,1)S(1)}, u32[]{:S(2)}, u32[]{:S(2)}) collective-permute-start(bf16[2,256,512]{2,1,0:T(8,128)(2,1)S(1)} %get-tuple-element.62), channel_id=1, source_target_pairs={{0,1},{1,0},{2,3},{3,2},{4,5},{5,4},{6,7},{7,6},{8,9},{9,8},{10,11... | collective-permute-start | bytes 1572872 | tf_op jit(solution)/shard_map/ppermute | solution.py:23
  63.1 6.4 %slice-start = ((bf16[1,256,768]{2,1,0:T(8,128)(2,1)}), bf16[1,256,256]{2,1,0:T(8,128)(2,1)S(1)}, s32[]{:S(2)}) async-start(bf16[1,256,768]{2,1,0:T(8,128)(2,1)} %copy-done.5), calls=%async_computation | async-start | bytes 262144 | tf_op jit(solution)/shard_map/slice | solution.py:267
  66.5 4.6 %copy-start.6 = (bf16[1,256,768]{2,1,0:T(8,128)(2,1)S(1)}, bf16[1,256,768]{2,1,0:T(8,128)(2,1)}, u32[]{:S(2)}) copy-start(bf16[1,256,768]{2,1,0:T(8,128)(2,1)} %copy-done.5) | copy-start | bytes 1179652
  69.1 9.8 %collective-permute-start.14 = (bf16[1,256,768]{2,1,0:T(8,128)(2,1)S(1)}, bf16[1,256,768]{2,1,0:T(8,128)(2,1)S(1)}, u32[]{:S(2)}, u32[]{:S(2)}) collective-permute-start(bf16[1,256,768]{2,1,0:T(8,128)(2,1)S(1)} %pad_maximum_fusion.2.refs_7_), channel_id=1, source_target_pairs={{0,2},{1,3},{2,0},{3,1},{4,6},{5,7},{6,4},{7,5},{8,10},{9,11},{10,... | collective-permute-start | bytes 1179656 | tf_op jit(solution)/shard_map/ppermute | solution.py:23
  69.5 1.6 %collective-permute-start.16 = (bf16[2,256,256]{2,1,0:T(8,128)(2,1)S(1)}, bf16[2,256,256]{2,1,0:T(8,128)(2,1)S(1)}, u32[]{:S(2)}, u32[]{:S(2)}) collective-permute-start(bf16[2,256,256]{2,1,0:T(8,128)(2,1)S(1)} %pad_maximum_fusion.4), channel_id=1, source_target_pairs={{0,1},{1,0},{2,3},{3,2},{4,5},{5,4},{6,7},{7,6},{8,9},{9,8},{10,11... | collective-permute-start | bytes 786440 | tf_op jit(solution)/shard_map/ppermute | solution.py:23
  69.6 4.9 %collective-permute-start.15 = (bf16[2,256,256]{2,1,0:T(8,128)(2,1)S(1)}, bf16[2,256,256]{2,1,0:T(8,128)(2,1)S(1)}, u32[]{:S(2)}, u32[]{:S(2)}) collective-permute-start(bf16[2,256,256]{2,1,0:T(8,128)(2,1)S(1)} %pad_maximum_fusion.3), channel_id=1, source_target_pairs={{0,1},{1,0},{2,3},{3,2},{4,5},{5,4},{6,7},{7,6},{8,9},{9,8},{10,11... | collective-permute-start | bytes 786440 | tf_op jit(solution)/shard_map/ppermute | solution.py:23
  79.0 1.7 %collective-permute-start.18 = (bf16[2,256,256]{2,1,0:T(8,128)(2,1)S(1)}, bf16[2,256,256]{2,1,0:T(8,128)(2,1)S(1)}, u32[]{:S(2)}, u32[]{:S(2)}) collective-permute-start(bf16[2,256,256]{2,1,0:T(8,128)(2,1)S(1)} %pad_maximum_fusion.5), channel_id=1, source_target_pairs={{0,1},{1,0},{2,3},{3,2},{4,5},{5,4},{6,7},{7,6},{8,9},{9,8},{10,11... | collective-permute-start | bytes 786440 | tf_op jit(solution)/shard_map/ppermute | solution.py:23
  79.2 6.0 %collective-permute-start.17 = (bf16[1,256,256]{2,1,0:T(8,128)(2,1)S(1)}, bf16[1,256,256]{2,1,0:T(8,128)(2,1)S(1)}, u32[]{:S(2)}, u32[]{:S(2)}) collective-permute-start(bf16[1,256,256]{2,1,0:T(8,128)(2,1)S(1)} %fusion.refs_7_.refs_0_), channel_id=1, source_target_pairs={{0,2},{1,3},{2,0},{3,1},{4,6},{5,7},{6,4},{7,5},{8,10},{9,11},{10,... | collective-permute-start | bytes 393224 | tf_op jit(solution)/shard_map/ppermute | solution.py:23
  85.2 1.6 %collective-permute-start.19 = (bf16[2,256,256]{2,1,0:T(8,128)(2,1)S(1)}, bf16[2,256,256]{2,1,0:T(8,128)(2,1)S(1)}, u32[]{:S(2)}, u32[]{:S(2)}) collective-permute-start(bf16[2,256,256]{2,1,0:T(8,128)(2,1)S(1)} %pad_maximum_fusion.6), channel_id=1, source_target_pairs={{0,1},{1,0},{2,3},{3,2},{4,5},{5,4},{6,7},{7,6},{8,9},{9,8},{10,11... | collective-permute-start | bytes 786440 | tf_op jit(solution)/shard_map/ppermute | solution.py:23
  89.1 5.5 %collective-permute-start.20 = (bf16[32,1536]{1,0:T(8,128)(2,1)S(1)}, bf16[32,1536]{1,0:T(8,128)(2,1)S(1)}, u32[]{:S(2)}, u32[]{:S(2)}) collective-permute-start(bf16[32,1536]{1,0:T(8,128)(2,1)S(1)} %get-tuple-element.74), channel_id=1, source_target_pairs={{0,12},{4,0},{8,4},{12,8},{1,13},{5,1},{9,5},{13,9},{2,14},{6,2},{... | collective-permute-start | bytes 294920 | tf_op jit(solution)/shard_map/ppermute | solution.py:385
  91.4 7.6 %collective-permute-start.22 = (bf16[32,1536]{1,0:T(8,128)(2,1)S(1)}, bf16[32,1536]{1,0:T(8,128)(2,1)S(1)}, u32[]{:S(2)}, u32[]{:S(2)}) collective-permute-start(bf16[32,1536]{1,0:T(8,128)(2,1)S(1)} %get-tuple-element.76), channel_id=1, source_target_pairs={{0,4},{4,8},{8,12},{12,0},{1,5},{5,9},{9,13},{13,1},{2,6},{6,10},{... | collective-permute-start | bytes 294920 | tf_op jit(solution)/shard_map/ppermute | solution.py:385
  94.6 9.3 %collective-permute-start.21 = (bf16[64,1536]{1,0:T(8,128)(2,1)S(1)}, bf16[64,1536]{1,0:T(8,128)(2,1)S(1)}, u32[]{:S(2)}, u32[]{:S(2)}) collective-permute-start(bf16[64,1536]{1,0:T(8,128)(2,1)S(1)} %pad_maximum_fusion.7), channel_id=1, source_target_pairs={{0,12},{4,0},{8,4},{12,8},{1,13},{5,1},{9,5},{13,9},{2,14},{6,2},{... | collective-permute-start | bytes 589832 | tf_op jit(solution)/shard_map/ppermute | solution.py:394
  99.0 7.8 %collective-permute-start.23 = (bf16[64,1536]{1,0:T(8,128)(2,1)S(1)}, bf16[64,1536]{1,0:T(8,128)(2,1)S(1)}, u32[]{:S(2)}, u32[]{:S(2)}) collective-permute-start(bf16[64,1536]{1,0:T(8,128)(2,1)S(1)} %pad_maximum_fusion.8), channel_id=1, source_target_pairs={{0,4},{4,8},{8,12},{12,0},{1,5},{5,9},{9,13},{13,1},{2,6},{6,10},{... | collective-permute-start | bytes 589832 | tf_op jit(solution)/shard_map/ppermute | solution.py:395
  (1 other events, 3.4 us)

commit v9 on v7

--- a/solution.py
+++ b/solution.py
@@ -128,8 +128,9 @@
 
 
 def products(rows, given, to, info):
-    most = rows.shape[0] // given.shape[1]
-    shares, width = to.shape[0], to.shape[2] // 2
+    count = rows.shape[0]
+    most = count // given.shape[1]
+    shares, _, width = to.shape
     for m in range(2):
         for x in range(given.shape[1]):
             mine = slice(x * most, (x + 1) * most)
@@ -137,7 +138,7 @@
             part = part.astype(jnp.bfloat16)
             for q in range(shares):
                 j = backwards(q, shares) ^ (info[1] >> 1)
-                to[j, mine, m * width : (m + 1) * width] = part[:, q * width : (q + 1) * width]
+                to[j, m * count + x * most : m * count + (x + 1) * most, :] = part[:, q * width : (q + 1) * width]
 
 
 def send_body(experts, info, own, outs, rest, fetch):
@@ -170,7 +171,7 @@
 
 def part_shape(given, most, n_dp):
     _, experts, _, half = given.shape
-    return jax.ShapeDtypeStruct((n_dp // 2, most * experts, 4 * half // n_dp), jnp.bfloat16)
+    return jax.ShapeDtypeStruct((n_dp // 2, 2 * most * experts, 2 * half // n_dp), jnp.bfloat16)
 
 
 def send_half(feeds, rank, info, given, weights, experts, most, n_dp, ahead, after):
@@ -192,17 +193,17 @@
     return call(keep_body, "keep_half", info, inputs, weights, ahead, [], outs, [])
 
 
-def down_body(lanes, experts, first, info, own, outs, rest, fetch):
+def down_body(places, experts, first, info, own, outs, rest, fetch):
     fetch()
-    parts, (rank, wt, given) = own[: len(lanes)], own[len(lanes) : len(lanes) + 3]
+    parts, (rank, wt, given) = own[: len(places)], own[len(places) : len(places) + 3]
     before = None if first else own[-1]
     hidden, mix, out = rest
     most = hidden.shape[0] // len(experts)
     width = parts[0].shape[-1]
     n_dp = hidden.shape[1] // width
-    for part, (at, shares) in zip(parts, lanes):
+    for part, (at, shares) in zip(parts, places):
         for j, l in enumerate(shares):
-            hidden[:, units_of(l, info, n_dp, width)] = part[j, :, at : at + width]
+            hidden[:, units_of(l, info, n_dp, width)] = part[j, at : at + hidden.shape[0], :]
     r = lax.broadcasted_iota(jnp.int32, (most, mix.shape[1]), 0).astype(jnp.float32)
     for x, e in enumerate(experts):
         mix[x * most : (x + 1) * most, :] = jnp.where(
@@ -229,7 +230,7 @@
 
 
 def down(parts, rank, wt, info, given, weights, total, experts, cuts, ahead, after):
-    parts, lanes = [part for part, *_ in parts], [tuple(where) for _, *where in parts]
+    parts, places = [part for part, *_ in parts], [tuple(where) for _, *where in parts]
     rows = parts[0].shape[1]
     _, hidden, local = given.shape
     kind = jnp.bfloat16 if len(cuts) > 1 else jnp.float32
@@ -241,7 +242,7 @@
         pltpu.VMEM((rows, local), jnp.bfloat16),
     ]
     inputs = [(x, VMEM) for x in (*parts, rank, wt, given, *before)]
-    body = functools.partial(down_body, lanes, experts, total is None)
+    body = functools.partial(down_body, places, experts, total is None)
     return call(body, "down", info, inputs, weights, ahead, after, outs, scratch)
 
 
@@ -249,8 +250,8 @@
     if after:
         late, *_ = lax.optimization_barrier((late, *after))
     gate_up = total + late.astype(jnp.float32)
-    width = gate_up.shape[2] // 2
-    return (jax.nn.silu(gate_up[:, :, :width]) * gate_up[:, :, width:]).astype(jnp.bfloat16)
+    rows = gate_up.shape[1] // 2
+    return (jax.nn.silu(gate_up[:, :rows]) * gate_up[:, rows:]).astype(jnp.bfloat16)
 
 
 def chip_sums(send, keep, bits):
@@ -261,10 +262,10 @@
 
 
 def everyone_s(share, other, at, bits):
-    width = share.shape[2]
+    rows = share.shape[1]
     top = 1 << bits[-1]
     parts = [(share, 0, [0]), (other, at, [top])]
-    held, whose = jnp.concatenate([share, other[:, :, at : at + width]], axis=0), [0, top]
+    held, whose = jnp.concatenate([share, other[:, at : at + rows]], axis=0), [0, top]
     for b in reversed(bits[:-1]):
         theirs = flip(held, "dp", 1 << b)
         parts.append((theirs, 0, [l | 1 << b for l in whose]))
@@ -278,18 +279,19 @@
     tok_rows, top = expert_ids.shape
     experts = w_gate.shape[0]
     capacity = 2 * tok_rows * top // (experts * n_owner)
-    per_chunk = 2 if experts % 2 == 0 else 1
     most = n_owner * capacity
-    chunks = experts // per_chunk
+    singles = experts < 4 or experts % 2 > 0
+    starts = list(range(experts)) if singles else [0, *range(1, experts, 2)]
+    of = [list(range(a, b)) for a, b in zip(starts, starts[1:] + [experts])]
+    chunks = len(of)
 
     meta = jnp.concatenate([expert_ids.T.astype(jnp.float32), scores.T], axis=0)
     me = lax.axis_index("dp").astype(jnp.int32)
     first = lax.axis_index("expert").astype(jnp.int32) * experts
     info = jnp.stack([first, me, backwards(me, n_dp)])
-    of = lambda c: list(range(c * per_chunk, (c + 1) * per_chunk))
     weights = (w_gate, w_up, w_down)
-    needs = [(of(c), side) for c in range(chunks) for side in (1, 0)] + [(of(c), None) for c in range(chunks)]
-    given = {0: stage(info, weights, needs[0], [])}
+    needs = [(of[c], side) for c in range(chunks) for side in (1, 0)] + [(of[c], None) for c in range(chunks)]
+    given = {k: stage(info, weights, needs[k], []) for k in (0, 1)}
 
     def fetched(k, outs):
         if k + 2 < len(needs):
@@ -298,13 +300,12 @@
 
     ahead = lambda k: needs[k + 2] if k + 2 < len(needs) else None
 
-    meta = lax.optimization_barrier((meta, given[0]))[0]
+    meta = lax.optimization_barrier((meta, given[0], given[1]))[0]
     metas = [meta] + [
         lax.ppermute(meta, "expert", [(i, (i - k) % n_owner) for i in range(n_owner)])
         for k in gathered_order(n_owner)[1:]
     ]
-    feeds, halfway = gathered(tokens, "expert", metas)
-    given[1] = stage(info, weights, needs[1], halfway)
+    feeds = gathered(tokens, "expert", metas)
     rank, wt = route(metas, info, experts)
 
     tall, wide = [feed.shape[0] for feed in feeds], tokens.shape[1]
@@ -315,7 +316,7 @@
 
     def add(c, after):
         k, cuts = 2 * chunks + c, tall if c == chunks - 1 else [sum(tall)]
-        outs = down(parts[c], rank, wt, info, given[k], weights, total, of(c), cuts, ahead(k), after)
+        outs = down(parts[c], rank, wt, info, given[k], weights, total, of[c], cuts, ahead(k), after)
         outs = fetched(k, outs)
         return outs if c == chunks - 1 else outs[0]
 
@@ -323,24 +324,24 @@
         last = c == chunks - 1
         k = 2 * c
         send, rows = fetched(
-            k, send_half(feeds, rank, info, given[k], weights, of(c), most, n_dp, ahead(k), sent[-1:] or [given[1]])
+            k, send_half(feeds, rank, info, given[k], weights, of[c], most, n_dp, ahead(k), sent[-1:])
         )
         k = 2 * c + 1
         (keep,) = fetched(k, keep_half(rows, info, given[k], weights, most, n_dp, ahead(k)))
         before, behind = kept, late
         kept, out = chip_sums(send, keep, bits)
-        width = out.shape[2]
+        sums = out.shape[1]
         if c > 0:
-            share = finish(before, behind[:, :, :width], [])
-            out = jnp.concatenate([out, share], axis=2)
+            share = finish(before, behind[:, : before.shape[1]], [])
+            out = jnp.concatenate([out, share], axis=1)
         sent.append(out)
         late = flip(out, "dp", cross)
         if c > 0:
-            parts.append(everyone_s(share, late, width, bits))
+            parts.append(everyone_s(share, late, sums, bits))
         if last:
             for d in range(min(c - 1, 2)):
                 total = add(d, [out] if d == 0 else [])
-    share = finish(kept, late[:, :, :width], [] if total is None else [total])
+    share = finish(kept, late[:, : kept.shape[1]], [] if total is None else [total])
     other = flip(share, "dp", cross)
     for c in range(max(min(chunks - 2, 2), 0), chunks - 1):
         total = add(c, [share])
@@ -360,16 +361,15 @@
     n = lax.axis_size(axis)
     up, down_ = [(i, (i + 1) % n) for i in range(n)], [(i, (i - 1) % n) for i in range(n)]
     below = above = x
-    found, halfway = [x], []
+    found = [x]
     for _ in range(1, n // 2):
         below, above = lax.ppermute(below, axis, up), lax.ppermute(above, axis, down_)
         found += [below, above]
     if n > 1:
         half = x.shape[0] // 2
         below, above, *_ = lax.optimization_barrier((below, above, *beside))
-        halfway = [below]
         found += [lax.ppermute(below[:half], axis, up), lax.ppermute(above[half:], axis, down_)]
-    return found, halfway
+    return found
 
 
 def returned(partials, axis):

time: 108 us -> 122 us (1.13)
  Pallas kernels: 53.5 us -> 58.8 us
  starting transfers between devices: 25.4 us -> 30.3 us
  waiting for transfers between devices: 24.9 us -> 28.6 us
    pallas_call x14 -> x17, Pallas kernels: 52.8 us -> 58 us  [call(): pl.pallas_call(whole, out_shape=tuple(outs), in_specs=[SMEM] + [spec for...]
    ppermute x13 -> x16, starting transfers between devices: 5.83 us -> 9.1 us  [flip(): lax.ppermute(x, axis, [(i, i ^ k) for i in range(lax.axis_size(axis))])]
    ppermute x13 -> x16, waiting for transfers between devices: 9.51 us -> 11.4 us  [flip(): lax.ppermute(x, axis, [(i, i ^ k) for i in range(lax.axis_size(axis))])]
    ppermute x1, waiting for transfers between devices: 0.01 us -> 1.79 us  [gathered(): lax.ppermute(below[:half], axis, up)]
    ppermute x1, starting transfers between devices: 2.27 us -> 3.93 us  [returned(): lax.ppermute(partials[-2], axis, down_)]
  transfers between devices with their start and end apart: 24 -> 27, of which waited for: 11 -> 11; matrix products, arithmetic and copies ran while one was open for 1% -> 1% of each run, Pallas kernels for 43% -> 40%
where the time goes in v9:
time: 122 us; the launch traced here: 121 us
  Pallas kernels  58.8 us (48%)
  starting transfers between devices  30.3 us (25%)
  waiting for transfers between devices  28.6 us (23%)
  other arithmetic  2.84 us (2%)
    pallas_call x17, Pallas kernels, call(): pl.pallas_call(whole, out_shape=tuple(outs), in_specs=[SMEM] + [spec for...  58 us
    ppermute x16, waiting for transfers between devices, flip(): lax.ppermute(x, axis, [(i, i ^ k) for i in range(lax.axis_size(axis))])  11.4 us
    ppermute x16, starting transfers between devices, flip(): lax.ppermute(x, axis, [(i, i ^ k) for i in range(lax.axis_size(axis))])  9.1 us
    ppermute x1, waiting for transfers between devices, returned(): low = lax.ppermute(a.astype(jnp.bfloat16), axis, down_)  4.89 us
    ppermute x3, waiting for transfers between devices, on_device(): lax.ppermute(meta, 'expert', [(i, (i - k) % n_owner) for i in range(n_own...  4.55 us
    ppermute x1, starting transfers between devices, returned(): low = lax.ppermute(a.astype(jnp.bfloat16), axis, down_)  4.33 us
    ppermute x1, starting transfers between devices, returned(): lax.ppermute(partials[-2], axis, down_)  3.93 us
    ppermute x3, starting transfers between devices, on_device(): lax.ppermute(meta, 'expert', [(i, (i - k) % n_owner) for i in range(n_own...  3.87 us
  transfers between devices with their start and end apart: 27, of which 11 were waited for; matrix products, arithmetic and copies ran while one was open for 1% of the time, Pallas kernels for 40%

profile of v9, /device:TPU:0, one launch (start us, length us, event | category | flops | bytes accessed | tf_op | source)
XLA Modules:
  0.0 121.3 jit_solution(1408438873383264136)
XLA Ops:
  0.0 3.0 %collective-permute-start = (bf16[64,1536]{1,0:T(8,128)(2,1)}, bf16[64,1536]{1,0:T(8,128)(2,1)S(1)}, u32[]{:S(2)}, u32[]{:S(2)}) collective-permute-start(bf16[64,1536]{1,0:T(8,128)(2,1)} %refs_0_.13), channel_id=1, source_target_pairs={{0,4},{4,8},{8,12},{12,0},{1,5},{5,9},{9,13},{13,1},{2,6},{6,10},{... | collective-permute-start | bytes 589832 | tf_op jit(solution)/shard_map/ppermute | solution.py:366
  3.0 2.0 %collective-permute-start.1 = (bf16[64,1536]{1,0:T(8,128)(2,1)}, bf16[64,1536]{1,0:T(8,128)(2,1)S(1)}, u32[]{:S(2)}, u32[]{:S(2)}) collective-permute-start(bf16[64,1536]{1,0:T(8,128)(2,1)} %refs_0_.13), channel_id=1, source_target_pairs={{0,12},{4,0},{8,4},{12,8},{1,13},{5,1},{9,5},{13,9},{2,14},{6,2},{... | collective-permute-start | bytes 589832 | tf_op jit(solution)/shard_map/ppermute | solution.py:366
  5.8 2.4 %stage.2.refs_6_ = bf16[2,1,1536,512]{3,2,1,0:T(8,128)(2,1)S(1)} custom-call(s32[3]{0:T(128)S(1)} %pad_add_fusion.info, bf16[8,1536,1024]{2,1,0:T(8,128)(2,1)} %refs_2_.8, bf16[8,1536,1024]{2,1,0:T(8,128)(2,1)} %refs_3_.7), custom_call_target="tpu_custom_call" | custom-call | flops 1 | bytes 1 | tf_op jit(solution)/shard_map/stage/pallas_call | solution.py:113
  8.3 2.4 %stage.3.refs_1_ = bf16[2,1,1536,512]{3,2,1,0:T(8,128)(2,1)S(1)} custom-call(s32[3]{0:T(128)S(1)} %pad_add_fusion.info, bf16[8,1536,1024]{2,1,0:T(8,128)(2,1)} %refs_2_.8, bf16[8,1536,1024]{2,1,0:T(8,128)(2,1)} %refs_3_.7), custom_call_target="tpu_custom_call" | custom-call | flops 1 | bytes 1 | tf_op jit(solution)/shard_map/stage/pallas_call | solution.py:113
  10.8 3.8 %collective-permute-start.3 = (f32[16,64]{1,0:T(8,128)S(1)}, f32[16,64]{1,0:T(8,128)S(1)}, u32[]{:S(2)}, u32[]{:S(2)}) collective-permute-start(f32[16,64]{1,0:T(8,128)S(1)} %pad_maximum_fusion.11.refs_0_), channel_id=1, source_target_pairs={{0,12},{4,0},{8,4},{12,8},{1,13},{5,1},{9,5},{13,9},{2,14},{6,2},{... | collective-permute-start | bytes 12296 | tf_op jit(solution)/shard_map/ppermute | solution.py:305
  16.3 2.9 %collective-permute-done.4.refs_3_ = f32[16,64]{1,0:T(8,128)S(1)} collective-permute-done((f32[16,64]{1,0:T(8,128)S(1)}, f32[16,64]{1,0:T(8,128)S(1)}, u32[]{:S(2)}, u32[]{:S(2)}) %collective-permute-start.4) | collective-permute-done | bytes 4128 | tf_op jit(solution)/shard_map/ppermute | solution.py:305
  19.3 3.9 %collective-permute-start.6 = (bf16[32,1536]{1,0:T(8,128)(2,1)S(1)}, bf16[32,1536]{1,0:T(8,128)(2,1)S(1)}, u32[]{:S(2)}, u32[]{:S(2)}) collective-permute-start(bf16[32,1536]{1,0:T(8,128)(2,1)S(1)} %slice.126), channel_id=1, source_target_pairs={{0,12},{4,0},{8,4},{12,8},{1,13},{5,1},{9,5},{13,9},{2,14},{6,2},{... | collective-permute-start | bytes 294920 | tf_op jit(solution)/shard_map/ppermute | solution.py:371
  23.9 1.8 %collective-permute-done.5.refs_3_ = bf16[32,1536]{1,0:T(8,128)(2,1)S(1)} collective-permute-done((bf16[32,1536]{1,0:T(8,128)(2,1)S(1)}, bf16[32,1536]{1,0:T(8,128)(2,1)S(1)}, u32[]{:S(2)}, u32[]{:S(2)}) %collective-permute-start.5) | collective-permute-done | bytes 98336 | tf_op jit(solution)/shard_map/ppermute | solution.py:371
  25.7 4.5 %send_half.5 = (bf16[2,256,256]{2,1,0:T(8,128)(2,1)S(1)}, bf16[128,1536]{1,0:T(8,128)(2,1)S(1)}, bf16[2,2,1536,512]{3,2,1,0:T(8,128)(2,1)S(1)}) custom-call(s32[3]{0:T(128)S(1)} %pad_add_fusion.info, bf16[64,1536]{1,0:T(8,128)(2,1)S(1)} %copy-done, bf16[64,1536]{1,0:T(8,128)(2,1)S(1)} %collective-permute-done.refs_1_, ...), custom_call_target="tpu_custom_call" | custom-call | flops 1 | bytes 1 | tf_op jit(solution)/shard_map/send_half/pallas_call | solution.py:113
  30.3 3.8 %keep_half.5 = (bf16[2,256,256]{2,1,0:T(8,128)(2,1)S(1)}, bf16[2,2,1536,512]{3,2,1,0:T(8,128)(2,1)S(1)}) custom-call(s32[3]{0:T(128)S(1)} %pad_add_fusion.info, bf16[128,1536]{1,0:T(8,128)(2,1)S(1)} %get-tuple-element.53.refs_0_, bf16[2,1,1536,512]{3,2,1,0:T(8,128)(2,1)S(1)} %stage.3.refs_1_, bf16[8,1536,1024]{2,1,0:T(8,128)(2,1)} %refs_2_.8, ...), custom_call_target="tpu_custom_call" | custom-call | flops 1 | bytes 1 | tf_op jit(solution)/shard_map/keep_half/pallas_call | solution.py:113
  34.2 1.8 %collective-permute-start.9 = (bf16[1,256,256]{2,1,0:T(8,128)(2,1)S(1)}, bf16[1,256,256]{2,1,0:T(8,128)(2,1)S(1)}, u32[]{:S(2)}, u32[]{:S(2)}) collective-permute-start(bf16[1,256,256]{2,1,0:T(8,128)(2,1)S(1)} %slice.230.refs_9_), channel_id=1, source_target_pairs={{0,2},{1,3},{2,0},{3,1},{4,6},{5,7},{6,4},{7,5},{8,10},{9,11},{10,... | collective-permute-start | bytes 393224 | tf_op jit(solution)/shard_map/ppermute | solution.py:23
  36.0 4.5 %send_half.6 = (bf16[2,512,256]{2,1,0:T(8,128)(2,1)S(1)}, bf16[256,1536]{1,0:T(8,128)(2,1)S(1)}, bf16[2,2,1536,512]{3,2,1,0:T(8,128)(2,1)S(1)}) custom-call(s32[3]{0:T(128)S(1)} %pad_add_fusion.info, bf16[64,1536]{1,0:T(8,128)(2,1)S(1)} %copy-done, bf16[64,1536]{1,0:T(8,128)(2,1)S(1)} %collective-permute-done.refs_1_, ...), custom_call_target="tpu_custom_call" | custom-call | flops 1 | bytes 1 | tf_op jit(solution)/shard_map/send_half/pallas_call | solution.py:113
  40.7 4.2 %keep_half.6 = (bf16[2,512,256]{2,1,0:T(8,128)(2,1)S(1)}, bf16[2,2,1536,512]{3,2,1,0:T(8,128)(2,1)S(1)}) custom-call(s32[3]{0:T(128)S(1)} %pad_add_fusion.info, bf16[256,1536]{1,0:T(8,128)(2,1)S(1)} %get-tuple-element.57.refs_0_, bf16[2,2,1536,512]{3,2,1,0:T(8,128)(2,1)S(1)} %get-tuple-element.58.refs_1_, bf16[8,1536,1024]{2,1,0:T(8,128)(2,1)} %refs_2_.8, ...), custom_call_target="tpu_custom_call" | custom-call | flops 1 | bytes 1 | tf_op jit(solution)/shard_map/keep_half/pallas_call | solution.py:113
  45.7 4.5 %send_half.7 = (bf16[2,512,256]{2,1,0:T(8,128)(2,1)S(1)}, bf16[256,1536]{1,0:T(8,128)(2,1)S(1)}, bf16[2,2,1536,512]{3,2,1,0:T(8,128)(2,1)S(1)}) custom-call(s32[3]{0:T(128)S(1)} %pad_add_fusion.info, bf16[64,1536]{1,0:T(8,128)(2,1)S(1)} %copy-done, bf16[64,1536]{1,0:T(8,128)(2,1)S(1)} %collective-permute-done.refs_1_, ...), custom_call_target="tpu_custom_call" | custom-call | flops 1 | bytes 1 | tf_op jit(solution)/shard_map/send_half/pallas_call | solution.py:113
  50.2 4.2 %keep_half.7 = (bf16[2,512,256]{2,1,0:T(8,128)(2,1)S(1)}, bf16[2,2,1536,512]{3,2,1,0:T(8,128)(2,1)S(1)}) custom-call(s32[3]{0:T(128)S(1)} %pad_add_fusion.info, bf16[256,1536]{1,0:T(8,128)(2,1)S(1)} %get-tuple-element.62.refs_0_, bf16[2,2,1536,512]{3,2,1,0:T(8,128)(2,1)S(1)} %get-tuple-element.63.refs_1_, bf16[8,1536,1024]{2,1,0:T(8,128)(2,1)} %refs_2_.8, ...), custom_call_target="tpu_custom_call" | custom-call | flops 1 | bytes 1 | tf_op jit(solution)/shard_map/keep_half/pallas_call | solution.py:113
  56.6 3.5 %send_half.8 = (bf16[2,512,256]{2,1,0:T(8,128)(2,1)S(1)}, bf16[256,1536]{1,0:T(8,128)(2,1)S(1)}, bf16[2,1,1536,512]{3,2,1,0:T(8,128)(2,1)S(1)}) custom-call(s32[3]{0:T(128)S(1)} %pad_add_fusion.info, bf16[64,1536]{1,0:T(8,128)(2,1)S(1)} %copy-done, bf16[64,1536]{1,0:T(8,128)(2,1)S(1)} %collective-permute-done.refs_1_, ...), custom_call_target="tpu_custom_call" | custom-call | flops 1 | bytes 1 | tf_op jit(solution)/shard_map/send_half/pallas_call | solution.py:113
  60.4 3.3 %keep_half.8 = (bf16[2,512,256]{2,1,0:T(8,128)(2,1)S(1)}, bf16[2,1,1536,512]{3,2,1,0:T(8,128)(2,1)S(1)}) custom-call(s32[3]{0:T(128)S(1)} %pad_add_fusion.info, bf16[256,1536]{1,0:T(8,128)(2,1)S(1)} %get-tuple-element.67.refs_0_, bf16[2,2,1536,512]{3,2,1,0:T(8,128)(2,1)S(1)} %get-tuple-element.68.refs_1_, bf16[8,1536,1024]{2,1,0:T(8,128)(2,1)} %refs_2_.8, ...), custom_call_target="tpu_custom_call" | custom-call | flops 1 | bytes 1 | tf_op jit(solution)/shard_map/keep_half/pallas_call | solution.py:113
  63.6 2.8 %collective-permute-done.13.refs_1_ = bf16[1,768,256]{2,1,0:T(8,128)(2,1)S(1)} collective-permute-done((bf16[1,768,256]{2,1,0:T(8,128)(2,1)S(1)}, bf16[1,768,256]{2,1,0:T(8,128)(2,1)S(1)}, u32[]{:S(2)}, u32[]{:S(2)}) %collective-permute-start.13) | collective-permute-done | bytes 393248 | tf_op jit(solution)/shard_map/ppermute | solution.py:23
  66.8 3.7 %send_half.9 = (bf16[2,256,256]{2,1,0:T(8,128)(2,1)S(1)}, bf16[128,1536]{1,0:T(8,128)(2,1)S(1)}, bf16[1,1024,1536]{2,1,0:T(8,128)(2,1)S(1)}) custom-call(s32[3]{0:T(128)S(1)} %pad_add_fusion.info, bf16[64,1536]{1,0:T(8,128)(2,1)S(1)} %copy-done, bf16[64,1536]{1,0:T(8,128)(2,1)S(1)} %collective-permute-done.refs_1_, ...), custom_call_target="tpu_custom_call" | custom-call | flops 1 | bytes 1 | tf_op jit(solution)/shard_map/send_half/pallas_call | solution.py:113
  70.5 1.8 %collective-permute-start.15 = (bf16[1,768,256]{2,1,0:T(8,128)(2,1)S(1)}, bf16[1,768,256]{2,1,0:T(8,128)(2,1)S(1)}, u32[]{:S(2)}, u32[]{:S(2)}) collective-permute-start(bf16[1,768,256]{2,1,0:T(8,128)(2,1)S(1)} %pad_maximum_fusion.1.refs_8_), channel_id=1, source_target_pairs={{0,2},{1,3},{2,0},{3,1},{4,6},{5,7},{6,4},{7,5},{8,10},{9,11},{10,... | collective-permute-start | bytes 1179656 | tf_op jit(solution)/shard_map/ppermute | solution.py:23
  72.6 3.5 %keep_half.9 = (bf16[2,256,256]{2,1,0:T(8,128)(2,1)S(1)}, bf16[2,1024,1536]{2,1,0:T(8,128)(2,1)S(1)}) custom-call(s32[3]{0:T(128)S(1)} %pad_add_fusion.info, bf16[128,1536]{1,0:T(8,128)(2,1)S(1)} %get-tuple-element.71.refs_0_, bf16[2,1,1536,512]{3,2,1,0:T(8,128)(2,1)S(1)} %get-tuple-element.72.refs_1_, bf16[8,1024,1536]{2,1,0:T(8,128)(2,1)} %refs_7_.13), custom_call_target="tpu_custom_call" | custom-call | flops 1 | bytes 1 | tf_op jit(solution)/shard_map/keep_half/pallas_call | solution.py:113
  76.2 5.8 %collective-permute-done.15.refs_1_ = bf16[1,768,256]{2,1,0:T(8,128)(2,1)S(1)} collective-permute-done((bf16[1,768,256]{2,1,0:T(8,128)(2,1)S(1)}, bf16[1,768,256]{2,1,0:T(8,128)(2,1)S(1)}, u32[]{:S(2)}, u32[]{:S(2)}) %collective-permute-start.15) | collective-permute-done | bytes 393248 | tf_op jit(solution)/shard_map/ppermute | solution.py:23
  82.2 1.8 %collective-permute-start.16 = (bf16[1,512,256]{2,1,0:T(8,128)(2,1)S(1)}, bf16[1,512,256]{2,1,0:T(8,128)(2,1)S(1)}, u32[]{:S(2)}, u32[]{:S(2)}) collective-permute-start(bf16[1,512,256]{2,1,0:T(8,128)(2,1)S(1)} %pad_maximum_fusion.3.refs_7_), channel_id=1, source_target_pairs={{0,2},{1,3},{2,0},{3,1},{4,6},{5,7},{6,4},{7,5},{8,10},{9,11},{10,... | collective-permute-start | bytes 786440 | tf_op jit(solution)/shard_map/ppermute | solution.py:23
  85.4 3.5 %down.5 = (f32[256,1536]{1,0:T(8,128)S(1)}, bf16[2,1024,1536]{2,1,0:T(8,128)(2,1)S(1)}) custom-call(s32[3]{0:T(128)S(1)} %pad_add_fusion.info, bf16[1,128,256]{2,1,0:T(8,128)(2,1)S(1)} %fusion.4.refs_0_, bf16[1,640,256]{2,1,0:T(8,128)(2,1)S(1)} %collective-permute-done.11.refs_1_, bf16[2,128,256]{2,1,0:T(8,128)(2,1)S(1)} %collective-permute-done.18.refs_2_, ...), custom_call_target="tpu_custom_call" | custom-call | flops 1 | bytes 1 | tf_op jit(solution)/shard_map/down/pallas_call | solution.py:113
  88.9 3.5 %down.6 = (f32[256,1536]{1,0:T(8,128)S(1)}, bf16[2,1024,1536]{2,1,0:T(8,128)(2,1)S(1)}) custom-call(s32[3]{0:T(128)S(1)} %pad_add_fusion.info, bf16[1,256,256]{2,1,0:T(8,128)(2,1)S(1)} %fusion.2.refs_0_, bf16[1,768,256]{2,1,0:T(8,128)(2,1)S(1)} %collective-permute-done.13.refs_1_, bf16[2,256,256]{2,1,0:T(8,128)(2,1)S(1)} %collective-permute-done.17.refs_2_, ...), custom_call_target="tpu_custom_call" | custom-call | flops 1 | bytes 1 | tf_op jit(solution)/shard_map/down/pallas_call | solution.py:113
  93.2 2.5 %down.7 = (f32[256,1536]{1,0:T(8,128)S(1)}, bf16[1,1024,1536]{2,1,0:T(8,128)(2,1)S(1)}) custom-call(s32[3]{0:T(128)S(1)} %pad_add_fusion.info, bf16[1,256,256]{2,1,0:T(8,128)(2,1)S(1)} %fusion.1.refs_0_, bf16[1,768,256]{2,1,0:T(8,128)(2,1)S(1)} %collective-permute-done.15.refs_1_, bf16[2,256,256]{2,1,0:T(8,128)(2,1)S(1)} %collective-permute-done.21.refs_2_, ...), custom_call_target="tpu_custom_call" | custom-call | flops 1 | bytes 1 | tf_op jit(solution)/shard_map/down/pallas_call | solution.py:113
  95.7 2.3 %down.8.refs_6_ = f32[256,1536]{1,0:T(8,128)S(1)} custom-call(s32[3]{0:T(128)S(1)} %pad_add_fusion.info, bf16[1,256,256]{2,1,0:T(8,128)(2,1)S(1)} %fusion.refs_0_, bf16[1,512,256]{2,1,0:T(8,128)(2,1)S(1)} %collective-permute-done.16.refs_1_, bf16[2,256,256]{2,1,0:T(8,128)(2,1)S(1)} %collective-permute-done.20.refs_2_, ...), custom_call_target="tpu_custom_call" | custom-call | flops 1 | bytes 1 | tf_op jit(solution)/shard_map/down/pallas_call | solution.py:113
  101.2 3.9 %collective-permute-start.23 = (bf16[32,1536]{1,0:T(8,128)(2,1)S(1)}, bf16[32,1536]{1,0:T(8,128)(2,1)S(1)}, u32[]{:S(2)}, u32[]{:S(2)}) collective-permute-start(bf16[32,1536]{1,0:T(8,128)(2,1)S(1)} %get-tuple-element.88), channel_id=1, source_target_pairs={{0,12},{4,0},{8,4},{12,8},{1,13},{5,1},{9,5},{13,9},{2,14},{6,2},{... | collective-permute-start | bytes 294920 | tf_op jit(solution)/shard_map/ppermute | solution.py:385
  105.2 3.1 %collective-permute-done.23 = bf16[32,1536]{1,0:T(8,128)(2,1)S(1)} collective-permute-done((bf16[32,1536]{1,0:T(8,128)(2,1)S(1)}, bf16[32,1536]{1,0:T(8,128)(2,1)S(1)}, u32[]{:S(2)}, u32[]{:S(2)}) %collective-permute-start.23) | collective-permute-done | bytes 98336 | tf_op jit(solution)/shard_map/ppermute | solution.py:385
  108.3 4.3 %collective-permute-start.24 = (bf16[64,1536]{1,0:T(8,128)(2,1)S(1)}, bf16[64,1536]{1,0:T(8,128)(2,1)S(1)}, u32[]{:S(2)}, u32[]{:S(2)}) collective-permute-start(bf16[64,1536]{1,0:T(8,128)(2,1)S(1)} %pad_maximum_fusion.7), channel_id=1, source_target_pairs={{0,12},{4,0},{8,4},{12,8},{1,13},{5,1},{9,5},{13,9},{2,14},{6,2},{... | collective-permute-start | bytes 589832 | tf_op jit(solution)/shard_map/ppermute | solution.py:394
  112.8 4.9 %collective-permute-done.24 = bf16[64,1536]{1,0:T(8,128)(2,1)S(1)} collective-permute-done((bf16[64,1536]{1,0:T(8,128)(2,1)S(1)}, bf16[64,1536]{1,0:T(8,128)(2,1)S(1)}, u32[]{:S(2)}, u32[]{:S(2)}) %collective-permute-start.24) | collective-permute-done | bytes 196640 | tf_op jit(solution)/shard_map/ppermute | solution.py:394
  117.7 2.9 %collective-permute-done.26 = bf16[64,1536]{1,0:T(8,128)(2,1)S(1)} collective-permute-done((bf16[64,1536]{1,0:T(8,128)(2,1)S(1)}, bf16[64,1536]{1,0:T(8,128)(2,1)S(1)}, u32[]{:S(2)}, u32[]{:S(2)}) %collective-permute-start.26) | collective-permute-done | bytes 196640 | tf_op jit(solution)/shard_map/ppermute | solution.py:395
  (89 shorter events, 14.0 us)
Async XLA Ops:
  0.0 19.2 %collective-permute-start = (bf16[64,1536]{1,0:T(8,128)(2,1)}, bf16[64,1536]{1,0:T(8,128)(2,1)S(1)}, u32[]{:S(2)}, u32[]{:S(2)}) collective-permute-start(bf16[64,1536]{1,0:T(8,128)(2,1)} %refs_0_.13), channel_id=1, source_target_pairs={{0,4},{4,8},{8,12},{12,0},{1,5},{5,9},{9,13},{13,1},{2,6},{6,10},{... | collective-permute-start | bytes 589832 | tf_op jit(solution)/shard_map/ppermute | solution.py:366
  3.0 16.2 %collective-permute-start.1 = (bf16[64,1536]{1,0:T(8,128)(2,1)}, bf16[64,1536]{1,0:T(8,128)(2,1)S(1)}, u32[]{:S(2)}, u32[]{:S(2)}) collective-permute-start(bf16[64,1536]{1,0:T(8,128)(2,1)} %refs_0_.13), channel_id=1, source_target_pairs={{0,12},{4,0},{8,4},{12,8},{1,13},{5,1},{9,5},{13,9},{2,14},{6,2},{... | collective-permute-start | bytes 589832 | tf_op jit(solution)/shard_map/ppermute | solution.py:366
  8.3 2.5 %copy-start.1 = (f32[64,8]{0,1:T(8,128)S(1)}, f32[64,8]{0,1:T(8,128)}, u32[]{:S(2)}) copy-start(f32[64,8]{0,1:T(8,128)} %param.8) | copy-start | bytes 6148
  8.3 17.4 %copy-start = (bf16[64,1536]{1,0:T(8,128)(2,1)S(1)}, bf16[64,1536]{1,0:T(8,128)(2,1)}, u32[]{:S(2)}) copy-start(bf16[64,1536]{1,0:T(8,128)(2,1)} %refs_0_.13) | copy-start | bytes 589828
  10.8 5.5 %collective-permute-start.2 = (f32[16,64]{1,0:T(8,128)S(1)}, f32[16,64]{1,0:T(8,128)S(1)}, u32[]{:S(2)}, u32[]{:S(2)}) collective-permute-start(f32[16,64]{1,0:T(8,128)S(1)} %pad_maximum_fusion.11.refs_0_), channel_id=1, source_target_pairs={{0,4},{4,8},{8,12},{12,0},{1,5},{5,9},{9,13},{13,1},{2,6},{6,10},{... | collective-permute-start | bytes 12296 | tf_op jit(solution)/shard_map/ppermute | solution.py:305
  10.8 5.4 %collective-permute-start.3 = (f32[16,64]{1,0:T(8,128)S(1)}, f32[16,64]{1,0:T(8,128)S(1)}, u32[]{:S(2)}, u32[]{:S(2)}) collective-permute-start(f32[16,64]{1,0:T(8,128)S(1)} %pad_maximum_fusion.11.refs_0_), channel_id=1, source_target_pairs={{0,12},{4,0},{8,4},{12,8},{1,13},{5,1},{9,5},{13,9},{2,14},{6,2},{... | collective-permute-start | bytes 12296 | tf_op jit(solution)/shard_map/ppermute | solution.py:305
  14.6 4.5 %collective-permute-start.4 = (f32[16,64]{1,0:T(8,128)S(1)}, f32[16,64]{1,0:T(8,128)S(1)}, u32[]{:S(2)}, u32[]{:S(2)}) collective-permute-start(f32[16,64]{1,0:T(8,128)S(1)} %pad_maximum_fusion.11.refs_0_), channel_id=1, source_target_pairs={{0,8},{4,12},{8,0},{12,4},{1,9},{5,13},{9,1},{13,5},{2,10},{6,14},... | collective-permute-start | bytes 12296 | tf_op jit(solution)/shard_map/ppermute | solution.py:305
  19.2 6.5 %collective-permute-start.5 = (bf16[32,1536]{1,0:T(8,128)(2,1)S(1)}, bf16[32,1536]{1,0:T(8,128)(2,1)S(1)}, u32[]{:S(2)}, u32[]{:S(2)}) collective-permute-start(bf16[32,1536]{1,0:T(8,128)(2,1)S(1)} %slice.125), channel_id=1, source_target_pairs={{0,4},{4,8},{8,12},{12,0},{1,5},{5,9},{9,13},{13,1},{2,6},{6,10},{... | collective-permute-start | bytes 294920 | tf_op jit(solution)/shard_map/ppermute | solution.py:371
  19.3 6.4 %collective-permute-start.6 = (bf16[32,1536]{1,0:T(8,128)(2,1)S(1)}, bf16[32,1536]{1,0:T(8,128)(2,1)S(1)}, u32[]{:S(2)}, u32[]{:S(2)}) collective-permute-start(bf16[32,1536]{1,0:T(8,128)(2,1)S(1)} %slice.126), channel_id=1, source_target_pairs={{0,12},{4,0},{8,4},{12,8},{1,13},{5,1},{9,5},{13,9},{2,14},{6,2},{... | collective-permute-start | bytes 294920 | tf_op jit(solution)/shard_map/ppermute | solution.py:371
  30.2 3.9 %collective-permute-start.7 = (bf16[2,256,256]{2,1,0:T(8,128)(2,1)S(1)}, bf16[2,256,256]{2,1,0:T(8,128)(2,1)S(1)}, u32[]{:S(2)}, u32[]{:S(2)}) collective-permute-start(bf16[2,256,256]{2,1,0:T(8,128)(2,1)S(1)} %get-tuple-element.55), channel_id=1, source_target_pairs={{0,1},{1,0},{2,3},{3,2},{4,5},{5,4},{6,7},{7,6},{8,9},{9,8},{10,11... | collective-permute-start | bytes 786440 | tf_op jit(solution)/shard_map/ppermute | solution.py:23
  34.2 10.8 %collective-permute-start.9 = (bf16[1,256,256]{2,1,0:T(8,128)(2,1)S(1)}, bf16[1,256,256]{2,1,0:T(8,128)(2,1)S(1)}, u32[]{:S(2)}, u32[]{:S(2)}) collective-permute-start(bf16[1,256,256]{2,1,0:T(8,128)(2,1)S(1)} %slice.230.refs_9_), channel_id=1, source_target_pairs={{0,2},{1,3},{2,0},{3,1},{4,6},{5,7},{6,4},{7,5},{8,10},{9,11},{10,... | collective-permute-start | bytes 393224 | tf_op jit(solution)/shard_map/ppermute | solution.py:23
  40.4 4.6 %collective-permute-start.8 = (bf16[2,512,256]{2,1,0:T(8,128)(2,1)S(1)}, bf16[2,512,256]{2,1,0:T(8,128)(2,1)S(1)}, u32[]{:S(2)}, u32[]{:S(2)}) collective-permute-start(bf16[2,512,256]{2,1,0:T(8,128)(2,1)S(1)} %get-tuple-element.60), channel_id=1, source_target_pairs={{0,1},{1,0},{2,3},{3,2},{4,5},{5,4},{6,7},{7,6},{8,9},{9,8},{10,11... | collective-permute-start | bytes 1572872 | tf_op jit(solution)/shard_map/ppermute | solution.py:23
  45.3 10.0 %collective-permute-start.11 = (bf16[1,640,256]{2,1,0:T(8,128)(2,1)S(1)}, bf16[1,640,256]{2,1,0:T(8,128)(2,1)S(1)}, u32[]{:S(2)}, u32[]{:S(2)}) collective-permute-start(bf16[1,640,256]{2,1,0:T(8,128)(2,1)S(1)} %pad_maximum_fusion.2.refs_9_), channel_id=1, source_target_pairs={{0,2},{1,3},{2,0},{3,1},{4,6},{5,7},{6,4},{7,5},{8,10},{9,11},{10,... | collective-permute-start | bytes 983048 | tf_op jit(solution)/shard_map/ppermute | solution.py:23
  50.1 5.3 %collective-permute-start.10 = (bf16[2,512,256]{2,1,0:T(8,128)(2,1)S(1)}, bf16[2,512,256]{2,1,0:T(8,128)(2,1)S(1)}, u32[]{:S(2)}, u32[]{:S(2)}) collective-permute-start(bf16[2,512,256]{2,1,0:T(8,128)(2,1)S(1)} %get-tuple-element.65), channel_id=1, source_target_pairs={{0,1},{1,0},{2,3},{3,2},{4,5},{5,4},{6,7},{7,6},{8,9},{9,8},{10,11... | collective-permute-start | bytes 1572872 | tf_op jit(solution)/shard_map/ppermute | solution.py:23
  55.6 10.8 %collective-permute-start.13 = (bf16[1,768,256]{2,1,0:T(8,128)(2,1)S(1)}, bf16[1,768,256]{2,1,0:T(8,128)(2,1)S(1)}, u32[]{:S(2)}, u32[]{:S(2)}) collective-permute-start(bf16[1,768,256]{2,1,0:T(8,128)(2,1)S(1)} %pad_maximum_fusion.refs_9_), channel_id=1, source_target_pairs={{0,2},{1,3},{2,0},{3,1},{4,6},{5,7},{6,4},{7,5},{8,10},{9,11},{10,... | collective-permute-start | bytes 1179656 | tf_op jit(solution)/shard_map/ppermute | solution.py:23
  60.1 6.4 %collective-permute-start.12 = (bf16[2,512,256]{2,1,0:T(8,128)(2,1)S(1)}, bf16[2,512,256]{2,1,0:T(8,128)(2,1)S(1)}, u32[]{:S(2)}, u32[]{:S(2)}) collective-permute-start(bf16[2,512,256]{2,1,0:T(8,128)(2,1)S(1)} %get-tuple-element.70), channel_id=1, source_target_pairs={{0,1},{1,0},{2,3},{3,2},{4,5},{5,4},{6,7},{7,6},{8,9},{9,8},{10,11... | collective-permute-start | bytes 1572872 | tf_op jit(solution)/shard_map/ppermute | solution.py:23
  70.4 5.7 %collective-permute-start.14 = (bf16[2,256,256]{2,1,0:T(8,128)(2,1)S(1)}, bf16[2,256,256]{2,1,0:T(8,128)(2,1)S(1)}, u32[]{:S(2)}, u32[]{:S(2)}) collective-permute-start(bf16[2,256,256]{2,1,0:T(8,128)(2,1)S(1)} %get-tuple-element.74), channel_id=1, source_target_pairs={{0,1},{1,0},{2,3},{3,2},{4,5},{5,4},{6,7},{7,6},{8,9},{9,8},{10,11... | collective-permute-start | bytes 786440 | tf_op jit(solution)/shard_map/ppermute | solution.py:23
  70.5 11.5 %collective-permute-start.15 = (bf16[1,768,256]{2,1,0:T(8,128)(2,1)S(1)}, bf16[1,768,256]{2,1,0:T(8,128)(2,1)S(1)}, u32[]{:S(2)}, u32[]{:S(2)}) collective-permute-start(bf16[1,768,256]{2,1,0:T(8,128)(2,1)S(1)} %pad_maximum_fusion.1.refs_8_), channel_id=1, source_target_pairs={{0,2},{1,3},{2,0},{3,1},{4,6},{5,7},{6,4},{7,5},{8,10},{9,11},{10,... | collective-permute-start | bytes 1179656 | tf_op jit(solution)/shard_map/ppermute | solution.py:23
  72.3 16.6 %collective-permute-start.17 = (bf16[2,256,256]{2,1,0:T(8,128)(2,1)S(1)}, bf16[2,256,256]{2,1,0:T(8,128)(2,1)S(1)}, u32[]{:S(2)}, u32[]{:S(2)}) collective-permute-start(bf16[2,256,256]{2,1,0:T(8,128)(2,1)S(1)} %pad_maximum_fusion.4), channel_id=1, source_target_pairs={{0,1},{1,0},{2,3},{3,2},{4,5},{5,4},{6,7},{7,6},{8,9},{9,8},{10,11... | collective-permute-start | bytes 786440 | tf_op jit(solution)/shard_map/ppermute | solution.py:23
  82.2 10.2 %collective-permute-start.16 = (bf16[1,512,256]{2,1,0:T(8,128)(2,1)S(1)}, bf16[1,512,256]{2,1,0:T(8,128)(2,1)S(1)}, u32[]{:S(2)}, u32[]{:S(2)}) collective-permute-start(bf16[1,512,256]{2,1,0:T(8,128)(2,1)S(1)} %pad_maximum_fusion.3.refs_7_), channel_id=1, source_target_pairs={{0,2},{1,3},{2,0},{3,1},{4,6},{5,7},{6,4},{7,5},{8,10},{9,11},{10,... | collective-permute-start | bytes 786440 | tf_op jit(solution)/shard_map/ppermute | solution.py:23
  84.0 1.4 %collective-permute-start.18 = (bf16[2,128,256]{2,1,0:T(8,128)(2,1)S(1)}, bf16[2,128,256]{2,1,0:T(8,128)(2,1)S(1)}, u32[]{:S(2)}, u32[]{:S(2)}) collective-permute-start(bf16[2,128,256]{2,1,0:T(8,128)(2,1)S(1)} %pad_maximum_fusion.9), channel_id=1, source_target_pairs={{0,1},{1,0},{2,3},{3,2},{4,5},{5,4},{6,7},{7,6},{8,9},{9,8},{10,11... | collective-permute-start | bytes 393224 | tf_op jit(solution)/shard_map/ppermute | solution.py:23
  84.2 9.0 %collective-permute-start.21 = (bf16[2,256,256]{2,1,0:T(8,128)(2,1)S(1)}, bf16[2,256,256]{2,1,0:T(8,128)(2,1)S(1)}, u32[]{:S(2)}, u32[]{:S(2)}) collective-permute-start(bf16[2,256,256]{2,1,0:T(8,128)(2,1)S(1)} %pad_maximum_fusion.6), channel_id=1, source_target_pairs={{0,1},{1,0},{2,3},{3,2},{4,5},{5,4},{6,7},{7,6},{8,9},{9,8},{10,11... | collective-permute-start | bytes 786440 | tf_op jit(solution)/shard_map/ppermute | solution.py:23
  92.5 3.2 %collective-permute-start.20 = (bf16[2,256,256]{2,1,0:T(8,128)(2,1)S(1)}, bf16[2,256,256]{2,1,0:T(8,128)(2,1)S(1)}, u32[]{:S(2)}, u32[]{:S(2)}) collective-permute-start(bf16[2,256,256]{2,1,0:T(8,128)(2,1)S(1)} %pad_maximum_fusion.5), channel_id=1, source_target_pairs={{0,1},{1,0},{2,3},{3,2},{4,5},{5,4},{6,7},{7,6},{8,9},{9,8},{10,11... | collective-permute-start | bytes 786440 | tf_op jit(solution)/shard_map/ppermute | solution.py:23
  92.8 5.2 %collective-permute-start.19 = (bf16[1,128,256]{2,1,0:T(8,128)(2,1)S(1)}, bf16[1,128,256]{2,1,0:T(8,128)(2,1)S(1)}, u32[]{:S(2)}, u32[]{:S(2)}) collective-permute-start(bf16[1,128,256]{2,1,0:T(8,128)(2,1)S(1)} %fusion.3.refs_8_.refs_7_.refs_0_), channel_id=1, source_target_pairs={{0,2},{1,3},{2,0},{3,1},{4,6},{5,7},{6,4},{7,5},{8,10},{9,11},{10,... | collective-permute-start | bytes 196616 | tf_op jit(solution)/shard_map/ppermute | solution.py:23
  98.0 1.4 %collective-permute-start.22 = (bf16[2,128,256]{2,1,0:T(8,128)(2,1)S(1)}, bf16[2,128,256]{2,1,0:T(8,128)(2,1)S(1)}, u32[]{:S(2)}, u32[]{:S(2)}) collective-permute-start(bf16[2,128,256]{2,1,0:T(8,128)(2,1)S(1)} %pad_maximum_fusion.10), channel_id=1, source_target_pairs={{0,1},{1,0},{2,3},{3,2},{4,5},{5,4},{6,7},{7,6},{8,9},{9,8},{10,11... | collective-permute-start | bytes 393224 | tf_op jit(solution)/shard_map/ppermute | solution.py:23
  101.2 7.1 %collective-permute-start.23 = (bf16[32,1536]{1,0:T(8,128)(2,1)S(1)}, bf16[32,1536]{1,0:T(8,128)(2,1)S(1)}, u32[]{:S(2)}, u32[]{:S(2)}) collective-permute-start(bf16[32,1536]{1,0:T(8,128)(2,1)S(1)} %get-tuple-element.88), channel_id=1, source_target_pairs={{0,12},{4,0},{8,4},{12,8},{1,13},{5,1},{9,5},{13,9},{2,14},{6,2},{... | collective-permute-start | bytes 294920 | tf_op jit(solution)/shard_map/ppermute | solution.py:385
  105.1 7.5 %collective-permute-start.25 = (bf16[32,1536]{1,0:T(8,128)(2,1)S(1)}, bf16[32,1536]{1,0:T(8,128)(2,1)S(1)}, u32[]{:S(2)}, u32[]{:S(2)}) collective-permute-start(bf16[32,1536]{1,0:T(8,128)(2,1)S(1)} %get-tuple-element.90), channel_id=1, source_target_pairs={{0,4},{4,8},{8,12},{12,0},{1,5},{5,9},{9,13},{13,1},{2,6},{6,10},{... | collective-permute-start | bytes 294920 | tf_op jit(solution)/shard_map/ppermute | solution.py:385
  108.3 9.3 %collective-permute-start.24 = (bf16[64,1536]{1,0:T(8,128)(2,1)S(1)}, bf16[64,1536]{1,0:T(8,128)(2,1)S(1)}, u32[]{:S(2)}, u32[]{:S(2)}) collective-permute-start(bf16[64,1536]{1,0:T(8,128)(2,1)S(1)} %pad_maximum_fusion.7), channel_id=1, source_target_pairs={{0,12},{4,0},{8,4},{12,8},{1,13},{5,1},{9,5},{13,9},{2,14},{6,2},{... | collective-permute-start | bytes 589832 | tf_op jit(solution)/shard_map/ppermute | solution.py:394
  112.7 7.8 %collective-permute-start.26 = (bf16[64,1536]{1,0:T(8,128)(2,1)S(1)}, bf16[64,1536]{1,0:T(8,128)(2,1)S(1)}, u32[]{:S(2)}, u32[]{:S(2)}) collective-permute-start(bf16[64,1536]{1,0:T(8,128)(2,1)S(1)} %pad_maximum_fusion.8), channel_id=1, source_target_pairs={{0,4},{4,8},{8,12},{12,0},{1,5},{5,9},{9,13},{13,1},{2,6},{6,10},{... | collective-permute-start | bytes 589832 | tf_op jit(solution)/shard_map/ppermute | solution.py:395

commit v10 on v7

--- a/solution.py
+++ b/solution.py
@@ -292,19 +292,18 @@
     given = {0: stage(info, weights, needs[0], [])}
 
     def fetched(k, outs):
-        if k + 2 < len(needs):
-            *outs, given[k + 2] = outs
+        if k + 1 < len(needs):
+            *outs, given[k + 1] = outs
         return outs
 
-    ahead = lambda k: needs[k + 2] if k + 2 < len(needs) else None
+    ahead = lambda k: needs[k + 1] if k + 1 < len(needs) else None
 
     meta = lax.optimization_barrier((meta, given[0]))[0]
     metas = [meta] + [
         lax.ppermute(meta, "expert", [(i, (i - k) % n_owner) for i in range(n_owner)])
         for k in gathered_order(n_owner)[1:]
     ]
-    feeds, halfway = gathered(tokens, "expert", metas)
-    given[1] = stage(info, weights, needs[1], halfway)
+    feeds = gathered(tokens, "expert", metas)
     rank, wt = route(metas, info, experts)
 
     tall, wide = [feed.shape[0] for feed in feeds], tokens.shape[1]
@@ -323,7 +322,7 @@
         last = c == chunks - 1
         k = 2 * c
         send, rows = fetched(
-            k, send_half(feeds, rank, info, given[k], weights, of(c), most, n_dp, ahead(k), sent[-1:] or [given[1]])
+            k, send_half(feeds, rank, info, given[k], weights, of(c), most, n_dp, ahead(k), sent[-1:])
         )
         k = 2 * c + 1
         (keep,) = fetched(k, keep_half(rows, info, given[k], weights, most, n_dp, ahead(k)))
@@ -360,16 +359,15 @@
     n = lax.axis_size(axis)
     up, down_ = [(i, (i + 1) % n) for i in range(n)], [(i, (i - 1) % n) for i in range(n)]
     below = above = x
-    found, halfway = [x], []
+    found = [x]
     for _ in range(1, n // 2):
         below, above = lax.ppermute(below, axis, up), lax.ppermute(above, axis, down_)
         found += [below, above]
     if n > 1:
         half = x.shape[0] // 2
         below, above, *_ = lax.optimization_barrier((below, above, *beside))
-        halfway = [below]
         found += [lax.ppermute(below[:half], axis, up), lax.ppermute(above[half:], axis, down_)]
-    return found, halfway
+    return found
 
 
 def returned(partials, axis):

time: 108 us -> 107 us (level)
  Pallas kernels: 53.5 us -> 51.3 us
  starting transfers between devices: 25.4 us -> 27.4 us
    pallas_call x14 -> x13, Pallas kernels: 52.8 us -> 50.5 us  [call(): pl.pallas_call(whole, out_shape=tuple(outs), in_specs=[SMEM] + [spec for...]
    ppermute x1, waiting for transfers between devices: 0.01 us -> 1.79 us  [gathered(): lax.ppermute(below[:half], axis, up)]
    ppermute x13, waiting for transfers between devices: 9.51 us -> 7.78 us  [flip(): lax.ppermute(x, axis, [(i, i ^ k) for i in range(lax.axis_size(axis))])]
    ppermute x1, starting transfers between devices: 2.27 us -> 3.94 us  [returned(): lax.ppermute(partials[-2], axis, down_)]
  transfers between devices with their start and end apart: 24 -> 24, of which waited for: 11 -> 12; matrix products, arithmetic and copies ran while one was open for 1% -> 1% of each run, Pallas kernels for 43% -> 42%
where the time goes in v10:
time: 107 us
  Pallas kernels  51.3 us (48%)
  starting transfers between devices  27.4 us (26%)
  waiting for transfers between devices  24.9 us (23%)
  other arithmetic  2.99 us (3%)
    pallas_call x13, Pallas kernels, call(): pl.pallas_call(whole, out_shape=tuple(outs), in_specs=[SMEM] + [spec for...  50.5 us
    ppermute x13, waiting for transfers between devices, flip(): lax.ppermute(x, axis, [(i, i ^ k) for i in range(lax.axis_size(axis))])  7.78 us
    ppermute x13, starting transfers between devices, flip(): lax.ppermute(x, axis, [(i, i ^ k) for i in range(lax.axis_size(axis))])  6.18 us
    ppermute x1, waiting for transfers between devices, returned(): low = lax.ppermute(a.astype(jnp.bfloat16), axis, down_)  4.85 us
    ppermute x3, waiting for transfers between devices, on_device(): lax.ppermute(meta, 'expert', [(i, (i - k) % n_owner) for i in range(n_own...  4.55 us
    ppermute x1, starting transfers between devices, returned(): low = lax.ppermute(a.astype(jnp.bfloat16), axis, down_)  4.33 us
    ppermute x1, starting transfers between devices, returned(): lax.ppermute(partials[-2], axis, down_)  3.94 us
    ppermute x3, starting transfers between devices, on_device(): lax.ppermute(meta, 'expert', [(i, (i - k) % n_owner) for i in range(n_own...  3.87 us
  transfers between devices with their start and end apart: 24, of which 12 were waited for; matrix products, arithmetic and copies ran while one was open for 1% of the time, Pallas kernels for 42%

profile of v10, /device:TPU:0, one launch (start us, length us, event | category | flops | bytes accessed | tf_op | source)
XLA Modules:
  0.0 107.3 jit_solution(2498491601881607078)
XLA Ops:
  0.0 3.0 %collective-permute-start = (bf16[64,1536]{1,0:T(8,128)(2,1)}, bf16[64,1536]{1,0:T(8,128)(2,1)S(1)}, u32[]{:S(2)}, u32[]{:S(2)}) collective-permute-start(bf16[64,1536]{1,0:T(8,128)(2,1)} %refs_0_.9), channel_id=1, source_target_pairs={{0,4},{4,8},{8,12},{12,0},{1,5},{5,9},{9,13},{13,1},{2,6},{6,10},{... | collective-permute-start | bytes 589832 | tf_op jit(solution)/shard_map/ppermute | solution.py:364
  3.0 2.0 %collective-permute-start.1 = (bf16[64,1536]{1,0:T(8,128)(2,1)}, bf16[64,1536]{1,0:T(8,128)(2,1)S(1)}, u32[]{:S(2)}, u32[]{:S(2)}) collective-permute-start(bf16[64,1536]{1,0:T(8,128)(2,1)} %refs_0_.9), channel_id=1, source_target_pairs={{0,12},{4,0},{8,4},{12,8},{1,13},{5,1},{9,5},{13,9},{2,14},{6,2},{... | collective-permute-start | bytes 589832 | tf_op jit(solution)/shard_map/ppermute | solution.py:364
  5.8 3.4 %stage.1.refs_6_ = bf16[2,2,1536,512]{3,2,1,0:T(8,128)(2,1)S(1)} custom-call(s32[3]{0:T(128)S(1)} %pad_add_fusion.info, bf16[8,1536,1024]{2,1,0:T(8,128)(2,1)} %refs_7_.9, bf16[8,1536,1024]{2,1,0:T(8,128)(2,1)} %refs_8_.7), custom_call_target="tpu_custom_call" | custom-call | flops 1 | bytes 1 | tf_op jit(solution)/shard_map/stage/pallas_call | solution.py:113
  9.3 3.8 %collective-permute-start.3 = (f32[16,64]{1,0:T(8,128)S(1)}, f32[16,64]{1,0:T(8,128)S(1)}, u32[]{:S(2)}, u32[]{:S(2)}) collective-permute-start(f32[16,64]{1,0:T(8,128)S(1)} %pad_maximum_fusion.9.refs_0_), channel_id=1, source_target_pairs={{0,12},{4,0},{8,4},{12,8},{1,13},{5,1},{9,5},{13,9},{2,14},{6,2},{... | collective-permute-start | bytes 12296 | tf_op jit(solution)/shard_map/ppermute | solution.py:303
  13.1 1.7 %collective-permute-done.2.refs_1_ = f32[16,64]{1,0:T(8,128)S(1)} collective-permute-done((f32[16,64]{1,0:T(8,128)S(1)}, f32[16,64]{1,0:T(8,128)S(1)}, u32[]{:S(2)}, u32[]{:S(2)}) %collective-permute-start.2) | collective-permute-done | bytes 4128 | tf_op jit(solution)/shard_map/ppermute | solution.py:303
  14.8 2.9 %collective-permute-done.4.refs_3_ = f32[16,64]{1,0:T(8,128)S(1)} collective-permute-done((f32[16,64]{1,0:T(8,128)S(1)}, f32[16,64]{1,0:T(8,128)S(1)}, u32[]{:S(2)}, u32[]{:S(2)}) %collective-permute-start.4) | collective-permute-done | bytes 4128 | tf_op jit(solution)/shard_map/ppermute | solution.py:303
  17.8 3.9 %collective-permute-start.6 = (bf16[32,1536]{1,0:T(8,128)(2,1)S(1)}, bf16[32,1536]{1,0:T(8,128)(2,1)S(1)}, u32[]{:S(2)}, u32[]{:S(2)}) collective-permute-start(bf16[32,1536]{1,0:T(8,128)(2,1)S(1)} %slice.105), channel_id=1, source_target_pairs={{0,12},{4,0},{8,4},{12,8},{1,13},{5,1},{9,5},{13,9},{2,14},{6,2},{... | collective-permute-start | bytes 294920 | tf_op jit(solution)/shard_map/ppermute | solution.py:369
  22.4 1.8 %collective-permute-done.5.refs_3_ = bf16[32,1536]{1,0:T(8,128)(2,1)S(1)} collective-permute-done((bf16[32,1536]{1,0:T(8,128)(2,1)S(1)}, bf16[32,1536]{1,0:T(8,128)(2,1)S(1)}, u32[]{:S(2)}, u32[]{:S(2)}) %collective-permute-start.5) | collective-permute-done | bytes 98336 | tf_op jit(solution)/shard_map/ppermute | solution.py:369
  24.2 4.5 %send_half.4 = (bf16[2,256,512]{2,1,0:T(8,128)(2,1)S(1)}, bf16[256,1536]{1,0:T(8,128)(2,1)S(1)}, bf16[2,2,1536,512]{3,2,1,0:T(8,128)(2,1)S(1)}) custom-call(s32[3]{0:T(128)S(1)} %pad_add_fusion.info, bf16[64,1536]{1,0:T(8,128)(2,1)S(1)} %copy-done, bf16[64,1536]{1,0:T(8,128)(2,1)S(1)} %collective-permute-done.refs_1_, ...), custom_call_target="tpu_custom_call" | custom-call | flops 1 | bytes 1 | tf_op jit(solution)/shard_map/send_half/pallas_call | solution.py:113
  28.7 4.2 %keep_half.4 = (bf16[2,256,512]{2,1,0:T(8,128)(2,1)S(1)}, bf16[2,2,1536,512]{3,2,1,0:T(8,128)(2,1)S(1)}) custom-call(s32[3]{0:T(128)S(1)} %pad_add_fusion.info, bf16[256,1536]{1,0:T(8,128)(2,1)S(1)} %get-tuple-element.47.refs_0_, bf16[2,2,1536,512]{3,2,1,0:T(8,128)(2,1)S(1)} %get-tuple-element.48.refs_1_, bf16[8,1536,1024]{2,1,0:T(8,128)(2,1)} %refs_7_.9, ...), custom_call_target="tpu_custom_call" | custom-call | flops 1 | bytes 1 | tf_op jit(solution)/shard_map/keep_half/pallas_call | solution.py:113
  33.2 1.8 %collective-permute-start.9 = (bf16[1,256,512]{2,1,0:T(8,128)(2,1)S(1)}, bf16[1,256,512]{2,1,0:T(8,128)(2,1)S(1)}, u32[]{:S(2)}, u32[]{:S(2)}) collective-permute-start(bf16[1,256,512]{2,1,0:T(8,128)(2,1)S(1)} %slice.189.refs_9_), channel_id=1, source_target_pairs={{0,2},{1,3},{2,0},{3,1},{4,6},{5,7},{6,4},{7,5},{8,10},{9,11},{10,... | collective-permute-start | bytes 786440 | tf_op jit(solution)/shard_map/ppermute | solution.py:23
  35.0 4.6 %send_half.5 = (bf16[2,256,512]{2,1,0:T(8,128)(2,1)S(1)}, bf16[256,1536]{1,0:T(8,128)(2,1)S(1)}, bf16[2,2,1536,512]{3,2,1,0:T(8,128)(2,1)S(1)}) custom-call(s32[3]{0:T(128)S(1)} %pad_add_fusion.info, bf16[64,1536]{1,0:T(8,128)(2,1)S(1)} %copy-done, bf16[64,1536]{1,0:T(8,128)(2,1)S(1)} %collective-permute-done.refs_1_, ...), custom_call_target="tpu_custom_call" | custom-call | flops 1 | bytes 1 | tf_op jit(solution)/shard_map/send_half/pallas_call | solution.py:113
  39.8 4.2 %keep_half.5 = (bf16[2,256,512]{2,1,0:T(8,128)(2,1)S(1)}, bf16[2,2,1536,512]{3,2,1,0:T(8,128)(2,1)S(1)}) custom-call(s32[3]{0:T(128)S(1)} %pad_add_fusion.info, bf16[256,1536]{1,0:T(8,128)(2,1)S(1)} %get-tuple-element.52.refs_0_, bf16[2,2,1536,512]{3,2,1,0:T(8,128)(2,1)S(1)} %get-tuple-element.53.refs_1_, bf16[8,1536,1024]{2,1,0:T(8,128)(2,1)} %refs_7_.9, ...), custom_call_target="tpu_custom_call" | custom-call | flops 1 | bytes 1 | tf_op jit(solution)/shard_map/keep_half/pallas_call | solution.py:113
  44.9 4.5 %send_half.6 = (bf16[2,256,512]{2,1,0:T(8,128)(2,1)S(1)}, bf16[256,1536]{1,0:T(8,128)(2,1)S(1)}, bf16[2,2,1536,512]{3,2,1,0:T(8,128)(2,1)S(1)}) custom-call(s32[3]{0:T(128)S(1)} %pad_add_fusion.info, bf16[64,1536]{1,0:T(8,128)(2,1)S(1)} %copy-done, bf16[64,1536]{1,0:T(8,128)(2,1)S(1)} %collective-permute-done.refs_1_, ...), custom_call_target="tpu_custom_call" | custom-call | flops 1 | bytes 1 | tf_op jit(solution)/shard_map/send_half/pallas_call | solution.py:113
  49.4 4.2 %keep_half.6 = (bf16[2,256,512]{2,1,0:T(8,128)(2,1)S(1)}, bf16[2,2,1536,512]{3,2,1,0:T(8,128)(2,1)S(1)}) custom-call(s32[3]{0:T(128)S(1)} %pad_add_fusion.info, bf16[256,1536]{1,0:T(8,128)(2,1)S(1)} %get-tuple-element.57.refs_0_, bf16[2,2,1536,512]{3,2,1,0:T(8,128)(2,1)S(1)} %get-tuple-element.58.refs_1_, bf16[8,1536,1024]{2,1,0:T(8,128)(2,1)} %refs_7_.9, ...), custom_call_target="tpu_custom_call" | custom-call | flops 1 | bytes 1 | tf_op jit(solution)/shard_map/keep_half/pallas_call | solution.py:113
  53.7 2.2 %collective-permute-done.11.refs_1_ = bf16[1,256,768]{2,1,0:T(8,128)(2,1)S(1)} collective-permute-done((bf16[1,256,768]{2,1,0:T(8,128)(2,1)S(1)}, bf16[1,256,768]{2,1,0:T(8,128)(2,1)S(1)}, u32[]{:S(2)}, u32[]{:S(2)}) %collective-permute-start.11) | collective-permute-done | bytes 393248 | tf_op jit(solution)/shard_map/ppermute | solution.py:23
  56.7 4.6 %send_half.7 = (bf16[2,256,512]{2,1,0:T(8,128)(2,1)S(1)}, bf16[256,1536]{1,0:T(8,128)(2,1)S(1)}, bf16[2,2,1536,512]{3,2,1,0:T(8,128)(2,1)S(1)}) custom-call(s32[3]{0:T(128)S(1)} %pad_add_fusion.info, bf16[64,1536]{1,0:T(8,128)(2,1)S(1)} %copy-done, bf16[64,1536]{1,0:T(8,128)(2,1)S(1)} %collective-permute-done.refs_1_, ...), custom_call_target="tpu_custom_call" | custom-call | flops 1 | bytes 1 | tf_op jit(solution)/shard_map/send_half/pallas_call | solution.py:113
  61.4 3.6 %keep_half.7 = (bf16[2,256,512]{2,1,0:T(8,128)(2,1)S(1)}, bf16[2,1024,1536]{2,1,0:T(8,128)(2,1)S(1)}) custom-call(s32[3]{0:T(128)S(1)} %pad_add_fusion.info, bf16[256,1536]{1,0:T(8,128)(2,1)S(1)} %get-tuple-element.62.refs_0_, bf16[2,2,1536,512]{3,2,1,0:T(8,128)(2,1)S(1)} %get-tuple-element.63.refs_1_, bf16[8,1024,1536]{2,1,0:T(8,128)(2,1)} %refs_7_.11), custom_call_target="tpu_custom_call" | custom-call | flops 1 | bytes 1 | tf_op jit(solution)/shard_map/keep_half/pallas_call | solution.py:113
  65.1 1.8 %collective-permute-done.13.refs_1_ = bf16[1,256,768]{2,1,0:T(8,128)(2,1)S(1)} collective-permute-done((bf16[1,256,768]{2,1,0:T(8,128)(2,1)S(1)}, bf16[1,256,768]{2,1,0:T(8,128)(2,1)S(1)}, u32[]{:S(2)}, u32[]{:S(2)}) %collective-permute-start.13) | collective-permute-done | bytes 393248 | tf_op jit(solution)/shard_map/ppermute | solution.py:23
  68.6 0.9 collective-permute-done.16.refs_2_
  69.5 3.4 %down.4 = (f32[256,1536]{1,0:T(8,128)S(1)}, bf16[2,1024,1536]{2,1,0:T(8,128)(2,1)S(1)}) custom-call(s32[3]{0:T(128)S(1)} %pad_add_fusion.info, bf16[1,256,256]{2,1,0:T(8,128)(2,1)S(1)} %fusion.3.refs_0_, bf16[1,256,768]{2,1,0:T(8,128)(2,1)S(1)} %copy-done.2, bf16[2,256,256]{2,1,0:T(8,128)(2,1)S(1)} %collective-permute-done.16.refs_2_, ...), custom_call_target="tpu_custom_call" | custom-call | flops 1 | bytes 1 | tf_op jit(solution)/shard_map/down/pallas_call | solution.py:113
  72.9 3.5 %down.5 = (f32[256,1536]{1,0:T(8,128)S(1)}, bf16[2,1024,1536]{2,1,0:T(8,128)(2,1)S(1)}) custom-call(s32[3]{0:T(128)S(1)} %pad_add_fusion.info, bf16[1,256,256]{2,1,0:T(8,128)(2,1)S(1)} %fusion.2.refs_0_, bf16[1,256,768]{2,1,0:T(8,128)(2,1)S(1)} %collective-permute-done.13.refs_1_, bf16[2,256,256]{2,1,0:T(8,128)(2,1)S(1)} %collective-permute-done.15.refs_2_, ...), custom_call_target="tpu_custom_call" | custom-call | flops 1 | bytes 1 | tf_op jit(solution)/shard_map/down/pallas_call | solution.py:113
  77.4 1.8 %collective-permute-start.17 = (bf16[1,256,256]{2,1,0:T(8,128)(2,1)S(1)}, bf16[1,256,256]{2,1,0:T(8,128)(2,1)S(1)}, u32[]{:S(2)}, u32[]{:S(2)}) collective-permute-start(bf16[1,256,256]{2,1,0:T(8,128)(2,1)S(1)} %fusion.refs_8_.refs_0_), channel_id=1, source_target_pairs={{0,2},{1,3},{2,0},{3,1},{4,6},{5,7},{6,4},{7,5},{8,10},{9,11},{10,... | collective-permute-start | bytes 393224 | tf_op jit(solution)/shard_map/ppermute | solution.py:23
  79.2 3.5 %down.6 = (f32[256,1536]{1,0:T(8,128)S(1)}, bf16[2,1024,1536]{2,1,0:T(8,128)(2,1)S(1)}) custom-call(s32[3]{0:T(128)S(1)} %pad_add_fusion.info, bf16[1,256,256]{2,1,0:T(8,128)(2,1)S(1)} %fusion.1.refs_0_, bf16[1,256,768]{2,1,0:T(8,128)(2,1)S(1)} %collective-permute-done.14.refs_1_, bf16[2,256,256]{2,1,0:T(8,128)(2,1)S(1)} %collective-permute-done.18.refs_2_, ...), custom_call_target="tpu_custom_call" | custom-call | flops 1 | bytes 1 | tf_op jit(solution)/shard_map/down/pallas_call | solution.py:113
  83.4 1.5 %collective-permute-done.19.refs_2_ = bf16[2,256,256]{2,1,0:T(8,128)(2,1)S(1)} collective-permute-done((bf16[2,256,256]{2,1,0:T(8,128)(2,1)S(1)}, bf16[2,256,256]{2,1,0:T(8,128)(2,1)S(1)}, u32[]{:S(2)}, u32[]{:S(2)}) %collective-permute-start.19) | collective-permute-done | bytes 262176 | tf_op jit(solution)/shard_map/ppermute | solution.py:23
  85.0 2.2 %down.7 = (bf16[64,1536]{1,0:T(8,128)(2,1)S(1)}, bf16[64,1536]{1,0:T(8,128)(2,1)S(1)}, bf16[64,1536]{1,0:T(8,128)(2,1)S(1)}, bf16[32,1536]{1,0:T(8,128)(2,1)S(1)}, bf16[32,1536]{1,0:T(8,128)(2,1)S(1)}) custom-call(s32[3]{0:T(128)S(1)} %pad_add_fusion.info, bf16[1,256,256]{2,1,0:T(8,128)(2,1)S(1)} %fusion.refs_8_.refs_0_, ...), custom_call_target="tpu_custom_call" | custom-call | flops 1 | bytes 1 | tf_op jit(solution)/shard_map/down/pallas_call | solution.py:113
  87.2 3.9 %collective-permute-start.20 = (bf16[32,1536]{1,0:T(8,128)(2,1)S(1)}, bf16[32,1536]{1,0:T(8,128)(2,1)S(1)}, u32[]{:S(2)}, u32[]{:S(2)}) collective-permute-start(bf16[32,1536]{1,0:T(8,128)(2,1)S(1)} %get-tuple-element.78), channel_id=1, source_target_pairs={{0,12},{4,0},{8,4},{12,8},{1,13},{5,1},{9,5},{13,9},{2,14},{6,2},{... | collective-permute-start | bytes 294920 | tf_op jit(solution)/shard_map/ppermute | solution.py:383
  91.3 3.1 %collective-permute-done.20 = bf16[32,1536]{1,0:T(8,128)(2,1)S(1)} collective-permute-done((bf16[32,1536]{1,0:T(8,128)(2,1)S(1)}, bf16[32,1536]{1,0:T(8,128)(2,1)S(1)}, u32[]{:S(2)}, u32[]{:S(2)}) %collective-permute-start.20) | collective-permute-done | bytes 98336 | tf_op jit(solution)/shard_map/ppermute | solution.py:383
  94.4 4.3 %collective-permute-start.21 = (bf16[64,1536]{1,0:T(8,128)(2,1)S(1)}, bf16[64,1536]{1,0:T(8,128)(2,1)S(1)}, u32[]{:S(2)}, u32[]{:S(2)}) collective-permute-start(bf16[64,1536]{1,0:T(8,128)(2,1)S(1)} %pad_maximum_fusion.7), channel_id=1, source_target_pairs={{0,12},{4,0},{8,4},{12,8},{1,13},{5,1},{9,5},{13,9},{2,14},{6,2},{... | collective-permute-start | bytes 589832 | tf_op jit(solution)/shard_map/ppermute | solution.py:392
  98.8 4.9 %collective-permute-done.21 = bf16[64,1536]{1,0:T(8,128)(2,1)S(1)} collective-permute-done((bf16[64,1536]{1,0:T(8,128)(2,1)S(1)}, bf16[64,1536]{1,0:T(8,128)(2,1)S(1)}, u32[]{:S(2)}, u32[]{:S(2)}) %collective-permute-start.21) | collective-permute-done | bytes 196640 | tf_op jit(solution)/shard_map/ppermute | solution.py:392
  103.7 2.9 %collective-permute-done.23 = bf16[64,1536]{1,0:T(8,128)(2,1)S(1)} collective-permute-done((bf16[64,1536]{1,0:T(8,128)(2,1)S(1)}, bf16[64,1536]{1,0:T(8,128)(2,1)S(1)}, u32[]{:S(2)}, u32[]{:S(2)}) %collective-permute-start.23) | collective-permute-done | bytes 196640 | tf_op jit(solution)/shard_map/ppermute | solution.py:393
  106.6 0.8 add_convert_fusion
  (78 shorter events, 7.4 us)
Async XLA Ops:
  0.0 17.7 %collective-permute-start = (bf16[64,1536]{1,0:T(8,128)(2,1)}, bf16[64,1536]{1,0:T(8,128)(2,1)S(1)}, u32[]{:S(2)}, u32[]{:S(2)}) collective-permute-start(bf16[64,1536]{1,0:T(8,128)(2,1)} %refs_0_.9), channel_id=1, source_target_pairs={{0,4},{4,8},{8,12},{12,0},{1,5},{5,9},{9,13},{13,1},{2,6},{6,10},{... | collective-permute-start | bytes 589832 | tf_op jit(solution)/shard_map/ppermute | solution.py:364
  3.0 14.7 %collective-permute-start.1 = (bf16[64,1536]{1,0:T(8,128)(2,1)}, bf16[64,1536]{1,0:T(8,128)(2,1)S(1)}, u32[]{:S(2)}, u32[]{:S(2)}) collective-permute-start(bf16[64,1536]{1,0:T(8,128)(2,1)} %refs_0_.9), channel_id=1, source_target_pairs={{0,12},{4,0},{8,4},{12,8},{1,13},{5,1},{9,5},{13,9},{2,14},{6,2},{... | collective-permute-start | bytes 589832 | tf_op jit(solution)/shard_map/ppermute | solution.py:364
  5.8 3.4 %copy-start.3 = (f32[64,8]{0,1:T(8,128)S(1)}, f32[64,8]{0,1:T(8,128)}, u32[]{:S(2)}) copy-start(f32[64,8]{0,1:T(8,128)} %param.8) | copy-start | bytes 6148
  5.8 18.4 %copy-start = (bf16[64,1536]{1,0:T(8,128)(2,1)S(1)}, bf16[64,1536]{1,0:T(8,128)(2,1)}, u32[]{:S(2)}) copy-start(bf16[64,1536]{1,0:T(8,128)(2,1)} %refs_0_.9) | copy-start | bytes 589828
  9.3 5.5 %collective-permute-start.2 = (f32[16,64]{1,0:T(8,128)S(1)}, f32[16,64]{1,0:T(8,128)S(1)}, u32[]{:S(2)}, u32[]{:S(2)}) collective-permute-start(f32[16,64]{1,0:T(8,128)S(1)} %pad_maximum_fusion.9.refs_0_), channel_id=1, source_target_pairs={{0,4},{4,8},{8,12},{12,0},{1,5},{5,9},{9,13},{13,1},{2,6},{6,10},{... | collective-permute-start | bytes 12296 | tf_op jit(solution)/shard_map/ppermute | solution.py:303
  9.3 5.5 %collective-permute-start.3 = (f32[16,64]{1,0:T(8,128)S(1)}, f32[16,64]{1,0:T(8,128)S(1)}, u32[]{:S(2)}, u32[]{:S(2)}) collective-permute-start(f32[16,64]{1,0:T(8,128)S(1)} %pad_maximum_fusion.9.refs_0_), channel_id=1, source_target_pairs={{0,12},{4,0},{8,4},{12,8},{1,13},{5,1},{9,5},{13,9},{2,14},{6,2},{... | collective-permute-start | bytes 12296 | tf_op jit(solution)/shard_map/ppermute | solution.py:303
  13.1 4.5 %collective-permute-start.4 = (f32[16,64]{1,0:T(8,128)S(1)}, f32[16,64]{1,0:T(8,128)S(1)}, u32[]{:S(2)}, u32[]{:S(2)}) collective-permute-start(f32[16,64]{1,0:T(8,128)S(1)} %pad_maximum_fusion.9.refs_0_), channel_id=1, source_target_pairs={{0,8},{4,12},{8,0},{12,4},{1,9},{5,13},{9,1},{13,5},{2,10},{6,14},... | collective-permute-start | bytes 12296 | tf_op jit(solution)/shard_map/ppermute | solution.py:303
  17.7 6.5 %collective-permute-start.5 = (bf16[32,1536]{1,0:T(8,128)(2,1)S(1)}, bf16[32,1536]{1,0:T(8,128)(2,1)S(1)}, u32[]{:S(2)}, u32[]{:S(2)}) collective-permute-start(bf16[32,1536]{1,0:T(8,128)(2,1)S(1)} %slice.104), channel_id=1, source_target_pairs={{0,4},{4,8},{8,12},{12,0},{1,5},{5,9},{9,13},{13,1},{2,6},{6,10},{... | collective-permute-start | bytes 294920 | tf_op jit(solution)/shard_map/ppermute | solution.py:369
  17.8 6.4 %collective-permute-start.6 = (bf16[32,1536]{1,0:T(8,128)(2,1)S(1)}, bf16[32,1536]{1,0:T(8,128)(2,1)S(1)}, u32[]{:S(2)}, u32[]{:S(2)}) collective-permute-start(bf16[32,1536]{1,0:T(8,128)(2,1)S(1)} %slice.105), channel_id=1, source_target_pairs={{0,12},{4,0},{8,4},{12,8},{1,13},{5,1},{9,5},{13,9},{2,14},{6,2},{... | collective-permute-start | bytes 294920 | tf_op jit(solution)/shard_map/ppermute | solution.py:369
  28.7 4.3 %collective-permute-start.7 = (bf16[2,256,512]{2,1,0:T(8,128)(2,1)S(1)}, bf16[2,256,512]{2,1,0:T(8,128)(2,1)S(1)}, u32[]{:S(2)}, u32[]{:S(2)}) collective-permute-start(bf16[2,256,512]{2,1,0:T(8,128)(2,1)S(1)} %get-tuple-element.51), channel_id=1, source_target_pairs={{0,1},{1,0},{2,3},{3,2},{4,5},{5,4},{6,7},{7,6},{8,9},{9,8},{10,11... | collective-permute-start | bytes 1572872 | tf_op jit(solution)/shard_map/ppermute | solution.py:23
  33.2 10.9 %collective-permute-start.9 = (bf16[1,256,512]{2,1,0:T(8,128)(2,1)S(1)}, bf16[1,256,512]{2,1,0:T(8,128)(2,1)S(1)}, u32[]{:S(2)}, u32[]{:S(2)}) collective-permute-start(bf16[1,256,512]{2,1,0:T(8,128)(2,1)S(1)} %slice.189.refs_9_), channel_id=1, source_target_pairs={{0,2},{1,3},{2,0},{3,1},{4,6},{5,7},{6,4},{7,5},{8,10},{9,11},{10,... | collective-permute-start | bytes 786440 | tf_op jit(solution)/shard_map/ppermute | solution.py:23
  39.6 4.7 %collective-permute-start.8 = (bf16[2,256,512]{2,1,0:T(8,128)(2,1)S(1)}, bf16[2,256,512]{2,1,0:T(8,128)(2,1)S(1)}, u32[]{:S(2)}, u32[]{:S(2)}) collective-permute-start(bf16[2,256,512]{2,1,0:T(8,128)(2,1)S(1)} %get-tuple-element.56), channel_id=1, source_target_pairs={{0,1},{1,0},{2,3},{3,2},{4,5},{5,4},{6,7},{7,6},{8,9},{9,8},{10,11... | collective-permute-start | bytes 1572872 | tf_op jit(solution)/shard_map/ppermute | solution.py:23
  44.5 11.4 %collective-permute-start.11 = (bf16[1,256,768]{2,1,0:T(8,128)(2,1)S(1)}, bf16[1,256,768]{2,1,0:T(8,128)(2,1)S(1)}, u32[]{:S(2)}, u32[]{:S(2)}) collective-permute-start(bf16[1,256,768]{2,1,0:T(8,128)(2,1)S(1)} %pad_maximum_fusion.refs_9_), channel_id=1, source_target_pairs={{0,2},{1,3},{2,0},{3,1},{4,6},{5,7},{6,4},{7,5},{8,10},{9,11},{10,... | collective-permute-start | bytes 1179656 | tf_op jit(solution)/shard_map/ppermute | solution.py:23
  49.3 6.7 %collective-permute-start.10 = (bf16[2,256,512]{2,1,0:T(8,128)(2,1)S(1)}, bf16[2,256,512]{2,1,0:T(8,128)(2,1)S(1)}, u32[]{:S(2)}, u32[]{:S(2)}) collective-permute-start(bf16[2,256,512]{2,1,0:T(8,128)(2,1)S(1)} %get-tuple-element.61), channel_id=1, source_target_pairs={{0,1},{1,0},{2,3},{3,2},{4,5},{5,4},{6,7},{7,6},{8,9},{9,8},{10,11... | collective-permute-start | bytes 1572872 | tf_op jit(solution)/shard_map/ppermute | solution.py:23
  55.9 5.5 %copy-start.1 = (bf16[1,256,768]{2,1,0:T(8,128)(2,1)}, bf16[1,256,768]{2,1,0:T(8,128)(2,1)S(1)}, u32[]{:S(2)}) copy-start(bf16[1,256,768]{2,1,0:T(8,128)(2,1)S(1)} %collective-permute-done.11.refs_1_) | copy-start | bytes 1179652
  56.3 10.6 %collective-permute-start.13 = (bf16[1,256,768]{2,1,0:T(8,128)(2,1)S(1)}, bf16[1,256,768]{2,1,0:T(8,128)(2,1)S(1)}, u32[]{:S(2)}, u32[]{:S(2)}) collective-permute-start(bf16[1,256,768]{2,1,0:T(8,128)(2,1)S(1)} %pad_maximum_fusion.1.refs_9_), channel_id=1, source_target_pairs={{0,2},{1,3},{2,0},{3,1},{4,6},{5,7},{6,4},{7,5},{8,10},{9,11},{10,... | collective-permute-start | bytes 1179656 | tf_op jit(solution)/shard_map/ppermute | solution.py:23
  61.3 5.7 %collective-permute-start.12 = (bf16[2,256,512]{2,1,0:T(8,128)(2,1)S(1)}, bf16[2,256,512]{2,1,0:T(8,128)(2,1)S(1)}, u32[]{:S(2)}, u32[]{:S(2)}) collective-permute-start(bf16[2,256,512]{2,1,0:T(8,128)(2,1)S(1)} %get-tuple-element.65), channel_id=1, source_target_pairs={{0,1},{1,0},{2,3},{3,2},{4,5},{5,4},{6,7},{7,6},{8,9},{9,8},{10,11... | collective-permute-start | bytes 1572872 | tf_op jit(solution)/shard_map/ppermute | solution.py:23
  61.4 6.4 %slice-start = ((bf16[1,256,768]{2,1,0:T(8,128)(2,1)}), bf16[1,256,256]{2,1,0:T(8,128)(2,1)S(1)}, s32[]{:S(2)}) async-start(bf16[1,256,768]{2,1,0:T(8,128)(2,1)} %copy-done.1), calls=%async_computation | async-start | bytes 262144 | tf_op jit(solution)/shard_map/slice | solution.py:267
  65.1 4.4 %copy-start.2 = (bf16[1,256,768]{2,1,0:T(8,128)(2,1)S(1)}, bf16[1,256,768]{2,1,0:T(8,128)(2,1)}, u32[]{:S(2)}) copy-start(bf16[1,256,768]{2,1,0:T(8,128)(2,1)} %copy-done.1) | copy-start | bytes 1179652
  67.2 9.8 %collective-permute-start.14 = (bf16[1,256,768]{2,1,0:T(8,128)(2,1)S(1)}, bf16[1,256,768]{2,1,0:T(8,128)(2,1)S(1)}, u32[]{:S(2)}, u32[]{:S(2)}) collective-permute-start(bf16[1,256,768]{2,1,0:T(8,128)(2,1)S(1)} %pad_maximum_fusion.2.refs_7_), channel_id=1, source_target_pairs={{0,2},{1,3},{2,0},{3,1},{4,6},{5,7},{6,4},{7,5},{8,10},{9,11},{10,... | collective-permute-start | bytes 1179656 | tf_op jit(solution)/shard_map/ppermute | solution.py:23
  67.9 1.6 %collective-permute-start.16 = (bf16[2,256,256]{2,1,0:T(8,128)(2,1)S(1)}, bf16[2,256,256]{2,1,0:T(8,128)(2,1)S(1)}, u32[]{:S(2)}, u32[]{:S(2)}) collective-permute-start(bf16[2,256,256]{2,1,0:T(8,128)(2,1)S(1)} %pad_maximum_fusion.4), channel_id=1, source_target_pairs={{0,1},{1,0},{2,3},{3,2},{4,5},{5,4},{6,7},{7,6},{8,9},{9,8},{10,11... | collective-permute-start | bytes 786440 | tf_op jit(solution)/shard_map/ppermute | solution.py:23
  68.0 4.9 %collective-permute-start.15 = (bf16[2,256,256]{2,1,0:T(8,128)(2,1)S(1)}, bf16[2,256,256]{2,1,0:T(8,128)(2,1)S(1)}, u32[]{:S(2)}, u32[]{:S(2)}) collective-permute-start(bf16[2,256,256]{2,1,0:T(8,128)(2,1)S(1)} %pad_maximum_fusion.3), channel_id=1, source_target_pairs={{0,1},{1,0},{2,3},{3,2},{4,5},{5,4},{6,7},{7,6},{8,9},{9,8},{10,11... | collective-permute-start | bytes 786440 | tf_op jit(solution)/shard_map/ppermute | solution.py:23
  77.1 2.1 %collective-permute-start.18 = (bf16[2,256,256]{2,1,0:T(8,128)(2,1)S(1)}, bf16[2,256,256]{2,1,0:T(8,128)(2,1)S(1)}, u32[]{:S(2)}, u32[]{:S(2)}) collective-permute-start(bf16[2,256,256]{2,1,0:T(8,128)(2,1)S(1)} %pad_maximum_fusion.5), channel_id=1, source_target_pairs={{0,1},{1,0},{2,3},{3,2},{4,5},{5,4},{6,7},{7,6},{8,9},{9,8},{10,11... | collective-permute-start | bytes 786440 | tf_op jit(solution)/shard_map/ppermute | solution.py:23
  77.4 6.0 %collective-permute-start.17 = (bf16[1,256,256]{2,1,0:T(8,128)(2,1)S(1)}, bf16[1,256,256]{2,1,0:T(8,128)(2,1)S(1)}, u32[]{:S(2)}, u32[]{:S(2)}) collective-permute-start(bf16[1,256,256]{2,1,0:T(8,128)(2,1)S(1)} %fusion.refs_8_.refs_0_), channel_id=1, source_target_pairs={{0,2},{1,3},{2,0},{3,1},{4,6},{5,7},{6,4},{7,5},{8,10},{9,11},{10,... | collective-permute-start | bytes 393224 | tf_op jit(solution)/shard_map/ppermute | solution.py:23
  83.4 1.6 %collective-permute-start.19 = (bf16[2,256,256]{2,1,0:T(8,128)(2,1)S(1)}, bf16[2,256,256]{2,1,0:T(8,128)(2,1)S(1)}, u32[]{:S(2)}, u32[]{:S(2)}) collective-permute-start(bf16[2,256,256]{2,1,0:T(8,128)(2,1)S(1)} %pad_maximum_fusion.6), channel_id=1, source_target_pairs={{0,1},{1,0},{2,3},{3,2},{4,5},{5,4},{6,7},{7,6},{8,9},{9,8},{10,11... | collective-permute-start | bytes 786440 | tf_op jit(solution)/shard_map/ppermute | solution.py:23
  87.2 7.1 %collective-permute-start.20 = (bf16[32,1536]{1,0:T(8,128)(2,1)S(1)}, bf16[32,1536]{1,0:T(8,128)(2,1)S(1)}, u32[]{:S(2)}, u32[]{:S(2)}) collective-permute-start(bf16[32,1536]{1,0:T(8,128)(2,1)S(1)} %get-tuple-element.78), channel_id=1, source_target_pairs={{0,12},{4,0},{8,4},{12,8},{1,13},{5,1},{9,5},{13,9},{2,14},{6,2},{... | collective-permute-start | bytes 294920 | tf_op jit(solution)/shard_map/ppermute | solution.py:383
  91.2 7.5 %collective-permute-start.22 = (bf16[32,1536]{1,0:T(8,128)(2,1)S(1)}, bf16[32,1536]{1,0:T(8,128)(2,1)S(1)}, u32[]{:S(2)}, u32[]{:S(2)}) collective-permute-start(bf16[32,1536]{1,0:T(8,128)(2,1)S(1)} %get-tuple-element.80), channel_id=1, source_target_pairs={{0,4},{4,8},{8,12},{12,0},{1,5},{5,9},{9,13},{13,1},{2,6},{6,10},{... | collective-permute-start | bytes 294920 | tf_op jit(solution)/shard_map/ppermute | solution.py:383
  94.4 9.3 %collective-permute-start.21 = (bf16[64,1536]{1,0:T(8,128)(2,1)S(1)}, bf16[64,1536]{1,0:T(8,128)(2,1)S(1)}, u32[]{:S(2)}, u32[]{:S(2)}) collective-permute-start(bf16[64,1536]{1,0:T(8,128)(2,1)S(1)} %pad_maximum_fusion.7), channel_id=1, source_target_pairs={{0,12},{4,0},{8,4},{12,8},{1,13},{5,1},{9,5},{13,9},{2,14},{6,2},{... | collective-permute-start | bytes 589832 | tf_op jit(solution)/shard_map/ppermute | solution.py:392
  98.8 7.8 %collective-permute-start.23 = (bf16[64,1536]{1,0:T(8,128)(2,1)S(1)}, bf16[64,1536]{1,0:T(8,128)(2,1)S(1)}, u32[]{:S(2)}, u32[]{:S(2)}) collective-permute-start(bf16[64,1536]{1,0:T(8,128)(2,1)S(1)} %pad_maximum_fusion.8), channel_id=1, source_target_pairs={{0,4},{4,8},{8,12},{12,0},{1,5},{5,9},{9,13},{13,1},{2,6},{6,10},{... | collective-permute-start | bytes 589832 | tf_op jit(solution)/shard_map/ppermute | solution.py:393

commit v11 on v10

--- a/solution.py
+++ b/solution.py
@@ -298,12 +298,11 @@
 
     ahead = lambda k: needs[k + 1] if k + 1 < len(needs) else None
 
-    meta = lax.optimization_barrier((meta, given[0]))[0]
     metas = [meta] + [
         lax.ppermute(meta, "expert", [(i, (i - k) % n_owner) for i in range(n_owner)])
         for k in gathered_order(n_owner)[1:]
     ]
-    feeds = gathered(tokens, "expert", metas)
+    feeds = gathered(tokens, "expert")
     rank, wt = route(metas, info, experts)
 
     tall, wide = [feed.shape[0] for feed in feeds], tokens.shape[1]
@@ -355,7 +354,7 @@
     return [0] + near + ([n // 2] if n > 1 else [])
 
 
-def gathered(x, axis, beside):
+def gathered(x, axis):
     n = lax.axis_size(axis)
     up, down_ = [(i, (i + 1) % n) for i in range(n)], [(i, (i - 1) % n) for i in range(n)]
     below = above = x
@@ -365,7 +364,6 @@
         found += [below, above]
     if n > 1:
         half = x.shape[0] // 2
-        below, above, *_ = lax.optimization_barrier((below, above, *beside))
         found += [lax.ppermute(below[:half], axis, up), lax.ppermute(above[half:], axis, down_)]
     return found
 

time: 107 us -> 103 us (0.963)
  waiting for transfers between devices: 24.9 us -> 22.3 us
  starting transfers between devices: 27.4 us -> 24.9 us
    ppermute x3, waiting for transfers between devices: 4.55 us -> 0.01 us  [on_device(): lax.ppermute(meta, 'expert', [(i, (i - k) % n_owner) for i in range(n_own...]
    ppermute x1, waiting for transfers between devices: 0.01 us -> 2.87 us  [gathered(): lax.ppermute(above, axis, down_)]
    ppermute x1, starting transfers between devices: 3.94 us -> 2.16 us  [returned(): lax.ppermute(partials[-2], axis, down_)]
    ppermute x1, waiting for transfers between devices: 1.79 us -> 0.01 us  [gathered(): lax.ppermute(below[:half], axis, up)]
  transfers between devices with their start and end apart: 24 -> 24, of which waited for: 12 -> 11; matrix products, arithmetic and copies ran while one was open for 1% -> 2% of each run, Pallas kernels for 42% -> 43%
where the time goes in v11:
time: 103 us
  Pallas kernels  51.3 us (50%)
  starting transfers between devices  24.9 us (24%)
  waiting for transfers between devices  22.3 us (22%)
  other arithmetic  3.68 us (4%)
    pallas_call x13, Pallas kernels, call(): pl.pallas_call(whole, out_shape=tuple(outs), in_specs=[SMEM] + [spec for...  50.5 us
    ppermute x13, waiting for transfers between devices, flip(): lax.ppermute(x, axis, [(i, i ^ k) for i in range(lax.axis_size(axis))])  7.78 us
    ppermute x13, starting transfers between devices, flip(): lax.ppermute(x, axis, [(i, i ^ k) for i in range(lax.axis_size(axis))])  6.17 us
    ppermute x1, waiting for transfers between devices, returned(): low = lax.ppermute(a.astype(jnp.bfloat16), axis, down_)  4.86 us
    ppermute x1, starting transfers between devices, returned(): low = lax.ppermute(a.astype(jnp.bfloat16), axis, down_)  4.33 us
    ppermute x3, starting transfers between devices, on_device(): lax.ppermute(meta, 'expert', [(i, (i - k) % n_owner) for i in range(n_own...  3.83 us
    ppermute x1, starting transfers between devices, gathered(): lax.ppermute(above[half:], axis, down_)  3.15 us
    ppermute x1, waiting for transfers between devices, returned(): lax.ppermute(partials[-2], axis, down_)  3.12 us
  transfers between devices with their start and end apart: 24, of which 11 were waited for; matrix products, arithmetic and copies ran while one was open for 2% of the time, Pallas kernels for 43%

profile of v11, /device:TPU:0, one launch (start us, length us, event | category | flops | bytes accessed | tf_op | source)
XLA Modules:
  0.0 102.9 jit_solution(3119925203694711909)
XLA Ops:
  0.0 3.0 %collective-permute-start = (bf16[64,1536]{1,0:T(8,128)(2,1)}, bf16[64,1536]{1,0:T(8,128)(2,1)S(1)}, u32[]{:S(2)}, u32[]{:S(2)}) collective-permute-start(bf16[64,1536]{1,0:T(8,128)(2,1)} %refs_0_.9), channel_id=1, source_target_pairs={{0,4},{4,8},{8,12},{12,0},{1,5},{5,9},{9,13},{13,1},{2,6},{6,10},{... | collective-permute-start | bytes 589832 | tf_op jit(solution)/shard_map/ppermute | solution.py:363
  3.0 2.0 %collective-permute-start.1 = (bf16[64,1536]{1,0:T(8,128)(2,1)}, bf16[64,1536]{1,0:T(8,128)(2,1)S(1)}, u32[]{:S(2)}, u32[]{:S(2)}) collective-permute-start(bf16[64,1536]{1,0:T(8,128)(2,1)} %refs_0_.9), channel_id=1, source_target_pairs={{0,12},{4,0},{8,4},{12,8},{1,13},{5,1},{9,5},{13,9},{2,14},{6,2},{... | collective-permute-start | bytes 589832 | tf_op jit(solution)/shard_map/ppermute | solution.py:363
  6.4 3.8 %collective-permute-start.5 = (f32[16,64]{1,0:T(8,128)S(1)}, f32[16,64]{1,0:T(8,128)S(1)}, u32[]{:S(2)}, u32[]{:S(2)}) collective-permute-start(f32[16,64]{1,0:T(8,128)S(1)} %pad_maximum_fusion.9.refs_0_), channel_id=1, source_target_pairs={{0,12},{4,0},{8,4},{12,8},{1,13},{5,1},{9,5},{13,9},{2,14},{6,2},{... | collective-permute-start | bytes 12296 | tf_op jit(solution)/shard_map/ppermute | solution.py:302
  10.3 0.8 collective-permute-done.refs_1_
  11.1 2.9 %collective-permute-done.1.refs_2_ = bf16[64,1536]{1,0:T(8,128)(2,1)S(1)} collective-permute-done((bf16[64,1536]{1,0:T(8,128)(2,1)}, bf16[64,1536]{1,0:T(8,128)(2,1)S(1)}, u32[]{:S(2)}, u32[]{:S(2)}) %collective-permute-start.1) | collective-permute-done | bytes 196640 | tf_op jit(solution)/shard_map/ppermute | solution.py:363
  14.0 3.2 %collective-permute-start.3 = (bf16[32,1536]{1,0:T(8,128)(2,1)S(1)}, bf16[32,1536]{1,0:T(8,128)(2,1)S(1)}, u32[]{:S(2)}, u32[]{:S(2)}) collective-permute-start(bf16[32,1536]{1,0:T(8,128)(2,1)S(1)} %slice.135), channel_id=1, source_target_pairs={{0,12},{4,0},{8,4},{12,8},{1,13},{5,1},{9,5},{13,9},{2,14},{6,2},{... | collective-permute-start | bytes 294920 | tf_op jit(solution)/shard_map/ppermute | solution.py:367
  17.2 3.4 %stage.1.refs_6_ = bf16[2,2,1536,512]{3,2,1,0:T(8,128)(2,1)S(1)} custom-call(s32[3]{0:T(128)S(1)} %pad_add_fusion.info, bf16[8,1536,1024]{2,1,0:T(8,128)(2,1)} %refs_7_.9, bf16[8,1536,1024]{2,1,0:T(8,128)(2,1)} %refs_8_.7), custom_call_target="tpu_custom_call" | custom-call | flops 1 | bytes 1 | tf_op jit(solution)/shard_map/stage/pallas_call | solution.py:113
  21.4 4.5 %send_half.4 = (bf16[2,256,512]{2,1,0:T(8,128)(2,1)S(1)}, bf16[256,1536]{1,0:T(8,128)(2,1)S(1)}, bf16[2,2,1536,512]{3,2,1,0:T(8,128)(2,1)S(1)}) custom-call(s32[3]{0:T(128)S(1)} %pad_add_fusion.info, bf16[64,1536]{1,0:T(8,128)(2,1)S(1)} %copy-done, bf16[64,1536]{1,0:T(8,128)(2,1)S(1)} %collective-permute-done.refs_1_, ...), custom_call_target="tpu_custom_call" | custom-call | flops 1 | bytes 1 | tf_op jit(solution)/shard_map/send_half/pallas_call | solution.py:113
  26.0 4.2 %keep_half.4 = (bf16[2,256,512]{2,1,0:T(8,128)(2,1)S(1)}, bf16[2,2,1536,512]{3,2,1,0:T(8,128)(2,1)S(1)}) custom-call(s32[3]{0:T(128)S(1)} %pad_add_fusion.info, bf16[256,1536]{1,0:T(8,128)(2,1)S(1)} %get-tuple-element.41.refs_0_, bf16[2,2,1536,512]{3,2,1,0:T(8,128)(2,1)S(1)} %get-tuple-element.42.refs_1_, bf16[8,1536,1024]{2,1,0:T(8,128)(2,1)} %refs_7_.9, ...), custom_call_target="tpu_custom_call" | custom-call | flops 1 | bytes 1 | tf_op jit(solution)/shard_map/keep_half/pallas_call | solution.py:113
  30.4 1.6 %collective-permute-start.9 = (bf16[1,256,512]{2,1,0:T(8,128)(2,1)S(1)}, bf16[1,256,512]{2,1,0:T(8,128)(2,1)S(1)}, u32[]{:S(2)}, u32[]{:S(2)}) collective-permute-start(bf16[1,256,512]{2,1,0:T(8,128)(2,1)S(1)} %slice.191.refs_9_), channel_id=1, source_target_pairs={{0,2},{1,3},{2,0},{3,1},{4,6},{5,7},{6,4},{7,5},{8,10},{9,11},{10,... | collective-permute-start | bytes 786440 | tf_op jit(solution)/shard_map/ppermute | solution.py:23
  32.0 4.6 %send_half.5 = (bf16[2,256,512]{2,1,0:T(8,128)(2,1)S(1)}, bf16[256,1536]{1,0:T(8,128)(2,1)S(1)}, bf16[2,2,1536,512]{3,2,1,0:T(8,128)(2,1)S(1)}) custom-call(s32[3]{0:T(128)S(1)} %pad_add_fusion.info, bf16[64,1536]{1,0:T(8,128)(2,1)S(1)} %copy-done, bf16[64,1536]{1,0:T(8,128)(2,1)S(1)} %collective-permute-done.refs_1_, ...), custom_call_target="tpu_custom_call" | custom-call | flops 1 | bytes 1 | tf_op jit(solution)/shard_map/send_half/pallas_call | solution.py:113
  36.9 4.2 %keep_half.5 = (bf16[2,256,512]{2,1,0:T(8,128)(2,1)S(1)}, bf16[2,2,1536,512]{3,2,1,0:T(8,128)(2,1)S(1)}) custom-call(s32[3]{0:T(128)S(1)} %pad_add_fusion.info, bf16[256,1536]{1,0:T(8,128)(2,1)S(1)} %get-tuple-element.46.refs_0_, bf16[2,2,1536,512]{3,2,1,0:T(8,128)(2,1)S(1)} %get-tuple-element.47.refs_1_, bf16[8,1536,1024]{2,1,0:T(8,128)(2,1)} %refs_7_.9, ...), custom_call_target="tpu_custom_call" | custom-call | flops 1 | bytes 1 | tf_op jit(solution)/shard_map/keep_half/pallas_call | solution.py:113
  42.1 4.5 %send_half.6 = (bf16[2,256,512]{2,1,0:T(8,128)(2,1)S(1)}, bf16[256,1536]{1,0:T(8,128)(2,1)S(1)}, bf16[2,2,1536,512]{3,2,1,0:T(8,128)(2,1)S(1)}) custom-call(s32[3]{0:T(128)S(1)} %pad_add_fusion.info, bf16[64,1536]{1,0:T(8,128)(2,1)S(1)} %copy-done, bf16[64,1536]{1,0:T(8,128)(2,1)S(1)} %collective-permute-done.refs_1_, ...), custom_call_target="tpu_custom_call" | custom-call | flops 1 | bytes 1 | tf_op jit(solution)/shard_map/send_half/pallas_call | solution.py:113
  46.7 4.2 %keep_half.6 = (bf16[2,256,512]{2,1,0:T(8,128)(2,1)S(1)}, bf16[2,2,1536,512]{3,2,1,0:T(8,128)(2,1)S(1)}) custom-call(s32[3]{0:T(128)S(1)} %pad_add_fusion.info, bf16[256,1536]{1,0:T(8,128)(2,1)S(1)} %get-tuple-element.51.refs_0_, bf16[2,2,1536,512]{3,2,1,0:T(8,128)(2,1)S(1)} %get-tuple-element.52.refs_1_, bf16[8,1536,1024]{2,1,0:T(8,128)(2,1)} %refs_7_.9, ...), custom_call_target="tpu_custom_call" | custom-call | flops 1 | bytes 1 | tf_op jit(solution)/shard_map/keep_half/pallas_call | solution.py:113
  50.9 2.0 %collective-permute-done.11.refs_1_ = bf16[1,256,768]{2,1,0:T(8,128)(2,1)S(1)} collective-permute-done((bf16[1,256,768]{2,1,0:T(8,128)(2,1)S(1)}, bf16[1,256,768]{2,1,0:T(8,128)(2,1)S(1)}, u32[]{:S(2)}, u32[]{:S(2)}) %collective-permute-start.11) | collective-permute-done | bytes 393248 | tf_op jit(solution)/shard_map/ppermute | solution.py:23
  53.9 4.6 %send_half.7 = (bf16[2,256,512]{2,1,0:T(8,128)(2,1)S(1)}, bf16[256,1536]{1,0:T(8,128)(2,1)S(1)}, bf16[2,2,1536,512]{3,2,1,0:T(8,128)(2,1)S(1)}) custom-call(s32[3]{0:T(128)S(1)} %pad_add_fusion.info, bf16[64,1536]{1,0:T(8,128)(2,1)S(1)} %copy-done, bf16[64,1536]{1,0:T(8,128)(2,1)S(1)} %collective-permute-done.refs_1_, ...), custom_call_target="tpu_custom_call" | custom-call | flops 1 | bytes 1 | tf_op jit(solution)/shard_map/send_half/pallas_call | solution.py:113
  58.7 3.6 %keep_half.7 = (bf16[2,256,512]{2,1,0:T(8,128)(2,1)S(1)}, bf16[2,1024,1536]{2,1,0:T(8,128)(2,1)S(1)}) custom-call(s32[3]{0:T(128)S(1)} %pad_add_fusion.info, bf16[256,1536]{1,0:T(8,128)(2,1)S(1)} %get-tuple-element.56.refs_0_, bf16[2,2,1536,512]{3,2,1,0:T(8,128)(2,1)S(1)} %get-tuple-element.57.refs_1_, bf16[8,1024,1536]{2,1,0:T(8,128)(2,1)} %refs_7_.11), custom_call_target="tpu_custom_call" | custom-call | flops 1 | bytes 1 | tf_op jit(solution)/shard_map/keep_half/pallas_call | solution.py:113
  62.3 1.6 %collective-permute-done.13.refs_1_ = bf16[1,256,768]{2,1,0:T(8,128)(2,1)S(1)} collective-permute-done((bf16[1,256,768]{2,1,0:T(8,128)(2,1)S(1)}, bf16[1,256,768]{2,1,0:T(8,128)(2,1)S(1)}, u32[]{:S(2)}, u32[]{:S(2)}) %collective-permute-start.13) | collective-permute-done | bytes 393248 | tf_op jit(solution)/shard_map/ppermute | solution.py:23
  65.6 0.9 collective-permute-done.16.refs_2_
  66.5 3.4 %down.4 = (f32[256,1536]{1,0:T(8,128)S(1)}, bf16[2,1024,1536]{2,1,0:T(8,128)(2,1)S(1)}) custom-call(s32[3]{0:T(128)S(1)} %pad_add_fusion.info, bf16[1,256,256]{2,1,0:T(8,128)(2,1)S(1)} %fusion.3.refs_0_, bf16[1,256,768]{2,1,0:T(8,128)(2,1)S(1)} %copy-done.2, bf16[2,256,256]{2,1,0:T(8,128)(2,1)S(1)} %collective-permute-done.16.refs_2_, ...), custom_call_target="tpu_custom_call" | custom-call | flops 1 | bytes 1 | tf_op jit(solution)/shard_map/down/pallas_call | solution.py:113
  70.0 3.5 %down.5 = (f32[256,1536]{1,0:T(8,128)S(1)}, bf16[2,1024,1536]{2,1,0:T(8,128)(2,1)S(1)}) custom-call(s32[3]{0:T(128)S(1)} %pad_add_fusion.info, bf16[1,256,256]{2,1,0:T(8,128)(2,1)S(1)} %fusion.2.refs_0_, bf16[1,256,768]{2,1,0:T(8,128)(2,1)S(1)} %collective-permute-done.13.refs_1_, bf16[2,256,256]{2,1,0:T(8,128)(2,1)S(1)} %collective-permute-done.15.refs_2_, ...), custom_call_target="tpu_custom_call" | custom-call | flops 1 | bytes 1 | tf_op jit(solution)/shard_map/down/pallas_call | solution.py:113
  73.5 0.9 collective-permute-done.14.refs_1_
  74.6 1.6 %collective-permute-start.17 = (bf16[1,256,256]{2,1,0:T(8,128)(2,1)S(1)}, bf16[1,256,256]{2,1,0:T(8,128)(2,1)S(1)}, u32[]{:S(2)}, u32[]{:S(2)}) collective-permute-start(bf16[1,256,256]{2,1,0:T(8,128)(2,1)S(1)} %fusion.refs_8_.refs_0_), channel_id=1, source_target_pairs={{0,2},{1,3},{2,0},{3,1},{4,6},{5,7},{6,4},{7,5},{8,10},{9,11},{10,... | collective-permute-start | bytes 393224 | tf_op jit(solution)/shard_map/ppermute | solution.py:23
  76.2 3.5 %down.6 = (f32[256,1536]{1,0:T(8,128)S(1)}, bf16[2,1024,1536]{2,1,0:T(8,128)(2,1)S(1)}) custom-call(s32[3]{0:T(128)S(1)} %pad_add_fusion.info, bf16[1,256,256]{2,1,0:T(8,128)(2,1)S(1)} %fusion.1.refs_0_, bf16[1,256,768]{2,1,0:T(8,128)(2,1)S(1)} %collective-permute-done.14.refs_1_, bf16[2,256,256]{2,1,0:T(8,128)(2,1)S(1)} %collective-permute-done.18.refs_2_, ...), custom_call_target="tpu_custom_call" | custom-call | flops 1 | bytes 1 | tf_op jit(solution)/shard_map/down/pallas_call | solution.py:113
  79.7 0.9 collective-permute-done.17.refs_1_
  80.7 1.5 %collective-permute-done.19.refs_2_ = bf16[2,256,256]{2,1,0:T(8,128)(2,1)S(1)} collective-permute-done((bf16[2,256,256]{2,1,0:T(8,128)(2,1)S(1)}, bf16[2,256,256]{2,1,0:T(8,128)(2,1)S(1)}, u32[]{:S(2)}, u32[]{:S(2)}) %collective-permute-start.19) | collective-permute-done | bytes 262176 | tf_op jit(solution)/shard_map/ppermute | solution.py:23
  82.2 2.3 %down.7 = (bf16[64,1536]{1,0:T(8,128)(2,1)S(1)}, bf16[64,1536]{1,0:T(8,128)(2,1)S(1)}, bf16[64,1536]{1,0:T(8,128)(2,1)S(1)}, bf16[32,1536]{1,0:T(8,128)(2,1)S(1)}, bf16[32,1536]{1,0:T(8,128)(2,1)S(1)}) custom-call(s32[3]{0:T(128)S(1)} %pad_add_fusion.info, bf16[1,256,256]{2,1,0:T(8,128)(2,1)S(1)} %fusion.refs_8_.refs_0_, ...), custom_call_target="tpu_custom_call" | custom-call | flops 1 | bytes 1 | tf_op jit(solution)/shard_map/down/pallas_call | solution.py:113
  84.5 2.2 %collective-permute-start.20 = (bf16[32,1536]{1,0:T(8,128)(2,1)S(1)}, bf16[32,1536]{1,0:T(8,128)(2,1)S(1)}, u32[]{:S(2)}, u32[]{:S(2)}) collective-permute-start(bf16[32,1536]{1,0:T(8,128)(2,1)S(1)} %get-tuple-element.72), channel_id=1, source_target_pairs={{0,12},{4,0},{8,4},{12,8},{1,13},{5,1},{9,5},{13,9},{2,14},{6,2},{... | collective-permute-start | bytes 294920 | tf_op jit(solution)/shard_map/ppermute | solution.py:381
  86.7 3.1 %collective-permute-done.20 = bf16[32,1536]{1,0:T(8,128)(2,1)S(1)} collective-permute-done((bf16[32,1536]{1,0:T(8,128)(2,1)S(1)}, bf16[32,1536]{1,0:T(8,128)(2,1)S(1)}, u32[]{:S(2)}, u32[]{:S(2)}) %collective-permute-start.20) | collective-permute-done | bytes 98336 | tf_op jit(solution)/shard_map/ppermute | solution.py:381
  89.9 4.3 %collective-permute-start.21 = (bf16[64,1536]{1,0:T(8,128)(2,1)S(1)}, bf16[64,1536]{1,0:T(8,128)(2,1)S(1)}, u32[]{:S(2)}, u32[]{:S(2)}) collective-permute-start(bf16[64,1536]{1,0:T(8,128)(2,1)S(1)} %pad_maximum_fusion.7), channel_id=1, source_target_pairs={{0,12},{4,0},{8,4},{12,8},{1,13},{5,1},{9,5},{13,9},{2,14},{6,2},{... | collective-permute-start | bytes 589832 | tf_op jit(solution)/shard_map/ppermute | solution.py:390
  94.4 4.9 %collective-permute-done.21 = bf16[64,1536]{1,0:T(8,128)(2,1)S(1)} collective-permute-done((bf16[64,1536]{1,0:T(8,128)(2,1)S(1)}, bf16[64,1536]{1,0:T(8,128)(2,1)S(1)}, u32[]{:S(2)}, u32[]{:S(2)}) %collective-permute-start.21) | collective-permute-done | bytes 196640 | tf_op jit(solution)/shard_map/ppermute | solution.py:390
  99.2 2.9 %collective-permute-done.23 = bf16[64,1536]{1,0:T(8,128)(2,1)S(1)} collective-permute-done((bf16[64,1536]{1,0:T(8,128)(2,1)S(1)}, bf16[64,1536]{1,0:T(8,128)(2,1)S(1)}, u32[]{:S(2)}, u32[]{:S(2)}) %collective-permute-start.23) | collective-permute-done | bytes 196640 | tf_op jit(solution)/shard_map/ppermute | solution.py:391
  (76 shorter events, 7.9 us)
Async XLA Ops:
  0.0 11.0 %collective-permute-start = (bf16[64,1536]{1,0:T(8,128)(2,1)}, bf16[64,1536]{1,0:T(8,128)(2,1)S(1)}, u32[]{:S(2)}, u32[]{:S(2)}) collective-permute-start(bf16[64,1536]{1,0:T(8,128)(2,1)} %refs_0_.9), channel_id=1, source_target_pairs={{0,4},{4,8},{8,12},{12,0},{1,5},{5,9},{9,13},{13,1},{2,6},{6,10},{... | collective-permute-start | bytes 589832 | tf_op jit(solution)/shard_map/ppermute | solution.py:363
  3.0 11.0 %collective-permute-start.1 = (bf16[64,1536]{1,0:T(8,128)(2,1)}, bf16[64,1536]{1,0:T(8,128)(2,1)S(1)}, u32[]{:S(2)}, u32[]{:S(2)}) collective-permute-start(bf16[64,1536]{1,0:T(8,128)(2,1)} %refs_0_.9), channel_id=1, source_target_pairs={{0,12},{4,0},{8,4},{12,8},{1,13},{5,1},{9,5},{13,9},{2,14},{6,2},{... | collective-permute-start | bytes 589832 | tf_op jit(solution)/shard_map/ppermute | solution.py:363
  6.4 14.2 %collective-permute-start.4 = (f32[16,64]{1,0:T(8,128)S(1)}, f32[16,64]{1,0:T(8,128)S(1)}, u32[]{:S(2)}, u32[]{:S(2)}) collective-permute-start(f32[16,64]{1,0:T(8,128)S(1)} %pad_maximum_fusion.9.refs_0_), channel_id=1, source_target_pairs={{0,4},{4,8},{8,12},{12,0},{1,5},{5,9},{9,13},{13,1},{2,6},{6,10},{... | collective-permute-start | bytes 12296 | tf_op jit(solution)/shard_map/ppermute | solution.py:302
  6.4 14.2 %collective-permute-start.5 = (f32[16,64]{1,0:T(8,128)S(1)}, f32[16,64]{1,0:T(8,128)S(1)}, u32[]{:S(2)}, u32[]{:S(2)}) collective-permute-start(f32[16,64]{1,0:T(8,128)S(1)} %pad_maximum_fusion.9.refs_0_), channel_id=1, source_target_pairs={{0,12},{4,0},{8,4},{12,8},{1,13},{5,1},{9,5},{13,9},{2,14},{6,2},{... | collective-permute-start | bytes 12296 | tf_op jit(solution)/shard_map/ppermute | solution.py:302
  10.3 10.4 %collective-permute-start.6 = (f32[16,64]{1,0:T(8,128)S(1)}, f32[16,64]{1,0:T(8,128)S(1)}, u32[]{:S(2)}, u32[]{:S(2)}) collective-permute-start(f32[16,64]{1,0:T(8,128)S(1)} %pad_maximum_fusion.9.refs_0_), channel_id=1, source_target_pairs={{0,8},{4,12},{8,0},{12,4},{1,9},{5,13},{9,1},{13,5},{2,10},{6,14},... | collective-permute-start | bytes 12296 | tf_op jit(solution)/shard_map/ppermute | solution.py:302
  11.0 10.4 %collective-permute-start.2 = (bf16[32,1536]{1,0:T(8,128)(2,1)S(1)}, bf16[32,1536]{1,0:T(8,128)(2,1)S(1)}, u32[]{:S(2)}, u32[]{:S(2)}) collective-permute-start(bf16[32,1536]{1,0:T(8,128)(2,1)S(1)} %slice.134), channel_id=1, source_target_pairs={{0,4},{4,8},{8,12},{12,0},{1,5},{5,9},{9,13},{13,1},{2,6},{6,10},{... | collective-permute-start | bytes 294920 | tf_op jit(solution)/shard_map/ppermute | solution.py:367
  14.0 7.4 %collective-permute-start.3 = (bf16[32,1536]{1,0:T(8,128)(2,1)S(1)}, bf16[32,1536]{1,0:T(8,128)(2,1)S(1)}, u32[]{:S(2)}, u32[]{:S(2)}) collective-permute-start(bf16[32,1536]{1,0:T(8,128)(2,1)S(1)} %slice.135), channel_id=1, source_target_pairs={{0,12},{4,0},{8,4},{12,8},{1,13},{5,1},{9,5},{13,9},{2,14},{6,2},{... | collective-permute-start | bytes 294920 | tf_op jit(solution)/shard_map/ppermute | solution.py:367
  17.2 4.2 %copy-start = (bf16[64,1536]{1,0:T(8,128)(2,1)S(1)}, bf16[64,1536]{1,0:T(8,128)(2,1)}, u32[]{:S(2)}) copy-start(bf16[64,1536]{1,0:T(8,128)(2,1)} %refs_0_.9) | copy-start | bytes 589828
  25.9 4.3 %collective-permute-start.7 = (bf16[2,256,512]{2,1,0:T(8,128)(2,1)S(1)}, bf16[2,256,512]{2,1,0:T(8,128)(2,1)S(1)}, u32[]{:S(2)}, u32[]{:S(2)}) collective-permute-start(bf16[2,256,512]{2,1,0:T(8,128)(2,1)S(1)} %get-tuple-element.45), channel_id=1, source_target_pairs={{0,1},{1,0},{2,3},{3,2},{4,5},{5,4},{6,7},{7,6},{8,9},{9,8},{10,11... | collective-permute-start | bytes 1572872 | tf_op jit(solution)/shard_map/ppermute | solution.py:23
  30.4 10.7 %collective-permute-start.9 = (bf16[1,256,512]{2,1,0:T(8,128)(2,1)S(1)}, bf16[1,256,512]{2,1,0:T(8,128)(2,1)S(1)}, u32[]{:S(2)}, u32[]{:S(2)}) collective-permute-start(bf16[1,256,512]{2,1,0:T(8,128)(2,1)S(1)} %slice.191.refs_9_), channel_id=1, source_target_pairs={{0,2},{1,3},{2,0},{3,1},{4,6},{5,7},{6,4},{7,5},{8,10},{9,11},{10,... | collective-permute-start | bytes 786440 | tf_op jit(solution)/shard_map/ppermute | solution.py:23
  36.6 4.7 %collective-permute-start.8 = (bf16[2,256,512]{2,1,0:T(8,128)(2,1)S(1)}, bf16[2,256,512]{2,1,0:T(8,128)(2,1)S(1)}, u32[]{:S(2)}, u32[]{:S(2)}) collective-permute-start(bf16[2,256,512]{2,1,0:T(8,128)(2,1)S(1)} %get-tuple-element.50), channel_id=1, source_target_pairs={{0,1},{1,0},{2,3},{3,2},{4,5},{5,4},{6,7},{7,6},{8,9},{9,8},{10,11... | collective-permute-start | bytes 1572872 | tf_op jit(solution)/shard_map/ppermute | solution.py:23
  41.5 11.4 %collective-permute-start.11 = (bf16[1,256,768]{2,1,0:T(8,128)(2,1)S(1)}, bf16[1,256,768]{2,1,0:T(8,128)(2,1)S(1)}, u32[]{:S(2)}, u32[]{:S(2)}) collective-permute-start(bf16[1,256,768]{2,1,0:T(8,128)(2,1)S(1)} %pad_maximum_fusion.refs_9_), channel_id=1, source_target_pairs={{0,2},{1,3},{2,0},{3,1},{4,6},{5,7},{6,4},{7,5},{8,10},{9,11},{10,... | collective-permute-start | bytes 1179656 | tf_op jit(solution)/shard_map/ppermute | solution.py:23
  46.6 6.5 %collective-permute-start.10 = (bf16[2,256,512]{2,1,0:T(8,128)(2,1)S(1)}, bf16[2,256,512]{2,1,0:T(8,128)(2,1)S(1)}, u32[]{:S(2)}, u32[]{:S(2)}) collective-permute-start(bf16[2,256,512]{2,1,0:T(8,128)(2,1)S(1)} %get-tuple-element.55), channel_id=1, source_target_pairs={{0,1},{1,0},{2,3},{3,2},{4,5},{5,4},{6,7},{7,6},{8,9},{9,8},{10,11... | collective-permute-start | bytes 1572872 | tf_op jit(solution)/shard_map/ppermute | solution.py:23
  52.9 5.7 %copy-start.1 = (bf16[1,256,768]{2,1,0:T(8,128)(2,1)}, bf16[1,256,768]{2,1,0:T(8,128)(2,1)S(1)}, u32[]{:S(2)}) copy-start(bf16[1,256,768]{2,1,0:T(8,128)(2,1)S(1)} %collective-permute-done.11.refs_1_) | copy-start | bytes 1179652
  53.3 10.6 %collective-permute-start.13 = (bf16[1,256,768]{2,1,0:T(8,128)(2,1)S(1)}, bf16[1,256,768]{2,1,0:T(8,128)(2,1)S(1)}, u32[]{:S(2)}, u32[]{:S(2)}) collective-permute-start(bf16[1,256,768]{2,1,0:T(8,128)(2,1)S(1)} %pad_maximum_fusion.1.refs_9_), channel_id=1, source_target_pairs={{0,2},{1,3},{2,0},{3,1},{4,6},{5,7},{6,4},{7,5},{8,10},{9,11},{10,... | collective-permute-start | bytes 1179656 | tf_op jit(solution)/shard_map/ppermute | solution.py:23
  58.6 5.5 %collective-permute-start.12 = (bf16[2,256,512]{2,1,0:T(8,128)(2,1)S(1)}, bf16[2,256,512]{2,1,0:T(8,128)(2,1)S(1)}, u32[]{:S(2)}, u32[]{:S(2)}) collective-permute-start(bf16[2,256,512]{2,1,0:T(8,128)(2,1)S(1)} %get-tuple-element.59), channel_id=1, source_target_pairs={{0,1},{1,0},{2,3},{3,2},{4,5},{5,4},{6,7},{7,6},{8,9},{9,8},{10,11... | collective-permute-start | bytes 1572872 | tf_op jit(solution)/shard_map/ppermute | solution.py:23
  58.7 6.2 %slice-start = ((bf16[1,256,768]{2,1,0:T(8,128)(2,1)}), bf16[1,256,256]{2,1,0:T(8,128)(2,1)S(1)}, s32[]{:S(2)}) async-start(bf16[1,256,768]{2,1,0:T(8,128)(2,1)} %copy-done.1), calls=%async_computation | async-start | bytes 262144 | tf_op jit(solution)/shard_map/slice | solution.py:267
  62.3 4.2 %copy-start.2 = (bf16[1,256,768]{2,1,0:T(8,128)(2,1)S(1)}, bf16[1,256,768]{2,1,0:T(8,128)(2,1)}, u32[]{:S(2)}) copy-start(bf16[1,256,768]{2,1,0:T(8,128)(2,1)} %copy-done.1) | copy-start | bytes 1179652
  64.3 10.0 %collective-permute-start.14 = (bf16[1,256,768]{2,1,0:T(8,128)(2,1)S(1)}, bf16[1,256,768]{2,1,0:T(8,128)(2,1)S(1)}, u32[]{:S(2)}, u32[]{:S(2)}) collective-permute-start(bf16[1,256,768]{2,1,0:T(8,128)(2,1)S(1)} %pad_maximum_fusion.2.refs_7_), channel_id=1, source_target_pairs={{0,2},{1,3},{2,0},{3,1},{4,6},{5,7},{6,4},{7,5},{8,10},{9,11},{10,... | collective-permute-start | bytes 1179656 | tf_op jit(solution)/shard_map/ppermute | solution.py:23
  64.9 1.6 %collective-permute-start.16 = (bf16[2,256,256]{2,1,0:T(8,128)(2,1)S(1)}, bf16[2,256,256]{2,1,0:T(8,128)(2,1)S(1)}, u32[]{:S(2)}, u32[]{:S(2)}) collective-permute-start(bf16[2,256,256]{2,1,0:T(8,128)(2,1)S(1)} %pad_maximum_fusion.4), channel_id=1, source_target_pairs={{0,1},{1,0},{2,3},{3,2},{4,5},{5,4},{6,7},{7,6},{8,9},{9,8},{10,11... | collective-permute-start | bytes 786440 | tf_op jit(solution)/shard_map/ppermute | solution.py:23
  65.1 4.9 %collective-permute-start.15 = (bf16[2,256,256]{2,1,0:T(8,128)(2,1)S(1)}, bf16[2,256,256]{2,1,0:T(8,128)(2,1)S(1)}, u32[]{:S(2)}, u32[]{:S(2)}) collective-permute-start(bf16[2,256,256]{2,1,0:T(8,128)(2,1)S(1)} %pad_maximum_fusion.3), channel_id=1, source_target_pairs={{0,1},{1,0},{2,3},{3,2},{4,5},{5,4},{6,7},{7,6},{8,9},{9,8},{10,11... | collective-permute-start | bytes 786440 | tf_op jit(solution)/shard_map/ppermute | solution.py:23
  74.4 1.8 %collective-permute-start.18 = (bf16[2,256,256]{2,1,0:T(8,128)(2,1)S(1)}, bf16[2,256,256]{2,1,0:T(8,128)(2,1)S(1)}, u32[]{:S(2)}, u32[]{:S(2)}) collective-permute-start(bf16[2,256,256]{2,1,0:T(8,128)(2,1)S(1)} %pad_maximum_fusion.5), channel_id=1, source_target_pairs={{0,1},{1,0},{2,3},{3,2},{4,5},{5,4},{6,7},{7,6},{8,9},{9,8},{10,11... | collective-permute-start | bytes 786440 | tf_op jit(solution)/shard_map/ppermute | solution.py:23
  74.6 6.0 %collective-permute-start.17 = (bf16[1,256,256]{2,1,0:T(8,128)(2,1)S(1)}, bf16[1,256,256]{2,1,0:T(8,128)(2,1)S(1)}, u32[]{:S(2)}, u32[]{:S(2)}) collective-permute-start(bf16[1,256,256]{2,1,0:T(8,128)(2,1)S(1)} %fusion.refs_8_.refs_0_), channel_id=1, source_target_pairs={{0,2},{1,3},{2,0},{3,1},{4,6},{5,7},{6,4},{7,5},{8,10},{9,11},{10,... | collective-permute-start | bytes 393224 | tf_op jit(solution)/shard_map/ppermute | solution.py:23
  80.6 1.6 %collective-permute-start.19 = (bf16[2,256,256]{2,1,0:T(8,128)(2,1)S(1)}, bf16[2,256,256]{2,1,0:T(8,128)(2,1)S(1)}, u32[]{:S(2)}, u32[]{:S(2)}) collective-permute-start(bf16[2,256,256]{2,1,0:T(8,128)(2,1)S(1)} %pad_maximum_fusion.6), channel_id=1, source_target_pairs={{0,1},{1,0},{2,3},{3,2},{4,5},{5,4},{6,7},{7,6},{8,9},{9,8},{10,11... | collective-permute-start | bytes 786440 | tf_op jit(solution)/shard_map/ppermute | solution.py:23
  84.5 5.4 %collective-permute-start.20 = (bf16[32,1536]{1,0:T(8,128)(2,1)S(1)}, bf16[32,1536]{1,0:T(8,128)(2,1)S(1)}, u32[]{:S(2)}, u32[]{:S(2)}) collective-permute-start(bf16[32,1536]{1,0:T(8,128)(2,1)S(1)} %get-tuple-element.72), channel_id=1, source_target_pairs={{0,12},{4,0},{8,4},{12,8},{1,13},{5,1},{9,5},{13,9},{2,14},{6,2},{... | collective-permute-start | bytes 294920 | tf_op jit(solution)/shard_map/ppermute | solution.py:381
  86.7 7.6 %collective-permute-start.22 = (bf16[32,1536]{1,0:T(8,128)(2,1)S(1)}, bf16[32,1536]{1,0:T(8,128)(2,1)S(1)}, u32[]{:S(2)}, u32[]{:S(2)}) collective-permute-start(bf16[32,1536]{1,0:T(8,128)(2,1)S(1)} %get-tuple-element.74), channel_id=1, source_target_pairs={{0,4},{4,8},{8,12},{12,0},{1,5},{5,9},{9,13},{13,1},{2,6},{6,10},{... | collective-permute-start | bytes 294920 | tf_op jit(solution)/shard_map/ppermute | solution.py:381
  89.9 9.3 %collective-permute-start.21 = (bf16[64,1536]{1,0:T(8,128)(2,1)S(1)}, bf16[64,1536]{1,0:T(8,128)(2,1)S(1)}, u32[]{:S(2)}, u32[]{:S(2)}) collective-permute-start(bf16[64,1536]{1,0:T(8,128)(2,1)S(1)} %pad_maximum_fusion.7), channel_id=1, source_target_pairs={{0,12},{4,0},{8,4},{12,8},{1,13},{5,1},{9,5},{13,9},{2,14},{6,2},{... | collective-permute-start | bytes 589832 | tf_op jit(solution)/shard_map/ppermute | solution.py:390
  94.3 7.8 %collective-permute-start.23 = (bf16[64,1536]{1,0:T(8,128)(2,1)S(1)}, bf16[64,1536]{1,0:T(8,128)(2,1)S(1)}, u32[]{:S(2)}, u32[]{:S(2)}) collective-permute-start(bf16[64,1536]{1,0:T(8,128)(2,1)S(1)} %pad_maximum_fusion.8), channel_id=1, source_target_pairs={{0,4},{4,8},{8,12},{12,0},{1,5},{5,9},{9,13},{13,1},{2,6},{6,10},{... | collective-permute-start | bytes 589832 | tf_op jit(solution)/shard_map/ppermute | solution.py:391

commit v12 on v11

--- a/solution.py
+++ b/solution.py
@@ -354,47 +354,51 @@
     return [0] + near + ([n // 2] if n > 1 else [])
 
 
+def ways(n):
+    return [(i, (i + 1) % n) for i in range(n)], [(i, (i - 1) % n) for i in range(n)]
+
+
 def gathered(x, axis):
     n = lax.axis_size(axis)
-    up, down_ = [(i, (i + 1) % n) for i in range(n)], [(i, (i - 1) % n) for i in range(n)]
-    below = above = x
+    up, down_ = ways(n)
+    half = x.shape[0] // 2
+    below = above = [x[:half], x[half:]]
     found = [x]
     for _ in range(1, n // 2):
-        below, above = lax.ppermute(below, axis, up), lax.ppermute(above, axis, down_)
-        found += [below, above]
+        far_up, far_down = lax.ppermute(below[0], axis, up), lax.ppermute(above[1], axis, down_)
+        below = [far_up, lax.ppermute(below[1], axis, up)]
+        above = [lax.ppermute(above[0], axis, down_), far_down]
+        found += below + above
     if n > 1:
-        half = x.shape[0] // 2
-        found += [lax.ppermute(below[:half], axis, up), lax.ppermute(above[half:], axis, down_)]
+        found += [lax.ppermute(below[0], axis, up), lax.ppermute(above[1], axis, down_)]
     return found
 
 
 def returned(partials, axis):
     n = lax.axis_size(axis)
-    up, down_ = [(i, (i + 1) % n) for i in range(n)], [(i, (i - 1) % n) for i in range(n)]
+    up, down_ = ways(n)
     wide = lambda x: x.astype(jnp.float32)
-    near = {0: partials[0]}
+    mixed = wide(partials[0])
     if n == 1:
-        return wide(near[0])
-    for k, partial in zip(gathered_order(n)[1:-1], partials[1:-2]):
-        near[k] = partial
-    half = partials[-1].shape[0]
-    low, high = lax.ppermute(partials[-2], axis, down_), lax.ppermute(partials[-1], axis, up)
-    halves = True
+        return mixed
+    half = mixed.shape[0] // 2
+
+    def hop(there, partial, perm):
+        total = partial if there is None else (wide(partial) + wide(there)).astype(jnp.bfloat16)
+        return lax.ppermute(total, axis, perm)
+
+    low = [hop(None, partials[-2], down_), None]
+    high = [None, hop(None, partials[-1], up)]
     for s in range(n // 2 - 1, 0, -1):
-        a, b = wide(near[-s]), wide(near[s])
-        if halves:
-            a = jnp.concatenate([a[:half] + wide(low), a[half:]], axis=0)
-            b = jnp.concatenate([b[:half], b[half:] + wide(high)], axis=0)
-        else:
-            a, b = a + wide(low), b + wide(high)
-        low = lax.ppermute(a.astype(jnp.bfloat16), axis, down_)
-        high = lax.ppermute(b.astype(jnp.bfloat16), axis, up)
-        halves = False
-    if halves:
-        back = jnp.concatenate([wide(low), wide(high)], axis=0)
-    else:
-        back = wide(low) + wide(high)
-    return wide(near[0]) + back
+        near = partials[4 * s - 3 : 4 * s + 1]
+        low = [hop(low[0], near[0], down_), hop(low[1], near[1], down_)]
+        high = [hop(high[0], near[2], up), hop(high[1], near[3], up)]
+    halves = []
+    for h, own in enumerate((mixed[:half], mixed[half:])):
+        for there in (low[h], high[h]):
+            own = own if there is None else own + wide(there)
+        halves.append(own)
+    return jnp.concatenate(halves, axis=0)
 
 
 def solution(mesh):

time: 103 us -> 105 us (1.019)
  starting transfers between devices: 24.9 us -> 34.5 us
  waiting for transfers between devices: 22.3 us -> 13.6 us
    ppermute x8 -> x12, waiting for transfers between devices: 14.5 us -> 4.26 us  [the longest x6 4.24 us: hop(): return lax.ppermute(total, axis, perm)]
    ppermute x8 -> x12, starting transfers between devices: 14.9 us -> 24.5 us  [the longest x6 11.6 us: hop(): return lax.ppermute(total, axis, perm)]
    ppermute x3, waiting for transfers between devices: 0.01 us -> 1.63 us  [on_device(): lax.ppermute(meta, 'expert', [(i, (i - k) % n_owner) for i in range(n_own...]
  transfers between devices with their start and end apart: 24 -> 28, of which waited for: 11 -> 8; matrix products, arithmetic and copies ran while one was open for 2% -> 2% of each run, Pallas kernels for 43% -> 43%
where the time goes in v12:
time: 105 us
  Pallas kernels  51.3 us (49%)
  starting transfers between devices  34.5 us (33%)
  waiting for transfers between devices  13.6 us (13%)
  other arithmetic  3.67 us (3%)
  local copies, waits for them, and re-layouts  1.14 us (1%)
    pallas_call x13, Pallas kernels, call(): pl.pallas_call(whole, out_shape=tuple(outs), in_specs=[SMEM] + [spec for...  50.6 us
    ppermute x6, starting transfers between devices, hop(): return lax.ppermute(total, axis, perm)  11.6 us
    ppermute x13, waiting for transfers between devices, flip(): lax.ppermute(x, axis, [(i, i ^ k) for i in range(lax.axis_size(axis))])  7.74 us
    ppermute x13, starting transfers between devices, flip(): lax.ppermute(x, axis, [(i, i ^ k) for i in range(lax.axis_size(axis))])  6.2 us
    ppermute x2, starting transfers between devices, gathered(): lax.ppermute(above[1], axis, down_)  5.91 us
    ppermute x6, waiting for transfers between devices, hop(): return lax.ppermute(total, axis, perm)  4.24 us
    ppermute x1, starting transfers between devices, gathered(): above = [lax.ppermute(above[0], axis, down_), far_down]  3.92 us
    ppermute x3, starting transfers between devices, on_device(): lax.ppermute(meta, 'expert', [(i, (i - k) % n_owner) for i in range(n_own...  3.83 us
  transfers between devices with their start and end apart: 28, of which 8 were waited for; matrix products, arithmetic and copies ran while one was open for 2% of the time, Pallas kernels for 43%

profile of v12, /device:TPU:0, one launch (start us, length us, event | category | flops | bytes accessed | tf_op | source)
XLA Modules:
  0.0 104.8 jit_solution(14281830281892359293)
XLA Ops:
  0.0 1.0 fusion.8
  1.0 3.1 %collective-permute-start = (bf16[32,1536]{1,0:T(8,128)(2,1)S(1)}, bf16[32,1536]{1,0:T(8,128)(2,1)S(1)}, u32[]{:S(2)}, u32[]{:S(2)}) collective-permute-start(bf16[32,1536]{1,0:T(8,128)(2,1)S(1)} %get-tuple-element.82), channel_id=1, source_target_pairs={{0,4},{4,8},{8,12},{12,0},{1,5},{5,9},{9,13},{13,1},{2,6},{6,10},{... | collective-permute-start | bytes 294920 | tf_op jit(solution)/shard_map/ppermute | solution.py:368
  4.0 2.1 %collective-permute-start.3 = (bf16[32,1536]{1,0:T(8,128)(2,1)S(1)}, bf16[32,1536]{1,0:T(8,128)(2,1)S(1)}, u32[]{:S(2)}, u32[]{:S(2)}) collective-permute-start(bf16[32,1536]{1,0:T(8,128)(2,1)S(1)} %get-tuple-element.81), channel_id=1, source_target_pairs={{0,12},{4,0},{8,4},{12,8},{1,13},{5,1},{9,5},{13,9},{2,14},{6,2},{... | collective-permute-start | bytes 294920 | tf_op jit(solution)/shard_map/ppermute | solution.py:368
  7.5 3.8 %collective-permute-start.7 = (f32[16,64]{1,0:T(8,128)S(1)}, f32[16,64]{1,0:T(8,128)S(1)}, u32[]{:S(2)}, u32[]{:S(2)}) collective-permute-start(f32[16,64]{1,0:T(8,128)S(1)} %pad_maximum_fusion.8.refs_0_), channel_id=1, source_target_pairs={{0,12},{4,0},{8,4},{12,8},{1,13},{5,1},{9,5},{13,9},{2,14},{6,2},{... | collective-permute-start | bytes 12296 | tf_op jit(solution)/shard_map/ppermute | solution.py:302
  11.3 1.6 %collective-permute-done.6.refs_1_ = f32[16,64]{1,0:T(8,128)S(1)} collective-permute-done((f32[16,64]{1,0:T(8,128)S(1)}, f32[16,64]{1,0:T(8,128)S(1)}, u32[]{:S(2)}, u32[]{:S(2)}) %collective-permute-start.6) | collective-permute-done | bytes 4128 | tf_op jit(solution)/shard_map/ppermute | solution.py:302
  13.0 3.9 %collective-permute-start.2 = (bf16[32,1536]{1,0:T(8,128)(2,1)S(1)}, bf16[32,1536]{1,0:T(8,128)(2,1)S(1)}, u32[]{:S(2)}, u32[]{:S(2)}) collective-permute-start(bf16[32,1536]{1,0:T(8,128)(2,1)S(1)} %get-tuple-element.82), channel_id=1, source_target_pairs={{0,12},{4,0},{8,4},{12,8},{1,13},{5,1},{9,5},{13,9},{2,14},{6,2},{... | collective-permute-start | bytes 294920 | tf_op jit(solution)/shard_map/ppermute | solution.py:370
  16.9 3.8 %collective-permute-start.5 = (bf16[32,1536]{1,0:T(8,128)(2,1)S(1)}, bf16[32,1536]{1,0:T(8,128)(2,1)S(1)}, u32[]{:S(2)}, u32[]{:S(2)}) collective-permute-start(bf16[32,1536]{1,0:T(8,128)(2,1)S(1)} %collective-permute-done.3.refs_4_), channel_id=1, source_target_pairs={{0,12},{4,0},{8,4},{12,8},{1,13},{5,1},{9,5},{13,9},{2,14},{6,2},{... | collective-permute-start | bytes 294920 | tf_op jit(solution)/shard_map/ppermute | solution.py:373
  20.8 3.4 %stage.1.refs_8_ = bf16[2,2,1536,512]{3,2,1,0:T(8,128)(2,1)S(1)} custom-call(s32[3]{0:T(128)S(1)} %pad_add_fusion.info, bf16[8,1536,1024]{2,1,0:T(8,128)(2,1)} %refs_9_.7, bf16[8,1536,1024]{2,1,0:T(8,128)(2,1)} %refs_10_.7), custom_call_target="tpu_custom_call" | custom-call | flops 1 | bytes 1 | tf_op jit(solution)/shard_map/stage/pallas_call | solution.py:113
  24.2 0.8 route.1
  25.0 4.5 %send_half.4 = (bf16[2,256,512]{2,1,0:T(8,128)(2,1)S(1)}, bf16[256,1536]{1,0:T(8,128)(2,1)S(1)}, bf16[2,2,1536,512]{3,2,1,0:T(8,128)(2,1)S(1)}) custom-call(s32[3]{0:T(128)S(1)} %pad_add_fusion.info, bf16[64,1536]{1,0:T(8,128)(2,1)S(1)} %copy-done, bf16[32,1536]{1,0:T(8,128)(2,1)S(1)} %collective-permute-done.refs_1_, ...), custom_call_target="tpu_custom_call" | custom-call | flops 1 | bytes 1 | tf_op jit(solution)/shard_map/send_half/pallas_call | solution.py:113
  29.6 4.2 %keep_half.4 = (bf16[2,256,512]{2,1,0:T(8,128)(2,1)S(1)}, bf16[2,2,1536,512]{3,2,1,0:T(8,128)(2,1)S(1)}) custom-call(s32[3]{0:T(128)S(1)} %pad_add_fusion.info, bf16[256,1536]{1,0:T(8,128)(2,1)S(1)} %get-tuple-element.43.refs_0_, bf16[2,2,1536,512]{3,2,1,0:T(8,128)(2,1)S(1)} %get-tuple-element.44.refs_1_, bf16[8,1536,1024]{2,1,0:T(8,128)(2,1)} %refs_9_.7, ...), custom_call_target="tpu_custom_call" | custom-call | flops 1 | bytes 1 | tf_op jit(solution)/shard_map/keep_half/pallas_call | solution.py:113
  34.0 1.7 %collective-permute-start.11 = (bf16[1,256,512]{2,1,0:T(8,128)(2,1)S(1)}, bf16[1,256,512]{2,1,0:T(8,128)(2,1)S(1)}, u32[]{:S(2)}, u32[]{:S(2)}) collective-permute-start(bf16[1,256,512]{2,1,0:T(8,128)(2,1)S(1)} %slice.179.refs_11_), channel_id=1, source_target_pairs={{0,2},{1,3},{2,0},{3,1},{4,6},{5,7},{6,4},{7,5},{8,10},{9,11},{10,... | collective-permute-start | bytes 786440 | tf_op jit(solution)/shard_map/ppermute | solution.py:23
  35.8 4.6 %send_half.5 = (bf16[2,256,512]{2,1,0:T(8,128)(2,1)S(1)}, bf16[256,1536]{1,0:T(8,128)(2,1)S(1)}, bf16[2,2,1536,512]{3,2,1,0:T(8,128)(2,1)S(1)}) custom-call(s32[3]{0:T(128)S(1)} %pad_add_fusion.info, bf16[64,1536]{1,0:T(8,128)(2,1)S(1)} %copy-done, bf16[32,1536]{1,0:T(8,128)(2,1)S(1)} %collective-permute-done.refs_1_, ...), custom_call_target="tpu_custom_call" | custom-call | flops 1 | bytes 1 | tf_op jit(solution)/shard_map/send_half/pallas_call | solution.py:113
  40.6 4.2 %keep_half.5 = (bf16[2,256,512]{2,1,0:T(8,128)(2,1)S(1)}, bf16[2,2,1536,512]{3,2,1,0:T(8,128)(2,1)S(1)}) custom-call(s32[3]{0:T(128)S(1)} %pad_add_fusion.info, bf16[256,1536]{1,0:T(8,128)(2,1)S(1)} %get-tuple-element.48.refs_0_, bf16[2,2,1536,512]{3,2,1,0:T(8,128)(2,1)S(1)} %get-tuple-element.49.refs_1_, bf16[8,1536,1024]{2,1,0:T(8,128)(2,1)} %refs_9_.7, ...), custom_call_target="tpu_custom_call" | custom-call | flops 1 | bytes 1 | tf_op jit(solution)/shard_map/keep_half/pallas_call | solution.py:113
  45.7 4.5 %send_half.6 = (bf16[2,256,512]{2,1,0:T(8,128)(2,1)S(1)}, bf16[256,1536]{1,0:T(8,128)(2,1)S(1)}, bf16[2,2,1536,512]{3,2,1,0:T(8,128)(2,1)S(1)}) custom-call(s32[3]{0:T(128)S(1)} %pad_add_fusion.info, bf16[64,1536]{1,0:T(8,128)(2,1)S(1)} %copy-done, bf16[32,1536]{1,0:T(8,128)(2,1)S(1)} %collective-permute-done.refs_1_, ...), custom_call_target="tpu_custom_call" | custom-call | flops 1 | bytes 1 | tf_op jit(solution)/shard_map/send_half/pallas_call | solution.py:113
  50.3 4.2 %keep_half.6 = (bf16[2,256,512]{2,1,0:T(8,128)(2,1)S(1)}, bf16[2,2,1536,512]{3,2,1,0:T(8,128)(2,1)S(1)}) custom-call(s32[3]{0:T(128)S(1)} %pad_add_fusion.info, bf16[256,1536]{1,0:T(8,128)(2,1)S(1)} %get-tuple-element.53.refs_0_, bf16[2,2,1536,512]{3,2,1,0:T(8,128)(2,1)S(1)} %get-tuple-element.54.refs_1_, bf16[8,1536,1024]{2,1,0:T(8,128)(2,1)} %refs_9_.7, ...), custom_call_target="tpu_custom_call" | custom-call | flops 1 | bytes 1 | tf_op jit(solution)/shard_map/keep_half/pallas_call | solution.py:113
  54.5 2.1 %collective-permute-done.13.refs_1_ = bf16[1,256,768]{2,1,0:T(8,128)(2,1)S(1)} collective-permute-done((bf16[1,256,768]{2,1,0:T(8,128)(2,1)S(1)}, bf16[1,256,768]{2,1,0:T(8,128)(2,1)S(1)}, u32[]{:S(2)}, u32[]{:S(2)}) %collective-permute-start.13) | collective-permute-done | bytes 393248 | tf_op jit(solution)/shard_map/ppermute | solution.py:23
  57.5 4.7 %send_half.7 = (bf16[2,256,512]{2,1,0:T(8,128)(2,1)S(1)}, bf16[256,1536]{1,0:T(8,128)(2,1)S(1)}, bf16[2,2,1536,512]{3,2,1,0:T(8,128)(2,1)S(1)}) custom-call(s32[3]{0:T(128)S(1)} %pad_add_fusion.info, bf16[64,1536]{1,0:T(8,128)(2,1)S(1)} %copy-done, bf16[32,1536]{1,0:T(8,128)(2,1)S(1)} %collective-permute-done.refs_1_, ...), custom_call_target="tpu_custom_call" | custom-call | flops 1 | bytes 1 | tf_op jit(solution)/shard_map/send_half/pallas_call | solution.py:113
  62.3 3.6 %keep_half.7 = (bf16[2,256,512]{2,1,0:T(8,128)(2,1)S(1)}, bf16[2,1024,1536]{2,1,0:T(8,128)(2,1)S(1)}) custom-call(s32[3]{0:T(128)S(1)} %pad_add_fusion.info, bf16[256,1536]{1,0:T(8,128)(2,1)S(1)} %get-tuple-element.58.refs_0_, bf16[2,2,1536,512]{3,2,1,0:T(8,128)(2,1)S(1)} %get-tuple-element.59.refs_1_, bf16[8,1024,1536]{2,1,0:T(8,128)(2,1)} %refs_7_.3), custom_call_target="tpu_custom_call" | custom-call | flops 1 | bytes 1 | tf_op jit(solution)/shard_map/keep_half/pallas_call | solution.py:113
  66.0 1.7 %collective-permute-done.15.refs_1_ = bf16[1,256,768]{2,1,0:T(8,128)(2,1)S(1)} collective-permute-done((bf16[1,256,768]{2,1,0:T(8,128)(2,1)S(1)}, bf16[1,256,768]{2,1,0:T(8,128)(2,1)S(1)}, u32[]{:S(2)}, u32[]{:S(2)}) %collective-permute-start.15) | collective-permute-done | bytes 393248 | tf_op jit(solution)/shard_map/ppermute | solution.py:23
  69.4 0.9 collective-permute-done.18.refs_2_
  70.3 3.4 %down.4 = (f32[256,1536]{1,0:T(8,128)S(1)}, bf16[2,1024,1536]{2,1,0:T(8,128)(2,1)S(1)}) custom-call(s32[3]{0:T(128)S(1)} %pad_add_fusion.info, bf16[1,256,256]{2,1,0:T(8,128)(2,1)S(1)} %fusion.3.refs_0_, bf16[1,256,768]{2,1,0:T(8,128)(2,1)S(1)} %copy-done.2, bf16[2,256,256]{2,1,0:T(8,128)(2,1)S(1)} %collective-permute-done.18.refs_2_, ...), custom_call_target="tpu_custom_call" | custom-call | flops 1 | bytes 1 | tf_op jit(solution)/shard_map/down/pallas_call | solution.py:113
  73.8 3.5 %down.5 = (f32[256,1536]{1,0:T(8,128)S(1)}, bf16[2,1024,1536]{2,1,0:T(8,128)(2,1)S(1)}) custom-call(s32[3]{0:T(128)S(1)} %pad_add_fusion.info, bf16[1,256,256]{2,1,0:T(8,128)(2,1)S(1)} %fusion.2.refs_0_, bf16[1,256,768]{2,1,0:T(8,128)(2,1)S(1)} %collective-permute-done.15.refs_1_, bf16[2,256,256]{2,1,0:T(8,128)(2,1)S(1)} %collective-permute-done.17.refs_2_, ...), custom_call_target="tpu_custom_call" | custom-call | flops 1 | bytes 1 | tf_op jit(solution)/shard_map/down/pallas_call | solution.py:113
  78.3 1.7 %collective-permute-start.19 = (bf16[1,256,256]{2,1,0:T(8,128)(2,1)S(1)}, bf16[1,256,256]{2,1,0:T(8,128)(2,1)S(1)}, u32[]{:S(2)}, u32[]{:S(2)}) collective-permute-start(bf16[1,256,256]{2,1,0:T(8,128)(2,1)S(1)} %fusion.refs_8_.refs_0_), channel_id=1, source_target_pairs={{0,2},{1,3},{2,0},{3,1},{4,6},{5,7},{6,4},{7,5},{8,10},{9,11},{10,... | collective-permute-start | bytes 393224 | tf_op jit(solution)/shard_map/ppermute | solution.py:23
  80.0 3.5 %down.6 = (f32[256,1536]{1,0:T(8,128)S(1)}, bf16[2,1024,1536]{2,1,0:T(8,128)(2,1)S(1)}) custom-call(s32[3]{0:T(128)S(1)} %pad_add_fusion.info, bf16[1,256,256]{2,1,0:T(8,128)(2,1)S(1)} %fusion.1.refs_0_, bf16[1,256,768]{2,1,0:T(8,128)(2,1)S(1)} %collective-permute-done.16.refs_1_, bf16[2,256,256]{2,1,0:T(8,128)(2,1)S(1)} %collective-permute-done.20.refs_2_, ...), custom_call_target="tpu_custom_call" | custom-call | flops 1 | bytes 1 | tf_op jit(solution)/shard_map/down/pallas_call | solution.py:113
  83.5 0.8 collective-permute-done.19.refs_1_
  84.3 1.5 %collective-permute-done.21.refs_2_ = bf16[2,256,256]{2,1,0:T(8,128)(2,1)S(1)} collective-permute-done((bf16[2,256,256]{2,1,0:T(8,128)(2,1)S(1)}, bf16[2,256,256]{2,1,0:T(8,128)(2,1)S(1)}, u32[]{:S(2)}, u32[]{:S(2)}) %collective-permute-start.21) | collective-permute-done | bytes 262176 | tf_op jit(solution)/shard_map/ppermute | solution.py:23
  85.9 2.2 %down.7 = (bf16[64,1536]{1,0:T(8,128)(2,1)S(1)}, bf16[32,1536]{1,0:T(8,128)(2,1)S(1)}, bf16[32,1536]{1,0:T(8,128)(2,1)S(1)}, bf16[32,1536]{1,0:T(8,128)(2,1)S(1)...) custom-call(s32[3]{0:T(128)S(1)} %pad_add_fusion.info, ...), custom_call_target="tpu_custom_call" | custom-call | flops 1 | bytes 1 | tf_op jit(solution)/shard_map/down/pallas_call | solution.py:113
  88.2 3.8 %collective-permute-start.22 = (bf16[32,1536]{1,0:T(8,128)(2,1)S(1)}, bf16[32,1536]{1,0:T(8,128)(2,1)S(1)}, u32[]{:S(2)}, u32[]{:S(2)}) collective-permute-start(bf16[32,1536]{1,0:T(8,128)(2,1)S(1)} %get-tuple-element.74), channel_id=1, source_target_pairs={{0,12},{4,0},{8,4},{12,8},{1,13},{5,1},{9,5},{13,9},{2,14},{6,2},{... | collective-permute-start | bytes 294920 | tf_op jit(solution)/shard_map/ppermute | solution.py:388
  92.0 3.8 %collective-permute-start.25 = (bf16[32,1536]{1,0:T(8,128)(2,1)S(1)}, bf16[32,1536]{1,0:T(8,128)(2,1)S(1)}, u32[]{:S(2)}, u32[]{:S(2)}) collective-permute-start(bf16[32,1536]{1,0:T(8,128)(2,1)S(1)} %get-tuple-element.76), channel_id=1, source_target_pairs={{0,12},{4,0},{8,4},{12,8},{1,13},{5,1},{9,5},{13,9},{2,14},{6,2},{... | collective-permute-start | bytes 294920 | tf_op jit(solution)/shard_map/ppermute | solution.py:388
  96.0 3.9 %collective-permute-start.23 = (bf16[32,1536]{1,0:T(8,128)(2,1)S(1)}, bf16[32,1536]{1,0:T(8,128)(2,1)S(1)}, u32[]{:S(2)}, u32[]{:S(2)}) collective-permute-start(bf16[32,1536]{1,0:T(8,128)(2,1)S(1)} %add_convert_fusion.1), channel_id=1, source_target_pairs={{0,12},{4,0},{8,4},{12,8},{1,13},{5,1},{9,5},{13,9},{2,14},{6,2},{... | collective-permute-start | bytes 294920 | tf_op jit(solution)/shard_map/ppermute | solution.py:388
  99.9 4.2 %collective-permute-done.27 = bf16[32,1536]{1,0:T(8,128)(2,1)S(1)} collective-permute-done((bf16[32,1536]{1,0:T(8,128)(2,1)S(1)}, bf16[32,1536]{1,0:T(8,128)(2,1)S(1)}, u32[]{:S(2)}, u32[]{:S(2)}) %collective-permute-start.27) | collective-permute-done | bytes 98336 | tf_op jit(solution)/shard_map/ppermute | solution.py:388
  (81 shorter events, 7.5 us)
Async XLA Ops:
  1.0 15.9 %collective-permute-start = (bf16[32,1536]{1,0:T(8,128)(2,1)S(1)}, bf16[32,1536]{1,0:T(8,128)(2,1)S(1)}, u32[]{:S(2)}, u32[]{:S(2)}) collective-permute-start(bf16[32,1536]{1,0:T(8,128)(2,1)S(1)} %get-tuple-element.82), channel_id=1, source_target_pairs={{0,4},{4,8},{8,12},{12,0},{1,5},{5,9},{9,13},{13,1},{2,6},{6,10},{... | collective-permute-start | bytes 294920 | tf_op jit(solution)/shard_map/ppermute | solution.py:368
  4.0 12.9 %collective-permute-start.3 = (bf16[32,1536]{1,0:T(8,128)(2,1)S(1)}, bf16[32,1536]{1,0:T(8,128)(2,1)S(1)}, u32[]{:S(2)}, u32[]{:S(2)}) collective-permute-start(bf16[32,1536]{1,0:T(8,128)(2,1)S(1)} %get-tuple-element.81), channel_id=1, source_target_pairs={{0,12},{4,0},{8,4},{12,8},{1,13},{5,1},{9,5},{13,9},{2,14},{6,2},{... | collective-permute-start | bytes 294920 | tf_op jit(solution)/shard_map/ppermute | solution.py:368
  7.5 5.4 %collective-permute-start.6 = (f32[16,64]{1,0:T(8,128)S(1)}, f32[16,64]{1,0:T(8,128)S(1)}, u32[]{:S(2)}, u32[]{:S(2)}) collective-permute-start(f32[16,64]{1,0:T(8,128)S(1)} %pad_maximum_fusion.8.refs_0_), channel_id=1, source_target_pairs={{0,4},{4,8},{8,12},{12,0},{1,5},{5,9},{9,13},{13,1},{2,6},{6,10},{... | collective-permute-start | bytes 12296 | tf_op jit(solution)/shard_map/ppermute | solution.py:302
  7.5 5.5 %collective-permute-start.7 = (f32[16,64]{1,0:T(8,128)S(1)}, f32[16,64]{1,0:T(8,128)S(1)}, u32[]{:S(2)}, u32[]{:S(2)}) collective-permute-start(f32[16,64]{1,0:T(8,128)S(1)} %pad_maximum_fusion.8.refs_0_), channel_id=1, source_target_pairs={{0,12},{4,0},{8,4},{12,8},{1,13},{5,1},{9,5},{13,9},{2,14},{6,2},{... | collective-permute-start | bytes 12296 | tf_op jit(solution)/shard_map/ppermute | solution.py:302
  11.3 12.9 %collective-permute-start.8 = (f32[16,64]{1,0:T(8,128)S(1)}, f32[16,64]{1,0:T(8,128)S(1)}, u32[]{:S(2)}, u32[]{:S(2)}) collective-permute-start(f32[16,64]{1,0:T(8,128)S(1)} %pad_maximum_fusion.8.refs_0_), channel_id=1, source_target_pairs={{0,8},{4,12},{8,0},{12,4},{1,9},{5,13},{9,1},{13,5},{2,10},{6,14},... | collective-permute-start | bytes 12296 | tf_op jit(solution)/shard_map/ppermute | solution.py:302
  13.0 12.0 %collective-permute-start.1 = (bf16[32,1536]{1,0:T(8,128)(2,1)S(1)}, bf16[32,1536]{1,0:T(8,128)(2,1)S(1)}, u32[]{:S(2)}, u32[]{:S(2)}) collective-permute-start(bf16[32,1536]{1,0:T(8,128)(2,1)S(1)} %get-tuple-element.81), channel_id=1, source_target_pairs={{0,4},{4,8},{8,12},{12,0},{1,5},{5,9},{9,13},{13,1},{2,6},{6,10},{... | collective-permute-start | bytes 294920 | tf_op jit(solution)/shard_map/ppermute | solution.py:369
  13.0 12.0 %collective-permute-start.2 = (bf16[32,1536]{1,0:T(8,128)(2,1)S(1)}, bf16[32,1536]{1,0:T(8,128)(2,1)S(1)}, u32[]{:S(2)}, u32[]{:S(2)}) collective-permute-start(bf16[32,1536]{1,0:T(8,128)(2,1)S(1)} %get-tuple-element.82), channel_id=1, source_target_pairs={{0,12},{4,0},{8,4},{12,8},{1,13},{5,1},{9,5},{13,9},{2,14},{6,2},{... | collective-permute-start | bytes 294920 | tf_op jit(solution)/shard_map/ppermute | solution.py:370
  16.9 8.1 %collective-permute-start.4 = (bf16[32,1536]{1,0:T(8,128)(2,1)S(1)}, bf16[32,1536]{1,0:T(8,128)(2,1)S(1)}, u32[]{:S(2)}, u32[]{:S(2)}) collective-permute-start(bf16[32,1536]{1,0:T(8,128)(2,1)S(1)} %collective-permute-done.refs_1_), channel_id=1, source_target_pairs={{0,4},{4,8},{8,12},{12,0},{1,5},{5,9},{9,13},{13,1},{2,6},{6,10},{... | collective-permute-start | bytes 294920 | tf_op jit(solution)/shard_map/ppermute | solution.py:373
  16.9 8.1 %collective-permute-start.5 = (bf16[32,1536]{1,0:T(8,128)(2,1)S(1)}, bf16[32,1536]{1,0:T(8,128)(2,1)S(1)}, u32[]{:S(2)}, u32[]{:S(2)}) collective-permute-start(bf16[32,1536]{1,0:T(8,128)(2,1)S(1)} %collective-permute-done.3.refs_4_), channel_id=1, source_target_pairs={{0,12},{4,0},{8,4},{12,8},{1,13},{5,1},{9,5},{13,9},{2,14},{6,2},{... | collective-permute-start | bytes 294920 | tf_op jit(solution)/shard_map/ppermute | solution.py:373
  20.8 4.2 %copy-start = (bf16[64,1536]{1,0:T(8,128)(2,1)S(1)}, bf16[64,1536]{1,0:T(8,128)(2,1)}, u32[]{:S(2)}) copy-start(bf16[64,1536]{1,0:T(8,128)(2,1)} %refs_0_.9) | copy-start | bytes 589828
  29.5 4.3 %collective-permute-start.9 = (bf16[2,256,512]{2,1,0:T(8,128)(2,1)S(1)}, bf16[2,256,512]{2,1,0:T(8,128)(2,1)S(1)}, u32[]{:S(2)}, u32[]{:S(2)}) collective-permute-start(bf16[2,256,512]{2,1,0:T(8,128)(2,1)S(1)} %get-tuple-element.47), channel_id=1, source_target_pairs={{0,1},{1,0},{2,3},{3,2},{4,5},{5,4},{6,7},{7,6},{8,9},{9,8},{10,11... | collective-permute-start | bytes 1572872 | tf_op jit(solution)/shard_map/ppermute | solution.py:23
  34.0 10.8 %collective-permute-start.11 = (bf16[1,256,512]{2,1,0:T(8,128)(2,1)S(1)}, bf16[1,256,512]{2,1,0:T(8,128)(2,1)S(1)}, u32[]{:S(2)}, u32[]{:S(2)}) collective-permute-start(bf16[1,256,512]{2,1,0:T(8,128)(2,1)S(1)} %slice.179.refs_11_), channel_id=1, source_target_pairs={{0,2},{1,3},{2,0},{3,1},{4,6},{5,7},{6,4},{7,5},{8,10},{9,11},{10,... | collective-permute-start | bytes 786440 | tf_op jit(solution)/shard_map/ppermute | solution.py:23
  40.4 4.7 %collective-permute-start.10 = (bf16[2,256,512]{2,1,0:T(8,128)(2,1)S(1)}, bf16[2,256,512]{2,1,0:T(8,128)(2,1)S(1)}, u32[]{:S(2)}, u32[]{:S(2)}) collective-permute-start(bf16[2,256,512]{2,1,0:T(8,128)(2,1)S(1)} %get-tuple-element.52), channel_id=1, source_target_pairs={{0,1},{1,0},{2,3},{3,2},{4,5},{5,4},{6,7},{7,6},{8,9},{9,8},{10,11... | collective-permute-start | bytes 1572872 | tf_op jit(solution)/shard_map/ppermute | solution.py:23
  45.3 11.4 %collective-permute-start.13 = (bf16[1,256,768]{2,1,0:T(8,128)(2,1)S(1)}, bf16[1,256,768]{2,1,0:T(8,128)(2,1)S(1)}, u32[]{:S(2)}, u32[]{:S(2)}) collective-permute-start(bf16[1,256,768]{2,1,0:T(8,128)(2,1)S(1)} %pad_maximum_fusion.refs_11_), channel_id=1, source_target_pairs={{0,2},{1,3},{2,0},{3,1},{4,6},{5,7},{6,4},{7,5},{8,10},{9,11},{10,... | collective-permute-start | bytes 1179656 | tf_op jit(solution)/shard_map/ppermute | solution.py:23
  50.2 6.6 %collective-permute-start.12 = (bf16[2,256,512]{2,1,0:T(8,128)(2,1)S(1)}, bf16[2,256,512]{2,1,0:T(8,128)(2,1)S(1)}, u32[]{:S(2)}, u32[]{:S(2)}) collective-permute-start(bf16[2,256,512]{2,1,0:T(8,128)(2,1)S(1)} %get-tuple-element.57), channel_id=1, source_target_pairs={{0,1},{1,0},{2,3},{3,2},{4,5},{5,4},{6,7},{7,6},{8,9},{9,8},{10,11... | collective-permute-start | bytes 1572872 | tf_op jit(solution)/shard_map/ppermute | solution.py:23
  56.7 5.6 %copy-start.1 = (bf16[1,256,768]{2,1,0:T(8,128)(2,1)}, bf16[1,256,768]{2,1,0:T(8,128)(2,1)S(1)}, u32[]{:S(2)}) copy-start(bf16[1,256,768]{2,1,0:T(8,128)(2,1)S(1)} %collective-permute-done.13.refs_1_) | copy-start | bytes 1179652
  57.1 10.6 %collective-permute-start.15 = (bf16[1,256,768]{2,1,0:T(8,128)(2,1)S(1)}, bf16[1,256,768]{2,1,0:T(8,128)(2,1)S(1)}, u32[]{:S(2)}, u32[]{:S(2)}) collective-permute-start(bf16[1,256,768]{2,1,0:T(8,128)(2,1)S(1)} %pad_maximum_fusion.1.refs_11_), channel_id=1, source_target_pairs={{0,2},{1,3},{2,0},{3,1},{4,6},{5,7},{6,4},{7,5},{8,10},{9,11},{10,... | collective-permute-start | bytes 1179656 | tf_op jit(solution)/shard_map/ppermute | solution.py:23
  62.2 5.6 %collective-permute-start.14 = (bf16[2,256,512]{2,1,0:T(8,128)(2,1)S(1)}, bf16[2,256,512]{2,1,0:T(8,128)(2,1)S(1)}, u32[]{:S(2)}, u32[]{:S(2)}) collective-permute-start(bf16[2,256,512]{2,1,0:T(8,128)(2,1)S(1)} %get-tuple-element.61), channel_id=1, source_target_pairs={{0,1},{1,0},{2,3},{3,2},{4,5},{5,4},{6,7},{7,6},{8,9},{9,8},{10,11... | collective-permute-start | bytes 1572872 | tf_op jit(solution)/shard_map/ppermute | solution.py:23
  62.3 6.4 %slice-start = ((bf16[1,256,768]{2,1,0:T(8,128)(2,1)}), bf16[1,256,256]{2,1,0:T(8,128)(2,1)S(1)}, s32[]{:S(2)}) async-start(bf16[1,256,768]{2,1,0:T(8,128)(2,1)} %copy-done.1), calls=%async_computation | async-start | bytes 262144 | tf_op jit(solution)/shard_map/slice | solution.py:267
  65.9 4.4 %copy-start.2 = (bf16[1,256,768]{2,1,0:T(8,128)(2,1)S(1)}, bf16[1,256,768]{2,1,0:T(8,128)(2,1)}, u32[]{:S(2)}) copy-start(bf16[1,256,768]{2,1,0:T(8,128)(2,1)} %copy-done.1) | copy-start | bytes 1179652
  68.1 9.9 %collective-permute-start.16 = (bf16[1,256,768]{2,1,0:T(8,128)(2,1)S(1)}, bf16[1,256,768]{2,1,0:T(8,128)(2,1)S(1)}, u32[]{:S(2)}, u32[]{:S(2)}) collective-permute-start(bf16[1,256,768]{2,1,0:T(8,128)(2,1)S(1)} %pad_maximum_fusion.2.refs_7_), channel_id=1, source_target_pairs={{0,2},{1,3},{2,0},{3,1},{4,6},{5,7},{6,4},{7,5},{8,10},{9,11},{10,... | collective-permute-start | bytes 1179656 | tf_op jit(solution)/shard_map/ppermute | solution.py:23
  68.7 1.6 %collective-permute-start.18 = (bf16[2,256,256]{2,1,0:T(8,128)(2,1)S(1)}, bf16[2,256,256]{2,1,0:T(8,128)(2,1)S(1)}, u32[]{:S(2)}, u32[]{:S(2)}) collective-permute-start(bf16[2,256,256]{2,1,0:T(8,128)(2,1)S(1)} %pad_maximum_fusion.4), channel_id=1, source_target_pairs={{0,1},{1,0},{2,3},{3,2},{4,5},{5,4},{6,7},{7,6},{8,9},{9,8},{10,11... | collective-permute-start | bytes 786440 | tf_op jit(solution)/shard_map/ppermute | solution.py:23
  68.8 4.9 %collective-permute-start.17 = (bf16[2,256,256]{2,1,0:T(8,128)(2,1)S(1)}, bf16[2,256,256]{2,1,0:T(8,128)(2,1)S(1)}, u32[]{:S(2)}, u32[]{:S(2)}) collective-permute-start(bf16[2,256,256]{2,1,0:T(8,128)(2,1)S(1)} %pad_maximum_fusion.3), channel_id=1, source_target_pairs={{0,1},{1,0},{2,3},{3,2},{4,5},{5,4},{6,7},{7,6},{8,9},{9,8},{10,11... | collective-permute-start | bytes 786440 | tf_op jit(solution)/shard_map/ppermute | solution.py:23
  78.0 2.0 %collective-permute-start.20 = (bf16[2,256,256]{2,1,0:T(8,128)(2,1)S(1)}, bf16[2,256,256]{2,1,0:T(8,128)(2,1)S(1)}, u32[]{:S(2)}, u32[]{:S(2)}) collective-permute-start(bf16[2,256,256]{2,1,0:T(8,128)(2,1)S(1)} %pad_maximum_fusion.5), channel_id=1, source_target_pairs={{0,1},{1,0},{2,3},{3,2},{4,5},{5,4},{6,7},{7,6},{8,9},{9,8},{10,11... | collective-permute-start | bytes 786440 | tf_op jit(solution)/shard_map/ppermute | solution.py:23
  78.3 6.0 %collective-permute-start.19 = (bf16[1,256,256]{2,1,0:T(8,128)(2,1)S(1)}, bf16[1,256,256]{2,1,0:T(8,128)(2,1)S(1)}, u32[]{:S(2)}, u32[]{:S(2)}) collective-permute-start(bf16[1,256,256]{2,1,0:T(8,128)(2,1)S(1)} %fusion.refs_8_.refs_0_), channel_id=1, source_target_pairs={{0,2},{1,3},{2,0},{3,1},{4,6},{5,7},{6,4},{7,5},{8,10},{9,11},{10,... | collective-permute-start | bytes 393224 | tf_op jit(solution)/shard_map/ppermute | solution.py:23
  84.3 1.6 %collective-permute-start.21 = (bf16[2,256,256]{2,1,0:T(8,128)(2,1)S(1)}, bf16[2,256,256]{2,1,0:T(8,128)(2,1)S(1)}, u32[]{:S(2)}, u32[]{:S(2)}) collective-permute-start(bf16[2,256,256]{2,1,0:T(8,128)(2,1)S(1)} %pad_maximum_fusion.6), channel_id=1, source_target_pairs={{0,1},{1,0},{2,3},{3,2},{4,5},{5,4},{6,7},{7,6},{8,9},{9,8},{10,11... | collective-permute-start | bytes 786440 | tf_op jit(solution)/shard_map/ppermute | solution.py:23
  88.1 7.7 %collective-permute-start.26 = (bf16[32,1536]{1,0:T(8,128)(2,1)S(1)}, bf16[32,1536]{1,0:T(8,128)(2,1)S(1)}, u32[]{:S(2)}, u32[]{:S(2)}) collective-permute-start(bf16[32,1536]{1,0:T(8,128)(2,1)S(1)} %get-tuple-element.78), channel_id=1, source_target_pairs={{0,4},{4,8},{8,12},{12,0},{1,5},{5,9},{9,13},{13,1},{2,6},{6,10},{... | collective-permute-start | bytes 294920 | tf_op jit(solution)/shard_map/ppermute | solution.py:388
  88.2 7.7 %collective-permute-start.22 = (bf16[32,1536]{1,0:T(8,128)(2,1)S(1)}, bf16[32,1536]{1,0:T(8,128)(2,1)S(1)}, u32[]{:S(2)}, u32[]{:S(2)}) collective-permute-start(bf16[32,1536]{1,0:T(8,128)(2,1)S(1)} %get-tuple-element.74), channel_id=1, source_target_pairs={{0,12},{4,0},{8,4},{12,8},{1,13},{5,1},{9,5},{13,9},{2,14},{6,2},{... | collective-permute-start | bytes 294920 | tf_op jit(solution)/shard_map/ppermute | solution.py:388
  92.0 7.9 %collective-permute-start.24 = (bf16[32,1536]{1,0:T(8,128)(2,1)S(1)}, bf16[32,1536]{1,0:T(8,128)(2,1)S(1)}, u32[]{:S(2)}, u32[]{:S(2)}) collective-permute-start(bf16[32,1536]{1,0:T(8,128)(2,1)S(1)} %get-tuple-element.75), channel_id=1, source_target_pairs={{0,4},{4,8},{8,12},{12,0},{1,5},{5,9},{9,13},{13,1},{2,6},{6,10},{... | collective-permute-start | bytes 294920 | tf_op jit(solution)/shard_map/ppermute | solution.py:388
  92.0 7.9 %collective-permute-start.25 = (bf16[32,1536]{1,0:T(8,128)(2,1)S(1)}, bf16[32,1536]{1,0:T(8,128)(2,1)S(1)}, u32[]{:S(2)}, u32[]{:S(2)}) collective-permute-start(bf16[32,1536]{1,0:T(8,128)(2,1)S(1)} %get-tuple-element.76), channel_id=1, source_target_pairs={{0,12},{4,0},{8,4},{12,8},{1,13},{5,1},{9,5},{13,9},{2,14},{6,2},{... | collective-permute-start | bytes 294920 | tf_op jit(solution)/shard_map/ppermute | solution.py:388
  95.8 8.2 %collective-permute-start.27 = (bf16[32,1536]{1,0:T(8,128)(2,1)S(1)}, bf16[32,1536]{1,0:T(8,128)(2,1)S(1)}, u32[]{:S(2)}, u32[]{:S(2)}) collective-permute-start(bf16[32,1536]{1,0:T(8,128)(2,1)S(1)} %add_convert_fusion), channel_id=1, source_target_pairs={{0,4},{4,8},{8,12},{12,0},{1,5},{5,9},{9,13},{13,1},{2,6},{6,10},{... | collective-permute-start | bytes 294920 | tf_op jit(solution)/shard_map/ppermute | solution.py:388
  96.0 8.1 %collective-permute-start.23 = (bf16[32,1536]{1,0:T(8,128)(2,1)S(1)}, bf16[32,1536]{1,0:T(8,128)(2,1)S(1)}, u32[]{:S(2)}, u32[]{:S(2)}) collective-permute-start(bf16[32,1536]{1,0:T(8,128)(2,1)S(1)} %add_convert_fusion.1), channel_id=1, source_target_pairs={{0,12},{4,0},{8,4},{12,8},{1,13},{5,1},{9,5},{13,9},{2,14},{6,2},{... | collective-permute-start | bytes 294920 | tf_op jit(solution)/shard_map/ppermute | solution.py:388

commit v13 on v12

--- a/solution.py
+++ b/solution.py
@@ -305,7 +305,7 @@
     feeds = gathered(tokens, "expert")
     rank, wt = route(metas, info, experts)
 
-    tall, wide = [feed.shape[0] for feed in feeds], tokens.shape[1]
+    tall, wide = [tok_rows] + [tok_rows // 2] * (2 * n_owner - 2), tokens.shape[1]
     bits = bits_of(n_dp)
     cross = 1 << bits[-1]
     sent, parts, total = [], [], None
@@ -360,17 +360,15 @@
 
 def gathered(x, axis):
     n = lax.axis_size(axis)
-    up, down_ = ways(n)
-    half = x.shape[0] // 2
-    below = above = [x[:half], x[half:]]
+    up, down_ = [(i, (i + 1) % n) for i in range(n)], [(i, (i - 1) % n) for i in range(n)]
+    below = above = x
     found = [x]
     for _ in range(1, n // 2):
-        far_up, far_down = lax.ppermute(below[0], axis, up), lax.ppermute(above[1], axis, down_)
-        below = [far_up, lax.ppermute(below[1], axis, up)]
-        above = [lax.ppermute(above[0], axis, down_), far_down]
-        found += below + above
+        below, above = lax.ppermute(below, axis, up), lax.ppermute(above, axis, down_)
+        found += [below, above]
     if n > 1:
-        found += [lax.ppermute(below[0], axis, up), lax.ppermute(above[1], axis, down_)]
+        half = x.shape[0] // 2
+        found += [lax.ppermute(below[:half], axis, up), lax.ppermute(above[half:], axis, down_)]
     return found
 
 

time: 105 us -> 101 us (0.962)
  starting transfers between devices: 34.5 us -> 29.9 us
  waiting for transfers between devices: 13.6 us -> 15.7 us
    ppermute x6 -> x4, starting transfers between devices: 12.9 us -> 8.27 us  [the longest x1 3.15 us: gathered(): lax.ppermute(above[half:], axis, down_)]
    ppermute x6 -> x4, waiting for transfers between devices: 0.02 us -> 3.65 us  [the longest x1 2.87 us: gathered(): lax.ppermute(above, axis, down_)]
    ppermute x3, waiting for transfers between devices: 1.63 us -> 0.01 us  [on_device(): lax.ppermute(meta, 'expert', [(i, (i - k) % n_owner) for i in range(n_own...]
  transfers between devices with their start and end apart: 28 -> 26, of which waited for: 8 -> 9; matrix products, arithmetic and copies ran while one was open for 2% -> 2% of each run, Pallas kernels for 43% -> 44%
where the time goes in v13:
time: 101 us
  Pallas kernels  51.3 us (51%)
  starting transfers between devices  29.9 us (30%)
  waiting for transfers between devices  15.7 us (16%)
  other arithmetic  3.68 us (4%)
    pallas_call x13, Pallas kernels, call(): pl.pallas_call(whole, out_shape=tuple(outs), in_specs=[SMEM] + [spec for...  50.5 us
    ppermute x6, starting transfers between devices, hop(): return lax.ppermute(total, axis, perm)  11.6 us
    ppermute x13, waiting for transfers between devices, flip(): lax.ppermute(x, axis, [(i, i ^ k) for i in range(lax.axis_size(axis))])  7.78 us
    ppermute x13, starting transfers between devices, flip(): lax.ppermute(x, axis, [(i, i ^ k) for i in range(lax.axis_size(axis))])  6.17 us
    ppermute x6, waiting for transfers between devices, hop(): return lax.ppermute(total, axis, perm)  4.24 us
    ppermute x3, starting transfers between devices, on_device(): lax.ppermute(meta, 'expert', [(i, (i - k) % n_owner) for i in range(n_own...  3.83 us
    ppermute x1, starting transfers between devices, gathered(): lax.ppermute(above[half:], axis, down_)  3.15 us
    ppermute x1, starting transfers between devices, gathered(): lax.ppermute(below, axis, up)  3.02 us
  transfers between devices with their start and end apart: 26, of which 9 were waited for; matrix products, arithmetic and copies ran while one was open for 2% of the time, Pallas kernels for 44%

profile of v13, /device:TPU:0, one launch (start us, length us, event | category | flops | bytes accessed | tf_op | source)
XLA Modules:
  0.0 101.2 jit_solution(961934033872395465)
XLA Ops:
  0.0 3.0 %collective-permute-start = (bf16[64,1536]{1,0:T(8,128)(2,1)}, bf16[64,1536]{1,0:T(8,128)(2,1)S(1)}, u32[]{:S(2)}, u32[]{:S(2)}) collective-permute-start(bf16[64,1536]{1,0:T(8,128)(2,1)} %refs_0_.9), channel_id=1, source_target_pairs={{0,4},{4,8},{8,12},{12,0},{1,5},{5,9},{9,13},{13,1},{2,6},{6,10},{... | collective-permute-start | bytes 589832 | tf_op jit(solution)/shard_map/ppermute | solution.py:367
  3.0 2.0 %collective-permute-start.1 = (bf16[64,1536]{1,0:T(8,128)(2,1)}, bf16[64,1536]{1,0:T(8,128)(2,1)S(1)}, u32[]{:S(2)}, u32[]{:S(2)}) collective-permute-start(bf16[64,1536]{1,0:T(8,128)(2,1)} %refs_0_.9), channel_id=1, source_target_pairs={{0,12},{4,0},{8,4},{12,8},{1,13},{5,1},{9,5},{13,9},{2,14},{6,2},{... | collective-permute-start | bytes 589832 | tf_op jit(solution)/shard_map/ppermute | solution.py:367
  6.4 3.8 %collective-permute-start.5 = (f32[16,64]{1,0:T(8,128)S(1)}, f32[16,64]{1,0:T(8,128)S(1)}, u32[]{:S(2)}, u32[]{:S(2)}) collective-permute-start(f32[16,64]{1,0:T(8,128)S(1)} %pad_maximum_fusion.8.refs_0_), channel_id=1, source_target_pairs={{0,12},{4,0},{8,4},{12,8},{1,13},{5,1},{9,5},{13,9},{2,14},{6,2},{... | collective-permute-start | bytes 12296 | tf_op jit(solution)/shard_map/ppermute | solution.py:302
  10.3 0.8 collective-permute-done.refs_1_
  11.1 2.9 %collective-permute-done.1.refs_2_ = bf16[64,1536]{1,0:T(8,128)(2,1)S(1)} collective-permute-done((bf16[64,1536]{1,0:T(8,128)(2,1)}, bf16[64,1536]{1,0:T(8,128)(2,1)S(1)}, u32[]{:S(2)}, u32[]{:S(2)}) %collective-permute-start.1) | collective-permute-done | bytes 196640 | tf_op jit(solution)/shard_map/ppermute | solution.py:367
  14.0 3.2 %collective-permute-start.3 = (bf16[32,1536]{1,0:T(8,128)(2,1)S(1)}, bf16[32,1536]{1,0:T(8,128)(2,1)S(1)}, u32[]{:S(2)}, u32[]{:S(2)}) collective-permute-start(bf16[32,1536]{1,0:T(8,128)(2,1)S(1)} %slice.117), channel_id=1, source_target_pairs={{0,12},{4,0},{8,4},{12,8},{1,13},{5,1},{9,5},{13,9},{2,14},{6,2},{... | collective-permute-start | bytes 294920 | tf_op jit(solution)/shard_map/ppermute | solution.py:371
  17.2 3.4 %stage.1.refs_6_ = bf16[2,2,1536,512]{3,2,1,0:T(8,128)(2,1)S(1)} custom-call(s32[3]{0:T(128)S(1)} %pad_add_fusion.info, bf16[8,1536,1024]{2,1,0:T(8,128)(2,1)} %refs_7_.9, bf16[8,1536,1024]{2,1,0:T(8,128)(2,1)} %refs_8_.7), custom_call_target="tpu_custom_call" | custom-call | flops 1 | bytes 1 | tf_op jit(solution)/shard_map/stage/pallas_call | solution.py:113
  20.7 0.8 route.1
  21.4 4.5 %send_half.4 = (bf16[2,256,512]{2,1,0:T(8,128)(2,1)S(1)}, bf16[256,1536]{1,0:T(8,128)(2,1)S(1)}, bf16[2,2,1536,512]{3,2,1,0:T(8,128)(2,1)S(1)}) custom-call(s32[3]{0:T(128)S(1)} %pad_add_fusion.info, bf16[64,1536]{1,0:T(8,128)(2,1)S(1)} %copy-done, bf16[64,1536]{1,0:T(8,128)(2,1)S(1)} %collective-permute-done.refs_1_, ...), custom_call_target="tpu_custom_call" | custom-call | flops 1 | bytes 1 | tf_op jit(solution)/shard_map/send_half/pallas_call | solution.py:113
  26.0 4.2 %keep_half.4 = (bf16[2,256,512]{2,1,0:T(8,128)(2,1)S(1)}, bf16[2,2,1536,512]{3,2,1,0:T(8,128)(2,1)S(1)}) custom-call(s32[3]{0:T(128)S(1)} %pad_add_fusion.info, bf16[256,1536]{1,0:T(8,128)(2,1)S(1)} %get-tuple-element.43.refs_0_, bf16[2,2,1536,512]{3,2,1,0:T(8,128)(2,1)S(1)} %get-tuple-element.44.refs_1_, bf16[8,1536,1024]{2,1,0:T(8,128)(2,1)} %refs_7_.9, ...), custom_call_target="tpu_custom_call" | custom-call | flops 1 | bytes 1 | tf_op jit(solution)/shard_map/keep_half/pallas_call | solution.py:113
  30.4 1.6 %collective-permute-start.9 = (bf16[1,256,512]{2,1,0:T(8,128)(2,1)S(1)}, bf16[1,256,512]{2,1,0:T(8,128)(2,1)S(1)}, u32[]{:S(2)}, u32[]{:S(2)}) collective-permute-start(bf16[1,256,512]{2,1,0:T(8,128)(2,1)S(1)} %slice.181.refs_9_), channel_id=1, source_target_pairs={{0,2},{1,3},{2,0},{3,1},{4,6},{5,7},{6,4},{7,5},{8,10},{9,11},{10,... | collective-permute-start | bytes 786440 | tf_op jit(solution)/shard_map/ppermute | solution.py:23
  32.0 4.6 %send_half.5 = (bf16[2,256,512]{2,1,0:T(8,128)(2,1)S(1)}, bf16[256,1536]{1,0:T(8,128)(2,1)S(1)}, bf16[2,2,1536,512]{3,2,1,0:T(8,128)(2,1)S(1)}) custom-call(s32[3]{0:T(128)S(1)} %pad_add_fusion.info, bf16[64,1536]{1,0:T(8,128)(2,1)S(1)} %copy-done, bf16[64,1536]{1,0:T(8,128)(2,1)S(1)} %collective-permute-done.refs_1_, ...), custom_call_target="tpu_custom_call" | custom-call | flops 1 | bytes 1 | tf_op jit(solution)/shard_map/send_half/pallas_call | solution.py:113
  36.9 4.2 %keep_half.5 = (bf16[2,256,512]{2,1,0:T(8,128)(2,1)S(1)}, bf16[2,2,1536,512]{3,2,1,0:T(8,128)(2,1)S(1)}) custom-call(s32[3]{0:T(128)S(1)} %pad_add_fusion.info, bf16[256,1536]{1,0:T(8,128)(2,1)S(1)} %get-tuple-element.48.refs_0_, bf16[2,2,1536,512]{3,2,1,0:T(8,128)(2,1)S(1)} %get-tuple-element.49.refs_1_, bf16[8,1536,1024]{2,1,0:T(8,128)(2,1)} %refs_7_.9, ...), custom_call_target="tpu_custom_call" | custom-call | flops 1 | bytes 1 | tf_op jit(solution)/shard_map/keep_half/pallas_call | solution.py:113
  42.1 4.5 %send_half.6 = (bf16[2,256,512]{2,1,0:T(8,128)(2,1)S(1)}, bf16[256,1536]{1,0:T(8,128)(2,1)S(1)}, bf16[2,2,1536,512]{3,2,1,0:T(8,128)(2,1)S(1)}) custom-call(s32[3]{0:T(128)S(1)} %pad_add_fusion.info, bf16[64,1536]{1,0:T(8,128)(2,1)S(1)} %copy-done, bf16[64,1536]{1,0:T(8,128)(2,1)S(1)} %collective-permute-done.refs_1_, ...), custom_call_target="tpu_custom_call" | custom-call | flops 1 | bytes 1 | tf_op jit(solution)/shard_map/send_half/pallas_call | solution.py:113
  46.7 4.2 %keep_half.6 = (bf16[2,256,512]{2,1,0:T(8,128)(2,1)S(1)}, bf16[2,2,1536,512]{3,2,1,0:T(8,128)(2,1)S(1)}) custom-call(s32[3]{0:T(128)S(1)} %pad_add_fusion.info, bf16[256,1536]{1,0:T(8,128)(2,1)S(1)} %get-tuple-element.53.refs_0_, bf16[2,2,1536,512]{3,2,1,0:T(8,128)(2,1)S(1)} %get-tuple-element.54.refs_1_, bf16[8,1536,1024]{2,1,0:T(8,128)(2,1)} %refs_7_.9, ...), custom_call_target="tpu_custom_call" | custom-call | flops 1 | bytes 1 | tf_op jit(solution)/shard_map/keep_half/pallas_call | solution.py:113
  50.9 2.0 %collective-permute-done.11.refs_1_ = bf16[1,256,768]{2,1,0:T(8,128)(2,1)S(1)} collective-permute-done((bf16[1,256,768]{2,1,0:T(8,128)(2,1)S(1)}, bf16[1,256,768]{2,1,0:T(8,128)(2,1)S(1)}, u32[]{:S(2)}, u32[]{:S(2)}) %collective-permute-start.11) | collective-permute-done | bytes 393248 | tf_op jit(solution)/shard_map/ppermute | solution.py:23
  53.9 4.6 %send_half.7 = (bf16[2,256,512]{2,1,0:T(8,128)(2,1)S(1)}, bf16[256,1536]{1,0:T(8,128)(2,1)S(1)}, bf16[2,2,1536,512]{3,2,1,0:T(8,128)(2,1)S(1)}) custom-call(s32[3]{0:T(128)S(1)} %pad_add_fusion.info, bf16[64,1536]{1,0:T(8,128)(2,1)S(1)} %copy-done, bf16[64,1536]{1,0:T(8,128)(2,1)S(1)} %collective-permute-done.refs_1_, ...), custom_call_target="tpu_custom_call" | custom-call | flops 1 | bytes 1 | tf_op jit(solution)/shard_map/send_half/pallas_call | solution.py:113
  58.7 3.6 %keep_half.7 = (bf16[2,256,512]{2,1,0:T(8,128)(2,1)S(1)}, bf16[2,1024,1536]{2,1,0:T(8,128)(2,1)S(1)}) custom-call(s32[3]{0:T(128)S(1)} %pad_add_fusion.info, bf16[256,1536]{1,0:T(8,128)(2,1)S(1)} %get-tuple-element.58.refs_0_, bf16[2,2,1536,512]{3,2,1,0:T(8,128)(2,1)S(1)} %get-tuple-element.59.refs_1_, bf16[8,1024,1536]{2,1,0:T(8,128)(2,1)} %refs_7_.11), custom_call_target="tpu_custom_call" | custom-call | flops 1 | bytes 1 | tf_op jit(solution)/shard_map/keep_half/pallas_call | solution.py:113
  62.3 1.6 %collective-permute-done.13.refs_1_ = bf16[1,256,768]{2,1,0:T(8,128)(2,1)S(1)} collective-permute-done((bf16[1,256,768]{2,1,0:T(8,128)(2,1)S(1)}, bf16[1,256,768]{2,1,0:T(8,128)(2,1)S(1)}, u32[]{:S(2)}, u32[]{:S(2)}) %collective-permute-start.13) | collective-permute-done | bytes 393248 | tf_op jit(solution)/shard_map/ppermute | solution.py:23
  65.6 0.9 collective-permute-done.16.refs_2_
  66.5 3.4 %down.4 = (f32[256,1536]{1,0:T(8,128)S(1)}, bf16[2,1024,1536]{2,1,0:T(8,128)(2,1)S(1)}) custom-call(s32[3]{0:T(128)S(1)} %pad_add_fusion.info, bf16[1,256,256]{2,1,0:T(8,128)(2,1)S(1)} %fusion.3.refs_0_, bf16[1,256,768]{2,1,0:T(8,128)(2,1)S(1)} %copy-done.2, bf16[2,256,256]{2,1,0:T(8,128)(2,1)S(1)} %collective-permute-done.16.refs_2_, ...), custom_call_target="tpu_custom_call" | custom-call | flops 1 | bytes 1 | tf_op jit(solution)/shard_map/down/pallas_call | solution.py:113
  70.0 3.5 %down.5 = (f32[256,1536]{1,0:T(8,128)S(1)}, bf16[2,1024,1536]{2,1,0:T(8,128)(2,1)S(1)}) custom-call(s32[3]{0:T(128)S(1)} %pad_add_fusion.info, bf16[1,256,256]{2,1,0:T(8,128)(2,1)S(1)} %fusion.2.refs_0_, bf16[1,256,768]{2,1,0:T(8,128)(2,1)S(1)} %collective-permute-done.13.refs_1_, bf16[2,256,256]{2,1,0:T(8,128)(2,1)S(1)} %collective-permute-done.15.refs_2_, ...), custom_call_target="tpu_custom_call" | custom-call | flops 1 | bytes 1 | tf_op jit(solution)/shard_map/down/pallas_call | solution.py:113
  73.5 0.9 collective-permute-done.14.refs_1_
  74.6 1.6 %collective-permute-start.17 = (bf16[1,256,256]{2,1,0:T(8,128)(2,1)S(1)}, bf16[1,256,256]{2,1,0:T(8,128)(2,1)S(1)}, u32[]{:S(2)}, u32[]{:S(2)}) collective-permute-start(bf16[1,256,256]{2,1,0:T(8,128)(2,1)S(1)} %fusion.refs_8_.refs_0_), channel_id=1, source_target_pairs={{0,2},{1,3},{2,0},{3,1},{4,6},{5,7},{6,4},{7,5},{8,10},{9,11},{10,... | collective-permute-start | bytes 393224 | tf_op jit(solution)/shard_map/ppermute | solution.py:23
  76.2 3.5 %down.6 = (f32[256,1536]{1,0:T(8,128)S(1)}, bf16[2,1024,1536]{2,1,0:T(8,128)(2,1)S(1)}) custom-call(s32[3]{0:T(128)S(1)} %pad_add_fusion.info, bf16[1,256,256]{2,1,0:T(8,128)(2,1)S(1)} %fusion.1.refs_0_, bf16[1,256,768]{2,1,0:T(8,128)(2,1)S(1)} %collective-permute-done.14.refs_1_, bf16[2,256,256]{2,1,0:T(8,128)(2,1)S(1)} %collective-permute-done.18.refs_2_, ...), custom_call_target="tpu_custom_call" | custom-call | flops 1 | bytes 1 | tf_op jit(solution)/shard_map/down/pallas_call | solution.py:113
  79.7 0.9 collective-permute-done.17.refs_1_
  80.7 1.5 %collective-permute-done.19.refs_2_ = bf16[2,256,256]{2,1,0:T(8,128)(2,1)S(1)} collective-permute-done((bf16[2,256,256]{2,1,0:T(8,128)(2,1)S(1)}, bf16[2,256,256]{2,1,0:T(8,128)(2,1)S(1)}, u32[]{:S(2)}, u32[]{:S(2)}) %collective-permute-start.19) | collective-permute-done | bytes 262176 | tf_op jit(solution)/shard_map/ppermute | solution.py:23
  82.2 2.3 %down.7 = (bf16[64,1536]{1,0:T(8,128)(2,1)S(1)}, bf16[32,1536]{1,0:T(8,128)(2,1)S(1)}, bf16[32,1536]{1,0:T(8,128)(2,1)S(1)}, bf16[32,1536]{1,0:T(8,128)(2,1)S(1)...) custom-call(s32[3]{0:T(128)S(1)} %pad_add_fusion.info, ...), custom_call_target="tpu_custom_call" | custom-call | flops 1 | bytes 1 | tf_op jit(solution)/shard_map/down/pallas_call | solution.py:113
  84.6 3.8 %collective-permute-start.20 = (bf16[32,1536]{1,0:T(8,128)(2,1)S(1)}, bf16[32,1536]{1,0:T(8,128)(2,1)S(1)}, u32[]{:S(2)}, u32[]{:S(2)}) collective-permute-start(bf16[32,1536]{1,0:T(8,128)(2,1)S(1)} %get-tuple-element.74), channel_id=1, source_target_pairs={{0,12},{4,0},{8,4},{12,8},{1,13},{5,1},{9,5},{13,9},{2,14},{6,2},{... | collective-permute-start | bytes 294920 | tf_op jit(solution)/shard_map/ppermute | solution.py:386
  88.4 3.8 %collective-permute-start.23 = (bf16[32,1536]{1,0:T(8,128)(2,1)S(1)}, bf16[32,1536]{1,0:T(8,128)(2,1)S(1)}, u32[]{:S(2)}, u32[]{:S(2)}) collective-permute-start(bf16[32,1536]{1,0:T(8,128)(2,1)S(1)} %get-tuple-element.76), channel_id=1, source_target_pairs={{0,12},{4,0},{8,4},{12,8},{1,13},{5,1},{9,5},{13,9},{2,14},{6,2},{... | collective-permute-start | bytes 294920 | tf_op jit(solution)/shard_map/ppermute | solution.py:386
  92.3 3.9 %collective-permute-start.21 = (bf16[32,1536]{1,0:T(8,128)(2,1)S(1)}, bf16[32,1536]{1,0:T(8,128)(2,1)S(1)}, u32[]{:S(2)}, u32[]{:S(2)}) collective-permute-start(bf16[32,1536]{1,0:T(8,128)(2,1)S(1)} %add_convert_fusion.1), channel_id=1, source_target_pairs={{0,12},{4,0},{8,4},{12,8},{1,13},{5,1},{9,5},{13,9},{2,14},{6,2},{... | collective-permute-start | bytes 294920 | tf_op jit(solution)/shard_map/ppermute | solution.py:386
  96.3 4.2 %collective-permute-done.25 = bf16[32,1536]{1,0:T(8,128)(2,1)S(1)} collective-permute-done((bf16[32,1536]{1,0:T(8,128)(2,1)S(1)}, bf16[32,1536]{1,0:T(8,128)(2,1)S(1)}, u32[]{:S(2)}, u32[]{:S(2)}) %collective-permute-start.25) | collective-permute-done | bytes 98336 | tf_op jit(solution)/shard_map/ppermute | solution.py:386
  (78 shorter events, 7.2 us)
Async XLA Ops:
  0.0 11.0 %collective-permute-start = (bf16[64,1536]{1,0:T(8,128)(2,1)}, bf16[64,1536]{1,0:T(8,128)(2,1)S(1)}, u32[]{:S(2)}, u32[]{:S(2)}) collective-permute-start(bf16[64,1536]{1,0:T(8,128)(2,1)} %refs_0_.9), channel_id=1, source_target_pairs={{0,4},{4,8},{8,12},{12,0},{1,5},{5,9},{9,13},{13,1},{2,6},{6,10},{... | collective-permute-start | bytes 589832 | tf_op jit(solution)/shard_map/ppermute | solution.py:367
  3.0 11.0 %collective-permute-start.1 = (bf16[64,1536]{1,0:T(8,128)(2,1)}, bf16[64,1536]{1,0:T(8,128)(2,1)S(1)}, u32[]{:S(2)}, u32[]{:S(2)}) collective-permute-start(bf16[64,1536]{1,0:T(8,128)(2,1)} %refs_0_.9), channel_id=1, source_target_pairs={{0,12},{4,0},{8,4},{12,8},{1,13},{5,1},{9,5},{13,9},{2,14},{6,2},{... | collective-permute-start | bytes 589832 | tf_op jit(solution)/shard_map/ppermute | solution.py:367
  6.4 14.2 %collective-permute-start.4 = (f32[16,64]{1,0:T(8,128)S(1)}, f32[16,64]{1,0:T(8,128)S(1)}, u32[]{:S(2)}, u32[]{:S(2)}) collective-permute-start(f32[16,64]{1,0:T(8,128)S(1)} %pad_maximum_fusion.8.refs_0_), channel_id=1, source_target_pairs={{0,4},{4,8},{8,12},{12,0},{1,5},{5,9},{9,13},{13,1},{2,6},{6,10},{... | collective-permute-start | bytes 12296 | tf_op jit(solution)/shard_map/ppermute | solution.py:302
  6.4 14.2 %collective-permute-start.5 = (f32[16,64]{1,0:T(8,128)S(1)}, f32[16,64]{1,0:T(8,128)S(1)}, u32[]{:S(2)}, u32[]{:S(2)}) collective-permute-start(f32[16,64]{1,0:T(8,128)S(1)} %pad_maximum_fusion.8.refs_0_), channel_id=1, source_target_pairs={{0,12},{4,0},{8,4},{12,8},{1,13},{5,1},{9,5},{13,9},{2,14},{6,2},{... | collective-permute-start | bytes 12296 | tf_op jit(solution)/shard_map/ppermute | solution.py:302
  10.3 10.4 %collective-permute-start.6 = (f32[16,64]{1,0:T(8,128)S(1)}, f32[16,64]{1,0:T(8,128)S(1)}, u32[]{:S(2)}, u32[]{:S(2)}) collective-permute-start(f32[16,64]{1,0:T(8,128)S(1)} %pad_maximum_fusion.8.refs_0_), channel_id=1, source_target_pairs={{0,8},{4,12},{8,0},{12,4},{1,9},{5,13},{9,1},{13,5},{2,10},{6,14},... | collective-permute-start | bytes 12296 | tf_op jit(solution)/shard_map/ppermute | solution.py:302
  11.0 10.4 %collective-permute-start.2 = (bf16[32,1536]{1,0:T(8,128)(2,1)S(1)}, bf16[32,1536]{1,0:T(8,128)(2,1)S(1)}, u32[]{:S(2)}, u32[]{:S(2)}) collective-permute-start(bf16[32,1536]{1,0:T(8,128)(2,1)S(1)} %slice.116), channel_id=1, source_target_pairs={{0,4},{4,8},{8,12},{12,0},{1,5},{5,9},{9,13},{13,1},{2,6},{6,10},{... | collective-permute-start | bytes 294920 | tf_op jit(solution)/shard_map/ppermute | solution.py:371
  14.0 7.4 %collective-permute-start.3 = (bf16[32,1536]{1,0:T(8,128)(2,1)S(1)}, bf16[32,1536]{1,0:T(8,128)(2,1)S(1)}, u32[]{:S(2)}, u32[]{:S(2)}) collective-permute-start(bf16[32,1536]{1,0:T(8,128)(2,1)S(1)} %slice.117), channel_id=1, source_target_pairs={{0,12},{4,0},{8,4},{12,8},{1,13},{5,1},{9,5},{13,9},{2,14},{6,2},{... | collective-permute-start | bytes 294920 | tf_op jit(solution)/shard_map/ppermute | solution.py:371
  17.2 4.2 %copy-start = (bf16[64,1536]{1,0:T(8,128)(2,1)S(1)}, bf16[64,1536]{1,0:T(8,128)(2,1)}, u32[]{:S(2)}) copy-start(bf16[64,1536]{1,0:T(8,128)(2,1)} %refs_0_.9) | copy-start | bytes 589828
  25.9 4.3 %collective-permute-start.7 = (bf16[2,256,512]{2,1,0:T(8,128)(2,1)S(1)}, bf16[2,256,512]{2,1,0:T(8,128)(2,1)S(1)}, u32[]{:S(2)}, u32[]{:S(2)}) collective-permute-start(bf16[2,256,512]{2,1,0:T(8,128)(2,1)S(1)} %get-tuple-element.47), channel_id=1, source_target_pairs={{0,1},{1,0},{2,3},{3,2},{4,5},{5,4},{6,7},{7,6},{8,9},{9,8},{10,11... | collective-permute-start | bytes 1572872 | tf_op jit(solution)/shard_map/ppermute | solution.py:23
  30.4 10.7 %collective-permute-start.9 = (bf16[1,256,512]{2,1,0:T(8,128)(2,1)S(1)}, bf16[1,256,512]{2,1,0:T(8,128)(2,1)S(1)}, u32[]{:S(2)}, u32[]{:S(2)}) collective-permute-start(bf16[1,256,512]{2,1,0:T(8,128)(2,1)S(1)} %slice.181.refs_9_), channel_id=1, source_target_pairs={{0,2},{1,3},{2,0},{3,1},{4,6},{5,7},{6,4},{7,5},{8,10},{9,11},{10,... | collective-permute-start | bytes 786440 | tf_op jit(solution)/shard_map/ppermute | solution.py:23
  36.6 4.7 %collective-permute-start.8 = (bf16[2,256,512]{2,1,0:T(8,128)(2,1)S(1)}, bf16[2,256,512]{2,1,0:T(8,128)(2,1)S(1)}, u32[]{:S(2)}, u32[]{:S(2)}) collective-permute-start(bf16[2,256,512]{2,1,0:T(8,128)(2,1)S(1)} %get-tuple-element.52), channel_id=1, source_target_pairs={{0,1},{1,0},{2,3},{3,2},{4,5},{5,4},{6,7},{7,6},{8,9},{9,8},{10,11... | collective-permute-start | bytes 1572872 | tf_op jit(solution)/shard_map/ppermute | solution.py:23
  41.5 11.4 %collective-permute-start.11 = (bf16[1,256,768]{2,1,0:T(8,128)(2,1)S(1)}, bf16[1,256,768]{2,1,0:T(8,128)(2,1)S(1)}, u32[]{:S(2)}, u32[]{:S(2)}) collective-permute-start(bf16[1,256,768]{2,1,0:T(8,128)(2,1)S(1)} %pad_maximum_fusion.refs_9_), channel_id=1, source_target_pairs={{0,2},{1,3},{2,0},{3,1},{4,6},{5,7},{6,4},{7,5},{8,10},{9,11},{10,... | collective-permute-start | bytes 1179656 | tf_op jit(solution)/shard_map/ppermute | solution.py:23
  46.6 6.5 %collective-permute-start.10 = (bf16[2,256,512]{2,1,0:T(8,128)(2,1)S(1)}, bf16[2,256,512]{2,1,0:T(8,128)(2,1)S(1)}, u32[]{:S(2)}, u32[]{:S(2)}) collective-permute-start(bf16[2,256,512]{2,1,0:T(8,128)(2,1)S(1)} %get-tuple-element.57), channel_id=1, source_target_pairs={{0,1},{1,0},{2,3},{3,2},{4,5},{5,4},{6,7},{7,6},{8,9},{9,8},{10,11... | collective-permute-start | bytes 1572872 | tf_op jit(solution)/shard_map/ppermute | solution.py:23
  52.9 5.7 %copy-start.1 = (bf16[1,256,768]{2,1,0:T(8,128)(2,1)}, bf16[1,256,768]{2,1,0:T(8,128)(2,1)S(1)}, u32[]{:S(2)}) copy-start(bf16[1,256,768]{2,1,0:T(8,128)(2,1)S(1)} %collective-permute-done.11.refs_1_) | copy-start | bytes 1179652
  53.3 10.6 %collective-permute-start.13 = (bf16[1,256,768]{2,1,0:T(8,128)(2,1)S(1)}, bf16[1,256,768]{2,1,0:T(8,128)(2,1)S(1)}, u32[]{:S(2)}, u32[]{:S(2)}) collective-permute-start(bf16[1,256,768]{2,1,0:T(8,128)(2,1)S(1)} %pad_maximum_fusion.1.refs_9_), channel_id=1, source_target_pairs={{0,2},{1,3},{2,0},{3,1},{4,6},{5,7},{6,4},{7,5},{8,10},{9,11},{10,... | collective-permute-start | bytes 1179656 | tf_op jit(solution)/shard_map/ppermute | solution.py:23
  58.6 5.5 %collective-permute-start.12 = (bf16[2,256,512]{2,1,0:T(8,128)(2,1)S(1)}, bf16[2,256,512]{2,1,0:T(8,128)(2,1)S(1)}, u32[]{:S(2)}, u32[]{:S(2)}) collective-permute-start(bf16[2,256,512]{2,1,0:T(8,128)(2,1)S(1)} %get-tuple-element.61), channel_id=1, source_target_pairs={{0,1},{1,0},{2,3},{3,2},{4,5},{5,4},{6,7},{7,6},{8,9},{9,8},{10,11... | collective-permute-start | bytes 1572872 | tf_op jit(solution)/shard_map/ppermute | solution.py:23
  58.7 6.2 %slice-start = ((bf16[1,256,768]{2,1,0:T(8,128)(2,1)}), bf16[1,256,256]{2,1,0:T(8,128)(2,1)S(1)}, s32[]{:S(2)}) async-start(bf16[1,256,768]{2,1,0:T(8,128)(2,1)} %copy-done.1), calls=%async_computation | async-start | bytes 262144 | tf_op jit(solution)/shard_map/slice | solution.py:267
  62.3 4.2 %copy-start.2 = (bf16[1,256,768]{2,1,0:T(8,128)(2,1)S(1)}, bf16[1,256,768]{2,1,0:T(8,128)(2,1)}, u32[]{:S(2)}) copy-start(bf16[1,256,768]{2,1,0:T(8,128)(2,1)} %copy-done.1) | copy-start | bytes 1179652
  64.3 10.0 %collective-permute-start.14 = (bf16[1,256,768]{2,1,0:T(8,128)(2,1)S(1)}, bf16[1,256,768]{2,1,0:T(8,128)(2,1)S(1)}, u32[]{:S(2)}, u32[]{:S(2)}) collective-permute-start(bf16[1,256,768]{2,1,0:T(8,128)(2,1)S(1)} %pad_maximum_fusion.2.refs_7_), channel_id=1, source_target_pairs={{0,2},{1,3},{2,0},{3,1},{4,6},{5,7},{6,4},{7,5},{8,10},{9,11},{10,... | collective-permute-start | bytes 1179656 | tf_op jit(solution)/shard_map/ppermute | solution.py:23
  64.9 1.6 %collective-permute-start.16 = (bf16[2,256,256]{2,1,0:T(8,128)(2,1)S(1)}, bf16[2,256,256]{2,1,0:T(8,128)(2,1)S(1)}, u32[]{:S(2)}, u32[]{:S(2)}) collective-permute-start(bf16[2,256,256]{2,1,0:T(8,128)(2,1)S(1)} %pad_maximum_fusion.4), channel_id=1, source_target_pairs={{0,1},{1,0},{2,3},{3,2},{4,5},{5,4},{6,7},{7,6},{8,9},{9,8},{10,11... | collective-permute-start | bytes 786440 | tf_op jit(solution)/shard_map/ppermute | solution.py:23
  65.1 4.9 %collective-permute-start.15 = (bf16[2,256,256]{2,1,0:T(8,128)(2,1)S(1)}, bf16[2,256,256]{2,1,0:T(8,128)(2,1)S(1)}, u32[]{:S(2)}, u32[]{:S(2)}) collective-permute-start(bf16[2,256,256]{2,1,0:T(8,128)(2,1)S(1)} %pad_maximum_fusion.3), channel_id=1, source_target_pairs={{0,1},{1,0},{2,3},{3,2},{4,5},{5,4},{6,7},{7,6},{8,9},{9,8},{10,11... | collective-permute-start | bytes 786440 | tf_op jit(solution)/shard_map/ppermute | solution.py:23
  74.4 1.8 %collective-permute-start.18 = (bf16[2,256,256]{2,1,0:T(8,128)(2,1)S(1)}, bf16[2,256,256]{2,1,0:T(8,128)(2,1)S(1)}, u32[]{:S(2)}, u32[]{:S(2)}) collective-permute-start(bf16[2,256,256]{2,1,0:T(8,128)(2,1)S(1)} %pad_maximum_fusion.5), channel_id=1, source_target_pairs={{0,1},{1,0},{2,3},{3,2},{4,5},{5,4},{6,7},{7,6},{8,9},{9,8},{10,11... | collective-permute-start | bytes 786440 | tf_op jit(solution)/shard_map/ppermute | solution.py:23
  74.6 6.0 %collective-permute-start.17 = (bf16[1,256,256]{2,1,0:T(8,128)(2,1)S(1)}, bf16[1,256,256]{2,1,0:T(8,128)(2,1)S(1)}, u32[]{:S(2)}, u32[]{:S(2)}) collective-permute-start(bf16[1,256,256]{2,1,0:T(8,128)(2,1)S(1)} %fusion.refs_8_.refs_0_), channel_id=1, source_target_pairs={{0,2},{1,3},{2,0},{3,1},{4,6},{5,7},{6,4},{7,5},{8,10},{9,11},{10,... | collective-permute-start | bytes 393224 | tf_op jit(solution)/shard_map/ppermute | solution.py:23
  80.6 1.6 %collective-permute-start.19 = (bf16[2,256,256]{2,1,0:T(8,128)(2,1)S(1)}, bf16[2,256,256]{2,1,0:T(8,128)(2,1)S(1)}, u32[]{:S(2)}, u32[]{:S(2)}) collective-permute-start(bf16[2,256,256]{2,1,0:T(8,128)(2,1)S(1)} %pad_maximum_fusion.6), channel_id=1, source_target_pairs={{0,1},{1,0},{2,3},{3,2},{4,5},{5,4},{6,7},{7,6},{8,9},{9,8},{10,11... | collective-permute-start | bytes 786440 | tf_op jit(solution)/shard_map/ppermute | solution.py:23
  84.5 7.7 %collective-permute-start.24 = (bf16[32,1536]{1,0:T(8,128)(2,1)S(1)}, bf16[32,1536]{1,0:T(8,128)(2,1)S(1)}, u32[]{:S(2)}, u32[]{:S(2)}) collective-permute-start(bf16[32,1536]{1,0:T(8,128)(2,1)S(1)} %get-tuple-element.78), channel_id=1, source_target_pairs={{0,4},{4,8},{8,12},{12,0},{1,5},{5,9},{9,13},{13,1},{2,6},{6,10},{... | collective-permute-start | bytes 294920 | tf_op jit(solution)/shard_map/ppermute | solution.py:386
  84.6 7.7 %collective-permute-start.20 = (bf16[32,1536]{1,0:T(8,128)(2,1)S(1)}, bf16[32,1536]{1,0:T(8,128)(2,1)S(1)}, u32[]{:S(2)}, u32[]{:S(2)}) collective-permute-start(bf16[32,1536]{1,0:T(8,128)(2,1)S(1)} %get-tuple-element.74), channel_id=1, source_target_pairs={{0,12},{4,0},{8,4},{12,8},{1,13},{5,1},{9,5},{13,9},{2,14},{6,2},{... | collective-permute-start | bytes 294920 | tf_op jit(solution)/shard_map/ppermute | solution.py:386
  88.4 7.9 %collective-permute-start.22 = (bf16[32,1536]{1,0:T(8,128)(2,1)S(1)}, bf16[32,1536]{1,0:T(8,128)(2,1)S(1)}, u32[]{:S(2)}, u32[]{:S(2)}) collective-permute-start(bf16[32,1536]{1,0:T(8,128)(2,1)S(1)} %get-tuple-element.75), channel_id=1, source_target_pairs={{0,4},{4,8},{8,12},{12,0},{1,5},{5,9},{9,13},{13,1},{2,6},{6,10},{... | collective-permute-start | bytes 294920 | tf_op jit(solution)/shard_map/ppermute | solution.py:386
  88.4 7.9 %collective-permute-start.23 = (bf16[32,1536]{1,0:T(8,128)(2,1)S(1)}, bf16[32,1536]{1,0:T(8,128)(2,1)S(1)}, u32[]{:S(2)}, u32[]{:S(2)}) collective-permute-start(bf16[32,1536]{1,0:T(8,128)(2,1)S(1)} %get-tuple-element.76), channel_id=1, source_target_pairs={{0,12},{4,0},{8,4},{12,8},{1,13},{5,1},{9,5},{13,9},{2,14},{6,2},{... | collective-permute-start | bytes 294920 | tf_op jit(solution)/shard_map/ppermute | solution.py:386
  92.2 8.2 %collective-permute-start.25 = (bf16[32,1536]{1,0:T(8,128)(2,1)S(1)}, bf16[32,1536]{1,0:T(8,128)(2,1)S(1)}, u32[]{:S(2)}, u32[]{:S(2)}) collective-permute-start(bf16[32,1536]{1,0:T(8,128)(2,1)S(1)} %add_convert_fusion), channel_id=1, source_target_pairs={{0,4},{4,8},{8,12},{12,0},{1,5},{5,9},{9,13},{13,1},{2,6},{6,10},{... | collective-permute-start | bytes 294920 | tf_op jit(solution)/shard_map/ppermute | solution.py:386
  92.3 8.1 %collective-permute-start.21 = (bf16[32,1536]{1,0:T(8,128)(2,1)S(1)}, bf16[32,1536]{1,0:T(8,128)(2,1)S(1)}, u32[]{:S(2)}, u32[]{:S(2)}) collective-permute-start(bf16[32,1536]{1,0:T(8,128)(2,1)S(1)} %add_convert_fusion.1), channel_id=1, source_target_pairs={{0,12},{4,0},{8,4},{12,8},{1,13},{5,1},{9,5},{13,9},{2,14},{6,2},{... | collective-permute-start | bytes 294920 | tf_op jit(solution)/shard_map/ppermute | solution.py:386

commit v14 on v13

--- a/solution.py
+++ b/solution.py
@@ -83,10 +83,14 @@
         return [pltpu.make_async_copy(weights[0].at[e], to.at[x], sem.at[x]) for x, e in enumerate(experts)]
     half = to.shape[-1]
     units = pl.ds(pl.multiple_of(((info[1] & 1) ^ side) * half, half), half)
+    depth = to.shape[2]
+    piece = depth // 3 if depth % 48 == 0 else depth
+    places = [
+        (m, x, pl.ds(at, piece)) for m in range(2) for x in range(len(experts)) for at in range(0, depth, piece)
+    ]
     return [
-        pltpu.make_async_copy(w.at[e, :, units], to.at[m, x], sem.at[m * len(experts) + x])
-        for m, w in enumerate(weights)
-        for x, e in enumerate(experts)
+        pltpu.make_async_copy(weights[m].at[experts[x], deep, units], to.at[m, x, deep], sem.at[i])
+        for i, (m, x, deep) in enumerate(places)
     ]
 
 
@@ -96,7 +100,7 @@
     weights = [] if ahead is None else weights[2:] if ahead[1] is None else weights[:2]
     if ahead is not None:
         outs.append(jax.ShapeDtypeStruct(set_shape(ahead, weights), jnp.bfloat16))
-        scratch = scratch + [pltpu.SemaphoreType.DMA((2 * len(ahead[0]),))]
+        scratch = scratch + [pltpu.SemaphoreType.DMA((6 * len(ahead[0]),))]
 
     def whole(info, *refs):
         own, far = refs[:n_in], refs[n_in : n_in + len(weights)]

time: 101 us -> 102 us (level)
  no operation moved by 1% of the time
where the time goes in v14:
time: 102 us
  Pallas kernels  51.8 us (51%)
  starting transfers between devices  29.9 us (29%)
  waiting for transfers between devices  15.4 us (15%)
  other arithmetic  3.68 us (4%)
    pallas_call x13, Pallas kernels, call(): pl.pallas_call(whole, out_shape=tuple(outs), in_specs=[SMEM] + [spec for...  51.1 us
    ppermute x6, starting transfers between devices, hop(): return lax.ppermute(total, axis, perm)  11.6 us
    ppermute x13, waiting for transfers between devices, flip(): lax.ppermute(x, axis, [(i, i ^ k) for i in range(lax.axis_size(axis))])  7.48 us
    ppermute x13, starting transfers between devices, flip(): lax.ppermute(x, axis, [(i, i ^ k) for i in range(lax.axis_size(axis))])  6.24 us
    ppermute x6, waiting for transfers between devices, hop(): return lax.ppermute(total, axis, perm)  4.24 us
    ppermute x3, starting transfers between devices, on_device(): lax.ppermute(meta, 'expert', [(i, (i - k) % n_owner) for i in range(n_own...  3.83 us
    ppermute x1, starting transfers between devices, gathered(): lax.ppermute(above[half:], axis, down_)  3.15 us
    ppermute x1, starting transfers between devices, gathered(): lax.ppermute(below, axis, up)  3.02 us
  transfers between devices with their start and end apart: 26, of which 9 were waited for; matrix products, arithmetic and copies ran while one was open for 2% of the time, Pallas kernels for 44%

profile of v14, /device:TPU:0, one launch (start us, length us, event | category | flops | bytes accessed | tf_op | source)
XLA Modules:
  0.0 101.5 jit_solution(15377890177713295932)
XLA Ops:
  0.0 3.0 %collective-permute-start = (bf16[64,1536]{1,0:T(8,128)(2,1)}, bf16[64,1536]{1,0:T(8,128)(2,1)S(1)}, u32[]{:S(2)}, u32[]{:S(2)}) collective-permute-start(bf16[64,1536]{1,0:T(8,128)(2,1)} %refs_0_.9), channel_id=1, source_target_pairs={{0,4},{4,8},{8,12},{12,0},{1,5},{5,9},{9,13},{13,1},{2,6},{6,10},{... | collective-permute-start | bytes 589832 | tf_op jit(solution)/shard_map/ppermute | solution.py:371
  3.0 2.0 %collective-permute-start.1 = (bf16[64,1536]{1,0:T(8,128)(2,1)}, bf16[64,1536]{1,0:T(8,128)(2,1)S(1)}, u32[]{:S(2)}, u32[]{:S(2)}) collective-permute-start(bf16[64,1536]{1,0:T(8,128)(2,1)} %refs_0_.9), channel_id=1, source_target_pairs={{0,12},{4,0},{8,4},{12,8},{1,13},{5,1},{9,5},{13,9},{2,14},{6,2},{... | collective-permute-start | bytes 589832 | tf_op jit(solution)/shard_map/ppermute | solution.py:371
  6.4 3.8 %collective-permute-start.5 = (f32[16,64]{1,0:T(8,128)S(1)}, f32[16,64]{1,0:T(8,128)S(1)}, u32[]{:S(2)}, u32[]{:S(2)}) collective-permute-start(f32[16,64]{1,0:T(8,128)S(1)} %pad_maximum_fusion.8.refs_0_), channel_id=1, source_target_pairs={{0,12},{4,0},{8,4},{12,8},{1,13},{5,1},{9,5},{13,9},{2,14},{6,2},{... | collective-permute-start | bytes 12296 | tf_op jit(solution)/shard_map/ppermute | solution.py:306
  10.3 0.8 collective-permute-done.refs_1_
  11.1 2.9 %collective-permute-done.1.refs_2_ = bf16[64,1536]{1,0:T(8,128)(2,1)S(1)} collective-permute-done((bf16[64,1536]{1,0:T(8,128)(2,1)}, bf16[64,1536]{1,0:T(8,128)(2,1)S(1)}, u32[]{:S(2)}, u32[]{:S(2)}) %collective-permute-start.1) | collective-permute-done | bytes 196640 | tf_op jit(solution)/shard_map/ppermute | solution.py:371
  14.0 3.2 %collective-permute-start.3 = (bf16[32,1536]{1,0:T(8,128)(2,1)S(1)}, bf16[32,1536]{1,0:T(8,128)(2,1)S(1)}, u32[]{:S(2)}, u32[]{:S(2)}) collective-permute-start(bf16[32,1536]{1,0:T(8,128)(2,1)S(1)} %slice.117), channel_id=1, source_target_pairs={{0,12},{4,0},{8,4},{12,8},{1,13},{5,1},{9,5},{13,9},{2,14},{6,2},{... | collective-permute-start | bytes 294920 | tf_op jit(solution)/shard_map/ppermute | solution.py:375
  17.2 3.4 %stage.1.refs_6_ = bf16[2,2,1536,512]{3,2,1,0:T(8,128)(2,1)S(1)} custom-call(s32[3]{0:T(128)S(1)} %pad_add_fusion.info, bf16[8,1536,1024]{2,1,0:T(8,128)(2,1)} %refs_7_.9, bf16[8,1536,1024]{2,1,0:T(8,128)(2,1)} %refs_8_.7), custom_call_target="tpu_custom_call" | custom-call | flops 1 | bytes 1 | tf_op jit(solution)/shard_map/stage/pallas_call | solution.py:117
  20.7 0.8 route.1
  21.5 4.5 %send_half.4 = (bf16[2,256,512]{2,1,0:T(8,128)(2,1)S(1)}, bf16[256,1536]{1,0:T(8,128)(2,1)S(1)}, bf16[2,2,1536,512]{3,2,1,0:T(8,128)(2,1)S(1)}) custom-call(s32[3]{0:T(128)S(1)} %pad_add_fusion.info, bf16[64,1536]{1,0:T(8,128)(2,1)S(1)} %copy-done, bf16[64,1536]{1,0:T(8,128)(2,1)S(1)} %collective-permute-done.refs_1_, ...), custom_call_target="tpu_custom_call" | custom-call | flops 1 | bytes 1 | tf_op jit(solution)/shard_map/send_half/pallas_call | solution.py:117
  26.1 4.3 %keep_half.4 = (bf16[2,256,512]{2,1,0:T(8,128)(2,1)S(1)}, bf16[2,2,1536,512]{3,2,1,0:T(8,128)(2,1)S(1)}) custom-call(s32[3]{0:T(128)S(1)} %pad_add_fusion.info, bf16[256,1536]{1,0:T(8,128)(2,1)S(1)} %get-tuple-element.43.refs_0_, bf16[2,2,1536,512]{3,2,1,0:T(8,128)(2,1)S(1)} %get-tuple-element.44.refs_1_, bf16[8,1536,1024]{2,1,0:T(8,128)(2,1)} %refs_7_.9, ...), custom_call_target="tpu_custom_call" | custom-call | flops 1 | bytes 1 | tf_op jit(solution)/shard_map/keep_half/pallas_call | solution.py:117
  30.6 1.6 %collective-permute-start.9 = (bf16[1,256,512]{2,1,0:T(8,128)(2,1)S(1)}, bf16[1,256,512]{2,1,0:T(8,128)(2,1)S(1)}, u32[]{:S(2)}, u32[]{:S(2)}) collective-permute-start(bf16[1,256,512]{2,1,0:T(8,128)(2,1)S(1)} %slice.181.refs_9_), channel_id=1, source_target_pairs={{0,2},{1,3},{2,0},{3,1},{4,6},{5,7},{6,4},{7,5},{8,10},{9,11},{10,... | collective-permute-start | bytes 786440 | tf_op jit(solution)/shard_map/ppermute | solution.py:23
  32.1 4.7 %send_half.5 = (bf16[2,256,512]{2,1,0:T(8,128)(2,1)S(1)}, bf16[256,1536]{1,0:T(8,128)(2,1)S(1)}, bf16[2,2,1536,512]{3,2,1,0:T(8,128)(2,1)S(1)}) custom-call(s32[3]{0:T(128)S(1)} %pad_add_fusion.info, bf16[64,1536]{1,0:T(8,128)(2,1)S(1)} %copy-done, bf16[64,1536]{1,0:T(8,128)(2,1)S(1)} %collective-permute-done.refs_1_, ...), custom_call_target="tpu_custom_call" | custom-call | flops 1 | bytes 1 | tf_op jit(solution)/shard_map/send_half/pallas_call | solution.py:117
  37.1 4.3 %keep_half.5 = (bf16[2,256,512]{2,1,0:T(8,128)(2,1)S(1)}, bf16[2,2,1536,512]{3,2,1,0:T(8,128)(2,1)S(1)}) custom-call(s32[3]{0:T(128)S(1)} %pad_add_fusion.info, bf16[256,1536]{1,0:T(8,128)(2,1)S(1)} %get-tuple-element.48.refs_0_, bf16[2,2,1536,512]{3,2,1,0:T(8,128)(2,1)S(1)} %get-tuple-element.49.refs_1_, bf16[8,1536,1024]{2,1,0:T(8,128)(2,1)} %refs_7_.9, ...), custom_call_target="tpu_custom_call" | custom-call | flops 1 | bytes 1 | tf_op jit(solution)/shard_map/keep_half/pallas_call | solution.py:117
  42.4 4.5 %send_half.6 = (bf16[2,256,512]{2,1,0:T(8,128)(2,1)S(1)}, bf16[256,1536]{1,0:T(8,128)(2,1)S(1)}, bf16[2,2,1536,512]{3,2,1,0:T(8,128)(2,1)S(1)}) custom-call(s32[3]{0:T(128)S(1)} %pad_add_fusion.info, bf16[64,1536]{1,0:T(8,128)(2,1)S(1)} %copy-done, bf16[64,1536]{1,0:T(8,128)(2,1)S(1)} %collective-permute-done.refs_1_, ...), custom_call_target="tpu_custom_call" | custom-call | flops 1 | bytes 1 | tf_op jit(solution)/shard_map/send_half/pallas_call | solution.py:117
  46.9 4.2 %keep_half.6 = (bf16[2,256,512]{2,1,0:T(8,128)(2,1)S(1)}, bf16[2,2,1536,512]{3,2,1,0:T(8,128)(2,1)S(1)}) custom-call(s32[3]{0:T(128)S(1)} %pad_add_fusion.info, bf16[256,1536]{1,0:T(8,128)(2,1)S(1)} %get-tuple-element.53.refs_0_, bf16[2,2,1536,512]{3,2,1,0:T(8,128)(2,1)S(1)} %get-tuple-element.54.refs_1_, bf16[8,1536,1024]{2,1,0:T(8,128)(2,1)} %refs_7_.9, ...), custom_call_target="tpu_custom_call" | custom-call | flops 1 | bytes 1 | tf_op jit(solution)/shard_map/keep_half/pallas_call | solution.py:117
  51.2 1.9 %collective-permute-done.11.refs_1_ = bf16[1,256,768]{2,1,0:T(8,128)(2,1)S(1)} collective-permute-done((bf16[1,256,768]{2,1,0:T(8,128)(2,1)S(1)}, bf16[1,256,768]{2,1,0:T(8,128)(2,1)S(1)}, u32[]{:S(2)}, u32[]{:S(2)}) %collective-permute-start.11) | collective-permute-done | bytes 393248 | tf_op jit(solution)/shard_map/ppermute | solution.py:23
  54.1 4.7 %send_half.7 = (bf16[2,256,512]{2,1,0:T(8,128)(2,1)S(1)}, bf16[256,1536]{1,0:T(8,128)(2,1)S(1)}, bf16[2,2,1536,512]{3,2,1,0:T(8,128)(2,1)S(1)}) custom-call(s32[3]{0:T(128)S(1)} %pad_add_fusion.info, bf16[64,1536]{1,0:T(8,128)(2,1)S(1)} %copy-done, bf16[64,1536]{1,0:T(8,128)(2,1)S(1)} %collective-permute-done.refs_1_, ...), custom_call_target="tpu_custom_call" | custom-call | flops 1 | bytes 1 | tf_op jit(solution)/shard_map/send_half/pallas_call | solution.py:117
  58.9 3.7 %keep_half.7 = (bf16[2,256,512]{2,1,0:T(8,128)(2,1)S(1)}, bf16[2,1024,1536]{2,1,0:T(8,128)(2,1)S(1)}) custom-call(s32[3]{0:T(128)S(1)} %pad_add_fusion.info, bf16[256,1536]{1,0:T(8,128)(2,1)S(1)} %get-tuple-element.58.refs_0_, bf16[2,2,1536,512]{3,2,1,0:T(8,128)(2,1)S(1)} %get-tuple-element.59.refs_1_, bf16[8,1024,1536]{2,1,0:T(8,128)(2,1)} %refs_7_.11), custom_call_target="tpu_custom_call" | custom-call | flops 1 | bytes 1 | tf_op jit(solution)/shard_map/keep_half/pallas_call | solution.py:117
  62.6 1.4 %collective-permute-done.13.refs_1_ = bf16[1,256,768]{2,1,0:T(8,128)(2,1)S(1)} collective-permute-done((bf16[1,256,768]{2,1,0:T(8,128)(2,1)S(1)}, bf16[1,256,768]{2,1,0:T(8,128)(2,1)S(1)}, u32[]{:S(2)}, u32[]{:S(2)}) %collective-permute-start.13) | collective-permute-done | bytes 393248 | tf_op jit(solution)/shard_map/ppermute | solution.py:23
  65.9 0.9 collective-permute-done.16.refs_2_
  66.8 3.5 %down.4 = (f32[256,1536]{1,0:T(8,128)S(1)}, bf16[2,1024,1536]{2,1,0:T(8,128)(2,1)S(1)}) custom-call(s32[3]{0:T(128)S(1)} %pad_add_fusion.info, bf16[1,256,256]{2,1,0:T(8,128)(2,1)S(1)} %fusion.3.refs_0_, bf16[1,256,768]{2,1,0:T(8,128)(2,1)S(1)} %copy-done.2, bf16[2,256,256]{2,1,0:T(8,128)(2,1)S(1)} %collective-permute-done.16.refs_2_, ...), custom_call_target="tpu_custom_call" | custom-call | flops 1 | bytes 1 | tf_op jit(solution)/shard_map/down/pallas_call | solution.py:117
  70.3 3.5 %down.5 = (f32[256,1536]{1,0:T(8,128)S(1)}, bf16[2,1024,1536]{2,1,0:T(8,128)(2,1)S(1)}) custom-call(s32[3]{0:T(128)S(1)} %pad_add_fusion.info, bf16[1,256,256]{2,1,0:T(8,128)(2,1)S(1)} %fusion.2.refs_0_, bf16[1,256,768]{2,1,0:T(8,128)(2,1)S(1)} %collective-permute-done.13.refs_1_, bf16[2,256,256]{2,1,0:T(8,128)(2,1)S(1)} %collective-permute-done.15.refs_2_, ...), custom_call_target="tpu_custom_call" | custom-call | flops 1 | bytes 1 | tf_op jit(solution)/shard_map/down/pallas_call | solution.py:117
  73.9 0.8 collective-permute-done.14.refs_1_
  75.0 1.6 %collective-permute-start.17 = (bf16[1,256,256]{2,1,0:T(8,128)(2,1)S(1)}, bf16[1,256,256]{2,1,0:T(8,128)(2,1)S(1)}, u32[]{:S(2)}, u32[]{:S(2)}) collective-permute-start(bf16[1,256,256]{2,1,0:T(8,128)(2,1)S(1)} %fusion.refs_8_.refs_0_), channel_id=1, source_target_pairs={{0,2},{1,3},{2,0},{3,1},{4,6},{5,7},{6,4},{7,5},{8,10},{9,11},{10,... | collective-permute-start | bytes 393224 | tf_op jit(solution)/shard_map/ppermute | solution.py:23
  76.5 3.5 %down.6 = (f32[256,1536]{1,0:T(8,128)S(1)}, bf16[2,1024,1536]{2,1,0:T(8,128)(2,1)S(1)}) custom-call(s32[3]{0:T(128)S(1)} %pad_add_fusion.info, bf16[1,256,256]{2,1,0:T(8,128)(2,1)S(1)} %fusion.1.refs_0_, bf16[1,256,768]{2,1,0:T(8,128)(2,1)S(1)} %collective-permute-done.14.refs_1_, bf16[2,256,256]{2,1,0:T(8,128)(2,1)S(1)} %collective-permute-done.18.refs_2_, ...), custom_call_target="tpu_custom_call" | custom-call | flops 1 | bytes 1 | tf_op jit(solution)/shard_map/down/pallas_call | solution.py:117
  80.0 0.9 collective-permute-done.17.refs_1_
  81.0 1.5 %collective-permute-done.19.refs_2_ = bf16[2,256,256]{2,1,0:T(8,128)(2,1)S(1)} collective-permute-done((bf16[2,256,256]{2,1,0:T(8,128)(2,1)S(1)}, bf16[2,256,256]{2,1,0:T(8,128)(2,1)S(1)}, u32[]{:S(2)}, u32[]{:S(2)}) %collective-permute-start.19) | collective-permute-done | bytes 262176 | tf_op jit(solution)/shard_map/ppermute | solution.py:23
  82.5 2.2 %down.7 = (bf16[64,1536]{1,0:T(8,128)(2,1)S(1)}, bf16[32,1536]{1,0:T(8,128)(2,1)S(1)}, bf16[32,1536]{1,0:T(8,128)(2,1)S(1)}, bf16[32,1536]{1,0:T(8,128)(2,1)S(1)...) custom-call(s32[3]{0:T(128)S(1)} %pad_add_fusion.info, ...), custom_call_target="tpu_custom_call" | custom-call | flops 1 | bytes 1 | tf_op jit(solution)/shard_map/down/pallas_call | solution.py:117
  84.9 3.8 %collective-permute-start.20 = (bf16[32,1536]{1,0:T(8,128)(2,1)S(1)}, bf16[32,1536]{1,0:T(8,128)(2,1)S(1)}, u32[]{:S(2)}, u32[]{:S(2)}) collective-permute-start(bf16[32,1536]{1,0:T(8,128)(2,1)S(1)} %get-tuple-element.74), channel_id=1, source_target_pairs={{0,12},{4,0},{8,4},{12,8},{1,13},{5,1},{9,5},{13,9},{2,14},{6,2},{... | collective-permute-start | bytes 294920 | tf_op jit(solution)/shard_map/ppermute | solution.py:390
  88.7 3.8 %collective-permute-start.23 = (bf16[32,1536]{1,0:T(8,128)(2,1)S(1)}, bf16[32,1536]{1,0:T(8,128)(2,1)S(1)}, u32[]{:S(2)}, u32[]{:S(2)}) collective-permute-start(bf16[32,1536]{1,0:T(8,128)(2,1)S(1)} %get-tuple-element.76), channel_id=1, source_target_pairs={{0,12},{4,0},{8,4},{12,8},{1,13},{5,1},{9,5},{13,9},{2,14},{6,2},{... | collective-permute-start | bytes 294920 | tf_op jit(solution)/shard_map/ppermute | solution.py:390
  92.6 3.9 %collective-permute-start.21 = (bf16[32,1536]{1,0:T(8,128)(2,1)S(1)}, bf16[32,1536]{1,0:T(8,128)(2,1)S(1)}, u32[]{:S(2)}, u32[]{:S(2)}) collective-permute-start(bf16[32,1536]{1,0:T(8,128)(2,1)S(1)} %add_convert_fusion.1), channel_id=1, source_target_pairs={{0,12},{4,0},{8,4},{12,8},{1,13},{5,1},{9,5},{13,9},{2,14},{6,2},{... | collective-permute-start | bytes 294920 | tf_op jit(solution)/shard_map/ppermute | solution.py:390
  96.6 4.2 %collective-permute-done.25 = bf16[32,1536]{1,0:T(8,128)(2,1)S(1)} collective-permute-done((bf16[32,1536]{1,0:T(8,128)(2,1)S(1)}, bf16[32,1536]{1,0:T(8,128)(2,1)S(1)}, u32[]{:S(2)}, u32[]{:S(2)}) %collective-permute-start.25) | collective-permute-done | bytes 98336 | tf_op jit(solution)/shard_map/ppermute | solution.py:390
  (78 shorter events, 7.3 us)
Async XLA Ops:
  0.0 11.0 %collective-permute-start = (bf16[64,1536]{1,0:T(8,128)(2,1)}, bf16[64,1536]{1,0:T(8,128)(2,1)S(1)}, u32[]{:S(2)}, u32[]{:S(2)}) collective-permute-start(bf16[64,1536]{1,0:T(8,128)(2,1)} %refs_0_.9), channel_id=1, source_target_pairs={{0,4},{4,8},{8,12},{12,0},{1,5},{5,9},{9,13},{13,1},{2,6},{6,10},{... | collective-permute-start | bytes 589832 | tf_op jit(solution)/shard_map/ppermute | solution.py:371
  3.0 11.0 %collective-permute-start.1 = (bf16[64,1536]{1,0:T(8,128)(2,1)}, bf16[64,1536]{1,0:T(8,128)(2,1)S(1)}, u32[]{:S(2)}, u32[]{:S(2)}) collective-permute-start(bf16[64,1536]{1,0:T(8,128)(2,1)} %refs_0_.9), channel_id=1, source_target_pairs={{0,12},{4,0},{8,4},{12,8},{1,13},{5,1},{9,5},{13,9},{2,14},{6,2},{... | collective-permute-start | bytes 589832 | tf_op jit(solution)/shard_map/ppermute | solution.py:371
  6.4 14.2 %collective-permute-start.4 = (f32[16,64]{1,0:T(8,128)S(1)}, f32[16,64]{1,0:T(8,128)S(1)}, u32[]{:S(2)}, u32[]{:S(2)}) collective-permute-start(f32[16,64]{1,0:T(8,128)S(1)} %pad_maximum_fusion.8.refs_0_), channel_id=1, source_target_pairs={{0,4},{4,8},{8,12},{12,0},{1,5},{5,9},{9,13},{13,1},{2,6},{6,10},{... | collective-permute-start | bytes 12296 | tf_op jit(solution)/shard_map/ppermute | solution.py:306
  6.4 14.2 %collective-permute-start.5 = (f32[16,64]{1,0:T(8,128)S(1)}, f32[16,64]{1,0:T(8,128)S(1)}, u32[]{:S(2)}, u32[]{:S(2)}) collective-permute-start(f32[16,64]{1,0:T(8,128)S(1)} %pad_maximum_fusion.8.refs_0_), channel_id=1, source_target_pairs={{0,12},{4,0},{8,4},{12,8},{1,13},{5,1},{9,5},{13,9},{2,14},{6,2},{... | collective-permute-start | bytes 12296 | tf_op jit(solution)/shard_map/ppermute | solution.py:306
  10.3 10.4 %collective-permute-start.6 = (f32[16,64]{1,0:T(8,128)S(1)}, f32[16,64]{1,0:T(8,128)S(1)}, u32[]{:S(2)}, u32[]{:S(2)}) collective-permute-start(f32[16,64]{1,0:T(8,128)S(1)} %pad_maximum_fusion.8.refs_0_), channel_id=1, source_target_pairs={{0,8},{4,12},{8,0},{12,4},{1,9},{5,13},{9,1},{13,5},{2,10},{6,14},... | collective-permute-start | bytes 12296 | tf_op jit(solution)/shard_map/ppermute | solution.py:306
  11.0 10.4 %collective-permute-start.2 = (bf16[32,1536]{1,0:T(8,128)(2,1)S(1)}, bf16[32,1536]{1,0:T(8,128)(2,1)S(1)}, u32[]{:S(2)}, u32[]{:S(2)}) collective-permute-start(bf16[32,1536]{1,0:T(8,128)(2,1)S(1)} %slice.116), channel_id=1, source_target_pairs={{0,4},{4,8},{8,12},{12,0},{1,5},{5,9},{9,13},{13,1},{2,6},{6,10},{... | collective-permute-start | bytes 294920 | tf_op jit(solution)/shard_map/ppermute | solution.py:375
  14.0 7.5 %collective-permute-start.3 = (bf16[32,1536]{1,0:T(8,128)(2,1)S(1)}, bf16[32,1536]{1,0:T(8,128)(2,1)S(1)}, u32[]{:S(2)}, u32[]{:S(2)}) collective-permute-start(bf16[32,1536]{1,0:T(8,128)(2,1)S(1)} %slice.117), channel_id=1, source_target_pairs={{0,12},{4,0},{8,4},{12,8},{1,13},{5,1},{9,5},{13,9},{2,14},{6,2},{... | collective-permute-start | bytes 294920 | tf_op jit(solution)/shard_map/ppermute | solution.py:375
  17.2 4.2 %copy-start = (bf16[64,1536]{1,0:T(8,128)(2,1)S(1)}, bf16[64,1536]{1,0:T(8,128)(2,1)}, u32[]{:S(2)}) copy-start(bf16[64,1536]{1,0:T(8,128)(2,1)} %refs_0_.9) | copy-start | bytes 589828
  26.0 4.4 %collective-permute-start.7 = (bf16[2,256,512]{2,1,0:T(8,128)(2,1)S(1)}, bf16[2,256,512]{2,1,0:T(8,128)(2,1)S(1)}, u32[]{:S(2)}, u32[]{:S(2)}) collective-permute-start(bf16[2,256,512]{2,1,0:T(8,128)(2,1)S(1)} %get-tuple-element.47), channel_id=1, source_target_pairs={{0,1},{1,0},{2,3},{3,2},{4,5},{5,4},{6,7},{7,6},{8,9},{9,8},{10,11... | collective-permute-start | bytes 1572872 | tf_op jit(solution)/shard_map/ppermute | solution.py:23
  30.6 10.8 %collective-permute-start.9 = (bf16[1,256,512]{2,1,0:T(8,128)(2,1)S(1)}, bf16[1,256,512]{2,1,0:T(8,128)(2,1)S(1)}, u32[]{:S(2)}, u32[]{:S(2)}) collective-permute-start(bf16[1,256,512]{2,1,0:T(8,128)(2,1)S(1)} %slice.181.refs_9_), channel_id=1, source_target_pairs={{0,2},{1,3},{2,0},{3,1},{4,6},{5,7},{6,4},{7,5},{8,10},{9,11},{10,... | collective-permute-start | bytes 786440 | tf_op jit(solution)/shard_map/ppermute | solution.py:23
  36.8 4.7 %collective-permute-start.8 = (bf16[2,256,512]{2,1,0:T(8,128)(2,1)S(1)}, bf16[2,256,512]{2,1,0:T(8,128)(2,1)S(1)}, u32[]{:S(2)}, u32[]{:S(2)}) collective-permute-start(bf16[2,256,512]{2,1,0:T(8,128)(2,1)S(1)} %get-tuple-element.52), channel_id=1, source_target_pairs={{0,1},{1,0},{2,3},{3,2},{4,5},{5,4},{6,7},{7,6},{8,9},{9,8},{10,11... | collective-permute-start | bytes 1572872 | tf_op jit(solution)/shard_map/ppermute | solution.py:23
  41.8 11.4 %collective-permute-start.11 = (bf16[1,256,768]{2,1,0:T(8,128)(2,1)S(1)}, bf16[1,256,768]{2,1,0:T(8,128)(2,1)S(1)}, u32[]{:S(2)}, u32[]{:S(2)}) collective-permute-start(bf16[1,256,768]{2,1,0:T(8,128)(2,1)S(1)} %pad_maximum_fusion.refs_9_), channel_id=1, source_target_pairs={{0,2},{1,3},{2,0},{3,1},{4,6},{5,7},{6,4},{7,5},{8,10},{9,11},{10,... | collective-permute-start | bytes 1179656 | tf_op jit(solution)/shard_map/ppermute | solution.py:23
  46.9 6.5 %collective-permute-start.10 = (bf16[2,256,512]{2,1,0:T(8,128)(2,1)S(1)}, bf16[2,256,512]{2,1,0:T(8,128)(2,1)S(1)}, u32[]{:S(2)}, u32[]{:S(2)}) collective-permute-start(bf16[2,256,512]{2,1,0:T(8,128)(2,1)S(1)} %get-tuple-element.57), channel_id=1, source_target_pairs={{0,1},{1,0},{2,3},{3,2},{4,5},{5,4},{6,7},{7,6},{8,9},{9,8},{10,11... | collective-permute-start | bytes 1572872 | tf_op jit(solution)/shard_map/ppermute | solution.py:23
  53.1 5.8 %copy-start.1 = (bf16[1,256,768]{2,1,0:T(8,128)(2,1)}, bf16[1,256,768]{2,1,0:T(8,128)(2,1)S(1)}, u32[]{:S(2)}) copy-start(bf16[1,256,768]{2,1,0:T(8,128)(2,1)S(1)} %collective-permute-done.11.refs_1_) | copy-start | bytes 1179652
  53.5 10.6 %collective-permute-start.13 = (bf16[1,256,768]{2,1,0:T(8,128)(2,1)S(1)}, bf16[1,256,768]{2,1,0:T(8,128)(2,1)S(1)}, u32[]{:S(2)}, u32[]{:S(2)}) collective-permute-start(bf16[1,256,768]{2,1,0:T(8,128)(2,1)S(1)} %pad_maximum_fusion.1.refs_9_), channel_id=1, source_target_pairs={{0,2},{1,3},{2,0},{3,1},{4,6},{5,7},{6,4},{7,5},{8,10},{9,11},{10,... | collective-permute-start | bytes 1179656 | tf_op jit(solution)/shard_map/ppermute | solution.py:23
  58.8 5.5 %collective-permute-start.12 = (bf16[2,256,512]{2,1,0:T(8,128)(2,1)S(1)}, bf16[2,256,512]{2,1,0:T(8,128)(2,1)S(1)}, u32[]{:S(2)}, u32[]{:S(2)}) collective-permute-start(bf16[2,256,512]{2,1,0:T(8,128)(2,1)S(1)} %get-tuple-element.61), channel_id=1, source_target_pairs={{0,1},{1,0},{2,3},{3,2},{4,5},{5,4},{6,7},{7,6},{8,9},{9,8},{10,11... | collective-permute-start | bytes 1572872 | tf_op jit(solution)/shard_map/ppermute | solution.py:23
  58.9 6.2 %slice-start = ((bf16[1,256,768]{2,1,0:T(8,128)(2,1)}), bf16[1,256,256]{2,1,0:T(8,128)(2,1)S(1)}, s32[]{:S(2)}) async-start(bf16[1,256,768]{2,1,0:T(8,128)(2,1)} %copy-done.1), calls=%async_computation | async-start | bytes 262144 | tf_op jit(solution)/shard_map/slice | solution.py:271
  62.6 4.1 %copy-start.2 = (bf16[1,256,768]{2,1,0:T(8,128)(2,1)S(1)}, bf16[1,256,768]{2,1,0:T(8,128)(2,1)}, u32[]{:S(2)}) copy-start(bf16[1,256,768]{2,1,0:T(8,128)(2,1)} %copy-done.1) | copy-start | bytes 1179652
  64.5 10.1 %collective-permute-start.14 = (bf16[1,256,768]{2,1,0:T(8,128)(2,1)S(1)}, bf16[1,256,768]{2,1,0:T(8,128)(2,1)S(1)}, u32[]{:S(2)}, u32[]{:S(2)}) collective-permute-start(bf16[1,256,768]{2,1,0:T(8,128)(2,1)S(1)} %pad_maximum_fusion.2.refs_7_), channel_id=1, source_target_pairs={{0,2},{1,3},{2,0},{3,1},{4,6},{5,7},{6,4},{7,5},{8,10},{9,11},{10,... | collective-permute-start | bytes 1179656 | tf_op jit(solution)/shard_map/ppermute | solution.py:23
  65.2 1.6 %collective-permute-start.16 = (bf16[2,256,256]{2,1,0:T(8,128)(2,1)S(1)}, bf16[2,256,256]{2,1,0:T(8,128)(2,1)S(1)}, u32[]{:S(2)}, u32[]{:S(2)}) collective-permute-start(bf16[2,256,256]{2,1,0:T(8,128)(2,1)S(1)} %pad_maximum_fusion.4), channel_id=1, source_target_pairs={{0,1},{1,0},{2,3},{3,2},{4,5},{5,4},{6,7},{7,6},{8,9},{9,8},{10,11... | collective-permute-start | bytes 786440 | tf_op jit(solution)/shard_map/ppermute | solution.py:23
  65.3 5.0 %collective-permute-start.15 = (bf16[2,256,256]{2,1,0:T(8,128)(2,1)S(1)}, bf16[2,256,256]{2,1,0:T(8,128)(2,1)S(1)}, u32[]{:S(2)}, u32[]{:S(2)}) collective-permute-start(bf16[2,256,256]{2,1,0:T(8,128)(2,1)S(1)} %pad_maximum_fusion.3), channel_id=1, source_target_pairs={{0,1},{1,0},{2,3},{3,2},{4,5},{5,4},{6,7},{7,6},{8,9},{9,8},{10,11... | collective-permute-start | bytes 786440 | tf_op jit(solution)/shard_map/ppermute | solution.py:23
  74.7 1.8 %collective-permute-start.18 = (bf16[2,256,256]{2,1,0:T(8,128)(2,1)S(1)}, bf16[2,256,256]{2,1,0:T(8,128)(2,1)S(1)}, u32[]{:S(2)}, u32[]{:S(2)}) collective-permute-start(bf16[2,256,256]{2,1,0:T(8,128)(2,1)S(1)} %pad_maximum_fusion.5), channel_id=1, source_target_pairs={{0,1},{1,0},{2,3},{3,2},{4,5},{5,4},{6,7},{7,6},{8,9},{9,8},{10,11... | collective-permute-start | bytes 786440 | tf_op jit(solution)/shard_map/ppermute | solution.py:23
  75.0 6.0 %collective-permute-start.17 = (bf16[1,256,256]{2,1,0:T(8,128)(2,1)S(1)}, bf16[1,256,256]{2,1,0:T(8,128)(2,1)S(1)}, u32[]{:S(2)}, u32[]{:S(2)}) collective-permute-start(bf16[1,256,256]{2,1,0:T(8,128)(2,1)S(1)} %fusion.refs_8_.refs_0_), channel_id=1, source_target_pairs={{0,2},{1,3},{2,0},{3,1},{4,6},{5,7},{6,4},{7,5},{8,10},{9,11},{10,... | collective-permute-start | bytes 393224 | tf_op jit(solution)/shard_map/ppermute | solution.py:23
  80.9 1.6 %collective-permute-start.19 = (bf16[2,256,256]{2,1,0:T(8,128)(2,1)S(1)}, bf16[2,256,256]{2,1,0:T(8,128)(2,1)S(1)}, u32[]{:S(2)}, u32[]{:S(2)}) collective-permute-start(bf16[2,256,256]{2,1,0:T(8,128)(2,1)S(1)} %pad_maximum_fusion.6), channel_id=1, source_target_pairs={{0,1},{1,0},{2,3},{3,2},{4,5},{5,4},{6,7},{7,6},{8,9},{9,8},{10,11... | collective-permute-start | bytes 786440 | tf_op jit(solution)/shard_map/ppermute | solution.py:23
  84.8 7.7 %collective-permute-start.24 = (bf16[32,1536]{1,0:T(8,128)(2,1)S(1)}, bf16[32,1536]{1,0:T(8,128)(2,1)S(1)}, u32[]{:S(2)}, u32[]{:S(2)}) collective-permute-start(bf16[32,1536]{1,0:T(8,128)(2,1)S(1)} %get-tuple-element.78), channel_id=1, source_target_pairs={{0,4},{4,8},{8,12},{12,0},{1,5},{5,9},{9,13},{13,1},{2,6},{6,10},{... | collective-permute-start | bytes 294920 | tf_op jit(solution)/shard_map/ppermute | solution.py:390
  84.9 7.7 %collective-permute-start.20 = (bf16[32,1536]{1,0:T(8,128)(2,1)S(1)}, bf16[32,1536]{1,0:T(8,128)(2,1)S(1)}, u32[]{:S(2)}, u32[]{:S(2)}) collective-permute-start(bf16[32,1536]{1,0:T(8,128)(2,1)S(1)} %get-tuple-element.74), channel_id=1, source_target_pairs={{0,12},{4,0},{8,4},{12,8},{1,13},{5,1},{9,5},{13,9},{2,14},{6,2},{... | collective-permute-start | bytes 294920 | tf_op jit(solution)/shard_map/ppermute | solution.py:390
  88.7 7.9 %collective-permute-start.22 = (bf16[32,1536]{1,0:T(8,128)(2,1)S(1)}, bf16[32,1536]{1,0:T(8,128)(2,1)S(1)}, u32[]{:S(2)}, u32[]{:S(2)}) collective-permute-start(bf16[32,1536]{1,0:T(8,128)(2,1)S(1)} %get-tuple-element.75), channel_id=1, source_target_pairs={{0,4},{4,8},{8,12},{12,0},{1,5},{5,9},{9,13},{13,1},{2,6},{6,10},{... | collective-permute-start | bytes 294920 | tf_op jit(solution)/shard_map/ppermute | solution.py:390
  88.7 7.9 %collective-permute-start.23 = (bf16[32,1536]{1,0:T(8,128)(2,1)S(1)}, bf16[32,1536]{1,0:T(8,128)(2,1)S(1)}, u32[]{:S(2)}, u32[]{:S(2)}) collective-permute-start(bf16[32,1536]{1,0:T(8,128)(2,1)S(1)} %get-tuple-element.76), channel_id=1, source_target_pairs={{0,12},{4,0},{8,4},{12,8},{1,13},{5,1},{9,5},{13,9},{2,14},{6,2},{... | collective-permute-start | bytes 294920 | tf_op jit(solution)/shard_map/ppermute | solution.py:390
  92.5 8.2 %collective-permute-start.25 = (bf16[32,1536]{1,0:T(8,128)(2,1)S(1)}, bf16[32,1536]{1,0:T(8,128)(2,1)S(1)}, u32[]{:S(2)}, u32[]{:S(2)}) collective-permute-start(bf16[32,1536]{1,0:T(8,128)(2,1)S(1)} %add_convert_fusion), channel_id=1, source_target_pairs={{0,4},{4,8},{8,12},{12,0},{1,5},{5,9},{9,13},{13,1},{2,6},{6,10},{... | collective-permute-start | bytes 294920 | tf_op jit(solution)/shard_map/ppermute | solution.py:390
  92.6 8.1 %collective-permute-start.21 = (bf16[32,1536]{1,0:T(8,128)(2,1)S(1)}, bf16[32,1536]{1,0:T(8,128)(2,1)S(1)}, u32[]{:S(2)}, u32[]{:S(2)}) collective-permute-start(bf16[32,1536]{1,0:T(8,128)(2,1)S(1)} %add_convert_fusion.1), channel_id=1, source_target_pairs={{0,12},{4,0},{8,4},{12,8},{1,13},{5,1},{9,5},{13,9},{2,14},{6,2},{... | collective-permute-start | bytes 294920 | tf_op jit(solution)/shard_map/ppermute | solution.py:390

commit v15 on v13

--- a/solution.py
+++ b/solution.py
@@ -196,13 +196,27 @@
     fetch()
     parts, (rank, wt, given) = own[: len(lanes)], own[len(lanes) : len(lanes) + 3]
     before = None if first else own[-1]
-    hidden, mix, out = rest
-    most = hidden.shape[0] // len(experts)
+    mix, out, *hidden = rest
+    hidden = hidden[0] if hidden else None
+    most = mix.shape[0] // len(experts)
     width = parts[0].shape[-1]
-    n_dp = hidden.shape[1] // width
-    for part, (at, shares) in zip(parts, lanes):
+    n_dp = given.shape[1] // width
+    for part, (at, shares) in zip(parts, lanes) if hidden is not None else ():
         for j, l in enumerate(shares):
             hidden[:, units_of(l, info, n_dp, width)] = part[j, :, at : at + width]
+
+    def product(x, mine, cols):
+        if hidden is not None:
+            return jnp.dot(hidden[mine], given[x, :, cols], preferred_element_type=jnp.float32)
+        total = 0.0
+        for part, (at, shares) in zip(parts, lanes):
+            for j, l in enumerate(shares):
+                weights = given[x, units_of(l, info, n_dp, width), cols]
+                total = total + jnp.dot(
+                    part[j, mine, at : at + width], weights, preferred_element_type=jnp.float32
+                )
+        return total
+
     r = lax.broadcasted_iota(jnp.int32, (most, mix.shape[1]), 0).astype(jnp.float32)
     for x, e in enumerate(experts):
         mix[x * most : (x + 1) * most, :] = jnp.where(
@@ -214,9 +228,7 @@
         cols = slice(i * block, (i + 1) * block)
         for x in range(len(experts)):
             mine = slice(x * most, (x + 1) * most)
-            out[mine, cols] = jnp.dot(
-                hidden[mine], given[x, :, cols], preferred_element_type=jnp.float32
-            ).astype(jnp.bfloat16)
+            out[mine, cols] = product(x, mine, cols).astype(jnp.bfloat16)
         total = lax.dot_general(
             mix[...], out[:, cols], (((0,), (0,)), ((), ())), preferred_element_type=jnp.float32
         )
@@ -236,10 +248,11 @@
     before = [] if total is None else [total]
     outs = [jax.ShapeDtypeStruct((cut, local), kind) for cut in cuts]
     scratch = [
-        pltpu.VMEM((rows, hidden), jnp.bfloat16),
         pltpu.VMEM((rows, rank.shape[1]), jnp.bfloat16),
         pltpu.VMEM((rows, local), jnp.bfloat16),
     ]
+    if sum(len(shares) for _, shares in lanes) * parts[0].shape[2] == hidden:
+        scratch.append(pltpu.VMEM((rows, hidden), jnp.bfloat16))
     inputs = [(x, VMEM) for x in (*parts, rank, wt, given, *before)]
     body = functools.partial(down_body, lanes, experts, total is None)
     return call(body, "down", info, inputs, weights, ahead, after, outs, scratch)
@@ -273,6 +286,16 @@
     return parts
 
 
+def spread(held, whose, bits):
+    parts, whose = [(held, 0, [whose])], [whose]
+    for b in reversed(bits[:-1]):
+        theirs = flip(held, "dp", 1 << b)
+        parts.append((theirs, 0, [l | 1 << b for l in whose]))
+        if b > 0:
+            held, whose = jnp.concatenate([held, theirs], axis=0), whose + parts[-1][2]
+    return parts
+
+
 def on_device(tokens, expert_ids, scores, w_gate, w_up, w_down):
     n_owner, n_dp = lax.axis_size("expert"), lax.axis_size("dp")
     tok_rows, top = expert_ids.shape
@@ -312,10 +335,9 @@
     share = kept = late = None
 
     def add(c, after):
-        k, cuts = 2 * chunks + c, tall if c == chunks - 1 else [sum(tall)]
-        outs = down(parts[c], rank, wt, info, given[k], weights, total, of(c), cuts, ahead(k), after)
-        outs = fetched(k, outs)
-        return outs if c == chunks - 1 else outs[0]
+        k = 2 * chunks + c
+        outs = down(parts[c], rank, wt, info, given[k], weights, total, of(c), [sum(tall)], ahead(k), after)
+        return fetched(k, outs)[0]
 
     for c in range(chunks):
         last = c == chunks - 1
@@ -342,10 +364,11 @@
     other = flip(share, "dp", cross)
     for c in range(max(min(chunks - 2, 2), 0), chunks - 1):
         total = add(c, [share])
-    if total is not None:
-        other = lax.optimization_barrier((other, total))[0]
-    parts.append(everyone_s(share, other, 0, bits))
-    total = add(chunks - 1, [])
+    k = 3 * chunks - 1
+    near = spread(share, 0, bits)
+    total = down(near, rank, wt, info, given[k], weights, total, of(chunks - 1), [sum(tall)], None, [])[0]
+    far = spread(lax.optimization_barrier((other, total))[0], cross, bits)
+    total = down(far, rank, wt, info, given[k], weights, total, of(chunks - 1), tall, None, [])
     return returned(total, "expert").astype(jnp.bfloat16)
 
 

time: 101 us -> 102 us (level)
  Pallas kernels: 51.3 us -> 52.5 us
  waiting for transfers between devices: 15.7 us -> 14.6 us
    pallas_call x13 -> x14, Pallas kernels: 50.5 us -> 51.7 us  [call(): pl.pallas_call(whole, out_shape=tuple(outs), in_specs=[SMEM] + [spec for...]
    ppermute x13 -> x14, waiting for transfers between devices: 7.78 us -> 6.67 us  [flip(): lax.ppermute(x, axis, [(i, i ^ k) for i in range(lax.axis_size(axis))])]
    ppermute x13 -> x14, starting transfers between devices: 6.17 us -> 6.67 us  [flip(): lax.ppermute(x, axis, [(i, i ^ k) for i in range(lax.axis_size(axis))])]
  transfers between devices with their start and end apart: 26 -> 27, of which waited for: 9 -> 8; matrix products, arithmetic and copies ran while one was open for 2% -> 2% of each run, Pallas kernels for 44% -> 45%
where the time goes in v15:
time: 102 us
  Pallas kernels  52.5 us (51%)
  starting transfers between devices  30.4 us (30%)
  waiting for transfers between devices  14.6 us (14%)
  other arithmetic  3.65 us (4%)
    pallas_call x14, Pallas kernels, call(): pl.pallas_call(whole, out_shape=tuple(outs), in_specs=[SMEM] + [spec for...  51.7 us
    ppermute x6, starting transfers between devices, hop(): return lax.ppermute(total, axis, perm)  11.6 us
    ppermute x14, waiting for transfers between devices, flip(): lax.ppermute(x, axis, [(i, i ^ k) for i in range(lax.axis_size(axis))])  6.67 us
    ppermute x14, starting transfers between devices, flip(): lax.ppermute(x, axis, [(i, i ^ k) for i in range(lax.axis_size(axis))])  6.67 us
    ppermute x6, waiting for transfers between devices, hop(): return lax.ppermute(total, axis, perm)  4.24 us
    ppermute x3, starting transfers between devices, on_device(): lax.ppermute(meta, 'expert', [(i, (i - k) % n_owner) for i in range(n_own...  3.83 us
    ppermute x1, starting transfers between devices, gathered(): lax.ppermute(above[half:], axis, down_)  3.15 us
    ppermute x1, starting transfers between devices, gathered(): lax.ppermute(below, axis, up)  3.02 us
  transfers between devices with their start and end apart: 27, of which 8 were waited for; matrix products, arithmetic and copies ran while one was open for 2% of the time, Pallas kernels for 45%

profile of v15, /device:TPU:0, one launch (start us, length us, event | category | flops | bytes accessed | tf_op | source)
XLA Modules:
  0.0 101.8 jit_solution(88139014072703092)
XLA Ops:
  0.0 3.0 %collective-permute-start = (bf16[64,1536]{1,0:T(8,128)(2,1)}, bf16[64,1536]{1,0:T(8,128)(2,1)S(1)}, u32[]{:S(2)}, u32[]{:S(2)}) collective-permute-start(bf16[64,1536]{1,0:T(8,128)(2,1)} %refs_0_.9), channel_id=1, source_target_pairs={{0,4},{4,8},{8,12},{12,0},{1,5},{5,9},{9,13},{13,1},{2,6},{6,10},{... | collective-permute-start | bytes 589832 | tf_op jit(solution)/shard_map/ppermute | solution.py:390
  3.0 2.0 %collective-permute-start.1 = (bf16[64,1536]{1,0:T(8,128)(2,1)}, bf16[64,1536]{1,0:T(8,128)(2,1)S(1)}, u32[]{:S(2)}, u32[]{:S(2)}) collective-permute-start(bf16[64,1536]{1,0:T(8,128)(2,1)} %refs_0_.9), channel_id=1, source_target_pairs={{0,12},{4,0},{8,4},{12,8},{1,13},{5,1},{9,5},{13,9},{2,14},{6,2},{... | collective-permute-start | bytes 589832 | tf_op jit(solution)/shard_map/ppermute | solution.py:390
  6.4 3.8 %collective-permute-start.5 = (f32[16,64]{1,0:T(8,128)S(1)}, f32[16,64]{1,0:T(8,128)S(1)}, u32[]{:S(2)}, u32[]{:S(2)}) collective-permute-start(f32[16,64]{1,0:T(8,128)S(1)} %pad_maximum_fusion.7.refs_0_), channel_id=1, source_target_pairs={{0,12},{4,0},{8,4},{12,8},{1,13},{5,1},{9,5},{13,9},{2,14},{6,2},{... | collective-permute-start | bytes 12296 | tf_op jit(solution)/shard_map/ppermute | solution.py:325
  10.3 0.8 collective-permute-done.refs_1_
  11.1 2.9 %collective-permute-done.1.refs_2_ = bf16[64,1536]{1,0:T(8,128)(2,1)S(1)} collective-permute-done((bf16[64,1536]{1,0:T(8,128)(2,1)}, bf16[64,1536]{1,0:T(8,128)(2,1)S(1)}, u32[]{:S(2)}, u32[]{:S(2)}) %collective-permute-start.1) | collective-permute-done | bytes 196640 | tf_op jit(solution)/shard_map/ppermute | solution.py:390
  14.0 3.2 %collective-permute-start.3 = (bf16[32,1536]{1,0:T(8,128)(2,1)S(1)}, bf16[32,1536]{1,0:T(8,128)(2,1)S(1)}, u32[]{:S(2)}, u32[]{:S(2)}) collective-permute-start(bf16[32,1536]{1,0:T(8,128)(2,1)S(1)} %slice.117), channel_id=1, source_target_pairs={{0,12},{4,0},{8,4},{12,8},{1,13},{5,1},{9,5},{13,9},{2,14},{6,2},{... | collective-permute-start | bytes 294920 | tf_op jit(solution)/shard_map/ppermute | solution.py:394
  17.2 3.4 %stage.1.refs_6_ = bf16[2,2,1536,512]{3,2,1,0:T(8,128)(2,1)S(1)} custom-call(s32[3]{0:T(128)S(1)} %pad_add_fusion.info, bf16[8,1536,1024]{2,1,0:T(8,128)(2,1)} %refs_7_.9, bf16[8,1536,1024]{2,1,0:T(8,128)(2,1)} %refs_8_.7), custom_call_target="tpu_custom_call" | custom-call | flops 1 | bytes 1 | tf_op jit(solution)/shard_map/stage/pallas_call | solution.py:113
  20.7 0.8 route.1
  21.4 4.5 %send_half.4 = (bf16[2,256,512]{2,1,0:T(8,128)(2,1)S(1)}, bf16[256,1536]{1,0:T(8,128)(2,1)S(1)}, bf16[2,2,1536,512]{3,2,1,0:T(8,128)(2,1)S(1)}) custom-call(s32[3]{0:T(128)S(1)} %pad_add_fusion.info, bf16[64,1536]{1,0:T(8,128)(2,1)S(1)} %copy-done, bf16[64,1536]{1,0:T(8,128)(2,1)S(1)} %collective-permute-done.refs_1_, ...), custom_call_target="tpu_custom_call" | custom-call | flops 1 | bytes 1 | tf_op jit(solution)/shard_map/send_half/pallas_call | solution.py:113
  26.0 4.2 %keep_half.4 = (bf16[2,256,512]{2,1,0:T(8,128)(2,1)S(1)}, bf16[2,2,1536,512]{3,2,1,0:T(8,128)(2,1)S(1)}) custom-call(s32[3]{0:T(128)S(1)} %pad_add_fusion.info, bf16[256,1536]{1,0:T(8,128)(2,1)S(1)} %get-tuple-element.43.refs_0_, bf16[2,2,1536,512]{3,2,1,0:T(8,128)(2,1)S(1)} %get-tuple-element.44.refs_1_, bf16[8,1536,1024]{2,1,0:T(8,128)(2,1)} %refs_7_.9, ...), custom_call_target="tpu_custom_call" | custom-call | flops 1 | bytes 1 | tf_op jit(solution)/shard_map/keep_half/pallas_call | solution.py:113
  30.4 1.6 %collective-permute-start.9 = (bf16[1,256,512]{2,1,0:T(8,128)(2,1)S(1)}, bf16[1,256,512]{2,1,0:T(8,128)(2,1)S(1)}, u32[]{:S(2)}, u32[]{:S(2)}) collective-permute-start(bf16[1,256,512]{2,1,0:T(8,128)(2,1)S(1)} %slice.181.refs_9_), channel_id=1, source_target_pairs={{0,2},{1,3},{2,0},{3,1},{4,6},{5,7},{6,4},{7,5},{8,10},{9,11},{10,... | collective-permute-start | bytes 786440 | tf_op jit(solution)/shard_map/ppermute | solution.py:23
  32.0 4.6 %send_half.5 = (bf16[2,256,512]{2,1,0:T(8,128)(2,1)S(1)}, bf16[256,1536]{1,0:T(8,128)(2,1)S(1)}, bf16[2,2,1536,512]{3,2,1,0:T(8,128)(2,1)S(1)}) custom-call(s32[3]{0:T(128)S(1)} %pad_add_fusion.info, bf16[64,1536]{1,0:T(8,128)(2,1)S(1)} %copy-done, bf16[64,1536]{1,0:T(8,128)(2,1)S(1)} %collective-permute-done.refs_1_, ...), custom_call_target="tpu_custom_call" | custom-call | flops 1 | bytes 1 | tf_op jit(solution)/shard_map/send_half/pallas_call | solution.py:113
  36.9 4.2 %keep_half.5 = (bf16[2,256,512]{2,1,0:T(8,128)(2,1)S(1)}, bf16[2,2,1536,512]{3,2,1,0:T(8,128)(2,1)S(1)}) custom-call(s32[3]{0:T(128)S(1)} %pad_add_fusion.info, bf16[256,1536]{1,0:T(8,128)(2,1)S(1)} %get-tuple-element.48.refs_0_, bf16[2,2,1536,512]{3,2,1,0:T(8,128)(2,1)S(1)} %get-tuple-element.49.refs_1_, bf16[8,1536,1024]{2,1,0:T(8,128)(2,1)} %refs_7_.9, ...), custom_call_target="tpu_custom_call" | custom-call | flops 1 | bytes 1 | tf_op jit(solution)/shard_map/keep_half/pallas_call | solution.py:113
  42.1 4.5 %send_half.6 = (bf16[2,256,512]{2,1,0:T(8,128)(2,1)S(1)}, bf16[256,1536]{1,0:T(8,128)(2,1)S(1)}, bf16[2,2,1536,512]{3,2,1,0:T(8,128)(2,1)S(1)}) custom-call(s32[3]{0:T(128)S(1)} %pad_add_fusion.info, bf16[64,1536]{1,0:T(8,128)(2,1)S(1)} %copy-done, bf16[64,1536]{1,0:T(8,128)(2,1)S(1)} %collective-permute-done.refs_1_, ...), custom_call_target="tpu_custom_call" | custom-call | flops 1 | bytes 1 | tf_op jit(solution)/shard_map/send_half/pallas_call | solution.py:113
  46.7 4.2 %keep_half.6 = (bf16[2,256,512]{2,1,0:T(8,128)(2,1)S(1)}, bf16[2,2,1536,512]{3,2,1,0:T(8,128)(2,1)S(1)}) custom-call(s32[3]{0:T(128)S(1)} %pad_add_fusion.info, bf16[256,1536]{1,0:T(8,128)(2,1)S(1)} %get-tuple-element.53.refs_0_, bf16[2,2,1536,512]{3,2,1,0:T(8,128)(2,1)S(1)} %get-tuple-element.54.refs_1_, bf16[8,1536,1024]{2,1,0:T(8,128)(2,1)} %refs_7_.9, ...), custom_call_target="tpu_custom_call" | custom-call | flops 1 | bytes 1 | tf_op jit(solution)/shard_map/keep_half/pallas_call | solution.py:113
  50.9 2.0 %collective-permute-done.11.refs_1_ = bf16[1,256,768]{2,1,0:T(8,128)(2,1)S(1)} collective-permute-done((bf16[1,256,768]{2,1,0:T(8,128)(2,1)S(1)}, bf16[1,256,768]{2,1,0:T(8,128)(2,1)S(1)}, u32[]{:S(2)}, u32[]{:S(2)}) %collective-permute-start.11) | collective-permute-done | bytes 393248 | tf_op jit(solution)/shard_map/ppermute | solution.py:23
  53.9 4.6 %send_half.7 = (bf16[2,256,512]{2,1,0:T(8,128)(2,1)S(1)}, bf16[256,1536]{1,0:T(8,128)(2,1)S(1)}, bf16[2,2,1536,512]{3,2,1,0:T(8,128)(2,1)S(1)}) custom-call(s32[3]{0:T(128)S(1)} %pad_add_fusion.info, bf16[64,1536]{1,0:T(8,128)(2,1)S(1)} %copy-done, bf16[64,1536]{1,0:T(8,128)(2,1)S(1)} %collective-permute-done.refs_1_, ...), custom_call_target="tpu_custom_call" | custom-call | flops 1 | bytes 1 | tf_op jit(solution)/shard_map/send_half/pallas_call | solution.py:113
  58.7 3.6 %keep_half.7 = (bf16[2,256,512]{2,1,0:T(8,128)(2,1)S(1)}, bf16[2,1024,1536]{2,1,0:T(8,128)(2,1)S(1)}) custom-call(s32[3]{0:T(128)S(1)} %pad_add_fusion.info, bf16[256,1536]{1,0:T(8,128)(2,1)S(1)} %get-tuple-element.58.refs_0_, bf16[2,2,1536,512]{3,2,1,0:T(8,128)(2,1)S(1)} %get-tuple-element.59.refs_1_, bf16[8,1024,1536]{2,1,0:T(8,128)(2,1)} %refs_7_.11), custom_call_target="tpu_custom_call" | custom-call | flops 1 | bytes 1 | tf_op jit(solution)/shard_map/keep_half/pallas_call | solution.py:113
  62.3 1.6 %collective-permute-done.13.refs_1_ = bf16[1,256,768]{2,1,0:T(8,128)(2,1)S(1)} collective-permute-done((bf16[1,256,768]{2,1,0:T(8,128)(2,1)S(1)}, bf16[1,256,768]{2,1,0:T(8,128)(2,1)S(1)}, u32[]{:S(2)}, u32[]{:S(2)}) %collective-permute-start.13) | collective-permute-done | bytes 393248 | tf_op jit(solution)/shard_map/ppermute | solution.py:23
  65.6 0.9 collective-permute-done.16.refs_2_
  66.5 3.4 %down.5 = (f32[256,1536]{1,0:T(8,128)S(1)}, bf16[2,1024,1536]{2,1,0:T(8,128)(2,1)S(1)}) custom-call(s32[3]{0:T(128)S(1)} %pad_add_fusion.info, bf16[1,256,256]{2,1,0:T(8,128)(2,1)S(1)} %fusion.3.refs_0_, bf16[1,256,768]{2,1,0:T(8,128)(2,1)S(1)} %copy-done.2, bf16[2,256,256]{2,1,0:T(8,128)(2,1)S(1)} %collective-permute-done.16.refs_2_, ...), custom_call_target="tpu_custom_call" | custom-call | flops 1 | bytes 1 | tf_op jit(solution)/shard_map/down/pallas_call | solution.py:113
  70.0 3.5 %down.6 = (f32[256,1536]{1,0:T(8,128)S(1)}, bf16[2,1024,1536]{2,1,0:T(8,128)(2,1)S(1)}) custom-call(s32[3]{0:T(128)S(1)} %pad_add_fusion.info, bf16[1,256,256]{2,1,0:T(8,128)(2,1)S(1)} %fusion.2.refs_0_, bf16[1,256,768]{2,1,0:T(8,128)(2,1)S(1)} %collective-permute-done.13.refs_1_, bf16[2,256,256]{2,1,0:T(8,128)(2,1)S(1)} %collective-permute-done.15.refs_2_, ...), custom_call_target="tpu_custom_call" | custom-call | flops 1 | bytes 1 | tf_op jit(solution)/shard_map/down/pallas_call | solution.py:113
  73.5 0.9 collective-permute-done.14.refs_1_
  75.2 1.5 %collective-permute-start.17 = (bf16[1,256,256]{2,1,0:T(8,128)(2,1)S(1)}, bf16[1,256,256]{2,1,0:T(8,128)(2,1)S(1)}, u32[]{:S(2)}, u32[]{:S(2)}) collective-permute-start(bf16[1,256,256]{2,1,0:T(8,128)(2,1)S(1)} %fusion.refs_8_.refs_0_), channel_id=1, source_target_pairs={{0,2},{1,3},{2,0},{3,1},{4,6},{5,7},{6,4},{7,5},{8,10},{9,11},{10,... | collective-permute-start | bytes 393224 | tf_op jit(solution)/shard_map/ppermute | solution.py:23
  76.7 3.5 %down.7 = (f32[256,1536]{1,0:T(8,128)S(1)}, bf16[2,1024,1536]{2,1,0:T(8,128)(2,1)S(1)}) custom-call(s32[3]{0:T(128)S(1)} %pad_add_fusion.info, bf16[1,256,256]{2,1,0:T(8,128)(2,1)S(1)} %fusion.1.refs_0_, bf16[1,256,768]{2,1,0:T(8,128)(2,1)S(1)} %collective-permute-done.14.refs_1_, bf16[2,256,256]{2,1,0:T(8,128)(2,1)S(1)} %collective-permute-done.19.refs_2_, ...), custom_call_target="tpu_custom_call" | custom-call | flops 1 | bytes 1 | tf_op jit(solution)/shard_map/down/pallas_call | solution.py:113
  80.2 1.7 %down.8.refs_5_ = f32[256,1536]{1,0:T(8,128)S(1)} custom-call(s32[3]{0:T(128)S(1)} %pad_add_fusion.info, bf16[1,256,256]{2,1,0:T(8,128)(2,1)S(1)} %fusion.refs_8_.refs_0_, bf16[1,256,256]{2,1,0:T(8,128)(2,1)S(1)} %collective-permute-done.18.refs_1_, f32[8,256]{1,0:T(8,128)S(1)} %get-tuple-element.42.refs_5_.refs_3_.refs_2_, ...), custom_call_target="tpu_custom_call" | custom-call | flops 1 | bytes 1 | tf_op jit(solution)/shard_map/down/pallas_call | solution.py:113
  82.0 1.3 %collective-permute-done.20.refs_1_ = bf16[1,256,256]{2,1,0:T(8,128)(2,1)S(1)} collective-permute-done((bf16[1,256,256]{2,1,0:T(8,128)(2,1)S(1)}, bf16[1,256,256]{2,1,0:T(8,128)(2,1)S(1)}, u32[]{:S(2)}, u32[]{:S(2)}) %collective-permute-start.20) | collective-permute-done | bytes 131104 | tf_op jit(solution)/shard_map/ppermute | solution.py:23
  83.3 1.7 %down.9 = (bf16[64,1536]{1,0:T(8,128)(2,1)S(1)}, bf16[32,1536]{1,0:T(8,128)(2,1)S(1)}, bf16[32,1536]{1,0:T(8,128)(2,1)S(1)}, bf16[32,1536]{1,0:T(8,128)(2,1)S(1)...) custom-call(s32[3]{0:T(128)S(1)} %pad_add_fusion.info, ...), custom_call_target="tpu_custom_call" | custom-call | flops 1 | bytes 1 | tf_op jit(solution)/shard_map/down/pallas_call | solution.py:113
  85.1 3.8 %collective-permute-start.21 = (bf16[32,1536]{1,0:T(8,128)(2,1)S(1)}, bf16[32,1536]{1,0:T(8,128)(2,1)S(1)}, u32[]{:S(2)}, u32[]{:S(2)}) collective-permute-start(bf16[32,1536]{1,0:T(8,128)(2,1)S(1)} %get-tuple-element.74), channel_id=1, source_target_pairs={{0,12},{4,0},{8,4},{12,8},{1,13},{5,1},{9,5},{13,9},{2,14},{6,2},{... | collective-permute-start | bytes 294920 | tf_op jit(solution)/shard_map/ppermute | solution.py:409
  89.0 3.8 %collective-permute-start.24 = (bf16[32,1536]{1,0:T(8,128)(2,1)S(1)}, bf16[32,1536]{1,0:T(8,128)(2,1)S(1)}, u32[]{:S(2)}, u32[]{:S(2)}) collective-permute-start(bf16[32,1536]{1,0:T(8,128)(2,1)S(1)} %get-tuple-element.76), channel_id=1, source_target_pairs={{0,12},{4,0},{8,4},{12,8},{1,13},{5,1},{9,5},{13,9},{2,14},{6,2},{... | collective-permute-start | bytes 294920 | tf_op jit(solution)/shard_map/ppermute | solution.py:409
  92.9 3.9 %collective-permute-start.22 = (bf16[32,1536]{1,0:T(8,128)(2,1)S(1)}, bf16[32,1536]{1,0:T(8,128)(2,1)S(1)}, u32[]{:S(2)}, u32[]{:S(2)}) collective-permute-start(bf16[32,1536]{1,0:T(8,128)(2,1)S(1)} %add_convert_fusion.1), channel_id=1, source_target_pairs={{0,12},{4,0},{8,4},{12,8},{1,13},{5,1},{9,5},{13,9},{2,14},{6,2},{... | collective-permute-start | bytes 294920 | tf_op jit(solution)/shard_map/ppermute | solution.py:409
  96.8 4.2 %collective-permute-done.26 = bf16[32,1536]{1,0:T(8,128)(2,1)S(1)} collective-permute-done((bf16[32,1536]{1,0:T(8,128)(2,1)S(1)}, bf16[32,1536]{1,0:T(8,128)(2,1)S(1)}, u32[]{:S(2)}, u32[]{:S(2)}) %collective-permute-start.26) | collective-permute-done | bytes 98336 | tf_op jit(solution)/shard_map/ppermute | solution.py:409
  (80 shorter events, 7.7 us)
Async XLA Ops:
  0.0 11.0 %collective-permute-start = (bf16[64,1536]{1,0:T(8,128)(2,1)}, bf16[64,1536]{1,0:T(8,128)(2,1)S(1)}, u32[]{:S(2)}, u32[]{:S(2)}) collective-permute-start(bf16[64,1536]{1,0:T(8,128)(2,1)} %refs_0_.9), channel_id=1, source_target_pairs={{0,4},{4,8},{8,12},{12,0},{1,5},{5,9},{9,13},{13,1},{2,6},{6,10},{... | collective-permute-start | bytes 589832 | tf_op jit(solution)/shard_map/ppermute | solution.py:390
  3.0 11.0 %collective-permute-start.1 = (bf16[64,1536]{1,0:T(8,128)(2,1)}, bf16[64,1536]{1,0:T(8,128)(2,1)S(1)}, u32[]{:S(2)}, u32[]{:S(2)}) collective-permute-start(bf16[64,1536]{1,0:T(8,128)(2,1)} %refs_0_.9), channel_id=1, source_target_pairs={{0,12},{4,0},{8,4},{12,8},{1,13},{5,1},{9,5},{13,9},{2,14},{6,2},{... | collective-permute-start | bytes 589832 | tf_op jit(solution)/shard_map/ppermute | solution.py:390
  6.4 14.2 %collective-permute-start.4 = (f32[16,64]{1,0:T(8,128)S(1)}, f32[16,64]{1,0:T(8,128)S(1)}, u32[]{:S(2)}, u32[]{:S(2)}) collective-permute-start(f32[16,64]{1,0:T(8,128)S(1)} %pad_maximum_fusion.7.refs_0_), channel_id=1, source_target_pairs={{0,4},{4,8},{8,12},{12,0},{1,5},{5,9},{9,13},{13,1},{2,6},{6,10},{... | collective-permute-start | bytes 12296 | tf_op jit(solution)/shard_map/ppermute | solution.py:325
  6.4 14.2 %collective-permute-start.5 = (f32[16,64]{1,0:T(8,128)S(1)}, f32[16,64]{1,0:T(8,128)S(1)}, u32[]{:S(2)}, u32[]{:S(2)}) collective-permute-start(f32[16,64]{1,0:T(8,128)S(1)} %pad_maximum_fusion.7.refs_0_), channel_id=1, source_target_pairs={{0,12},{4,0},{8,4},{12,8},{1,13},{5,1},{9,5},{13,9},{2,14},{6,2},{... | collective-permute-start | bytes 12296 | tf_op jit(solution)/shard_map/ppermute | solution.py:325
  10.3 10.4 %collective-permute-start.6 = (f32[16,64]{1,0:T(8,128)S(1)}, f32[16,64]{1,0:T(8,128)S(1)}, u32[]{:S(2)}, u32[]{:S(2)}) collective-permute-start(f32[16,64]{1,0:T(8,128)S(1)} %pad_maximum_fusion.7.refs_0_), channel_id=1, source_target_pairs={{0,8},{4,12},{8,0},{12,4},{1,9},{5,13},{9,1},{13,5},{2,10},{6,14},... | collective-permute-start | bytes 12296 | tf_op jit(solution)/shard_map/ppermute | solution.py:325
  11.0 10.4 %collective-permute-start.2 = (bf16[32,1536]{1,0:T(8,128)(2,1)S(1)}, bf16[32,1536]{1,0:T(8,128)(2,1)S(1)}, u32[]{:S(2)}, u32[]{:S(2)}) collective-permute-start(bf16[32,1536]{1,0:T(8,128)(2,1)S(1)} %slice.116), channel_id=1, source_target_pairs={{0,4},{4,8},{8,12},{12,0},{1,5},{5,9},{9,13},{13,1},{2,6},{6,10},{... | collective-permute-start | bytes 294920 | tf_op jit(solution)/shard_map/ppermute | solution.py:394
  14.0 7.4 %collective-permute-start.3 = (bf16[32,1536]{1,0:T(8,128)(2,1)S(1)}, bf16[32,1536]{1,0:T(8,128)(2,1)S(1)}, u32[]{:S(2)}, u32[]{:S(2)}) collective-permute-start(bf16[32,1536]{1,0:T(8,128)(2,1)S(1)} %slice.117), channel_id=1, source_target_pairs={{0,12},{4,0},{8,4},{12,8},{1,13},{5,1},{9,5},{13,9},{2,14},{6,2},{... | collective-permute-start | bytes 294920 | tf_op jit(solution)/shard_map/ppermute | solution.py:394
  17.2 4.2 %copy-start = (bf16[64,1536]{1,0:T(8,128)(2,1)S(1)}, bf16[64,1536]{1,0:T(8,128)(2,1)}, u32[]{:S(2)}) copy-start(bf16[64,1536]{1,0:T(8,128)(2,1)} %refs_0_.9) | copy-start | bytes 589828
  25.9 4.3 %collective-permute-start.7 = (bf16[2,256,512]{2,1,0:T(8,128)(2,1)S(1)}, bf16[2,256,512]{2,1,0:T(8,128)(2,1)S(1)}, u32[]{:S(2)}, u32[]{:S(2)}) collective-permute-start(bf16[2,256,512]{2,1,0:T(8,128)(2,1)S(1)} %get-tuple-element.47), channel_id=1, source_target_pairs={{0,1},{1,0},{2,3},{3,2},{4,5},{5,4},{6,7},{7,6},{8,9},{9,8},{10,11... | collective-permute-start | bytes 1572872 | tf_op jit(solution)/shard_map/ppermute | solution.py:23
  30.4 10.7 %collective-permute-start.9 = (bf16[1,256,512]{2,1,0:T(8,128)(2,1)S(1)}, bf16[1,256,512]{2,1,0:T(8,128)(2,1)S(1)}, u32[]{:S(2)}, u32[]{:S(2)}) collective-permute-start(bf16[1,256,512]{2,1,0:T(8,128)(2,1)S(1)} %slice.181.refs_9_), channel_id=1, source_target_pairs={{0,2},{1,3},{2,0},{3,1},{4,6},{5,7},{6,4},{7,5},{8,10},{9,11},{10,... | collective-permute-start | bytes 786440 | tf_op jit(solution)/shard_map/ppermute | solution.py:23
  36.6 4.7 %collective-permute-start.8 = (bf16[2,256,512]{2,1,0:T(8,128)(2,1)S(1)}, bf16[2,256,512]{2,1,0:T(8,128)(2,1)S(1)}, u32[]{:S(2)}, u32[]{:S(2)}) collective-permute-start(bf16[2,256,512]{2,1,0:T(8,128)(2,1)S(1)} %get-tuple-element.52), channel_id=1, source_target_pairs={{0,1},{1,0},{2,3},{3,2},{4,5},{5,4},{6,7},{7,6},{8,9},{9,8},{10,11... | collective-permute-start | bytes 1572872 | tf_op jit(solution)/shard_map/ppermute | solution.py:23
  41.5 11.4 %collective-permute-start.11 = (bf16[1,256,768]{2,1,0:T(8,128)(2,1)S(1)}, bf16[1,256,768]{2,1,0:T(8,128)(2,1)S(1)}, u32[]{:S(2)}, u32[]{:S(2)}) collective-permute-start(bf16[1,256,768]{2,1,0:T(8,128)(2,1)S(1)} %pad_maximum_fusion.refs_9_), channel_id=1, source_target_pairs={{0,2},{1,3},{2,0},{3,1},{4,6},{5,7},{6,4},{7,5},{8,10},{9,11},{10,... | collective-permute-start | bytes 1179656 | tf_op jit(solution)/shard_map/ppermute | solution.py:23
  46.6 6.5 %collective-permute-start.10 = (bf16[2,256,512]{2,1,0:T(8,128)(2,1)S(1)}, bf16[2,256,512]{2,1,0:T(8,128)(2,1)S(1)}, u32[]{:S(2)}, u32[]{:S(2)}) collective-permute-start(bf16[2,256,512]{2,1,0:T(8,128)(2,1)S(1)} %get-tuple-element.57), channel_id=1, source_target_pairs={{0,1},{1,0},{2,3},{3,2},{4,5},{5,4},{6,7},{7,6},{8,9},{9,8},{10,11... | collective-permute-start | bytes 1572872 | tf_op jit(solution)/shard_map/ppermute | solution.py:23
  52.9 5.7 %copy-start.1 = (bf16[1,256,768]{2,1,0:T(8,128)(2,1)}, bf16[1,256,768]{2,1,0:T(8,128)(2,1)S(1)}, u32[]{:S(2)}) copy-start(bf16[1,256,768]{2,1,0:T(8,128)(2,1)S(1)} %collective-permute-done.11.refs_1_) | copy-start | bytes 1179652
  53.3 10.6 %collective-permute-start.13 = (bf16[1,256,768]{2,1,0:T(8,128)(2,1)S(1)}, bf16[1,256,768]{2,1,0:T(8,128)(2,1)S(1)}, u32[]{:S(2)}, u32[]{:S(2)}) collective-permute-start(bf16[1,256,768]{2,1,0:T(8,128)(2,1)S(1)} %pad_maximum_fusion.1.refs_9_), channel_id=1, source_target_pairs={{0,2},{1,3},{2,0},{3,1},{4,6},{5,7},{6,4},{7,5},{8,10},{9,11},{10,... | collective-permute-start | bytes 1179656 | tf_op jit(solution)/shard_map/ppermute | solution.py:23
  58.6 5.5 %collective-permute-start.12 = (bf16[2,256,512]{2,1,0:T(8,128)(2,1)S(1)}, bf16[2,256,512]{2,1,0:T(8,128)(2,1)S(1)}, u32[]{:S(2)}, u32[]{:S(2)}) collective-permute-start(bf16[2,256,512]{2,1,0:T(8,128)(2,1)S(1)} %get-tuple-element.61), channel_id=1, source_target_pairs={{0,1},{1,0},{2,3},{3,2},{4,5},{5,4},{6,7},{7,6},{8,9},{9,8},{10,11... | collective-permute-start | bytes 1572872 | tf_op jit(solution)/shard_map/ppermute | solution.py:23
  58.7 6.2 %slice-start = ((bf16[1,256,768]{2,1,0:T(8,128)(2,1)}), bf16[1,256,256]{2,1,0:T(8,128)(2,1)S(1)}, s32[]{:S(2)}) async-start(bf16[1,256,768]{2,1,0:T(8,128)(2,1)} %copy-done.1), calls=%async_computation | async-start | bytes 262144 | tf_op jit(solution)/shard_map/slice | solution.py:280
  62.3 4.2 %copy-start.2 = (bf16[1,256,768]{2,1,0:T(8,128)(2,1)S(1)}, bf16[1,256,768]{2,1,0:T(8,128)(2,1)}, u32[]{:S(2)}) copy-start(bf16[1,256,768]{2,1,0:T(8,128)(2,1)} %copy-done.1) | copy-start | bytes 1179652
  64.3 10.0 %collective-permute-start.14 = (bf16[1,256,768]{2,1,0:T(8,128)(2,1)S(1)}, bf16[1,256,768]{2,1,0:T(8,128)(2,1)S(1)}, u32[]{:S(2)}, u32[]{:S(2)}) collective-permute-start(bf16[1,256,768]{2,1,0:T(8,128)(2,1)S(1)} %pad_maximum_fusion.2.refs_7_), channel_id=1, source_target_pairs={{0,2},{1,3},{2,0},{3,1},{4,6},{5,7},{6,4},{7,5},{8,10},{9,11},{10,... | collective-permute-start | bytes 1179656 | tf_op jit(solution)/shard_map/ppermute | solution.py:23
  64.9 1.6 %collective-permute-start.16 = (bf16[2,256,256]{2,1,0:T(8,128)(2,1)S(1)}, bf16[2,256,256]{2,1,0:T(8,128)(2,1)S(1)}, u32[]{:S(2)}, u32[]{:S(2)}) collective-permute-start(bf16[2,256,256]{2,1,0:T(8,128)(2,1)S(1)} %pad_maximum_fusion.4), channel_id=1, source_target_pairs={{0,1},{1,0},{2,3},{3,2},{4,5},{5,4},{6,7},{7,6},{8,9},{9,8},{10,11... | collective-permute-start | bytes 786440 | tf_op jit(solution)/shard_map/ppermute | solution.py:23
  65.1 4.9 %collective-permute-start.15 = (bf16[2,256,256]{2,1,0:T(8,128)(2,1)S(1)}, bf16[2,256,256]{2,1,0:T(8,128)(2,1)S(1)}, u32[]{:S(2)}, u32[]{:S(2)}) collective-permute-start(bf16[2,256,256]{2,1,0:T(8,128)(2,1)S(1)} %pad_maximum_fusion.3), channel_id=1, source_target_pairs={{0,1},{1,0},{2,3},{3,2},{4,5},{5,4},{6,7},{7,6},{8,9},{9,8},{10,11... | collective-permute-start | bytes 786440 | tf_op jit(solution)/shard_map/ppermute | solution.py:23
  74.4 2.3 %collective-permute-start.19 = (bf16[2,256,256]{2,1,0:T(8,128)(2,1)S(1)}, bf16[2,256,256]{2,1,0:T(8,128)(2,1)S(1)}, u32[]{:S(2)}, u32[]{:S(2)}) collective-permute-start(bf16[2,256,256]{2,1,0:T(8,128)(2,1)S(1)} %pad_maximum_fusion.5), channel_id=1, source_target_pairs={{0,1},{1,0},{2,3},{3,2},{4,5},{5,4},{6,7},{7,6},{8,9},{9,8},{10,11... | collective-permute-start | bytes 786440 | tf_op jit(solution)/shard_map/ppermute | solution.py:23
  74.6 5.5 %collective-permute-start.18 = (bf16[1,256,256]{2,1,0:T(8,128)(2,1)S(1)}, bf16[1,256,256]{2,1,0:T(8,128)(2,1)S(1)}, u32[]{:S(2)}, u32[]{:S(2)}) collective-permute-start(bf16[1,256,256]{2,1,0:T(8,128)(2,1)S(1)} %fusion.refs_8_.refs_0_), channel_id=1, source_target_pairs={{0,1},{1,0},{2,3},{3,2},{4,5},{5,4},{6,7},{7,6},{8,9},{9,8},{10,11... | collective-permute-start | bytes 393224 | tf_op jit(solution)/shard_map/ppermute | solution.py:23
  75.2 6.7 %collective-permute-start.17 = (bf16[1,256,256]{2,1,0:T(8,128)(2,1)S(1)}, bf16[1,256,256]{2,1,0:T(8,128)(2,1)S(1)}, u32[]{:S(2)}, u32[]{:S(2)}) collective-permute-start(bf16[1,256,256]{2,1,0:T(8,128)(2,1)S(1)} %fusion.refs_8_.refs_0_), channel_id=1, source_target_pairs={{0,2},{1,3},{2,0},{3,1},{4,6},{5,7},{6,4},{7,5},{8,10},{9,11},{10,... | collective-permute-start | bytes 393224 | tf_op jit(solution)/shard_map/ppermute | solution.py:23
  81.9 1.4 %collective-permute-start.20 = (bf16[1,256,256]{2,1,0:T(8,128)(2,1)S(1)}, bf16[1,256,256]{2,1,0:T(8,128)(2,1)S(1)}, u32[]{:S(2)}, u32[]{:S(2)}) collective-permute-start(bf16[1,256,256]{2,1,0:T(8,128)(2,1)S(1)} %collective-permute-done.17.refs_0_), channel_id=1, source_target_pairs={{0,1},{1,0},{2,3},{3,2},{4,5},{5,4},{6,7},{7,6},{8,9},{9,8},{10,11... | collective-permute-start | bytes 393224 | tf_op jit(solution)/shard_map/ppermute | solution.py:23
  85.1 7.7 %collective-permute-start.25 = (bf16[32,1536]{1,0:T(8,128)(2,1)S(1)}, bf16[32,1536]{1,0:T(8,128)(2,1)S(1)}, u32[]{:S(2)}, u32[]{:S(2)}) collective-permute-start(bf16[32,1536]{1,0:T(8,128)(2,1)S(1)} %get-tuple-element.78), channel_id=1, source_target_pairs={{0,4},{4,8},{8,12},{12,0},{1,5},{5,9},{9,13},{13,1},{2,6},{6,10},{... | collective-permute-start | bytes 294920 | tf_op jit(solution)/shard_map/ppermute | solution.py:409
  85.1 7.7 %collective-permute-start.21 = (bf16[32,1536]{1,0:T(8,128)(2,1)S(1)}, bf16[32,1536]{1,0:T(8,128)(2,1)S(1)}, u32[]{:S(2)}, u32[]{:S(2)}) collective-permute-start(bf16[32,1536]{1,0:T(8,128)(2,1)S(1)} %get-tuple-element.74), channel_id=1, source_target_pairs={{0,12},{4,0},{8,4},{12,8},{1,13},{5,1},{9,5},{13,9},{2,14},{6,2},{... | collective-permute-start | bytes 294920 | tf_op jit(solution)/shard_map/ppermute | solution.py:409
  89.0 7.9 %collective-permute-start.23 = (bf16[32,1536]{1,0:T(8,128)(2,1)S(1)}, bf16[32,1536]{1,0:T(8,128)(2,1)S(1)}, u32[]{:S(2)}, u32[]{:S(2)}) collective-permute-start(bf16[32,1536]{1,0:T(8,128)(2,1)S(1)} %get-tuple-element.75), channel_id=1, source_target_pairs={{0,4},{4,8},{8,12},{12,0},{1,5},{5,9},{9,13},{13,1},{2,6},{6,10},{... | collective-permute-start | bytes 294920 | tf_op jit(solution)/shard_map/ppermute | solution.py:409
  89.0 7.9 %collective-permute-start.24 = (bf16[32,1536]{1,0:T(8,128)(2,1)S(1)}, bf16[32,1536]{1,0:T(8,128)(2,1)S(1)}, u32[]{:S(2)}, u32[]{:S(2)}) collective-permute-start(bf16[32,1536]{1,0:T(8,128)(2,1)S(1)} %get-tuple-element.76), channel_id=1, source_target_pairs={{0,12},{4,0},{8,4},{12,8},{1,13},{5,1},{9,5},{13,9},{2,14},{6,2},{... | collective-permute-start | bytes 294920 | tf_op jit(solution)/shard_map/ppermute | solution.py:409
  92.8 8.2 %collective-permute-start.26 = (bf16[32,1536]{1,0:T(8,128)(2,1)S(1)}, bf16[32,1536]{1,0:T(8,128)(2,1)S(1)}, u32[]{:S(2)}, u32[]{:S(2)}) collective-permute-start(bf16[32,1536]{1,0:T(8,128)(2,1)S(1)} %add_convert_fusion), channel_id=1, source_target_pairs={{0,4},{4,8},{8,12},{12,0},{1,5},{5,9},{9,13},{13,1},{2,6},{6,10},{... | collective-permute-start | bytes 294920 | tf_op jit(solution)/shard_map/ppermute | solution.py:409
  92.9 8.1 %collective-permute-start.22 = (bf16[32,1536]{1,0:T(8,128)(2,1)S(1)}, bf16[32,1536]{1,0:T(8,128)(2,1)S(1)}, u32[]{:S(2)}, u32[]{:S(2)}) collective-permute-start(bf16[32,1536]{1,0:T(8,128)(2,1)S(1)} %add_convert_fusion.1), channel_id=1, source_target_pairs={{0,12},{4,0},{8,4},{12,8},{1,13},{5,1},{9,5},{13,9},{2,14},{6,2},{... | collective-permute-start | bytes 294920 | tf_op jit(solution)/shard_map/ppermute | solution.py:409

commit v16 on v13

--- a/solution.py
+++ b/solution.py
@@ -330,14 +330,18 @@
         width = out.shape[2]
         if c > 0:
             share = finish(before, behind[:, :, :width], [])
-            out = jnp.concatenate([out, share], axis=2)
+            alone = last and c > 1
+            out = lax.optimization_barrier((out, share))[0] if alone else jnp.concatenate([out, share], axis=2)
         sent.append(out)
         late = flip(out, "dp", cross)
-        if c > 0:
+        if c > 0 and not alone:
             parts.append(everyone_s(share, late, width, bits))
         if last:
             for d in range(min(c - 1, 2)):
                 total = add(d, [out] if d == 0 else [])
+                if d == 0:
+                    share = lax.optimization_barrier((share, total))[0]
+                    parts.append(everyone_s(share, flip(share, "dp", cross), 0, bits))
     share = finish(kept, late[:, :, :width], [] if total is None else [total])
     other = flip(share, "dp", cross)
     for c in range(max(min(chunks - 2, 2), 0), chunks - 1):

time: 101 us -> 105 us (1.040)
  waiting for transfers between devices: 15.7 us -> 20.7 us
    ppermute x6, waiting for transfers between devices: 4.24 us -> 8.16 us  [hop(): return lax.ppermute(total, axis, perm)]
    ppermute x6, starting transfers between devices: 11.6 us -> 10 us  [hop(): return lax.ppermute(total, axis, perm)]
    ppermute x13 -> x14, waiting for transfers between devices: 7.78 us -> 8.89 us  [flip(): lax.ppermute(x, axis, [(i, i ^ k) for i in range(lax.axis_size(axis))])]
    ppermute x13 -> x14, starting transfers between devices: 6.17 us -> 6.79 us  [flip(): lax.ppermute(x, axis, [(i, i ^ k) for i in range(lax.axis_size(axis))])]
  transfers between devices with their start and end apart: 26 -> 27, of which waited for: 9 -> 11; matrix products, arithmetic and copies ran while one was open for 2% -> 2% of each run, Pallas kernels for 44% -> 42%
where the time goes in v16:
time: 105 us
  Pallas kernels  51.3 us (49%)
  starting transfers between devices  28.9 us (28%)
  waiting for transfers between devices  20.7 us (20%)
  other arithmetic  3.67 us (3%)
    pallas_call x13, Pallas kernels, call(): pl.pallas_call(whole, out_shape=tuple(outs), in_specs=[SMEM] + [spec for...  50.5 us
    ppermute x6, starting transfers between devices, hop(): return lax.ppermute(total, axis, perm)  10 us
    ppermute x14, waiting for transfers between devices, flip(): lax.ppermute(x, axis, [(i, i ^ k) for i in range(lax.axis_size(axis))])  8.89 us
    ppermute x6, waiting for transfers between devices, hop(): return lax.ppermute(total, axis, perm)  8.16 us
    ppermute x14, starting transfers between devices, flip(): lax.ppermute(x, axis, [(i, i ^ k) for i in range(lax.axis_size(axis))])  6.79 us
    ppermute x3, starting transfers between devices, on_device(): lax.ppermute(meta, 'expert', [(i, (i - k) % n_owner) for i in range(n_own...  3.83 us
    ppermute x1, starting transfers between devices, gathered(): lax.ppermute(above[half:], axis, down_)  3.15 us
    ppermute x1, starting transfers between devices, gathered(): lax.ppermute(below, axis, up)  3.02 us
  transfers between devices with their start and end apart: 27, of which 11 were waited for; matrix products, arithmetic and copies ran while one was open for 2% of the time, Pallas kernels for 42%

profile of v16, /device:TPU:0, one launch (start us, length us, event | category | flops | bytes accessed | tf_op | source)
XLA Modules:
  0.0 105.2 jit_solution(897338616568236690)
XLA Ops:
  0.0 3.0 %collective-permute-start = (bf16[64,1536]{1,0:T(8,128)(2,1)}, bf16[64,1536]{1,0:T(8,128)(2,1)S(1)}, u32[]{:S(2)}, u32[]{:S(2)}) collective-permute-start(bf16[64,1536]{1,0:T(8,128)(2,1)} %refs_0_.9), channel_id=1, source_target_pairs={{0,4},{4,8},{8,12},{12,0},{1,5},{5,9},{9,13},{13,1},{2,6},{6,10},{... | collective-permute-start | bytes 589832 | tf_op jit(solution)/shard_map/ppermute | solution.py:371
  3.0 2.0 %collective-permute-start.1 = (bf16[64,1536]{1,0:T(8,128)(2,1)}, bf16[64,1536]{1,0:T(8,128)(2,1)S(1)}, u32[]{:S(2)}, u32[]{:S(2)}) collective-permute-start(bf16[64,1536]{1,0:T(8,128)(2,1)} %refs_0_.9), channel_id=1, source_target_pairs={{0,12},{4,0},{8,4},{12,8},{1,13},{5,1},{9,5},{13,9},{2,14},{6,2},{... | collective-permute-start | bytes 589832 | tf_op jit(solution)/shard_map/ppermute | solution.py:371
  6.4 3.8 %collective-permute-start.5 = (f32[16,64]{1,0:T(8,128)S(1)}, f32[16,64]{1,0:T(8,128)S(1)}, u32[]{:S(2)}, u32[]{:S(2)}) collective-permute-start(f32[16,64]{1,0:T(8,128)S(1)} %pad_maximum_fusion.7.refs_0_), channel_id=1, source_target_pairs={{0,12},{4,0},{8,4},{12,8},{1,13},{5,1},{9,5},{13,9},{2,14},{6,2},{... | collective-permute-start | bytes 12296 | tf_op jit(solution)/shard_map/ppermute | solution.py:302
  10.3 0.8 collective-permute-done.refs_1_
  11.1 2.9 %collective-permute-done.1.refs_2_ = bf16[64,1536]{1,0:T(8,128)(2,1)S(1)} collective-permute-done((bf16[64,1536]{1,0:T(8,128)(2,1)}, bf16[64,1536]{1,0:T(8,128)(2,1)S(1)}, u32[]{:S(2)}, u32[]{:S(2)}) %collective-permute-start.1) | collective-permute-done | bytes 196640 | tf_op jit(solution)/shard_map/ppermute | solution.py:371
  14.0 3.2 %collective-permute-start.3 = (bf16[32,1536]{1,0:T(8,128)(2,1)S(1)}, bf16[32,1536]{1,0:T(8,128)(2,1)S(1)}, u32[]{:S(2)}, u32[]{:S(2)}) collective-permute-start(bf16[32,1536]{1,0:T(8,128)(2,1)S(1)} %slice.109), channel_id=1, source_target_pairs={{0,12},{4,0},{8,4},{12,8},{1,13},{5,1},{9,5},{13,9},{2,14},{6,2},{... | collective-permute-start | bytes 294920 | tf_op jit(solution)/shard_map/ppermute | solution.py:375
  17.2 3.4 %stage.1.refs_6_ = bf16[2,2,1536,512]{3,2,1,0:T(8,128)(2,1)S(1)} custom-call(s32[3]{0:T(128)S(1)} %pad_add_fusion.info, bf16[8,1536,1024]{2,1,0:T(8,128)(2,1)} %refs_7_.9, bf16[8,1536,1024]{2,1,0:T(8,128)(2,1)} %refs_8_.7), custom_call_target="tpu_custom_call" | custom-call | flops 1 | bytes 1 | tf_op jit(solution)/shard_map/stage/pallas_call | solution.py:113
  21.4 4.5 %send_half.4 = (bf16[2,256,512]{2,1,0:T(8,128)(2,1)S(1)}, bf16[256,1536]{1,0:T(8,128)(2,1)S(1)}, bf16[2,2,1536,512]{3,2,1,0:T(8,128)(2,1)S(1)}) custom-call(s32[3]{0:T(128)S(1)} %pad_add_fusion.info, bf16[64,1536]{1,0:T(8,128)(2,1)S(1)} %copy-done, bf16[64,1536]{1,0:T(8,128)(2,1)S(1)} %collective-permute-done.refs_1_, ...), custom_call_target="tpu_custom_call" | custom-call | flops 1 | bytes 1 | tf_op jit(solution)/shard_map/send_half/pallas_call | solution.py:113
  26.0 4.2 %keep_half.4 = (bf16[2,256,512]{2,1,0:T(8,128)(2,1)S(1)}, bf16[2,2,1536,512]{3,2,1,0:T(8,128)(2,1)S(1)}) custom-call(s32[3]{0:T(128)S(1)} %pad_add_fusion.info, bf16[256,1536]{1,0:T(8,128)(2,1)S(1)} %get-tuple-element.45.refs_0_, bf16[2,2,1536,512]{3,2,1,0:T(8,128)(2,1)S(1)} %get-tuple-element.46.refs_1_, bf16[8,1536,1024]{2,1,0:T(8,128)(2,1)} %refs_7_.9, ...), custom_call_target="tpu_custom_call" | custom-call | flops 1 | bytes 1 | tf_op jit(solution)/shard_map/keep_half/pallas_call | solution.py:113
  30.5 1.6 %collective-permute-start.9 = (bf16[1,256,512]{2,1,0:T(8,128)(2,1)S(1)}, bf16[1,256,512]{2,1,0:T(8,128)(2,1)S(1)}, u32[]{:S(2)}, u32[]{:S(2)}) collective-permute-start(bf16[1,256,512]{2,1,0:T(8,128)(2,1)S(1)} %slice.171.refs_9_), channel_id=1, source_target_pairs={{0,2},{1,3},{2,0},{3,1},{4,6},{5,7},{6,4},{7,5},{8,10},{9,11},{10,... | collective-permute-start | bytes 786440 | tf_op jit(solution)/shard_map/ppermute | solution.py:23
  32.0 4.6 %send_half.5 = (bf16[2,256,512]{2,1,0:T(8,128)(2,1)S(1)}, bf16[256,1536]{1,0:T(8,128)(2,1)S(1)}, bf16[2,2,1536,512]{3,2,1,0:T(8,128)(2,1)S(1)}) custom-call(s32[3]{0:T(128)S(1)} %pad_add_fusion.info, bf16[64,1536]{1,0:T(8,128)(2,1)S(1)} %copy-done, bf16[64,1536]{1,0:T(8,128)(2,1)S(1)} %collective-permute-done.refs_1_, ...), custom_call_target="tpu_custom_call" | custom-call | flops 1 | bytes 1 | tf_op jit(solution)/shard_map/send_half/pallas_call | solution.py:113
  36.9 4.2 %keep_half.5 = (bf16[2,256,512]{2,1,0:T(8,128)(2,1)S(1)}, bf16[2,2,1536,512]{3,2,1,0:T(8,128)(2,1)S(1)}) custom-call(s32[3]{0:T(128)S(1)} %pad_add_fusion.info, bf16[256,1536]{1,0:T(8,128)(2,1)S(1)} %get-tuple-element.50.refs_0_, bf16[2,2,1536,512]{3,2,1,0:T(8,128)(2,1)S(1)} %get-tuple-element.51.refs_1_, bf16[8,1536,1024]{2,1,0:T(8,128)(2,1)} %refs_7_.9, ...), custom_call_target="tpu_custom_call" | custom-call | flops 1 | bytes 1 | tf_op jit(solution)/shard_map/keep_half/pallas_call | solution.py:113
  42.1 4.5 %send_half.6 = (bf16[2,256,512]{2,1,0:T(8,128)(2,1)S(1)}, bf16[256,1536]{1,0:T(8,128)(2,1)S(1)}, bf16[2,2,1536,512]{3,2,1,0:T(8,128)(2,1)S(1)}) custom-call(s32[3]{0:T(128)S(1)} %pad_add_fusion.info, bf16[64,1536]{1,0:T(8,128)(2,1)S(1)} %copy-done, bf16[64,1536]{1,0:T(8,128)(2,1)S(1)} %collective-permute-done.refs_1_, ...), custom_call_target="tpu_custom_call" | custom-call | flops 1 | bytes 1 | tf_op jit(solution)/shard_map/send_half/pallas_call | solution.py:113
  46.7 4.2 %keep_half.6 = (bf16[2,256,512]{2,1,0:T(8,128)(2,1)S(1)}, bf16[2,2,1536,512]{3,2,1,0:T(8,128)(2,1)S(1)}) custom-call(s32[3]{0:T(128)S(1)} %pad_add_fusion.info, bf16[256,1536]{1,0:T(8,128)(2,1)S(1)} %get-tuple-element.55.refs_0_, bf16[2,2,1536,512]{3,2,1,0:T(8,128)(2,1)S(1)} %get-tuple-element.56.refs_1_, bf16[8,1536,1024]{2,1,0:T(8,128)(2,1)} %refs_7_.9, ...), custom_call_target="tpu_custom_call" | custom-call | flops 1 | bytes 1 | tf_op jit(solution)/shard_map/keep_half/pallas_call | solution.py:113
  50.9 2.0 %collective-permute-done.11.refs_1_ = bf16[1,256,768]{2,1,0:T(8,128)(2,1)S(1)} collective-permute-done((bf16[1,256,768]{2,1,0:T(8,128)(2,1)S(1)}, bf16[1,256,768]{2,1,0:T(8,128)(2,1)S(1)}, u32[]{:S(2)}, u32[]{:S(2)}) %collective-permute-start.11) | collective-permute-done | bytes 393248 | tf_op jit(solution)/shard_map/ppermute | solution.py:23
  54.1 4.7 %send_half.7 = (bf16[2,256,512]{2,1,0:T(8,128)(2,1)S(1)}, bf16[256,1536]{1,0:T(8,128)(2,1)S(1)}, bf16[2,2,1536,512]{3,2,1,0:T(8,128)(2,1)S(1)}) custom-call(s32[3]{0:T(128)S(1)} %pad_add_fusion.info, bf16[64,1536]{1,0:T(8,128)(2,1)S(1)} %copy-done, bf16[64,1536]{1,0:T(8,128)(2,1)S(1)} %collective-permute-done.refs_1_, ...), custom_call_target="tpu_custom_call" | custom-call | flops 1 | bytes 1 | tf_op jit(solution)/shard_map/send_half/pallas_call | solution.py:113
  59.3 3.6 %keep_half.7 = (bf16[2,256,512]{2,1,0:T(8,128)(2,1)S(1)}, bf16[2,1024,1536]{2,1,0:T(8,128)(2,1)S(1)}) custom-call(s32[3]{0:T(128)S(1)} %pad_add_fusion.info, bf16[256,1536]{1,0:T(8,128)(2,1)S(1)} %get-tuple-element.60.refs_0_, bf16[2,2,1536,512]{3,2,1,0:T(8,128)(2,1)S(1)} %get-tuple-element.61.refs_1_, bf16[8,1024,1536]{2,1,0:T(8,128)(2,1)} %refs_7_.11), custom_call_target="tpu_custom_call" | custom-call | flops 1 | bytes 1 | tf_op jit(solution)/shard_map/keep_half/pallas_call | solution.py:113
  62.9 1.0 collective-permute-done.13.refs_1_
  65.0 3.4 %down.4 = (f32[256,1536]{1,0:T(8,128)S(1)}, bf16[2,1024,1536]{2,1,0:T(8,128)(2,1)S(1)}) custom-call(s32[3]{0:T(128)S(1)} %pad_add_fusion.info, bf16[1,256,256]{2,1,0:T(8,128)(2,1)S(1)} %fusion.3.refs_0_, bf16[1,256,768]{2,1,0:T(8,128)(2,1)S(1)} %collective-permute-done.11.refs_1_, bf16[2,256,256]{2,1,0:T(8,128)(2,1)S(1)} %collective-permute-done.16.refs_2_, ...), custom_call_target="tpu_custom_call" | custom-call | flops 1 | bytes 1 | tf_op jit(solution)/shard_map/down/pallas_call | solution.py:113
  68.5 1.6 %collective-permute-start.18 = (bf16[1,256,256]{2,1,0:T(8,128)(2,1)S(1)}, bf16[1,256,256]{2,1,0:T(8,128)(2,1)S(1)}, u32[]{:S(2)}, u32[]{:S(2)}) collective-permute-start(bf16[1,256,256]{2,1,0:T(8,128)(2,1)S(1)} %fusion.1.refs_0_), channel_id=1, source_target_pairs={{0,2},{1,3},{2,0},{3,1},{4,6},{5,7},{6,4},{7,5},{8,10},{9,11},{10,... | collective-permute-start | bytes 393224 | tf_op jit(solution)/shard_map/ppermute | solution.py:23
  70.0 3.5 %down.5 = (f32[256,1536]{1,0:T(8,128)S(1)}, bf16[2,1024,1536]{2,1,0:T(8,128)(2,1)S(1)}) custom-call(s32[3]{0:T(128)S(1)} %pad_add_fusion.info, bf16[1,256,256]{2,1,0:T(8,128)(2,1)S(1)} %fusion.2.refs_0_, bf16[1,256,768]{2,1,0:T(8,128)(2,1)S(1)} %collective-permute-done.13.refs_1_, bf16[2,256,256]{2,1,0:T(8,128)(2,1)S(1)} %collective-permute-done.15.refs_2_, ...), custom_call_target="tpu_custom_call" | custom-call | flops 1 | bytes 1 | tf_op jit(solution)/shard_map/down/pallas_call | solution.py:113
  73.5 2.5 %collective-permute-done.18.refs_1_ = bf16[1,256,256]{2,1,0:T(8,128)(2,1)S(1)} collective-permute-done((bf16[1,256,256]{2,1,0:T(8,128)(2,1)S(1)}, bf16[1,256,256]{2,1,0:T(8,128)(2,1)S(1)}, u32[]{:S(2)}, u32[]{:S(2)}) %collective-permute-start.18) | collective-permute-done | bytes 131104 | tf_op jit(solution)/shard_map/ppermute | solution.py:23
  77.6 3.5 %down.6 = (f32[256,1536]{1,0:T(8,128)S(1)}, bf16[2,1024,1536]{2,1,0:T(8,128)(2,1)S(1)}) custom-call(s32[3]{0:T(128)S(1)} %pad_add_fusion.info, bf16[1,256,256]{2,1,0:T(8,128)(2,1)S(1)} %fusion.1.refs_0_, bf16[1,256,256]{2,1,0:T(8,128)(2,1)S(1)} %collective-permute-done.18.refs_1_, bf16[2,256,256]{2,1,0:T(8,128)(2,1)S(1)} %collective-permute-done.19.refs_2_, ...), custom_call_target="tpu_custom_call" | custom-call | flops 1 | bytes 1 | tf_op jit(solution)/shard_map/down/pallas_call | solution.py:113
  81.1 1.1 %collective-permute-done.17.refs_1_ = bf16[1,256,256]{2,1,0:T(8,128)(2,1)S(1)} collective-permute-done((bf16[1,256,256]{2,1,0:T(8,128)(2,1)S(1)}, bf16[1,256,256]{2,1,0:T(8,128)(2,1)S(1)}, u32[]{:S(2)}, u32[]{:S(2)}) %collective-permute-start.17) | collective-permute-done | bytes 131104 | tf_op jit(solution)/shard_map/ppermute | solution.py:23
  82.3 1.5 %collective-permute-done.20.refs_2_ = bf16[2,256,256]{2,1,0:T(8,128)(2,1)S(1)} collective-permute-done((bf16[2,256,256]{2,1,0:T(8,128)(2,1)S(1)}, bf16[2,256,256]{2,1,0:T(8,128)(2,1)S(1)}, u32[]{:S(2)}, u32[]{:S(2)}) %collective-permute-start.20) | collective-permute-done | bytes 262176 | tf_op jit(solution)/shard_map/ppermute | solution.py:23
  83.9 2.3 %down.7 = (bf16[64,1536]{1,0:T(8,128)(2,1)S(1)}, bf16[32,1536]{1,0:T(8,128)(2,1)S(1)}, bf16[32,1536]{1,0:T(8,128)(2,1)S(1)}, bf16[32,1536]{1,0:T(8,128)(2,1)S(1)...) custom-call(s32[3]{0:T(128)S(1)} %pad_add_fusion.info, ...), custom_call_target="tpu_custom_call" | custom-call | flops 1 | bytes 1 | tf_op jit(solution)/shard_map/down/pallas_call | solution.py:113
  86.1 2.2 %collective-permute-start.21 = (bf16[32,1536]{1,0:T(8,128)(2,1)S(1)}, bf16[32,1536]{1,0:T(8,128)(2,1)S(1)}, u32[]{:S(2)}, u32[]{:S(2)}) collective-permute-start(bf16[32,1536]{1,0:T(8,128)(2,1)S(1)} %get-tuple-element.78), channel_id=1, source_target_pairs={{0,12},{4,0},{8,4},{12,8},{1,13},{5,1},{9,5},{13,9},{2,14},{6,2},{... | collective-permute-start | bytes 294920 | tf_op jit(solution)/shard_map/ppermute | solution.py:390
  88.3 3.9 %collective-permute-start.24 = (bf16[32,1536]{1,0:T(8,128)(2,1)S(1)}, bf16[32,1536]{1,0:T(8,128)(2,1)S(1)}, u32[]{:S(2)}, u32[]{:S(2)}) collective-permute-start(bf16[32,1536]{1,0:T(8,128)(2,1)S(1)} %get-tuple-element.80), channel_id=1, source_target_pairs={{0,12},{4,0},{8,4},{12,8},{1,13},{5,1},{9,5},{13,9},{2,14},{6,2},{... | collective-permute-start | bytes 294920 | tf_op jit(solution)/shard_map/ppermute | solution.py:390
  92.2 3.7 %collective-permute-start.22 = (bf16[32,1536]{1,0:T(8,128)(2,1)S(1)}, bf16[32,1536]{1,0:T(8,128)(2,1)S(1)}, u32[]{:S(2)}, u32[]{:S(2)}) collective-permute-start(bf16[32,1536]{1,0:T(8,128)(2,1)S(1)} %add_convert_fusion.1), channel_id=1, source_target_pairs={{0,12},{4,0},{8,4},{12,8},{1,13},{5,1},{9,5},{13,9},{2,14},{6,2},{... | collective-permute-start | bytes 294920 | tf_op jit(solution)/shard_map/ppermute | solution.py:390
  95.9 2.1 %collective-permute-done.25 = bf16[32,1536]{1,0:T(8,128)(2,1)S(1)} collective-permute-done((bf16[32,1536]{1,0:T(8,128)(2,1)S(1)}, bf16[32,1536]{1,0:T(8,128)(2,1)S(1)}, u32[]{:S(2)}, u32[]{:S(2)}) %collective-permute-start.25) | collective-permute-done | bytes 98336 | tf_op jit(solution)/shard_map/ppermute | solution.py:390
  98.3 1.6 %collective-permute-done.22 = bf16[32,1536]{1,0:T(8,128)(2,1)S(1)} collective-permute-done((bf16[32,1536]{1,0:T(8,128)(2,1)S(1)}, bf16[32,1536]{1,0:T(8,128)(2,1)S(1)}, u32[]{:S(2)}, u32[]{:S(2)}) %collective-permute-start.22) | collective-permute-done | bytes 98336 | tf_op jit(solution)/shard_map/ppermute | solution.py:390
  100.0 4.5 %collective-permute-done.26 = bf16[32,1536]{1,0:T(8,128)(2,1)S(1)} collective-permute-done((bf16[32,1536]{1,0:T(8,128)(2,1)S(1)}, bf16[32,1536]{1,0:T(8,128)(2,1)S(1)}, u32[]{:S(2)}, u32[]{:S(2)}) %collective-permute-start.26) | collective-permute-done | bytes 98336 | tf_op jit(solution)/shard_map/ppermute | solution.py:390
  (72 shorter events, 9.5 us)
Async XLA Ops:
  0.0 11.0 %collective-permute-start = (bf16[64,1536]{1,0:T(8,128)(2,1)}, bf16[64,1536]{1,0:T(8,128)(2,1)S(1)}, u32[]{:S(2)}, u32[]{:S(2)}) collective-permute-start(bf16[64,1536]{1,0:T(8,128)(2,1)} %refs_0_.9), channel_id=1, source_target_pairs={{0,4},{4,8},{8,12},{12,0},{1,5},{5,9},{9,13},{13,1},{2,6},{6,10},{... | collective-permute-start | bytes 589832 | tf_op jit(solution)/shard_map/ppermute | solution.py:371
  3.0 11.0 %collective-permute-start.1 = (bf16[64,1536]{1,0:T(8,128)(2,1)}, bf16[64,1536]{1,0:T(8,128)(2,1)S(1)}, u32[]{:S(2)}, u32[]{:S(2)}) collective-permute-start(bf16[64,1536]{1,0:T(8,128)(2,1)} %refs_0_.9), channel_id=1, source_target_pairs={{0,12},{4,0},{8,4},{12,8},{1,13},{5,1},{9,5},{13,9},{2,14},{6,2},{... | collective-permute-start | bytes 589832 | tf_op jit(solution)/shard_map/ppermute | solution.py:371
  6.4 14.2 %collective-permute-start.4 = (f32[16,64]{1,0:T(8,128)S(1)}, f32[16,64]{1,0:T(8,128)S(1)}, u32[]{:S(2)}, u32[]{:S(2)}) collective-permute-start(f32[16,64]{1,0:T(8,128)S(1)} %pad_maximum_fusion.7.refs_0_), channel_id=1, source_target_pairs={{0,4},{4,8},{8,12},{12,0},{1,5},{5,9},{9,13},{13,1},{2,6},{6,10},{... | collective-permute-start | bytes 12296 | tf_op jit(solution)/shard_map/ppermute | solution.py:302
  6.4 14.2 %collective-permute-start.5 = (f32[16,64]{1,0:T(8,128)S(1)}, f32[16,64]{1,0:T(8,128)S(1)}, u32[]{:S(2)}, u32[]{:S(2)}) collective-permute-start(f32[16,64]{1,0:T(8,128)S(1)} %pad_maximum_fusion.7.refs_0_), channel_id=1, source_target_pairs={{0,12},{4,0},{8,4},{12,8},{1,13},{5,1},{9,5},{13,9},{2,14},{6,2},{... | collective-permute-start | bytes 12296 | tf_op jit(solution)/shard_map/ppermute | solution.py:302
  10.3 10.4 %collective-permute-start.6 = (f32[16,64]{1,0:T(8,128)S(1)}, f32[16,64]{1,0:T(8,128)S(1)}, u32[]{:S(2)}, u32[]{:S(2)}) collective-permute-start(f32[16,64]{1,0:T(8,128)S(1)} %pad_maximum_fusion.7.refs_0_), channel_id=1, source_target_pairs={{0,8},{4,12},{8,0},{12,4},{1,9},{5,13},{9,1},{13,5},{2,10},{6,14},... | collective-permute-start | bytes 12296 | tf_op jit(solution)/shard_map/ppermute | solution.py:302
  11.0 10.4 %collective-permute-start.2 = (bf16[32,1536]{1,0:T(8,128)(2,1)S(1)}, bf16[32,1536]{1,0:T(8,128)(2,1)S(1)}, u32[]{:S(2)}, u32[]{:S(2)}) collective-permute-start(bf16[32,1536]{1,0:T(8,128)(2,1)S(1)} %slice.108), channel_id=1, source_target_pairs={{0,4},{4,8},{8,12},{12,0},{1,5},{5,9},{9,13},{13,1},{2,6},{6,10},{... | collective-permute-start | bytes 294920 | tf_op jit(solution)/shard_map/ppermute | solution.py:375
  14.0 7.4 %collective-permute-start.3 = (bf16[32,1536]{1,0:T(8,128)(2,1)S(1)}, bf16[32,1536]{1,0:T(8,128)(2,1)S(1)}, u32[]{:S(2)}, u32[]{:S(2)}) collective-permute-start(bf16[32,1536]{1,0:T(8,128)(2,1)S(1)} %slice.109), channel_id=1, source_target_pairs={{0,12},{4,0},{8,4},{12,8},{1,13},{5,1},{9,5},{13,9},{2,14},{6,2},{... | collective-permute-start | bytes 294920 | tf_op jit(solution)/shard_map/ppermute | solution.py:375
  17.2 4.2 %copy-start = (bf16[64,1536]{1,0:T(8,128)(2,1)S(1)}, bf16[64,1536]{1,0:T(8,128)(2,1)}, u32[]{:S(2)}) copy-start(bf16[64,1536]{1,0:T(8,128)(2,1)} %refs_0_.9) | copy-start | bytes 589828
  25.9 4.3 %collective-permute-start.7 = (bf16[2,256,512]{2,1,0:T(8,128)(2,1)S(1)}, bf16[2,256,512]{2,1,0:T(8,128)(2,1)S(1)}, u32[]{:S(2)}, u32[]{:S(2)}) collective-permute-start(bf16[2,256,512]{2,1,0:T(8,128)(2,1)S(1)} %get-tuple-element.49), channel_id=1, source_target_pairs={{0,1},{1,0},{2,3},{3,2},{4,5},{5,4},{6,7},{7,6},{8,9},{9,8},{10,11... | collective-permute-start | bytes 1572872 | tf_op jit(solution)/shard_map/ppermute | solution.py:23
  30.5 10.7 %collective-permute-start.9 = (bf16[1,256,512]{2,1,0:T(8,128)(2,1)S(1)}, bf16[1,256,512]{2,1,0:T(8,128)(2,1)S(1)}, u32[]{:S(2)}, u32[]{:S(2)}) collective-permute-start(bf16[1,256,512]{2,1,0:T(8,128)(2,1)S(1)} %slice.171.refs_9_), channel_id=1, source_target_pairs={{0,2},{1,3},{2,0},{3,1},{4,6},{5,7},{6,4},{7,5},{8,10},{9,11},{10,... | collective-permute-start | bytes 786440 | tf_op jit(solution)/shard_map/ppermute | solution.py:23
  36.6 4.7 %collective-permute-start.8 = (bf16[2,256,512]{2,1,0:T(8,128)(2,1)S(1)}, bf16[2,256,512]{2,1,0:T(8,128)(2,1)S(1)}, u32[]{:S(2)}, u32[]{:S(2)}) collective-permute-start(bf16[2,256,512]{2,1,0:T(8,128)(2,1)S(1)} %get-tuple-element.54), channel_id=1, source_target_pairs={{0,1},{1,0},{2,3},{3,2},{4,5},{5,4},{6,7},{7,6},{8,9},{9,8},{10,11... | collective-permute-start | bytes 1572872 | tf_op jit(solution)/shard_map/ppermute | solution.py:23
  41.5 11.4 %collective-permute-start.11 = (bf16[1,256,768]{2,1,0:T(8,128)(2,1)S(1)}, bf16[1,256,768]{2,1,0:T(8,128)(2,1)S(1)}, u32[]{:S(2)}, u32[]{:S(2)}) collective-permute-start(bf16[1,256,768]{2,1,0:T(8,128)(2,1)S(1)} %pad_maximum_fusion.refs_9_), channel_id=1, source_target_pairs={{0,2},{1,3},{2,0},{3,1},{4,6},{5,7},{6,4},{7,5},{8,10},{9,11},{10,... | collective-permute-start | bytes 1179656 | tf_op jit(solution)/shard_map/ppermute | solution.py:23
  46.6 6.5 %collective-permute-start.10 = (bf16[2,256,512]{2,1,0:T(8,128)(2,1)S(1)}, bf16[2,256,512]{2,1,0:T(8,128)(2,1)S(1)}, u32[]{:S(2)}, u32[]{:S(2)}) collective-permute-start(bf16[2,256,512]{2,1,0:T(8,128)(2,1)S(1)} %get-tuple-element.59), channel_id=1, source_target_pairs={{0,1},{1,0},{2,3},{3,2},{4,5},{5,4},{6,7},{7,6},{8,9},{9,8},{10,11... | collective-permute-start | bytes 1572872 | tf_op jit(solution)/shard_map/ppermute | solution.py:23
  53.3 10.6 %collective-permute-start.13 = (bf16[1,256,768]{2,1,0:T(8,128)(2,1)S(1)}, bf16[1,256,768]{2,1,0:T(8,128)(2,1)S(1)}, u32[]{:S(2)}, u32[]{:S(2)}) collective-permute-start(bf16[1,256,768]{2,1,0:T(8,128)(2,1)S(1)} %pad_maximum_fusion.1.refs_9_), channel_id=1, source_target_pairs={{0,2},{1,3},{2,0},{3,1},{4,6},{5,7},{6,4},{7,5},{8,10},{9,11},{10,... | collective-permute-start | bytes 1179656 | tf_op jit(solution)/shard_map/ppermute | solution.py:23
  54.0 11.0 %collective-permute-start.16 = (bf16[2,256,256]{2,1,0:T(8,128)(2,1)S(1)}, bf16[2,256,256]{2,1,0:T(8,128)(2,1)S(1)}, u32[]{:S(2)}, u32[]{:S(2)}) collective-permute-start(bf16[2,256,256]{2,1,0:T(8,128)(2,1)S(1)} %pad_maximum_fusion.3), channel_id=1, source_target_pairs={{0,1},{1,0},{2,3},{3,2},{4,5},{5,4},{6,7},{7,6},{8,9},{9,8},{10,11... | collective-permute-start | bytes 786440 | tf_op jit(solution)/shard_map/ppermute | solution.py:23
  58.7 5.5 %collective-permute-start.12 = (bf16[2,256,512]{2,1,0:T(8,128)(2,1)S(1)}, bf16[2,256,512]{2,1,0:T(8,128)(2,1)S(1)}, u32[]{:S(2)}, u32[]{:S(2)}) collective-permute-start(bf16[2,256,512]{2,1,0:T(8,128)(2,1)S(1)} %get-tuple-element.63), channel_id=1, source_target_pairs={{0,1},{1,0},{2,3},{3,2},{4,5},{5,4},{6,7},{7,6},{8,9},{9,8},{10,11... | collective-permute-start | bytes 1572872 | tf_op jit(solution)/shard_map/ppermute | solution.py:23
  64.0 6.1 %collective-permute-start.15 = (bf16[2,256,256]{2,1,0:T(8,128)(2,1)S(1)}, bf16[2,256,256]{2,1,0:T(8,128)(2,1)S(1)}, u32[]{:S(2)}, u32[]{:S(2)}) collective-permute-start(bf16[2,256,256]{2,1,0:T(8,128)(2,1)S(1)} %pad_maximum_fusion.2), channel_id=1, source_target_pairs={{0,1},{1,0},{2,3},{3,2},{4,5},{5,4},{6,7},{7,6},{8,9},{9,8},{10,11... | collective-permute-start | bytes 786440 | tf_op jit(solution)/shard_map/ppermute | solution.py:23
  64.4 11.7 %collective-permute-start.14 = (bf16[1,256,512]{2,1,0:T(8,128)(2,1)S(1)}, bf16[1,256,512]{2,1,0:T(8,128)(2,1)S(1)}, u32[]{:S(2)}, u32[]{:S(2)}) collective-permute-start(bf16[1,256,512]{2,1,0:T(8,128)(2,1)S(1)} %slice.168.refs_7_), channel_id=1, source_target_pairs={{0,2},{1,3},{2,0},{3,1},{4,6},{5,7},{6,4},{7,5},{8,10},{9,11},{10,... | collective-permute-start | bytes 786440 | tf_op jit(solution)/shard_map/ppermute | solution.py:23
  68.5 7.5 %collective-permute-start.18 = (bf16[1,256,256]{2,1,0:T(8,128)(2,1)S(1)}, bf16[1,256,256]{2,1,0:T(8,128)(2,1)S(1)}, u32[]{:S(2)}, u32[]{:S(2)}) collective-permute-start(bf16[1,256,256]{2,1,0:T(8,128)(2,1)S(1)} %fusion.1.refs_0_), channel_id=1, source_target_pairs={{0,2},{1,3},{2,0},{3,1},{4,6},{5,7},{6,4},{7,5},{8,10},{9,11},{10,... | collective-permute-start | bytes 393224 | tf_op jit(solution)/shard_map/ppermute | solution.py:23
  76.0 1.6 %collective-permute-start.19 = (bf16[2,256,256]{2,1,0:T(8,128)(2,1)S(1)}, bf16[2,256,256]{2,1,0:T(8,128)(2,1)S(1)}, u32[]{:S(2)}, u32[]{:S(2)}) collective-permute-start(bf16[2,256,256]{2,1,0:T(8,128)(2,1)S(1)} %pad_maximum_fusion.4), channel_id=1, source_target_pairs={{0,1},{1,0},{2,3},{3,2},{4,5},{5,4},{6,7},{7,6},{8,9},{9,8},{10,11... | collective-permute-start | bytes 786440 | tf_op jit(solution)/shard_map/ppermute | solution.py:23
  76.3 6.0 %collective-permute-start.17 = (bf16[1,256,256]{2,1,0:T(8,128)(2,1)S(1)}, bf16[1,256,256]{2,1,0:T(8,128)(2,1)S(1)}, u32[]{:S(2)}, u32[]{:S(2)}) collective-permute-start(bf16[1,256,256]{2,1,0:T(8,128)(2,1)S(1)} %fusion.refs_8_.refs_0_), channel_id=1, source_target_pairs={{0,2},{1,3},{2,0},{3,1},{4,6},{5,7},{6,4},{7,5},{8,10},{9,11},{10,... | collective-permute-start | bytes 393224 | tf_op jit(solution)/shard_map/ppermute | solution.py:23
  82.3 1.6 %collective-permute-start.20 = (bf16[2,256,256]{2,1,0:T(8,128)(2,1)S(1)}, bf16[2,256,256]{2,1,0:T(8,128)(2,1)S(1)}, u32[]{:S(2)}, u32[]{:S(2)}) collective-permute-start(bf16[2,256,256]{2,1,0:T(8,128)(2,1)S(1)} %pad_maximum_fusion.5), channel_id=1, source_target_pairs={{0,1},{1,0},{2,3},{3,2},{4,5},{5,4},{6,7},{7,6},{8,9},{9,8},{10,11... | collective-permute-start | bytes 786440 | tf_op jit(solution)/shard_map/ppermute | solution.py:23
  86.1 6.0 %collective-permute-start.21 = (bf16[32,1536]{1,0:T(8,128)(2,1)S(1)}, bf16[32,1536]{1,0:T(8,128)(2,1)S(1)}, u32[]{:S(2)}, u32[]{:S(2)}) collective-permute-start(bf16[32,1536]{1,0:T(8,128)(2,1)S(1)} %get-tuple-element.78), channel_id=1, source_target_pairs={{0,12},{4,0},{8,4},{12,8},{1,13},{5,1},{9,5},{13,9},{2,14},{6,2},{... | collective-permute-start | bytes 294920 | tf_op jit(solution)/shard_map/ppermute | solution.py:390
  88.3 10.0 %collective-permute-start.23 = (bf16[32,1536]{1,0:T(8,128)(2,1)S(1)}, bf16[32,1536]{1,0:T(8,128)(2,1)S(1)}, u32[]{:S(2)}, u32[]{:S(2)}) collective-permute-start(bf16[32,1536]{1,0:T(8,128)(2,1)S(1)} %get-tuple-element.79), channel_id=1, source_target_pairs={{0,4},{4,8},{8,12},{12,0},{1,5},{5,9},{9,13},{13,1},{2,6},{6,10},{... | collective-permute-start | bytes 294920 | tf_op jit(solution)/shard_map/ppermute | solution.py:390
  88.3 9.6 %collective-permute-start.25 = (bf16[32,1536]{1,0:T(8,128)(2,1)S(1)}, bf16[32,1536]{1,0:T(8,128)(2,1)S(1)}, u32[]{:S(2)}, u32[]{:S(2)}) collective-permute-start(bf16[32,1536]{1,0:T(8,128)(2,1)S(1)} %get-tuple-element.82), channel_id=1, source_target_pairs={{0,4},{4,8},{8,12},{12,0},{1,5},{5,9},{9,13},{13,1},{2,6},{6,10},{... | collective-permute-start | bytes 294920 | tf_op jit(solution)/shard_map/ppermute | solution.py:390
  88.3 10.0 %collective-permute-start.24 = (bf16[32,1536]{1,0:T(8,128)(2,1)S(1)}, bf16[32,1536]{1,0:T(8,128)(2,1)S(1)}, u32[]{:S(2)}, u32[]{:S(2)}) collective-permute-start(bf16[32,1536]{1,0:T(8,128)(2,1)S(1)} %get-tuple-element.80), channel_id=1, source_target_pairs={{0,12},{4,0},{8,4},{12,8},{1,13},{5,1},{9,5},{13,9},{2,14},{6,2},{... | collective-permute-start | bytes 294920 | tf_op jit(solution)/shard_map/ppermute | solution.py:390
  92.2 7.8 %collective-permute-start.22 = (bf16[32,1536]{1,0:T(8,128)(2,1)S(1)}, bf16[32,1536]{1,0:T(8,128)(2,1)S(1)}, u32[]{:S(2)}, u32[]{:S(2)}) collective-permute-start(bf16[32,1536]{1,0:T(8,128)(2,1)S(1)} %add_convert_fusion.1), channel_id=1, source_target_pairs={{0,12},{4,0},{8,4},{12,8},{1,13},{5,1},{9,5},{13,9},{2,14},{6,2},{... | collective-permute-start | bytes 294920 | tf_op jit(solution)/shard_map/ppermute | solution.py:390
  98.0 6.5 %collective-permute-start.26 = (bf16[32,1536]{1,0:T(8,128)(2,1)S(1)}, bf16[32,1536]{1,0:T(8,128)(2,1)S(1)}, u32[]{:S(2)}, u32[]{:S(2)}) collective-permute-start(bf16[32,1536]{1,0:T(8,128)(2,1)S(1)} %add_convert_fusion), channel_id=1, source_target_pairs={{0,4},{4,8},{8,12},{12,0},{1,5},{5,9},{9,13},{13,1},{2,6},{6,10},{... | collective-permute-start | bytes 294920 | tf_op jit(solution)/shard_map/ppermute | solution.py:390

commit v17 on v13

--- a/solution.py
+++ b/solution.py
@@ -209,7 +209,7 @@
             r == rank[e : e + 1, :], wt[e : e + 1, :], 0.0
         ).astype(jnp.bfloat16)
     local = out.shape[1]
-    block = 512 if local % 512 == 0 else 256 if local % 256 == 0 else local
+    block = local // 2 if local % 512 == 0 else 256 if local % 256 == 0 else local
     for i in range(local // block):
         cols = slice(i * block, (i + 1) * block)
         for x in range(len(experts)):

time: 101 us -> 101 us (level)
  waiting for transfers between devices: 15.7 us -> 14.5 us
    ppermute x13, waiting for transfers between devices: 7.78 us -> 6.6 us  [flip(): lax.ppermute(x, axis, [(i, i ^ k) for i in range(lax.axis_size(axis))])]
  transfers between devices with their start and end apart: 26 -> 26, of which waited for: 9 -> 9; matrix products, arithmetic and copies ran while one was open for 2% -> 2% of each run, Pallas kernels for 44% -> 45%
where the time goes in v17:
time: 101 us
  Pallas kernels  52.2 us (52%)
  starting transfers between devices  29.9 us (30%)
  waiting for transfers between devices  14.5 us (14%)
  other arithmetic  3.68 us (4%)
    pallas_call x13, Pallas kernels, call(): pl.pallas_call(whole, out_shape=tuple(outs), in_specs=[SMEM] + [spec for...  51.5 us
    ppermute x6, starting transfers between devices, hop(): return lax.ppermute(total, axis, perm)  11.6 us
    ppermute x13, waiting for transfers between devices, flip(): lax.ppermute(x, axis, [(i, i ^ k) for i in range(lax.axis_size(axis))])  6.6 us
    ppermute x13, starting transfers between devices, flip(): lax.ppermute(x, axis, [(i, i ^ k) for i in range(lax.axis_size(axis))])  6.21 us
    ppermute x6, waiting for transfers between devices, hop(): return lax.ppermute(total, axis, perm)  4.24 us
    ppermute x3, starting transfers between devices, on_device(): lax.ppermute(meta, 'expert', [(i, (i - k) % n_owner) for i in range(n_own...  3.83 us
    ppermute x1, starting transfers between devices, gathered(): lax.ppermute(above[half:], axis, down_)  3.15 us
    ppermute x1, starting transfers between devices, gathered(): lax.ppermute(below, axis, up)  3.02 us
  transfers between devices with their start and end apart: 26, of which 9 were waited for; matrix products, arithmetic and copies ran while one was open for 2% of the time, Pallas kernels for 45%

profile of v17, /device:TPU:0, one launch (start us, length us, event | category | flops | bytes accessed | tf_op | source)
XLA Modules:
  0.0 101.0 jit_solution(14405118403868058419)
XLA Ops:
  0.0 3.0 %collective-permute-start = (bf16[64,1536]{1,0:T(8,128)(2,1)}, bf16[64,1536]{1,0:T(8,128)(2,1)S(1)}, u32[]{:S(2)}, u32[]{:S(2)}) collective-permute-start(bf16[64,1536]{1,0:T(8,128)(2,1)} %refs_0_.9), channel_id=1, source_target_pairs={{0,4},{4,8},{8,12},{12,0},{1,5},{5,9},{9,13},{13,1},{2,6},{6,10},{... | collective-permute-start | bytes 589832 | tf_op jit(solution)/shard_map/ppermute | solution.py:367
  3.0 2.0 %collective-permute-start.1 = (bf16[64,1536]{1,0:T(8,128)(2,1)}, bf16[64,1536]{1,0:T(8,128)(2,1)S(1)}, u32[]{:S(2)}, u32[]{:S(2)}) collective-permute-start(bf16[64,1536]{1,0:T(8,128)(2,1)} %refs_0_.9), channel_id=1, source_target_pairs={{0,12},{4,0},{8,4},{12,8},{1,13},{5,1},{9,5},{13,9},{2,14},{6,2},{... | collective-permute-start | bytes 589832 | tf_op jit(solution)/shard_map/ppermute | solution.py:367
  5.7 0.7 pad_maximum_fusion.8.refs_0_
  6.4 3.8 %collective-permute-start.5 = (f32[16,64]{1,0:T(8,128)S(1)}, f32[16,64]{1,0:T(8,128)S(1)}, u32[]{:S(2)}, u32[]{:S(2)}) collective-permute-start(f32[16,64]{1,0:T(8,128)S(1)} %pad_maximum_fusion.8.refs_0_), channel_id=1, source_target_pairs={{0,12},{4,0},{8,4},{12,8},{1,13},{5,1},{9,5},{13,9},{2,14},{6,2},{... | collective-permute-start | bytes 12296 | tf_op jit(solution)/shard_map/ppermute | solution.py:302
  10.3 0.8 collective-permute-done.refs_1_
  11.1 2.9 %collective-permute-done.1.refs_2_ = bf16[64,1536]{1,0:T(8,128)(2,1)S(1)} collective-permute-done((bf16[64,1536]{1,0:T(8,128)(2,1)}, bf16[64,1536]{1,0:T(8,128)(2,1)S(1)}, u32[]{:S(2)}, u32[]{:S(2)}) %collective-permute-start.1) | collective-permute-done | bytes 196640 | tf_op jit(solution)/shard_map/ppermute | solution.py:367
  14.0 3.2 %collective-permute-start.3 = (bf16[32,1536]{1,0:T(8,128)(2,1)S(1)}, bf16[32,1536]{1,0:T(8,128)(2,1)S(1)}, u32[]{:S(2)}, u32[]{:S(2)}) collective-permute-start(bf16[32,1536]{1,0:T(8,128)(2,1)S(1)} %slice.117), channel_id=1, source_target_pairs={{0,12},{4,0},{8,4},{12,8},{1,13},{5,1},{9,5},{13,9},{2,14},{6,2},{... | collective-permute-start | bytes 294920 | tf_op jit(solution)/shard_map/ppermute | solution.py:371
  17.2 3.4 %stage.1.refs_6_ = bf16[2,2,1536,512]{3,2,1,0:T(8,128)(2,1)S(1)} custom-call(s32[3]{0:T(128)S(1)} %pad_add_fusion.info, bf16[8,1536,1024]{2,1,0:T(8,128)(2,1)} %refs_7_.9, bf16[8,1536,1024]{2,1,0:T(8,128)(2,1)} %refs_8_.7), custom_call_target="tpu_custom_call" | custom-call | flops 1 | bytes 1 | tf_op jit(solution)/shard_map/stage/pallas_call | solution.py:113
  20.7 0.8 route.1
  21.4 4.5 %send_half.4 = (bf16[2,256,512]{2,1,0:T(8,128)(2,1)S(1)}, bf16[256,1536]{1,0:T(8,128)(2,1)S(1)}, bf16[2,2,1536,512]{3,2,1,0:T(8,128)(2,1)S(1)}) custom-call(s32[3]{0:T(128)S(1)} %pad_add_fusion.info, bf16[64,1536]{1,0:T(8,128)(2,1)S(1)} %copy-done, bf16[64,1536]{1,0:T(8,128)(2,1)S(1)} %collective-permute-done.refs_1_, ...), custom_call_target="tpu_custom_call" | custom-call | flops 1 | bytes 1 | tf_op jit(solution)/shard_map/send_half/pallas_call | solution.py:113
  26.0 4.2 %keep_half.4 = (bf16[2,256,512]{2,1,0:T(8,128)(2,1)S(1)}, bf16[2,2,1536,512]{3,2,1,0:T(8,128)(2,1)S(1)}) custom-call(s32[3]{0:T(128)S(1)} %pad_add_fusion.info, bf16[256,1536]{1,0:T(8,128)(2,1)S(1)} %get-tuple-element.43.refs_0_, bf16[2,2,1536,512]{3,2,1,0:T(8,128)(2,1)S(1)} %get-tuple-element.44.refs_1_, bf16[8,1536,1024]{2,1,0:T(8,128)(2,1)} %refs_7_.9, ...), custom_call_target="tpu_custom_call" | custom-call | flops 1 | bytes 1 | tf_op jit(solution)/shard_map/keep_half/pallas_call | solution.py:113
  30.4 1.6 %collective-permute-start.9 = (bf16[1,256,512]{2,1,0:T(8,128)(2,1)S(1)}, bf16[1,256,512]{2,1,0:T(8,128)(2,1)S(1)}, u32[]{:S(2)}, u32[]{:S(2)}) collective-permute-start(bf16[1,256,512]{2,1,0:T(8,128)(2,1)S(1)} %slice.181.refs_9_), channel_id=1, source_target_pairs={{0,2},{1,3},{2,0},{3,1},{4,6},{5,7},{6,4},{7,5},{8,10},{9,11},{10,... | collective-permute-start | bytes 786440 | tf_op jit(solution)/shard_map/ppermute | solution.py:23
  32.0 4.6 %send_half.5 = (bf16[2,256,512]{2,1,0:T(8,128)(2,1)S(1)}, bf16[256,1536]{1,0:T(8,128)(2,1)S(1)}, bf16[2,2,1536,512]{3,2,1,0:T(8,128)(2,1)S(1)}) custom-call(s32[3]{0:T(128)S(1)} %pad_add_fusion.info, bf16[64,1536]{1,0:T(8,128)(2,1)S(1)} %copy-done, bf16[64,1536]{1,0:T(8,128)(2,1)S(1)} %collective-permute-done.refs_1_, ...), custom_call_target="tpu_custom_call" | custom-call | flops 1 | bytes 1 | tf_op jit(solution)/shard_map/send_half/pallas_call | solution.py:113
  36.9 4.2 %keep_half.5 = (bf16[2,256,512]{2,1,0:T(8,128)(2,1)S(1)}, bf16[2,2,1536,512]{3,2,1,0:T(8,128)(2,1)S(1)}) custom-call(s32[3]{0:T(128)S(1)} %pad_add_fusion.info, bf16[256,1536]{1,0:T(8,128)(2,1)S(1)} %get-tuple-element.48.refs_0_, bf16[2,2,1536,512]{3,2,1,0:T(8,128)(2,1)S(1)} %get-tuple-element.49.refs_1_, bf16[8,1536,1024]{2,1,0:T(8,128)(2,1)} %refs_7_.9, ...), custom_call_target="tpu_custom_call" | custom-call | flops 1 | bytes 1 | tf_op jit(solution)/shard_map/keep_half/pallas_call | solution.py:113
  42.1 4.5 %send_half.6 = (bf16[2,256,512]{2,1,0:T(8,128)(2,1)S(1)}, bf16[256,1536]{1,0:T(8,128)(2,1)S(1)}, bf16[2,2,1536,512]{3,2,1,0:T(8,128)(2,1)S(1)}) custom-call(s32[3]{0:T(128)S(1)} %pad_add_fusion.info, bf16[64,1536]{1,0:T(8,128)(2,1)S(1)} %copy-done, bf16[64,1536]{1,0:T(8,128)(2,1)S(1)} %collective-permute-done.refs_1_, ...), custom_call_target="tpu_custom_call" | custom-call | flops 1 | bytes 1 | tf_op jit(solution)/shard_map/send_half/pallas_call | solution.py:113
  46.7 4.2 %keep_half.6 = (bf16[2,256,512]{2,1,0:T(8,128)(2,1)S(1)}, bf16[2,2,1536,512]{3,2,1,0:T(8,128)(2,1)S(1)}) custom-call(s32[3]{0:T(128)S(1)} %pad_add_fusion.info, bf16[256,1536]{1,0:T(8,128)(2,1)S(1)} %get-tuple-element.53.refs_0_, bf16[2,2,1536,512]{3,2,1,0:T(8,128)(2,1)S(1)} %get-tuple-element.54.refs_1_, bf16[8,1536,1024]{2,1,0:T(8,128)(2,1)} %refs_7_.9, ...), custom_call_target="tpu_custom_call" | custom-call | flops 1 | bytes 1 | tf_op jit(solution)/shard_map/keep_half/pallas_call | solution.py:113
  50.9 2.0 %collective-permute-done.11.refs_1_ = bf16[1,256,768]{2,1,0:T(8,128)(2,1)S(1)} collective-permute-done((bf16[1,256,768]{2,1,0:T(8,128)(2,1)S(1)}, bf16[1,256,768]{2,1,0:T(8,128)(2,1)S(1)}, u32[]{:S(2)}, u32[]{:S(2)}) %collective-permute-start.11) | collective-permute-done | bytes 393248 | tf_op jit(solution)/shard_map/ppermute | solution.py:23
  53.9 4.6 %send_half.7 = (bf16[2,256,512]{2,1,0:T(8,128)(2,1)S(1)}, bf16[256,1536]{1,0:T(8,128)(2,1)S(1)}, bf16[2,2,1536,512]{3,2,1,0:T(8,128)(2,1)S(1)}) custom-call(s32[3]{0:T(128)S(1)} %pad_add_fusion.info, bf16[64,1536]{1,0:T(8,128)(2,1)S(1)} %copy-done, bf16[64,1536]{1,0:T(8,128)(2,1)S(1)} %collective-permute-done.refs_1_, ...), custom_call_target="tpu_custom_call" | custom-call | flops 1 | bytes 1 | tf_op jit(solution)/shard_map/send_half/pallas_call | solution.py:113
  58.7 3.6 %keep_half.7 = (bf16[2,256,512]{2,1,0:T(8,128)(2,1)S(1)}, bf16[2,1024,1536]{2,1,0:T(8,128)(2,1)S(1)}) custom-call(s32[3]{0:T(128)S(1)} %pad_add_fusion.info, bf16[256,1536]{1,0:T(8,128)(2,1)S(1)} %get-tuple-element.58.refs_0_, bf16[2,2,1536,512]{3,2,1,0:T(8,128)(2,1)S(1)} %get-tuple-element.59.refs_1_, bf16[8,1024,1536]{2,1,0:T(8,128)(2,1)} %refs_7_.11), custom_call_target="tpu_custom_call" | custom-call | flops 1 | bytes 1 | tf_op jit(solution)/shard_map/keep_half/pallas_call | solution.py:113
  62.3 1.6 %collective-permute-done.13.refs_1_ = bf16[1,256,768]{2,1,0:T(8,128)(2,1)S(1)} collective-permute-done((bf16[1,256,768]{2,1,0:T(8,128)(2,1)S(1)}, bf16[1,256,768]{2,1,0:T(8,128)(2,1)S(1)}, u32[]{:S(2)}, u32[]{:S(2)}) %collective-permute-start.13) | collective-permute-done | bytes 393248 | tf_op jit(solution)/shard_map/ppermute | solution.py:23
  65.6 0.9 collective-permute-done.16.refs_2_
  66.5 3.8 %down.4 = (f32[256,1536]{1,0:T(8,128)S(1)}, bf16[2,1024,1536]{2,1,0:T(8,128)(2,1)S(1)}) custom-call(s32[3]{0:T(128)S(1)} %pad_add_fusion.info, bf16[1,256,256]{2,1,0:T(8,128)(2,1)S(1)} %fusion.3.refs_0_, bf16[1,256,768]{2,1,0:T(8,128)(2,1)S(1)} %copy-done.2, bf16[2,256,256]{2,1,0:T(8,128)(2,1)S(1)} %collective-permute-done.16.refs_2_, ...), custom_call_target="tpu_custom_call" | custom-call | flops 1 | bytes 1 | tf_op jit(solution)/shard_map/down/pallas_call | solution.py:113
  70.3 3.9 %down.5 = (f32[256,1536]{1,0:T(8,128)S(1)}, bf16[2,1024,1536]{2,1,0:T(8,128)(2,1)S(1)}) custom-call(s32[3]{0:T(128)S(1)} %pad_add_fusion.info, bf16[1,256,256]{2,1,0:T(8,128)(2,1)S(1)} %fusion.2.refs_0_, bf16[1,256,768]{2,1,0:T(8,128)(2,1)S(1)} %collective-permute-done.13.refs_1_, bf16[2,256,256]{2,1,0:T(8,128)(2,1)S(1)} %collective-permute-done.15.refs_2_, ...), custom_call_target="tpu_custom_call" | custom-call | flops 1 | bytes 1 | tf_op jit(solution)/shard_map/down/pallas_call | solution.py:113
  74.7 1.6 %collective-permute-start.17 = (bf16[1,256,256]{2,1,0:T(8,128)(2,1)S(1)}, bf16[1,256,256]{2,1,0:T(8,128)(2,1)S(1)}, u32[]{:S(2)}, u32[]{:S(2)}) collective-permute-start(bf16[1,256,256]{2,1,0:T(8,128)(2,1)S(1)} %fusion.refs_8_.refs_0_), channel_id=1, source_target_pairs={{0,2},{1,3},{2,0},{3,1},{4,6},{5,7},{6,4},{7,5},{8,10},{9,11},{10,... | collective-permute-start | bytes 393224 | tf_op jit(solution)/shard_map/ppermute | solution.py:23
  76.2 3.9 %down.6 = (f32[256,1536]{1,0:T(8,128)S(1)}, bf16[2,1024,1536]{2,1,0:T(8,128)(2,1)S(1)}) custom-call(s32[3]{0:T(128)S(1)} %pad_add_fusion.info, bf16[1,256,256]{2,1,0:T(8,128)(2,1)S(1)} %fusion.1.refs_0_, bf16[1,256,768]{2,1,0:T(8,128)(2,1)S(1)} %collective-permute-done.14.refs_1_, bf16[2,256,256]{2,1,0:T(8,128)(2,1)S(1)} %collective-permute-done.18.refs_2_, ...), custom_call_target="tpu_custom_call" | custom-call | flops 1 | bytes 1 | tf_op jit(solution)/shard_map/down/pallas_call | solution.py:113
  80.7 1.5 %collective-permute-done.19.refs_2_ = bf16[2,256,256]{2,1,0:T(8,128)(2,1)S(1)} collective-permute-done((bf16[2,256,256]{2,1,0:T(8,128)(2,1)S(1)}, bf16[2,256,256]{2,1,0:T(8,128)(2,1)S(1)}, u32[]{:S(2)}, u32[]{:S(2)}) %collective-permute-start.19) | collective-permute-done | bytes 262176 | tf_op jit(solution)/shard_map/ppermute | solution.py:23
  82.2 2.0 %down.7 = (bf16[64,1536]{1,0:T(8,128)(2,1)S(1)}, bf16[32,1536]{1,0:T(8,128)(2,1)S(1)}, bf16[32,1536]{1,0:T(8,128)(2,1)S(1)}, bf16[32,1536]{1,0:T(8,128)(2,1)S(1)...) custom-call(s32[3]{0:T(128)S(1)} %pad_add_fusion.info, ...), custom_call_target="tpu_custom_call" | custom-call | flops 1 | bytes 1 | tf_op jit(solution)/shard_map/down/pallas_call | solution.py:113
  84.3 3.8 %collective-permute-start.20 = (bf16[32,1536]{1,0:T(8,128)(2,1)S(1)}, bf16[32,1536]{1,0:T(8,128)(2,1)S(1)}, u32[]{:S(2)}, u32[]{:S(2)}) collective-permute-start(bf16[32,1536]{1,0:T(8,128)(2,1)S(1)} %get-tuple-element.74), channel_id=1, source_target_pairs={{0,12},{4,0},{8,4},{12,8},{1,13},{5,1},{9,5},{13,9},{2,14},{6,2},{... | collective-permute-start | bytes 294920 | tf_op jit(solution)/shard_map/ppermute | solution.py:386
  88.2 3.8 %collective-permute-start.23 = (bf16[32,1536]{1,0:T(8,128)(2,1)S(1)}, bf16[32,1536]{1,0:T(8,128)(2,1)S(1)}, u32[]{:S(2)}, u32[]{:S(2)}) collective-permute-start(bf16[32,1536]{1,0:T(8,128)(2,1)S(1)} %get-tuple-element.76), channel_id=1, source_target_pairs={{0,12},{4,0},{8,4},{12,8},{1,13},{5,1},{9,5},{13,9},{2,14},{6,2},{... | collective-permute-start | bytes 294920 | tf_op jit(solution)/shard_map/ppermute | solution.py:386
  92.1 3.9 %collective-permute-start.21 = (bf16[32,1536]{1,0:T(8,128)(2,1)S(1)}, bf16[32,1536]{1,0:T(8,128)(2,1)S(1)}, u32[]{:S(2)}, u32[]{:S(2)}) collective-permute-start(bf16[32,1536]{1,0:T(8,128)(2,1)S(1)} %add_convert_fusion.1), channel_id=1, source_target_pairs={{0,12},{4,0},{8,4},{12,8},{1,13},{5,1},{9,5},{13,9},{2,14},{6,2},{... | collective-permute-start | bytes 294920 | tf_op jit(solution)/shard_map/ppermute | solution.py:386
  96.0 4.2 %collective-permute-done.25 = bf16[32,1536]{1,0:T(8,128)(2,1)S(1)} collective-permute-done((bf16[32,1536]{1,0:T(8,128)(2,1)S(1)}, bf16[32,1536]{1,0:T(8,128)(2,1)S(1)}, u32[]{:S(2)}, u32[]{:S(2)}) %collective-permute-start.25) | collective-permute-done | bytes 98336 | tf_op jit(solution)/shard_map/ppermute | solution.py:386
  100.3 0.7 pad_maximum_fusion.7
  (78 shorter events, 6.5 us)
Async XLA Ops:
  0.0 11.0 %collective-permute-start = (bf16[64,1536]{1,0:T(8,128)(2,1)}, bf16[64,1536]{1,0:T(8,128)(2,1)S(1)}, u32[]{:S(2)}, u32[]{:S(2)}) collective-permute-start(bf16[64,1536]{1,0:T(8,128)(2,1)} %refs_0_.9), channel_id=1, source_target_pairs={{0,4},{4,8},{8,12},{12,0},{1,5},{5,9},{9,13},{13,1},{2,6},{6,10},{... | collective-permute-start | bytes 589832 | tf_op jit(solution)/shard_map/ppermute | solution.py:367
  3.0 11.0 %collective-permute-start.1 = (bf16[64,1536]{1,0:T(8,128)(2,1)}, bf16[64,1536]{1,0:T(8,128)(2,1)S(1)}, u32[]{:S(2)}, u32[]{:S(2)}) collective-permute-start(bf16[64,1536]{1,0:T(8,128)(2,1)} %refs_0_.9), channel_id=1, source_target_pairs={{0,12},{4,0},{8,4},{12,8},{1,13},{5,1},{9,5},{13,9},{2,14},{6,2},{... | collective-permute-start | bytes 589832 | tf_op jit(solution)/shard_map/ppermute | solution.py:367
  6.4 14.2 %collective-permute-start.4 = (f32[16,64]{1,0:T(8,128)S(1)}, f32[16,64]{1,0:T(8,128)S(1)}, u32[]{:S(2)}, u32[]{:S(2)}) collective-permute-start(f32[16,64]{1,0:T(8,128)S(1)} %pad_maximum_fusion.8.refs_0_), channel_id=1, source_target_pairs={{0,4},{4,8},{8,12},{12,0},{1,5},{5,9},{9,13},{13,1},{2,6},{6,10},{... | collective-permute-start | bytes 12296 | tf_op jit(solution)/shard_map/ppermute | solution.py:302
  6.4 14.2 %collective-permute-start.5 = (f32[16,64]{1,0:T(8,128)S(1)}, f32[16,64]{1,0:T(8,128)S(1)}, u32[]{:S(2)}, u32[]{:S(2)}) collective-permute-start(f32[16,64]{1,0:T(8,128)S(1)} %pad_maximum_fusion.8.refs_0_), channel_id=1, source_target_pairs={{0,12},{4,0},{8,4},{12,8},{1,13},{5,1},{9,5},{13,9},{2,14},{6,2},{... | collective-permute-start | bytes 12296 | tf_op jit(solution)/shard_map/ppermute | solution.py:302
  10.3 10.4 %collective-permute-start.6 = (f32[16,64]{1,0:T(8,128)S(1)}, f32[16,64]{1,0:T(8,128)S(1)}, u32[]{:S(2)}, u32[]{:S(2)}) collective-permute-start(f32[16,64]{1,0:T(8,128)S(1)} %pad_maximum_fusion.8.refs_0_), channel_id=1, source_target_pairs={{0,8},{4,12},{8,0},{12,4},{1,9},{5,13},{9,1},{13,5},{2,10},{6,14},... | collective-permute-start | bytes 12296 | tf_op jit(solution)/shard_map/ppermute | solution.py:302
  11.0 10.4 %collective-permute-start.2 = (bf16[32,1536]{1,0:T(8,128)(2,1)S(1)}, bf16[32,1536]{1,0:T(8,128)(2,1)S(1)}, u32[]{:S(2)}, u32[]{:S(2)}) collective-permute-start(bf16[32,1536]{1,0:T(8,128)(2,1)S(1)} %slice.116), channel_id=1, source_target_pairs={{0,4},{4,8},{8,12},{12,0},{1,5},{5,9},{9,13},{13,1},{2,6},{6,10},{... | collective-permute-start | bytes 294920 | tf_op jit(solution)/shard_map/ppermute | solution.py:371
  14.0 7.4 %collective-permute-start.3 = (bf16[32,1536]{1,0:T(8,128)(2,1)S(1)}, bf16[32,1536]{1,0:T(8,128)(2,1)S(1)}, u32[]{:S(2)}, u32[]{:S(2)}) collective-permute-start(bf16[32,1536]{1,0:T(8,128)(2,1)S(1)} %slice.117), channel_id=1, source_target_pairs={{0,12},{4,0},{8,4},{12,8},{1,13},{5,1},{9,5},{13,9},{2,14},{6,2},{... | collective-permute-start | bytes 294920 | tf_op jit(solution)/shard_map/ppermute | solution.py:371
  17.2 4.2 %copy-start = (bf16[64,1536]{1,0:T(8,128)(2,1)S(1)}, bf16[64,1536]{1,0:T(8,128)(2,1)}, u32[]{:S(2)}) copy-start(bf16[64,1536]{1,0:T(8,128)(2,1)} %refs_0_.9) | copy-start | bytes 589828
  25.9 4.3 %collective-permute-start.7 = (bf16[2,256,512]{2,1,0:T(8,128)(2,1)S(1)}, bf16[2,256,512]{2,1,0:T(8,128)(2,1)S(1)}, u32[]{:S(2)}, u32[]{:S(2)}) collective-permute-start(bf16[2,256,512]{2,1,0:T(8,128)(2,1)S(1)} %get-tuple-element.47), channel_id=1, source_target_pairs={{0,1},{1,0},{2,3},{3,2},{4,5},{5,4},{6,7},{7,6},{8,9},{9,8},{10,11... | collective-permute-start | bytes 1572872 | tf_op jit(solution)/shard_map/ppermute | solution.py:23
  30.4 10.7 %collective-permute-start.9 = (bf16[1,256,512]{2,1,0:T(8,128)(2,1)S(1)}, bf16[1,256,512]{2,1,0:T(8,128)(2,1)S(1)}, u32[]{:S(2)}, u32[]{:S(2)}) collective-permute-start(bf16[1,256,512]{2,1,0:T(8,128)(2,1)S(1)} %slice.181.refs_9_), channel_id=1, source_target_pairs={{0,2},{1,3},{2,0},{3,1},{4,6},{5,7},{6,4},{7,5},{8,10},{9,11},{10,... | collective-permute-start | bytes 786440 | tf_op jit(solution)/shard_map/ppermute | solution.py:23
  36.6 4.7 %collective-permute-start.8 = (bf16[2,256,512]{2,1,0:T(8,128)(2,1)S(1)}, bf16[2,256,512]{2,1,0:T(8,128)(2,1)S(1)}, u32[]{:S(2)}, u32[]{:S(2)}) collective-permute-start(bf16[2,256,512]{2,1,0:T(8,128)(2,1)S(1)} %get-tuple-element.52), channel_id=1, source_target_pairs={{0,1},{1,0},{2,3},{3,2},{4,5},{5,4},{6,7},{7,6},{8,9},{9,8},{10,11... | collective-permute-start | bytes 1572872 | tf_op jit(solution)/shard_map/ppermute | solution.py:23
  41.5 11.4 %collective-permute-start.11 = (bf16[1,256,768]{2,1,0:T(8,128)(2,1)S(1)}, bf16[1,256,768]{2,1,0:T(8,128)(2,1)S(1)}, u32[]{:S(2)}, u32[]{:S(2)}) collective-permute-start(bf16[1,256,768]{2,1,0:T(8,128)(2,1)S(1)} %pad_maximum_fusion.refs_9_), channel_id=1, source_target_pairs={{0,2},{1,3},{2,0},{3,1},{4,6},{5,7},{6,4},{7,5},{8,10},{9,11},{10,... | collective-permute-start | bytes 1179656 | tf_op jit(solution)/shard_map/ppermute | solution.py:23
  46.6 6.5 %collective-permute-start.10 = (bf16[2,256,512]{2,1,0:T(8,128)(2,1)S(1)}, bf16[2,256,512]{2,1,0:T(8,128)(2,1)S(1)}, u32[]{:S(2)}, u32[]{:S(2)}) collective-permute-start(bf16[2,256,512]{2,1,0:T(8,128)(2,1)S(1)} %get-tuple-element.57), channel_id=1, source_target_pairs={{0,1},{1,0},{2,3},{3,2},{4,5},{5,4},{6,7},{7,6},{8,9},{9,8},{10,11... | collective-permute-start | bytes 1572872 | tf_op jit(solution)/shard_map/ppermute | solution.py:23
  52.9 5.7 %copy-start.1 = (bf16[1,256,768]{2,1,0:T(8,128)(2,1)}, bf16[1,256,768]{2,1,0:T(8,128)(2,1)S(1)}, u32[]{:S(2)}) copy-start(bf16[1,256,768]{2,1,0:T(8,128)(2,1)S(1)} %collective-permute-done.11.refs_1_) | copy-start | bytes 1179652
  53.3 10.6 %collective-permute-start.13 = (bf16[1,256,768]{2,1,0:T(8,128)(2,1)S(1)}, bf16[1,256,768]{2,1,0:T(8,128)(2,1)S(1)}, u32[]{:S(2)}, u32[]{:S(2)}) collective-permute-start(bf16[1,256,768]{2,1,0:T(8,128)(2,1)S(1)} %pad_maximum_fusion.1.refs_9_), channel_id=1, source_target_pairs={{0,2},{1,3},{2,0},{3,1},{4,6},{5,7},{6,4},{7,5},{8,10},{9,11},{10,... | collective-permute-start | bytes 1179656 | tf_op jit(solution)/shard_map/ppermute | solution.py:23
  58.6 5.5 %collective-permute-start.12 = (bf16[2,256,512]{2,1,0:T(8,128)(2,1)S(1)}, bf16[2,256,512]{2,1,0:T(8,128)(2,1)S(1)}, u32[]{:S(2)}, u32[]{:S(2)}) collective-permute-start(bf16[2,256,512]{2,1,0:T(8,128)(2,1)S(1)} %get-tuple-element.61), channel_id=1, source_target_pairs={{0,1},{1,0},{2,3},{3,2},{4,5},{5,4},{6,7},{7,6},{8,9},{9,8},{10,11... | collective-permute-start | bytes 1572872 | tf_op jit(solution)/shard_map/ppermute | solution.py:23
  58.7 6.2 %slice-start = ((bf16[1,256,768]{2,1,0:T(8,128)(2,1)}), bf16[1,256,256]{2,1,0:T(8,128)(2,1)S(1)}, s32[]{:S(2)}) async-start(bf16[1,256,768]{2,1,0:T(8,128)(2,1)} %copy-done.1), calls=%async_computation | async-start | bytes 262144 | tf_op jit(solution)/shard_map/slice | solution.py:267
  62.3 4.2 %copy-start.2 = (bf16[1,256,768]{2,1,0:T(8,128)(2,1)S(1)}, bf16[1,256,768]{2,1,0:T(8,128)(2,1)}, u32[]{:S(2)}) copy-start(bf16[1,256,768]{2,1,0:T(8,128)(2,1)} %copy-done.1) | copy-start | bytes 1179652
  64.3 10.0 %collective-permute-start.14 = (bf16[1,256,768]{2,1,0:T(8,128)(2,1)S(1)}, bf16[1,256,768]{2,1,0:T(8,128)(2,1)S(1)}, u32[]{:S(2)}, u32[]{:S(2)}) collective-permute-start(bf16[1,256,768]{2,1,0:T(8,128)(2,1)S(1)} %pad_maximum_fusion.2.refs_7_), channel_id=1, source_target_pairs={{0,2},{1,3},{2,0},{3,1},{4,6},{5,7},{6,4},{7,5},{8,10},{9,11},{10,... | collective-permute-start | bytes 1179656 | tf_op jit(solution)/shard_map/ppermute | solution.py:23
  64.9 1.6 %collective-permute-start.16 = (bf16[2,256,256]{2,1,0:T(8,128)(2,1)S(1)}, bf16[2,256,256]{2,1,0:T(8,128)(2,1)S(1)}, u32[]{:S(2)}, u32[]{:S(2)}) collective-permute-start(bf16[2,256,256]{2,1,0:T(8,128)(2,1)S(1)} %pad_maximum_fusion.4), channel_id=1, source_target_pairs={{0,1},{1,0},{2,3},{3,2},{4,5},{5,4},{6,7},{7,6},{8,9},{9,8},{10,11... | collective-permute-start | bytes 786440 | tf_op jit(solution)/shard_map/ppermute | solution.py:23
  65.1 5.3 %collective-permute-start.15 = (bf16[2,256,256]{2,1,0:T(8,128)(2,1)S(1)}, bf16[2,256,256]{2,1,0:T(8,128)(2,1)S(1)}, u32[]{:S(2)}, u32[]{:S(2)}) collective-permute-start(bf16[2,256,256]{2,1,0:T(8,128)(2,1)S(1)} %pad_maximum_fusion.3), channel_id=1, source_target_pairs={{0,1},{1,0},{2,3},{3,2},{4,5},{5,4},{6,7},{7,6},{8,9},{9,8},{10,11... | collective-permute-start | bytes 786440 | tf_op jit(solution)/shard_map/ppermute | solution.py:23
  74.4 1.9 %collective-permute-start.18 = (bf16[2,256,256]{2,1,0:T(8,128)(2,1)S(1)}, bf16[2,256,256]{2,1,0:T(8,128)(2,1)S(1)}, u32[]{:S(2)}, u32[]{:S(2)}) collective-permute-start(bf16[2,256,256]{2,1,0:T(8,128)(2,1)S(1)} %pad_maximum_fusion.5), channel_id=1, source_target_pairs={{0,1},{1,0},{2,3},{3,2},{4,5},{5,4},{6,7},{7,6},{8,9},{9,8},{10,11... | collective-permute-start | bytes 786440 | tf_op jit(solution)/shard_map/ppermute | solution.py:23
  74.7 5.9 %collective-permute-start.17 = (bf16[1,256,256]{2,1,0:T(8,128)(2,1)S(1)}, bf16[1,256,256]{2,1,0:T(8,128)(2,1)S(1)}, u32[]{:S(2)}, u32[]{:S(2)}) collective-permute-start(bf16[1,256,256]{2,1,0:T(8,128)(2,1)S(1)} %fusion.refs_8_.refs_0_), channel_id=1, source_target_pairs={{0,2},{1,3},{2,0},{3,1},{4,6},{5,7},{6,4},{7,5},{8,10},{9,11},{10,... | collective-permute-start | bytes 393224 | tf_op jit(solution)/shard_map/ppermute | solution.py:23
  80.6 1.6 %collective-permute-start.19 = (bf16[2,256,256]{2,1,0:T(8,128)(2,1)S(1)}, bf16[2,256,256]{2,1,0:T(8,128)(2,1)S(1)}, u32[]{:S(2)}, u32[]{:S(2)}) collective-permute-start(bf16[2,256,256]{2,1,0:T(8,128)(2,1)S(1)} %pad_maximum_fusion.6), channel_id=1, source_target_pairs={{0,1},{1,0},{2,3},{3,2},{4,5},{5,4},{6,7},{7,6},{8,9},{9,8},{10,11... | collective-permute-start | bytes 786440 | tf_op jit(solution)/shard_map/ppermute | solution.py:23
  84.3 7.7 %collective-permute-start.24 = (bf16[32,1536]{1,0:T(8,128)(2,1)S(1)}, bf16[32,1536]{1,0:T(8,128)(2,1)S(1)}, u32[]{:S(2)}, u32[]{:S(2)}) collective-permute-start(bf16[32,1536]{1,0:T(8,128)(2,1)S(1)} %get-tuple-element.78), channel_id=1, source_target_pairs={{0,4},{4,8},{8,12},{12,0},{1,5},{5,9},{9,13},{13,1},{2,6},{6,10},{... | collective-permute-start | bytes 294920 | tf_op jit(solution)/shard_map/ppermute | solution.py:386
  84.3 7.7 %collective-permute-start.20 = (bf16[32,1536]{1,0:T(8,128)(2,1)S(1)}, bf16[32,1536]{1,0:T(8,128)(2,1)S(1)}, u32[]{:S(2)}, u32[]{:S(2)}) collective-permute-start(bf16[32,1536]{1,0:T(8,128)(2,1)S(1)} %get-tuple-element.74), channel_id=1, source_target_pairs={{0,12},{4,0},{8,4},{12,8},{1,13},{5,1},{9,5},{13,9},{2,14},{6,2},{... | collective-permute-start | bytes 294920 | tf_op jit(solution)/shard_map/ppermute | solution.py:386
  88.2 7.9 %collective-permute-start.22 = (bf16[32,1536]{1,0:T(8,128)(2,1)S(1)}, bf16[32,1536]{1,0:T(8,128)(2,1)S(1)}, u32[]{:S(2)}, u32[]{:S(2)}) collective-permute-start(bf16[32,1536]{1,0:T(8,128)(2,1)S(1)} %get-tuple-element.75), channel_id=1, source_target_pairs={{0,4},{4,8},{8,12},{12,0},{1,5},{5,9},{9,13},{13,1},{2,6},{6,10},{... | collective-permute-start | bytes 294920 | tf_op jit(solution)/shard_map/ppermute | solution.py:386
  88.2 7.9 %collective-permute-start.23 = (bf16[32,1536]{1,0:T(8,128)(2,1)S(1)}, bf16[32,1536]{1,0:T(8,128)(2,1)S(1)}, u32[]{:S(2)}, u32[]{:S(2)}) collective-permute-start(bf16[32,1536]{1,0:T(8,128)(2,1)S(1)} %get-tuple-element.76), channel_id=1, source_target_pairs={{0,12},{4,0},{8,4},{12,8},{1,13},{5,1},{9,5},{13,9},{2,14},{6,2},{... | collective-permute-start | bytes 294920 | tf_op jit(solution)/shard_map/ppermute | solution.py:386
  92.0 8.2 %collective-permute-start.25 = (bf16[32,1536]{1,0:T(8,128)(2,1)S(1)}, bf16[32,1536]{1,0:T(8,128)(2,1)S(1)}, u32[]{:S(2)}, u32[]{:S(2)}) collective-permute-start(bf16[32,1536]{1,0:T(8,128)(2,1)S(1)} %add_convert_fusion), channel_id=1, source_target_pairs={{0,4},{4,8},{8,12},{12,0},{1,5},{5,9},{9,13},{13,1},{2,6},{6,10},{... | collective-permute-start | bytes 294920 | tf_op jit(solution)/shard_map/ppermute | solution.py:386
  92.1 8.1 %collective-permute-start.21 = (bf16[32,1536]{1,0:T(8,128)(2,1)S(1)}, bf16[32,1536]{1,0:T(8,128)(2,1)S(1)}, u32[]{:S(2)}, u32[]{:S(2)}) collective-permute-start(bf16[32,1536]{1,0:T(8,128)(2,1)S(1)} %add_convert_fusion.1), channel_id=1, source_target_pairs={{0,12},{4,0},{8,4},{12,8},{1,13},{5,1},{9,5},{13,9},{2,14},{6,2},{... | collective-permute-start | bytes 294920 | tf_op jit(solution)/shard_map/ppermute | solution.py:386

commit v18 on v17

--- a/solution.py
+++ b/solution.py
@@ -209,7 +209,7 @@
             r == rank[e : e + 1, :], wt[e : e + 1, :], 0.0
         ).astype(jnp.bfloat16)
     local = out.shape[1]
-    block = local // 2 if local % 512 == 0 else 256 if local % 256 == 0 else local
+    block = local
     for i in range(local // block):
         cols = slice(i * block, (i + 1) * block)
         for x in range(len(experts)):

time: 101 us -> 101 us (level)
  Pallas kernels: 52.2 us -> 51 us
    pallas_call x13, Pallas kernels: 51.5 us -> 50.2 us  [call(): pl.pallas_call(whole, out_shape=tuple(outs), in_specs=[SMEM] + [spec for...]
  transfers between devices with their start and end apart: 26 -> 26, of which waited for: 9 -> 9; matrix products, arithmetic and copies ran while one was open for 2% -> 2% of each run, Pallas kernels for 45% -> 44%
where the time goes in v18:
time: 101 us
  Pallas kernels  51 us (50%)
  starting transfers between devices  29.9 us (30%)
  waiting for transfers between devices  15.5 us (15%)
  other arithmetic  3.68 us (4%)
    pallas_call x13, Pallas kernels, call(): pl.pallas_call(whole, out_shape=tuple(outs), in_specs=[SMEM] + [spec for...  50.2 us
    ppermute x6, starting transfers between devices, hop(): return lax.ppermute(total, axis, perm)  11.6 us
    ppermute x13, waiting for transfers between devices, flip(): lax.ppermute(x, axis, [(i, i ^ k) for i in range(lax.axis_size(axis))])  7.61 us
    ppermute x13, starting transfers between devices, flip(): lax.ppermute(x, axis, [(i, i ^ k) for i in range(lax.axis_size(axis))])  6.17 us
    ppermute x6, waiting for transfers between devices, hop(): return lax.ppermute(total, axis, perm)  4.24 us
    ppermute x3, starting transfers between devices, on_device(): lax.ppermute(meta, 'expert', [(i, (i - k) % n_owner) for i in range(n_own...  3.83 us
    ppermute x1, starting transfers between devices, gathered(): lax.ppermute(above[half:], axis, down_)  3.15 us
    ppermute x1, starting transfers between devices, gathered(): lax.ppermute(below, axis, up)  3.02 us
  transfers between devices with their start and end apart: 26, of which 9 were waited for; matrix products, arithmetic and copies ran while one was open for 2% of the time, Pallas kernels for 44%

profile of v18, /device:TPU:0, one launch (start us, length us, event | category | flops | bytes accessed | tf_op | source)
XLA Modules:
  0.0 100.8 jit_solution(4502035284230386340)
XLA Ops:
  0.0 3.0 %collective-permute-start = (bf16[64,1536]{1,0:T(8,128)(2,1)}, bf16[64,1536]{1,0:T(8,128)(2,1)S(1)}, u32[]{:S(2)}, u32[]{:S(2)}) collective-permute-start(bf16[64,1536]{1,0:T(8,128)(2,1)} %refs_0_.9), channel_id=1, source_target_pairs={{0,4},{4,8},{8,12},{12,0},{1,5},{5,9},{9,13},{13,1},{2,6},{6,10},{... | collective-permute-start | bytes 589832 | tf_op jit(solution)/shard_map/ppermute | solution.py:367
  3.0 2.0 %collective-permute-start.1 = (bf16[64,1536]{1,0:T(8,128)(2,1)}, bf16[64,1536]{1,0:T(8,128)(2,1)S(1)}, u32[]{:S(2)}, u32[]{:S(2)}) collective-permute-start(bf16[64,1536]{1,0:T(8,128)(2,1)} %refs_0_.9), channel_id=1, source_target_pairs={{0,12},{4,0},{8,4},{12,8},{1,13},{5,1},{9,5},{13,9},{2,14},{6,2},{... | collective-permute-start | bytes 589832 | tf_op jit(solution)/shard_map/ppermute | solution.py:367
  6.4 3.8 %collective-permute-start.5 = (f32[16,64]{1,0:T(8,128)S(1)}, f32[16,64]{1,0:T(8,128)S(1)}, u32[]{:S(2)}, u32[]{:S(2)}) collective-permute-start(f32[16,64]{1,0:T(8,128)S(1)} %pad_maximum_fusion.8.refs_0_), channel_id=1, source_target_pairs={{0,12},{4,0},{8,4},{12,8},{1,13},{5,1},{9,5},{13,9},{2,14},{6,2},{... | collective-permute-start | bytes 12296 | tf_op jit(solution)/shard_map/ppermute | solution.py:302
  10.3 0.8 collective-permute-done.refs_1_
  11.1 2.9 %collective-permute-done.1.refs_2_ = bf16[64,1536]{1,0:T(8,128)(2,1)S(1)} collective-permute-done((bf16[64,1536]{1,0:T(8,128)(2,1)}, bf16[64,1536]{1,0:T(8,128)(2,1)S(1)}, u32[]{:S(2)}, u32[]{:S(2)}) %collective-permute-start.1) | collective-permute-done | bytes 196640 | tf_op jit(solution)/shard_map/ppermute | solution.py:367
  14.0 3.2 %collective-permute-start.3 = (bf16[32,1536]{1,0:T(8,128)(2,1)S(1)}, bf16[32,1536]{1,0:T(8,128)(2,1)S(1)}, u32[]{:S(2)}, u32[]{:S(2)}) collective-permute-start(bf16[32,1536]{1,0:T(8,128)(2,1)S(1)} %slice.117), channel_id=1, source_target_pairs={{0,12},{4,0},{8,4},{12,8},{1,13},{5,1},{9,5},{13,9},{2,14},{6,2},{... | collective-permute-start | bytes 294920 | tf_op jit(solution)/shard_map/ppermute | solution.py:371
  17.2 3.4 %stage.1.refs_6_ = bf16[2,2,1536,512]{3,2,1,0:T(8,128)(2,1)S(1)} custom-call(s32[3]{0:T(128)S(1)} %pad_add_fusion.info, bf16[8,1536,1024]{2,1,0:T(8,128)(2,1)} %refs_7_.9, bf16[8,1536,1024]{2,1,0:T(8,128)(2,1)} %refs_8_.7), custom_call_target="tpu_custom_call" | custom-call | flops 1 | bytes 1 | tf_op jit(solution)/shard_map/stage/pallas_call | solution.py:113
  20.7 0.8 route.1
  21.4 4.5 %send_half.4 = (bf16[2,256,512]{2,1,0:T(8,128)(2,1)S(1)}, bf16[256,1536]{1,0:T(8,128)(2,1)S(1)}, bf16[2,2,1536,512]{3,2,1,0:T(8,128)(2,1)S(1)}) custom-call(s32[3]{0:T(128)S(1)} %pad_add_fusion.info, bf16[64,1536]{1,0:T(8,128)(2,1)S(1)} %copy-done, bf16[64,1536]{1,0:T(8,128)(2,1)S(1)} %collective-permute-done.refs_1_, ...), custom_call_target="tpu_custom_call" | custom-call | flops 1 | bytes 1 | tf_op jit(solution)/shard_map/send_half/pallas_call | solution.py:113
  26.0 4.2 %keep_half.4 = (bf16[2,256,512]{2,1,0:T(8,128)(2,1)S(1)}, bf16[2,2,1536,512]{3,2,1,0:T(8,128)(2,1)S(1)}) custom-call(s32[3]{0:T(128)S(1)} %pad_add_fusion.info, bf16[256,1536]{1,0:T(8,128)(2,1)S(1)} %get-tuple-element.43.refs_0_, bf16[2,2,1536,512]{3,2,1,0:T(8,128)(2,1)S(1)} %get-tuple-element.44.refs_1_, bf16[8,1536,1024]{2,1,0:T(8,128)(2,1)} %refs_7_.9, ...), custom_call_target="tpu_custom_call" | custom-call | flops 1 | bytes 1 | tf_op jit(solution)/shard_map/keep_half/pallas_call | solution.py:113
  30.4 1.6 %collective-permute-start.9 = (bf16[1,256,512]{2,1,0:T(8,128)(2,1)S(1)}, bf16[1,256,512]{2,1,0:T(8,128)(2,1)S(1)}, u32[]{:S(2)}, u32[]{:S(2)}) collective-permute-start(bf16[1,256,512]{2,1,0:T(8,128)(2,1)S(1)} %slice.181.refs_9_), channel_id=1, source_target_pairs={{0,2},{1,3},{2,0},{3,1},{4,6},{5,7},{6,4},{7,5},{8,10},{9,11},{10,... | collective-permute-start | bytes 786440 | tf_op jit(solution)/shard_map/ppermute | solution.py:23
  32.0 4.6 %send_half.5 = (bf16[2,256,512]{2,1,0:T(8,128)(2,1)S(1)}, bf16[256,1536]{1,0:T(8,128)(2,1)S(1)}, bf16[2,2,1536,512]{3,2,1,0:T(8,128)(2,1)S(1)}) custom-call(s32[3]{0:T(128)S(1)} %pad_add_fusion.info, bf16[64,1536]{1,0:T(8,128)(2,1)S(1)} %copy-done, bf16[64,1536]{1,0:T(8,128)(2,1)S(1)} %collective-permute-done.refs_1_, ...), custom_call_target="tpu_custom_call" | custom-call | flops 1 | bytes 1 | tf_op jit(solution)/shard_map/send_half/pallas_call | solution.py:113
  36.9 4.2 %keep_half.5 = (bf16[2,256,512]{2,1,0:T(8,128)(2,1)S(1)}, bf16[2,2,1536,512]{3,2,1,0:T(8,128)(2,1)S(1)}) custom-call(s32[3]{0:T(128)S(1)} %pad_add_fusion.info, bf16[256,1536]{1,0:T(8,128)(2,1)S(1)} %get-tuple-element.48.refs_0_, bf16[2,2,1536,512]{3,2,1,0:T(8,128)(2,1)S(1)} %get-tuple-element.49.refs_1_, bf16[8,1536,1024]{2,1,0:T(8,128)(2,1)} %refs_7_.9, ...), custom_call_target="tpu_custom_call" | custom-call | flops 1 | bytes 1 | tf_op jit(solution)/shard_map/keep_half/pallas_call | solution.py:113
  42.1 4.5 %send_half.6 = (bf16[2,256,512]{2,1,0:T(8,128)(2,1)S(1)}, bf16[256,1536]{1,0:T(8,128)(2,1)S(1)}, bf16[2,2,1536,512]{3,2,1,0:T(8,128)(2,1)S(1)}) custom-call(s32[3]{0:T(128)S(1)} %pad_add_fusion.info, bf16[64,1536]{1,0:T(8,128)(2,1)S(1)} %copy-done, bf16[64,1536]{1,0:T(8,128)(2,1)S(1)} %collective-permute-done.refs_1_, ...), custom_call_target="tpu_custom_call" | custom-call | flops 1 | bytes 1 | tf_op jit(solution)/shard_map/send_half/pallas_call | solution.py:113
  46.7 4.2 %keep_half.6 = (bf16[2,256,512]{2,1,0:T(8,128)(2,1)S(1)}, bf16[2,2,1536,512]{3,2,1,0:T(8,128)(2,1)S(1)}) custom-call(s32[3]{0:T(128)S(1)} %pad_add_fusion.info, bf16[256,1536]{1,0:T(8,128)(2,1)S(1)} %get-tuple-element.53.refs_0_, bf16[2,2,1536,512]{3,2,1,0:T(8,128)(2,1)S(1)} %get-tuple-element.54.refs_1_, bf16[8,1536,1024]{2,1,0:T(8,128)(2,1)} %refs_7_.9, ...), custom_call_target="tpu_custom_call" | custom-call | flops 1 | bytes 1 | tf_op jit(solution)/shard_map/keep_half/pallas_call | solution.py:113
  50.9 2.0 %collective-permute-done.11.refs_1_ = bf16[1,256,768]{2,1,0:T(8,128)(2,1)S(1)} collective-permute-done((bf16[1,256,768]{2,1,0:T(8,128)(2,1)S(1)}, bf16[1,256,768]{2,1,0:T(8,128)(2,1)S(1)}, u32[]{:S(2)}, u32[]{:S(2)}) %collective-permute-start.11) | collective-permute-done | bytes 393248 | tf_op jit(solution)/shard_map/ppermute | solution.py:23
  53.9 4.6 %send_half.7 = (bf16[2,256,512]{2,1,0:T(8,128)(2,1)S(1)}, bf16[256,1536]{1,0:T(8,128)(2,1)S(1)}, bf16[2,2,1536,512]{3,2,1,0:T(8,128)(2,1)S(1)}) custom-call(s32[3]{0:T(128)S(1)} %pad_add_fusion.info, bf16[64,1536]{1,0:T(8,128)(2,1)S(1)} %copy-done, bf16[64,1536]{1,0:T(8,128)(2,1)S(1)} %collective-permute-done.refs_1_, ...), custom_call_target="tpu_custom_call" | custom-call | flops 1 | bytes 1 | tf_op jit(solution)/shard_map/send_half/pallas_call | solution.py:113
  58.7 3.6 %keep_half.7 = (bf16[2,256,512]{2,1,0:T(8,128)(2,1)S(1)}, bf16[2,1024,1536]{2,1,0:T(8,128)(2,1)S(1)}) custom-call(s32[3]{0:T(128)S(1)} %pad_add_fusion.info, bf16[256,1536]{1,0:T(8,128)(2,1)S(1)} %get-tuple-element.58.refs_0_, bf16[2,2,1536,512]{3,2,1,0:T(8,128)(2,1)S(1)} %get-tuple-element.59.refs_1_, bf16[8,1024,1536]{2,1,0:T(8,128)(2,1)} %refs_7_.11), custom_call_target="tpu_custom_call" | custom-call | flops 1 | bytes 1 | tf_op jit(solution)/shard_map/keep_half/pallas_call | solution.py:113
  62.3 1.6 %collective-permute-done.13.refs_1_ = bf16[1,256,768]{2,1,0:T(8,128)(2,1)S(1)} collective-permute-done((bf16[1,256,768]{2,1,0:T(8,128)(2,1)S(1)}, bf16[1,256,768]{2,1,0:T(8,128)(2,1)S(1)}, u32[]{:S(2)}, u32[]{:S(2)}) %collective-permute-start.13) | collective-permute-done | bytes 393248 | tf_op jit(solution)/shard_map/ppermute | solution.py:23
  65.6 0.9 collective-permute-done.16.refs_2_
  66.5 3.6 %down.4 = (f32[256,1536]{1,0:T(8,128)S(1)}, bf16[2,1024,1536]{2,1,0:T(8,128)(2,1)S(1)}) custom-call(s32[3]{0:T(128)S(1)} %pad_add_fusion.info, bf16[1,256,256]{2,1,0:T(8,128)(2,1)S(1)} %fusion.3.refs_0_, bf16[1,256,768]{2,1,0:T(8,128)(2,1)S(1)} %copy-done.2, bf16[2,256,256]{2,1,0:T(8,128)(2,1)S(1)} %collective-permute-done.16.refs_2_, ...), custom_call_target="tpu_custom_call" | custom-call | flops 1 | bytes 1 | tf_op jit(solution)/shard_map/down/pallas_call | solution.py:113
  70.2 3.5 %down.5 = (f32[256,1536]{1,0:T(8,128)S(1)}, bf16[2,1024,1536]{2,1,0:T(8,128)(2,1)S(1)}) custom-call(s32[3]{0:T(128)S(1)} %pad_add_fusion.info, bf16[1,256,256]{2,1,0:T(8,128)(2,1)S(1)} %fusion.2.refs_0_, bf16[1,256,768]{2,1,0:T(8,128)(2,1)S(1)} %collective-permute-done.13.refs_1_, bf16[2,256,256]{2,1,0:T(8,128)(2,1)S(1)} %collective-permute-done.15.refs_2_, ...), custom_call_target="tpu_custom_call" | custom-call | flops 1 | bytes 1 | tf_op jit(solution)/shard_map/down/pallas_call | solution.py:113
  74.6 1.6 %collective-permute-start.17 = (bf16[1,256,256]{2,1,0:T(8,128)(2,1)S(1)}, bf16[1,256,256]{2,1,0:T(8,128)(2,1)S(1)}, u32[]{:S(2)}, u32[]{:S(2)}) collective-permute-start(bf16[1,256,256]{2,1,0:T(8,128)(2,1)S(1)} %fusion.refs_8_.refs_0_), channel_id=1, source_target_pairs={{0,2},{1,3},{2,0},{3,1},{4,6},{5,7},{6,4},{7,5},{8,10},{9,11},{10,... | collective-permute-start | bytes 393224 | tf_op jit(solution)/shard_map/ppermute | solution.py:23
  76.2 3.4 %down.6 = (f32[256,1536]{1,0:T(8,128)S(1)}, bf16[2,1024,1536]{2,1,0:T(8,128)(2,1)S(1)}) custom-call(s32[3]{0:T(128)S(1)} %pad_add_fusion.info, bf16[1,256,256]{2,1,0:T(8,128)(2,1)S(1)} %fusion.1.refs_0_, bf16[1,256,768]{2,1,0:T(8,128)(2,1)S(1)} %collective-permute-done.14.refs_1_, bf16[2,256,256]{2,1,0:T(8,128)(2,1)S(1)} %collective-permute-done.18.refs_2_, ...), custom_call_target="tpu_custom_call" | custom-call | flops 1 | bytes 1 | tf_op jit(solution)/shard_map/down/pallas_call | solution.py:113
  79.7 0.9 collective-permute-done.17.refs_1_
  80.7 1.5 %collective-permute-done.19.refs_2_ = bf16[2,256,256]{2,1,0:T(8,128)(2,1)S(1)} collective-permute-done((bf16[2,256,256]{2,1,0:T(8,128)(2,1)S(1)}, bf16[2,256,256]{2,1,0:T(8,128)(2,1)S(1)}, u32[]{:S(2)}, u32[]{:S(2)}) %collective-permute-start.19) | collective-permute-done | bytes 262176 | tf_op jit(solution)/shard_map/ppermute | solution.py:23
  82.2 1.8 %down.7 = (bf16[64,1536]{1,0:T(8,128)(2,1)S(1)}, bf16[32,1536]{1,0:T(8,128)(2,1)S(1)}, bf16[32,1536]{1,0:T(8,128)(2,1)S(1)}, bf16[32,1536]{1,0:T(8,128)(2,1)S(1)...) custom-call(s32[3]{0:T(128)S(1)} %pad_add_fusion.info, ...), custom_call_target="tpu_custom_call" | custom-call | flops 1 | bytes 1 | tf_op jit(solution)/shard_map/down/pallas_call | solution.py:113
  84.1 3.8 %collective-permute-start.20 = (bf16[32,1536]{1,0:T(8,128)(2,1)S(1)}, bf16[32,1536]{1,0:T(8,128)(2,1)S(1)}, u32[]{:S(2)}, u32[]{:S(2)}) collective-permute-start(bf16[32,1536]{1,0:T(8,128)(2,1)S(1)} %get-tuple-element.74), channel_id=1, source_target_pairs={{0,12},{4,0},{8,4},{12,8},{1,13},{5,1},{9,5},{13,9},{2,14},{6,2},{... | collective-permute-start | bytes 294920 | tf_op jit(solution)/shard_map/ppermute | solution.py:386
  87.9 3.8 %collective-permute-start.23 = (bf16[32,1536]{1,0:T(8,128)(2,1)S(1)}, bf16[32,1536]{1,0:T(8,128)(2,1)S(1)}, u32[]{:S(2)}, u32[]{:S(2)}) collective-permute-start(bf16[32,1536]{1,0:T(8,128)(2,1)S(1)} %get-tuple-element.76), channel_id=1, source_target_pairs={{0,12},{4,0},{8,4},{12,8},{1,13},{5,1},{9,5},{13,9},{2,14},{6,2},{... | collective-permute-start | bytes 294920 | tf_op jit(solution)/shard_map/ppermute | solution.py:386
  91.9 3.9 %collective-permute-start.21 = (bf16[32,1536]{1,0:T(8,128)(2,1)S(1)}, bf16[32,1536]{1,0:T(8,128)(2,1)S(1)}, u32[]{:S(2)}, u32[]{:S(2)}) collective-permute-start(bf16[32,1536]{1,0:T(8,128)(2,1)S(1)} %add_convert_fusion.1), channel_id=1, source_target_pairs={{0,12},{4,0},{8,4},{12,8},{1,13},{5,1},{9,5},{13,9},{2,14},{6,2},{... | collective-permute-start | bytes 294920 | tf_op jit(solution)/shard_map/ppermute | solution.py:386
  95.8 4.2 %collective-permute-done.25 = bf16[32,1536]{1,0:T(8,128)(2,1)S(1)} collective-permute-done((bf16[32,1536]{1,0:T(8,128)(2,1)S(1)}, bf16[32,1536]{1,0:T(8,128)(2,1)S(1)}, u32[]{:S(2)}, u32[]{:S(2)}) %collective-permute-start.25) | collective-permute-done | bytes 98336 | tf_op jit(solution)/shard_map/ppermute | solution.py:386
  100.1 0.7 pad_maximum_fusion.7
  (78 shorter events, 7.2 us)
Async XLA Ops:
  0.0 11.0 %collective-permute-start = (bf16[64,1536]{1,0:T(8,128)(2,1)}, bf16[64,1536]{1,0:T(8,128)(2,1)S(1)}, u32[]{:S(2)}, u32[]{:S(2)}) collective-permute-start(bf16[64,1536]{1,0:T(8,128)(2,1)} %refs_0_.9), channel_id=1, source_target_pairs={{0,4},{4,8},{8,12},{12,0},{1,5},{5,9},{9,13},{13,1},{2,6},{6,10},{... | collective-permute-start | bytes 589832 | tf_op jit(solution)/shard_map/ppermute | solution.py:367
  3.0 11.0 %collective-permute-start.1 = (bf16[64,1536]{1,0:T(8,128)(2,1)}, bf16[64,1536]{1,0:T(8,128)(2,1)S(1)}, u32[]{:S(2)}, u32[]{:S(2)}) collective-permute-start(bf16[64,1536]{1,0:T(8,128)(2,1)} %refs_0_.9), channel_id=1, source_target_pairs={{0,12},{4,0},{8,4},{12,8},{1,13},{5,1},{9,5},{13,9},{2,14},{6,2},{... | collective-permute-start | bytes 589832 | tf_op jit(solution)/shard_map/ppermute | solution.py:367
  6.4 14.2 %collective-permute-start.4 = (f32[16,64]{1,0:T(8,128)S(1)}, f32[16,64]{1,0:T(8,128)S(1)}, u32[]{:S(2)}, u32[]{:S(2)}) collective-permute-start(f32[16,64]{1,0:T(8,128)S(1)} %pad_maximum_fusion.8.refs_0_), channel_id=1, source_target_pairs={{0,4},{4,8},{8,12},{12,0},{1,5},{5,9},{9,13},{13,1},{2,6},{6,10},{... | collective-permute-start | bytes 12296 | tf_op jit(solution)/shard_map/ppermute | solution.py:302
  6.4 14.2 %collective-permute-start.5 = (f32[16,64]{1,0:T(8,128)S(1)}, f32[16,64]{1,0:T(8,128)S(1)}, u32[]{:S(2)}, u32[]{:S(2)}) collective-permute-start(f32[16,64]{1,0:T(8,128)S(1)} %pad_maximum_fusion.8.refs_0_), channel_id=1, source_target_pairs={{0,12},{4,0},{8,4},{12,8},{1,13},{5,1},{9,5},{13,9},{2,14},{6,2},{... | collective-permute-start | bytes 12296 | tf_op jit(solution)/shard_map/ppermute | solution.py:302
  10.3 10.4 %collective-permute-start.6 = (f32[16,64]{1,0:T(8,128)S(1)}, f32[16,64]{1,0:T(8,128)S(1)}, u32[]{:S(2)}, u32[]{:S(2)}) collective-permute-start(f32[16,64]{1,0:T(8,128)S(1)} %pad_maximum_fusion.8.refs_0_), channel_id=1, source_target_pairs={{0,8},{4,12},{8,0},{12,4},{1,9},{5,13},{9,1},{13,5},{2,10},{6,14},... | collective-permute-start | bytes 12296 | tf_op jit(solution)/shard_map/ppermute | solution.py:302
  11.0 10.4 %collective-permute-start.2 = (bf16[32,1536]{1,0:T(8,128)(2,1)S(1)}, bf16[32,1536]{1,0:T(8,128)(2,1)S(1)}, u32[]{:S(2)}, u32[]{:S(2)}) collective-permute-start(bf16[32,1536]{1,0:T(8,128)(2,1)S(1)} %slice.116), channel_id=1, source_target_pairs={{0,4},{4,8},{8,12},{12,0},{1,5},{5,9},{9,13},{13,1},{2,6},{6,10},{... | collective-permute-start | bytes 294920 | tf_op jit(solution)/shard_map/ppermute | solution.py:371
  14.0 7.4 %collective-permute-start.3 = (bf16[32,1536]{1,0:T(8,128)(2,1)S(1)}, bf16[32,1536]{1,0:T(8,128)(2,1)S(1)}, u32[]{:S(2)}, u32[]{:S(2)}) collective-permute-start(bf16[32,1536]{1,0:T(8,128)(2,1)S(1)} %slice.117), channel_id=1, source_target_pairs={{0,12},{4,0},{8,4},{12,8},{1,13},{5,1},{9,5},{13,9},{2,14},{6,2},{... | collective-permute-start | bytes 294920 | tf_op jit(solution)/shard_map/ppermute | solution.py:371
  17.2 4.2 %copy-start = (bf16[64,1536]{1,0:T(8,128)(2,1)S(1)}, bf16[64,1536]{1,0:T(8,128)(2,1)}, u32[]{:S(2)}) copy-start(bf16[64,1536]{1,0:T(8,128)(2,1)} %refs_0_.9) | copy-start | bytes 589828
  25.9 4.3 %collective-permute-start.7 = (bf16[2,256,512]{2,1,0:T(8,128)(2,1)S(1)}, bf16[2,256,512]{2,1,0:T(8,128)(2,1)S(1)}, u32[]{:S(2)}, u32[]{:S(2)}) collective-permute-start(bf16[2,256,512]{2,1,0:T(8,128)(2,1)S(1)} %get-tuple-element.47), channel_id=1, source_target_pairs={{0,1},{1,0},{2,3},{3,2},{4,5},{5,4},{6,7},{7,6},{8,9},{9,8},{10,11... | collective-permute-start | bytes 1572872 | tf_op jit(solution)/shard_map/ppermute | solution.py:23
  30.4 10.7 %collective-permute-start.9 = (bf16[1,256,512]{2,1,0:T(8,128)(2,1)S(1)}, bf16[1,256,512]{2,1,0:T(8,128)(2,1)S(1)}, u32[]{:S(2)}, u32[]{:S(2)}) collective-permute-start(bf16[1,256,512]{2,1,0:T(8,128)(2,1)S(1)} %slice.181.refs_9_), channel_id=1, source_target_pairs={{0,2},{1,3},{2,0},{3,1},{4,6},{5,7},{6,4},{7,5},{8,10},{9,11},{10,... | collective-permute-start | bytes 786440 | tf_op jit(solution)/shard_map/ppermute | solution.py:23
  36.6 4.7 %collective-permute-start.8 = (bf16[2,256,512]{2,1,0:T(8,128)(2,1)S(1)}, bf16[2,256,512]{2,1,0:T(8,128)(2,1)S(1)}, u32[]{:S(2)}, u32[]{:S(2)}) collective-permute-start(bf16[2,256,512]{2,1,0:T(8,128)(2,1)S(1)} %get-tuple-element.52), channel_id=1, source_target_pairs={{0,1},{1,0},{2,3},{3,2},{4,5},{5,4},{6,7},{7,6},{8,9},{9,8},{10,11... | collective-permute-start | bytes 1572872 | tf_op jit(solution)/shard_map/ppermute | solution.py:23
  41.5 11.4 %collective-permute-start.11 = (bf16[1,256,768]{2,1,0:T(8,128)(2,1)S(1)}, bf16[1,256,768]{2,1,0:T(8,128)(2,1)S(1)}, u32[]{:S(2)}, u32[]{:S(2)}) collective-permute-start(bf16[1,256,768]{2,1,0:T(8,128)(2,1)S(1)} %pad_maximum_fusion.refs_9_), channel_id=1, source_target_pairs={{0,2},{1,3},{2,0},{3,1},{4,6},{5,7},{6,4},{7,5},{8,10},{9,11},{10,... | collective-permute-start | bytes 1179656 | tf_op jit(solution)/shard_map/ppermute | solution.py:23
  46.6 6.5 %collective-permute-start.10 = (bf16[2,256,512]{2,1,0:T(8,128)(2,1)S(1)}, bf16[2,256,512]{2,1,0:T(8,128)(2,1)S(1)}, u32[]{:S(2)}, u32[]{:S(2)}) collective-permute-start(bf16[2,256,512]{2,1,0:T(8,128)(2,1)S(1)} %get-tuple-element.57), channel_id=1, source_target_pairs={{0,1},{1,0},{2,3},{3,2},{4,5},{5,4},{6,7},{7,6},{8,9},{9,8},{10,11... | collective-permute-start | bytes 1572872 | tf_op jit(solution)/shard_map/ppermute | solution.py:23
  52.9 5.7 %copy-start.1 = (bf16[1,256,768]{2,1,0:T(8,128)(2,1)}, bf16[1,256,768]{2,1,0:T(8,128)(2,1)S(1)}, u32[]{:S(2)}) copy-start(bf16[1,256,768]{2,1,0:T(8,128)(2,1)S(1)} %collective-permute-done.11.refs_1_) | copy-start | bytes 1179652
  53.3 10.6 %collective-permute-start.13 = (bf16[1,256,768]{2,1,0:T(8,128)(2,1)S(1)}, bf16[1,256,768]{2,1,0:T(8,128)(2,1)S(1)}, u32[]{:S(2)}, u32[]{:S(2)}) collective-permute-start(bf16[1,256,768]{2,1,0:T(8,128)(2,1)S(1)} %pad_maximum_fusion.1.refs_9_), channel_id=1, source_target_pairs={{0,2},{1,3},{2,0},{3,1},{4,6},{5,7},{6,4},{7,5},{8,10},{9,11},{10,... | collective-permute-start | bytes 1179656 | tf_op jit(solution)/shard_map/ppermute | solution.py:23
  58.6 5.5 %collective-permute-start.12 = (bf16[2,256,512]{2,1,0:T(8,128)(2,1)S(1)}, bf16[2,256,512]{2,1,0:T(8,128)(2,1)S(1)}, u32[]{:S(2)}, u32[]{:S(2)}) collective-permute-start(bf16[2,256,512]{2,1,0:T(8,128)(2,1)S(1)} %get-tuple-element.61), channel_id=1, source_target_pairs={{0,1},{1,0},{2,3},{3,2},{4,5},{5,4},{6,7},{7,6},{8,9},{9,8},{10,11... | collective-permute-start | bytes 1572872 | tf_op jit(solution)/shard_map/ppermute | solution.py:23
  58.7 6.2 %slice-start = ((bf16[1,256,768]{2,1,0:T(8,128)(2,1)}), bf16[1,256,256]{2,1,0:T(8,128)(2,1)S(1)}, s32[]{:S(2)}) async-start(bf16[1,256,768]{2,1,0:T(8,128)(2,1)} %copy-done.1), calls=%async_computation | async-start | bytes 262144 | tf_op jit(solution)/shard_map/slice | solution.py:267
  62.3 4.2 %copy-start.2 = (bf16[1,256,768]{2,1,0:T(8,128)(2,1)S(1)}, bf16[1,256,768]{2,1,0:T(8,128)(2,1)}, u32[]{:S(2)}) copy-start(bf16[1,256,768]{2,1,0:T(8,128)(2,1)} %copy-done.1) | copy-start | bytes 1179652
  64.3 10.0 %collective-permute-start.14 = (bf16[1,256,768]{2,1,0:T(8,128)(2,1)S(1)}, bf16[1,256,768]{2,1,0:T(8,128)(2,1)S(1)}, u32[]{:S(2)}, u32[]{:S(2)}) collective-permute-start(bf16[1,256,768]{2,1,0:T(8,128)(2,1)S(1)} %pad_maximum_fusion.2.refs_7_), channel_id=1, source_target_pairs={{0,2},{1,3},{2,0},{3,1},{4,6},{5,7},{6,4},{7,5},{8,10},{9,11},{10,... | collective-permute-start | bytes 1179656 | tf_op jit(solution)/shard_map/ppermute | solution.py:23
  64.9 1.6 %collective-permute-start.16 = (bf16[2,256,256]{2,1,0:T(8,128)(2,1)S(1)}, bf16[2,256,256]{2,1,0:T(8,128)(2,1)S(1)}, u32[]{:S(2)}, u32[]{:S(2)}) collective-permute-start(bf16[2,256,256]{2,1,0:T(8,128)(2,1)S(1)} %pad_maximum_fusion.4), channel_id=1, source_target_pairs={{0,1},{1,0},{2,3},{3,2},{4,5},{5,4},{6,7},{7,6},{8,9},{9,8},{10,11... | collective-permute-start | bytes 786440 | tf_op jit(solution)/shard_map/ppermute | solution.py:23
  65.1 5.1 %collective-permute-start.15 = (bf16[2,256,256]{2,1,0:T(8,128)(2,1)S(1)}, bf16[2,256,256]{2,1,0:T(8,128)(2,1)S(1)}, u32[]{:S(2)}, u32[]{:S(2)}) collective-permute-start(bf16[2,256,256]{2,1,0:T(8,128)(2,1)S(1)} %pad_maximum_fusion.3), channel_id=1, source_target_pairs={{0,1},{1,0},{2,3},{3,2},{4,5},{5,4},{6,7},{7,6},{8,9},{9,8},{10,11... | collective-permute-start | bytes 786440 | tf_op jit(solution)/shard_map/ppermute | solution.py:23
  74.4 1.8 %collective-permute-start.18 = (bf16[2,256,256]{2,1,0:T(8,128)(2,1)S(1)}, bf16[2,256,256]{2,1,0:T(8,128)(2,1)S(1)}, u32[]{:S(2)}, u32[]{:S(2)}) collective-permute-start(bf16[2,256,256]{2,1,0:T(8,128)(2,1)S(1)} %pad_maximum_fusion.5), channel_id=1, source_target_pairs={{0,1},{1,0},{2,3},{3,2},{4,5},{5,4},{6,7},{7,6},{8,9},{9,8},{10,11... | collective-permute-start | bytes 786440 | tf_op jit(solution)/shard_map/ppermute | solution.py:23
  74.6 6.0 %collective-permute-start.17 = (bf16[1,256,256]{2,1,0:T(8,128)(2,1)S(1)}, bf16[1,256,256]{2,1,0:T(8,128)(2,1)S(1)}, u32[]{:S(2)}, u32[]{:S(2)}) collective-permute-start(bf16[1,256,256]{2,1,0:T(8,128)(2,1)S(1)} %fusion.refs_8_.refs_0_), channel_id=1, source_target_pairs={{0,2},{1,3},{2,0},{3,1},{4,6},{5,7},{6,4},{7,5},{8,10},{9,11},{10,... | collective-permute-start | bytes 393224 | tf_op jit(solution)/shard_map/ppermute | solution.py:23
  80.6 1.6 %collective-permute-start.19 = (bf16[2,256,256]{2,1,0:T(8,128)(2,1)S(1)}, bf16[2,256,256]{2,1,0:T(8,128)(2,1)S(1)}, u32[]{:S(2)}, u32[]{:S(2)}) collective-permute-start(bf16[2,256,256]{2,1,0:T(8,128)(2,1)S(1)} %pad_maximum_fusion.6), channel_id=1, source_target_pairs={{0,1},{1,0},{2,3},{3,2},{4,5},{5,4},{6,7},{7,6},{8,9},{9,8},{10,11... | collective-permute-start | bytes 786440 | tf_op jit(solution)/shard_map/ppermute | solution.py:23
  84.0 7.7 %collective-permute-start.24 = (bf16[32,1536]{1,0:T(8,128)(2,1)S(1)}, bf16[32,1536]{1,0:T(8,128)(2,1)S(1)}, u32[]{:S(2)}, u32[]{:S(2)}) collective-permute-start(bf16[32,1536]{1,0:T(8,128)(2,1)S(1)} %get-tuple-element.78), channel_id=1, source_target_pairs={{0,4},{4,8},{8,12},{12,0},{1,5},{5,9},{9,13},{13,1},{2,6},{6,10},{... | collective-permute-start | bytes 294920 | tf_op jit(solution)/shard_map/ppermute | solution.py:386
  84.1 7.7 %collective-permute-start.20 = (bf16[32,1536]{1,0:T(8,128)(2,1)S(1)}, bf16[32,1536]{1,0:T(8,128)(2,1)S(1)}, u32[]{:S(2)}, u32[]{:S(2)}) collective-permute-start(bf16[32,1536]{1,0:T(8,128)(2,1)S(1)} %get-tuple-element.74), channel_id=1, source_target_pairs={{0,12},{4,0},{8,4},{12,8},{1,13},{5,1},{9,5},{13,9},{2,14},{6,2},{... | collective-permute-start | bytes 294920 | tf_op jit(solution)/shard_map/ppermute | solution.py:386
  87.9 7.9 %collective-permute-start.22 = (bf16[32,1536]{1,0:T(8,128)(2,1)S(1)}, bf16[32,1536]{1,0:T(8,128)(2,1)S(1)}, u32[]{:S(2)}, u32[]{:S(2)}) collective-permute-start(bf16[32,1536]{1,0:T(8,128)(2,1)S(1)} %get-tuple-element.75), channel_id=1, source_target_pairs={{0,4},{4,8},{8,12},{12,0},{1,5},{5,9},{9,13},{13,1},{2,6},{6,10},{... | collective-permute-start | bytes 294920 | tf_op jit(solution)/shard_map/ppermute | solution.py:386
  87.9 7.9 %collective-permute-start.23 = (bf16[32,1536]{1,0:T(8,128)(2,1)S(1)}, bf16[32,1536]{1,0:T(8,128)(2,1)S(1)}, u32[]{:S(2)}, u32[]{:S(2)}) collective-permute-start(bf16[32,1536]{1,0:T(8,128)(2,1)S(1)} %get-tuple-element.76), channel_id=1, source_target_pairs={{0,12},{4,0},{8,4},{12,8},{1,13},{5,1},{9,5},{13,9},{2,14},{6,2},{... | collective-permute-start | bytes 294920 | tf_op jit(solution)/shard_map/ppermute | solution.py:386
  91.8 8.2 %collective-permute-start.25 = (bf16[32,1536]{1,0:T(8,128)(2,1)S(1)}, bf16[32,1536]{1,0:T(8,128)(2,1)S(1)}, u32[]{:S(2)}, u32[]{:S(2)}) collective-permute-start(bf16[32,1536]{1,0:T(8,128)(2,1)S(1)} %add_convert_fusion), channel_id=1, source_target_pairs={{0,4},{4,8},{8,12},{12,0},{1,5},{5,9},{9,13},{13,1},{2,6},{6,10},{... | collective-permute-start | bytes 294920 | tf_op jit(solution)/shard_map/ppermute | solution.py:386
  91.9 8.1 %collective-permute-start.21 = (bf16[32,1536]{1,0:T(8,128)(2,1)S(1)}, bf16[32,1536]{1,0:T(8,128)(2,1)S(1)}, u32[]{:S(2)}, u32[]{:S(2)}) collective-permute-start(bf16[32,1536]{1,0:T(8,128)(2,1)S(1)} %add_convert_fusion.1), channel_id=1, source_target_pairs={{0,12},{4,0},{8,4},{12,8},{1,13},{5,1},{9,5},{13,9},{2,14},{6,2},{... | collective-permute-start | bytes 294920 | tf_op jit(solution)/shard_map/ppermute | solution.py:386
